TPU v7x, 32 devices: a whole 2x2x4 slice. The times are simulated.
32 devices in a mesh: pool: 4 (over x, core), dp: 8 (over z, y).
Axes of the slice: x: 2, y: 2, z: 4, core: 2. Of those that a mesh axis runs over, the one named last changes fastest.
Arguments:
- queries: bfloat16 [4, 8, 256, 2048], P('pool', 'dp'), may hold values from -48 to 48
- cotangent: bfloat16 [4, 8, 256, 2048], P('pool', 'dp'), may hold values from -6 to 6
- cond: bfloat16 [4, 8, 4, 512], P('pool', 'dp'), may hold values from -6 to 6
- nbr_owner: int32 [4, 8, 4, 2], P('pool', 'dp'), may hold values from 0 to 7, as said below
- nbr_block: int32 [4, 8, 4, 2], P('pool', 'dp'), may hold values from 0 to 15
- database: bfloat16 [4, 8, 16, 128, 512], P('pool', 'dp'), may hold values from -6 to 6
- lengths: int32 [4, 8, 16], P('pool', 'dp'), may hold values from 1 to 128, as said below
- gain: float32 [512], replicated, may hold values from 0.25 to 1.75
- w_down: bfloat16 [512, 256], replicated, may hold values from -0.25 to 0.25
- w_up: bfloat16 [256, 512], replicated, may hold values from -0.375 to 0.375
- w_kv: bfloat16 [512, 4096], replicated, may hold values from -0.25 to 0.25
Outputs:
- attn_out: bfloat16 [4, 8, 256, 2048], P('pool', 'dp')
- q_grad: bfloat16 [4, 8, 256, 2048], P('pool', 'dp')
- cond_grad: float32 [4, 8, 4, 512], P('pool', 'dp')
- adapter_grad: float32 [512, 512], P(('pool', 'dp'))
Inputs may be any that keep to these rules, and one draw needn't show every extreme that they name: `nbr_owner`: among the 8 neighbours of each of the decoder devices (pool index below 4-1) that share one index of dp, no encoder device is named more than 4 times, and one encoder device, the same for every index of dp, is named exactly 4 times. Entries at pool index 4-1 are not read. `lengths`: every encoder device holds a block of length 128.
All inputs are finite; a program needn't handle non-finite values.
Results may differ from a plain program's by a relative error of at most 0.013.
The roundings to bfloat16 on the way count: a program that leaves them out, or rounds other values in their place, can miss the bound.
Values may be sent and summed in bfloat16 or wider, within the bound.
No kernel may reach another device: no remote copies, remote signals or barrier semaphores. Data moves between devices by JAX's collectives and lax.ppermute only.
A program may use at most 192 MiB of HBM per device.

v0:
```python
import jax
import jax.numpy as jnp
from jax import lax
from jax.sharding import PartitionSpec as P

HEADS = 16
HEAD = 128
SPAN = 64


EPSILON = 1e-06
FLOOR = -1e30


def spread(block, axis, owner):
    block = jnp.where(lax.axis_index(axis) == owner, block, jnp.zeros_like(block))
    return lax.psum(block, axis)


def encode_rows(block_rows, cond_rows, gain, w_down, w_up):
    x_full = block_rows.astype(jnp.float32) + cond_rows.astype(jnp.float32)[..., None, :]
    inv_rms = lax.rsqrt(jnp.mean(x_full * x_full, axis=-1, keepdims=True) + EPSILON)
    hidden = (x_full * inv_rms * gain).astype(jnp.bfloat16)
    flat_hidden = hidden.reshape(-1, hidden.shape[-1])
    latent = jnp.dot(flat_hidden, w_down, preferred_element_type=jnp.float32).astype(jnp.bfloat16)
    branch = jnp.dot(latent, w_up, preferred_element_type=jnp.float32).reshape(x_full.shape)
    encoded = (x_full + branch).astype(jnp.bfloat16)
    return (
        encoded,
        x_full,
        inv_rms,
        hidden,
        latent.reshape(x_full.shape[:-1] + (latent.shape[-1],)),
    )


def encode_back(enc_grad, x_full, inv_rms, gain, w_down, w_up):
    flat_grad = enc_grad.reshape(-1, enc_grad.shape[-1])
    lat_grad = jnp.dot(flat_grad, w_up.T, preferred_element_type=jnp.float32).astype(jnp.bfloat16)
    hid_grad = jnp.dot(lat_grad, w_down.T, preferred_element_type=jnp.float32).reshape(x_full.shape)
    scaled = hid_grad * gain
    normed = x_full * inv_rms
    x_grad = enc_grad.astype(jnp.float32) + inv_rms * (
        scaled - normed * jnp.mean(scaled * normed, axis=-1, keepdims=True)
    )
    return (jnp.sum(x_grad, axis=-2), lat_grad.reshape(x_full.shape[:-1] + (lat_grad.shape[-1],)))


def attend(query_rows, cot_rows, encoded, block_len, w_kv):
    token_count, head_cols = query_rows.shape
    block_count, slot_len, enc_width = encoded.shape
    span_count = token_count // SPAN
    key_count = block_count * slot_len // span_count
    scaling = HEAD ** (-0.5)
    key_value = jnp.dot(
        encoded.reshape(block_count * slot_len, enc_width), w_kv, preferred_element_type=jnp.float32
    ).astype(jnp.bfloat16)
    key_rows = key_value[:, :head_cols].reshape(span_count, key_count, HEADS, HEAD)
    value_rows = key_value[:, head_cols:].reshape(span_count, key_count, HEADS, HEAD)
    q_heads = query_rows.reshape(span_count, SPAN, HEADS, HEAD)
    out_grad = cot_rows.reshape(span_count, SPAN, HEADS, HEAD)
    usable = (jnp.arange(slot_len, dtype=jnp.int32)[None, :] < block_len[:, None]).reshape(
        span_count, 1, 1, key_count
    )
    scores = (
        jnp.einsum("cqhd,ckhd->chqk", q_heads, key_rows, preferred_element_type=jnp.float32)
        * scaling
    )
    scores = jnp.where(usable, scores, FLOOR)
    row_max = jnp.max(scores, axis=-1, keepdims=True)
    raised = jnp.exp(scores - row_max)
    probs = raised / jnp.sum(raised, axis=-1, keepdims=True)
    probs_b = probs.astype(jnp.bfloat16)
    attn_out = (
        jnp.einsum("chqk,ckhd->cqhd", probs_b, value_rows, preferred_element_type=jnp.float32)
        .astype(jnp.bfloat16)
        .reshape(token_count, head_cols)
    )
    d_probs = jnp.einsum(
        "cqhd,ckhd->chqk", out_grad, value_rows, preferred_element_type=jnp.float32
    )
    delta = jnp.sum(probs * d_probs, axis=-1, keepdims=True)
    d_scores = (probs * (d_probs - delta)).astype(jnp.bfloat16)
    q_grad = (
        (
            jnp.einsum("chqk,ckhd->cqhd", d_scores, key_rows, preferred_element_type=jnp.float32)
            * scaling
        )
        .astype(jnp.bfloat16)
        .reshape(token_count, head_cols)
    )
    key_grad = (
        jnp.einsum("chqk,cqhd->ckhd", d_scores, q_heads, preferred_element_type=jnp.float32)
        * scaling
    ).astype(jnp.bfloat16)
    value_grad = jnp.einsum(
        "chqk,cqhd->ckhd", probs_b, out_grad, preferred_element_type=jnp.float32
    ).astype(jnp.bfloat16)
    kv_grad = jnp.concatenate(
        [
            key_grad.reshape(block_count * slot_len, head_cols),
            value_grad.reshape(block_count * slot_len, head_cols),
        ],
        axis=1,
    )
    enc_grad = lax.dot_general(
        kv_grad, w_kv, (((1,), (1,)), ((), ())), preferred_element_type=jnp.float32
    ).astype(jnp.bfloat16)
    return (attn_out, q_grad, enc_grad.reshape(block_count, slot_len, enc_width))


def body(
    queries, cotangent, cond, nbr_owner, nbr_block, database, lengths, gain, w_down, w_up, w_kv
):
    pool_count = lax.axis_size("pool")
    columns = lax.axis_size("dp")
    relay_row = pool_count - 1
    pool_index = lax.axis_index("pool")
    on_encoder = pool_index == relay_row
    span_count = cond.shape[2]
    enc_width = cond.shape[3]
    nbr_count = nbr_owner.shape[3]
    per_device = span_count * nbr_count
    slot_len = database.shape[3]
    live_count = relay_row * per_device
    capacity = max(2, live_count // columns + 1)
    slot_count = columns * capacity
    token_count = queries.shape[2]
    head_cols = queries.shape[3]
    rank_width = w_down.shape[1]
    lead_shape = (columns, capacity, slot_len)
    owners_all, blocks_all = (
        lax.all_gather(nbr_owner.reshape(1, per_device), "pool", axis=0, tiled=True),
        lax.all_gather(nbr_block.reshape(1, per_device), "pool", axis=0, tiled=True),
    )
    req_owner = owners_all[:relay_row].reshape(live_count)
    req_block = blocks_all[:relay_row].reshape(live_count)
    owner_hot = (req_owner[:, None] == jnp.arange(columns, dtype=jnp.int32)[None, :]).astype(
        jnp.int32
    )
    slot_rank = jnp.sum(jnp.cumsum(owner_hot, axis=0) * owner_hot, axis=1) - 1
    position = req_owner * capacity + slot_rank
    placing = jnp.arange(slot_count, dtype=jnp.int32)[:, None] == position[None, :]
    slot_block = jnp.sum(jnp.where(placing, req_block[None, :], 0), axis=1).reshape(
        columns, capacity
    )
    got_block = lax.all_to_all(slot_block, "dp", split_axis=0, concat_axis=0, tiled=True)
    store_rows = database.reshape(database.shape[2], slot_len, enc_width)
    store_len = lengths.reshape(lengths.shape[2])
    flat_block = got_block.reshape(slot_count)
    block_rows = jnp.take(store_rows, flat_block, axis=0).reshape(lead_shape + (enc_width,))
    block_hot = flat_block[:, None] == jnp.arange(store_len.shape[0], dtype=jnp.int32)[None, :]
    row_len = jnp.sum(jnp.where(block_hot, store_len[None, :], 0), axis=1).reshape(
        columns, capacity
    )
    back_enc, back_len = (
        lax.all_to_all(block_rows, "dp", split_axis=0, concat_axis=0, tiled=True),
        lax.all_to_all(row_len, "dp", split_axis=0, concat_axis=0, tiled=True),
    )
    mine_enc = jnp.take(
        back_enc.reshape(slot_count, slot_len, enc_width), position, axis=0
    ).reshape(relay_row, per_device, slot_len, enc_width)
    mine_len = jnp.take(back_len.reshape(slot_count), position, axis=0).reshape(
        relay_row, per_device
    )
    down_enc, down_len = (spread(mine_enc, "pool", relay_row), spread(mine_len, "pool", relay_row))
    own_row = jnp.minimum(pool_index, relay_row - 1)
    my_enc = lax.dynamic_index_in_dim(down_enc, own_row, 0, keepdims=False)
    my_len = lax.dynamic_index_in_dim(down_len, own_row, 0, keepdims=False)
    query_flat = queries.reshape(token_count, head_cols)
    cot_flat = cotangent.reshape(token_count, head_cols)
    cond_local = jnp.repeat(cond.reshape(span_count, enc_width), nbr_count, axis=0)

    def local_run(query_rows, cot_rows, raw_rows, len_rows, cond_rows):
        enc_rows, x_in, rms_in, hid_in, lat_in = encode_rows(
            raw_rows, cond_rows, gain, w_down, w_up
        )
        out_rows, qgrad_rows, grad_rows = attend(query_rows, cot_rows, enc_rows, len_rows, w_kv)
        nbr_grad, latgrad_rows = encode_back(grad_rows, x_in, rms_in, gain, w_down, w_up)
        span_grad = jnp.sum(nbr_grad.reshape(span_count, nbr_count, enc_width), axis=1)
        return (out_rows, qgrad_rows, span_grad, hid_in, latgrad_rows, grad_rows, lat_in)

    def local_skip(*unused):
        return (
            jnp.zeros((token_count, head_cols), jnp.bfloat16),
            jnp.zeros((token_count, head_cols), jnp.bfloat16),
            jnp.zeros((span_count, enc_width), jnp.float32),
            jnp.zeros((per_device, slot_len, enc_width), jnp.bfloat16),
            jnp.zeros((per_device, slot_len, rank_width), jnp.bfloat16),
            jnp.zeros((per_device, slot_len, enc_width), jnp.bfloat16),
            jnp.zeros((per_device, slot_len, rank_width), jnp.bfloat16),
        )

    attn_out, q_grad, my_cond, hid_used, lat_grad, enc_grad, lat_used = lax.cond(
        on_encoder, local_skip, local_run, query_flat, cot_flat, my_enc, my_len, cond_local
    )
    term_rows = per_device * slot_len
    flat_hidden = hid_used.reshape(term_rows, enc_width)
    flat_latgrad = lat_grad.reshape(term_rows, rank_width)
    flat_grads = enc_grad.reshape(term_rows, enc_width)
    flat_latent = lat_used.reshape(term_rows, rank_width)
    term_on = jnp.logical_not(on_encoder)

    def compute(unused):
        down_part = lax.dot_general(
            flat_hidden, flat_latgrad, (((0,), (0,)), ((), ())), preferred_element_type=jnp.float32
        )
        up_part = lax.dot_general(
            flat_grads, flat_latent, (((0,), (0,)), ((), ())), preferred_element_type=jnp.float32
        )
        return jnp.concatenate([down_part, up_part], axis=1)

    def nothing(unused):
        return jnp.zeros(
            (enc_width // (pool_count * columns) * lax.axis_size(("pool", "dp")), 2 * rank_width),
            jnp.float32,
        )

    adapter_grad = lax.psum_scatter(
        lax.cond(term_on, compute, nothing, 0), ("pool", "dp"), scatter_dimension=0, tiled=True
    )
    return (
        attn_out.reshape(1, 1, token_count, head_cols),
        q_grad.reshape(1, 1, token_count, head_cols),
        my_cond.reshape(1, 1, span_count, enc_width),
        adapter_grad,
    )


def solution(mesh):
    return jax.shard_map(
        body,
        mesh=mesh,
        in_specs=(
            P("pool", "dp", None, None),
            P("pool", "dp", None, None),
            P("pool", "dp", None, None),
            P("pool", "dp", None, None),
            P("pool", "dp", None, None),
            P("pool", "dp", None, None, None),
            P("pool", "dp", None),
            P(),
            P(),
            P(),
            P(),
        ),
        out_specs=(
            P("pool", "dp", None, None),
            P("pool", "dp", None, None),
            P("pool", "dp", None, None),
            P(("pool", "dp"), None),
        ),
        check_vma=False,
    )
```

profile of v0, /device:TPU:0, one launch (start us, length us, event | category | flops | bytes accessed | tf_op | source)
XLA Modules:
  0.0 441.8 jit_solution(9874154827118637415)
XLA Ops:
  7.2 0.9 copy.104
  8.2 5.9 %all-gather.1 = s32[4,1,8]{2,1,0:T(1,128)S(1)} all-gather(s32[1,1,8]{2,1,0:T(1,128)S(1)} %reshape.394), channel_id=1, replica_groups=mesh['pool'=4,'dp'=8] {'pool'}, dimensions={0}, use_global_device_ids=true | all-gather | bytes 160 | tf_op jit(solution)/shard_map/all_gather | solution.py:134
  14.1 0.8 copy.103
  15.1 5.3 %all-gather = s32[4,1,8]{2,1,0:T(1,128)S(1)} all-gather(s32[1,1,8]{2,1,0:T(1,128)S(1)} %reshape.392), channel_id=1, replica_groups=mesh['pool'=4,'dp'=8] {'pool'}, dimensions={0}, use_global_device_ids=true | all-gather | bytes 160 | tf_op jit(solution)/shard_map/all_gather | solution.py:133
  21.0 12.4 %all_to_all.23 = s32[8,1,4]{2,1,0:T(1,128)S(1)} all-to-all(s32[8,1,4]{2,1,0:T(1,128)S(1)} %bitcast.163), channel_id=1, replica_groups=mesh['pool'=4,'dp'=8] {'dp'}, dimensions={0} | all-to-all | bytes 256 | tf_op jit(solution)/shard_map/all_to_all | solution.py:147
  34.9 0.7 select_reduce_fusion.2
  36.3 3.3 all-to-all-start.2
  39.6 2.7 gather_fusion
  42.4 4.6 %broadcast_select_fusion = bf16[8,4,128,512]{3,2,1,0:T(8,128)(2,1)} fusion(bf16[8,4,128,512]{3,2,1,0:T(8,128)(2,1)} %bitcast.150, pred[8,4]{1,0:T(8,128)(4,1)S(1)} %copy.107), kind=kLoop, calls=%fused_computation.73 | loop fusion | flops 2097152 | bytes 8388640 | tf_op jit(solution)/shard_map/jit(_take)/select_n | solution.py:151
  47.0 5.9 %all-to-all-start.1 = ((bf16[8,4,128,512]{3,2,1,0:T(8,128)(2,1)}), bf16[8,4,128,512]{3,2,1,0:T(8,128)(2,1)}, u32[]{:S(2)}, u32[]{:S(2)}) async-start(bf16[8,4,128,512]{3,2,1,0:T(8,128)(2,1)} %broadcast_select_fusion), calls=%async_computation.1 | async-start | bytes 8388608 | tf_op jit(solution)/shard_map/all_to_all | solution.py:157
  53.9 0.7 gather_fusion.2
  54.7 90.3 %all-to-all-done.1 = bf16[8,4,128,512]{3,2,1,0:T(8,128)(2,1)} async-done(((bf16[8,4,128,512]{3,2,1,0:T(8,128)(2,1)}), bf16[8,4,128,512]{3,2,1,0:T(8,128)(2,1)}, u32[]{:S(2)}, u32[]{:S(2)}) %all-to-all-start.1) | async-done | bytes 4194336 | tf_op jit(solution)/shard_map/all_to_all | solution.py:157
  145.0 4.7 %gather_fusion.1 = bf16[24,128,512]{2,1,0:T(8,128)(2,1)} fusion(bf16[32,128,512]{2,1,0:T(8,128)(2,1)} %bitcast.21, s32[1024]{0:T(1024)S(1)} %pad_clamp_fusion), kind=kCustom, calls=%fused_computation.1 | custom fusion | bytes 6291552 | tf_op jit(solution)/shard_map/jit(_take)/gather | solution.py:160
  149.7 4.0 select_select_fusion
  153.8 4.9 %psum.15 = s32[3,8]{1,0:T(4,128)S(1)} all-reduce(s32[3,8]{1,0:T(4,128)S(1)} %get-tuple-element.173), channel_id=1, replica_groups=mesh['pool'=4,'dp'=8] {'pool'}, use_global_device_ids=true, to_apply=%region_5.6 | all-reduce | flops 24 | bytes 192 | tf_op jit(solution)/shard_map/psum | solution.py:17
  158.7 62.6 %all-reduce.2.cloned.1.call-done = bf16[3,8,128,512]{3,2,1,0:T(8,128)(2,1)} async-done(((bf16[3,8,128,512]{3,2,1,0:T(8,128)(2,1)}), bf16[3,8,128,512]{3,2,1,0:T(8,128)(2,1)}) %all-reduce.2.cloned.1.call-update) | async-done | bytes 3145744 | tf_op jit(solution)/shard_map/psum | solution.py:17
  221.4 73.1 %conditional.2 = (bf16[1,1,256,2048]{3,2,1,0:T(8,128)(2,1)}, bf16[1,1,256,2048]{3,2,1,0:T(8,128)(2,1)}, f32[1,1,4,512]{3,2,1,0:T(4,128)S(1)}, bf16[1024,512]{1,0...) conditional(s32[]{:T(128)} %convert_element_type.138, ...), branch_computations={%region_6.14_spmd, %region_14.15_spmd} | conditional | flops 11337201664 | bytes 347482880 | solution.py:194
  221.4 1.4 constant_dynamic-slice_fusion
  222.9 1.7 multiply_reduce_fusion.1
  224.6 1.6 multiply_convert_fusion.2
  227.1 5.3 %convolution_convert_fusion = bf16[1024,4096]{1,0:T(8,128)(2,1)S(1)} fusion(bf16[1024,512]{1,0:T(8,128)(2,1)S(1)} %add_convert_fusion, bf16[512,4096]{1,0:T(8,128)(2,1)S(1)} %copy-done.21), kind=kOutput, calls=%fused_computation.10 | convolution fusion | flops 4299161600 | bytes 13631488 | tf_op jit(solution)/shard_map/cond/branch_0_fun/dot_general | solution.py:55
  232.3 1.2 slice_bitcast_fusion.1
  233.5 3.3 copy.115
  236.9 1.4 copy.113
  238.6 3.6 fusion.17
  242.3 5.3 %fusion.54 = (f32[4,16,64]{2,1,0:T(8,128)S(1)}, f32[4,16,64,256]{3,2,1,0:T(8,128)S(1)}) fusion(f32[4,16,256,64]{2,3,1,0:T(8,128)} %fusion.17, pred[4,256]{1,0:T(4,128)(4,1)S(1)} %bitcast_compare_fusion), kind=kOutput, calls=%fused_computation.101 | output fusion | flops 6291711 | bytes 8406016 | tf_op jit(solution)/shard_map/cond/branch_0_fun/sub | solution.py:71
  247.7 1.7 fusion.34
  250.3 1.3 reshape.335
  251.6 1.4 copy.116
  253.1 6.0 %fusion.6 = (f32[4,16,64]{2,1,0:T(8,128)S(1)}, f32[4,16,256,64]{2,3,1,0:T(8,128)S(1)}) fusion(f32[4,16,64,256]{3,2,1,0:T(8,128)} %copy-done.10, f32[4,16,64]{2,1,0:T(8,128)S(1)} %get-tuple-element.179, bf16[4,64,16,128]{3,2,1,0:T(8,128)(2,1)S(1)} %bitcast.160, bf16[4,256,16,128]{3,2,1,0:T(8,128)(2,1)} %bitcast.156), kind=kOutput, calls=%fused_computation.18 | convolution fusion | flops 271577088 | bytes 13664256 | tf_op jit(solution)/shard_map/cond/branch_0_fun/cqhd,ckhd->chqk/dot_general | solution.py:79
  259.1 1.5 fusion.8
  261.3 1.4 fusion.37
  262.7 0.7 copy.97
  263.4 1.3 reshape.336
  264.7 4.5 %convert_bitcast_fusion = bf16[4,256,16,128]{3,1,2,0:T(8,128)(2,1)S(1)} fusion(bf16[4,64,16,128]{3,2,1,0:T(8,128)(2,1)} %bitcast.161, f32[4,16,64,256]{3,2,1,0:T(8,128)} %copy-done.10, f32[4,16,64]{2,1,0:T(8,128)S(1)} %get-tuple-element.179), kind=kOutput, calls=%fused_computation.25 | convolution fusion | flops 272629760 | bytes 9453568 | tf_op jit(solution)/shard_map/cond/branch_0_fun/chqk,cqhd->ckhd/dot_general | solution.py:96
  269.2 2.7 copy.101
  271.9 1.6 fusion.5
  273.6 2.7 copy.99
  276.3 4.7 %copy_bitcast_fusion = (bf16[1024,2048]{1,0:T(8,128)(2,1)S(1)}, bf16[1024,2048]{1,0:T(8,128)(2,1)S(1)}) fusion(bf16[128,8,16,128]{3,2,1,0:T(8,128)(2,1)S(1)} %bitcast.151, bf16[128,8,16,128]{3,2,1,0:T(8,128)(2,1)S(1)} %bitcast.152), kind=kLoop, calls=%fused_computation.12 | loop fusion | bytes 16777216 | tf_op jit(solution)/shard_map/cond/branch_0_fun/reshape | solution.py:102
  281.0 7.8 %fusion.28 = bf16[1024,512]{1,0:T(8,128)(2,1)} fusion(bf16[512,4096]{1,0:T(8,128)(2,1)} %get-tuple-element.168, bf16[1024,2048]{1,0:T(8,128)(2,1)S(1)} %get-tuple-element.185, bf16[1024,2048]{1,0:T(8,128)(2,1)S(1)} %get-tuple-element.186), kind=kOutput, calls=%fused_computation.49 | convolution fusion | flops 4312268800 | bytes 13631488 | tf_op jit(solution)/shard_map/cond/branch_0_fun/dot_general | solution.py:106
  288.8 1.7 convolution_convert_fusion.1
  290.5 0.8 copy-done.8
  292.0 2.1 fusion.21
  294.5 3.6 conditional.3
  294.5 2.0 fusion.56
  296.5 1.5 fusion.55
  298.1 1.3 copy.109
  299.5 135.3 %reduce-scatter.2.cloned.1.call-done = f32[16,512]{1,0:T(8,128)} async-done(((f32[512,512]{1,0:T(8,128)}), f32[16,512]{1,0:T(8,128)}) %reduce-scatter.2.cloned.1.call-update) | async-done | bytes 32784 | tf_op jit(solution)/shard_map/reduce_scatter | solution.py:219
  (96 shorter events, 8.0 us)
Async XLA Ops:
  7.2 32.5 %copy-start = (bf16[1,1,16,128,512]{4,3,2,1,0:T(8,128)(2,1)S(1)}, bf16[1,1,16,128,512]{4,3,2,1,0:T(8,128)(2,1)}, u32[]{:S(2)}) copy-start(bf16[1,1,16,128,512]{4,3,2,1,0:T(8,128)(2,1)} %param.20) | copy-start | bytes 6291460
  36.3 10.7 %all-to-all-start.2 = ((s32[8,1,4]{2,1,0:T(1,128)}), s32[8,1,4]{2,1,0:T(1,128)S(1)}, u32[]{:S(2)}, u32[]{:S(2)}) async-start(s32[8,1,4]{2,1,0:T(1,128)} %bitcast.26), calls=%async_computation.2 | async-start | bytes 8192 | tf_op jit(solution)/shard_map/all_to_all | solution.py:158
  47.0 98.0 %all-to-all-start.1 = ((bf16[8,4,128,512]{3,2,1,0:T(8,128)(2,1)}), bf16[8,4,128,512]{3,2,1,0:T(8,128)(2,1)}, u32[]{:S(2)}, u32[]{:S(2)}) async-start(bf16[8,4,128,512]{3,2,1,0:T(8,128)(2,1)} %broadcast_select_fusion), calls=%async_computation.1 | async-start | bytes 8388608 | tf_op jit(solution)/shard_map/all_to_all | solution.py:157
  52.9 168.4 %all-reduce.2.cloned.1.call-start = ((), (), s32[]{:S(2)}) async-start(), calls=%async_computation.4 | async-start | bytes 6291456 | tf_op jit(solution)/shard_map/psum | solution.py:17
  149.7 71.7 %copy-start.14 = (bf16[256,512]{1,0:T(8,128)(2,1)S(1)}, bf16[256,512]{1,0:T(8,128)(2,1)}, u32[]{:S(2)}) copy-start(bf16[256,512]{1,0:T(8,128)(2,1)} %param.24) | copy-start | bytes 786436
  149.7 71.7 %copy-start.15 = (bf16[512,256]{1,0:T(8,128)(2,1)S(1)}, bf16[512,256]{1,0:T(8,128)(2,1)}, u32[]{:S(2)}) copy-start(bf16[512,256]{1,0:T(8,128)(2,1)} %param.23) | copy-start | bytes 786436
  149.7 71.7 %copy-start.18 = (f32[512]{0:T(512)S(1)}, f32[512]{0:T(512)}, u32[]{:S(2)}) copy-start(f32[512]{0:T(512)} %param.22) | copy-start | bytes 6148
  149.7 71.7 %copy-start.20 = (bf16[1,1,4,512]{3,2,1,0:T(4,128)(2,1)S(1)}, bf16[1,1,4,512]{3,2,1,0:T(4,128)(2,1)}, u32[]{:S(2)}) copy-start(bf16[1,1,4,512]{3,2,1,0:T(4,128)(2,1)} %param.17) | copy-start | bytes 12292
  153.7 281.0 %reduce-scatter.2.cloned.1.call-start = ((), (), s32[]{:S(2)}) async-start(), calls=%async_computation.5 | async-start | bytes 1081344 | tf_op jit(solution)/shard_map/reduce_scatter | solution.py:219
  221.4 5.7 %copy-start.16 = (bf16[512,256]{1,0:T(8,128)(2,1)}, bf16[512,256]{1,0:T(8,128)(2,1)S(1)}, u32[]{:S(2)}) copy-start(bf16[512,256]{1,0:T(8,128)(2,1)S(1)} %get-tuple-element.166) | copy-start | bytes 786436 | tf_op jit(solution)/shard_map/cond
  222.9 4.2 copy-start.21
  226.6 5.7 %copy-start.7 = (bf16[1024,256]{1,0:T(8,128)(2,1)}, bf16[1024,256]{1,0:T(8,128)(2,1)S(1)}, u32[]{:S(2)}) copy-start(bf16[1024,256]{1,0:T(8,128)(2,1)S(1)} %convolution_convert_fusion.2) | copy-start | bytes 1572868 | tf_op jit(solution)/shard_map/cond
  236.9 1.4 copy-start.12
  238.3 3.8 copy-start.2
  242.3 5.4 %copy-start.9 = (bf16[128,8,16,128]{3,2,1,0:T(8,128)(2,1)S(1)}, bf16[128,8,16,128]{3,2,1,0:T(8,128)(2,1)}, u32[]{:S(2)}) copy-start(bf16[128,8,16,128]{3,2,1,0:T(8,128)(2,1)} %copy.115) | copy-start | bytes 12582916 | tf_op jit(solution)/shard_map/cond
  247.7 2.0 copy-start.10
  253.1 6.1 %copy-start.13 = (bf16[32,8,16,128]{3,2,1,0:T(8,128)(2,1)}, bf16[32,8,16,128]{3,2,1,0:T(8,128)(2,1)S(1)}, u32[]{:S(2)}) copy-start(bf16[32,8,16,128]{3,2,1,0:T(8,128)(2,1)S(1)} %copy.116) | copy-start | bytes 3145732 | tf_op jit(solution)/shard_map/cond
  253.1 6.0 %copy-start.11 = (f32[4,16,64,256]{3,2,1,0:T(8,128)S(1)}, f32[4,16,64,256]{3,2,1,0:T(8,128)}, u32[]{:S(2)}) copy-start(f32[4,16,64,256]{3,2,1,0:T(8,128)} %copy-done.10) | copy-start | bytes 12582916 | tf_op jit(solution)/shard_map/cond
  259.1 2.2 copy-start.3
  261.3 1.4 copy-start.5
  269.2 2.7 copy-start.6
  281.0 10.4 %copy-start.4 = (bf16[3,8,128,512]{3,2,1,0:T(8,128)(2,1)S(1)}, bf16[3,8,128,512]{3,2,1,0:T(8,128)(2,1)}, u32[]{:S(2)}) copy-start(bf16[3,8,128,512]{3,2,1,0:T(8,128)(2,1)} %get-tuple-element.125) | copy-start | bytes 9437188 | tf_op jit(solution)/shard_map/cond
  281.0 10.3 %copy-start.17 = (bf16[512,256]{1,0:T(8,128)(2,1)S(1)}, bf16[512,256]{1,0:T(8,128)(2,1)}, u32[]{:S(2)}) copy-start(bf16[512,256]{1,0:T(8,128)(2,1)} %copy-done.16) | copy-start | bytes 786436 | tf_op jit(solution)/shard_map/cond
  290.5 0.8 copy-start.8
  294.5 5.0 %copy-start.19 = (f32[1,1,4,512]{3,2,1,0:T(4,128)}, f32[1,1,4,512]{3,2,1,0:T(4,128)S(1)}, u32[]{:S(2)}) copy-start(f32[1,1,4,512]{3,2,1,0:T(4,128)S(1)} %get-tuple-element.148) | copy-start | bytes 24580
  294.5 140.3 %copy-start.1 = (bf16[1,1,16,128,512]{4,3,2,1,0:T(8,128)(2,1)S(1)}, bf16[1,1,16,128,512]{4,3,2,1,0:T(8,128)(2,1)}, u32[]{:S(2)}) copy-start(bf16[1,1,16,128,512]{4,3,2,1,0:T(8,128)(2,1)} %param.20) | copy-start | bytes 6291460
Sparse Core Ops, SparseCore 0:
  153.9 67.4 all-reduce.1
  299.6 135.0 reduce-scatter.1
where the time goes:
time: 446 us; the launch traced here: 442 us
  waiting for transfers between devices  288 us (65%)
  matrix products  38.6 us (9%)
  local copies, waits for them, and re-layouts  38.5 us (9%)
  blocking collectives  28.5 us (6%)
  other arithmetic  23.6 us (5%)
  between operations  14.4 us (3%)
  starting transfers between devices  9.31 us (2%)
    reduce_scatter x1, waiting for transfers between devices, body(): lax.psum_scatter(lax.cond(term_on, compute, nothing, 0), ('pool', 'dp'),...  135 us
    all_to_all x1, waiting for transfers between devices, body(): lax.all_to_all(block_rows, 'dp', split_axis=0, concat_axis=0, tiled=True)  90.3 us
    psum x1, waiting for transfers between devices, spread(): return lax.psum(block, axis)  62.6 us
    all_to_all x1, blocking collectives, body(): lax.all_to_all(slot_block, 'dp', split_axis=0, concat_axis=0, tiled=True)  12.4 us
    cond x36, local copies, waits for them, and re-layouts  9.46 us
  transfers between devices with their start and end apart: 4, of which 3 were waited for; matrix products, arithmetic and copies ran while one was open for 2% of the time, Pallas kernels for 0%

commit v1 on v0

v1 whole, which is shorter than its diff:
```python
import functools

import jax
import jax.numpy as jnp
from jax import lax
from jax.experimental import pallas as pl
from jax.experimental.pallas import tpu as pltpu
from jax.sharding import PartitionSpec as P

HEADS = 16
HEAD = 128
SPAN = 64

EPSILON = 1e-06
FLOOR = -1e30
LOG2E = 1.4426950408889634

NT = (((1,), (1,)), ((), ()))
TN = (((0,), (0,)), ((), ()))


def dot(a, b, dims=(((1,), (0,)), ((), ()))):
    return lax.dot_general(a, b, dims, preferred_element_type=jnp.float32)


def two_heads(rows):
    blank = jnp.zeros((rows.shape[0], HEAD), rows.dtype)
    return jnp.concatenate(
        [
            jnp.concatenate([rows[:, :HEAD], blank], axis=1),
            jnp.concatenate([blank, rows[:, HEAD:]], axis=1),
        ],
        axis=0,
    )


def span_kernel(
    raw_count, nbr_count, meta,
    q_ref, cot_ref, cond_ref, *rest,
):
    raw_refs = rest[:raw_count]
    (gain_ref, down_ref, up_ref, kv_ref, kvt_ref, upt_ref, downt_ref,
     out_ref, qg_ref, cg_ref, ad_ref, kvg_ref, acc_ref) = rest[raw_count:]
    span = pl.program_id(0)
    slot_len, width = raw_refs[0].shape[1:]
    key_count = nbr_count * slot_len
    head_cols = q_ref.shape[1]
    rank = down_ref.shape[1]
    scaling = HEAD ** (-0.5)
    pool_index = meta[0]
    live = pool_index < raw_count

    raw = raw_refs[raw_count - 1][...]
    for p in range(raw_count - 1):
        raw = jnp.where(pool_index == p, raw_refs[p][...], raw)
    x_full = raw.reshape(key_count, width).astype(jnp.float32) + cond_ref[
        pl.ds(span, 1), :
    ]
    inv_rms = lax.rsqrt(jnp.mean(x_full * x_full, axis=-1, keepdims=True) + EPSILON)
    gain = gain_ref[...]
    hidden = (x_full * inv_rms * gain).astype(jnp.bfloat16)
    latent = dot(hidden, down_ref[...]).astype(jnp.bfloat16)
    encoded = (x_full + dot(latent, up_ref[...])).astype(jnp.bfloat16)

    slot = lax.broadcasted_iota(jnp.int32, (key_count, 2 * SPAN), 0)
    limit = jnp.zeros((key_count, 2 * SPAN), jnp.int32)
    for n in range(nbr_count):
        here = jnp.logical_and(slot >= n * slot_len, slot < (n + 1) * slot_len)
        limit = jnp.where(here, n * slot_len + meta[1 + span * nbr_count + n], limit)
    usable = slot < limit

    for pair in range(HEADS // 2):
        cols = pl.ds(pair * 2 * HEAD, 2 * HEAD)
        vcols = pl.ds(head_cols + pair * 2 * HEAD, 2 * HEAD)
        keys = dot(encoded, kv_ref[:, cols]).astype(jnp.bfloat16)
        values = dot(encoded, kv_ref[:, vcols]).astype(jnp.bfloat16)
        q2 = two_heads(q_ref[:, cols])
        cot2 = two_heads(cot_ref[:, cols])
        scores = jnp.where(usable, dot(keys, q2, NT), FLOOR)
        row_max = jnp.max(scores, axis=0, keepdims=True)
        raised = jnp.exp2((scores - row_max) * (scaling * LOG2E))
        inv_sum = 1.0 / jnp.sum(raised, axis=0, keepdims=True)
        probs = raised * inv_sum
        probs_b = probs.astype(jnp.bfloat16)
        d_probs = dot(values, cot2, NT)
        delta = jnp.sum(probs * d_probs, axis=0, keepdims=True)
        d_scores = (probs * (d_probs - delta) * scaling).astype(jnp.bfloat16)
        kvg_ref[:, cols] = dot(d_scores, q2).astype(jnp.bfloat16)
        kvg_ref[:, vcols] = dot(probs_b, cot2).astype(jnp.bfloat16)
        probs_t = probs_b.T
        d_scores_t = d_scores.T
        outs, grads = [], []
        for h in range(2):
            lanes = slice(h * HEAD, (h + 1) * HEAD)
            tokens = slice(h * SPAN, (h + 1) * SPAN)
            outs.append(dot(probs_t[tokens], values[:, lanes]))
            grads.append(dot(d_scores_t[tokens], keys[:, lanes]))
        out_ref[:, cols] = jnp.where(live, jnp.concatenate(outs, axis=1), 0.0).astype(jnp.bfloat16)
        qg_ref[:, cols] = jnp.where(live, jnp.concatenate(grads, axis=1), 0.0).astype(jnp.bfloat16)

    enc_grad = dot(kvg_ref[...], kvt_ref[...]).astype(jnp.bfloat16)
    lat_grad = dot(enc_grad, upt_ref[...]).astype(jnp.bfloat16)
    scaled = dot(lat_grad, downt_ref[...]) * gain
    normed = x_full * inv_rms
    x_grad = enc_grad.astype(jnp.float32) + inv_rms * (
        scaled - normed * jnp.mean(scaled * normed, axis=-1, keepdims=True)
    )
    span_grad = jnp.sum(x_grad, axis=0, keepdims=True)
    cg_ref[pl.ds(span, 1), :] = jnp.where(live, span_grad, 0.0)

    @pl.when(span == 0)
    def _():
        acc_ref[...] = jnp.zeros_like(acc_ref)

    acc_ref[:, :rank] += dot(hidden, lat_grad, TN)
    acc_ref[:, rank:] += dot(enc_grad, latent, TN)

    @pl.when(span == pl.num_programs(0) - 1)
    def _():
        ad_ref[...] = jnp.where(live, acc_ref[...], 0.0).astype(ad_ref.dtype)


def run_spans(meta, query, cot, cond, raws, gain, w_down, w_up, w_kv, nbr_count):
    span_count, width = cond.shape
    token_count, head_cols = query.shape
    slot_len = raws[0].shape[1]
    rank = w_down.shape[1]
    whole = lambda a: pl.BlockSpec(a.shape, lambda s, m: (0,) * a.ndim, pipeline_mode=pl.Buffered(1))
    tokens = pl.BlockSpec((SPAN, head_cols), lambda s, m: (s, 0))
    weights = [gain.reshape(1, width), w_down, w_up, w_kv, w_kv.T, w_up.T, w_down.T]
    rows = span_count * nbr_count * slot_len
    flops = 2 * rows * (2 * width * 2 * head_cols + 6 * width * rank + 6 * SPAN * head_cols)
    return pl.pallas_call(
        functools.partial(span_kernel, len(raws), nbr_count),
        grid_spec=pltpu.PrefetchScalarGridSpec(
            num_scalar_prefetch=1,
            grid=(span_count,),
            in_specs=[tokens, tokens, whole(cond)]
            + [pl.BlockSpec((nbr_count, slot_len, width), lambda s, m: (s, 0, 0))] * len(raws)
            + [whole(w) for w in weights],
            out_specs=[
                tokens,
                tokens,
                pl.BlockSpec((span_count, width), lambda s, m: (0, 0)),
                pl.BlockSpec((width, 2 * rank), lambda s, m: (0, 0)),
            ],
            scratch_shapes=[
                pltpu.VMEM((nbr_count * slot_len, 2 * head_cols), jnp.bfloat16),
                pltpu.VMEM((width, 2 * rank), jnp.float32),
            ],
        ),
        out_shape=[
            jax.ShapeDtypeStruct((token_count, head_cols), jnp.bfloat16),
            jax.ShapeDtypeStruct((token_count, head_cols), jnp.bfloat16),
            jax.ShapeDtypeStruct((span_count, width), jnp.float32),
            jax.ShapeDtypeStruct((width, 2 * rank), jnp.bfloat16),
        ],
        compiler_params=pltpu.CompilerParams(vmem_limit_bytes=48 * 2**20),
        cost_estimate=pl.CostEstimate(
            flops=flops, bytes_accessed=16 * 2**20, transcendentals=rows * SPAN * HEADS
        ),
    )(meta, query, cot, cond, *raws, *weights)


def body(
    queries, cotangent, cond, nbr_owner, nbr_block, database, lengths, gain, w_down, w_up, w_kv
):
    axes = ("pool", "dp")
    pool_count = lax.axis_size("pool")
    columns = lax.axis_size("dp")
    relay_row = pool_count - 1
    pool_index = lax.axis_index("pool")
    me = lax.axis_index("dp")
    span_count, width = cond.shape[2:]
    nbr_count = nbr_owner.shape[3]
    per_device = span_count * nbr_count
    block_count, slot_len = database.shape[2:4]
    live_count = relay_row * per_device
    capacity = max(2, live_count // columns + 1)
    slot_count = columns * capacity
    token_count, head_cols = queries.shape[2:]

    def at(pool, dp):
        return pool * columns + dp % columns

    info = jnp.concatenate([nbr_owner.reshape(-1), nbr_block.reshape(-1), lengths.reshape(-1)])
    table = lax.all_gather(info, axes, axis=0).reshape(pool_count, columns, -1)
    by_column = jnp.swapaxes(table[:relay_row], 0, 1)
    owners = by_column[:, :, :per_device].reshape(columns, live_count)
    blocks = by_column[:, :, per_device : 2 * per_device].reshape(columns, live_count)
    store_len = table[relay_row, :, 2 * per_device :]
    order = jnp.arange(live_count, dtype=jnp.int32)
    same = owners[:, :, None] == owners[:, None, :]
    rank = jnp.sum(jnp.where(same & (order[None, :] < order[:, None])[None], 1, 0), axis=2)

    target = (me + jnp.arange(columns, dtype=jnp.int32)) % columns
    ring = jnp.arange(capacity, dtype=jnp.int32)
    mine = (owners == me)[:, None, :] & (rank[:, None, :] == ring[None, :, None])
    slot_block = jnp.sum(jnp.where(mine, blocks[:, None, :], 0), axis=2)
    slot_block = jnp.take(slot_block, target, axis=0).reshape(slot_count)
    store = database.reshape(block_count, slot_len, width)
    sends = jnp.take(store, slot_block, axis=0).reshape(columns, capacity, slot_len, width)

    arrived = [sends[0]]
    for shift in range(1, columns):
        hops = [(at(relay_row, j), at(relay_row, j + shift)) for j in range(columns)]
        arrived.append(lax.ppermute(sends[shift], axes, hops))
    arrived = jnp.concatenate(arrived, axis=0)

    my_owner = lax.dynamic_index_in_dim(owners, me, 0, keepdims=False)
    my_block = lax.dynamic_index_in_dim(blocks, me, 0, keepdims=False)
    my_rank = lax.dynamic_index_in_dim(rank, me, 0, keepdims=False)
    position = ((me - my_owner) % columns) * capacity + my_rank
    wanted = jnp.take(arrived, position, axis=0).reshape(relay_row, per_device, slot_len, width)
    raws = [
        lax.ppermute(
            wanted[p], axes, [(at(relay_row, j), at(p, j)) for j in range(columns)]
        )
        for p in range(relay_row)
    ]

    own_row = jnp.minimum(pool_index, relay_row - 1)
    pick = my_owner * block_count + my_block
    hot = pick[:, None] == jnp.arange(columns * block_count, dtype=jnp.int32)[None, :]
    wanted_len = jnp.sum(jnp.where(hot, store_len.reshape(1, -1), 0), axis=1)
    my_len = lax.dynamic_index_in_dim(
        wanted_len.reshape(relay_row, per_device), own_row, 0, keepdims=False
    )
    meta = jnp.concatenate([pool_index[None], my_len]).astype(jnp.int32)

    attn_out, q_grad, cond_grad, terms = run_spans(
        meta,
        queries.reshape(token_count, head_cols),
        cotangent.reshape(token_count, head_cols),
        cond.reshape(span_count, width).astype(jnp.float32),
        raws,
        gain,
        w_down,
        w_up,
        w_kv,
        nbr_count,
    )
    parts = lax.all_to_all(terms, axes, split_axis=0, concat_axis=0, tiled=True)
    adapter_grad = jnp.sum(
        parts.reshape(pool_count * columns, -1, terms.shape[1]).astype(jnp.float32), axis=0
    )
    return (
        attn_out.reshape(1, 1, token_count, head_cols),
        q_grad.reshape(1, 1, token_count, head_cols),
        cond_grad.reshape(1, 1, span_count, width),
        adapter_grad,
    )


def solution(mesh):
    return jax.shard_map(
        body,
        mesh=mesh,
        in_specs=(
            P("pool", "dp", None, None),
            P("pool", "dp", None, None),
            P("pool", "dp", None, None),
            P("pool", "dp", None, None),
            P("pool", "dp", None, None),
            P("pool", "dp", None, None, None),
            P("pool", "dp", None),
            P(),
            P(),
            P(),
            P(),
        ),
        out_specs=(
            P("pool", "dp", None, None),
            P("pool", "dp", None, None),
            P("pool", "dp", None, None),
            P(("pool", "dp"), None),
        ),
        check_vma=False,
    )
```

time: 446 us -> 204 us (0.46)
  waiting for transfers between devices: 288 us -> 25.2 us
  blocking collectives: 28.5 us -> 86.4 us
  matrix products: 38.6 us -> 0 us
  Pallas kernels: 0 us -> 35.7 us
  other arithmetic: 23.6 us -> 7.31 us
  between operations: 14.4 us -> 0.85 us
    reduce_scatter x1 -> x0, waiting for transfers between devices: 135 us -> none  [body(): lax.psum_scatter(lax.cond(term_on, compute, nothing, 0), ('pool', 'dp'),...]
    all_to_all x2 -> x0, waiting for transfers between devices: 90.3 us -> none  [the longest x1 90.3 us: body(): lax.all_to_all(block_rows, 'dp', split_axis=0, concat_axis=0, tiled=True)]
    psum x1 -> x0, waiting for transfers between devices: 62.6 us -> none  [spread(): return lax.psum(block, axis)]
    unnamed x0 -> x1, blocking collectives: none -> 42 us
    dot_general x14 -> x0, matrix products: 38.6 us -> none  [the longest x1 7.85 us: attend(): lax.dot_general(kv_grad, w_kv, (((1,), (1,)), ((), ())), preferred_elemen...]
    pallas_call x0 -> x1, Pallas kernels: none -> 35.7 us  [run_spans(): pl.pallas_call(functools.partial(span_kernel, len(raws), nbr_count), grid...]
    all_to_all x1, blocking collectives: 12.4 us -> 44.5 us  [body(): parts = lax.all_to_all(terms, axes, split_axis=0, concat_axis=0, tiled=True)]
    ppermute x0 -> x10, waiting for transfers between devices: none -> 25.2 us  [the longest x3 25.2 us: body(): lax.ppermute(wanted[p], axes, [(at(relay_row, j), at(p, j)) for j in rang...]
  transfers between devices with their start and end apart: 4 -> 10, of which waited for: 3 -> 1; matrix products, arithmetic and copies ran while one was open for 2% -> 9% of each run, Pallas kernels for 0% -> 0%
where the time goes in v1:
time: 204 us; the launch traced here: 203 us
  blocking collectives  86.4 us (42%)
  Pallas kernels  35.7 us (18%)
  local copies, waits for them, and re-layouts  34.5 us (17%)
  waiting for transfers between devices  25.2 us (12%)
  starting transfers between devices  13.3 us (7%)
  other arithmetic  7.31 us (4%)
    all_to_all x1, blocking collectives, body(): parts = lax.all_to_all(terms, axes, split_axis=0, concat_axis=0, tiled=True)  44.5 us
    unnamed x1, blocking collectives  42 us
    pallas_call x1, Pallas kernels, run_spans(): pl.pallas_call(functools.partial(span_kernel, len(raws), nbr_count), grid...  35.7 us
    ppermute x3, waiting for transfers between devices, body(): lax.ppermute(wanted[p], axes, [(at(relay_row, j), at(p, j)) for j in rang...  25.2 us
    unnamed x26, local copies, waits for them, and re-layouts  21.2 us
    ppermute x7, starting transfers between devices, body(): arrived.append(lax.ppermute(sends[shift], axes, hops))  8.71 us
    gather x1, local copies, waits for them, and re-layouts, body(): jnp.take(arrived, position, axis=0)  4.71 us
    ppermute x3, starting transfers between devices, body(): lax.ppermute(wanted[p], axes, [(at(relay_row, j), at(p, j)) for j in rang...  4.62 us
  transfers between devices with their start and end apart: 10, of which 1 were waited for; matrix products, arithmetic and copies ran while one was open for 9% of the time, Pallas kernels for 0%

profile of v1, /device:TPU:0, one launch (start us, length us, event | category | flops | bytes accessed | tf_op | source)
XLA Modules:
  0.0 203.4 jit_solution(8582247105116169371)
XLA Ops:
  0.7 0.9 copy.27
  1.6 0.1 reshape.289
  1.7 0.8 copy.28
  2.5 0.1 reshape.290
  2.6 0.8 add_dynamic-update-slice_fusion
  3.4 42.0 %all-reduce = s32[1024]{0:T(1024)S(1)} all-reduce(s32[1024]{0:T(1024)S(1)} %add_dynamic-update-slice_fusion), channel_id=2, replica_groups=mesh['pool'=4,'dp'=8] {'pool','dp'}, use_global_device_ids=true, to_apply=%add | all-reduce | flops 1024 | bytes 8192
  45.5 0.1 reshape.292
  45.6 0.3 select_reduce_fusion
  45.9 0.1 reshape.293
  46.0 0.1 select_reduce_fusion.1
  46.1 0.1 copy.31
  46.2 0.6 gather_fusion
  46.9 0.1 select_n.147
  47.1 2.8 %gather_fusion.1 = bf16[32,128,512]{2,1,0:T(8,128)(2,1)} fusion(bf16[16,128,512]{2,1,0:T(8,128)(2,1)S(1)} %bitcast.44, s32[1024]{0:T(1024)S(1)} %pad_clamp_fusion.1), kind=kCustom, calls=%fused_computation.1 | custom fusion | bytes 8388736 | tf_op jit(solution)/shard_map/jit(_take)/gather | solution.py:202
  49.8 2.6 %broadcast_select_fusion = bf16[32,128,512]{2,1,0:T(8,128)(2,1)S(1)} fusion(bf16[32,128,512]{2,1,0:T(8,128)(2,1)} %gather_fusion.1, pred[32]{0:T(512)(128)(4,1)S(1)} %compare_and_fusion), kind=kLoop, calls=%fused_computation.3 | loop fusion | flops 2097152 | bytes 8388640 | tf_op jit(solution)/shard_map/jit(_take)/select_n | solution.py:202
  52.5 1.7 fusion.15
  54.2 1.5 collective-permute-start
  55.7 1.5 collective-permute-start.1
  57.2 1.5 collective-permute-start.2
  58.6 1.5 collective-permute-start.3
  60.1 1.5 collective-permute-start.4
  61.6 0.7 collective-permute-start.5
  62.3 1.9 constant_dynamic-update-slice_fusion.6
  64.2 0.7 collective-permute-start.6
  64.9 1.9 constant_dynamic-update-slice_fusion.5
  66.7 1.9 constant_dynamic-update-slice_fusion.4
  68.6 1.9 constant_dynamic-update-slice_fusion.3
  70.5 1.9 constant_dynamic-update-slice_fusion.2
  72.4 0.8 constant_dynamic-update-slice_fusion.1
  73.2 0.8 constant_dynamic-update-slice_fusion
  74.1 4.7 %gather_fusion.2 = bf16[24,128,512]{2,1,0:T(8,128)(2,1)} fusion(bf16[32,128,512]{2,1,0:T(8,128)(2,1)} %constant_dynamic-update-slice_fusion, s32[1024]{0:T(1024)S(1)} %pad_clamp_fusion), kind=kCustom, calls=%fused_computation.2 | custom fusion | bytes 6291552 | tf_op jit(solution)/shard_map/jit(_take)/gather | solution.py:214
  78.8 2.2 %broadcast_select_fusion.1 = bf16[24,128,512]{2,1,0:T(8,128)(2,1)S(1)} fusion(bf16[24,128,512]{2,1,0:T(8,128)(2,1)} %gather_fusion.2, pred[24]{0:T(512)(128)(4,1)S(1)} %compare_and_fusion.2), kind=kLoop, calls=%fused_computation.4 | loop fusion | flops 1572864 | bytes 6291480 | tf_op jit(solution)/shard_map/jit(_take)/select_n | solution.py:214
  81.0 1.7 fusion.16
  82.8 1.3 collective-permute-start.7
  84.0 1.7 collective-permute-start.8
  85.7 1.7 collective-permute-start.9
  87.5 0.1 broadcast_in_dim.76
  87.6 0.2 select_reduce_fusion.2
  87.8 0.1 reshape.295
  87.9 6.5 %copy.32 = bf16[512,4096]{0,1:T(8,128)(2,1)} copy(bf16[512,4096]{1,0:T(8,128)(2,1)} %rest_6_.1) | data formatting | bytes 8388608 | tf_op args[10]
  94.4 0.1 copy.33
  94.6 0.1 copy.34
  94.8 25.2 %collective-permute-done.7.rest_0_ = bf16[8,128,512]{2,1,0:T(8,128)(2,1)} collective-permute-done((bf16[8,128,512]{2,1,0:T(8,128)(2,1)}, bf16[8,128,512]{2,1,0:T(8,128)(2,1)}, u32[]{:S(2)}, u32[]{:S(2)}) %collective-permute-start.7) | collective-permute-done | bytes 1048608 | tf_op jit(solution)/shard_map/ppermute | solution.py:216
  120.0 1.2 copy-done.3
  121.2 1.2 copy-done.4
  122.5 35.7 %shard_map.138 = (bf16[256,2048]{1,0:T(8,128)(2,1)}, bf16[256,2048]{1,0:T(8,128)(2,1)}, f32[4,512]{1,0:T(4,128)}, bf16[512,512]{1,0:T(8,128)(2,1)S(1)}) custom-call(s32[9]{0:T(128)S(1)} %pad_add_fusion.meta, bf16[256,2048]{1,0:T(8,128)(2,1)S(1)} %bitcast.48, bf16[256,2048]{1,0:T(8,128)(2,1)S(1)} %bitcast.49, f32[4,512]{1,0:T(4,128)S(1)} %bitcast_convert_fusion.cond_ref, ...), custom_call_target="tpu_custom_call" | custom-call | flops 11811160064 | bytes 16777216 | tf_op jit(solution)/shard_map/pallas_call | solution.py:133
  158.2 44.5 %all_to_all.9 = bf16[32,16,512]{2,1,0:T(8,128)(2,1)S(1)} all-to-all(bf16[32,16,512]{2,1,0:T(8,128)(2,1)S(1)} %bitcast.45), channel_id=1, replica_groups=mesh['pool'=4,'dp'=8] {'pool','dp'}, dimensions={0} | all-to-all | bytes 1048576 | tf_op jit(solution)/shard_map/all_to_all | solution.py:243
  202.7 0.7 convert_reduce_fusion
  (45 shorter events, 0.7 us)
Async XLA Ops:
  0.6 46.4 %copy-start = (bf16[1,1,16,128,512]{4,3,2,1,0:T(8,128)(2,1)S(1)}, bf16[1,1,16,128,512]{4,3,2,1,0:T(8,128)(2,1)}, u32[]{:S(2)}) copy-start(bf16[1,1,16,128,512]{4,3,2,1,0:T(8,128)(2,1)} %param.16) | copy-start | bytes 6291460
  54.2 7.4 %collective-permute-start = (bf16[4,128,512]{2,1,0:T(8,128)(2,1)}, bf16[4,128,512]{2,1,0:T(8,128)(2,1)}, u32[]{:S(2)}, u32[]{:S(2)}) collective-permute-start(bf16[4,128,512]{2,1,0:T(8,128)(2,1)} %get-tuple-element.18), channel_id=1, source_target_pairs={{24,25},{25,26},{26,27},{27,28},{28,29},{29,30},{30,31},{31,24}} | collective-permute-start | bytes 1572872 | tf_op jit(solution)/shard_map/ppermute | solution.py:207
  55.7 8.5 %collective-permute-start.1 = (bf16[4,128,512]{2,1,0:T(8,128)(2,1)}, bf16[4,128,512]{2,1,0:T(8,128)(2,1)}, u32[]{:S(2)}, u32[]{:S(2)}) collective-permute-start(bf16[4,128,512]{2,1,0:T(8,128)(2,1)} %get-tuple-element.17), channel_id=1, source_target_pairs={{24,26},{25,27},{26,28},{27,29},{28,30},{29,31},{30,24},{31,25}} | collective-permute-start | bytes 1572872 | tf_op jit(solution)/shard_map/ppermute | solution.py:207
  57.2 9.6 %collective-permute-start.2 = (bf16[4,128,512]{2,1,0:T(8,128)(2,1)}, bf16[4,128,512]{2,1,0:T(8,128)(2,1)}, u32[]{:S(2)}, u32[]{:S(2)}) collective-permute-start(bf16[4,128,512]{2,1,0:T(8,128)(2,1)} %get-tuple-element.16), channel_id=1, source_target_pairs={{24,27},{25,28},{26,29},{27,30},{28,31},{29,24},{30,25},{31,26}} | collective-permute-start | bytes 1572872 | tf_op jit(solution)/shard_map/ppermute | solution.py:207
  58.6 10.0 %collective-permute-start.3 = (bf16[4,128,512]{2,1,0:T(8,128)(2,1)}, bf16[4,128,512]{2,1,0:T(8,128)(2,1)}, u32[]{:S(2)}, u32[]{:S(2)}) collective-permute-start(bf16[4,128,512]{2,1,0:T(8,128)(2,1)} %get-tuple-element.15), channel_id=1, source_target_pairs={{24,28},{25,29},{26,30},{27,31},{28,24},{29,25},{30,26},{31,27}} | collective-permute-start | bytes 1572872 | tf_op jit(solution)/shard_map/ppermute | solution.py:207
  60.1 10.4 %collective-permute-start.4 = (bf16[4,128,512]{2,1,0:T(8,128)(2,1)}, bf16[4,128,512]{2,1,0:T(8,128)(2,1)}, u32[]{:S(2)}, u32[]{:S(2)}) collective-permute-start(bf16[4,128,512]{2,1,0:T(8,128)(2,1)} %get-tuple-element.14), channel_id=1, source_target_pairs={{24,29},{25,30},{26,31},{27,24},{28,25},{29,26},{30,27},{31,28}} | collective-permute-start | bytes 1572872 | tf_op jit(solution)/shard_map/ppermute | solution.py:207
  61.6 10.8 %collective-permute-start.5 = (bf16[4,128,512]{2,1,0:T(8,128)(2,1)S(1)}, bf16[4,128,512]{2,1,0:T(8,128)(2,1)S(1)}, u32[]{:S(2)}, u32[]{:S(2)}) collective-permute-start(bf16[4,128,512]{2,1,0:T(8,128)(2,1)S(1)} %get-tuple-element.13), channel_id=1, source_target_pairs={{24,30},{25,31},{26,24},{27,25},{28,26},{29,27},{30,28},{31,29}} | collective-permute-start | bytes 1572872 | tf_op jit(solution)/shard_map/ppermute | solution.py:207
  64.2 9.1 %collective-permute-start.6 = (bf16[4,128,512]{2,1,0:T(8,128)(2,1)S(1)}, bf16[4,128,512]{2,1,0:T(8,128)(2,1)S(1)}, u32[]{:S(2)}, u32[]{:S(2)}) collective-permute-start(bf16[4,128,512]{2,1,0:T(8,128)(2,1)S(1)} %get-tuple-element.12), channel_id=1, source_target_pairs={{24,31},{25,24},{26,25},{27,26},{28,27},{29,28},{30,29},{31,30}} | collective-permute-start | bytes 1572872 | tf_op jit(solution)/shard_map/ppermute | solution.py:207
  82.8 37.2 %collective-permute-start.7 = (bf16[8,128,512]{2,1,0:T(8,128)(2,1)}, bf16[8,128,512]{2,1,0:T(8,128)(2,1)}, u32[]{:S(2)}, u32[]{:S(2)}) collective-permute-start(bf16[8,128,512]{2,1,0:T(8,128)(2,1)} %get-tuple-element.22), channel_id=1, source_target_pairs={{24,0},{25,1},{26,2},{27,3},{28,4},{29,5},{30,6},{31,7}} | collective-permute-start | bytes 3145736 | tf_op jit(solution)/shard_map/ppermute | solution.py:216
  84.0 35.9 %collective-permute-start.8 = (bf16[8,128,512]{2,1,0:T(8,128)(2,1)}, bf16[8,128,512]{2,1,0:T(8,128)(2,1)}, u32[]{:S(2)}, u32[]{:S(2)}) collective-permute-start(bf16[8,128,512]{2,1,0:T(8,128)(2,1)} %get-tuple-element.21), channel_id=1, source_target_pairs={{24,8},{25,9},{26,10},{27,11},{28,12},{29,13},{30,14},{31,15}} | collective-permute-start | bytes 3145736 | tf_op jit(solution)/shard_map/ppermute | solution.py:216
  85.7 34.3 %collective-permute-start.9 = (bf16[8,128,512]{2,1,0:T(8,128)(2,1)}, bf16[8,128,512]{2,1,0:T(8,128)(2,1)}, u32[]{:S(2)}, u32[]{:S(2)}) collective-permute-start(bf16[8,128,512]{2,1,0:T(8,128)(2,1)} %get-tuple-element.20), channel_id=1, source_target_pairs={{24,16},{25,17},{26,18},{27,19},{28,20},{29,21},{30,22},{31,23}} | collective-permute-start | bytes 3145736 | tf_op jit(solution)/shard_map/ppermute | solution.py:216
  87.9 6.5 %copy-start.2 = (bf16[256,512]{1,0:T(8,128)(2,1)S(1)}, bf16[256,512]{1,0:T(8,128)(2,1)}, u32[]{:S(2)}) copy-start(bf16[256,512]{1,0:T(8,128)(2,1)} %rest_5_.1) | copy-start | bytes 786436
  87.9 6.7 %copy-start.1 = (bf16[512,256]{1,0:T(8,128)(2,1)S(1)}, bf16[512,256]{1,0:T(8,128)(2,1)}, u32[]{:S(2)}) copy-start(bf16[512,256]{1,0:T(8,128)(2,1)} %rest_4_.1) | copy-start | bytes 786436
  87.9 6.9 %copy-start.6 = (bf16[1,1,4,512]{3,2,1,0:T(4,128)(2,1)S(1)}, bf16[1,1,4,512]{3,2,1,0:T(4,128)(2,1)}, u32[]{:S(2)}) copy-start(bf16[1,1,4,512]{3,2,1,0:T(4,128)(2,1)} %param.13) | copy-start | bytes 12292
  87.9 32.1 %copy-start.5 = (f32[512]{0:T(512)S(1)}, f32[512]{0:T(512)}, u32[]{:S(2)}) copy-start(f32[512]{0:T(512)} %param.18) | copy-start | bytes 6148
  120.0 1.2 copy-start.3
  121.2 1.2 copy-start.4

commit v2 on v1

--- a/solution.py
+++ b/solution.py
@@ -35,24 +35,35 @@
 
 
 def span_kernel(
-    raw_count, nbr_count, meta,
+    held_count, nbr_count, meta,
     q_ref, cot_ref, cond_ref, *rest,
 ):
-    raw_refs = rest[:raw_count]
+    held_refs = rest[:held_count]
     (gain_ref, down_ref, up_ref, kv_ref, kvt_ref, upt_ref, downt_ref,
-     out_ref, qg_ref, cg_ref, ad_ref, kvg_ref, acc_ref) = rest[raw_count:]
+     out_ref, qg_ref, cg_ref, ad_ref, kvg_ref, acc_ref, raw_ref, sems) = rest[held_count:]
     span = pl.program_id(0)
-    slot_len, width = raw_refs[0].shape[1:]
+    per_device, slot_len, width = raw_ref.shape
     key_count = nbr_count * slot_len
     head_cols = q_ref.shape[1]
     rank = down_ref.shape[1]
     scaling = HEAD ** (-0.5)
-    pool_index = meta[0]
-    live = pool_index < raw_count
-
-    raw = raw_refs[raw_count - 1][...]
-    for p in range(raw_count - 1):
-        raw = jnp.where(pool_index == p, raw_refs[p][...], raw)
+    live = meta[0] == 1
+    lens, which, index = 1, 1 + per_device, 1 + 2 * per_device
+
+    @pl.when(span == 0)
+    def _():
+        for n in range(per_device):
+            for b, held in enumerate(held_refs):
+                @pl.when(meta[which + n] == b)
+                def _():
+                    pltpu.make_async_copy(
+                        held.at[meta[index + n]], raw_ref.at[n], sems.at[n]
+                    ).start()
+
+    for n in range(nbr_count):
+        item = span * nbr_count + n
+        pltpu.make_async_copy(held_refs[0].at[0], raw_ref.at[item], sems.at[item]).wait()
+    raw = raw_ref[pl.ds(span * nbr_count, nbr_count)]
     x_full = raw.reshape(key_count, width).astype(jnp.float32) + cond_ref[
         pl.ds(span, 1), :
     ]
@@ -66,7 +77,7 @@
     limit = jnp.zeros((key_count, 2 * SPAN), jnp.int32)
     for n in range(nbr_count):
         here = jnp.logical_and(slot >= n * slot_len, slot < (n + 1) * slot_len)
-        limit = jnp.where(here, n * slot_len + meta[1 + span * nbr_count + n], limit)
+        limit = jnp.where(here, n * slot_len + meta[lens + span * nbr_count + n], limit)
     usable = slot < limit
 
     for pair in range(HEADS // 2):
@@ -120,23 +131,24 @@
         ad_ref[...] = jnp.where(live, acc_ref[...], 0.0).astype(ad_ref.dtype)
 
 
-def run_spans(meta, query, cot, cond, raws, gain, w_down, w_up, w_kv, nbr_count):
+def run_spans(meta, query, cot, cond, held, gain, w_down, w_up, w_kv, nbr_count):
     span_count, width = cond.shape
     token_count, head_cols = query.shape
-    slot_len = raws[0].shape[1]
+    slot_len = held[0].shape[1]
     rank = w_down.shape[1]
     whole = lambda a: pl.BlockSpec(a.shape, lambda s, m: (0,) * a.ndim, pipeline_mode=pl.Buffered(1))
     tokens = pl.BlockSpec((SPAN, head_cols), lambda s, m: (s, 0))
     weights = [gain.reshape(1, width), w_down, w_up, w_kv, w_kv.T, w_up.T, w_down.T]
-    rows = span_count * nbr_count * slot_len
+    per_device = span_count * nbr_count
+    rows = per_device * slot_len
     flops = 2 * rows * (2 * width * 2 * head_cols + 6 * width * rank + 6 * SPAN * head_cols)
     return pl.pallas_call(
-        functools.partial(span_kernel, len(raws), nbr_count),
+        functools.partial(span_kernel, len(held), nbr_count),
         grid_spec=pltpu.PrefetchScalarGridSpec(
             num_scalar_prefetch=1,
             grid=(span_count,),
             in_specs=[tokens, tokens, whole(cond)]
-            + [pl.BlockSpec((nbr_count, slot_len, width), lambda s, m: (s, 0, 0))] * len(raws)
+            + [pl.BlockSpec(memory_space=pl.ANY)] * len(held)
             + [whole(w) for w in weights],
             out_specs=[
                 tokens,
@@ -147,6 +159,8 @@
             scratch_shapes=[
                 pltpu.VMEM((nbr_count * slot_len, 2 * head_cols), jnp.bfloat16),
                 pltpu.VMEM((width, 2 * rank), jnp.float32),
+                pltpu.VMEM((per_device, slot_len, width), jnp.bfloat16),
+                pltpu.SemaphoreType.DMA((per_device,)),
             ],
         ),
         out_shape=[
@@ -159,7 +173,55 @@
         cost_estimate=pl.CostEstimate(
             flops=flops, bytes_accessed=16 * 2**20, transcendentals=rows * SPAN * HEADS
         ),
-    )(meta, query, cot, cond, *raws, *weights)
+    )(meta, query, cot, cond, *held, *weights)
+
+
+def pick_kernel(held_count, meta, *refs):
+    held_refs, out_ref, sems = refs[:held_count], refs[held_count], refs[held_count + 1]
+    for b, held in enumerate(held_refs):
+        @pl.when(meta[0] == b)
+        def _():
+            for n in range(out_ref.shape[0]):
+                pltpu.make_async_copy(held.at[meta[1 + n]], out_ref.at[n], sems.at[n]).start()
+    for n in range(out_ref.shape[0]):
+        pltpu.make_async_copy(held_refs[0].at[0], out_ref.at[n], sems.at[n]).wait()
+
+
+def pick(which, index, held):
+    count = index.shape[0]
+    meta = jnp.concatenate([jnp.reshape(which, (1,)), index]).astype(jnp.int32)
+    return pl.pallas_call(
+        functools.partial(pick_kernel, len(held)),
+        grid_spec=pltpu.PrefetchScalarGridSpec(
+            num_scalar_prefetch=1,
+            grid=(1,),
+            in_specs=[pl.BlockSpec(memory_space=pl.ANY)] * len(held),
+            out_specs=pl.BlockSpec(memory_space=pl.ANY),
+            scratch_shapes=[pltpu.SemaphoreType.DMA((count,))],
+        ),
+        out_shape=jax.ShapeDtypeStruct((count,) + held[0].shape[1:], held[0].dtype),
+    )(meta, *held)
+
+
+def place_requests(owners, per_device, pool_count, lanes):
+    half = pool_count // 2
+    count = owners.shape[1]
+    order = jnp.arange(count, dtype=jnp.int32)
+    side = (order // per_device) // half
+    mate = side[:, None] == side[None, :]
+    before = order[None, :] < order[:, None]
+    same = owners[:, :, None] == owners[:, None, :]
+    lower = owners[:, None, :] < owners[:, :, None]
+    total = lambda mask: jnp.sum(mask.astype(jnp.int32), axis=2)
+    rank = total(same & (mate & before)[None])
+    crosses = rank >= lanes
+    far = crosses[:, None, :]
+    number = total(far & mate[None] & (lower | (same & before[None])))
+    first = total(far & ~mate[None] & lower)
+    guests = total(far & ~mate[None] & same)
+    lane = jnp.where(crosses, number, first + guests + rank) % lanes
+    row = jnp.where(crosses, 1 - side[None, :], side[None, :]) * half + lane % half
+    return row, lane // half, crosses, number // half
 
 
 def body(
@@ -169,7 +231,8 @@
     pool_count = lax.axis_size("pool")
     columns = lax.axis_size("dp")
     relay_row = pool_count - 1
-    pool_index = lax.axis_index("pool")
+    half = pool_count // 2
+    row = lax.axis_index("pool")
     me = lax.axis_index("dp")
     span_count, width = cond.shape[2:]
     nbr_count = nbr_owner.shape[3]
@@ -177,73 +240,99 @@
     block_count, slot_len = database.shape[2:4]
     live_count = relay_row * per_device
     capacity = max(2, live_count // columns + 1)
-    slot_count = columns * capacity
+    slots = -(-capacity // pool_count)
+    lanes = half * slots
+    most = 0
+    if capacity > lanes:
+        for rows in (half, relay_row - half):
+            full, left = divmod(rows * per_device, capacity)
+            most = max(most, full * (capacity - lanes) + max(0, left - lanes))
+    crossing = -(-most // half)
     token_count, head_cols = queries.shape[2:]
 
-    def at(pool, dp):
-        return pool * columns + dp % columns
+    def hop(array, pairs):
+        return lax.ppermute(
+            array, axes, [(a * columns + j, b * columns + j) for a, b in pairs for j in range(columns)]
+        )
+
+    store = database.reshape(block_count, slot_len, width)
+    across = hop(store, [(relay_row, relay_row - half)])
+    stores = [store, across]
+    held_by = jnp.where(row == relay_row, 0, 1)
+    for step in range(1, half):
+        stores.append(hop(store, [(relay_row, relay_row - step)]))
+        held_by = jnp.where(row == relay_row - step, len(stores) - 1, held_by)
+        stores.append(hop(across, [(relay_row - half, relay_row - half - step)]))
+        held_by = jnp.where(row == relay_row - half - step, len(stores) - 1, held_by)
 
     info = jnp.concatenate([nbr_owner.reshape(-1), nbr_block.reshape(-1), lengths.reshape(-1)])
-    table = lax.all_gather(info, axes, axis=0).reshape(pool_count, columns, -1)
+    info = jnp.pad(info, (0, -info.shape[0] % 128))
+    table = lax.all_gather(info.reshape(1, -1, 128), "dp", axis=0, tiled=True)
+    table = lax.all_gather(table.reshape(1, columns, -1, 128), "pool", axis=0, tiled=True)
+    table = table.reshape(pool_count, columns, -1)
     by_column = jnp.swapaxes(table[:relay_row], 0, 1)
     owners = by_column[:, :, :per_device].reshape(columns, live_count)
     blocks = by_column[:, :, per_device : 2 * per_device].reshape(columns, live_count)
-    store_len = table[relay_row, :, 2 * per_device :]
-    order = jnp.arange(live_count, dtype=jnp.int32)
-    same = owners[:, :, None] == owners[:, None, :]
-    rank = jnp.sum(jnp.where(same & (order[None, :] < order[:, None])[None], 1, 0), axis=2)
-
-    target = (me + jnp.arange(columns, dtype=jnp.int32)) % columns
-    ring = jnp.arange(capacity, dtype=jnp.int32)
-    mine = (owners == me)[:, None, :] & (rank[:, None, :] == ring[None, :, None])
-    slot_block = jnp.sum(jnp.where(mine, blocks[:, None, :], 0), axis=2)
-    slot_block = jnp.take(slot_block, target, axis=0).reshape(slot_count)
-    store = database.reshape(block_count, slot_len, width)
-    sends = jnp.take(store, slot_block, axis=0).reshape(columns, capacity, slot_len, width)
-
-    arrived = [sends[0]]
-    for shift in range(1, columns):
-        hops = [(at(relay_row, j), at(relay_row, j + shift)) for j in range(columns)]
-        arrived.append(lax.ppermute(sends[shift], axes, hops))
-    arrived = jnp.concatenate(arrived, axis=0)
-
-    my_owner = lax.dynamic_index_in_dim(owners, me, 0, keepdims=False)
-    my_block = lax.dynamic_index_in_dim(blocks, me, 0, keepdims=False)
-    my_rank = lax.dynamic_index_in_dim(rank, me, 0, keepdims=False)
-    position = ((me - my_owner) % columns) * capacity + my_rank
-    wanted = jnp.take(arrived, position, axis=0).reshape(relay_row, per_device, slot_len, width)
-    raws = [
-        lax.ppermute(
-            wanted[p], axes, [(at(relay_row, j), at(p, j)) for j in range(columns)]
-        )
-        for p in range(relay_row)
-    ]
-
-    own_row = jnp.minimum(pool_index, relay_row - 1)
-    pick = my_owner * block_count + my_block
-    hot = pick[:, None] == jnp.arange(columns * block_count, dtype=jnp.int32)[None, :]
+    store_len = table[relay_row, :, 2 * per_device : 2 * per_device + block_count]
+    carrier, slot, crosses, number = place_requests(owners, per_device, pool_count, lanes)
+
+    ring = jnp.arange(slots, dtype=jnp.int32)
+    mine = ((owners == me) & (carrier == row))[:, None, :] & (slot[:, None, :] == ring[None, :, None])
+    slot_block = jnp.sum(jnp.where(mine, blocks[:, None, :], 0), axis=2).reshape(-1)
+    sends = pick(held_by, slot_block, stores)
+    arrived = lax.all_to_all(sends, "dp", split_axis=0, concat_axis=0, tiled=True)
+
+    mine_of = lambda a: lax.dynamic_index_in_dim(a, me, 0, keepdims=False)
+    my_owner, my_block, my_carrier, my_slot, my_cross, my_number = map(
+        mine_of, (owners, blocks, carrier, slot, crosses, number)
+    )
+    place = my_owner * slots + my_slot
+    share = lambda a, step: hop(
+        a,
+        [(p, p // half * half + (p + step) % half) for p in range(pool_count)],
+    )
+    held = [arrived] + [share(arrived, step) for step in range(1, half)]
+    if crossing:
+        ring = jnp.arange(crossing, dtype=jnp.int32)
+        mine = (my_cross & (my_carrier == row))[None, :] & (my_number[None, :] == ring[:, None])
+        leaving = pick(0, jnp.sum(jnp.where(mine, place[None, :], 0), axis=1), [arrived])
+        landed = hop(leaving, [(p, (p + half) % pool_count) for p in range(pool_count)])
+        held += [landed] + [share(landed, step) for step in range(1, half)]
+    origin = jnp.where(my_cross, (my_carrier + half) % pool_count, my_carrier)
+    which = (row - origin) % half + jnp.where(my_cross, half, 0)
+    index = jnp.where(my_cross, my_number, place)
+
+    own_row = jnp.minimum(row, relay_row - 1)
+    hot = (my_owner * block_count + my_block)[:, None] == jnp.arange(
+        columns * block_count, dtype=jnp.int32
+    )[None, :]
     wanted_len = jnp.sum(jnp.where(hot, store_len.reshape(1, -1), 0), axis=1)
-    my_len = lax.dynamic_index_in_dim(
-        wanted_len.reshape(relay_row, per_device), own_row, 0, keepdims=False
-    )
-    meta = jnp.concatenate([pool_index[None], my_len]).astype(jnp.int32)
+    own = lambda a: lax.dynamic_index_in_dim(
+        a.reshape(relay_row, per_device), own_row, 0, keepdims=False
+    )
+    live = (row < relay_row).astype(jnp.int32)
+    meta = jnp.concatenate([live[None], own(wanted_len), own(which), own(index)]).astype(jnp.int32)
 
     attn_out, q_grad, cond_grad, terms = run_spans(
         meta,
         queries.reshape(token_count, head_cols),
         cotangent.reshape(token_count, head_cols),
         cond.reshape(span_count, width).astype(jnp.float32),
-        raws,
+        held,
         gain,
         w_down,
         w_up,
         w_kv,
         nbr_count,
     )
-    parts = lax.all_to_all(terms, axes, split_axis=0, concat_axis=0, tiled=True)
-    adapter_grad = jnp.sum(
-        parts.reshape(pool_count * columns, -1, terms.shape[1]).astype(jnp.float32), axis=0
-    )
+
+    def scatter_sum(array, axis):
+        parts = lax.all_to_all(array, axis, split_axis=0, concat_axis=0, tiled=True)
+        return jnp.sum(
+            parts.reshape(lax.axis_size(axis), -1, array.shape[1]).astype(jnp.float32), axis=0
+        )
+
+    adapter_grad = scatter_sum(scatter_sum(terms, "pool").astype(jnp.bfloat16), "dp")
     return (
         attn_out.reshape(1, 1, token_count, head_cols),
         q_grad.reshape(1, 1, token_count, head_cols),

time: 204 us -> 217 us (1.064)
  Pallas kernels: 35.7 us -> 87.9 us
  local copies, waits for them, and re-layouts: 34.5 us -> 12.4 us
  blocking collectives: 86.4 us -> 70.4 us
  waiting for transfers between devices: 25.2 us -> 30.5 us
  starting transfers between devices: 13.3 us -> 9.2 us
  other arithmetic: 7.31 us -> 4.93 us
    pallas_call x1 -> x3, Pallas kernels: 35.7 us -> 87.9 us  [the longest x2 51.4 us: pick(): pl.pallas_call(functools.partial(pick_kernel, len(held)), grid_spec=pltpu...]
    all_gather x0 -> x2, blocking collectives: none -> 47.6 us  [the longest x1 25.4 us: body(): lax.all_gather(table.reshape(1, columns, -1, 128), 'pool', axis=0, tiled=...]
    unnamed x1 -> x0, blocking collectives: 42 us -> none
    all_to_all x0 -> x1, waiting for transfers between devices: none -> 24.2 us  [body(): lax.all_to_all(sends, 'dp', split_axis=0, concat_axis=0, tiled=True)]
    all_to_all x1 -> x2, blocking collectives: 44.5 us -> 22.8 us  [scatter_sum(): parts = lax.all_to_all(array, axis, split_axis=0, concat_axis=0, tiled=True)]
    ppermute x10 -> x6, waiting for transfers between devices: 25.2 us -> 6.28 us  [hop(): lax.ppermute(array, axes, [(a * columns + j, b * columns + j) for a, b in...]
    unnamed x26 -> x24, local copies, waits for them, and re-layouts: 21.2 us -> 10.7 us
    gather x3 -> x0, local copies, waits for them, and re-layouts: 8.04 us -> none  [the longest x1 4.71 us: body(): jnp.take(arrived, position, axis=0)]
  transfers between devices with their start and end apart: 10 -> 7, of which waited for: 1 -> 3; matrix products, arithmetic and copies ran while one was open for 9% -> 7% of each run, Pallas kernels for 0% -> 0%
where the time goes in v2:
time: 217 us; the launch traced here: 216 us
  Pallas kernels  87.9 us (41%)
  blocking collectives  70.4 us (32%)
  waiting for transfers between devices  30.5 us (14%)
  local copies, waits for them, and re-layouts  12.4 us (6%)
  starting transfers between devices  9.2 us (4%)
  other arithmetic  4.93 us (2%)
    pallas_call x2, Pallas kernels, pick(): pl.pallas_call(functools.partial(pick_kernel, len(held)), grid_spec=pltpu...  51.4 us
    pallas_call x1, Pallas kernels, run_spans(): pl.pallas_call(functools.partial(span_kernel, len(held), nbr_count), grid...  36.5 us
    all_gather x1, blocking collectives, body(): lax.all_gather(table.reshape(1, columns, -1, 128), 'pool', axis=0, tiled=...  25.4 us
    all_to_all x1, waiting for transfers between devices, body(): lax.all_to_all(sends, 'dp', split_axis=0, concat_axis=0, tiled=True)  24.2 us
    all_to_all x2, blocking collectives, scatter_sum(): parts = lax.all_to_all(array, axis, split_axis=0, concat_axis=0, tiled=True)  22.8 us
    all_gather x1, blocking collectives, body(): table = lax.all_gather(info.reshape(1, -1, 128), 'dp', axis=0, tiled=True)  22.1 us
    unnamed x24, local copies, waits for them, and re-layouts  10.7 us
    ppermute x6, waiting for transfers between devices, hop(): lax.ppermute(array, axes, [(a * columns + j, b * columns + j) for a, b in...  6.28 us
  transfers between devices with their start and end apart: 7, of which 3 were waited for; matrix products, arithmetic and copies ran while one was open for 7% of the time, Pallas kernels for 0%

profile of v2, /device:TPU:0, one launch (start us, length us, event | category | flops | bytes accessed | tf_op | source)
XLA Modules:
  0.0 216.2 jit_solution(3130344596929987831)
XLA Ops:
  0.6 0.8 collective-permute-start
  1.4 2.0 collective-permute-start.1
  3.4 1.3 collective-permute-start.2
  4.7 0.8 copy.49
  5.5 0.1 reshape.301
  5.6 0.8 copy.50
  6.3 0.1 reshape.302
  6.4 0.7 pad_add_fusion
  7.1 22.1 %all-gather.2 = s32[8,1,128]{2,1,0:T(1,128)S(1)} all-gather(s32[1,1,128]{2,1,0:T(1,128)S(1)} %pad_bitcast_fusion), channel_id=2, replica_groups=mesh['pool'=4,'dp'=8] {'dp'}, dimensions={0}, use_global_device_ids=true | all-gather | bytes 4608 | tf_op jit(solution)/shard_map/all_gather | solution.py:270
  29.3 25.4 %all-gather.1 = s32[32,1,128]{2,1,0:T(1,128)S(1)} all-gather(s32[8,1,128]{2,1,0:T(1,128)S(1)} %all-gather.2), channel_id=3, replica_groups=mesh['pool'=4,'dp'=8] {'pool'}, dimensions={0}, use_global_device_ids=true | all-gather | bytes 20480 | tf_op jit(solution)/shard_map/all_gather | solution.py:271
  54.7 0.1 reshape.306
  54.8 0.1 broadcast_compare_fusion
  54.9 0.3 convert_reduce_fusion.4
  55.2 0.1 ge.13
  55.3 0.6 convert_reduce_fusion.1
  55.9 0.1 reduce_sum.91
  56.1 0.2 select_reduce_fusion
  56.3 0.6 pad_add_fusion.2.meta
  56.9 33.7 %shard_map.138 = bf16[8,128,512]{2,1,0:T(8,128)(2,1)} custom-call(s32[9]{0:T(128)} %pad_add_fusion.2.meta, bf16[16,128,512]{2,1,0:T(8,128)(2,1)} %bitcast.49, bf16[16,128,512]{2,1,0:T(8,128)(2,1)} %copy-done.7, bf16[16,128,512]{2,1,0:T(8,128)(2,1)} %collective-permute-done.1.refs_2_, bf16[16,128,512]{2,1,0:T(8,128)(2,1)} %collective-permute-done.2.refs_3_), custom_call_target="tpu_custom_call" | custom-call | tf_op jit(solution)/shard_map/pallas_call | solution.py:193
  90.6 3.7 %all-to-all-start = ((bf16[8,128,512]{2,1,0:T(8,128)(2,1)}), bf16[8,128,512]{2,1,0:T(8,128)(2,1)S(1)}, u32[]{:S(2)}, u32[]{:S(2)}) async-start(bf16[8,128,512]{2,1,0:T(8,128)(2,1)} %shard_map.138), calls=%async_computation | async-start | bytes 2097152 | tf_op jit(solution)/shard_map/all_to_all | solution.py:283
  94.3 0.1 reshape.307
  94.5 0.5 broadcast.432
  95.0 0.7 fusion.32
  95.7 0.1 select_reduce_fusion.2
  95.8 0.6 pad_add_fusion.3.meta
  96.4 24.2 %all-to-all-done.refs_0_.rest_0_ = bf16[8,128,512]{2,1,0:T(8,128)(2,1)S(1)} async-done(((bf16[8,128,512]{2,1,0:T(8,128)(2,1)}), bf16[8,128,512]{2,1,0:T(8,128)(2,1)S(1)}, u32[]{:S(2)}, u32[]{:S(2)}) %all-to-all-start) | async-done | bytes 1048608 | tf_op jit(solution)/shard_map/all_to_all | solution.py:283
  120.6 1.0 copy-done
  121.6 17.7 %shard_map.139 = bf16[4,128,512]{2,1,0:T(8,128)(2,1)} custom-call(s32[5]{0:T(128)} %pad_add_fusion.3.meta, bf16[8,128,512]{2,1,0:T(8,128)(2,1)} %copy-done), custom_call_target="tpu_custom_call" | custom-call | tf_op jit(solution)/shard_map/pallas_call | solution.py:193
  139.2 1.5 collective-permute-start.4
  140.8 0.1 broadcast_in_dim.82
  140.9 0.1 squeeze.25
  141.0 0.1 squeeze.26
  141.0 0.1 squeeze.28
  141.1 0.1 add.147
  141.2 0.2 select_reduce_fusion.1
  141.4 0.1 reshape.309
  141.5 0.2 copy.60
  141.6 0.1 copy.59
  141.8 6.6 %copy.58 = bf16[512,4096]{0,1:T(8,128)(2,1)} copy(bf16[512,4096]{1,0:T(8,128)(2,1)} %rest_7_.1) | data formatting | bytes 8388608 | tf_op args[10]
  148.5 4.3 %collective-permute-done.4.rest_2_ = bf16[4,128,512]{2,1,0:T(8,128)(2,1)} collective-permute-done((bf16[4,128,512]{2,1,0:T(8,128)(2,1)}, bf16[4,128,512]{2,1,0:T(8,128)(2,1)}, u32[]{:S(2)}, u32[]{:S(2)}) %collective-permute-start.4) | collective-permute-done | bytes 524320 | tf_op jit(solution)/shard_map/ppermute | solution.py:254
  152.8 0.1 pad_add_fusion.1.meta
  152.9 2.0 collective-permute-done.5.rest_3_
  154.9 1.2 copy-done.5
  156.1 36.5 %shard_map.140 = (bf16[256,2048]{1,0:T(8,128)(2,1)}, bf16[256,2048]{1,0:T(8,128)(2,1)}, f32[4,512]{1,0:T(4,128)}, bf16[512,512]{1,0:T(8,128)(2,1)S(1)}) custom-call(s32[25]{0:T(128)S(1)} %pad_add_fusion.1.meta, bf16[256,2048]{1,0:T(8,128)(2,1)S(1)} %bitcast.43, bf16[256,2048]{1,0:T(8,128)(2,1)S(1)} %bitcast.44, f32[4,512]{1,0:T(4,128)S(1)} %bitcast_convert_fusion.cond_ref, ...), custom_call_target="tpu_custom_call" | custom-call | flops 11811160064 | bytes 16777216 | tf_op jit(solution)/shard_map/pallas_call | solution.py:145
  192.7 11.4 %all_to_all.23 = bf16[4,128,512]{2,1,0:T(8,128)(2,1)S(1)} all-to-all(bf16[4,128,512]{2,1,0:T(8,128)(2,1)S(1)} %bitcast.40), channel_id=1, replica_groups=mesh['pool'=4,'dp'=8] {'pool'}, dimensions={0} | all-to-all | bytes 1048576 | tf_op jit(solution)/shard_map/all_to_all | solution.py:330
  204.1 0.1 reduce_sum.94
  204.2 11.4 %all_to_all.24 = bf16[8,16,512]{2,1,0:T(8,128)(2,1)S(1)} all-to-all(bf16[8,16,512]{2,1,0:T(8,128)(2,1)S(1)} %bitcast.50), channel_id=1, replica_groups=mesh['pool'=4,'dp'=8] {'dp'}, dimensions={0} | all-to-all | bytes 262144 | tf_op jit(solution)/shard_map/all_to_all | solution.py:330
  215.5 0.6 convert_reduce_fusion
  (42 shorter events, 0.4 us)
Async XLA Ops:
  0.6 2.8 %collective-permute-start = (bf16[16,128,512]{2,1,0:T(8,128)(2,1)}, bf16[16,128,512]{2,1,0:T(8,128)(2,1)S(1)}, u32[]{:S(2)}, u32[]{:S(2)}) collective-permute-start(bf16[16,128,512]{2,1,0:T(8,128)(2,1)} %bitcast.47), channel_id=1, source_target_pairs={{24,8},{25,9},{26,10},{27,11},{28,12},{29,13},{30,14},{31,15}} | collective-permute-start | bytes 6291464 | tf_op jit(solution)/shard_map/ppermute | solution.py:254
  1.4 55.4 %collective-permute-start.1 = (bf16[16,128,512]{2,1,0:T(8,128)(2,1)}, bf16[16,128,512]{2,1,0:T(8,128)(2,1)}, u32[]{:S(2)}, u32[]{:S(2)}) collective-permute-start(bf16[16,128,512]{2,1,0:T(8,128)(2,1)} %bitcast.48), channel_id=1, source_target_pairs={{24,16},{25,17},{26,18},{27,19},{28,20},{29,21},{30,22},{31,23}} | collective-permute-start | bytes 6291464 | tf_op jit(solution)/shard_map/ppermute | solution.py:254
  3.4 53.5 %copy-start.7 = (bf16[16,128,512]{2,1,0:T(8,128)(2,1)}, bf16[16,128,512]{2,1,0:T(8,128)(2,1)S(1)}, u32[]{:S(2)}) copy-start(bf16[16,128,512]{2,1,0:T(8,128)(2,1)S(1)} %collective-permute-done.refs_1_) | copy-start | bytes 6291460
  3.4 53.5 %collective-permute-start.2 = (bf16[16,128,512]{2,1,0:T(8,128)(2,1)S(1)}, bf16[16,128,512]{2,1,0:T(8,128)(2,1)}, u32[]{:S(2)}, u32[]{:S(2)}) collective-permute-start(bf16[16,128,512]{2,1,0:T(8,128)(2,1)S(1)} %collective-permute-done.refs_1_), channel_id=1, source_target_pairs={{8,0},{9,1},{10,2},{11,3},{12,4},{13,5},{14,6},{15,7}} | collective-permute-start | bytes 6291464 | tf_op jit(solution)/shard_map/ppermute | solution.py:254
  90.6 50.9 %copy-start.2 = (bf16[512,256]{1,0:T(8,128)(2,1)S(1)}, bf16[512,256]{1,0:T(8,128)(2,1)}, u32[]{:S(2)}) copy-start(bf16[512,256]{1,0:T(8,128)(2,1)} %rest_5_.1) | copy-start | bytes 786436
  90.6 51.0 %copy-start.3 = (bf16[256,512]{1,0:T(8,128)(2,1)S(1)}, bf16[256,512]{1,0:T(8,128)(2,1)}, u32[]{:S(2)}) copy-start(bf16[256,512]{1,0:T(8,128)(2,1)} %rest_6_.1) | copy-start | bytes 786436
  90.6 30.0 %all-to-all-start = ((bf16[8,128,512]{2,1,0:T(8,128)(2,1)}), bf16[8,128,512]{2,1,0:T(8,128)(2,1)S(1)}, u32[]{:S(2)}, u32[]{:S(2)}) async-start(bf16[8,128,512]{2,1,0:T(8,128)(2,1)} %shard_map.138), calls=%async_computation | async-start | bytes 2097152 | tf_op jit(solution)/shard_map/all_to_all | solution.py:283
  120.6 1.0 copy-start
  139.2 13.5 %collective-permute-start.4 = (bf16[4,128,512]{2,1,0:T(8,128)(2,1)}, bf16[4,128,512]{2,1,0:T(8,128)(2,1)}, u32[]{:S(2)}, u32[]{:S(2)}) collective-permute-start(bf16[4,128,512]{2,1,0:T(8,128)(2,1)} %shard_map.139), channel_id=1, source_target_pairs={{0,16},{1,17},{2,18},{3,19},{4,20},{5,21},{6,22},{7,23},{8,24},{9,... | collective-permute-start | bytes 1572872 | tf_op jit(solution)/shard_map/ppermute | solution.py:254
  140.7 14.2 %collective-permute-start.3 = (bf16[8,128,512]{2,1,0:T(8,128)(2,1)}, bf16[8,128,512]{2,1,0:T(8,128)(2,1)}, u32[]{:S(2)}, u32[]{:S(2)}) collective-permute-start(bf16[8,128,512]{2,1,0:T(8,128)(2,1)} %copy-done), channel_id=1, source_target_pairs={{0,8},{1,9},{2,10},{3,11},{4,12},{5,13},{6,14},{7,15},{8,0},{9,1},... | collective-permute-start | bytes 3145736 | tf_op jit(solution)/shard_map/ppermute | solution.py:254
  141.8 11.1 %copy-start.8 = (bf16[1,1,4,512]{3,2,1,0:T(4,128)(2,1)S(1)}, bf16[1,1,4,512]{3,2,1,0:T(4,128)(2,1)}, u32[]{:S(2)}) copy-start(bf16[1,1,4,512]{3,2,1,0:T(4,128)(2,1)} %param.13) | copy-start | bytes 12292
  141.8 13.1 %copy-start.1 = (bf16[8,128,512]{2,1,0:T(8,128)(2,1)S(1)}, bf16[8,128,512]{2,1,0:T(8,128)(2,1)}, u32[]{:S(2)}) copy-start(bf16[8,128,512]{2,1,0:T(8,128)(2,1)} %copy-done) | copy-start | bytes 3145732
  141.8 13.1 %copy-start.4 = (bf16[1,1,256,2048]{3,2,1,0:T(8,128)(2,1)S(1)}, bf16[1,1,256,2048]{3,2,1,0:T(8,128)(2,1)}, u32[]{:S(2)}) copy-start(bf16[1,1,256,2048]{3,2,1,0:T(8,128)(2,1)} %param.11) | copy-start | bytes 3145732
  141.8 13.1 %copy-start.6 = (f32[512]{0:T(512)S(1)}, f32[512]{0:T(512)}, u32[]{:S(2)}) copy-start(f32[512]{0:T(512)} %param.18) | copy-start | bytes 6148
  152.8 2.1 collective-permute-start.5
  154.9 1.2 copy-start.5

commit v3 on v2

--- a/solution.py
+++ b/solution.py
@@ -10,6 +10,7 @@
 HEADS = 16
 HEAD = 128
 SPAN = 64
+PARTS = 1
 
 EPSILON = 1e-06
 FLOOR = -1e30
@@ -35,14 +36,15 @@
 
 
 def span_kernel(
-    held_count, nbr_count, meta,
+    held_count, nbr_count, parts, meta,
     q_ref, cot_ref, cond_ref, *rest,
 ):
     held_refs = rest[:held_count]
     (gain_ref, down_ref, up_ref, kv_ref, kvt_ref, upt_ref, downt_ref,
-     out_ref, qg_ref, cg_ref, ad_ref, kvg_ref, acc_ref, raw_ref, sems) = rest[held_count:]
+     out_ref, qg_ref, cg_ref, ad_ref, kvg_ref, acc_ref, raw_ref) = rest[held_count:]
     span = pl.program_id(0)
-    per_device, slot_len, width = raw_ref.shape
+    per_device = pl.num_programs(0) * nbr_count
+    slot_len, width = raw_ref.shape[1:]
     key_count = nbr_count * slot_len
     head_cols = q_ref.shape[1]
     rank = down_ref.shape[1]
@@ -50,20 +52,17 @@
     live = meta[0] == 1
     lens, which, index = 1, 1 + per_device, 1 + 2 * per_device
 
-    @pl.when(span == 0)
-    def _():
-        for n in range(per_device):
-            for b, held in enumerate(held_refs):
-                @pl.when(meta[which + n] == b)
-                def _():
-                    pltpu.make_async_copy(
-                        held.at[meta[index + n]], raw_ref.at[n], sems.at[n]
-                    ).start()
-
     for n in range(nbr_count):
         item = span * nbr_count + n
-        pltpu.make_async_copy(held_refs[0].at[0], raw_ref.at[item], sems.at[item]).wait()
-    raw = raw_ref[pl.ds(span * nbr_count, nbr_count)]
+        for b, held in enumerate(held_refs):
+            part, source = b % parts, b // parts
+            piece = held.shape[1]
+
+            @pl.when(meta[which + item] == source)
+            def _():
+                raw_ref[n, part * piece : (part + 1) * piece] = held[meta[index + item]]
+
+    raw = raw_ref[...]
     x_full = raw.reshape(key_count, width).astype(jnp.float32) + cond_ref[
         pl.ds(span, 1), :
     ]
@@ -131,10 +130,10 @@
         ad_ref[...] = jnp.where(live, acc_ref[...], 0.0).astype(ad_ref.dtype)
 
 
-def run_spans(meta, query, cot, cond, held, gain, w_down, w_up, w_kv, nbr_count):
+def run_spans(meta, query, cot, cond, held, parts, gain, w_down, w_up, w_kv, nbr_count):
     span_count, width = cond.shape
     token_count, head_cols = query.shape
-    slot_len = held[0].shape[1]
+    slot_len = held[0].shape[1] * parts
     rank = w_down.shape[1]
     whole = lambda a: pl.BlockSpec(a.shape, lambda s, m: (0,) * a.ndim, pipeline_mode=pl.Buffered(1))
     tokens = pl.BlockSpec((SPAN, head_cols), lambda s, m: (s, 0))
@@ -143,12 +142,12 @@
     rows = per_device * slot_len
     flops = 2 * rows * (2 * width * 2 * head_cols + 6 * width * rank + 6 * SPAN * head_cols)
     return pl.pallas_call(
-        functools.partial(span_kernel, len(held), nbr_count),
+        functools.partial(span_kernel, len(held), nbr_count, parts),
         grid_spec=pltpu.PrefetchScalarGridSpec(
             num_scalar_prefetch=1,
             grid=(span_count,),
             in_specs=[tokens, tokens, whole(cond)]
-            + [pl.BlockSpec(memory_space=pl.ANY)] * len(held)
+            + [pl.BlockSpec(memory_space=pltpu.VMEM)] * len(held)
             + [whole(w) for w in weights],
             out_specs=[
                 tokens,
@@ -159,8 +158,7 @@
             scratch_shapes=[
                 pltpu.VMEM((nbr_count * slot_len, 2 * head_cols), jnp.bfloat16),
                 pltpu.VMEM((width, 2 * rank), jnp.float32),
-                pltpu.VMEM((per_device, slot_len, width), jnp.bfloat16),
-                pltpu.SemaphoreType.DMA((per_device,)),
+                pltpu.VMEM((nbr_count, slot_len, width), jnp.bfloat16),
             ],
         ),
         out_shape=[
@@ -169,7 +167,7 @@
             jax.ShapeDtypeStruct((span_count, width), jnp.float32),
             jax.ShapeDtypeStruct((width, 2 * rank), jnp.bfloat16),
         ],
-        compiler_params=pltpu.CompilerParams(vmem_limit_bytes=48 * 2**20),
+        compiler_params=pltpu.CompilerParams(vmem_limit_bytes=40 * 2**20),
         cost_estimate=pl.CostEstimate(
             flops=flops, bytes_accessed=16 * 2**20, transcendentals=rows * SPAN * HEADS
         ),
@@ -177,14 +175,12 @@
 
 
 def pick_kernel(held_count, meta, *refs):
-    held_refs, out_ref, sems = refs[:held_count], refs[held_count], refs[held_count + 1]
+    held_refs, out_ref = refs[:held_count], refs[held_count]
     for b, held in enumerate(held_refs):
         @pl.when(meta[0] == b)
         def _():
             for n in range(out_ref.shape[0]):
-                pltpu.make_async_copy(held.at[meta[1 + n]], out_ref.at[n], sems.at[n]).start()
-    for n in range(out_ref.shape[0]):
-        pltpu.make_async_copy(held_refs[0].at[0], out_ref.at[n], sems.at[n]).wait()
+                out_ref[n] = held[meta[1 + n]]
 
 
 def pick(which, index, held):
@@ -195,11 +191,11 @@
         grid_spec=pltpu.PrefetchScalarGridSpec(
             num_scalar_prefetch=1,
             grid=(1,),
-            in_specs=[pl.BlockSpec(memory_space=pl.ANY)] * len(held),
-            out_specs=pl.BlockSpec(memory_space=pl.ANY),
-            scratch_shapes=[pltpu.SemaphoreType.DMA((count,))],
+            in_specs=[pl.BlockSpec(memory_space=pltpu.VMEM)] * len(held),
+            out_specs=pl.BlockSpec(memory_space=pltpu.VMEM),
         ),
         out_shape=jax.ShapeDtypeStruct((count,) + held[0].shape[1:], held[0].dtype),
+        compiler_params=pltpu.CompilerParams(vmem_limit_bytes=24 * 2**20),
     )(meta, *held)
 
 
@@ -255,20 +251,18 @@
             array, axes, [(a * columns + j, b * columns + j) for a, b in pairs for j in range(columns)]
         )
 
-    store = database.reshape(block_count, slot_len, width)
-    across = hop(store, [(relay_row, relay_row - half)])
-    stores = [store, across]
-    held_by = jnp.where(row == relay_row, 0, 1)
-    for step in range(1, half):
-        stores.append(hop(store, [(relay_row, relay_row - step)]))
-        held_by = jnp.where(row == relay_row - step, len(stores) - 1, held_by)
-        stores.append(hop(across, [(relay_row - half, relay_row - half - step)]))
-        held_by = jnp.where(row == relay_row - half - step, len(stores) - 1, held_by)
+    parts = PARTS if slot_len % (PARTS * 16) == 0 else 1
+    piece = slot_len // parts
+    full_store = database.reshape(block_count, slot_len, width)
+    store = [full_store[:, i * piece : (i + 1) * piece] for i in range(parts)]
+
+    across = [hop(a, [(relay_row, relay_row - half)]) for a in store]
 
     info = jnp.concatenate([nbr_owner.reshape(-1), nbr_block.reshape(-1), lengths.reshape(-1)])
     info = jnp.pad(info, (0, -info.shape[0] % 128))
     table = lax.all_gather(info.reshape(1, -1, 128), "dp", axis=0, tiled=True)
     table = lax.all_gather(table.reshape(1, columns, -1, 128), "pool", axis=0, tiled=True)
+    across, table = lax.optimization_barrier((across, table))
     table = table.reshape(pool_count, columns, -1)
     by_column = jnp.swapaxes(table[:relay_row], 0, 1)
     owners = by_column[:, :, :per_device].reshape(columns, live_count)
@@ -279,28 +273,39 @@
     ring = jnp.arange(slots, dtype=jnp.int32)
     mine = ((owners == me) & (carrier == row))[:, None, :] & (slot[:, None, :] == ring[None, :, None])
     slot_block = jnp.sum(jnp.where(mine, blocks[:, None, :], 0), axis=2).reshape(-1)
-    sends = pick(held_by, slot_block, stores)
-    arrived = lax.all_to_all(sends, "dp", split_axis=0, concat_axis=0, tiled=True)
 
     mine_of = lambda a: lax.dynamic_index_in_dim(a, me, 0, keepdims=False)
     my_owner, my_block, my_carrier, my_slot, my_cross, my_number = map(
         mine_of, (owners, blocks, carrier, slot, crosses, number)
     )
     place = my_owner * slots + my_slot
-    share = lambda a, step: hop(
-        a,
-        [(p, p // half * half + (p + step) % half) for p in range(pool_count)],
-    )
-    held = [arrived] + [share(arrived, step) for step in range(1, half)]
-    if crossing:
-        ring = jnp.arange(crossing, dtype=jnp.int32)
-        mine = (my_cross & (my_carrier == row))[None, :] & (my_number[None, :] == ring[:, None])
-        leaving = pick(0, jnp.sum(jnp.where(mine, place[None, :], 0), axis=1), [arrived])
-        landed = hop(leaving, [(p, (p + half) % pool_count) for p in range(pool_count)])
-        held += [landed] + [share(landed, step) for step in range(1, half)]
+    ring = jnp.arange(crossing, dtype=jnp.int32)
+    mine = (my_cross & (my_carrier == row))[None, :] & (my_number[None, :] == ring[:, None])
+    leaving_place = jnp.sum(jnp.where(mine, place[None, :], 0), axis=1)
+
+    def share(array, step):
+        return hop(array, [(p, p // half * half + (p + step) % half) for p in range(pool_count)])
+
+    held = []
+    for i in range(parts):
+        stores = [store[i], across[i]]
+        held_by = jnp.where(row == relay_row, 0, 1)
+        for step in range(1, half):
+            for near, array in ((relay_row, store[i]), (relay_row - half, across[i])):
+                stores.append(hop(array, [(near, near - step)]))
+                held_by = jnp.where(row == near - step, len(stores) - 1, held_by)
+        sends = pick(held_by, slot_block, stores)
+        arrived = lax.all_to_all(sends, "dp", split_axis=0, concat_axis=0, tiled=True)
+        here = [arrived] + [share(arrived, step) for step in range(1, half)]
+        if crossing:
+            leaving = pick(0, leaving_place, [arrived])
+            landed = hop(leaving, [(p, (p + half) % pool_count) for p in range(pool_count)])
+            here += [landed] + [share(landed, step) for step in range(1, half)]
+        held.append(here)
     origin = jnp.where(my_cross, (my_carrier + half) % pool_count, my_carrier)
     which = (row - origin) % half + jnp.where(my_cross, half, 0)
     index = jnp.where(my_cross, my_number, place)
+    held = [here[b] for b in range(len(held[0])) for here in held]
 
     own_row = jnp.minimum(row, relay_row - 1)
     hot = (my_owner * block_count + my_block)[:, None] == jnp.arange(
@@ -319,6 +324,7 @@
         cotangent.reshape(token_count, head_cols),
         cond.reshape(span_count, width).astype(jnp.float32),
         held,
+        parts,
         gain,
         w_down,
         w_up,

time: 217 us -> 154 us (0.71)
  Pallas kernels: 87.9 us -> 39.2 us
  blocking collectives: 70.4 us -> 50 us
  waiting for transfers between devices: 30.5 us -> 35.3 us
  local copies, waits for them, and re-layouts: 12.4 us -> 16.3 us
    pallas_call x2, Pallas kernels: 51.4 us -> 4.38 us  [pick(): pl.pallas_call(functools.partial(pick_kernel, len(held)), grid_spec=pltpu...]
    all_gather x1, blocking collectives: 25.4 us -> 5.17 us  [body(): lax.all_gather(table.reshape(1, columns, -1, 128), 'pool', axis=0, tiled=...]
    ppermute x6, waiting for transfers between devices: 6.28 us -> 10.6 us  [hop(): lax.ppermute(array, axes, [(a * columns + j, b * columns + j) for a, b in...]
    unnamed x24 -> x22, local copies, waits for them, and re-layouts: 10.7 us -> 14.5 us
  transfers between devices with their start and end apart: 7 -> 7, of which waited for: 3 -> 4; matrix products, arithmetic and copies ran while one was open for 7% -> 9% of each run, Pallas kernels for 0% -> 0%
where the time goes in v3:
time: 154 us
  blocking collectives  50 us (32%)
  Pallas kernels  39.2 us (25%)
  waiting for transfers between devices  35.3 us (23%)
  local copies, waits for them, and re-layouts  16.3 us (11%)
  starting transfers between devices  7.93 us (5%)
  other arithmetic  3.91 us (3%)
    pallas_call x1, Pallas kernels, run_spans(): pl.pallas_call(functools.partial(span_kernel, len(held), nbr_count, parts...  34.9 us
    all_to_all x1, waiting for transfers between devices, body(): lax.all_to_all(sends, 'dp', split_axis=0, concat_axis=0, tiled=True)  24.7 us
    all_to_all x2, blocking collectives, scatter_sum(): parts = lax.all_to_all(array, axis, split_axis=0, concat_axis=0, tiled=True)  22.7 us
    all_gather x1, blocking collectives, body(): table = lax.all_gather(info.reshape(1, -1, 128), 'dp', axis=0, tiled=True)  22.1 us
    unnamed x22, local copies, waits for them, and re-layouts  14.5 us
    ppermute x6, waiting for transfers between devices, hop(): lax.ppermute(array, axes, [(a * columns + j, b * columns + j) for a, b in...  10.6 us
    all_gather x1, blocking collectives, body(): lax.all_gather(table.reshape(1, columns, -1, 128), 'pool', axis=0, tiled=...  5.17 us
    pallas_call x2, Pallas kernels, pick(): pl.pallas_call(functools.partial(pick_kernel, len(held)), grid_spec=pltpu...  4.38 us
  transfers between devices with their start and end apart: 7, of which 4 were waited for; matrix products, arithmetic and copies ran while one was open for 9% of the time, Pallas kernels for 0%

profile of v3, /device:TPU:0, one launch (start us, length us, event | category | flops | bytes accessed | tf_op | source)
XLA Modules:
  0.0 153.5 jit_solution(11557634763111800422)
XLA Ops:
  0.6 0.8 collective-permute-start
  1.4 2.0 %collective-permute-start.1 = (bf16[16,128,512]{2,1,0:T(8,128)(2,1)}, bf16[16,128,512]{2,1,0:T(8,128)(2,1)}, u32[]{:S(2)}, u32[]{:S(2)}) collective-permute-start(bf16[16,128,512]{2,1,0:T(8,128)(2,1)} %bitcast.41), channel_id=1, source_target_pairs={{24,16},{25,17},{26,18},{27,19},{28,20},{29,21},{30,22},{31,23}} | collective-permute-start | bytes 6291464 | tf_op jit(solution)/shard_map/ppermute | solution.py:250
  3.5 0.8 copy.48
  4.2 0.1 reshape.302
  4.3 0.8 copy.49
  5.1 0.1 reshape.303
  5.2 0.7 pad_add_fusion
  5.9 22.1 %all-gather.2 = s32[8,1,128]{2,1,0:T(1,128)S(1)} all-gather(s32[1,1,128]{2,1,0:T(1,128)S(1)} %pad_bitcast_fusion), channel_id=2, replica_groups=mesh['pool'=4,'dp'=8] {'dp'}, dimensions={0}, use_global_device_ids=true | all-gather | bytes 4608 | tf_op jit(solution)/shard_map/all_gather | solution.py:263
  28.0 5.2 %all-gather.1 = s32[32,1,128]{2,1,0:T(1,128)S(1)} all-gather(s32[8,1,128]{2,1,0:T(1,128)S(1)} %all-gather.2), channel_id=3, replica_groups=mesh['pool'=4,'dp'=8] {'pool'}, dimensions={0}, use_global_device_ids=true | all-gather | bytes 20480 | tf_op jit(solution)/shard_map/all_gather | solution.py:264
  33.2 1.3 collective-permute-start.2
  34.7 0.1 reshape.307
  34.7 0.3 convert_reduce_fusion.4
  35.0 0.1 ge.13
  35.1 0.6 convert_reduce_fusion.1
  35.7 0.1 reduce_sum.91
  35.8 0.1 add.148
  35.9 0.2 select_reduce_fusion
  36.2 3.2 %collective-permute-done.2.refs_3_ = bf16[16,128,512]{2,1,0:T(8,128)(2,1)} collective-permute-done((bf16[16,128,512]{2,1,0:T(8,128)(2,1)S(1)}, bf16[16,128,512]{2,1,0:T(8,128)(2,1)}, u32[]{:S(2)}, u32[]{:S(2)}) %collective-permute-start.2) | collective-permute-done | bytes 2097184 | tf_op jit(solution)/shard_map/ppermute | solution.py:250
  39.4 1.6 %copy-done.1 = bf16[1,1,16,128,512]{4,3,2,1,0:T(8,128)(2,1)S(1)} copy-done((bf16[1,1,16,128,512]{4,3,2,1,0:T(8,128)(2,1)S(1)}, bf16[1,1,16,128,512]{4,3,2,1,0:T(8,128)(2,1)}, u32[]{:S(2)}) %copy-start.1) | copy-done | bytes 2097176
  41.0 3.8 %shard_map.138 = bf16[8,128,512]{2,1,0:T(8,128)(2,1)} custom-call(s32[9]{0:T(128)S(1)} %pad_add_fusion.2.meta, bf16[16,128,512]{2,1,0:T(8,128)(2,1)S(1)} %bitcast.42, bf16[16,128,512]{2,1,0:T(8,128)(2,1)S(1)} %collective-permute-done.refs_1_, bf16[16,128,512]{2,1,0:T(8,128)(2,1)} %collective-permute-done.1.refs_2_, ...), custom_call_target="tpu_custom_call" | custom-call | tf_op jit(solution)/shard_map/pallas_call | solution.py:189
  44.8 3.7 %all-to-all-start = ((bf16[8,128,512]{2,1,0:T(8,128)(2,1)}), bf16[8,128,512]{2,1,0:T(8,128)(2,1)S(1)}, u32[]{:S(2)}, u32[]{:S(2)}) async-start(bf16[8,128,512]{2,1,0:T(8,128)(2,1)} %shard_map.138), calls=%async_computation | async-start | bytes 2097152 | tf_op jit(solution)/shard_map/all_to_all | solution.py:298
  48.5 0.1 reshape.308
  48.6 0.5 broadcast.432
  49.2 0.7 fusion.32
  49.8 0.1 select_reduce_fusion.2
  50.0 24.7 %all-to-all-done.refs_0_.rest_0_ = bf16[8,128,512]{2,1,0:T(8,128)(2,1)S(1)} async-done(((bf16[8,128,512]{2,1,0:T(8,128)(2,1)}), bf16[8,128,512]{2,1,0:T(8,128)(2,1)S(1)}, u32[]{:S(2)}, u32[]{:S(2)}) %all-to-all-start) | async-done | bytes 1048608 | tf_op jit(solution)/shard_map/all_to_all | solution.py:298
  74.8 0.6 shard_map.139
  75.5 0.1 copy.58
  75.7 0.1 copy.57
  75.8 6.5 %copy.56 = bf16[512,4096]{0,1:T(8,128)(2,1)} copy(bf16[512,4096]{1,0:T(8,128)(2,1)} %rest_7_.1) | data formatting | bytes 8388608 | tf_op args[10]
  82.4 0.1 broadcast_in_dim.82
  82.5 0.1 squeeze.25
  82.6 0.1 squeeze.26
  82.7 0.1 squeeze.28
  82.8 0.1 add.147
  82.9 5.7 %collective-permute-done.4.rest_2_ = bf16[4,128,512]{2,1,0:T(8,128)(2,1)S(1)} collective-permute-done((bf16[4,128,512]{2,1,0:T(8,128)(2,1)S(1)}, bf16[4,128,512]{2,1,0:T(8,128)(2,1)S(1)}, u32[]{:S(2)}, u32[]{:S(2)}) %collective-permute-start.4) | collective-permute-done | bytes 524320 | tf_op jit(solution)/shard_map/ppermute | solution.py:250
  88.6 0.2 select_reduce_fusion.1
  88.7 0.1 reshape.310
  88.9 0.1 pad_add_fusion.1.meta
  88.9 1.7 %collective-permute-done.5.rest_3_ = bf16[4,128,512]{2,1,0:T(8,128)(2,1)} collective-permute-done((bf16[4,128,512]{2,1,0:T(8,128)(2,1)S(1)}, bf16[4,128,512]{2,1,0:T(8,128)(2,1)}, u32[]{:S(2)}, u32[]{:S(2)}) %collective-permute-start.5) | collective-permute-done | bytes 524320 | tf_op jit(solution)/shard_map/ppermute | solution.py:250
  90.6 2.2 %copy-done = bf16[512,4096]{1,0:T(8,128)(2,1)S(1)} copy-done((bf16[512,4096]{1,0:T(8,128)(2,1)S(1)}, bf16[512,4096]{1,0:T(8,128)(2,1)}, u32[]{:S(2)}) %copy-start) | copy-done | bytes 4194328
  92.8 1.2 copy-done.4
  94.0 1.2 copy-done.5
  95.3 34.9 %shard_map.140 = (bf16[256,2048]{1,0:T(8,128)(2,1)}, bf16[256,2048]{1,0:T(8,128)(2,1)}, f32[4,512]{1,0:T(4,128)}, bf16[512,512]{1,0:T(8,128)(2,1)S(1)}) custom-call(s32[25]{0:T(128)S(1)} %pad_add_fusion.1.meta, bf16[256,2048]{1,0:T(8,128)(2,1)S(1)} %bitcast.46, bf16[256,2048]{1,0:T(8,128)(2,1)S(1)} %bitcast.47, f32[4,512]{1,0:T(4,128)S(1)} %bitcast_convert_fusion.cond_ref, ...), custom_call_target="tpu_custom_call" | custom-call | flops 11811160064 | bytes 16777216 | tf_op jit(solution)/shard_map/pallas_call | solution.py:144
  130.1 11.2 %all_to_all.23 = bf16[4,128,512]{2,1,0:T(8,128)(2,1)S(1)} all-to-all(bf16[4,128,512]{2,1,0:T(8,128)(2,1)S(1)} %bitcast.43), channel_id=1, replica_groups=mesh['pool'=4,'dp'=8] {'pool'}, dimensions={0} | all-to-all | bytes 1048576 | tf_op jit(solution)/shard_map/all_to_all | solution.py:336
  141.4 0.1 reduce_sum.94
  141.4 11.5 %all_to_all.24 = bf16[8,16,512]{2,1,0:T(8,128)(2,1)S(1)} all-to-all(bf16[8,16,512]{2,1,0:T(8,128)(2,1)S(1)} %bitcast.50), channel_id=1, replica_groups=mesh['pool'=4,'dp'=8] {'dp'}, dimensions={0} | all-to-all | bytes 262144 | tf_op jit(solution)/shard_map/all_to_all | solution.py:336
  152.9 0.6 convert_reduce_fusion
  (40 shorter events, 0.7 us)
Async XLA Ops:
  0.6 32.6 %collective-permute-start = (bf16[16,128,512]{2,1,0:T(8,128)(2,1)}, bf16[16,128,512]{2,1,0:T(8,128)(2,1)S(1)}, u32[]{:S(2)}, u32[]{:S(2)}) collective-permute-start(bf16[16,128,512]{2,1,0:T(8,128)(2,1)} %bitcast.40), channel_id=1, source_target_pairs={{24,8},{25,9},{26,10},{27,11},{28,12},{29,13},{30,14},{31,15}} | collective-permute-start | bytes 6291464 | tf_op jit(solution)/shard_map/ppermute | solution.py:250
  1.4 34.7 %collective-permute-start.1 = (bf16[16,128,512]{2,1,0:T(8,128)(2,1)}, bf16[16,128,512]{2,1,0:T(8,128)(2,1)}, u32[]{:S(2)}, u32[]{:S(2)}) collective-permute-start(bf16[16,128,512]{2,1,0:T(8,128)(2,1)} %bitcast.41), channel_id=1, source_target_pairs={{24,16},{25,17},{26,18},{27,19},{28,20},{29,21},{30,22},{31,23}} | collective-permute-start | bytes 6291464 | tf_op jit(solution)/shard_map/ppermute | solution.py:250
  33.2 6.2 %collective-permute-start.2 = (bf16[16,128,512]{2,1,0:T(8,128)(2,1)S(1)}, bf16[16,128,512]{2,1,0:T(8,128)(2,1)}, u32[]{:S(2)}, u32[]{:S(2)}) collective-permute-start(bf16[16,128,512]{2,1,0:T(8,128)(2,1)S(1)} %collective-permute-done.refs_1_), channel_id=1, source_target_pairs={{8,0},{9,1},{10,2},{11,3},{12,4},{13,5},{14,6},{15,7}} | collective-permute-start | bytes 6291464 | tf_op jit(solution)/shard_map/ppermute | solution.py:250
  39.4 1.6 %copy-start.1 = (bf16[1,1,16,128,512]{4,3,2,1,0:T(8,128)(2,1)S(1)}, bf16[1,1,16,128,512]{4,3,2,1,0:T(8,128)(2,1)}, u32[]{:S(2)}) copy-start(bf16[1,1,16,128,512]{4,3,2,1,0:T(8,128)(2,1)} %param.16) | copy-start | bytes 6291460
  44.8 30.7 %copy-start.2 = (bf16[512,256]{1,0:T(8,128)(2,1)S(1)}, bf16[512,256]{1,0:T(8,128)(2,1)}, u32[]{:S(2)}) copy-start(bf16[512,256]{1,0:T(8,128)(2,1)} %rest_5_.1) | copy-start | bytes 786436
  44.8 30.9 %copy-start.3 = (bf16[256,512]{1,0:T(8,128)(2,1)S(1)}, bf16[256,512]{1,0:T(8,128)(2,1)}, u32[]{:S(2)}) copy-start(bf16[256,512]{1,0:T(8,128)(2,1)} %rest_6_.1) | copy-start | bytes 786436
  44.8 30.0 %all-to-all-start = ((bf16[8,128,512]{2,1,0:T(8,128)(2,1)}), bf16[8,128,512]{2,1,0:T(8,128)(2,1)S(1)}, u32[]{:S(2)}, u32[]{:S(2)}) async-start(bf16[8,128,512]{2,1,0:T(8,128)(2,1)} %shard_map.138), calls=%async_computation | async-start | bytes 2097152 | tf_op jit(solution)/shard_map/all_to_all | solution.py:298
  75.3 13.2 %collective-permute-start.4 = (bf16[4,128,512]{2,1,0:T(8,128)(2,1)S(1)}, bf16[4,128,512]{2,1,0:T(8,128)(2,1)S(1)}, u32[]{:S(2)}, u32[]{:S(2)}) collective-permute-start(bf16[4,128,512]{2,1,0:T(8,128)(2,1)S(1)} %shard_map.139), channel_id=1, source_target_pairs={{0,16},{1,17},{2,18},{3,19},{4,20},{5,21},{6,22},{7,23},{8,24},{9,... | collective-permute-start | bytes 1572872 | tf_op jit(solution)/shard_map/ppermute | solution.py:250
  75.4 15.2 %collective-permute-start.3 = (bf16[8,128,512]{2,1,0:T(8,128)(2,1)S(1)}, bf16[8,128,512]{2,1,0:T(8,128)(2,1)}, u32[]{:S(2)}, u32[]{:S(2)}) collective-permute-start(bf16[8,128,512]{2,1,0:T(8,128)(2,1)S(1)} %all-to-all-done.refs_0_.rest_0_), channel_id=1, source_target_pairs={{0,8},{1,9},{2,10},{3,11},{4,12},{5,13},{6,14},{7,15},{8,0},{9,1},... | collective-permute-start | bytes 3145736 | tf_op jit(solution)/shard_map/ppermute | solution.py:250
  75.8 6.5 %copy-start.7 = (bf16[1,1,4,512]{3,2,1,0:T(4,128)(2,1)S(1)}, bf16[1,1,4,512]{3,2,1,0:T(4,128)(2,1)}, u32[]{:S(2)}) copy-start(bf16[1,1,4,512]{3,2,1,0:T(4,128)(2,1)} %param.13) | copy-start | bytes 12292
  75.8 14.8 %copy-start.6 = (f32[512]{0:T(512)S(1)}, f32[512]{0:T(512)}, u32[]{:S(2)}) copy-start(f32[512]{0:T(512)} %param.18) | copy-start | bytes 6148
  88.6 2.0 %collective-permute-start.5 = (bf16[4,128,512]{2,1,0:T(8,128)(2,1)S(1)}, bf16[4,128,512]{2,1,0:T(8,128)(2,1)}, u32[]{:S(2)}, u32[]{:S(2)}) collective-permute-start(bf16[4,128,512]{2,1,0:T(8,128)(2,1)S(1)} %collective-permute-done.4.rest_2_), channel_id=1, source_target_pairs={{0,8},{1,9},{2,10},{3,11},{4,12},{5,13},{6,14},{7,15},{8,0},{9,1},... | collective-permute-start | bytes 1572872 | tf_op jit(solution)/shard_map/ppermute | solution.py:250
  90.6 2.2 %copy-start = (bf16[512,4096]{1,0:T(8,128)(2,1)S(1)}, bf16[512,4096]{1,0:T(8,128)(2,1)}, u32[]{:S(2)}) copy-start(bf16[512,4096]{1,0:T(8,128)(2,1)} %rest_7_.1) | copy-start | bytes 12582916
  92.8 1.2 copy-start.4
  94.0 1.2 copy-start.5

commit v4 on v3

--- a/solution.py
+++ b/solution.py
@@ -10,7 +10,7 @@
 HEADS = 16
 HEAD = 128
 SPAN = 64
-PARTS = 1
+PARTS = 2
 
 EPSILON = 1e-06
 FLOOR = -1e30

time: 154 us -> 161 us (1.045)
  waiting for transfers between devices: 35.3 us -> 21.1 us
  starting transfers between devices: 7.93 us -> 17.8 us
  local copies, waits for them, and re-layouts: 16.3 us -> 24.5 us
  Pallas kernels: 39.2 us -> 42.2 us
    all_to_all x1 -> x2, waiting for transfers between devices: 24.7 us -> 15.1 us  [body(): lax.all_to_all(sends, 'dp', split_axis=0, concat_axis=0, tiled=True)]
    unnamed x22 -> x44, local copies, waits for them, and re-layouts: 14.5 us -> 21 us
    ppermute x6 -> x12, starting transfers between devices: 4.24 us -> 9.33 us  [hop(): lax.ppermute(array, axes, [(a * columns + j, b * columns + j) for a, b in...]
    all_to_all x1 -> x2, starting transfers between devices: 3.69 us -> 8.43 us  [body(): lax.all_to_all(sends, 'dp', split_axis=0, concat_axis=0, tiled=True)]
    ppermute x6 -> x12, waiting for transfers between devices: 10.6 us -> 6 us  [hop(): lax.ppermute(array, axes, [(a * columns + j, b * columns + j) for a, b in...]
    pallas_call x2 -> x4, Pallas kernels: 4.38 us -> 7.27 us  [pick(): pl.pallas_call(functools.partial(pick_kernel, len(held)), grid_spec=pltpu...]
    slice x0 -> x1, local copies, waits for them, and re-layouts: none -> 1.75 us  [body(): store = [full_store[:, i * piece:(i + 1) * piece] for i in range(parts)]]
  transfers between devices with their start and end apart: 7 -> 14, of which waited for: 4 -> 5; matrix products, arithmetic and copies ran while one was open for 9% -> 8% of each run, Pallas kernels for 0% -> 5%
where the time goes in v4:
time: 161 us; the launch traced here: 160 us
  blocking collectives  50.7 us (31%)
  Pallas kernels  42.2 us (26%)
  local copies, waits for them, and re-layouts  24.5 us (15%)
  waiting for transfers between devices  21.1 us (13%)
  starting transfers between devices  17.8 us (11%)
  other arithmetic  3.25 us (2%)
    pallas_call x1, Pallas kernels, run_spans(): pl.pallas_call(functools.partial(span_kernel, len(held), nbr_count, parts...  34.9 us
    all_to_all x2, blocking collectives, scatter_sum(): parts = lax.all_to_all(array, axis, split_axis=0, concat_axis=0, tiled=True)  23.3 us
    all_gather x1, blocking collectives, body(): table = lax.all_gather(info.reshape(1, -1, 128), 'dp', axis=0, tiled=True)  22.1 us
    unnamed x44, local copies, waits for them, and re-layouts  21 us
    all_to_all x2, waiting for transfers between devices, body(): lax.all_to_all(sends, 'dp', split_axis=0, concat_axis=0, tiled=True)  15.1 us
    ppermute x12, starting transfers between devices, hop(): lax.ppermute(array, axes, [(a * columns + j, b * columns + j) for a, b in...  9.33 us
    all_to_all x2, starting transfers between devices, body(): lax.all_to_all(sends, 'dp', split_axis=0, concat_axis=0, tiled=True)  8.43 us
    pallas_call x4, Pallas kernels, pick(): pl.pallas_call(functools.partial(pick_kernel, len(held)), grid_spec=pltpu...  7.27 us
  transfers between devices with their start and end apart: 14, of which 5 were waited for; matrix products, arithmetic and copies ran while one was open for 8% of the time, Pallas kernels for 5%

profile of v4, /device:TPU:0, one launch (start us, length us, event | category | flops | bytes accessed | tf_op | source)
XLA Modules:
  0.0 160.3 jit_solution(18026774823523067501)
XLA Ops:
  0.7 1.8 %fusion.34 = (bf16[16,64,512]{2,1,0:T(8,128)(2,1)S(1)}, bf16[16,64,512]{2,1,0:T(8,128)(2,1)S(1)}) fusion(bf16[16,128,512]{2,1,0:T(8,128)(2,1)} %bitcast.47), kind=kLoop, calls=%fused_computation.120 | loop fusion | bytes 4194304 | tf_op jit(solution)/shard_map/slice | solution.py:257
  2.4 0.7 collective-permute-start.1
  3.2 1.6 %collective-permute-start = (bf16[16,64,512]{2,1,0:T(8,128)(2,1)S(1)}, bf16[16,64,512]{2,1,0:T(8,128)(2,1)}, u32[]{:S(2)}, u32[]{:S(2)}) collective-permute-start(bf16[16,64,512]{2,1,0:T(8,128)(2,1)S(1)} %get-tuple-element.26.refs_0_), channel_id=1, source_target_pairs={{24,8},{25,9},{26,10},{27,11},{28,12},{29,13},{30,14},{31,15}} | collective-permute-start | bytes 3145736 | tf_op jit(solution)/shard_map/ppermute | solution.py:250
  4.8 1.6 %collective-permute-start.4 = (bf16[16,64,512]{2,1,0:T(8,128)(2,1)S(1)}, bf16[16,64,512]{2,1,0:T(8,128)(2,1)}, u32[]{:S(2)}, u32[]{:S(2)}) collective-permute-start(bf16[16,64,512]{2,1,0:T(8,128)(2,1)S(1)} %get-tuple-element.25.refs_0_), channel_id=1, source_target_pairs={{24,16},{25,17},{26,18},{27,19},{28,20},{29,21},{30,22},{31,23}} | collective-permute-start | bytes 3145736 | tf_op jit(solution)/shard_map/ppermute | solution.py:250
  6.4 1.7 %collective-permute-start.2 = (bf16[16,64,512]{2,1,0:T(8,128)(2,1)S(1)}, bf16[16,64,512]{2,1,0:T(8,128)(2,1)}, u32[]{:S(2)}, u32[]{:S(2)}) collective-permute-start(bf16[16,64,512]{2,1,0:T(8,128)(2,1)S(1)} %get-tuple-element.26.refs_0_), channel_id=1, source_target_pairs={{24,16},{25,17},{26,18},{27,19},{28,20},{29,21},{30,22},{31,23}} | collective-permute-start | bytes 3145736 | tf_op jit(solution)/shard_map/ppermute | solution.py:250
  8.5 22.1 %all-gather.2 = s32[8,1,128]{2,1,0:T(1,128)S(1)} all-gather(s32[1,1,128]{2,1,0:T(1,128)S(1)} %pad_bitcast_fusion), channel_id=2, replica_groups=mesh['pool'=4,'dp'=8] {'dp'}, dimensions={0}, use_global_device_ids=true | all-gather | bytes 4608 | tf_op jit(solution)/shard_map/all_gather | solution.py:263
  30.7 5.2 %all-gather.1 = s32[32,1,128]{2,1,0:T(1,128)S(1)} all-gather(s32[8,1,128]{2,1,0:T(1,128)S(1)} %all-gather.2), channel_id=3, replica_groups=mesh['pool'=4,'dp'=8] {'pool'}, dimensions={0}, use_global_device_ids=true | all-gather | bytes 20480 | tf_op jit(solution)/shard_map/all_gather | solution.py:264
  36.0 1.3 collective-permute-start.3
  37.4 0.3 convert_reduce_fusion.4
  37.8 0.6 convert_reduce_fusion.1
  38.6 1.3 collective-permute-start.5
  39.8 0.2 select_reduce_fusion
  40.1 0.8 collective-permute-done.3.refs_3_
  40.9 3.2 %shard_map.138 = bf16[8,64,512]{2,1,0:T(8,128)(2,1)} custom-call(s32[9]{0:T(128)S(1)} %pad_add_fusion.2.meta, bf16[16,64,512]{2,1,0:T(8,128)(2,1)S(1)} %get-tuple-element.26.refs_0_, bf16[16,64,512]{2,1,0:T(8,128)(2,1)} %collective-permute-done.refs_1_, bf16[16,64,512]{2,1,0:T(8,128)(2,1)} %collective-permute-done.2.refs_2_, ...), custom_call_target="tpu_custom_call" | custom-call | tf_op jit(solution)/shard_map/pallas_call | solution.py:189
  44.1 3.5 %all-to-all-start = ((bf16[8,64,512]{2,1,0:T(8,128)(2,1)}), bf16[8,64,512]{2,1,0:T(8,128)(2,1)S(1)}, u32[]{:S(2)}, u32[]{:S(2)}) async-start(bf16[8,64,512]{2,1,0:T(8,128)(2,1)} %shard_map.138), calls=%async_computation | async-start | bytes 1048576 | tf_op jit(solution)/shard_map/all_to_all | solution.py:298
  47.6 0.1 copy.58
  47.8 1.8 %copy.57 = bf16[256,512]{0,1:T(8,128)(2,1)} copy(bf16[256,512]{1,0:T(8,128)(2,1)} %rest_10_.1) | data formatting | bytes 524288 | tf_op args[9]
  49.6 6.4 %copy.56 = bf16[512,4096]{0,1:T(8,128)(2,1)} copy(bf16[512,4096]{1,0:T(8,128)(2,1)} %rest_11_.1) | data formatting | bytes 8388608 | tf_op args[10]
  56.0 2.9 %shard_map.139 = bf16[8,64,512]{2,1,0:T(8,128)(2,1)} custom-call(s32[9]{0:T(128)S(1)} %pad_add_fusion.2.meta, bf16[16,64,512]{2,1,0:T(8,128)(2,1)S(1)} %get-tuple-element.25.refs_0_, bf16[16,64,512]{2,1,0:T(8,128)(2,1)S(1)} %collective-permute-done.1.refs_1_, bf16[16,64,512]{2,1,0:T(8,128)(2,1)} %collective-permute-done.4.refs_2_, ...), custom_call_target="tpu_custom_call" | custom-call | tf_op jit(solution)/shard_map/pallas_call | solution.py:189
  58.9 3.1 %all-to-all-done.refs_0_.rest_0_ = bf16[8,64,512]{2,1,0:T(8,128)(2,1)S(1)} async-done(((bf16[8,64,512]{2,1,0:T(8,128)(2,1)}), bf16[8,64,512]{2,1,0:T(8,128)(2,1)S(1)}, u32[]{:S(2)}, u32[]{:S(2)}) %all-to-all-start) | async-done | bytes 524320 | tf_op jit(solution)/shard_map/all_to_all | solution.py:298
  62.0 4.9 %all-to-all-start.1 = ((bf16[8,64,512]{2,1,0:T(8,128)(2,1)}), bf16[8,64,512]{2,1,0:T(8,128)(2,1)S(1)}, u32[]{:S(2)}, u32[]{:S(2)}) async-start(bf16[8,64,512]{2,1,0:T(8,128)(2,1)} %shard_map.139), calls=%async_computation.1 | async-start | bytes 1048576 | tf_op jit(solution)/shard_map/all_to_all | solution.py:298
  67.4 0.5 broadcast.432
  67.9 0.7 fusion.32
  68.9 0.6 shard_map.140
  69.5 0.3 collective-permute-start.8
  69.7 12.0 %all-to-all-done.1.refs_0_.rest_1_ = bf16[8,64,512]{2,1,0:T(8,128)(2,1)S(1)} async-done(((bf16[8,64,512]{2,1,0:T(8,128)(2,1)}), bf16[8,64,512]{2,1,0:T(8,128)(2,1)S(1)}, u32[]{:S(2)}, u32[]{:S(2)}) %all-to-all-start.1) | async-done | bytes 524320 | tf_op jit(solution)/shard_map/all_to_all | solution.py:298
  81.7 0.6 shard_map.141
  82.3 0.2 collective-permute-start.9
  82.7 0.5 collective-permute-start.7
  83.2 0.2 select_reduce_fusion.1
  83.4 0.1 collective-permute-start.10
  83.5 0.7 copy-done.8
  84.2 5.1 %collective-permute-done.9.rest_5_ = bf16[4,64,512]{2,1,0:T(8,128)(2,1)} collective-permute-done((bf16[4,64,512]{2,1,0:T(8,128)(2,1)S(1)}, bf16[4,64,512]{2,1,0:T(8,128)(2,1)}, u32[]{:S(2)}, u32[]{:S(2)}) %collective-permute-start.9) | collective-permute-done | bytes 262176 | tf_op jit(solution)/shard_map/ppermute | solution.py:250
  89.5 0.7 copy-done.10
  90.2 0.8 copy-done.6
  91.1 0.7 copy-done.12
  91.8 2.2 %copy-done = bf16[512,4096]{1,0:T(8,128)(2,1)S(1)} copy-done((bf16[512,4096]{1,0:T(8,128)(2,1)S(1)}, bf16[512,4096]{1,0:T(8,128)(2,1)}, u32[]{:S(2)}) %copy-start) | copy-done | bytes 4194328
  94.0 0.9 copy-done.3
  95.0 1.2 copy-done.4
  96.2 1.2 copy-done.5
  97.4 1.0 copy-done.7
  98.5 0.9 copy-done.9
  99.4 0.9 copy-done.11
  100.4 0.9 copy-done.13
  101.3 34.9 %shard_map.142 = (bf16[256,2048]{1,0:T(8,128)(2,1)}, bf16[256,2048]{1,0:T(8,128)(2,1)}, f32[4,512]{1,0:T(4,128)}, bf16[512,512]{1,0:T(8,128)(2,1)S(1)}) custom-call(s32[25]{0:T(128)S(1)} %pad_add_fusion.1.meta, bf16[256,2048]{1,0:T(8,128)(2,1)S(1)} %bitcast.43, bf16[256,2048]{1,0:T(8,128)(2,1)S(1)} %bitcast.44, f32[4,512]{1,0:T(4,128)S(1)} %bitcast_convert_fusion.cond_ref, ...), custom_call_target="tpu_custom_call" | custom-call | flops 11811160064 | bytes 16777216 | tf_op jit(solution)/shard_map/pallas_call | solution.py:144
  136.2 11.2 %all_to_all.28 = bf16[4,128,512]{2,1,0:T(8,128)(2,1)S(1)} all-to-all(bf16[4,128,512]{2,1,0:T(8,128)(2,1)S(1)} %bitcast.40), channel_id=1, replica_groups=mesh['pool'=4,'dp'=8] {'pool'}, dimensions={0} | all-to-all | bytes 1048576 | tf_op jit(solution)/shard_map/all_to_all | solution.py:336
  147.6 12.1 %all_to_all.29 = bf16[8,16,512]{2,1,0:T(8,128)(2,1)S(1)} all-to-all(bf16[8,16,512]{2,1,0:T(8,128)(2,1)S(1)} %bitcast.48), channel_id=1, replica_groups=mesh['pool'=4,'dp'=8] {'dp'}, dimensions={0} | all-to-all | bytes 262144 | tf_op jit(solution)/shard_map/all_to_all | solution.py:336
  159.7 0.6 convert_reduce_fusion
  (79 shorter events, 2.3 us)
Async XLA Ops:
  0.6 7.5 %copy-start.16 = (s32[1,1,4,2]{2,3,1,0:T(2,128)S(1)}, s32[1,1,4,2]{2,3,1,0:T(2,128)}, u32[]{:S(2)}) copy-start(s32[1,1,4,2]{2,3,1,0:T(2,128)} %param.14) | copy-start | bytes 100
  0.6 7.6 %copy-start.17 = (s32[1,1,4,2]{2,3,1,0:T(2,128)S(1)}, s32[1,1,4,2]{2,3,1,0:T(2,128)}, u32[]{:S(2)}) copy-start(s32[1,1,4,2]{2,3,1,0:T(2,128)} %param.15) | copy-start | bytes 100
  0.7 7.8 %copy-start.18 = (s32[1,1,16]{2,1,0:T(1,128)S(1)}, s32[1,1,16]{2,1,0:T(1,128)}, u32[]{:S(2)}) copy-start(s32[1,1,16]{2,1,0:T(1,128)} %param.17) | copy-start | bytes 196
  0.7 47.0 %copy-start.1 = (bf16[512,256]{1,0:T(8,128)(2,1)S(1)}, bf16[512,256]{1,0:T(8,128)(2,1)}, u32[]{:S(2)}) copy-start(bf16[512,256]{1,0:T(8,128)(2,1)} %rest_9_.1) | copy-start | bytes 786436
  2.4 33.5 %collective-permute-start.1 = (bf16[16,64,512]{2,1,0:T(8,128)(2,1)S(1)}, bf16[16,64,512]{2,1,0:T(8,128)(2,1)S(1)}, u32[]{:S(2)}, u32[]{:S(2)}) collective-permute-start(bf16[16,64,512]{2,1,0:T(8,128)(2,1)S(1)} %get-tuple-element.25.refs_0_), channel_id=1, source_target_pairs={{24,8},{25,9},{26,10},{27,11},{28,12},{29,13},{30,14},{31,15}} | collective-permute-start | bytes 3145736 | tf_op jit(solution)/shard_map/ppermute | solution.py:250
  3.2 32.8 %collective-permute-start = (bf16[16,64,512]{2,1,0:T(8,128)(2,1)S(1)}, bf16[16,64,512]{2,1,0:T(8,128)(2,1)}, u32[]{:S(2)}, u32[]{:S(2)}) collective-permute-start(bf16[16,64,512]{2,1,0:T(8,128)(2,1)S(1)} %get-tuple-element.26.refs_0_), channel_id=1, source_target_pairs={{24,8},{25,9},{26,10},{27,11},{28,12},{29,13},{30,14},{31,15}} | collective-permute-start | bytes 3145736 | tf_op jit(solution)/shard_map/ppermute | solution.py:250
  4.8 51.2 %collective-permute-start.4 = (bf16[16,64,512]{2,1,0:T(8,128)(2,1)S(1)}, bf16[16,64,512]{2,1,0:T(8,128)(2,1)}, u32[]{:S(2)}, u32[]{:S(2)}) collective-permute-start(bf16[16,64,512]{2,1,0:T(8,128)(2,1)S(1)} %get-tuple-element.25.refs_0_), channel_id=1, source_target_pairs={{24,16},{25,17},{26,18},{27,19},{28,20},{29,21},{30,22},{31,23}} | collective-permute-start | bytes 3145736 | tf_op jit(solution)/shard_map/ppermute | solution.py:250
  6.4 33.7 %collective-permute-start.2 = (bf16[16,64,512]{2,1,0:T(8,128)(2,1)S(1)}, bf16[16,64,512]{2,1,0:T(8,128)(2,1)}, u32[]{:S(2)}, u32[]{:S(2)}) collective-permute-start(bf16[16,64,512]{2,1,0:T(8,128)(2,1)S(1)} %get-tuple-element.26.refs_0_), channel_id=1, source_target_pairs={{24,16},{25,17},{26,18},{27,19},{28,20},{29,21},{30,22},{31,23}} | collective-permute-start | bytes 3145736 | tf_op jit(solution)/shard_map/ppermute | solution.py:250
  36.0 4.9 %collective-permute-start.3 = (bf16[16,64,512]{2,1,0:T(8,128)(2,1)}, bf16[16,64,512]{2,1,0:T(8,128)(2,1)}, u32[]{:S(2)}, u32[]{:S(2)}) collective-permute-start(bf16[16,64,512]{2,1,0:T(8,128)(2,1)} %collective-permute-done.refs_1_), channel_id=1, source_target_pairs={{8,0},{9,1},{10,2},{11,3},{12,4},{13,5},{14,6},{15,7}} | collective-permute-start | bytes 3145736 | tf_op jit(solution)/shard_map/ppermute | solution.py:250
  38.6 17.5 %collective-permute-start.5 = (bf16[16,64,512]{2,1,0:T(8,128)(2,1)S(1)}, bf16[16,64,512]{2,1,0:T(8,128)(2,1)}, u32[]{:S(2)}, u32[]{:S(2)}) collective-permute-start(bf16[16,64,512]{2,1,0:T(8,128)(2,1)S(1)} %collective-permute-done.1.refs_1_), channel_id=1, source_target_pairs={{8,0},{9,1},{10,2},{11,3},{12,4},{13,5},{14,6},{15,7}} | collective-permute-start | bytes 3145736 | tf_op jit(solution)/shard_map/ppermute | solution.py:250
  44.1 17.9 %all-to-all-start = ((bf16[8,64,512]{2,1,0:T(8,128)(2,1)}), bf16[8,64,512]{2,1,0:T(8,128)(2,1)S(1)}, u32[]{:S(2)}, u32[]{:S(2)}) async-start(bf16[8,64,512]{2,1,0:T(8,128)(2,1)} %shard_map.138), calls=%async_computation | async-start | bytes 1048576 | tf_op jit(solution)/shard_map/all_to_all | solution.py:298
  56.0 10.9 %copy-start.15 = (bf16[1,1,4,512]{3,2,1,0:T(4,128)(2,1)S(1)}, bf16[1,1,4,512]{3,2,1,0:T(4,128)(2,1)}, u32[]{:S(2)}) copy-start(bf16[1,1,4,512]{3,2,1,0:T(4,128)(2,1)} %param.13) | copy-start | bytes 12292
  56.0 35.8 %copy-start.2 = (bf16[256,512]{1,0:T(8,128)(2,1)S(1)}, bf16[256,512]{1,0:T(8,128)(2,1)}, u32[]{:S(2)}) copy-start(bf16[256,512]{1,0:T(8,128)(2,1)} %rest_10_.1) | copy-start | bytes 786436
  56.0 35.8 %copy-start.14 = (f32[512]{0:T(512)S(1)}, f32[512]{0:T(512)}, u32[]{:S(2)}) copy-start(f32[512]{0:T(512)} %param.18) | copy-start | bytes 6148
  62.0 19.7 %all-to-all-start.1 = ((bf16[8,64,512]{2,1,0:T(8,128)(2,1)}), bf16[8,64,512]{2,1,0:T(8,128)(2,1)S(1)}, u32[]{:S(2)}, u32[]{:S(2)}) async-start(bf16[8,64,512]{2,1,0:T(8,128)(2,1)} %shard_map.139), calls=%async_computation.1 | async-start | bytes 1048576 | tf_op jit(solution)/shard_map/all_to_all | solution.py:298
  69.5 13.9 %collective-permute-start.8 = (bf16[4,64,512]{2,1,0:T(8,128)(2,1)S(1)}, bf16[4,64,512]{2,1,0:T(8,128)(2,1)S(1)}, u32[]{:S(2)}, u32[]{:S(2)}) collective-permute-start(bf16[4,64,512]{2,1,0:T(8,128)(2,1)S(1)} %shard_map.140), channel_id=1, source_target_pairs={{0,16},{1,17},{2,18},{3,19},{4,20},{5,21},{6,22},{7,23},{8,24},{9,... | collective-permute-start | bytes 786440 | tf_op jit(solution)/shard_map/ppermute | solution.py:250
  82.3 7.0 %collective-permute-start.9 = (bf16[4,64,512]{2,1,0:T(8,128)(2,1)S(1)}, bf16[4,64,512]{2,1,0:T(8,128)(2,1)}, u32[]{:S(2)}, u32[]{:S(2)}) collective-permute-start(bf16[4,64,512]{2,1,0:T(8,128)(2,1)S(1)} %shard_map.141), channel_id=1, source_target_pairs={{0,16},{1,17},{2,18},{3,19},{4,20},{5,21},{6,22},{7,23},{8,24},{9,... | collective-permute-start | bytes 786440 | tf_op jit(solution)/shard_map/ppermute | solution.py:250
  82.7 7.6 %collective-permute-start.6 = (bf16[8,64,512]{2,1,0:T(8,128)(2,1)S(1)}, bf16[8,64,512]{2,1,0:T(8,128)(2,1)S(1)}, u32[]{:S(2)}, u32[]{:S(2)}) collective-permute-start(bf16[8,64,512]{2,1,0:T(8,128)(2,1)S(1)} %all-to-all-done.refs_0_.rest_0_), channel_id=1, source_target_pairs={{0,8},{1,9},{2,10},{3,11},{4,12},{5,13},{6,14},{7,15},{8,0},{9,1},... | collective-permute-start | bytes 1572872 | tf_op jit(solution)/shard_map/ppermute | solution.py:250
  82.7 9.1 %collective-permute-start.7 = (bf16[8,64,512]{2,1,0:T(8,128)(2,1)S(1)}, bf16[8,64,512]{2,1,0:T(8,128)(2,1)}, u32[]{:S(2)}, u32[]{:S(2)}) collective-permute-start(bf16[8,64,512]{2,1,0:T(8,128)(2,1)S(1)} %all-to-all-done.1.refs_0_.rest_1_), channel_id=1, source_target_pairs={{0,8},{1,9},{2,10},{3,11},{4,12},{5,13},{6,14},{7,15},{8,0},{9,1},... | collective-permute-start | bytes 1572872 | tf_op jit(solution)/shard_map/ppermute | solution.py:250
  83.4 6.2 %collective-permute-start.10 = (bf16[4,64,512]{2,1,0:T(8,128)(2,1)S(1)}, bf16[4,64,512]{2,1,0:T(8,128)(2,1)S(1)}, u32[]{:S(2)}, u32[]{:S(2)}) collective-permute-start(bf16[4,64,512]{2,1,0:T(8,128)(2,1)S(1)} %collective-permute-done.8.rest_4_), channel_id=1, source_target_pairs={{0,8},{1,9},{2,10},{3,11},{4,12},{5,13},{6,14},{7,15},{8,0},{9,1},... | collective-permute-start | bytes 786440 | tf_op jit(solution)/shard_map/ppermute | solution.py:250
  83.5 0.7 copy-start.8
  89.3 1.7 %collective-permute-start.11 = (bf16[4,64,512]{2,1,0:T(8,128)(2,1)}, bf16[4,64,512]{2,1,0:T(8,128)(2,1)S(1)}, u32[]{:S(2)}, u32[]{:S(2)}) collective-permute-start(bf16[4,64,512]{2,1,0:T(8,128)(2,1)} %collective-permute-done.9.rest_5_), channel_id=1, source_target_pairs={{0,8},{1,9},{2,10},{3,11},{4,12},{5,13},{6,14},{7,15},{8,0},{9,1},... | collective-permute-start | bytes 786440 | tf_op jit(solution)/shard_map/ppermute | solution.py:250
  89.5 0.7 copy-start.10
  90.2 0.8 copy-start.6
  91.1 0.7 copy-start.12
  91.8 2.2 %copy-start = (bf16[512,4096]{1,0:T(8,128)(2,1)S(1)}, bf16[512,4096]{1,0:T(8,128)(2,1)}, u32[]{:S(2)}) copy-start(bf16[512,4096]{1,0:T(8,128)(2,1)} %rest_11_.1) | copy-start | bytes 12582916
  94.0 0.9 copy-start.3
  95.0 1.2 copy-start.4
  96.2 1.2 copy-start.5
  97.4 1.0 copy-start.7
  98.5 0.9 copy-start.9
  99.4 0.9 copy-start.11
  100.4 0.9 copy-start.13

commit v5 on v3

--- a/solution.py
+++ b/solution.py
@@ -24,53 +24,78 @@
     return lax.dot_general(a, b, dims, preferred_element_type=jnp.float32)
 
 
-def two_heads(rows):
-    blank = jnp.zeros((rows.shape[0], HEAD), rows.dtype)
-    return jnp.concatenate(
-        [
-            jnp.concatenate([rows[:, :HEAD], blank], axis=1),
-            jnp.concatenate([blank, rows[:, HEAD:]], axis=1),
-        ],
-        axis=0,
-    )
-
-
 def span_kernel(
     held_count, nbr_count, parts, meta,
-    q_ref, cot_ref, cond_ref, *rest,
+    q_ref, cot_ref, cond_ref, gain_ref, down_ref, up_ref, upt_ref, downt_ref, *rest,
 ):
     held_refs = rest[:held_count]
-    (gain_ref, down_ref, up_ref, kv_ref, kvt_ref, upt_ref, downt_ref,
-     out_ref, qg_ref, cg_ref, ad_ref, kvg_ref, acc_ref, raw_ref) = rest[held_count:]
+    (kv_hbm, kvt_hbm, out_ref, qg_ref, cg_ref, ad_ref,
+     raw_ref, kv_ref, kvt_ref, proj_ref, grad_ref, score_ref, dprob_ref, prob_ref, dscore_ref,
+     q2_ref, cot2_ref, acc_ref, sems, kv_sem) = rest[held_count:]
     span = pl.program_id(0)
-    per_device = pl.num_programs(0) * nbr_count
-    slot_len, width = raw_ref.shape[1:]
+    per_device, slot_len, width = raw_ref.shape
     key_count = nbr_count * slot_len
     head_cols = q_ref.shape[1]
     rank = down_ref.shape[1]
     scaling = HEAD ** (-0.5)
     live = meta[0] == 1
     lens, which, index = 1, 1 + per_device, 1 + 2 * per_device
+    piece = slot_len // parts
+    pairs = [pl.ds(i * 2 * HEAD, 2 * HEAD) for i in range(HEADS // 2)]
+    value_pairs = [pl.ds(head_cols + i * 2 * HEAD, 2 * HEAD) for i in range(HEADS // 2)]
+    lanes = [pl.ds(i * 2 * SPAN, 2 * SPAN) for i in range(HEADS // 2)]
+    kv_copy = pltpu.make_async_copy(kv_hbm, kv_ref, kv_sem.at[0])
+    kvt_copy = pltpu.make_async_copy(kvt_hbm, kvt_ref, kv_sem.at[1])
+
+    @pl.when(span == 0)
+    def _():
+        for n in range(per_device):
+            for b, held in enumerate(held_refs):
+                @pl.when(meta[which + n] == b // parts)
+                def _():
+                    part = b % parts
+                    pltpu.make_async_copy(
+                        held.at[meta[index + n]],
+                        raw_ref.at[n, pl.ds(part * piece, piece)],
+                        sems.at[n * parts + part],
+                    ).start()
+        kv_copy.start()
+        kvt_copy.start()
+
+    q2_ref[...] = jnp.zeros_like(q2_ref)
+    cot2_ref[...] = jnp.zeros_like(cot2_ref)
+    for i in range(HEADS):
+        cols = pl.ds(i * HEAD, HEAD)
+        tokens = pl.ds(i % 2 * SPAN, SPAN)
+        q2_ref[tokens, cols] = q_ref[:, cols]
+        cot2_ref[tokens, cols] = cot_ref[:, cols]
 
     for n in range(nbr_count):
-        item = span * nbr_count + n
-        for b, held in enumerate(held_refs):
-            part, source = b % parts, b // parts
-            piece = held.shape[1]
-
-            @pl.when(meta[which + item] == source)
-            def _():
-                raw_ref[n, part * piece : (part + 1) * piece] = held[meta[index + item]]
-
-    raw = raw_ref[...]
-    x_full = raw.reshape(key_count, width).astype(jnp.float32) + cond_ref[
-        pl.ds(span, 1), :
-    ]
+        for part in range(parts):
+            item = span * nbr_count + n
+            pltpu.make_async_copy(
+                held_refs[0].at[0],
+                raw_ref.at[item, pl.ds(part * piece, piece)],
+                sems.at[item * parts + part],
+            ).wait()
+    raw = raw_ref[pl.ds(span * nbr_count, nbr_count)]
+    x_full = raw.reshape(key_count, width).astype(jnp.float32) + cond_ref[pl.ds(span, 1), :]
     inv_rms = lax.rsqrt(jnp.mean(x_full * x_full, axis=-1, keepdims=True) + EPSILON)
     gain = gain_ref[...]
     hidden = (x_full * inv_rms * gain).astype(jnp.bfloat16)
     latent = dot(hidden, down_ref[...]).astype(jnp.bfloat16)
     encoded = (x_full + dot(latent, up_ref[...])).astype(jnp.bfloat16)
+
+    @pl.when(span == 0)
+    def _():
+        kv_copy.wait()
+
+    for cols in pairs + value_pairs:
+        proj_ref[:, cols] = dot(encoded, kv_ref[:, cols]).astype(jnp.bfloat16)
+
+    for cols, value_cols, lane in zip(pairs, value_pairs, lanes):
+        score_ref[:, lane] = dot(proj_ref[:, cols], q2_ref[:, cols], NT)
+        dprob_ref[:, lane] = dot(proj_ref[:, value_cols], cot2_ref[:, cols], NT)
 
     slot = lax.broadcasted_iota(jnp.int32, (key_count, 2 * SPAN), 0)
     limit = jnp.zeros((key_count, 2 * SPAN), jnp.int32)
@@ -78,37 +103,35 @@
         here = jnp.logical_and(slot >= n * slot_len, slot < (n + 1) * slot_len)
         limit = jnp.where(here, n * slot_len + meta[lens + span * nbr_count + n], limit)
     usable = slot < limit
-
-    for pair in range(HEADS // 2):
-        cols = pl.ds(pair * 2 * HEAD, 2 * HEAD)
-        vcols = pl.ds(head_cols + pair * 2 * HEAD, 2 * HEAD)
-        keys = dot(encoded, kv_ref[:, cols]).astype(jnp.bfloat16)
-        values = dot(encoded, kv_ref[:, vcols]).astype(jnp.bfloat16)
-        q2 = two_heads(q_ref[:, cols])
-        cot2 = two_heads(cot_ref[:, cols])
-        scores = jnp.where(usable, dot(keys, q2, NT), FLOOR)
+    for lane in lanes:
+        scores = jnp.where(usable, score_ref[:, lane], FLOOR)
         row_max = jnp.max(scores, axis=0, keepdims=True)
         raised = jnp.exp2((scores - row_max) * (scaling * LOG2E))
-        inv_sum = 1.0 / jnp.sum(raised, axis=0, keepdims=True)
-        probs = raised * inv_sum
-        probs_b = probs.astype(jnp.bfloat16)
-        d_probs = dot(values, cot2, NT)
+        probs = raised * (1.0 / jnp.sum(raised, axis=0, keepdims=True))
+        d_probs = dprob_ref[:, lane]
         delta = jnp.sum(probs * d_probs, axis=0, keepdims=True)
-        d_scores = (probs * (d_probs - delta) * scaling).astype(jnp.bfloat16)
-        kvg_ref[:, cols] = dot(d_scores, q2).astype(jnp.bfloat16)
-        kvg_ref[:, vcols] = dot(probs_b, cot2).astype(jnp.bfloat16)
-        probs_t = probs_b.T
-        d_scores_t = d_scores.T
-        outs, grads = [], []
-        for h in range(2):
-            lanes = slice(h * HEAD, (h + 1) * HEAD)
-            tokens = slice(h * SPAN, (h + 1) * SPAN)
-            outs.append(dot(probs_t[tokens], values[:, lanes]))
-            grads.append(dot(d_scores_t[tokens], keys[:, lanes]))
-        out_ref[:, cols] = jnp.where(live, jnp.concatenate(outs, axis=1), 0.0).astype(jnp.bfloat16)
-        qg_ref[:, cols] = jnp.where(live, jnp.concatenate(grads, axis=1), 0.0).astype(jnp.bfloat16)
-
-    enc_grad = dot(kvg_ref[...], kvt_ref[...]).astype(jnp.bfloat16)
+        prob_ref[:, lane] = probs.astype(jnp.bfloat16)
+        dscore_ref[:, lane] = (probs * (d_probs - delta) * scaling).astype(jnp.bfloat16)
+
+    for cols, value_cols, lane in zip(pairs, value_pairs, lanes):
+        grad_ref[:, cols] = dot(dscore_ref[:, lane], q2_ref[:, cols]).astype(jnp.bfloat16)
+        grad_ref[:, value_cols] = dot(prob_ref[:, lane], cot2_ref[:, cols]).astype(jnp.bfloat16)
+
+    def diagonal(both):
+        return jnp.concatenate([both[:SPAN, :HEAD], both[SPAN:, HEAD:]], axis=1)
+
+    for cols, value_cols, lane in zip(pairs, value_pairs, lanes):
+        out = diagonal(dot(prob_ref[:, lane].T, proj_ref[:, value_cols]))
+        grad = diagonal(dot(dscore_ref[:, lane].T, proj_ref[:, cols]))
+        out_ref[:, cols] = jnp.where(live, out, 0.0).astype(jnp.bfloat16)
+        qg_ref[:, cols] = jnp.where(live, grad, 0.0).astype(jnp.bfloat16)
+
+    @pl.when(span == 0)
+    def _():
+        kvt_copy.wait()
+        acc_ref[...] = jnp.zeros_like(acc_ref)
+
+    enc_grad = dot(grad_ref[...], kvt_ref[...]).astype(jnp.bfloat16)
     lat_grad = dot(enc_grad, upt_ref[...]).astype(jnp.bfloat16)
     scaled = dot(lat_grad, downt_ref[...]) * gain
     normed = x_full * inv_rms
@@ -117,11 +140,6 @@
     )
     span_grad = jnp.sum(x_grad, axis=0, keepdims=True)
     cg_ref[pl.ds(span, 1), :] = jnp.where(live, span_grad, 0.0)
-
-    @pl.when(span == 0)
-    def _():
-        acc_ref[...] = jnp.zeros_like(acc_ref)
-
     acc_ref[:, :rank] += dot(hidden, lat_grad, TN)
     acc_ref[:, rank:] += dot(enc_grad, latent, TN)
 
@@ -137,18 +155,21 @@
     rank = w_down.shape[1]
     whole = lambda a: pl.BlockSpec(a.shape, lambda s, m: (0,) * a.ndim, pipeline_mode=pl.Buffered(1))
     tokens = pl.BlockSpec((SPAN, head_cols), lambda s, m: (s, 0))
-    weights = [gain.reshape(1, width), w_down, w_up, w_kv, w_kv.T, w_up.T, w_down.T]
+    small = [cond, gain.reshape(1, width), w_down, w_up, w_up.T, w_down.T]
+    large = list(held) + [w_kv, w_kv.T]
     per_device = span_count * nbr_count
+    keys = nbr_count * slot_len
     rows = per_device * slot_len
+    lanes = SPAN * HEADS
     flops = 2 * rows * (2 * width * 2 * head_cols + 6 * width * rank + 6 * SPAN * head_cols)
     return pl.pallas_call(
         functools.partial(span_kernel, len(held), nbr_count, parts),
         grid_spec=pltpu.PrefetchScalarGridSpec(
             num_scalar_prefetch=1,
             grid=(span_count,),
-            in_specs=[tokens, tokens, whole(cond)]
-            + [pl.BlockSpec(memory_space=pltpu.VMEM)] * len(held)
-            + [whole(w) for w in weights],
+            in_specs=[tokens, tokens]
+            + [whole(a) for a in small]
+            + [pl.BlockSpec(memory_space=pltpu.HBM)] * len(large),
             out_specs=[
                 tokens,
                 tokens,
@@ -156,9 +177,20 @@
                 pl.BlockSpec((width, 2 * rank), lambda s, m: (0, 0)),
             ],
             scratch_shapes=[
-                pltpu.VMEM((nbr_count * slot_len, 2 * head_cols), jnp.bfloat16),
+                pltpu.VMEM((per_device, slot_len, width), jnp.bfloat16),
+                pltpu.VMEM((width, 2 * head_cols), jnp.bfloat16),
+                pltpu.VMEM((2 * head_cols, width), jnp.bfloat16),
+                pltpu.VMEM((keys, 2 * head_cols), jnp.bfloat16),
+                pltpu.VMEM((keys, 2 * head_cols), jnp.bfloat16),
+                pltpu.VMEM((keys, lanes), jnp.float32),
+                pltpu.VMEM((keys, lanes), jnp.float32),
+                pltpu.VMEM((keys, lanes), jnp.bfloat16),
+                pltpu.VMEM((keys, lanes), jnp.bfloat16),
+                pltpu.VMEM((2 * SPAN, head_cols), jnp.bfloat16),
+                pltpu.VMEM((2 * SPAN, head_cols), jnp.bfloat16),
                 pltpu.VMEM((width, 2 * rank), jnp.float32),
-                pltpu.VMEM((nbr_count, slot_len, width), jnp.bfloat16),
+                pltpu.SemaphoreType.DMA((per_device * parts,)),
+                pltpu.SemaphoreType.DMA((2,)),
             ],
         ),
         out_shape=[
@@ -167,20 +199,22 @@
             jax.ShapeDtypeStruct((span_count, width), jnp.float32),
             jax.ShapeDtypeStruct((width, 2 * rank), jnp.bfloat16),
         ],
-        compiler_params=pltpu.CompilerParams(vmem_limit_bytes=40 * 2**20),
+        compiler_params=pltpu.CompilerParams(vmem_limit_bytes=60 * 2**20),
         cost_estimate=pl.CostEstimate(
             flops=flops, bytes_accessed=16 * 2**20, transcendentals=rows * SPAN * HEADS
         ),
-    )(meta, query, cot, cond, *held, *weights)
+    )(meta, query, cot, *small, *large)
 
 
 def pick_kernel(held_count, meta, *refs):
-    held_refs, out_ref = refs[:held_count], refs[held_count]
+    held_refs, out_ref, sems = refs[:held_count], refs[held_count], refs[held_count + 1]
     for b, held in enumerate(held_refs):
         @pl.when(meta[0] == b)
         def _():
             for n in range(out_ref.shape[0]):
-                out_ref[n] = held[meta[1 + n]]
+                pltpu.make_async_copy(held.at[meta[1 + n]], out_ref.at[n], sems.at[n]).start()
+    for n in range(out_ref.shape[0]):
+        pltpu.make_async_copy(held_refs[0].at[0], out_ref.at[n], sems.at[n]).wait()
 
 
 def pick(which, index, held):
@@ -191,11 +225,12 @@
         grid_spec=pltpu.PrefetchScalarGridSpec(
             num_scalar_prefetch=1,
             grid=(1,),
-            in_specs=[pl.BlockSpec(memory_space=pltpu.VMEM)] * len(held),
+            in_specs=[pl.BlockSpec(memory_space=pltpu.HBM)] * len(held),
             out_specs=pl.BlockSpec(memory_space=pltpu.VMEM),
+            scratch_shapes=[pltpu.SemaphoreType.DMA((count,))],
         ),
         out_shape=jax.ShapeDtypeStruct((count,) + held[0].shape[1:], held[0].dtype),
-        compiler_params=pltpu.CompilerParams(vmem_limit_bytes=24 * 2**20),
+        compiler_params=pltpu.CompilerParams(vmem_limit_bytes=60 * 2**20),
     )(meta, *held)
 
 
@@ -260,8 +295,7 @@
 
     info = jnp.concatenate([nbr_owner.reshape(-1), nbr_block.reshape(-1), lengths.reshape(-1)])
     info = jnp.pad(info, (0, -info.shape[0] % 128))
-    table = lax.all_gather(info.reshape(1, -1, 128), "dp", axis=0, tiled=True)
-    table = lax.all_gather(table.reshape(1, columns, -1, 128), "pool", axis=0, tiled=True)
+    table = lax.all_gather(info.reshape(1, -1, 128), axes, axis=0, tiled=True)
     across, table = lax.optimization_barrier((across, table))
     table = table.reshape(pool_count, columns, -1)
     by_column = jnp.swapaxes(table[:relay_row], 0, 1)

time: 154 us -> 190 us (1.23)
  blocking collectives: 50 us -> 95.2 us
  Pallas kernels: 39.2 us -> 33.6 us
  waiting for transfers between devices: 35.3 us -> 31.9 us
  local copies, waits for them, and re-layouts: 16.3 us -> 13.6 us
  other arithmetic: 3.91 us -> 6.02 us
    all_gather x2 -> x1, blocking collectives: 27.3 us -> 71.4 us  [body(): table = lax.all_gather(info.reshape(1, -1, 128), axes, axis=0, tiled=True)]
    pallas_call x1, Pallas kernels: 34.9 us -> 28 us  [run_spans(): pl.pallas_call(functools.partial(span_kernel, len(held), nbr_count, parts...]
    ppermute x6, waiting for transfers between devices: 10.6 us -> 7.66 us  [hop(): lax.ppermute(array, axes, [(a * columns + j, b * columns + j) for a, b in...]
    unnamed x22, local copies, waits for them, and re-layouts: 14.5 us -> 11.9 us
where the time goes in v5:
time: 190 us; the launch traced here: 189 us
  blocking collectives  95.2 us (50%)
  Pallas kernels  33.6 us (18%)
  waiting for transfers between devices  31.9 us (17%)
  local copies, waits for them, and re-layouts  13.6 us (7%)
  starting transfers between devices  7.89 us (4%)
  other arithmetic  6.02 us (3%)
    all_gather x1, blocking collectives, body(): table = lax.all_gather(info.reshape(1, -1, 128), axes, axis=0, tiled=True)  71.4 us
    pallas_call x1, Pallas kernels, run_spans(): pl.pallas_call(functools.partial(span_kernel, len(held), nbr_count, parts...  28 us
    all_to_all x1, waiting for transfers between devices, body(): lax.all_to_all(sends, 'dp', split_axis=0, concat_axis=0, tiled=True)  24.2 us
    all_to_all x2, blocking collectives, scatter_sum(): parts = lax.all_to_all(array, axis, split_axis=0, concat_axis=0, tiled=True)  23.8 us
    unnamed x22, local copies, waits for them, and re-layouts  11.9 us
    ppermute x6, waiting for transfers between devices, hop(): lax.ppermute(array, axes, [(a * columns + j, b * columns + j) for a, b in...  7.66 us
    pallas_call x2, Pallas kernels, pick(): pl.pallas_call(functools.partial(pick_kernel, len(held)), grid_spec=pltpu...  5.63 us
    ppermute x6, starting transfers between devices, hop(): lax.ppermute(array, axes, [(a * columns + j, b * columns + j) for a, b in...  4.18 us
  transfers between devices with their start and end apart: 7, of which 4 were waited for; matrix products, arithmetic and copies ran while one was open for 9% of the time, Pallas kernels for 0%

profile of v5, /device:TPU:0, one launch (start us, length us, event | category | flops | bytes accessed | tf_op | source)
XLA Modules:
  0.0 189.1 jit_solution(14461060090102309649)
XLA Ops:
  0.6 0.8 collective-permute-start
  1.4 2.0 %collective-permute-start.1 = (bf16[16,128,512]{2,1,0:T(8,128)(2,1)}, bf16[16,128,512]{2,1,0:T(8,128)(2,1)}, u32[]{:S(2)}, u32[]{:S(2)}) collective-permute-start(bf16[16,128,512]{2,1,0:T(8,128)(2,1)} %bitcast.42), channel_id=1, source_target_pairs={{24,16},{25,17},{26,18},{27,19},{28,20},{29,21},{30,22},{31,23}} | collective-permute-start | bytes 6291464 | tf_op jit(solution)/shard_map/ppermute | solution.py:285
  3.4 0.8 copy.49
  4.2 0.1 reshape.299
  4.2 0.8 copy.50
  5.0 0.1 reshape.300
  5.1 0.7 pad_add_fusion
  5.8 71.4 %all-gather.1 = s32[32,1,128]{2,1,0:T(1,128)S(1)} all-gather(s32[1,1,128]{2,1,0:T(1,128)S(1)} %pad_bitcast_fusion), channel_id=2, replica_groups=mesh['pool'=4,'dp'=8] {'pool','dp'}, dimensions={0}, use_global_device_ids=true | all-gather | bytes 16896 | tf_op jit(solution)/shard_map/all_gather | solution.py:298
  77.2 1.3 collective-permute-start.2
  78.7 0.1 reshape.303
  78.8 0.3 convert_reduce_fusion.4
  79.1 0.1 ge.13
  79.2 0.6 convert_reduce_fusion.1
  79.7 0.1 reduce_sum.91
  79.9 0.2 select_reduce_fusion
  80.1 0.6 pad_add_fusion.2.meta
  80.7 2.7 %collective-permute-done.2.refs_3_ = bf16[16,128,512]{2,1,0:T(8,128)(2,1)} collective-permute-done((bf16[16,128,512]{2,1,0:T(8,128)(2,1)S(1)}, bf16[16,128,512]{2,1,0:T(8,128)(2,1)}, u32[]{:S(2)}, u32[]{:S(2)}) %collective-permute-start.2) | collective-permute-done | bytes 2097184 | tf_op jit(solution)/shard_map/ppermute | solution.py:285
  83.4 3.0 %shard_map.138 = bf16[8,128,512]{2,1,0:T(8,128)(2,1)} custom-call(s32[9]{0:T(128)} %pad_add_fusion.2.meta, bf16[16,128,512]{2,1,0:T(8,128)(2,1)} %bitcast.43, bf16[16,128,512]{2,1,0:T(8,128)(2,1)} %copy-done.1, bf16[16,128,512]{2,1,0:T(8,128)(2,1)} %collective-permute-done.1.refs_2_, bf16[16,128,512]{2,1,0:T(8,128)(2,1)} %collective-permute-done.2.refs_3_), custom_call_target="tpu_custom_call" | custom-call | tf_op jit(solution)/shard_map/pallas_call | solution.py:223
  86.5 3.7 %all-to-all-start = ((bf16[8,128,512]{2,1,0:T(8,128)(2,1)}), bf16[8,128,512]{2,1,0:T(8,128)(2,1)S(1)}, u32[]{:S(2)}, u32[]{:S(2)}) async-start(bf16[8,128,512]{2,1,0:T(8,128)(2,1)} %shard_map.138), calls=%async_computation | async-start | bytes 2097152 | tf_op jit(solution)/shard_map/all_to_all | solution.py:332
  90.2 0.1 reshape.304
  90.3 0.5 broadcast.432
  90.8 0.7 fusion.32
  91.5 0.1 select_reduce_fusion.2
  91.6 0.6 pad_add_fusion.3.meta
  92.2 24.2 %all-to-all-done.refs_0_.rest_0_ = bf16[8,128,512]{2,1,0:T(8,128)(2,1)S(1)} async-done(((bf16[8,128,512]{2,1,0:T(8,128)(2,1)}), bf16[8,128,512]{2,1,0:T(8,128)(2,1)S(1)}, u32[]{:S(2)}, u32[]{:S(2)}) %all-to-all-start) | async-done | bytes 1048608 | tf_op jit(solution)/shard_map/all_to_all | solution.py:332
  116.4 1.0 copy-done
  117.4 2.6 %shard_map.139 = bf16[4,128,512]{2,1,0:T(8,128)(2,1)} custom-call(s32[5]{0:T(128)} %pad_add_fusion.3.meta, bf16[8,128,512]{2,1,0:T(8,128)(2,1)} %copy-done), custom_call_target="tpu_custom_call" | custom-call | tf_op jit(solution)/shard_map/pallas_call | solution.py:223
  120.2 0.9 copy.55
  121.1 0.8 copy.54
  121.9 6.5 %copy.60 = bf16[512,4096]{0,1:T(8,128)(2,1)} copy(bf16[512,4096]{1,0:T(8,128)(2,1)} %rest_4_.1) | data formatting | bytes 8388608 | tf_op args[10]
  128.4 0.6 bitcast_convert_fusion.cond_ref
  129.1 0.1 broadcast_in_dim.82
  129.2 0.1 squeeze.25
  129.2 0.1 squeeze.26
  129.3 0.1 squeeze.28
  129.4 0.1 add.147
  129.5 3.9 %collective-permute-done.4.rest_2_ = bf16[4,128,512]{2,1,0:T(8,128)(2,1)S(1)} collective-permute-done((bf16[4,128,512]{2,1,0:T(8,128)(2,1)}, bf16[4,128,512]{2,1,0:T(8,128)(2,1)S(1)}, u32[]{:S(2)}, u32[]{:S(2)}) %collective-permute-start.4) | collective-permute-done | bytes 524320 | tf_op jit(solution)/shard_map/ppermute | solution.py:285
  133.4 0.2 select_reduce_fusion.1
  133.6 0.1 reshape.306
  133.7 0.6 pad_add_fusion.1.meta
  134.3 1.0 collective-permute-done.5.rest_3_
  135.3 0.8 copy-done.7
  136.1 0.4 copy-done.5
  136.5 28.0 %shard_map.140 = (bf16[256,2048]{1,0:T(8,128)(2,1)}, bf16[256,2048]{1,0:T(8,128)(2,1)}, f32[4,512]{1,0:T(4,128)}, bf16[512,512]{1,0:T(8,128)(2,1)}) custom-call(s32[25]{0:T(128)} %pad_add_fusion.1.meta, bf16[256,2048]{1,0:T(8,128)(2,1)} %bitcast.53, bf16[256,2048]{1,0:T(8,128)(2,1)} %bitcast.54, f32[4,512]{1,0:T(4,128)} %bitcast_convert_fusion.cond_ref, ...), custom_call_target="tpu_custom_call" | custom-call | flops 11811160064 | bytes 16777216 | tf_op jit(solution)/shard_map/pallas_call | solution.py:165
  164.5 12.3 %all_to_all.23 = bf16[4,128,512]{2,1,0:T(8,128)(2,1)S(1)} all-to-all(bf16[4,128,512]{2,1,0:T(8,128)(2,1)} %bitcast.44), channel_id=1, replica_groups=mesh['pool'=4,'dp'=8] {'pool'}, dimensions={0} | all-to-all | bytes 1048576 | tf_op jit(solution)/shard_map/all_to_all | solution.py:370
  176.8 0.1 reduce_sum.94
  176.9 11.5 %all_to_all.24 = bf16[8,16,512]{2,1,0:T(8,128)(2,1)S(1)} all-to-all(bf16[8,16,512]{2,1,0:T(8,128)(2,1)S(1)} %bitcast.45), channel_id=1, replica_groups=mesh['pool'=4,'dp'=8] {'dp'}, dimensions={0} | all-to-all | bytes 262144 | tf_op jit(solution)/shard_map/all_to_all | solution.py:370
  188.4 0.6 convert_reduce_fusion
  (39 shorter events, 0.6 us)
Async XLA Ops:
  0.6 76.6 %collective-permute-start = (bf16[16,128,512]{2,1,0:T(8,128)(2,1)}, bf16[16,128,512]{2,1,0:T(8,128)(2,1)S(1)}, u32[]{:S(2)}, u32[]{:S(2)}) collective-permute-start(bf16[16,128,512]{2,1,0:T(8,128)(2,1)} %bitcast.41), channel_id=1, source_target_pairs={{24,8},{25,9},{26,10},{27,11},{28,12},{29,13},{30,14},{31,15}} | collective-permute-start | bytes 6291464 | tf_op jit(solution)/shard_map/ppermute | solution.py:285
  1.4 79.3 %collective-permute-start.1 = (bf16[16,128,512]{2,1,0:T(8,128)(2,1)}, bf16[16,128,512]{2,1,0:T(8,128)(2,1)}, u32[]{:S(2)}, u32[]{:S(2)}) collective-permute-start(bf16[16,128,512]{2,1,0:T(8,128)(2,1)} %bitcast.42), channel_id=1, source_target_pairs={{24,16},{25,17},{26,18},{27,19},{28,20},{29,21},{30,22},{31,23}} | collective-permute-start | bytes 6291464 | tf_op jit(solution)/shard_map/ppermute | solution.py:285
  77.2 6.2 %copy-start.1 = (bf16[16,128,512]{2,1,0:T(8,128)(2,1)}, bf16[16,128,512]{2,1,0:T(8,128)(2,1)S(1)}, u32[]{:S(2)}) copy-start(bf16[16,128,512]{2,1,0:T(8,128)(2,1)S(1)} %collective-permute-done.refs_1_) | copy-start | bytes 6291460
  77.2 6.2 %collective-permute-start.2 = (bf16[16,128,512]{2,1,0:T(8,128)(2,1)S(1)}, bf16[16,128,512]{2,1,0:T(8,128)(2,1)}, u32[]{:S(2)}, u32[]{:S(2)}) collective-permute-start(bf16[16,128,512]{2,1,0:T(8,128)(2,1)S(1)} %collective-permute-done.refs_1_), channel_id=1, source_target_pairs={{8,0},{9,1},{10,2},{11,3},{12,4},{13,5},{14,6},{15,7}} | collective-permute-start | bytes 6291464 | tf_op jit(solution)/shard_map/ppermute | solution.py:285
  86.4 33.8 %copy-start.2 = (bf16[512,256]{1,0:T(8,128)(2,1)S(1)}, bf16[512,256]{1,0:T(8,128)(2,1)}, u32[]{:S(2)}) copy-start(bf16[512,256]{1,0:T(8,128)(2,1)} %down_ref.1) | copy-start | bytes 786436
  86.4 34.6 %copy-start.3 = (bf16[256,512]{1,0:T(8,128)(2,1)S(1)}, bf16[256,512]{1,0:T(8,128)(2,1)}, u32[]{:S(2)}) copy-start(bf16[256,512]{1,0:T(8,128)(2,1)} %up_ref.1) | copy-start | bytes 786436
  86.5 30.0 %all-to-all-start = ((bf16[8,128,512]{2,1,0:T(8,128)(2,1)}), bf16[8,128,512]{2,1,0:T(8,128)(2,1)S(1)}, u32[]{:S(2)}, u32[]{:S(2)}) async-start(bf16[8,128,512]{2,1,0:T(8,128)(2,1)} %shard_map.138), calls=%async_computation | async-start | bytes 2097152 | tf_op jit(solution)/shard_map/all_to_all | solution.py:332
  116.4 1.0 copy-start
  120.0 13.4 %collective-permute-start.4 = (bf16[4,128,512]{2,1,0:T(8,128)(2,1)}, bf16[4,128,512]{2,1,0:T(8,128)(2,1)S(1)}, u32[]{:S(2)}, u32[]{:S(2)}) collective-permute-start(bf16[4,128,512]{2,1,0:T(8,128)(2,1)} %shard_map.139), channel_id=1, source_target_pairs={{0,16},{1,17},{2,18},{3,19},{4,20},{5,21},{6,22},{7,23},{8,24},{9,... | collective-permute-start | bytes 1572872 | tf_op jit(solution)/shard_map/ppermute | solution.py:285
  120.1 15.2 %collective-permute-start.3 = (bf16[8,128,512]{2,1,0:T(8,128)(2,1)}, bf16[8,128,512]{2,1,0:T(8,128)(2,1)S(1)}, u32[]{:S(2)}, u32[]{:S(2)}) collective-permute-start(bf16[8,128,512]{2,1,0:T(8,128)(2,1)} %copy-done), channel_id=1, source_target_pairs={{0,8},{1,9},{2,10},{3,11},{4,12},{5,13},{6,14},{7,15},{8,0},{9,1},... | collective-permute-start | bytes 3145736 | tf_op jit(solution)/shard_map/ppermute | solution.py:285
  121.9 6.5 %copy-start.4 = (bf16[1,1,4,512]{3,2,1,0:T(4,128)(2,1)S(1)}, bf16[1,1,4,512]{3,2,1,0:T(4,128)(2,1)}, u32[]{:S(2)}) copy-start(bf16[1,1,4,512]{3,2,1,0:T(4,128)(2,1)} %param.13) | copy-start | bytes 12292
  133.4 1.9 %copy-start.6 = (bf16[4,128,512]{2,1,0:T(8,128)(2,1)}, bf16[4,128,512]{2,1,0:T(8,128)(2,1)S(1)}, u32[]{:S(2)}) copy-start(bf16[4,128,512]{2,1,0:T(8,128)(2,1)S(1)} %collective-permute-done.4.rest_2_) | copy-start | bytes 1572868
  133.4 1.9 %collective-permute-start.5 = (bf16[4,128,512]{2,1,0:T(8,128)(2,1)S(1)}, bf16[4,128,512]{2,1,0:T(8,128)(2,1)S(1)}, u32[]{:S(2)}, u32[]{:S(2)}) collective-permute-start(bf16[4,128,512]{2,1,0:T(8,128)(2,1)S(1)} %collective-permute-done.4.rest_2_), channel_id=1, source_target_pairs={{0,8},{1,9},{2,10},{3,11},{4,12},{5,13},{6,14},{7,15},{8,0},{9,1},... | collective-permute-start | bytes 1572872 | tf_op jit(solution)/shard_map/ppermute | solution.py:285
  135.3 0.8 copy-start.7
  135.3 1.2 copy-start.5

commit v6 on v5

--- a/solution.py
+++ b/solution.py
@@ -10,7 +10,7 @@
 HEADS = 16
 HEAD = 128
 SPAN = 64
-PARTS = 1
+PARTS = 2
 
 EPSILON = 1e-06
 FLOOR = -1e30
@@ -197,7 +197,7 @@
             jax.ShapeDtypeStruct((token_count, head_cols), jnp.bfloat16),
             jax.ShapeDtypeStruct((token_count, head_cols), jnp.bfloat16),
             jax.ShapeDtypeStruct((span_count, width), jnp.float32),
-            jax.ShapeDtypeStruct((width, 2 * rank), jnp.bfloat16),
+            jax.ShapeDtypeStruct((width, 2 * rank), jnp.float32),
         ],
         compiler_params=pltpu.CompilerParams(vmem_limit_bytes=60 * 2**20),
         cost_estimate=pl.CostEstimate(
@@ -253,6 +253,34 @@
     lane = jnp.where(crosses, number, first + guests + rank) % lanes
     row = jnp.where(crosses, 1 - side[None, :], side[None, :]) * half + lane % half
     return row, lane // half, crosses, number // half
+
+
+def scatter_sum(total, axes):
+    width = total.shape[1]
+    sizes = [lax.axis_size(axis) for axis in axes]
+    total = total.reshape(tuple(sizes) + (-1, width)).astype(jnp.float32)
+    for at, axis in enumerate(axes):
+        size, index = sizes[at], lax.axis_index(axis)
+        if size & (size - 1):
+            lead = (size,) + tuple(d for i, d in enumerate(total.shape) if i != at)
+            parts = jnp.moveaxis(total, at, 0).astype(jnp.bfloat16)
+            parts = lax.all_to_all(parts, axis, split_axis=0, concat_axis=0, tiled=True)
+            total = jnp.sum(parts.reshape(lead).astype(jnp.float32), axis=0)
+            total = jnp.expand_dims(total, at)
+            continue
+        bit = 1
+        while bit < size:
+            shape = total.shape
+            split = total.reshape(shape[:at] + (shape[at] // 2, 2) + shape[at + 1 :])
+            mine = (index // bit) % 2
+            keep = lax.dynamic_index_in_dim(split, mine, at + 1, keepdims=False)
+            give = lax.dynamic_index_in_dim(split, 1 - mine, at + 1, keepdims=False)
+            got = lax.ppermute(
+                give.astype(jnp.bfloat16), axis, [(i, i ^ bit) for i in range(size)]
+            )
+            total = keep + got.astype(jnp.float32)
+            bit *= 2
+    return total.reshape(-1, width)
 
 
 def body(
@@ -291,11 +319,15 @@
     full_store = database.reshape(block_count, slot_len, width)
     store = [full_store[:, i * piece : (i + 1) * piece] for i in range(parts)]
 
+    def to_all(array, axis):
+        copies = jnp.broadcast_to(array[None], (lax.axis_size(axis),) + array.shape)
+        return lax.all_to_all(copies, axis, split_axis=0, concat_axis=0, tiled=True)
+
     across = [hop(a, [(relay_row, relay_row - half)]) for a in store]
 
     info = jnp.concatenate([nbr_owner.reshape(-1), nbr_block.reshape(-1), lengths.reshape(-1)])
     info = jnp.pad(info, (0, -info.shape[0] % 128))
-    table = lax.all_gather(info.reshape(1, -1, 128), axes, axis=0, tiled=True)
+    table = to_all(to_all(info.reshape(-1, 128), "dp"), "pool")
     across, table = lax.optimization_barrier((across, table))
     table = table.reshape(pool_count, columns, -1)
     by_column = jnp.swapaxes(table[:relay_row], 0, 1)
@@ -366,13 +398,7 @@
         nbr_count,
     )
 
-    def scatter_sum(array, axis):
-        parts = lax.all_to_all(array, axis, split_axis=0, concat_axis=0, tiled=True)
-        return jnp.sum(
-            parts.reshape(lax.axis_size(axis), -1, array.shape[1]).astype(jnp.float32), axis=0
-        )
-
-    adapter_grad = scatter_sum(scatter_sum(terms, "pool").astype(jnp.bfloat16), "dp")
+    adapter_grad = scatter_sum(terms, axes)
     return (
         attn_out.reshape(1, 1, token_count, head_cols),
         q_grad.reshape(1, 1, token_count, head_cols),

time: 190 us -> 147 us (0.77)
  blocking collectives: 95.2 us -> 0 us
  starting transfers between devices: 7.89 us -> 38.3 us
  waiting for transfers between devices: 31.9 us -> 45.1 us
  Pallas kernels: 33.6 us -> 38.5 us
  local copies, waits for them, and re-layouts: 13.6 us -> 16.1 us
    all_gather x1 -> x0, blocking collectives: 71.4 us -> none  [body(): table = lax.all_gather(info.reshape(1, -1, 128), axes, axis=0, tiled=True)]
    all_to_all x2 -> x0, blocking collectives: 23.8 us -> none  [scatter_sum(): parts = lax.all_to_all(array, axis, split_axis=0, concat_axis=0, tiled=True)]
    ppermute x0 -> x5, waiting for transfers between devices: none -> 13.5 us  [scatter_sum(): lax.ppermute(give.astype(jnp.bfloat16), axis, [(i, i ^ bit) for i in rang...]
    all_to_all x1 -> x2, waiting for transfers between devices: 24.2 us -> 12.5 us  [body(): lax.all_to_all(sends, 'dp', split_axis=0, concat_axis=0, tiled=True)]
    all_to_all x0 -> x2, starting transfers between devices: none -> 11.4 us  [to_all(): return lax.all_to_all(copies, axis, split_axis=0, concat_axis=0, tiled=True)]
    all_to_all x0 -> x2, waiting for transfers between devices: none -> 10.1 us  [to_all(): return lax.all_to_all(copies, axis, split_axis=0, concat_axis=0, tiled=True)]
    ppermute x0 -> x5, starting transfers between devices: none -> 6.72 us  [scatter_sum(): lax.ppermute(give.astype(jnp.bfloat16), axis, [(i, i ^ bit) for i in rang...]
    all_to_all x1 -> x2, starting transfers between devices: 3.7 us -> 10.2 us  [body(): lax.all_to_all(sends, 'dp', split_axis=0, concat_axis=0, tiled=True)]
  transfers between devices with their start and end apart: 7 -> 21, of which waited for: 4 -> 13; matrix products, arithmetic and copies ran while one was open for 9% -> 11% of each run, Pallas kernels for 0% -> 7%
where the time goes in v6:
time: 147 us; the launch traced here: 146 us
  waiting for transfers between devices  45.1 us (31%)
  Pallas kernels  38.5 us (26%)
  starting transfers between devices  38.3 us (26%)
  local copies, waits for them, and re-layouts  16.1 us (11%)
  other arithmetic  6.63 us (5%)
    pallas_call x1, Pallas kernels, run_spans(): pl.pallas_call(functools.partial(span_kernel, len(held), nbr_count, parts...  28.3 us
    ppermute x5, waiting for transfers between devices, scatter_sum(): lax.ppermute(give.astype(jnp.bfloat16), axis, [(i, i ^ bit) for i in rang...  13.5 us
    all_to_all x2, waiting for transfers between devices, body(): lax.all_to_all(sends, 'dp', split_axis=0, concat_axis=0, tiled=True)  12.5 us
    all_to_all x2, starting transfers between devices, to_all(): return lax.all_to_all(copies, axis, split_axis=0, concat_axis=0, tiled=True)  11.4 us
    unnamed x39, local copies, waits for them, and re-layouts  10.3 us
    all_to_all x2, starting transfers between devices, body(): lax.all_to_all(sends, 'dp', split_axis=0, concat_axis=0, tiled=True)  10.2 us
    pallas_call x4, Pallas kernels, pick(): pl.pallas_call(functools.partial(pick_kernel, len(held)), grid_spec=pltpu...  10.1 us
    all_to_all x2, waiting for transfers between devices, to_all(): return lax.all_to_all(copies, axis, split_axis=0, concat_axis=0, tiled=True)  10.1 us
  transfers between devices with their start and end apart: 21, of which 13 were waited for; matrix products, arithmetic and copies ran while one was open for 11% of the time, Pallas kernels for 7%

profile of v6, /device:TPU:0, one launch (start us, length us, event | category | flops | bytes accessed | tf_op | source)
XLA Modules:
  0.0 145.5 jit_solution(5568221719072381762)
XLA Ops:
  0.7 1.7 %fusion.36 = (bf16[16,64,512]{2,1,0:T(8,128)(2,1)S(1)}, bf16[16,64,512]{2,1,0:T(8,128)(2,1)S(1)}) fusion(bf16[16,128,512]{2,1,0:T(8,128)(2,1)} %bitcast.58), kind=kLoop, calls=%fused_computation.129 | loop fusion | bytes 4194304 | tf_op jit(solution)/shard_map/slice | solution.py:320
  2.4 0.7 collective-permute-start
  3.2 1.6 %collective-permute-start.1 = (bf16[16,64,512]{2,1,0:T(8,128)(2,1)S(1)}, bf16[16,64,512]{2,1,0:T(8,128)(2,1)}, u32[]{:S(2)}, u32[]{:S(2)}) collective-permute-start(bf16[16,64,512]{2,1,0:T(8,128)(2,1)S(1)} %get-tuple-element.25.refs_0_), channel_id=1, source_target_pairs={{24,8},{25,9},{26,10},{27,11},{28,12},{29,13},{30,14},{31,15}} | collective-permute-start | bytes 3145736 | tf_op jit(solution)/shard_map/ppermute | solution.py:313
  4.8 1.6 %collective-permute-start.4 = (bf16[16,64,512]{2,1,0:T(8,128)(2,1)S(1)}, bf16[16,64,512]{2,1,0:T(8,128)(2,1)}, u32[]{:S(2)}, u32[]{:S(2)}) collective-permute-start(bf16[16,64,512]{2,1,0:T(8,128)(2,1)S(1)} %get-tuple-element.25.refs_0_), channel_id=1, source_target_pairs={{24,16},{25,17},{26,18},{27,19},{28,20},{29,21},{30,22},{31,23}} | collective-permute-start | bytes 3145736 | tf_op jit(solution)/shard_map/ppermute | solution.py:313
  6.5 1.7 %collective-permute-start.2 = (bf16[16,64,512]{2,1,0:T(8,128)(2,1)S(1)}, bf16[16,64,512]{2,1,0:T(8,128)(2,1)}, u32[]{:S(2)}, u32[]{:S(2)}) collective-permute-start(bf16[16,64,512]{2,1,0:T(8,128)(2,1)S(1)} %get-tuple-element.26.refs_0_), channel_id=1, source_target_pairs={{24,16},{25,17},{26,18},{27,19},{28,20},{29,21},{30,22},{31,23}} | collective-permute-start | bytes 3145736 | tf_op jit(solution)/shard_map/ppermute | solution.py:313
  8.6 0.6 broadcast_in_dim.95
  9.2 7.3 %all-to-all-start = ((s32[8,1,128]{2,1,0:T(1,128)}), s32[8,1,128]{2,1,0:T(1,128)S(1)}, u32[]{:S(2)}, u32[]{:S(2)}) async-start(s32[8,1,128]{2,1,0:T(1,128)} %broadcast_in_dim.95), calls=%async_computation | async-start | bytes 8192 | tf_op jit(solution)/shard_map/all_to_all | solution.py:324
  16.6 6.3 %all-to-all-done = s32[8,1,128]{2,1,0:T(1,128)S(1)} async-done(((s32[8,1,128]{2,1,0:T(1,128)}), s32[8,1,128]{2,1,0:T(1,128)S(1)}, u32[]{:S(2)}, u32[]{:S(2)}) %all-to-all-start) | async-done | bytes 4128 | tf_op jit(solution)/shard_map/all_to_all | solution.py:324
  22.8 0.6 broadcast_in_dim.97
  23.5 4.2 %all-to-all-start.1 = ((s32[4,8,1,128]{3,1,2,0:T(8,128)}), s32[4,8,1,128]{3,1,2,0:T(8,128)S(1)}, u32[]{:S(2)}, u32[]{:S(2)}) async-start(s32[4,8,1,128]{3,1,2,0:T(8,128)} %broadcast_in_dim.97), calls=%async_computation.1 | async-start | bytes 32768 | tf_op jit(solution)/shard_map/all_to_all | solution.py:324
  27.6 3.8 %all-to-all-done.1 = s32[4,8,1,128]{3,1,2,0:T(8,128)S(1)} async-done(((s32[4,8,1,128]{3,1,2,0:T(8,128)}), s32[4,8,1,128]{3,1,2,0:T(8,128)S(1)}, u32[]{:S(2)}, u32[]{:S(2)}) %all-to-all-start.1) | async-done | bytes 16416 | tf_op jit(solution)/shard_map/all_to_all | solution.py:324
  31.5 1.3 collective-permute-start.5
  33.3 0.6 convert_reduce_fusion
  34.0 1.3 collective-permute-start.3
  35.6 0.6 pad_add_fusion.2.meta
  36.4 2.6 %shard_map.139 = bf16[8,64,512]{2,1,0:T(8,128)(2,1)} custom-call(s32[9]{0:T(128)} %pad_add_fusion.2.meta, bf16[16,64,512]{2,1,0:T(8,128)(2,1)} %copy-done.1, bf16[16,64,512]{2,1,0:T(8,128)(2,1)} %collective-permute-done.1.refs_1_, bf16[16,64,512]{2,1,0:T(8,128)(2,1)} %collective-permute-done.4.refs_2_, bf16[16,64,512]{2,1,0:T(8,128)(2,1)} %collective-permute-done.5.refs_3_), custom_call_target="tpu_custom_call" | custom-call | tf_op jit(solution)/shard_map/pallas_call | solution.py:223
  39.0 5.2 %all-to-all-start.3 = ((bf16[8,64,512]{2,1,0:T(8,128)(2,1)}), bf16[8,64,512]{2,1,0:T(8,128)(2,1)S(1)}, u32[]{:S(2)}, u32[]{:S(2)}) async-start(bf16[8,64,512]{2,1,0:T(8,128)(2,1)} %shard_map.139), calls=%async_computation.3 | async-start | bytes 1048576 | tf_op jit(solution)/shard_map/all_to_all | solution.py:364
  44.3 2.6 %shard_map.138 = bf16[8,64,512]{2,1,0:T(8,128)(2,1)} custom-call(s32[9]{0:T(128)} %pad_add_fusion.2.meta, bf16[16,64,512]{2,1,0:T(8,128)(2,1)} %copy-done, bf16[16,64,512]{2,1,0:T(8,128)(2,1)} %copy-done.4, bf16[16,64,512]{2,1,0:T(8,128)(2,1)} %collective-permute-done.2.refs_2_, bf16[16,64,512]{2,1,0:T(8,128)(2,1)} %collective-permute-done.3.refs_3_), custom_call_target="tpu_custom_call" | custom-call | tf_op jit(solution)/shard_map/pallas_call | solution.py:223
  46.9 11.6 %all-to-all-done.3.refs_0_.rest_1_ = bf16[8,64,512]{2,1,0:T(8,128)(2,1)S(1)} async-done(((bf16[8,64,512]{2,1,0:T(8,128)(2,1)}), bf16[8,64,512]{2,1,0:T(8,128)(2,1)S(1)}, u32[]{:S(2)}, u32[]{:S(2)}) %all-to-all-start.3) | async-done | bytes 524320 | tf_op jit(solution)/shard_map/all_to_all | solution.py:364
  58.4 5.1 %all-to-all-start.2 = ((bf16[8,64,512]{2,1,0:T(8,128)(2,1)}), bf16[8,64,512]{2,1,0:T(8,128)(2,1)S(1)}, u32[]{:S(2)}, u32[]{:S(2)}) async-start(bf16[8,64,512]{2,1,0:T(8,128)(2,1)} %shard_map.138), calls=%async_computation.2 | async-start | bytes 1048576 | tf_op jit(solution)/shard_map/all_to_all | solution.py:364
  63.5 0.6 bitcast_convert_fusion.1.cond_ref
  64.1 6.5 %copy.49 = bf16[512,4096]{0,1:T(8,128)(2,1)} copy(bf16[512,4096]{1,0:T(8,128)(2,1)} %rest_8_.1) | data formatting | bytes 8388608 | tf_op args[10]
  70.7 0.8 copy.47
  71.5 0.8 copy.48
  73.1 0.7 fusion.34
  74.2 0.6 pad_add_fusion.3.meta
  74.8 2.5 %shard_map.141 = bf16[4,64,512]{2,1,0:T(8,128)(2,1)} custom-call(s32[5]{0:T(128)} %pad_add_fusion.3.meta, bf16[8,64,512]{2,1,0:T(8,128)(2,1)} %copy-done.2), custom_call_target="tpu_custom_call" | custom-call | tf_op jit(solution)/shard_map/pallas_call | solution.py:223
  77.3 1.0 all-to-all-done.2.refs_0_.rest_0_
  78.3 0.8 copy-done.3
  79.1 2.4 %shard_map.140 = bf16[4,64,512]{2,1,0:T(8,128)(2,1)} custom-call(s32[5]{0:T(128)} %pad_add_fusion.3.meta, bf16[8,64,512]{2,1,0:T(8,128)(2,1)} %copy-done.3), custom_call_target="tpu_custom_call" | custom-call | tf_op jit(solution)/shard_map/pallas_call | solution.py:223
  81.6 1.1 collective-permute-start.8
  83.5 3.2 %collective-permute-done.9.rest_5_ = bf16[4,64,512]{2,1,0:T(8,128)(2,1)S(1)} collective-permute-done((bf16[4,64,512]{2,1,0:T(8,128)(2,1)}, bf16[4,64,512]{2,1,0:T(8,128)(2,1)S(1)}, u32[]{:S(2)}, u32[]{:S(2)}) %collective-permute-start.9) | collective-permute-done | bytes 262176 | tf_op jit(solution)/shard_map/ppermute | solution.py:313
  86.7 4.6 %collective-permute-done.8.rest_4_ = bf16[4,64,512]{2,1,0:T(8,128)(2,1)S(1)} collective-permute-done((bf16[4,64,512]{2,1,0:T(8,128)(2,1)}, bf16[4,64,512]{2,1,0:T(8,128)(2,1)S(1)}, u32[]{:S(2)}, u32[]{:S(2)}) %collective-permute-start.8) | collective-permute-done | bytes 262176 | tf_op jit(solution)/shard_map/ppermute | solution.py:313
  91.4 0.6 pad_add_fusion.1.meta
  92.0 0.9 collective-permute-done.10.rest_6_
  93.0 0.7 copy-done.16
  94.0 28.3 %shard_map.142 = (bf16[256,2048]{1,0:T(8,128)(2,1)}, bf16[256,2048]{1,0:T(8,128)(2,1)}, f32[4,512]{1,0:T(4,128)}, f32[512,512]{1,0:T(8,128)}) custom-call(s32[25]{0:T(128)} %pad_add_fusion.1.meta, bf16[256,2048]{1,0:T(8,128)(2,1)} %bitcast.72, bf16[256,2048]{1,0:T(8,128)(2,1)} %bitcast.73, f32[4,512]{1,0:T(4,128)} %bitcast_convert_fusion.1.cond_ref, ...), custom_call_target="tpu_custom_call" | custom-call | flops 11811160064 | bytes 16777216 | tf_op jit(solution)/shard_map/pallas_call | solution.py:165
  122.3 1.1 fusion
  123.6 1.4 collective-permute-done.12
  125.0 1.1 bitcast_add_fusion
  126.5 5.3 %collective-permute-done.13 = bf16[1,8,16,512]{3,2,1,0:T(8,128)(2,1)S(1)} collective-permute-done((bf16[1,8,16,512]{3,2,1,0:T(8,128)(2,1)S(1)}, bf16[1,8,16,512]{3,2,1,0:T(8,128)(2,1)S(1)}, u32[]{:S(2)}, u32[]{:S(2)}) %collective-permute-start.13) | collective-permute-done | bytes 131104 | tf_op jit(solution)/shard_map/ppermute | solution.py:278
  131.8 1.7 %collective-permute-start.14 = (bf16[1,4,16,512]{3,2,1,0:T(8,128)(2,1)S(1)}, bf16[1,4,16,512]{3,2,1,0:T(8,128)(2,1)S(1)}, u32[]{:S(2)}, u32[]{:S(2)}) collective-permute-start(bf16[1,4,16,512]{3,2,1,0:T(8,128)(2,1)S(1)} %fusion.2), channel_id=1, source_target_pairs={{0,1},{1,0},{2,3},{3,2},{4,5},{5,4},{6,7},{7,6},{8,9},{9,8},{10,11... | collective-permute-start | bytes 196616 | tf_op jit(solution)/shard_map/ppermute | solution.py:278
  133.5 2.6 %collective-permute-done.14 = bf16[1,4,16,512]{3,2,1,0:T(8,128)(2,1)S(1)} collective-permute-done((bf16[1,4,16,512]{3,2,1,0:T(8,128)(2,1)S(1)}, bf16[1,4,16,512]{3,2,1,0:T(8,128)(2,1)S(1)}, u32[]{:S(2)}, u32[]{:S(2)}) %collective-permute-start.14) | collective-permute-done | bytes 65568 | tf_op jit(solution)/shard_map/ppermute | solution.py:278
  136.2 1.7 %collective-permute-start.15 = (bf16[1,2,16,512]{3,2,1,0:T(8,128)(2,1)S(1)}, bf16[1,2,16,512]{3,2,1,0:T(8,128)(2,1)S(1)}, u32[]{:S(2)}, u32[]{:S(2)}) collective-permute-start(bf16[1,2,16,512]{3,2,1,0:T(8,128)(2,1)S(1)} %fusion.3), channel_id=1, source_target_pairs={{0,2},{1,3},{2,0},{3,1},{4,6},{5,7},{6,4},{7,5},{8,10},{9,11},{10,... | collective-permute-start | bytes 98312 | tf_op jit(solution)/shard_map/ppermute | solution.py:278
  137.9 2.3 %collective-permute-done.15 = bf16[1,2,16,512]{3,2,1,0:T(8,128)(2,1)S(1)} collective-permute-done((bf16[1,2,16,512]{3,2,1,0:T(8,128)(2,1)S(1)}, bf16[1,2,16,512]{3,2,1,0:T(8,128)(2,1)S(1)}, u32[]{:S(2)}, u32[]{:S(2)}) %collective-permute-start.15) | collective-permute-done | bytes 32800 | tf_op jit(solution)/shard_map/ppermute | solution.py:278
  140.2 2.8 %collective-permute-start.16 = (bf16[1,1,16,512]{3,2,1,0:T(8,128)(2,1)S(1)}, bf16[1,1,16,512]{3,2,1,0:T(8,128)(2,1)S(1)}, u32[]{:S(2)}, u32[]{:S(2)}) collective-permute-start(bf16[1,1,16,512]{3,2,1,0:T(8,128)(2,1)S(1)} %dynamic-slice_convert_fusion.3), channel_id=1, source_target_pairs={{0,4},{1,5},{2,6},{3,7},{4,0},{5,1},{6,2},{7,3},{8,12},{9,13},{10,... | collective-permute-start | bytes 49160 | tf_op jit(solution)/shard_map/ppermute | solution.py:278
  143.0 1.9 %collective-permute-done.16 = bf16[1,1,16,512]{3,2,1,0:T(8,128)(2,1)S(1)} collective-permute-done((bf16[1,1,16,512]{3,2,1,0:T(8,128)(2,1)S(1)}, bf16[1,1,16,512]{3,2,1,0:T(8,128)(2,1)S(1)}, u32[]{:S(2)}, u32[]{:S(2)}) %collective-permute-start.16) | collective-permute-done | bytes 16416 | tf_op jit(solution)/shard_map/ppermute | solution.py:278
  144.9 0.6 add_bitcast_fusion
  (94 shorter events, 5.0 us)
Async XLA Ops:
  0.6 7.5 %copy-start.8 = (s32[1,1,4,2]{2,3,1,0:T(2,128)S(1)}, s32[1,1,4,2]{2,3,1,0:T(2,128)}, u32[]{:S(2)}) copy-start(s32[1,1,4,2]{2,3,1,0:T(2,128)} %param.14) | copy-start | bytes 100
  0.6 7.7 %copy-start.9 = (s32[1,1,4,2]{2,3,1,0:T(2,128)S(1)}, s32[1,1,4,2]{2,3,1,0:T(2,128)}, u32[]{:S(2)}) copy-start(s32[1,1,4,2]{2,3,1,0:T(2,128)} %param.15) | copy-start | bytes 100
  0.7 7.8 %copy-start.10 = (s32[1,1,16]{2,1,0:T(1,128)S(1)}, s32[1,1,16]{2,1,0:T(1,128)}, u32[]{:S(2)}) copy-start(s32[1,1,16]{2,1,0:T(1,128)} %param.17) | copy-start | bytes 196
  2.4 34.0 %copy-start.1 = (bf16[16,64,512]{2,1,0:T(8,128)(2,1)}, bf16[16,64,512]{2,1,0:T(8,128)(2,1)S(1)}, u32[]{:S(2)}) copy-start(bf16[16,64,512]{2,1,0:T(8,128)(2,1)S(1)} %get-tuple-element.25.refs_0_) | copy-start | bytes 3145732
  2.4 41.8 %copy-start = (bf16[16,64,512]{2,1,0:T(8,128)(2,1)}, bf16[16,64,512]{2,1,0:T(8,128)(2,1)S(1)}, u32[]{:S(2)}) copy-start(bf16[16,64,512]{2,1,0:T(8,128)(2,1)S(1)} %get-tuple-element.26.refs_0_) | copy-start | bytes 3145732
  2.4 29.0 %collective-permute-start = (bf16[16,64,512]{2,1,0:T(8,128)(2,1)S(1)}, bf16[16,64,512]{2,1,0:T(8,128)(2,1)S(1)}, u32[]{:S(2)}, u32[]{:S(2)}) collective-permute-start(bf16[16,64,512]{2,1,0:T(8,128)(2,1)S(1)} %get-tuple-element.26.refs_0_), channel_id=1, source_target_pairs={{24,8},{25,9},{26,10},{27,11},{28,12},{29,13},{30,14},{31,15}} | collective-permute-start | bytes 3145736 | tf_op jit(solution)/shard_map/ppermute | solution.py:313
  3.2 28.3 %collective-permute-start.1 = (bf16[16,64,512]{2,1,0:T(8,128)(2,1)S(1)}, bf16[16,64,512]{2,1,0:T(8,128)(2,1)}, u32[]{:S(2)}, u32[]{:S(2)}) collective-permute-start(bf16[16,64,512]{2,1,0:T(8,128)(2,1)S(1)} %get-tuple-element.25.refs_0_), channel_id=1, source_target_pairs={{24,8},{25,9},{26,10},{27,11},{28,12},{29,13},{30,14},{31,15}} | collective-permute-start | bytes 3145736 | tf_op jit(solution)/shard_map/ppermute | solution.py:313
  4.8 31.4 %collective-permute-start.4 = (bf16[16,64,512]{2,1,0:T(8,128)(2,1)S(1)}, bf16[16,64,512]{2,1,0:T(8,128)(2,1)}, u32[]{:S(2)}, u32[]{:S(2)}) collective-permute-start(bf16[16,64,512]{2,1,0:T(8,128)(2,1)S(1)} %get-tuple-element.25.refs_0_), channel_id=1, source_target_pairs={{24,16},{25,17},{26,18},{27,19},{28,20},{29,21},{30,22},{31,23}} | collective-permute-start | bytes 3145736 | tf_op jit(solution)/shard_map/ppermute | solution.py:313
  6.5 37.8 %collective-permute-start.2 = (bf16[16,64,512]{2,1,0:T(8,128)(2,1)S(1)}, bf16[16,64,512]{2,1,0:T(8,128)(2,1)}, u32[]{:S(2)}, u32[]{:S(2)}) collective-permute-start(bf16[16,64,512]{2,1,0:T(8,128)(2,1)S(1)} %get-tuple-element.26.refs_0_), channel_id=1, source_target_pairs={{24,16},{25,17},{26,18},{27,19},{28,20},{29,21},{30,22},{31,23}} | collective-permute-start | bytes 3145736 | tf_op jit(solution)/shard_map/ppermute | solution.py:313
  9.2 13.7 %all-to-all-start = ((s32[8,1,128]{2,1,0:T(1,128)}), s32[8,1,128]{2,1,0:T(1,128)S(1)}, u32[]{:S(2)}, u32[]{:S(2)}) async-start(s32[8,1,128]{2,1,0:T(1,128)} %broadcast_in_dim.95), calls=%async_computation | async-start | bytes 8192 | tf_op jit(solution)/shard_map/all_to_all | solution.py:324
  23.5 8.0 %all-to-all-start.1 = ((s32[4,8,1,128]{3,1,2,0:T(8,128)}), s32[4,8,1,128]{3,1,2,0:T(8,128)S(1)}, u32[]{:S(2)}, u32[]{:S(2)}) async-start(s32[4,8,1,128]{3,1,2,0:T(8,128)} %broadcast_in_dim.97), calls=%async_computation.1 | async-start | bytes 32768 | tf_op jit(solution)/shard_map/all_to_all | solution.py:324
  31.5 12.8 %copy-start.4 = (bf16[16,64,512]{2,1,0:T(8,128)(2,1)}, bf16[16,64,512]{2,1,0:T(8,128)(2,1)S(1)}, u32[]{:S(2)}) copy-start(bf16[16,64,512]{2,1,0:T(8,128)(2,1)S(1)} %collective-permute-done.refs_1_) | copy-start | bytes 3145732
  31.5 4.9 %collective-permute-start.5 = (bf16[16,64,512]{2,1,0:T(8,128)(2,1)}, bf16[16,64,512]{2,1,0:T(8,128)(2,1)}, u32[]{:S(2)}, u32[]{:S(2)}) collective-permute-start(bf16[16,64,512]{2,1,0:T(8,128)(2,1)} %collective-permute-done.1.refs_1_), channel_id=1, source_target_pairs={{8,0},{9,1},{10,2},{11,3},{12,4},{13,5},{14,6},{15,7}} | collective-permute-start | bytes 3145736 | tf_op jit(solution)/shard_map/ppermute | solution.py:313
  34.0 10.2 %collective-permute-start.3 = (bf16[16,64,512]{2,1,0:T(8,128)(2,1)S(1)}, bf16[16,64,512]{2,1,0:T(8,128)(2,1)}, u32[]{:S(2)}, u32[]{:S(2)}) collective-permute-start(bf16[16,64,512]{2,1,0:T(8,128)(2,1)S(1)} %collective-permute-done.refs_1_), channel_id=1, source_target_pairs={{8,0},{9,1},{10,2},{11,3},{12,4},{13,5},{14,6},{15,7}} | collective-permute-start | bytes 3145736 | tf_op jit(solution)/shard_map/ppermute | solution.py:313
  39.0 24.5 %copy-start.7 = (bf16[1,1,4,512]{3,2,1,0:T(4,128)(2,1)S(1)}, bf16[1,1,4,512]{3,2,1,0:T(4,128)(2,1)}, u32[]{:S(2)}) copy-start(bf16[1,1,4,512]{3,2,1,0:T(4,128)(2,1)} %param.13) | copy-start | bytes 12292
  39.0 19.4 %all-to-all-start.3 = ((bf16[8,64,512]{2,1,0:T(8,128)(2,1)}), bf16[8,64,512]{2,1,0:T(8,128)(2,1)S(1)}, u32[]{:S(2)}, u32[]{:S(2)}) async-start(bf16[8,64,512]{2,1,0:T(8,128)(2,1)} %shard_map.139), calls=%async_computation.3 | async-start | bytes 1048576 | tf_op jit(solution)/shard_map/all_to_all | solution.py:364
  58.4 12.2 %copy-start.2 = (bf16[8,64,512]{2,1,0:T(8,128)(2,1)}, bf16[8,64,512]{2,1,0:T(8,128)(2,1)S(1)}, u32[]{:S(2)}) copy-start(bf16[8,64,512]{2,1,0:T(8,128)(2,1)S(1)} %all-to-all-done.3.refs_0_.rest_1_) | copy-start | bytes 1572868
  58.4 19.9 %all-to-all-start.2 = ((bf16[8,64,512]{2,1,0:T(8,128)(2,1)}), bf16[8,64,512]{2,1,0:T(8,128)(2,1)S(1)}, u32[]{:S(2)}, u32[]{:S(2)}) async-start(bf16[8,64,512]{2,1,0:T(8,128)(2,1)} %shard_map.138), calls=%async_computation.2 | async-start | bytes 1048576 | tf_op jit(solution)/shard_map/all_to_all | solution.py:364
  64.1 6.5 %copy-start.6 = (bf16[256,512]{1,0:T(8,128)(2,1)S(1)}, bf16[256,512]{1,0:T(8,128)(2,1)}, u32[]{:S(2)}) copy-start(bf16[256,512]{1,0:T(8,128)(2,1)} %up_ref.1) | copy-start | bytes 786436
  64.1 7.4 %copy-start.5 = (bf16[512,256]{1,0:T(8,128)(2,1)S(1)}, bf16[512,256]{1,0:T(8,128)(2,1)}, u32[]{:S(2)}) copy-start(bf16[512,256]{1,0:T(8,128)(2,1)} %down_ref.1) | copy-start | bytes 786436
  77.3 9.4 %collective-permute-start.9 = (bf16[4,64,512]{2,1,0:T(8,128)(2,1)}, bf16[4,64,512]{2,1,0:T(8,128)(2,1)S(1)}, u32[]{:S(2)}, u32[]{:S(2)}) collective-permute-start(bf16[4,64,512]{2,1,0:T(8,128)(2,1)} %shard_map.141), channel_id=1, source_target_pairs={{0,16},{1,17},{2,18},{3,19},{4,20},{5,21},{6,22},{7,23},{8,24},{9,... | collective-permute-start | bytes 786440 | tf_op jit(solution)/shard_map/ppermute | solution.py:313
  78.3 0.8 copy-start.3
  81.6 9.8 %collective-permute-start.8 = (bf16[4,64,512]{2,1,0:T(8,128)(2,1)}, bf16[4,64,512]{2,1,0:T(8,128)(2,1)S(1)}, u32[]{:S(2)}, u32[]{:S(2)}) collective-permute-start(bf16[4,64,512]{2,1,0:T(8,128)(2,1)} %shard_map.140), channel_id=1, source_target_pairs={{0,16},{1,17},{2,18},{3,19},{4,20},{5,21},{6,22},{7,23},{8,24},{9,... | collective-permute-start | bytes 786440 | tf_op jit(solution)/shard_map/ppermute | solution.py:313
  83.0 9.9 %collective-permute-start.7 = (bf16[8,64,512]{2,1,0:T(8,128)(2,1)}, bf16[8,64,512]{2,1,0:T(8,128)(2,1)S(1)}, u32[]{:S(2)}, u32[]{:S(2)}) collective-permute-start(bf16[8,64,512]{2,1,0:T(8,128)(2,1)} %copy-done.2), channel_id=1, source_target_pairs={{0,8},{1,9},{2,10},{3,11},{4,12},{5,13},{6,14},{7,15},{8,0},{9,1},... | collective-permute-start | bytes 1572872 | tf_op jit(solution)/shard_map/ppermute | solution.py:313
  83.0 9.9 %collective-permute-start.6 = (bf16[8,64,512]{2,1,0:T(8,128)(2,1)}, bf16[8,64,512]{2,1,0:T(8,128)(2,1)S(1)}, u32[]{:S(2)}, u32[]{:S(2)}) collective-permute-start(bf16[8,64,512]{2,1,0:T(8,128)(2,1)} %copy-done.3), channel_id=1, source_target_pairs={{0,8},{1,9},{2,10},{3,11},{4,12},{5,13},{6,14},{7,15},{8,0},{9,1},... | collective-permute-start | bytes 1572872 | tf_op jit(solution)/shard_map/ppermute | solution.py:313
  86.7 6.2 %copy-start.13 = (bf16[4,64,512]{2,1,0:T(8,128)(2,1)}, bf16[4,64,512]{2,1,0:T(8,128)(2,1)S(1)}, u32[]{:S(2)}) copy-start(bf16[4,64,512]{2,1,0:T(8,128)(2,1)S(1)} %collective-permute-done.9.rest_5_) | copy-start | bytes 786436
  86.7 5.3 %collective-permute-start.11 = (bf16[4,64,512]{2,1,0:T(8,128)(2,1)S(1)}, bf16[4,64,512]{2,1,0:T(8,128)(2,1)S(1)}, u32[]{:S(2)}, u32[]{:S(2)}) collective-permute-start(bf16[4,64,512]{2,1,0:T(8,128)(2,1)S(1)} %collective-permute-done.9.rest_5_), channel_id=1, source_target_pairs={{0,8},{1,9},{2,10},{3,11},{4,12},{5,13},{6,14},{7,15},{8,0},{9,1},... | collective-permute-start | bytes 786440 | tf_op jit(solution)/shard_map/ppermute | solution.py:313
  91.4 1.6 %copy-start.14 = (bf16[4,64,512]{2,1,0:T(8,128)(2,1)}, bf16[4,64,512]{2,1,0:T(8,128)(2,1)S(1)}, u32[]{:S(2)}) copy-start(bf16[4,64,512]{2,1,0:T(8,128)(2,1)S(1)} %collective-permute-done.8.rest_4_) | copy-start | bytes 786436
  91.4 1.5 %collective-permute-start.10 = (bf16[4,64,512]{2,1,0:T(8,128)(2,1)S(1)}, bf16[4,64,512]{2,1,0:T(8,128)(2,1)S(1)}, u32[]{:S(2)}, u32[]{:S(2)}) collective-permute-start(bf16[4,64,512]{2,1,0:T(8,128)(2,1)S(1)} %collective-permute-done.8.rest_4_), channel_id=1, source_target_pairs={{0,8},{1,9},{2,10},{3,11},{4,12},{5,13},{6,14},{7,15},{8,0},{9,1},... | collective-permute-start | bytes 786440 | tf_op jit(solution)/shard_map/ppermute | solution.py:313
  92.0 0.9 copy-start.15
  92.9 0.7 copy-start.16
  92.9 0.9 copy-start.11
  92.9 1.0 copy-start.12
  123.4 1.6 %collective-permute-start.12 = (bf16[2,8,16,512]{3,2,1,0:T(8,128)(2,1)S(1)}, bf16[2,8,16,512]{3,2,1,0:T(8,128)(2,1)S(1)}, u32[]{:S(2)}, u32[]{:S(2)}) collective-permute-start(bf16[2,8,16,512]{3,2,1,0:T(8,128)(2,1)S(1)} %fusion), channel_id=1, source_target_pairs={{0,8},{8,0},{16,24},{24,16},{1,9},{9,1},{17,25},{25,17},{2,10},{10... | collective-permute-start | bytes 786440 | tf_op jit(solution)/shard_map/ppermute | solution.py:278
  126.2 5.6 %collective-permute-start.13 = (bf16[1,8,16,512]{3,2,1,0:T(8,128)(2,1)S(1)}, bf16[1,8,16,512]{3,2,1,0:T(8,128)(2,1)S(1)}, u32[]{:S(2)}, u32[]{:S(2)}) collective-permute-start(bf16[1,8,16,512]{3,2,1,0:T(8,128)(2,1)S(1)} %dynamic-slice_convert_fusion), channel_id=1, source_target_pairs={{0,16},{8,24},{16,0},{24,8},{1,17},{9,25},{17,1},{25,9},{2,18},{10... | collective-permute-start | bytes 393224 | tf_op jit(solution)/shard_map/ppermute | solution.py:278
  131.8 4.3 %collective-permute-start.14 = (bf16[1,4,16,512]{3,2,1,0:T(8,128)(2,1)S(1)}, bf16[1,4,16,512]{3,2,1,0:T(8,128)(2,1)S(1)}, u32[]{:S(2)}, u32[]{:S(2)}) collective-permute-start(bf16[1,4,16,512]{3,2,1,0:T(8,128)(2,1)S(1)} %fusion.2), channel_id=1, source_target_pairs={{0,1},{1,0},{2,3},{3,2},{4,5},{5,4},{6,7},{7,6},{8,9},{9,8},{10,11... | collective-permute-start | bytes 196616 | tf_op jit(solution)/shard_map/ppermute | solution.py:278
  136.2 4.0 %collective-permute-start.15 = (bf16[1,2,16,512]{3,2,1,0:T(8,128)(2,1)S(1)}, bf16[1,2,16,512]{3,2,1,0:T(8,128)(2,1)S(1)}, u32[]{:S(2)}, u32[]{:S(2)}) collective-permute-start(bf16[1,2,16,512]{3,2,1,0:T(8,128)(2,1)S(1)} %fusion.3), channel_id=1, source_target_pairs={{0,2},{1,3},{2,0},{3,1},{4,6},{5,7},{6,4},{7,5},{8,10},{9,11},{10,... | collective-permute-start | bytes 98312 | tf_op jit(solution)/shard_map/ppermute | solution.py:278
  140.2 4.7 %collective-permute-start.16 = (bf16[1,1,16,512]{3,2,1,0:T(8,128)(2,1)S(1)}, bf16[1,1,16,512]{3,2,1,0:T(8,128)(2,1)S(1)}, u32[]{:S(2)}, u32[]{:S(2)}) collective-permute-start(bf16[1,1,16,512]{3,2,1,0:T(8,128)(2,1)S(1)} %dynamic-slice_convert_fusion.3), channel_id=1, source_target_pairs={{0,4},{1,5},{2,6},{3,7},{4,0},{5,1},{6,2},{7,3},{8,12},{9,13},{10,... | collective-permute-start | bytes 49160 | tf_op jit(solution)/shard_map/ppermute | solution.py:278

commit v7 on v6

--- a/solution.py
+++ b/solution.py
@@ -148,7 +148,7 @@
         ad_ref[...] = jnp.where(live, acc_ref[...], 0.0).astype(ad_ref.dtype)
 
 
-def run_spans(meta, query, cot, cond, held, parts, gain, w_down, w_up, w_kv, nbr_count):
+def run_spans(meta, query, cot, cond, held, parts, gain, w_down, w_up, w_kv, w_kv_t, nbr_count):
     span_count, width = cond.shape
     token_count, head_cols = query.shape
     slot_len = held[0].shape[1] * parts
@@ -156,7 +156,7 @@
     whole = lambda a: pl.BlockSpec(a.shape, lambda s, m: (0,) * a.ndim, pipeline_mode=pl.Buffered(1))
     tokens = pl.BlockSpec((SPAN, head_cols), lambda s, m: (s, 0))
     small = [cond, gain.reshape(1, width), w_down, w_up, w_up.T, w_down.T]
-    large = list(held) + [w_kv, w_kv.T]
+    large = list(held) + [w_kv, w_kv_t]
     per_device = span_count * nbr_count
     keys = nbr_count * slot_len
     rows = per_device * slot_len
@@ -207,14 +207,12 @@
 
 
 def pick_kernel(held_count, meta, *refs):
-    held_refs, out_ref, sems = refs[:held_count], refs[held_count], refs[held_count + 1]
+    held_refs, out_ref = refs[:held_count], refs[held_count]
     for b, held in enumerate(held_refs):
         @pl.when(meta[0] == b)
         def _():
             for n in range(out_ref.shape[0]):
-                pltpu.make_async_copy(held.at[meta[1 + n]], out_ref.at[n], sems.at[n]).start()
-    for n in range(out_ref.shape[0]):
-        pltpu.make_async_copy(held_refs[0].at[0], out_ref.at[n], sems.at[n]).wait()
+                out_ref[n] = held[meta[1 + n]]
 
 
 def pick(which, index, held):
@@ -225,12 +223,11 @@
         grid_spec=pltpu.PrefetchScalarGridSpec(
             num_scalar_prefetch=1,
             grid=(1,),
-            in_specs=[pl.BlockSpec(memory_space=pltpu.HBM)] * len(held),
+            in_specs=[pl.BlockSpec(memory_space=pltpu.VMEM)] * len(held),
             out_specs=pl.BlockSpec(memory_space=pltpu.VMEM),
-            scratch_shapes=[pltpu.SemaphoreType.DMA((count,))],
         ),
         out_shape=jax.ShapeDtypeStruct((count,) + held[0].shape[1:], held[0].dtype),
-        compiler_params=pltpu.CompilerParams(vmem_limit_bytes=60 * 2**20),
+        compiler_params=pltpu.CompilerParams(vmem_limit_bytes=16 * 2**20),
     )(meta, *held)
 
 
@@ -323,12 +320,14 @@
         copies = jnp.broadcast_to(array[None], (lax.axis_size(axis),) + array.shape)
         return lax.all_to_all(copies, axis, split_axis=0, concat_axis=0, tiled=True)
 
-    across = [hop(a, [(relay_row, relay_row - half)]) for a in store]
-
     info = jnp.concatenate([nbr_owner.reshape(-1), nbr_block.reshape(-1), lengths.reshape(-1)])
     info = jnp.pad(info, (0, -info.shape[0] % 128))
-    table = to_all(to_all(info.reshape(-1, 128), "dp"), "pool")
-    across, table = lax.optimization_barrier((across, table))
+    over = lambda a: hop(a, [(relay_row, relay_row - half)])
+    across = [over(store[0])]
+    table = to_all(info.reshape(-1, 128), "dp")
+    store[1:], table = lax.optimization_barrier((store[1:], table))
+    across += [over(a) for a in store[1:]]
+    table = to_all(table, "pool")
     table = table.reshape(pool_count, columns, -1)
     by_column = jnp.swapaxes(table[:relay_row], 0, 1)
     owners = by_column[:, :, :per_device].reshape(columns, live_count)
@@ -353,14 +352,20 @@
         return hop(array, [(p, p // half * half + (p + step) % half) for p in range(pool_count)])
 
     held = []
+    weight, weight_t = w_kv, None
     for i in range(parts):
-        stores = [store[i], across[i]]
-        held_by = jnp.where(row == relay_row, 0, 1)
+        near = jnp.where(row == relay_row, store[i], across[i])
+        stores = [near]
+        held_by = jnp.where(row % half == half - 1, 0, 1)
         for step in range(1, half):
-            for near, array in ((relay_row, store[i]), (relay_row - half, across[i])):
-                stores.append(hop(array, [(near, near - step)]))
-                held_by = jnp.where(row == near - step, len(stores) - 1, held_by)
-        sends = pick(held_by, slot_block, stores)
+            stores.append(hop(near, [(p, p - step) for p in (relay_row, relay_row - half)]))
+            held_by = jnp.where(row % half == half - 1 - step, step, held_by)
+        wanted = slot_block
+        if i == 1:
+            weight_t, wanted = lax.optimization_barrier((weight.T, wanted))
+        sends = pick(held_by, wanted, stores)
+        if i == 0:
+            weight, sends = lax.optimization_barrier((weight, sends))
         arrived = lax.all_to_all(sends, "dp", split_axis=0, concat_axis=0, tiled=True)
         here = [arrived] + [share(arrived, step) for step in range(1, half)]
         if crossing:
@@ -368,6 +373,7 @@
             landed = hop(leaving, [(p, (p + half) % pool_count) for p in range(pool_count)])
             here += [landed] + [share(landed, step) for step in range(1, half)]
         held.append(here)
+    weight_t = weight.T if weight_t is None else weight_t
     origin = jnp.where(my_cross, (my_carrier + half) % pool_count, my_carrier)
     which = (row - origin) % half + jnp.where(my_cross, half, 0)
     index = jnp.where(my_cross, my_number, place)
@@ -395,6 +401,7 @@
         w_down,
         w_up,
         w_kv,
+        weight_t,
         nbr_count,
     )
 

time: 147 us -> 144 us (0.980)
  waiting for transfers between devices: 45.1 us -> 51.1 us
  starting transfers between devices: 38.3 us -> 32.7 us
  Pallas kernels: 38.5 us -> 33.4 us
  other arithmetic: 6.63 us -> 9.38 us
    optimization_barrier x1, local copies, waits for them, and re-layouts: 0.01 us -> 6.54 us  [body(): weight, sends = lax.optimization_barrier((weight, sends))]
    unnamed x39 -> x29, local copies, waits for them, and re-layouts: 10.3 us -> 3.93 us
    pallas_call x4, Pallas kernels: 10.1 us -> 5.12 us  [pick(): pl.pallas_call(functools.partial(pick_kernel, len(held)), grid_spec=pltpu...]
    ppermute x12 -> x10, starting transfers between devices: 9.89 us -> 5.74 us  [hop(): lax.ppermute(array, axes, [(a * columns + j, b * columns + j) for a, b in...]
    all_to_all x2, waiting for transfers between devices: 12.5 us -> 15.7 us  [body(): lax.all_to_all(sends, 'dp', split_axis=0, concat_axis=0, tiled=True)]
    select_n x0 -> x2, other arithmetic: none -> 3.08 us  [body(): near = jnp.where(row == relay_row, store[i], across[i])]
    all_to_all x2, waiting for transfers between devices: 10.1 us -> 12.9 us  [to_all(): return lax.all_to_all(copies, axis, split_axis=0, concat_axis=0, tiled=True)]
    ppermute x5, starting transfers between devices: 6.72 us -> 4.43 us  [scatter_sum(): lax.ppermute(give.astype(jnp.bfloat16), axis, [(i, i ^ bit) for i in rang...]
  transfers between devices with their start and end apart: 21 -> 19, of which waited for: 13 -> 11; matrix products, arithmetic and copies ran while one was open for 11% -> 14% of each run, Pallas kernels for 7% -> 4%
where the time goes in v7:
time: 144 us; the launch traced here: 143 us
  waiting for transfers between devices  51.1 us (35%)
  Pallas kernels  33.4 us (23%)
  starting transfers between devices  32.7 us (23%)
  local copies, waits for them, and re-layouts  15.9 us (11%)
  other arithmetic  9.38 us (7%)
    pallas_call x1, Pallas kernels, run_spans(): pl.pallas_call(functools.partial(span_kernel, len(held), nbr_count, parts...  28.3 us
    ppermute x5, waiting for transfers between devices, scatter_sum(): lax.ppermute(give.astype(jnp.bfloat16), axis, [(i, i ^ bit) for i in rang...  15.8 us
    all_to_all x2, waiting for transfers between devices, body(): lax.all_to_all(sends, 'dp', split_axis=0, concat_axis=0, tiled=True)  15.7 us
    all_to_all x2, waiting for transfers between devices, to_all(): return lax.all_to_all(copies, axis, split_axis=0, concat_axis=0, tiled=True)  12.9 us
    all_to_all x2, starting transfers between devices, to_all(): return lax.all_to_all(copies, axis, split_axis=0, concat_axis=0, tiled=True)  11.7 us
    all_to_all x2, starting transfers between devices, body(): lax.all_to_all(sends, 'dp', split_axis=0, concat_axis=0, tiled=True)  10.7 us
    ppermute x10, waiting for transfers between devices, hop(): lax.ppermute(array, axes, [(a * columns + j, b * columns + j) for a, b in...  6.69 us
    optimization_barrier x1, local copies, waits for them, and re-layouts, body(): weight, sends = lax.optimization_barrier((weight, sends))  6.54 us
  transfers between devices with their start and end apart: 19, of which 11 were waited for; matrix products, arithmetic and copies ran while one was open for 14% of the time, Pallas kernels for 4%

profile of v7, /device:TPU:0, one launch (start us, length us, event | category | flops | bytes accessed | tf_op | source)
XLA Modules:
  0.0 143.5 jit_solution(10681471792160629936)
XLA Ops:
  0.6 1.3 slice.33
  2.0 0.7 collective-permute-start
  2.7 0.8 copy.44
  3.5 0.8 copy.45
  4.4 0.7 pad_add_fusion
  5.1 0.6 broadcast_in_dim.95
  5.7 7.3 %all-to-all-start = ((s32[8,1,128]{2,1,0:T(1,128)}), s32[8,1,128]{2,1,0:T(1,128)S(1)}, u32[]{:S(2)}, u32[]{:S(2)}) async-start(s32[8,1,128]{2,1,0:T(1,128)} %broadcast_in_dim.95), calls=%async_computation | async-start | bytes 8192 | tf_op jit(solution)/shard_map/all_to_all | solution.py:321
  13.0 1.7 %broadcast_select_fusion.1 = (bf16[16,64,512]{2,1,0:T(8,128)(2,1)S(1)}, bf16[16,64,512]{2,1,0:T(8,128)(2,1)S(1)}) fusion(bf16[16,64,512]{2,1,0:T(8,128)(2,1)S(1)} %collective-permute-done, pred[]{:T(512)S(6)} %eq.148, bf16[16,128,512]{2,1,0:T(8,128)(2,1)} %bitcast.59), kind=kLoop, calls=%fused_computation.1 | loop fusion | flops 524288 | bytes 5242881 | tf_op jit(solution)/shard_map/jit(_where)/select_n | solution.py:357
  14.8 4.6 %all-to-all-done = s32[8,1,128]{2,1,0:T(1,128)S(1)} async-done(((s32[8,1,128]{2,1,0:T(1,128)}), s32[8,1,128]{2,1,0:T(1,128)S(1)}, u32[]{:S(2)}, u32[]{:S(2)}) %all-to-all-start) | async-done | bytes 4128 | tf_op jit(solution)/shard_map/all_to_all | solution.py:321
  19.4 1.6 %collective-permute-start.2 = (bf16[16,64,512]{2,1,0:T(8,128)(2,1)S(1)}, bf16[16,64,512]{2,1,0:T(8,128)(2,1)}, u32[]{:S(2)}, u32[]{:S(2)}) collective-permute-start(bf16[16,64,512]{2,1,0:T(8,128)(2,1)S(1)} %get-tuple-element.18), channel_id=1, source_target_pairs={{24,8},{25,9},{26,10},{27,11},{28,12},{29,13},{30,14},{31,15}} | collective-permute-start | bytes 3145736 | tf_op jit(solution)/shard_map/ppermute | solution.py:310
  21.1 0.6 broadcast_in_dim.97
  21.7 4.5 %all-to-all-start.1 = ((s32[4,8,1,128]{3,1,2,0:T(8,128)}), s32[4,8,1,128]{3,1,2,0:T(8,128)S(1)}, u32[]{:S(2)}, u32[]{:S(2)}) async-start(s32[4,8,1,128]{3,1,2,0:T(8,128)} %broadcast_in_dim.97), calls=%async_computation.1 | async-start | bytes 32768 | tf_op jit(solution)/shard_map/all_to_all | solution.py:321
  26.2 1.3 collective-permute-start.1
  27.5 8.3 %all-to-all-done.1 = s32[4,8,1,128]{3,1,2,0:T(8,128)S(1)} async-done(((s32[4,8,1,128]{3,1,2,0:T(8,128)}), s32[4,8,1,128]{3,1,2,0:T(8,128)S(1)}, u32[]{:S(2)}, u32[]{:S(2)}) %all-to-all-start.1) | async-done | bytes 16416 | tf_op jit(solution)/shard_map/all_to_all | solution.py:321
  36.3 0.6 convert_reduce_fusion
  37.1 1.4 broadcast_select_fusion.refs_0_
  38.5 1.3 collective-permute-start.3
  40.1 1.4 shard_map.138
  41.5 6.4 %all-to-all-start.2 = ((bf16[8,64,512]{2,1,0:T(8,128)(2,1)}), bf16[8,64,512]{2,1,0:T(8,128)(2,1)S(1)}, u32[]{:S(2)}, u32[]{:S(2)}) async-start(bf16[8,64,512]{2,1,0:T(8,128)(2,1)} %shard_map.138), calls=%async_computation.2 | async-start | bytes 1048576 | tf_op jit(solution)/shard_map/all_to_all | solution.py:369
  47.9 6.5 %copy.49 = bf16[512,4096]{0,1:T(8,128)(2,1)} copy(bf16[512,4096]{1,0:T(8,128)(2,1)} %rest_8_.1) | data formatting | bytes 8388608 | tf_op jit(solution)/shard_map/optimization_barrier | solution.py:368
  54.5 2.6 %shard_map.139 = bf16[8,64,512]{2,1,0:T(8,128)(2,1)} custom-call(s32[9]{0:T(128)S(1)} %pad_add_fusion.3.meta, bf16[16,64,512]{2,1,0:T(8,128)(2,1)S(1)} %broadcast_select_fusion.refs_0_, bf16[16,64,512]{2,1,0:T(8,128)(2,1)} %collective-permute-done.3.refs_1_), custom_call_target="tpu_custom_call" | custom-call | tf_op jit(solution)/shard_map/pallas_call | solution.py:221
  57.1 5.9 %all-to-all-done.2.refs_0_.rest_0_ = bf16[8,64,512]{2,1,0:T(8,128)(2,1)S(1)} async-done(((bf16[8,64,512]{2,1,0:T(8,128)(2,1)}), bf16[8,64,512]{2,1,0:T(8,128)(2,1)S(1)}, u32[]{:S(2)}, u32[]{:S(2)}) %all-to-all-start.2) | async-done | bytes 524320 | tf_op jit(solution)/shard_map/all_to_all | solution.py:369
  63.0 4.4 %all-to-all-start.3 = ((bf16[8,64,512]{2,1,0:T(8,128)(2,1)}), bf16[8,64,512]{2,1,0:T(8,128)(2,1)S(1)}, u32[]{:S(2)}, u32[]{:S(2)}) async-start(bf16[8,64,512]{2,1,0:T(8,128)(2,1)} %shard_map.139), calls=%async_computation.3 | async-start | bytes 1048576 | tf_op jit(solution)/shard_map/all_to_all | solution.py:369
  67.4 0.6 bitcast_convert_fusion.1.cond_ref
  68.0 0.8 copy.47
  68.8 0.8 copy.48
  69.9 0.5 broadcast.446
  70.4 0.7 fusion.34
  71.6 0.6 shard_map.140
  72.3 9.9 %all-to-all-done.3.refs_0_.rest_1_ = bf16[8,64,512]{2,1,0:T(8,128)(2,1)S(1)} async-done(((bf16[8,64,512]{2,1,0:T(8,128)(2,1)}), bf16[8,64,512]{2,1,0:T(8,128)(2,1)S(1)}, u32[]{:S(2)}, u32[]{:S(2)}) %all-to-all-start.3) | async-done | bytes 524320 | tf_op jit(solution)/shard_map/all_to_all | solution.py:369
  82.1 0.6 shard_map.141
  83.2 0.5 collective-permute-start.5
  83.9 5.8 %collective-permute-done.7.rest_5_ = bf16[4,64,512]{2,1,0:T(8,128)(2,1)S(1)} collective-permute-done((bf16[4,64,512]{2,1,0:T(8,128)(2,1)S(1)}, bf16[4,64,512]{2,1,0:T(8,128)(2,1)S(1)}, u32[]{:S(2)}, u32[]{:S(2)}) %collective-permute-start.7) | collective-permute-done | bytes 262176 | tf_op jit(solution)/shard_map/ppermute | solution.py:310
  89.7 0.6 pad_add_fusion.1.meta
  90.3 0.9 collective-permute-done.9.rest_7_
  91.4 0.5 copy-done.11
  91.9 28.3 %shard_map.142 = (bf16[256,2048]{1,0:T(8,128)(2,1)}, bf16[256,2048]{1,0:T(8,128)(2,1)}, f32[4,512]{1,0:T(4,128)}, f32[512,512]{1,0:T(8,128)}) custom-call(s32[25]{0:T(128)} %pad_add_fusion.1.meta, bf16[256,2048]{1,0:T(8,128)(2,1)} %bitcast.75, bf16[256,2048]{1,0:T(8,128)(2,1)} %bitcast.76, f32[4,512]{1,0:T(4,128)} %bitcast_convert_fusion.1.cond_ref, ...), custom_call_target="tpu_custom_call" | custom-call | flops 11811160064 | bytes 16777216 | tf_op jit(solution)/shard_map/pallas_call | solution.py:165
  120.3 1.1 fusion
  121.5 1.4 collective-permute-done.10
  122.9 1.1 bitcast_add_fusion
  124.1 0.3 collective-permute-start.11
  124.5 5.3 %collective-permute-done.11 = bf16[1,8,16,512]{3,2,1,0:T(8,128)(2,1)S(1)} collective-permute-done((bf16[1,8,16,512]{3,2,1,0:T(8,128)(2,1)S(1)}, bf16[1,8,16,512]{3,2,1,0:T(8,128)(2,1)S(1)}, u32[]{:S(2)}, u32[]{:S(2)}) %collective-permute-start.11) | collective-permute-done | bytes 131104 | tf_op jit(solution)/shard_map/ppermute | solution.py:275
  129.8 1.9 %collective-permute-start.12 = (bf16[1,4,16,512]{3,2,1,0:T(8,128)(2,1)S(1)}, bf16[1,4,16,512]{3,2,1,0:T(8,128)(2,1)S(1)}, u32[]{:S(2)}, u32[]{:S(2)}) collective-permute-start(bf16[1,4,16,512]{3,2,1,0:T(8,128)(2,1)S(1)} %fusion.2), channel_id=1, source_target_pairs={{0,1},{1,0},{2,3},{3,2},{4,5},{5,4},{6,7},{7,6},{8,9},{9,8},{10,11... | collective-permute-start | bytes 196616 | tf_op jit(solution)/shard_map/ppermute | solution.py:275
  131.7 2.4 %collective-permute-done.12 = bf16[1,4,16,512]{3,2,1,0:T(8,128)(2,1)S(1)} collective-permute-done((bf16[1,4,16,512]{3,2,1,0:T(8,128)(2,1)S(1)}, bf16[1,4,16,512]{3,2,1,0:T(8,128)(2,1)S(1)}, u32[]{:S(2)}, u32[]{:S(2)}) %collective-permute-start.12) | collective-permute-done | bytes 65568 | tf_op jit(solution)/shard_map/ppermute | solution.py:275
  134.5 3.7 %collective-permute-done.13 = bf16[1,2,16,512]{3,2,1,0:T(8,128)(2,1)S(1)} collective-permute-done((bf16[1,2,16,512]{3,2,1,0:T(8,128)(2,1)S(1)}, bf16[1,2,16,512]{3,2,1,0:T(8,128)(2,1)S(1)}, u32[]{:S(2)}, u32[]{:S(2)}) %collective-permute-start.13) | collective-permute-done | bytes 32800 | tf_op jit(solution)/shard_map/ppermute | solution.py:275
  138.2 1.6 %collective-permute-start.14 = (bf16[1,1,16,512]{3,2,1,0:T(8,128)(2,1)S(1)}, bf16[1,1,16,512]{3,2,1,0:T(8,128)(2,1)S(1)}, u32[]{:S(2)}, u32[]{:S(2)}) collective-permute-start(bf16[1,1,16,512]{3,2,1,0:T(8,128)(2,1)S(1)} %dynamic-slice_convert_fusion.3), channel_id=1, source_target_pairs={{0,4},{1,5},{2,6},{3,7},{4,0},{5,1},{6,2},{7,3},{8,12},{9,13},{10,... | collective-permute-start | bytes 49160 | tf_op jit(solution)/shard_map/ppermute | solution.py:275
  139.8 3.1 %collective-permute-done.14 = bf16[1,1,16,512]{3,2,1,0:T(8,128)(2,1)S(1)} collective-permute-done((bf16[1,1,16,512]{3,2,1,0:T(8,128)(2,1)S(1)}, bf16[1,1,16,512]{3,2,1,0:T(8,128)(2,1)S(1)}, u32[]{:S(2)}, u32[]{:S(2)}) %collective-permute-start.14) | collective-permute-done | bytes 16416 | tf_op jit(solution)/shard_map/ppermute | solution.py:275
  142.9 0.6 add_bitcast_fusion
  (83 shorter events, 3.7 us)
Async XLA Ops:
  2.0 11.1 %collective-permute-start = (bf16[16,64,512]{2,1,0:T(8,128)(2,1)S(1)}, bf16[16,64,512]{2,1,0:T(8,128)(2,1)S(1)}, u32[]{:S(2)}, u32[]{:S(2)}) collective-permute-start(bf16[16,64,512]{2,1,0:T(8,128)(2,1)S(1)} %slice.33), channel_id=1, source_target_pairs={{24,8},{25,9},{26,10},{27,11},{28,12},{29,13},{30,14},{31,15}} | collective-permute-start | bytes 3145736 | tf_op jit(solution)/shard_map/ppermute | solution.py:310
  5.7 13.7 %all-to-all-start = ((s32[8,1,128]{2,1,0:T(1,128)}), s32[8,1,128]{2,1,0:T(1,128)S(1)}, u32[]{:S(2)}, u32[]{:S(2)}) async-start(s32[8,1,128]{2,1,0:T(1,128)} %broadcast_in_dim.95), calls=%async_computation | async-start | bytes 8192 | tf_op jit(solution)/shard_map/all_to_all | solution.py:321
  14.8 22.3 %copy-start.2 = (bf16[16,64,512]{2,1,0:T(8,128)(2,1)}, bf16[16,64,512]{2,1,0:T(8,128)(2,1)S(1)}, u32[]{:S(2)}) copy-start(bf16[16,64,512]{2,1,0:T(8,128)(2,1)S(1)} %get-tuple-element.18) | copy-start | bytes 3145732
  19.4 17.7 %collective-permute-start.2 = (bf16[16,64,512]{2,1,0:T(8,128)(2,1)S(1)}, bf16[16,64,512]{2,1,0:T(8,128)(2,1)}, u32[]{:S(2)}, u32[]{:S(2)}) collective-permute-start(bf16[16,64,512]{2,1,0:T(8,128)(2,1)S(1)} %get-tuple-element.18), channel_id=1, source_target_pairs={{24,8},{25,9},{26,10},{27,11},{28,12},{29,13},{30,14},{31,15}} | collective-permute-start | bytes 3145736 | tf_op jit(solution)/shard_map/ppermute | solution.py:310
  21.7 14.1 %all-to-all-start.1 = ((s32[4,8,1,128]{3,1,2,0:T(8,128)}), s32[4,8,1,128]{3,1,2,0:T(8,128)S(1)}, u32[]{:S(2)}, u32[]{:S(2)}) async-start(s32[4,8,1,128]{3,1,2,0:T(8,128)} %broadcast_in_dim.97), calls=%async_computation.1 | async-start | bytes 32768 | tf_op jit(solution)/shard_map/all_to_all | solution.py:321
  26.2 13.9 %collective-permute-start.1 = (bf16[16,64,512]{2,1,0:T(8,128)(2,1)S(1)}, bf16[16,64,512]{2,1,0:T(8,128)(2,1)S(1)}, u32[]{:S(2)}, u32[]{:S(2)}) collective-permute-start(bf16[16,64,512]{2,1,0:T(8,128)(2,1)S(1)} %get-tuple-element.31.refs_0_), channel_id=1, source_target_pairs={{24,16},{25,17},{26,18},{27,19},{28,20},{29,21},{30,22},{31,23},{8... | collective-permute-start | bytes 3145736 | tf_op jit(solution)/shard_map/ppermute | solution.py:310
  38.5 16.1 %collective-permute-start.3 = (bf16[16,64,512]{2,1,0:T(8,128)(2,1)S(1)}, bf16[16,64,512]{2,1,0:T(8,128)(2,1)}, u32[]{:S(2)}, u32[]{:S(2)}) collective-permute-start(bf16[16,64,512]{2,1,0:T(8,128)(2,1)S(1)} %broadcast_select_fusion.refs_0_), channel_id=1, source_target_pairs={{24,16},{25,17},{26,18},{27,19},{28,20},{29,21},{30,22},{31,23},{8... | collective-permute-start | bytes 3145736 | tf_op jit(solution)/shard_map/ppermute | solution.py:310
  41.5 21.4 %all-to-all-start.2 = ((bf16[8,64,512]{2,1,0:T(8,128)(2,1)}), bf16[8,64,512]{2,1,0:T(8,128)(2,1)S(1)}, u32[]{:S(2)}, u32[]{:S(2)}) async-start(bf16[8,64,512]{2,1,0:T(8,128)(2,1)} %shard_map.138), calls=%async_computation.2 | async-start | bytes 1048576 | tf_op jit(solution)/shard_map/all_to_all | solution.py:369
  47.9 19.5 %copy-start.5 = (bf16[1,1,4,512]{3,2,1,0:T(4,128)(2,1)S(1)}, bf16[1,1,4,512]{3,2,1,0:T(4,128)(2,1)}, u32[]{:S(2)}) copy-start(bf16[1,1,4,512]{3,2,1,0:T(4,128)(2,1)} %param.13) | copy-start | bytes 12292
  47.9 20.1 %copy-start.4 = (bf16[256,512]{1,0:T(8,128)(2,1)S(1)}, bf16[256,512]{1,0:T(8,128)(2,1)}, u32[]{:S(2)}) copy-start(bf16[256,512]{1,0:T(8,128)(2,1)} %up_ref.1) | copy-start | bytes 786436
  54.5 14.3 %copy-start.3 = (bf16[512,256]{1,0:T(8,128)(2,1)S(1)}, bf16[512,256]{1,0:T(8,128)(2,1)}, u32[]{:S(2)}) copy-start(bf16[512,256]{1,0:T(8,128)(2,1)} %down_ref.1) | copy-start | bytes 786436
  63.0 28.2 %copy-start = (bf16[8,64,512]{2,1,0:T(8,128)(2,1)}, bf16[8,64,512]{2,1,0:T(8,128)(2,1)S(1)}, u32[]{:S(2)}) copy-start(bf16[8,64,512]{2,1,0:T(8,128)(2,1)S(1)} %all-to-all-done.2.refs_0_.rest_0_) | copy-start | bytes 1572868
  63.0 19.1 %all-to-all-start.3 = ((bf16[8,64,512]{2,1,0:T(8,128)(2,1)}), bf16[8,64,512]{2,1,0:T(8,128)(2,1)S(1)}, u32[]{:S(2)}, u32[]{:S(2)}) async-start(bf16[8,64,512]{2,1,0:T(8,128)(2,1)} %shard_map.139), calls=%async_computation.3 | async-start | bytes 1048576 | tf_op jit(solution)/shard_map/all_to_all | solution.py:369
  72.2 11.5 %collective-permute-start.6 = (bf16[4,64,512]{2,1,0:T(8,128)(2,1)S(1)}, bf16[4,64,512]{2,1,0:T(8,128)(2,1)S(1)}, u32[]{:S(2)}, u32[]{:S(2)}) collective-permute-start(bf16[4,64,512]{2,1,0:T(8,128)(2,1)S(1)} %shard_map.140), channel_id=1, source_target_pairs={{0,16},{1,17},{2,18},{3,19},{4,20},{5,21},{6,22},{7,23},{8,24},{9,... | collective-permute-start | bytes 786440 | tf_op jit(solution)/shard_map/ppermute | solution.py:310
  82.1 9.1 %copy-start.1 = (bf16[8,64,512]{2,1,0:T(8,128)(2,1)}, bf16[8,64,512]{2,1,0:T(8,128)(2,1)S(1)}, u32[]{:S(2)}) copy-start(bf16[8,64,512]{2,1,0:T(8,128)(2,1)S(1)} %all-to-all-done.3.refs_0_.rest_1_) | copy-start | bytes 1572868
  82.7 6.9 %collective-permute-start.7 = (bf16[4,64,512]{2,1,0:T(8,128)(2,1)S(1)}, bf16[4,64,512]{2,1,0:T(8,128)(2,1)S(1)}, u32[]{:S(2)}, u32[]{:S(2)}) collective-permute-start(bf16[4,64,512]{2,1,0:T(8,128)(2,1)S(1)} %shard_map.141), channel_id=1, source_target_pairs={{0,16},{1,17},{2,18},{3,19},{4,20},{5,21},{6,22},{7,23},{8,24},{9,... | collective-permute-start | bytes 786440 | tf_op jit(solution)/shard_map/ppermute | solution.py:310
  83.2 7.1 %collective-permute-start.4 = (bf16[8,64,512]{2,1,0:T(8,128)(2,1)S(1)}, bf16[8,64,512]{2,1,0:T(8,128)(2,1)S(1)}, u32[]{:S(2)}, u32[]{:S(2)}) collective-permute-start(bf16[8,64,512]{2,1,0:T(8,128)(2,1)S(1)} %all-to-all-done.2.refs_0_.rest_0_), channel_id=1, source_target_pairs={{0,8},{1,9},{2,10},{3,11},{4,12},{5,13},{6,14},{7,15},{8,0},{9,1},... | collective-permute-start | bytes 1572872 | tf_op jit(solution)/shard_map/ppermute | solution.py:310
  83.2 7.1 %collective-permute-start.5 = (bf16[8,64,512]{2,1,0:T(8,128)(2,1)S(1)}, bf16[8,64,512]{2,1,0:T(8,128)(2,1)S(1)}, u32[]{:S(2)}, u32[]{:S(2)}) collective-permute-start(bf16[8,64,512]{2,1,0:T(8,128)(2,1)S(1)} %all-to-all-done.3.refs_0_.rest_1_), channel_id=1, source_target_pairs={{0,8},{1,9},{2,10},{3,11},{4,12},{5,13},{6,14},{7,15},{8,0},{9,1},... | collective-permute-start | bytes 1572872 | tf_op jit(solution)/shard_map/ppermute | solution.py:310
  83.7 7.5 %copy-start.8 = (bf16[4,64,512]{2,1,0:T(8,128)(2,1)}, bf16[4,64,512]{2,1,0:T(8,128)(2,1)S(1)}, u32[]{:S(2)}) copy-start(bf16[4,64,512]{2,1,0:T(8,128)(2,1)S(1)} %collective-permute-done.6.rest_4_) | copy-start | bytes 786436
  83.7 6.6 %collective-permute-start.8 = (bf16[4,64,512]{2,1,0:T(8,128)(2,1)S(1)}, bf16[4,64,512]{2,1,0:T(8,128)(2,1)S(1)}, u32[]{:S(2)}, u32[]{:S(2)}) collective-permute-start(bf16[4,64,512]{2,1,0:T(8,128)(2,1)S(1)} %collective-permute-done.6.rest_4_), channel_id=1, source_target_pairs={{0,8},{1,9},{2,10},{3,11},{4,12},{5,13},{6,14},{7,15},{8,0},{9,1},... | collective-permute-start | bytes 786440 | tf_op jit(solution)/shard_map/ppermute | solution.py:310
  89.7 1.6 %copy-start.9 = (bf16[4,64,512]{2,1,0:T(8,128)(2,1)}, bf16[4,64,512]{2,1,0:T(8,128)(2,1)S(1)}, u32[]{:S(2)}) copy-start(bf16[4,64,512]{2,1,0:T(8,128)(2,1)S(1)} %collective-permute-done.7.rest_5_) | copy-start | bytes 786436
  89.7 1.5 %collective-permute-start.9 = (bf16[4,64,512]{2,1,0:T(8,128)(2,1)S(1)}, bf16[4,64,512]{2,1,0:T(8,128)(2,1)S(1)}, u32[]{:S(2)}, u32[]{:S(2)}) collective-permute-start(bf16[4,64,512]{2,1,0:T(8,128)(2,1)S(1)} %collective-permute-done.7.rest_5_), channel_id=1, source_target_pairs={{0,8},{1,9},{2,10},{3,11},{4,12},{5,13},{6,14},{7,15},{8,0},{9,1},... | collective-permute-start | bytes 786440 | tf_op jit(solution)/shard_map/ppermute | solution.py:310
  90.3 0.9 copy-start.10
  90.3 0.9 copy-start.6
  90.3 1.1 copy-start.7
  91.2 0.7 copy-start.11
  121.3 1.6 %collective-permute-start.10 = (bf16[2,8,16,512]{3,2,1,0:T(8,128)(2,1)S(1)}, bf16[2,8,16,512]{3,2,1,0:T(8,128)(2,1)S(1)}, u32[]{:S(2)}, u32[]{:S(2)}) collective-permute-start(bf16[2,8,16,512]{3,2,1,0:T(8,128)(2,1)S(1)} %fusion), channel_id=1, source_target_pairs={{0,8},{8,0},{16,24},{24,16},{1,9},{9,1},{17,25},{25,17},{2,10},{10... | collective-permute-start | bytes 786440 | tf_op jit(solution)/shard_map/ppermute | solution.py:275
  124.1 5.6 %collective-permute-start.11 = (bf16[1,8,16,512]{3,2,1,0:T(8,128)(2,1)S(1)}, bf16[1,8,16,512]{3,2,1,0:T(8,128)(2,1)S(1)}, u32[]{:S(2)}, u32[]{:S(2)}) collective-permute-start(bf16[1,8,16,512]{3,2,1,0:T(8,128)(2,1)S(1)} %dynamic-slice_convert_fusion), channel_id=1, source_target_pairs={{0,16},{8,24},{16,0},{24,8},{1,17},{9,25},{17,1},{25,9},{2,18},{10... | collective-permute-start | bytes 393224 | tf_op jit(solution)/shard_map/ppermute | solution.py:275
  129.8 4.3 %collective-permute-start.12 = (bf16[1,4,16,512]{3,2,1,0:T(8,128)(2,1)S(1)}, bf16[1,4,16,512]{3,2,1,0:T(8,128)(2,1)S(1)}, u32[]{:S(2)}, u32[]{:S(2)}) collective-permute-start(bf16[1,4,16,512]{3,2,1,0:T(8,128)(2,1)S(1)} %fusion.2), channel_id=1, source_target_pairs={{0,1},{1,0},{2,3},{3,2},{4,5},{5,4},{6,7},{7,6},{8,9},{9,8},{10,11... | collective-permute-start | bytes 196616 | tf_op jit(solution)/shard_map/ppermute | solution.py:275
  134.2 4.0 %collective-permute-start.13 = (bf16[1,2,16,512]{3,2,1,0:T(8,128)(2,1)S(1)}, bf16[1,2,16,512]{3,2,1,0:T(8,128)(2,1)S(1)}, u32[]{:S(2)}, u32[]{:S(2)}) collective-permute-start(bf16[1,2,16,512]{3,2,1,0:T(8,128)(2,1)S(1)} %fusion.3), channel_id=1, source_target_pairs={{0,2},{1,3},{2,0},{3,1},{4,6},{5,7},{6,4},{7,5},{8,10},{9,11},{10,... | collective-permute-start | bytes 98312 | tf_op jit(solution)/shard_map/ppermute | solution.py:275
  138.2 4.7 %collective-permute-start.14 = (bf16[1,1,16,512]{3,2,1,0:T(8,128)(2,1)S(1)}, bf16[1,1,16,512]{3,2,1,0:T(8,128)(2,1)S(1)}, u32[]{:S(2)}, u32[]{:S(2)}) collective-permute-start(bf16[1,1,16,512]{3,2,1,0:T(8,128)(2,1)S(1)} %dynamic-slice_convert_fusion.3), channel_id=1, source_target_pairs={{0,4},{1,5},{2,6},{3,7},{4,0},{5,1},{6,2},{7,3},{8,12},{9,13},{10,... | collective-permute-start | bytes 49160 | tf_op jit(solution)/shard_map/ppermute | solution.py:275

commit v8 on v6

--- a/solution.py
+++ b/solution.py
@@ -10,7 +10,6 @@
 HEADS = 16
 HEAD = 128
 SPAN = 64
-PARTS = 2
 
 EPSILON = 1e-06
 FLOOR = -1e30
@@ -25,22 +24,21 @@
 
 
 def span_kernel(
-    held_count, nbr_count, parts, meta,
-    q_ref, cot_ref, cond_ref, gain_ref, down_ref, up_ref, upt_ref, downt_ref, *rest,
+    nbr_count, meta,
+    q_ref, cot_ref, own_ref, got_ref, cond_ref, gain_ref, down_ref, up_ref, upt_ref, downt_ref,
+    kv_hbm, kvt_hbm, out_ref, qg_ref, cg_ref, ad_ref,
+    kv_ref, kvt_ref, proj_ref, grad_ref, score_ref, dprob_ref, prob_ref, dscore_ref,
+    q2_ref, cot2_ref, acc_ref, kv_sem,
 ):
-    held_refs = rest[:held_count]
-    (kv_hbm, kvt_hbm, out_ref, qg_ref, cg_ref, ad_ref,
-     raw_ref, kv_ref, kvt_ref, proj_ref, grad_ref, score_ref, dprob_ref, prob_ref, dscore_ref,
-     q2_ref, cot2_ref, acc_ref, sems, kv_sem) = rest[held_count:]
     span = pl.program_id(0)
-    per_device, slot_len, width = raw_ref.shape
+    slot_len, width = own_ref.shape[1:]
     key_count = nbr_count * slot_len
     head_cols = q_ref.shape[1]
     rank = down_ref.shape[1]
     scaling = HEAD ** (-0.5)
     live = meta[0] == 1
-    lens, which, index = 1, 1 + per_device, 1 + 2 * per_device
-    piece = slot_len // parts
+    carrier = meta[1] == 1
+    lens = 2
     pairs = [pl.ds(i * 2 * HEAD, 2 * HEAD) for i in range(HEADS // 2)]
     value_pairs = [pl.ds(head_cols + i * 2 * HEAD, 2 * HEAD) for i in range(HEADS // 2)]
     lanes = [pl.ds(i * 2 * SPAN, 2 * SPAN) for i in range(HEADS // 2)]
@@ -49,16 +47,6 @@
 
     @pl.when(span == 0)
     def _():
-        for n in range(per_device):
-            for b, held in enumerate(held_refs):
-                @pl.when(meta[which + n] == b // parts)
-                def _():
-                    part = b % parts
-                    pltpu.make_async_copy(
-                        held.at[meta[index + n]],
-                        raw_ref.at[n, pl.ds(part * piece, piece)],
-                        sems.at[n * parts + part],
-                    ).start()
         kv_copy.start()
         kvt_copy.start()
 
@@ -70,15 +58,7 @@
         q2_ref[tokens, cols] = q_ref[:, cols]
         cot2_ref[tokens, cols] = cot_ref[:, cols]
 
-    for n in range(nbr_count):
-        for part in range(parts):
-            item = span * nbr_count + n
-            pltpu.make_async_copy(
-                held_refs[0].at[0],
-                raw_ref.at[item, pl.ds(part * piece, piece)],
-                sems.at[item * parts + part],
-            ).wait()
-    raw = raw_ref[pl.ds(span * nbr_count, nbr_count)]
+    raw = jnp.where(carrier, own_ref[...], got_ref[...])
     x_full = raw.reshape(key_count, width).astype(jnp.float32) + cond_ref[pl.ds(span, 1), :]
     inv_rms = lax.rsqrt(jnp.mean(x_full * x_full, axis=-1, keepdims=True) + EPSILON)
     gain = gain_ref[...]
@@ -148,26 +128,27 @@
         ad_ref[...] = jnp.where(live, acc_ref[...], 0.0).astype(ad_ref.dtype)
 
 
-def run_spans(meta, query, cot, cond, held, parts, gain, w_down, w_up, w_kv, nbr_count):
+def run_spans(meta, query, cot, own, got, cond, gain, w_down, w_up, w_kv, w_kv_t, nbr_count):
     span_count, width = cond.shape
     token_count, head_cols = query.shape
-    slot_len = held[0].shape[1] * parts
+    slot_len = own.shape[1]
     rank = w_down.shape[1]
     whole = lambda a: pl.BlockSpec(a.shape, lambda s, m: (0,) * a.ndim, pipeline_mode=pl.Buffered(1))
     tokens = pl.BlockSpec((SPAN, head_cols), lambda s, m: (s, 0))
     small = [cond, gain.reshape(1, width), w_down, w_up, w_up.T, w_down.T]
-    large = list(held) + [w_kv, w_kv.T]
+    blocks = pl.BlockSpec((nbr_count, slot_len, width), lambda s, m: (s, 0, 0))
+    large = [w_kv, w_kv_t]
     per_device = span_count * nbr_count
     keys = nbr_count * slot_len
     rows = per_device * slot_len
     lanes = SPAN * HEADS
     flops = 2 * rows * (2 * width * 2 * head_cols + 6 * width * rank + 6 * SPAN * head_cols)
     return pl.pallas_call(
-        functools.partial(span_kernel, len(held), nbr_count, parts),
+        functools.partial(span_kernel, nbr_count),
         grid_spec=pltpu.PrefetchScalarGridSpec(
             num_scalar_prefetch=1,
             grid=(span_count,),
-            in_specs=[tokens, tokens]
+            in_specs=[tokens, tokens, blocks, blocks]
             + [whole(a) for a in small]
             + [pl.BlockSpec(memory_space=pltpu.HBM)] * len(large),
             out_specs=[
@@ -177,7 +158,6 @@
                 pl.BlockSpec((width, 2 * rank), lambda s, m: (0, 0)),
             ],
             scratch_shapes=[
-                pltpu.VMEM((per_device, slot_len, width), jnp.bfloat16),
                 pltpu.VMEM((width, 2 * head_cols), jnp.bfloat16),
                 pltpu.VMEM((2 * head_cols, width), jnp.bfloat16),
                 pltpu.VMEM((keys, 2 * head_cols), jnp.bfloat16),
@@ -189,7 +169,6 @@
                 pltpu.VMEM((2 * SPAN, head_cols), jnp.bfloat16),
                 pltpu.VMEM((2 * SPAN, head_cols), jnp.bfloat16),
                 pltpu.VMEM((width, 2 * rank), jnp.float32),
-                pltpu.SemaphoreType.DMA((per_device * parts,)),
                 pltpu.SemaphoreType.DMA((2,)),
             ],
         ),
@@ -203,39 +182,43 @@
         cost_estimate=pl.CostEstimate(
             flops=flops, bytes_accessed=16 * 2**20, transcendentals=rows * SPAN * HEADS
         ),
-    )(meta, query, cot, *small, *large)
+    )(meta, query, cot, own, got, *small, *large)
 
 
 def pick_kernel(held_count, meta, *refs):
-    held_refs, out_ref, sems = refs[:held_count], refs[held_count], refs[held_count + 1]
-    for b, held in enumerate(held_refs):
-        @pl.when(meta[0] == b)
-        def _():
-            for n in range(out_ref.shape[0]):
-                pltpu.make_async_copy(held.at[meta[1 + n]], out_ref.at[n], sems.at[n]).start()
-    for n in range(out_ref.shape[0]):
-        pltpu.make_async_copy(held_refs[0].at[0], out_ref.at[n], sems.at[n]).wait()
-
-
-def pick(which, index, held):
+    held_refs, out_refs = refs[:held_count], refs[held_count:]
+    count = sum(out.shape[0] for out in out_refs)
+    start = 0
+    for out in out_refs:
+        def one(n, _, out=out, start=start):
+            for b, held in enumerate(held_refs):
+                @pl.when(meta[start + n] == b)
+                def _():
+                    out[n] = held[meta[count + start + n]]
+            return 0
+
+        lax.fori_loop(0, out.shape[0], one, 0)
+        start += out.shape[0]
+
+
+def pick(which, index, held, outs):
     count = index.shape[0]
-    meta = jnp.concatenate([jnp.reshape(which, (1,)), index]).astype(jnp.int32)
+    meta = jnp.concatenate([which, index]).astype(jnp.int32)
+    shape = jax.ShapeDtypeStruct((count // outs,) + held[0].shape[1:], held[0].dtype)
     return pl.pallas_call(
         functools.partial(pick_kernel, len(held)),
         grid_spec=pltpu.PrefetchScalarGridSpec(
             num_scalar_prefetch=1,
             grid=(1,),
-            in_specs=[pl.BlockSpec(memory_space=pltpu.HBM)] * len(held),
-            out_specs=pl.BlockSpec(memory_space=pltpu.VMEM),
-            scratch_shapes=[pltpu.SemaphoreType.DMA((count,))],
+            in_specs=[pl.BlockSpec(memory_space=pltpu.VMEM)] * len(held),
+            out_specs=[pl.BlockSpec(memory_space=pltpu.VMEM)] * outs,
         ),
-        out_shape=jax.ShapeDtypeStruct((count,) + held[0].shape[1:], held[0].dtype),
-        compiler_params=pltpu.CompilerParams(vmem_limit_bytes=60 * 2**20),
+        out_shape=[shape] * outs,
+        compiler_params=pltpu.CompilerParams(vmem_limit_bytes=20 * 2**20),
     )(meta, *held)
 
 
-def place_requests(owners, per_device, pool_count, lanes):
-    half = pool_count // 2
+def place_requests(owners, per_device, half, lanes):
     count = owners.shape[1]
     order = jnp.arange(count, dtype=jnp.int32)
     side = (order // per_device) // half
@@ -248,11 +231,9 @@
     crosses = rank >= lanes
     far = crosses[:, None, :]
     number = total(far & mate[None] & (lower | (same & before[None])))
-    first = total(far & ~mate[None] & lower)
     guests = total(far & ~mate[None] & same)
-    lane = jnp.where(crosses, number, first + guests + rank) % lanes
-    row = jnp.where(crosses, 1 - side[None, :], side[None, :]) * half + lane % half
-    return row, lane // half, crosses, number // half
+    slot = jnp.where(crosses, rank - lanes, guests + rank)
+    return slot, crosses, number, jnp.broadcast_to(side[None], owners.shape)
 
 
 def scatter_sum(total, axes):
@@ -299,31 +280,27 @@
     block_count, slot_len = database.shape[2:4]
     live_count = relay_row * per_device
     capacity = max(2, live_count // columns + 1)
-    slots = -(-capacity // pool_count)
-    lanes = half * slots
-    most = 0
-    if capacity > lanes:
-        for rows in (half, relay_row - half):
-            full, left = divmod(rows * per_device, capacity)
-            most = max(most, full * (capacity - lanes) + max(0, left - lanes))
-    crossing = -(-most // half)
+    lanes = -(-capacity // 2)
+    crossing = 0
+    for rows in (half, relay_row - half):
+        full, left = divmod(rows * per_device, capacity)
+        crossing = max(crossing, full * (capacity - lanes) + max(0, left - lanes))
     token_count, head_cols = queries.shape[2:]
-
-    def hop(array, pairs):
+    carriers = (half - 1, relay_row)
+
+    def hop(array, pairs, shift=0):
         return lax.ppermute(
-            array, axes, [(a * columns + j, b * columns + j) for a, b in pairs for j in range(columns)]
+            array,
+            axes,
+            [(a * columns + j, b * columns + (j + shift) % columns) for a, b in pairs for j in range(columns)],
         )
-
-    parts = PARTS if slot_len % (PARTS * 16) == 0 else 1
-    piece = slot_len // parts
-    full_store = database.reshape(block_count, slot_len, width)
-    store = [full_store[:, i * piece : (i + 1) * piece] for i in range(parts)]
 
     def to_all(array, axis):
         copies = jnp.broadcast_to(array[None], (lax.axis_size(axis),) + array.shape)
         return lax.all_to_all(copies, axis, split_axis=0, concat_axis=0, tiled=True)
 
-    across = [hop(a, [(relay_row, relay_row - half)]) for a in store]
+    store = database.reshape(block_count, slot_len, width)
+    across = hop(store, [(relay_row, half - 1)])
 
     info = jnp.concatenate([nbr_owner.reshape(-1), nbr_block.reshape(-1), lengths.reshape(-1)])
     info = jnp.pad(info, (0, -info.shape[0] % 128))
@@ -334,70 +311,77 @@
     owners = by_column[:, :, :per_device].reshape(columns, live_count)
     blocks = by_column[:, :, per_device : 2 * per_device].reshape(columns, live_count)
     store_len = table[relay_row, :, 2 * per_device : 2 * per_device + block_count]
-    carrier, slot, crosses, number = place_requests(owners, per_device, pool_count, lanes)
-
-    ring = jnp.arange(slots, dtype=jnp.int32)
-    mine = ((owners == me) & (carrier == row))[:, None, :] & (slot[:, None, :] == ring[None, :, None])
-    slot_block = jnp.sum(jnp.where(mine, blocks[:, None, :], 0), axis=2).reshape(-1)
+    slot, crosses, number, side = place_requests(owners, per_device, half, lanes)
+    held_side = jnp.where(crosses, 1 - side, side)
+    my_side = row // half
+
+    target = (me + jnp.arange(columns, dtype=jnp.int32)) % columns
+    ring = jnp.arange(lanes, dtype=jnp.int32)
+    mine = ((owners == me) & (held_side == my_side))[:, None, :] & (
+        slot[:, None, :] == ring[None, :, None]
+    )
+    slot_block = jnp.sum(jnp.where(mine, blocks[:, None, :], 0), axis=2)
+    slot_block = jnp.take(slot_block, target, axis=0).reshape(-1)
+    source = jnp.broadcast_to(jnp.where(row == relay_row, 0, 1), slot_block.shape)
+    sends = pick(source, slot_block, [store, across], columns)
+    w_kv, sends = lax.optimization_barrier((w_kv, sends))
+    arrived = [sends[0]] + [
+        hop(sends[shift], [(c, c) for c in carriers], shift) for shift in range(1, columns)
+    ]
 
     mine_of = lambda a: lax.dynamic_index_in_dim(a, me, 0, keepdims=False)
-    my_owner, my_block, my_carrier, my_slot, my_cross, my_number = map(
-        mine_of, (owners, blocks, carrier, slot, crosses, number)
-    )
-    place = my_owner * slots + my_slot
-    ring = jnp.arange(crossing, dtype=jnp.int32)
-    mine = (my_cross & (my_carrier == row))[None, :] & (my_number[None, :] == ring[:, None])
-    leaving_place = jnp.sum(jnp.where(mine, place[None, :], 0), axis=1)
-
-    def share(array, step):
-        return hop(array, [(p, p // half * half + (p + step) % half) for p in range(pool_count)])
-
-    held = []
-    for i in range(parts):
-        stores = [store[i], across[i]]
-        held_by = jnp.where(row == relay_row, 0, 1)
-        for step in range(1, half):
-            for near, array in ((relay_row, store[i]), (relay_row - half, across[i])):
-                stores.append(hop(array, [(near, near - step)]))
-                held_by = jnp.where(row == near - step, len(stores) - 1, held_by)
-        sends = pick(held_by, slot_block, stores)
-        arrived = lax.all_to_all(sends, "dp", split_axis=0, concat_axis=0, tiled=True)
-        here = [arrived] + [share(arrived, step) for step in range(1, half)]
-        if crossing:
-            leaving = pick(0, leaving_place, [arrived])
-            landed = hop(leaving, [(p, (p + half) % pool_count) for p in range(pool_count)])
-            here += [landed] + [share(landed, step) for step in range(1, half)]
-        held.append(here)
-    origin = jnp.where(my_cross, (my_carrier + half) % pool_count, my_carrier)
-    which = (row - origin) % half + jnp.where(my_cross, half, 0)
-    index = jnp.where(my_cross, my_number, place)
-    held = [here[b] for b in range(len(held[0])) for here in held]
+    my_owner, my_block, my_slot, my_cross, my_number, my_held = map(
+        mine_of, (owners, blocks, slot, crosses, number, held_side)
+    )
+    shift = (me - my_owner) % columns
+    w_kv_t = w_kv.T
+    if crossing:
+        ring = jnp.arange(crossing, dtype=jnp.int32)
+        mine = (my_cross & (my_held == my_side))[None, :] & (my_number[None, :] == ring[:, None])
+        chosen = lambda a: jnp.sum(jnp.where(mine, a[None, :], 0), axis=1)
+        w_kv_t, leaving = lax.optimization_barrier((w_kv_t, (chosen(shift), chosen(my_slot))))
+        (leaving,) = pick(*leaving, arrived, 1)
+        arrived.append(hop(leaving, [carriers, carriers[::-1]]))
+    source = jnp.where(my_cross, columns, shift).reshape(relay_row, per_device)
+    index = jnp.where(my_cross, my_number, my_slot).reshape(relay_row, per_device)
+    order = jnp.minimum(my_side * half + jnp.arange(half, dtype=jnp.int32), relay_row - 1)
+    sorted_rows = pick(
+        jnp.take(source, order, axis=0).reshape(-1),
+        jnp.take(index, order, axis=0).reshape(-1),
+        arrived,
+        half,
+    )
+    got = jnp.zeros_like(sorted_rows[0])
+    for place in range(half - 1):
+        passed = hop(sorted_rows[place], [(c, c - (half - 1 - place)) for c in carriers])
+        got = passed if half == 2 else jnp.where(row % half == place, passed, got)
+    own = sorted_rows[half - 1]
 
     own_row = jnp.minimum(row, relay_row - 1)
     hot = (my_owner * block_count + my_block)[:, None] == jnp.arange(
         columns * block_count, dtype=jnp.int32
     )[None, :]
     wanted_len = jnp.sum(jnp.where(hot, store_len.reshape(1, -1), 0), axis=1)
-    own = lambda a: lax.dynamic_index_in_dim(
-        a.reshape(relay_row, per_device), own_row, 0, keepdims=False
-    )
-    live = (row < relay_row).astype(jnp.int32)
-    meta = jnp.concatenate([live[None], own(wanted_len), own(which), own(index)]).astype(jnp.int32)
+    my_len = lax.dynamic_index_in_dim(
+        wanted_len.reshape(relay_row, per_device), own_row, 0, keepdims=False
+    )
+    flags = jnp.stack([row < relay_row, row % half == half - 1])
+    meta = jnp.concatenate([flags.astype(jnp.int32), my_len])
 
     attn_out, q_grad, cond_grad, terms = run_spans(
         meta,
         queries.reshape(token_count, head_cols),
         cotangent.reshape(token_count, head_cols),
+        own,
+        got,
         cond.reshape(span_count, width).astype(jnp.float32),
-        held,
-        parts,
         gain,
         w_down,
         w_up,
         w_kv,
+        w_kv_t,
         nbr_count,
     )
-
     adapter_grad = scatter_sum(terms, axes)
     return (
         attn_out.reshape(1, 1, token_count, head_cols),

time: 147 us -> 152 us (1.034)
  waiting for transfers between devices: 45.1 us -> 57.6 us
  starting transfers between devices: 38.3 us -> 27.7 us
  local copies, waits for them, and re-layouts: 16.1 us -> 24.6 us
  Pallas kernels: 38.5 us -> 34.4 us
    ppermute x12 -> x10, waiting for transfers between devices: 8.89 us -> 29.8 us  [hop(): lax.ppermute(array, axes, [(a * columns + j, b * columns + (j + shift) %...]
    all_to_all x2 -> x0, waiting for transfers between devices: 12.5 us -> none  [body(): lax.all_to_all(sends, 'dp', split_axis=0, concat_axis=0, tiled=True)]
    all_to_all x2 -> x0, starting transfers between devices: 10.2 us -> none  [body(): lax.all_to_all(sends, 'dp', split_axis=0, concat_axis=0, tiled=True)]
    optimization_barrier x1, local copies, waits for them, and re-layouts: 0.01 us -> 6.47 us  [body(): w_kv, sends = lax.optimization_barrier((w_kv, sends))]
    pallas_call x4 -> x3, Pallas kernels: 10.1 us -> 6.25 us  [pick(): pl.pallas_call(functools.partial(pick_kernel, len(held)), grid_spec=pltpu...]
    ppermute x5, starting transfers between devices: 6.72 us -> 9.63 us  [scatter_sum(): lax.ppermute(give.astype(jnp.bfloat16), axis, [(i, i ^ bit) for i in rang...]
    all_to_all x2, waiting for transfers between devices: 10.1 us -> 12.6 us  [to_all(): return lax.all_to_all(copies, axis, split_axis=0, concat_axis=0, tiled=True)]
    unnamed x39 -> x24, local copies, waits for them, and re-layouts: 10.3 us -> 12.7 us
  transfers between devices with their start and end apart: 21 -> 17, of which waited for: 13 -> 8; matrix products, arithmetic and copies ran while one was open for 11% -> 12% of each run, Pallas kernels for 7% -> 0%
where the time goes in v8:
time: 152 us; the launch traced here: 151 us
  waiting for transfers between devices  57.6 us (38%)
  Pallas kernels  34.4 us (23%)
  starting transfers between devices  27.7 us (18%)
  local copies, waits for them, and re-layouts  24.6 us (16%)
  other arithmetic  5.6 us (4%)
    ppermute x10, waiting for transfers between devices, hop(): lax.ppermute(array, axes, [(a * columns + j, b * columns + (j + shift) %...  29.8 us
    pallas_call x1, Pallas kernels, run_spans(): pl.pallas_call(functools.partial(span_kernel, nbr_count), grid_spec=pltpu...  28.2 us
    ppermute x5, waiting for transfers between devices, scatter_sum(): lax.ppermute(give.astype(jnp.bfloat16), axis, [(i, i ^ bit) for i in rang...  15.2 us
    unnamed x24, local copies, waits for them, and re-layouts  12.7 us
    all_to_all x2, waiting for transfers between devices, to_all(): return lax.all_to_all(copies, axis, split_axis=0, concat_axis=0, tiled=True)  12.6 us
    all_to_all x2, starting transfers between devices, to_all(): return lax.all_to_all(copies, axis, split_axis=0, concat_axis=0, tiled=True)  10.5 us
    ppermute x5, starting transfers between devices, scatter_sum(): lax.ppermute(give.astype(jnp.bfloat16), axis, [(i, i ^ bit) for i in rang...  9.63 us
    ppermute x10, starting transfers between devices, hop(): lax.ppermute(array, axes, [(a * columns + j, b * columns + (j + shift) %...  7.52 us
  transfers between devices with their start and end apart: 17, of which 8 were waited for; matrix products, arithmetic and copies ran while one was open for 12% of the time, Pallas kernels for 0%

profile of v8, /device:TPU:0, one launch (start us, length us, event | category | flops | bytes accessed | tf_op | source)
XLA Modules:
  0.0 150.9 jit_solution(15937399681682822069)
XLA Ops:
  0.6 0.8 collective-permute-start
  1.4 0.8 copy.45
  2.3 0.8 copy.46
  3.1 0.7 pad_add_fusion
  4.5 7.3 %all-to-all-start = ((s32[8,1,128]{2,1,0:T(1,128)}), s32[8,1,128]{2,1,0:T(1,128)S(1)}, u32[]{:S(2)}, u32[]{:S(2)}) async-start(s32[8,1,128]{2,1,0:T(1,128)} %broadcast_in_dim.103), calls=%async_computation | async-start | bytes 8192 | tf_op jit(solution)/shard_map/all_to_all | solution.py:300
  11.9 6.3 %all-to-all-done = s32[8,1,128]{2,1,0:T(1,128)S(1)} async-done(((s32[8,1,128]{2,1,0:T(1,128)}), s32[8,1,128]{2,1,0:T(1,128)S(1)}, u32[]{:S(2)}, u32[]{:S(2)}) %all-to-all-start) | async-done | bytes 4128 | tf_op jit(solution)/shard_map/all_to_all | solution.py:300
  18.1 0.6 broadcast_in_dim.105
  18.8 3.3 %all-to-all-start.1 = ((s32[4,8,1,128]{3,1,2,0:T(8,128)}), s32[4,8,1,128]{3,1,2,0:T(8,128)S(1)}, u32[]{:S(2)}, u32[]{:S(2)}) async-start(s32[4,8,1,128]{3,1,2,0:T(8,128)} %broadcast_in_dim.105), calls=%async_computation.1 | async-start | bytes 32768 | tf_op jit(solution)/shard_map/all_to_all | solution.py:300
  22.1 6.3 %all-to-all-done.1 = s32[4,8,1,128]{3,1,2,0:T(8,128)S(1)} async-done(((s32[4,8,1,128]{3,1,2,0:T(8,128)}), s32[4,8,1,128]{3,1,2,0:T(8,128)S(1)}, u32[]{:S(2)}, u32[]{:S(2)}) %all-to-all-start.1) | async-done | bytes 16416 | tf_op jit(solution)/shard_map/all_to_all | solution.py:300
  30.5 1.6 %copy-done = bf16[1,1,16,128,512]{4,3,2,1,0:T(8,128)(2,1)S(1)} copy-done((bf16[1,1,16,128,512]{4,3,2,1,0:T(8,128)(2,1)S(1)}, bf16[1,1,16,128,512]{4,3,2,1,0:T(8,128)(2,1)}, u32[]{:S(2)}) %copy-start) | copy-done | bytes 2097176
  32.0 2.1 %shard_map.138 = (bf16[2,128,512]{2,1,0:T(8,128)(2,1)S(1)}, bf16[2,128,512]{2,1,0:T(8,128)(2,1)S(1)}, bf16[2,128,512]{2,1,0:T(8,128)(2,1)S(1)}, bf16[2,128,512]{...) custom-call(s32[32]{0:T(128)S(1)} %concatenate.18.meta, ...), custom_call_target="tpu_custom_call" | custom-call | tf_op jit(solution)/shard_map/pallas_call | solution.py:208
  34.1 0.7 collective-permute-start.1
  34.8 0.7 collective-permute-start.2
  35.5 0.7 collective-permute-start.3
  36.2 0.7 collective-permute-start.4
  36.9 0.7 collective-permute-start.5
  37.6 0.7 collective-permute-start.6
  38.3 0.7 collective-permute-start.7
  39.0 6.5 %copy.50 = bf16[512,4096]{0,1:T(8,128)(2,1)} copy(bf16[512,4096]{1,0:T(8,128)(2,1)} %kv_hbm) | data formatting | bytes 8388608 | tf_op jit(solution)/shard_map/optimization_barrier | solution.py:327
  45.8 1.2 shard_map.139
  47.0 0.7 copy-done.1
  47.7 0.7 copy-done.3
  48.4 0.7 copy-done.5
  49.1 0.7 collective-permute-start.8
  51.7 0.9 copy-done.2
  52.6 0.9 copy-done.4
  53.6 0.9 copy-done.6
  54.5 3.0 %shard_map.140 = (bf16[8,128,512]{2,1,0:T(8,128)(2,1)}, bf16[8,128,512]{2,1,0:T(8,128)(2,1)S(1)}) custom-call(s32[32]{0:T(128)S(1)} %pad_add_fusion.2.meta, bf16[2,128,512]{2,1,0:T(8,128)(2,1)S(1)} %get-tuple-element.43.refs_0_, bf16[2,128,512]{2,1,0:T(8,128)(2,1)S(1)} %collective-permute-done.1.refs_1_, ...), custom_call_target="tpu_custom_call" | custom-call | tf_op jit(solution)/shard_map/pallas_call | solution.py:208
  57.5 1.3 collective-permute-start.9
  58.8 1.8 %copy.51 = bf16[256,512]{0,1:T(8,128)(2,1)} copy(bf16[256,512]{1,0:T(8,128)(2,1)} %up_ref.1) | data formatting | bytes 524288 | tf_op args[9]
  60.6 1.8 %copy.52 = bf16[512,256]{0,1:T(8,128)(2,1)} copy(bf16[512,256]{1,0:T(8,128)(2,1)} %down_ref.1) | data formatting | bytes 524288 | tf_op args[8]
  62.4 0.6 bitcast_convert_fusion.1.cond_ref
  63.5 0.7 pad_add_fusion.1.meta
  64.1 29.8 %collective-permute-done.9.got_ref = bf16[8,128,512]{2,1,0:T(8,128)(2,1)S(1)} collective-permute-done((bf16[8,128,512]{2,1,0:T(8,128)(2,1)}, bf16[8,128,512]{2,1,0:T(8,128)(2,1)S(1)}, u32[]{:S(2)}, u32[]{:S(2)}) %collective-permute-start.9) | collective-permute-done | bytes 1048608 | tf_op jit(solution)/shard_map/ppermute | solution.py:292
  94.0 1.0 copy-done.9
  94.9 28.2 %shard_map.141 = (bf16[256,2048]{1,0:T(8,128)(2,1)}, bf16[256,2048]{1,0:T(8,128)(2,1)}, f32[4,512]{1,0:T(4,128)}, f32[512,512]{1,0:T(8,128)}) custom-call(s32[10]{0:T(128)} %pad_add_fusion.1.meta, bf16[256,2048]{1,0:T(8,128)(2,1)} %bitcast.71, bf16[256,2048]{1,0:T(8,128)(2,1)} %bitcast.72, bf16[8,128,512]{2,1,0:T(8,128)(2,1)} %copy-done.7, ...), custom_call_target="tpu_custom_call" | custom-call | flops 11811160064 | bytes 16777216 | tf_op jit(solution)/shard_map/pallas_call | solution.py:146
  123.1 1.1 fusion
  124.2 3.2 %collective-permute-start.10 = (bf16[2,8,16,512]{3,2,1,0:T(8,128)(2,1)S(1)}, bf16[2,8,16,512]{3,2,1,0:T(8,128)(2,1)S(1)}, u32[]{:S(2)}, u32[]{:S(2)}) collective-permute-start(bf16[2,8,16,512]{3,2,1,0:T(8,128)(2,1)S(1)} %fusion), channel_id=1, source_target_pairs={{0,8},{8,0},{16,24},{24,16},{1,9},{9,1},{17,25},{25,17},{2,10},{10... | collective-permute-start | bytes 786440 | tf_op jit(solution)/shard_map/ppermute | solution.py:259
  127.4 1.2 collective-permute-done.10
  128.5 1.1 bitcast_add_fusion
  130.1 5.5 %collective-permute-done.11 = bf16[1,8,16,512]{3,2,1,0:T(8,128)(2,1)S(1)} collective-permute-done((bf16[1,8,16,512]{3,2,1,0:T(8,128)(2,1)S(1)}, bf16[1,8,16,512]{3,2,1,0:T(8,128)(2,1)S(1)}, u32[]{:S(2)}, u32[]{:S(2)}) %collective-permute-start.11) | collective-permute-done | bytes 131104 | tf_op jit(solution)/shard_map/ppermute | solution.py:259
  135.6 3.7 %collective-permute-start.12 = (bf16[1,4,16,512]{3,2,1,0:T(8,128)(2,1)S(1)}, bf16[1,4,16,512]{3,2,1,0:T(8,128)(2,1)S(1)}, u32[]{:S(2)}, u32[]{:S(2)}) collective-permute-start(bf16[1,4,16,512]{3,2,1,0:T(8,128)(2,1)S(1)} %fusion.3), channel_id=1, source_target_pairs={{0,1},{1,0},{2,3},{3,2},{4,5},{5,4},{6,7},{7,6},{8,9},{9,8},{10,11... | collective-permute-start | bytes 196616 | tf_op jit(solution)/shard_map/ppermute | solution.py:259
  139.3 2.2 %collective-permute-done.12 = bf16[1,4,16,512]{3,2,1,0:T(8,128)(2,1)S(1)} collective-permute-done((bf16[1,4,16,512]{3,2,1,0:T(8,128)(2,1)S(1)}, bf16[1,4,16,512]{3,2,1,0:T(8,128)(2,1)S(1)}, u32[]{:S(2)}, u32[]{:S(2)}) %collective-permute-start.12) | collective-permute-done | bytes 65568 | tf_op jit(solution)/shard_map/ppermute | solution.py:259
  141.6 1.2 collective-permute-start.13
  142.8 2.8 %collective-permute-done.13 = bf16[1,2,16,512]{3,2,1,0:T(8,128)(2,1)S(1)} collective-permute-done((bf16[1,2,16,512]{3,2,1,0:T(8,128)(2,1)S(1)}, bf16[1,2,16,512]{3,2,1,0:T(8,128)(2,1)S(1)}, u32[]{:S(2)}, u32[]{:S(2)}) %collective-permute-start.13) | collective-permute-done | bytes 32800 | tf_op jit(solution)/shard_map/ppermute | solution.py:259
  145.6 1.2 collective-permute-start.14
  146.8 3.5 %collective-permute-done.14 = bf16[1,1,16,512]{3,2,1,0:T(8,128)(2,1)S(1)} collective-permute-done((bf16[1,1,16,512]{3,2,1,0:T(8,128)(2,1)S(1)}, bf16[1,1,16,512]{3,2,1,0:T(8,128)(2,1)S(1)}, u32[]{:S(2)}, u32[]{:S(2)}) %collective-permute-start.14) | collective-permute-done | bytes 16416 | tf_op jit(solution)/shard_map/ppermute | solution.py:259
  150.3 0.6 add_bitcast_fusion
  (82 shorter events, 6.1 us)
Async XLA Ops:
  0.6 27.8 %collective-permute-start = (bf16[16,128,512]{2,1,0:T(8,128)(2,1)}, bf16[16,128,512]{2,1,0:T(8,128)(2,1)S(1)}, u32[]{:S(2)}, u32[]{:S(2)}) collective-permute-start(bf16[16,128,512]{2,1,0:T(8,128)(2,1)} %bitcast.57), channel_id=1, source_target_pairs={{24,8},{25,9},{26,10},{27,11},{28,12},{29,13},{30,14},{31,15}} | collective-permute-start | bytes 6291464 | tf_op jit(solution)/shard_map/ppermute | solution.py:292
  4.5 13.7 %all-to-all-start = ((s32[8,1,128]{2,1,0:T(1,128)}), s32[8,1,128]{2,1,0:T(1,128)S(1)}, u32[]{:S(2)}, u32[]{:S(2)}) async-start(s32[8,1,128]{2,1,0:T(1,128)} %broadcast_in_dim.103), calls=%async_computation | async-start | bytes 8192 | tf_op jit(solution)/shard_map/all_to_all | solution.py:300
  18.8 9.6 %all-to-all-start.1 = ((s32[4,8,1,128]{3,1,2,0:T(8,128)}), s32[4,8,1,128]{3,1,2,0:T(8,128)S(1)}, u32[]{:S(2)}, u32[]{:S(2)}) async-start(s32[4,8,1,128]{3,1,2,0:T(8,128)} %broadcast_in_dim.105), calls=%async_computation.1 | async-start | bytes 32768 | tf_op jit(solution)/shard_map/all_to_all | solution.py:300
  30.5 1.6 %copy-start = (bf16[1,1,16,128,512]{4,3,2,1,0:T(8,128)(2,1)S(1)}, bf16[1,1,16,128,512]{4,3,2,1,0:T(8,128)(2,1)}, u32[]{:S(2)}) copy-start(bf16[1,1,16,128,512]{4,3,2,1,0:T(8,128)(2,1)} %param.18) | copy-start | bytes 6291460
  34.1 3.5 %collective-permute-start.1 = (bf16[2,128,512]{2,1,0:T(8,128)(2,1)S(1)}, bf16[2,128,512]{2,1,0:T(8,128)(2,1)S(1)}, u32[]{:S(2)}, u32[]{:S(2)}) collective-permute-start(bf16[2,128,512]{2,1,0:T(8,128)(2,1)S(1)} %get-tuple-element.44), channel_id=1, source_target_pairs={{8,9},{9,10},{10,11},{11,12},{12,13},{13,14},{14,15},{15,8},{24,25... | collective-permute-start | bytes 786440 | tf_op jit(solution)/shard_map/ppermute | solution.py:292
  34.8 3.5 %collective-permute-start.2 = (bf16[2,128,512]{2,1,0:T(8,128)(2,1)S(1)}, bf16[2,128,512]{2,1,0:T(8,128)(2,1)S(1)}, u32[]{:S(2)}, u32[]{:S(2)}) collective-permute-start(bf16[2,128,512]{2,1,0:T(8,128)(2,1)S(1)} %get-tuple-element.45), channel_id=1, source_target_pairs={{8,10},{9,11},{10,12},{11,13},{12,14},{13,15},{14,8},{15,9},{24,26... | collective-permute-start | bytes 786440 | tf_op jit(solution)/shard_map/ppermute | solution.py:292
  35.5 10.2 %collective-permute-start.3 = (bf16[2,128,512]{2,1,0:T(8,128)(2,1)}, bf16[2,128,512]{2,1,0:T(8,128)(2,1)S(1)}, u32[]{:S(2)}, u32[]{:S(2)}) collective-permute-start(bf16[2,128,512]{2,1,0:T(8,128)(2,1)} %get-tuple-element.46), channel_id=1, source_target_pairs={{8,11},{9,12},{10,13},{11,14},{12,15},{13,8},{14,9},{15,10},{24,27... | collective-permute-start | bytes 786440 | tf_op jit(solution)/shard_map/ppermute | solution.py:292
  36.2 9.5 %collective-permute-start.4 = (bf16[2,128,512]{2,1,0:T(8,128)(2,1)}, bf16[2,128,512]{2,1,0:T(8,128)(2,1)S(1)}, u32[]{:S(2)}, u32[]{:S(2)}) collective-permute-start(bf16[2,128,512]{2,1,0:T(8,128)(2,1)} %get-tuple-element.47), channel_id=1, source_target_pairs={{8,12},{9,13},{10,14},{11,15},{12,8},{13,9},{14,10},{15,11},{24,28... | collective-permute-start | bytes 786440 | tf_op jit(solution)/shard_map/ppermute | solution.py:292
  36.9 8.9 %collective-permute-start.5 = (bf16[2,128,512]{2,1,0:T(8,128)(2,1)}, bf16[2,128,512]{2,1,0:T(8,128)(2,1)S(1)}, u32[]{:S(2)}, u32[]{:S(2)}) collective-permute-start(bf16[2,128,512]{2,1,0:T(8,128)(2,1)} %get-tuple-element.48), channel_id=1, source_target_pairs={{8,13},{9,14},{10,15},{11,8},{12,9},{13,10},{14,11},{15,12},{24,29... | collective-permute-start | bytes 786440 | tf_op jit(solution)/shard_map/ppermute | solution.py:292
  37.6 8.1 %collective-permute-start.6 = (bf16[2,128,512]{2,1,0:T(8,128)(2,1)}, bf16[2,128,512]{2,1,0:T(8,128)(2,1)S(1)}, u32[]{:S(2)}, u32[]{:S(2)}) collective-permute-start(bf16[2,128,512]{2,1,0:T(8,128)(2,1)} %get-tuple-element.49), channel_id=1, source_target_pairs={{8,14},{9,15},{10,8},{11,9},{12,10},{13,11},{14,12},{15,13},{24,30... | collective-permute-start | bytes 786440 | tf_op jit(solution)/shard_map/ppermute | solution.py:292
  38.3 7.4 %collective-permute-start.7 = (bf16[2,128,512]{2,1,0:T(8,128)(2,1)}, bf16[2,128,512]{2,1,0:T(8,128)(2,1)S(1)}, u32[]{:S(2)}, u32[]{:S(2)}) collective-permute-start(bf16[2,128,512]{2,1,0:T(8,128)(2,1)} %get-tuple-element.50), channel_id=1, source_target_pairs={{8,15},{9,8},{10,9},{11,10},{12,11},{13,12},{14,13},{15,14},{24,31... | collective-permute-start | bytes 786440 | tf_op jit(solution)/shard_map/ppermute | solution.py:292
  45.5 16.9 %copy-start.8 = (bf16[1,1,4,512]{3,2,1,0:T(4,128)(2,1)S(1)}, bf16[1,1,4,512]{3,2,1,0:T(4,128)(2,1)}, u32[]{:S(2)}) copy-start(bf16[1,1,4,512]{3,2,1,0:T(4,128)(2,1)} %param.15) | copy-start | bytes 12292
  47.0 0.7 copy-start.1
  47.7 0.7 copy-start.3
  48.4 0.7 copy-start.5
  49.1 2.6 %collective-permute-start.8 = (bf16[8,128,512]{2,1,0:T(8,128)(2,1)S(1)}, bf16[8,128,512]{2,1,0:T(8,128)(2,1)S(1)}, u32[]{:S(2)}, u32[]{:S(2)}) collective-permute-start(bf16[8,128,512]{2,1,0:T(8,128)(2,1)S(1)} %shard_map.139), channel_id=1, source_target_pairs={{8,24},{9,25},{10,26},{11,27},{12,28},{13,29},{14,30},{15,31},{24,... | collective-permute-start | bytes 3145736 | tf_op jit(solution)/shard_map/ppermute | solution.py:292
  51.7 1.0 copy-start.2
  52.6 0.9 copy-start.4
  53.6 0.9 copy-start.6
  57.5 36.5 %copy-start.7 = (bf16[8,128,512]{2,1,0:T(8,128)(2,1)}, bf16[8,128,512]{2,1,0:T(8,128)(2,1)S(1)}, u32[]{:S(2)}) copy-start(bf16[8,128,512]{2,1,0:T(8,128)(2,1)S(1)} %get-tuple-element.54.own_ref) | copy-start | bytes 3145732
  57.5 36.5 %collective-permute-start.9 = (bf16[8,128,512]{2,1,0:T(8,128)(2,1)}, bf16[8,128,512]{2,1,0:T(8,128)(2,1)S(1)}, u32[]{:S(2)}, u32[]{:S(2)}) collective-permute-start(bf16[8,128,512]{2,1,0:T(8,128)(2,1)} %get-tuple-element.55), channel_id=1, source_target_pairs={{8,0},{9,1},{10,2},{11,3},{12,4},{13,5},{14,6},{15,7},{24,16},{25,... | collective-permute-start | bytes 3145736 | tf_op jit(solution)/shard_map/ppermute | solution.py:292
  93.9 1.0 copy-start.9
  124.2 4.3 %collective-permute-start.10 = (bf16[2,8,16,512]{3,2,1,0:T(8,128)(2,1)S(1)}, bf16[2,8,16,512]{3,2,1,0:T(8,128)(2,1)S(1)}, u32[]{:S(2)}, u32[]{:S(2)}) collective-permute-start(bf16[2,8,16,512]{3,2,1,0:T(8,128)(2,1)S(1)} %fusion), channel_id=1, source_target_pairs={{0,8},{8,0},{16,24},{24,16},{1,9},{9,1},{17,25},{25,17},{2,10},{10... | collective-permute-start | bytes 786440 | tf_op jit(solution)/shard_map/ppermute | solution.py:259
  129.7 5.8 %collective-permute-start.11 = (bf16[1,8,16,512]{3,2,1,0:T(8,128)(2,1)S(1)}, bf16[1,8,16,512]{3,2,1,0:T(8,128)(2,1)S(1)}, u32[]{:S(2)}, u32[]{:S(2)}) collective-permute-start(bf16[1,8,16,512]{3,2,1,0:T(8,128)(2,1)S(1)} %dynamic-slice_convert_fusion), channel_id=1, source_target_pairs={{0,16},{8,24},{16,0},{24,8},{1,17},{9,25},{17,1},{25,9},{2,18},{10... | collective-permute-start | bytes 393224 | tf_op jit(solution)/shard_map/ppermute | solution.py:259
  135.6 6.0 %collective-permute-start.12 = (bf16[1,4,16,512]{3,2,1,0:T(8,128)(2,1)S(1)}, bf16[1,4,16,512]{3,2,1,0:T(8,128)(2,1)S(1)}, u32[]{:S(2)}, u32[]{:S(2)}) collective-permute-start(bf16[1,4,16,512]{3,2,1,0:T(8,128)(2,1)S(1)} %fusion.3), channel_id=1, source_target_pairs={{0,1},{1,0},{2,3},{3,2},{4,5},{5,4},{6,7},{7,6},{8,9},{9,8},{10,11... | collective-permute-start | bytes 196616 | tf_op jit(solution)/shard_map/ppermute | solution.py:259
  141.6 4.0 %collective-permute-start.13 = (bf16[1,2,16,512]{3,2,1,0:T(8,128)(2,1)S(1)}, bf16[1,2,16,512]{3,2,1,0:T(8,128)(2,1)S(1)}, u32[]{:S(2)}, u32[]{:S(2)}) collective-permute-start(bf16[1,2,16,512]{3,2,1,0:T(8,128)(2,1)S(1)} %fusion.4), channel_id=1, source_target_pairs={{0,2},{1,3},{2,0},{3,1},{4,6},{5,7},{6,4},{7,5},{8,10},{9,11},{10,... | collective-permute-start | bytes 98312 | tf_op jit(solution)/shard_map/ppermute | solution.py:259
  145.6 4.7 %collective-permute-start.14 = (bf16[1,1,16,512]{3,2,1,0:T(8,128)(2,1)S(1)}, bf16[1,1,16,512]{3,2,1,0:T(8,128)(2,1)S(1)}, u32[]{:S(2)}, u32[]{:S(2)}) collective-permute-start(bf16[1,1,16,512]{3,2,1,0:T(8,128)(2,1)S(1)} %dynamic-slice_convert_fusion.3), channel_id=1, source_target_pairs={{0,4},{1,5},{2,6},{3,7},{4,0},{5,1},{6,2},{7,3},{8,12},{9,13},{10,... | collective-permute-start | bytes 49160 | tf_op jit(solution)/shard_map/ppermute | solution.py:259

commit v9 on v7

--- a/solution.py
+++ b/solution.py
@@ -324,10 +324,9 @@
     info = jnp.pad(info, (0, -info.shape[0] % 128))
     over = lambda a: hop(a, [(relay_row, relay_row - half)])
     across = [over(store[0])]
-    table = to_all(info.reshape(-1, 128), "dp")
-    store[1:], table = lax.optimization_barrier((store[1:], table))
+    table = to_all(info.reshape(-1, 128), axes)
+    store[1:], across, table = lax.optimization_barrier((store[1:], across, table))
     across += [over(a) for a in store[1:]]
-    table = to_all(table, "pool")
     table = table.reshape(pool_count, columns, -1)
     by_column = jnp.swapaxes(table[:relay_row], 0, 1)
     owners = by_column[:, :, :per_device].reshape(columns, live_count)

time: 144 us -> 133 us (0.924)
  waiting for transfers between devices: 51.1 us -> 32.6 us
  starting transfers between devices: 32.7 us -> 40.8 us
    ppermute x10, starting transfers between devices: 5.74 us -> 19.4 us  [hop(): lax.ppermute(array, axes, [(a * columns + j, b * columns + j) for a, b in...]
    all_to_all x2, waiting for transfers between devices: 15.7 us -> 7.09 us  [body(): lax.all_to_all(sends, 'dp', split_axis=0, concat_axis=0, tiled=True)]
    ppermute x10, waiting for transfers between devices: 6.69 us -> 0.46 us  [hop(): lax.ppermute(array, axes, [(a * columns + j, b * columns + j) for a, b in...]
    all_to_all x2 -> x1, waiting for transfers between devices: 12.9 us -> 8.1 us  [to_all(): return lax.all_to_all(copies, axis, split_axis=0, concat_axis=0, tiled=True)]
    all_to_all x2 -> x1, starting transfers between devices: 11.7 us -> 8.23 us  [to_all(): return lax.all_to_all(copies, axis, split_axis=0, concat_axis=0, tiled=True)]
    slice x1, local copies, waits for them, and re-layouts: 1.32 us -> 3.23 us  [body(): store = [full_store[:, i * piece:(i + 1) * piece] for i in range(parts)]]
    unnamed x29 -> x36, local copies, waits for them, and re-layouts: 3.93 us -> 2.61 us
  transfers between devices with their start and end apart: 19 -> 18, of which waited for: 11 -> 9; matrix products, arithmetic and copies ran while one was open for 14% -> 13% of each run, Pallas kernels for 4% -> 4%
where the time goes in v9:
time: 133 us; the launch traced here: 132 us
  starting transfers between devices  40.8 us (31%)
  Pallas kernels  33.4 us (25%)
  waiting for transfers between devices  32.6 us (25%)
  local copies, waits for them, and re-layouts  15.8 us (12%)
  other arithmetic  8.28 us (6%)
    pallas_call x1, Pallas kernels, run_spans(): pl.pallas_call(functools.partial(span_kernel, len(held), nbr_count, parts...  28.3 us
    ppermute x10, starting transfers between devices, hop(): lax.ppermute(array, axes, [(a * columns + j, b * columns + j) for a, b in...  19.4 us
    ppermute x5, waiting for transfers between devices, scatter_sum(): lax.ppermute(give.astype(jnp.bfloat16), axis, [(i, i ^ bit) for i in rang...  17 us
    all_to_all x2, starting transfers between devices, body(): lax.all_to_all(sends, 'dp', split_axis=0, concat_axis=0, tiled=True)  9.74 us
    all_to_all x1, starting transfers between devices, to_all(): return lax.all_to_all(copies, axis, split_axis=0, concat_axis=0, tiled=True)  8.23 us
    all_to_all x1, waiting for transfers between devices, to_all(): return lax.all_to_all(copies, axis, split_axis=0, concat_axis=0, tiled=True)  8.1 us
    all_to_all x2, waiting for transfers between devices, body(): lax.all_to_all(sends, 'dp', split_axis=0, concat_axis=0, tiled=True)  7.09 us
    optimization_barrier x1, local copies, waits for them, and re-layouts, body(): weight, sends = lax.optimization_barrier((weight, sends))  6.46 us
  transfers between devices with their start and end apart: 18, of which 9 were waited for; matrix products, arithmetic and copies ran while one was open for 13% of the time, Pallas kernels for 4%

profile of v9, /device:TPU:0, one launch (start us, length us, event | category | flops | bytes accessed | tf_op | source)
XLA Modules:
  0.0 132.0 jit_solution(8153021028881716420)
XLA Ops:
  0.7 3.2 %fusion.37 = (bf16[16,64,512]{2,1,0:T(8,128)(2,1)}, bf16[16,64,512]{2,1,0:T(8,128)(2,1)}) fusion(bf16[16,128,512]{2,1,0:T(8,128)(2,1)} %bitcast.57), kind=kLoop, calls=%fused_computation.134 | loop fusion | bytes 4194304 | tf_op jit(solution)/shard_map/slice | solution.py:317
  3.9 0.7 collective-permute-start
  5.1 0.6 broadcast_in_dim.87
  5.7 8.2 %all-to-all-start = ((s32[32,1,128]{2,1,0:T(1,128)}), s32[32,1,128]{2,1,0:T(1,128)S(1)}, u32[]{:S(2)}, u32[]{:S(2)}) async-start(s32[32,1,128]{2,1,0:T(1,128)} %broadcast_in_dim.87), calls=%async_computation | async-start | bytes 32768 | tf_op jit(solution)/shard_map/all_to_all | solution.py:321
  14.1 8.1 %all-to-all-done = s32[32,1,128]{2,1,0:T(1,128)S(1)} async-done(((s32[32,1,128]{2,1,0:T(1,128)}), s32[32,1,128]{2,1,0:T(1,128)S(1)}, u32[]{:S(2)}, u32[]{:S(2)}) %all-to-all-start) | async-done | bytes 16416 | tf_op jit(solution)/shard_map/all_to_all | solution.py:321
  22.2 1.6 %collective-permute-start.2 = (bf16[16,64,512]{2,1,0:T(8,128)(2,1)}, bf16[16,64,512]{2,1,0:T(8,128)(2,1)}, u32[]{:S(2)}, u32[]{:S(2)}) collective-permute-start(bf16[16,64,512]{2,1,0:T(8,128)(2,1)} %get-tuple-element.20), channel_id=1, source_target_pairs={{24,8},{25,9},{26,10},{27,11},{28,12},{29,13},{30,14},{31,15}} | collective-permute-start | bytes 3145736 | tf_op jit(solution)/shard_map/ppermute | solution.py:310
  23.9 1.3 %broadcast_select_fusion.1.refs_0_ = bf16[16,64,512]{2,1,0:T(8,128)(2,1)S(1)} fusion(bf16[16,64,512]{2,1,0:T(8,128)(2,1)} %copy-done.3, pred[]{:T(512)S(6)} %eq.148, bf16[16,128,512]{2,1,0:T(8,128)(2,1)S(1)} %bitcast.58), kind=kLoop, calls=%fused_computation.1 | loop fusion | flops 524288 | bytes 3145729 | tf_op jit(solution)/shard_map/jit(_where)/select_n | solution.py:356
  25.3 1.3 collective-permute-start.1
  26.6 0.3 convert_reduce_fusion.3
  27.0 0.6 convert_reduce_fusion
  27.7 1.3 %broadcast_select_fusion.refs_0_ = bf16[16,64,512]{2,1,0:T(8,128)(2,1)S(1)} fusion(bf16[16,64,512]{2,1,0:T(8,128)(2,1)} %get-tuple-element.20, bf16[16,64,512]{2,1,0:T(8,128)(2,1)} %collective-permute-done.2, pred[]{:T(512)S(6)} %eq.148), kind=kLoop, calls=%fused_computation | loop fusion | flops 524288 | bytes 3145729 | tf_op jit(solution)/shard_map/jit(_where)/select_n | solution.py:356
  29.1 1.3 collective-permute-start.3
  30.4 0.2 select_reduce_fusion
  30.7 1.4 %shard_map.138 = bf16[8,64,512]{2,1,0:T(8,128)(2,1)} custom-call(s32[9]{0:T(128)S(1)} %pad_add_fusion.2.meta, bf16[16,64,512]{2,1,0:T(8,128)(2,1)S(1)} %broadcast_select_fusion.1.refs_0_, bf16[16,64,512]{2,1,0:T(8,128)(2,1)S(1)} %collective-permute-done.1.refs_1_), custom_call_target="tpu_custom_call" | custom-call | tf_op jit(solution)/shard_map/pallas_call | solution.py:221
  32.0 4.9 %all-to-all-start.1 = ((bf16[8,64,512]{2,1,0:T(8,128)(2,1)}), bf16[8,64,512]{2,1,0:T(8,128)(2,1)S(1)}, u32[]{:S(2)}, u32[]{:S(2)}) async-start(bf16[8,64,512]{2,1,0:T(8,128)(2,1)} %shard_map.138), calls=%async_computation.1 | async-start | bytes 1048576 | tf_op jit(solution)/shard_map/all_to_all | solution.py:368
  36.9 6.5 %copy.67 = bf16[512,4096]{0,1:T(8,128)(2,1)} copy(bf16[512,4096]{1,0:T(8,128)(2,1)} %rest_8_.1) | data formatting | bytes 8388608 | tf_op jit(solution)/shard_map/optimization_barrier | solution.py:367
  43.5 2.6 %shard_map.139 = bf16[8,64,512]{2,1,0:T(8,128)(2,1)} custom-call(s32[9]{0:T(128)S(1)} %pad_add_fusion.3.meta, bf16[16,64,512]{2,1,0:T(8,128)(2,1)S(1)} %broadcast_select_fusion.refs_0_, bf16[16,64,512]{2,1,0:T(8,128)(2,1)} %collective-permute-done.3.refs_1_), custom_call_target="tpu_custom_call" | custom-call | tf_op jit(solution)/shard_map/pallas_call | solution.py:221
  46.1 1.1 all-to-all-done.1.refs_0_.rest_0_
  47.2 4.9 %all-to-all-start.2 = ((bf16[8,64,512]{2,1,0:T(8,128)(2,1)}), bf16[8,64,512]{2,1,0:T(8,128)(2,1)S(1)}, u32[]{:S(2)}, u32[]{:S(2)}) async-start(bf16[8,64,512]{2,1,0:T(8,128)(2,1)} %shard_map.139), calls=%async_computation.2 | async-start | bytes 1048576 | tf_op jit(solution)/shard_map/all_to_all | solution.py:368
  52.1 0.6 bitcast_convert_fusion.1.cond_ref
  52.7 0.8 copy.61
  53.5 0.8 copy.62
  54.6 0.5 broadcast.445
  55.1 0.7 fusion.35
  56.3 0.6 shard_map.140
  57.0 5.9 %all-to-all-done.2.refs_0_.rest_1_ = bf16[8,64,512]{2,1,0:T(8,128)(2,1)S(1)} async-done(((bf16[8,64,512]{2,1,0:T(8,128)(2,1)}), bf16[8,64,512]{2,1,0:T(8,128)(2,1)S(1)}, u32[]{:S(2)}, u32[]{:S(2)}) %all-to-all-start.2) | async-done | bytes 524320 | tf_op jit(solution)/shard_map/all_to_all | solution.py:368
  62.9 0.6 shard_map.141
  63.9 9.5 %collective-permute-start.4 = (bf16[8,64,512]{2,1,0:T(8,128)(2,1)S(1)}, bf16[8,64,512]{2,1,0:T(8,128)(2,1)S(1)}, u32[]{:S(2)}, u32[]{:S(2)}) collective-permute-start(bf16[8,64,512]{2,1,0:T(8,128)(2,1)S(1)} %all-to-all-done.1.refs_0_.rest_0_), channel_id=1, source_target_pairs={{0,8},{1,9},{2,10},{3,11},{4,12},{5,13},{6,14},{7,15},{8,0},{9,1},... | collective-permute-start | bytes 1572872 | tf_op jit(solution)/shard_map/ppermute | solution.py:310
  73.5 0.5 collective-permute-start.8
  74.1 4.2 %collective-permute-start.9 = (bf16[4,64,512]{2,1,0:T(8,128)(2,1)S(1)}, bf16[4,64,512]{2,1,0:T(8,128)(2,1)S(1)}, u32[]{:S(2)}, u32[]{:S(2)}) collective-permute-start(bf16[4,64,512]{2,1,0:T(8,128)(2,1)S(1)} %collective-permute-done.7.rest_5_), channel_id=1, source_target_pairs={{0,8},{1,9},{2,10},{3,11},{4,12},{5,13},{6,14},{7,15},{8,0},{9,1},... | collective-permute-start | bytes 786440 | tf_op jit(solution)/shard_map/ppermute | solution.py:310
  78.3 0.7 pad_add_fusion.1.meta
  79.0 0.4 collective-permute-done.9.rest_7_
  79.5 0.2 copy-done.14
  79.8 0.2 copy-done.11
  80.2 28.3 %shard_map.142 = (bf16[256,2048]{1,0:T(8,128)(2,1)}, bf16[256,2048]{1,0:T(8,128)(2,1)}, f32[4,512]{1,0:T(4,128)}, f32[512,512]{1,0:T(8,128)}) custom-call(s32[25]{0:T(128)} %pad_add_fusion.1.meta, bf16[256,2048]{1,0:T(8,128)(2,1)} %bitcast.73, bf16[256,2048]{1,0:T(8,128)(2,1)} %bitcast.74, f32[4,512]{1,0:T(4,128)} %bitcast_convert_fusion.1.cond_ref, ...), custom_call_target="tpu_custom_call" | custom-call | flops 11811160064 | bytes 16777216 | tf_op jit(solution)/shard_map/pallas_call | solution.py:165
  108.5 1.1 fusion
  109.6 0.4 collective-permute-start.10
  110.0 1.2 collective-permute-done.10
  111.2 1.1 bitcast_add_fusion
  112.3 0.4 collective-permute-start.11
  112.7 5.5 %collective-permute-done.11 = bf16[1,8,16,512]{3,2,1,0:T(8,128)(2,1)S(1)} collective-permute-done((bf16[1,8,16,512]{3,2,1,0:T(8,128)(2,1)S(1)}, bf16[1,8,16,512]{3,2,1,0:T(8,128)(2,1)S(1)}, u32[]{:S(2)}, u32[]{:S(2)}) %collective-permute-start.11) | collective-permute-done | bytes 131104 | tf_op jit(solution)/shard_map/ppermute | solution.py:275
  118.2 1.5 %collective-permute-start.12 = (bf16[1,4,16,512]{3,2,1,0:T(8,128)(2,1)S(1)}, bf16[1,4,16,512]{3,2,1,0:T(8,128)(2,1)S(1)}, u32[]{:S(2)}, u32[]{:S(2)}) collective-permute-start(bf16[1,4,16,512]{3,2,1,0:T(8,128)(2,1)S(1)} %fusion.2), channel_id=1, source_target_pairs={{0,1},{1,0},{2,3},{3,2},{4,5},{5,4},{6,7},{7,6},{8,9},{9,8},{10,11... | collective-permute-start | bytes 196616 | tf_op jit(solution)/shard_map/ppermute | solution.py:275
  119.8 2.8 %collective-permute-done.12 = bf16[1,4,16,512]{3,2,1,0:T(8,128)(2,1)S(1)} collective-permute-done((bf16[1,4,16,512]{3,2,1,0:T(8,128)(2,1)S(1)}, bf16[1,4,16,512]{3,2,1,0:T(8,128)(2,1)S(1)}, u32[]{:S(2)}, u32[]{:S(2)}) %collective-permute-start.12) | collective-permute-done | bytes 65568 | tf_op jit(solution)/shard_map/ppermute | solution.py:275
  122.6 0.2 collective-permute-start.13
  122.9 3.7 %collective-permute-done.13 = bf16[1,2,16,512]{3,2,1,0:T(8,128)(2,1)S(1)} collective-permute-done((bf16[1,2,16,512]{3,2,1,0:T(8,128)(2,1)S(1)}, bf16[1,2,16,512]{3,2,1,0:T(8,128)(2,1)S(1)}, u32[]{:S(2)}, u32[]{:S(2)}) %collective-permute-start.13) | collective-permute-done | bytes 32800 | tf_op jit(solution)/shard_map/ppermute | solution.py:275
  126.6 0.9 collective-permute-start.14
  127.5 3.8 %collective-permute-done.14 = bf16[1,1,16,512]{3,2,1,0:T(8,128)(2,1)S(1)} collective-permute-done((bf16[1,1,16,512]{3,2,1,0:T(8,128)(2,1)S(1)}, bf16[1,1,16,512]{3,2,1,0:T(8,128)(2,1)S(1)}, u32[]{:S(2)}, u32[]{:S(2)}) %collective-permute-start.14) | collective-permute-done | bytes 16416 | tf_op jit(solution)/shard_map/ppermute | solution.py:275
  131.3 0.6 add_bitcast_fusion
  (89 shorter events, 2.9 us)
Async XLA Ops:
  0.6 4.0 %copy-start.7 = (s32[1,1,4,2]{2,3,1,0:T(2,128)S(1)}, s32[1,1,4,2]{2,3,1,0:T(2,128)}, u32[]{:S(2)}) copy-start(s32[1,1,4,2]{2,3,1,0:T(2,128)} %param.14) | copy-start | bytes 100
  0.6 4.2 %copy-start.8 = (s32[1,1,4,2]{2,3,1,0:T(2,128)S(1)}, s32[1,1,4,2]{2,3,1,0:T(2,128)}, u32[]{:S(2)}) copy-start(s32[1,1,4,2]{2,3,1,0:T(2,128)} %param.15) | copy-start | bytes 100
  0.7 4.3 %copy-start.9 = (s32[1,1,16]{2,1,0:T(1,128)S(1)}, s32[1,1,16]{2,1,0:T(1,128)}, u32[]{:S(2)}) copy-start(s32[1,1,16]{2,1,0:T(1,128)} %param.17) | copy-start | bytes 196
  0.7 23.3 %copy-start.2 = (bf16[1,1,16,128,512]{4,3,2,1,0:T(8,128)(2,1)S(1)}, bf16[1,1,16,128,512]{4,3,2,1,0:T(8,128)(2,1)}, u32[]{:S(2)}) copy-start(bf16[1,1,16,128,512]{4,3,2,1,0:T(8,128)(2,1)} %param.16) | copy-start | bytes 6291460
  3.9 18.3 %collective-permute-start = (bf16[16,64,512]{2,1,0:T(8,128)(2,1)}, bf16[16,64,512]{2,1,0:T(8,128)(2,1)S(1)}, u32[]{:S(2)}, u32[]{:S(2)}) collective-permute-start(bf16[16,64,512]{2,1,0:T(8,128)(2,1)} %get-tuple-element.33), channel_id=1, source_target_pairs={{24,8},{25,9},{26,10},{27,11},{28,12},{29,13},{30,14},{31,15}} | collective-permute-start | bytes 3145736 | tf_op jit(solution)/shard_map/ppermute | solution.py:310
  5.7 16.5 %all-to-all-start = ((s32[32,1,128]{2,1,0:T(1,128)}), s32[32,1,128]{2,1,0:T(1,128)S(1)}, u32[]{:S(2)}, u32[]{:S(2)}) async-start(s32[32,1,128]{2,1,0:T(1,128)} %broadcast_in_dim.87), calls=%async_computation | async-start | bytes 32768 | tf_op jit(solution)/shard_map/all_to_all | solution.py:321
  22.2 1.7 %copy-start.3 = (bf16[16,64,512]{2,1,0:T(8,128)(2,1)}, bf16[16,64,512]{2,1,0:T(8,128)(2,1)S(1)}, u32[]{:S(2)}) copy-start(bf16[16,64,512]{2,1,0:T(8,128)(2,1)S(1)} %collective-permute-done) | copy-start | bytes 3145732
  22.2 5.5 %collective-permute-start.2 = (bf16[16,64,512]{2,1,0:T(8,128)(2,1)}, bf16[16,64,512]{2,1,0:T(8,128)(2,1)}, u32[]{:S(2)}, u32[]{:S(2)}) collective-permute-start(bf16[16,64,512]{2,1,0:T(8,128)(2,1)} %get-tuple-element.20), channel_id=1, source_target_pairs={{24,8},{25,9},{26,10},{27,11},{28,12},{29,13},{30,14},{31,15}} | collective-permute-start | bytes 3145736 | tf_op jit(solution)/shard_map/ppermute | solution.py:310
  25.3 5.4 %collective-permute-start.1 = (bf16[16,64,512]{2,1,0:T(8,128)(2,1)S(1)}, bf16[16,64,512]{2,1,0:T(8,128)(2,1)S(1)}, u32[]{:S(2)}, u32[]{:S(2)}) collective-permute-start(bf16[16,64,512]{2,1,0:T(8,128)(2,1)S(1)} %broadcast_select_fusion.1.refs_0_), channel_id=1, source_target_pairs={{24,16},{25,17},{26,18},{27,19},{28,20},{29,21},{30,22},{31,23},{8... | collective-permute-start | bytes 3145736 | tf_op jit(solution)/shard_map/ppermute | solution.py:310
  29.1 14.4 %collective-permute-start.3 = (bf16[16,64,512]{2,1,0:T(8,128)(2,1)S(1)}, bf16[16,64,512]{2,1,0:T(8,128)(2,1)}, u32[]{:S(2)}, u32[]{:S(2)}) collective-permute-start(bf16[16,64,512]{2,1,0:T(8,128)(2,1)S(1)} %broadcast_select_fusion.refs_0_), channel_id=1, source_target_pairs={{24,16},{25,17},{26,18},{27,19},{28,20},{29,21},{30,22},{31,23},{8... | collective-permute-start | bytes 3145736 | tf_op jit(solution)/shard_map/ppermute | solution.py:310
  32.0 15.2 %all-to-all-start.1 = ((bf16[8,64,512]{2,1,0:T(8,128)(2,1)}), bf16[8,64,512]{2,1,0:T(8,128)(2,1)S(1)}, u32[]{:S(2)}, u32[]{:S(2)}) async-start(bf16[8,64,512]{2,1,0:T(8,128)(2,1)} %shard_map.138), calls=%async_computation.1 | async-start | bytes 1048576 | tf_op jit(solution)/shard_map/all_to_all | solution.py:368
  43.4 8.7 %copy-start.6 = (bf16[1,1,4,512]{3,2,1,0:T(4,128)(2,1)S(1)}, bf16[1,1,4,512]{3,2,1,0:T(4,128)(2,1)}, u32[]{:S(2)}) copy-start(bf16[1,1,4,512]{3,2,1,0:T(4,128)(2,1)} %param.13) | copy-start | bytes 12292
  43.4 9.3 %copy-start.5 = (bf16[256,512]{1,0:T(8,128)(2,1)S(1)}, bf16[256,512]{1,0:T(8,128)(2,1)}, u32[]{:S(2)}) copy-start(bf16[256,512]{1,0:T(8,128)(2,1)} %up_ref.1) | copy-start | bytes 786436
  43.5 10.0 %copy-start.4 = (bf16[512,256]{1,0:T(8,128)(2,1)S(1)}, bf16[512,256]{1,0:T(8,128)(2,1)}, u32[]{:S(2)}) copy-start(bf16[512,256]{1,0:T(8,128)(2,1)} %down_ref.1) | copy-start | bytes 786436
  47.2 32.2 %copy-start = (bf16[8,64,512]{2,1,0:T(8,128)(2,1)}, bf16[8,64,512]{2,1,0:T(8,128)(2,1)S(1)}, u32[]{:S(2)}) copy-start(bf16[8,64,512]{2,1,0:T(8,128)(2,1)S(1)} %all-to-all-done.1.refs_0_.rest_0_) | copy-start | bytes 1572868
  47.2 15.7 %all-to-all-start.2 = ((bf16[8,64,512]{2,1,0:T(8,128)(2,1)}), bf16[8,64,512]{2,1,0:T(8,128)(2,1)S(1)}, u32[]{:S(2)}, u32[]{:S(2)}) async-start(bf16[8,64,512]{2,1,0:T(8,128)(2,1)} %shard_map.139), calls=%async_computation.2 | async-start | bytes 1048576 | tf_op jit(solution)/shard_map/all_to_all | solution.py:368
  56.9 16.6 %collective-permute-start.6 = (bf16[4,64,512]{2,1,0:T(8,128)(2,1)S(1)}, bf16[4,64,512]{2,1,0:T(8,128)(2,1)S(1)}, u32[]{:S(2)}, u32[]{:S(2)}) collective-permute-start(bf16[4,64,512]{2,1,0:T(8,128)(2,1)S(1)} %shard_map.140), channel_id=1, source_target_pairs={{0,16},{1,17},{2,18},{3,19},{4,20},{5,21},{6,22},{7,23},{8,24},{9,... | collective-permute-start | bytes 786440 | tf_op jit(solution)/shard_map/ppermute | solution.py:310
  62.9 16.5 %copy-start.1 = (bf16[8,64,512]{2,1,0:T(8,128)(2,1)}, bf16[8,64,512]{2,1,0:T(8,128)(2,1)S(1)}, u32[]{:S(2)}) copy-start(bf16[8,64,512]{2,1,0:T(8,128)(2,1)S(1)} %all-to-all-done.2.refs_0_.rest_1_) | copy-start | bytes 1572868
  63.5 10.6 %collective-permute-start.7 = (bf16[4,64,512]{2,1,0:T(8,128)(2,1)S(1)}, bf16[4,64,512]{2,1,0:T(8,128)(2,1)S(1)}, u32[]{:S(2)}, u32[]{:S(2)}) collective-permute-start(bf16[4,64,512]{2,1,0:T(8,128)(2,1)S(1)} %shard_map.141), channel_id=1, source_target_pairs={{0,16},{1,17},{2,18},{3,19},{4,20},{5,21},{6,22},{7,23},{8,24},{9,... | collective-permute-start | bytes 786440 | tf_op jit(solution)/shard_map/ppermute | solution.py:310
  63.9 15.0 %collective-permute-start.4 = (bf16[8,64,512]{2,1,0:T(8,128)(2,1)S(1)}, bf16[8,64,512]{2,1,0:T(8,128)(2,1)S(1)}, u32[]{:S(2)}, u32[]{:S(2)}) collective-permute-start(bf16[8,64,512]{2,1,0:T(8,128)(2,1)S(1)} %all-to-all-done.1.refs_0_.rest_0_), channel_id=1, source_target_pairs={{0,8},{1,9},{2,10},{3,11},{4,12},{5,13},{6,14},{7,15},{8,0},{9,1},... | collective-permute-start | bytes 1572872 | tf_op jit(solution)/shard_map/ppermute | solution.py:310
  73.4 5.5 %collective-permute-start.5 = (bf16[8,64,512]{2,1,0:T(8,128)(2,1)S(1)}, bf16[8,64,512]{2,1,0:T(8,128)(2,1)S(1)}, u32[]{:S(2)}, u32[]{:S(2)}) collective-permute-start(bf16[8,64,512]{2,1,0:T(8,128)(2,1)S(1)} %all-to-all-done.2.refs_0_.rest_1_), channel_id=1, source_target_pairs={{0,8},{1,9},{2,10},{3,11},{4,12},{5,13},{6,14},{7,15},{8,0},{9,1},... | collective-permute-start | bytes 1572872 | tf_op jit(solution)/shard_map/ppermute | solution.py:310
  73.5 5.9 %copy-start.12 = (bf16[4,64,512]{2,1,0:T(8,128)(2,1)}, bf16[4,64,512]{2,1,0:T(8,128)(2,1)S(1)}, u32[]{:S(2)}) copy-start(bf16[4,64,512]{2,1,0:T(8,128)(2,1)S(1)} %collective-permute-done.6.rest_4_) | copy-start | bytes 786436
  73.5 5.4 %collective-permute-start.8 = (bf16[4,64,512]{2,1,0:T(8,128)(2,1)S(1)}, bf16[4,64,512]{2,1,0:T(8,128)(2,1)S(1)}, u32[]{:S(2)}, u32[]{:S(2)}) collective-permute-start(bf16[4,64,512]{2,1,0:T(8,128)(2,1)S(1)} %collective-permute-done.6.rest_4_), channel_id=1, source_target_pairs={{0,8},{1,9},{2,10},{3,11},{4,12},{5,13},{6,14},{7,15},{8,0},{9,1},... | collective-permute-start | bytes 786440 | tf_op jit(solution)/shard_map/ppermute | solution.py:310
  74.1 5.4 %copy-start.13 = (bf16[4,64,512]{2,1,0:T(8,128)(2,1)}, bf16[4,64,512]{2,1,0:T(8,128)(2,1)S(1)}, u32[]{:S(2)}) copy-start(bf16[4,64,512]{2,1,0:T(8,128)(2,1)S(1)} %collective-permute-done.7.rest_5_) | copy-start | bytes 786436
  74.1 5.4 %collective-permute-start.9 = (bf16[4,64,512]{2,1,0:T(8,128)(2,1)S(1)}, bf16[4,64,512]{2,1,0:T(8,128)(2,1)S(1)}, u32[]{:S(2)}, u32[]{:S(2)}) collective-permute-start(bf16[4,64,512]{2,1,0:T(8,128)(2,1)S(1)} %collective-permute-done.7.rest_5_), channel_id=1, source_target_pairs={{0,8},{1,9},{2,10},{3,11},{4,12},{5,13},{6,14},{7,15},{8,0},{9,1},... | collective-permute-start | bytes 786440 | tf_op jit(solution)/shard_map/ppermute | solution.py:310
  79.0 0.7 copy-start.14
  79.0 0.9 copy-start.10
  79.0 1.1 copy-start.11
  79.4 0.7 copy-start.15
  109.6 1.6 %collective-permute-start.10 = (bf16[2,8,16,512]{3,2,1,0:T(8,128)(2,1)S(1)}, bf16[2,8,16,512]{3,2,1,0:T(8,128)(2,1)S(1)}, u32[]{:S(2)}, u32[]{:S(2)}) collective-permute-start(bf16[2,8,16,512]{3,2,1,0:T(8,128)(2,1)S(1)} %fusion), channel_id=1, source_target_pairs={{0,8},{8,0},{16,24},{24,16},{1,9},{9,1},{17,25},{25,17},{2,10},{10... | collective-permute-start | bytes 786440 | tf_op jit(solution)/shard_map/ppermute | solution.py:275
  112.3 5.8 %collective-permute-start.11 = (bf16[1,8,16,512]{3,2,1,0:T(8,128)(2,1)S(1)}, bf16[1,8,16,512]{3,2,1,0:T(8,128)(2,1)S(1)}, u32[]{:S(2)}, u32[]{:S(2)}) collective-permute-start(bf16[1,8,16,512]{3,2,1,0:T(8,128)(2,1)S(1)} %dynamic-slice_convert_fusion), channel_id=1, source_target_pairs={{0,16},{8,24},{16,0},{24,8},{1,17},{9,25},{17,1},{25,9},{2,18},{10... | collective-permute-start | bytes 393224 | tf_op jit(solution)/shard_map/ppermute | solution.py:275
  118.2 4.3 %collective-permute-start.12 = (bf16[1,4,16,512]{3,2,1,0:T(8,128)(2,1)S(1)}, bf16[1,4,16,512]{3,2,1,0:T(8,128)(2,1)S(1)}, u32[]{:S(2)}, u32[]{:S(2)}) collective-permute-start(bf16[1,4,16,512]{3,2,1,0:T(8,128)(2,1)S(1)} %fusion.2), channel_id=1, source_target_pairs={{0,1},{1,0},{2,3},{3,2},{4,5},{5,4},{6,7},{7,6},{8,9},{9,8},{10,11... | collective-permute-start | bytes 196616 | tf_op jit(solution)/shard_map/ppermute | solution.py:275
  122.6 4.0 %collective-permute-start.13 = (bf16[1,2,16,512]{3,2,1,0:T(8,128)(2,1)S(1)}, bf16[1,2,16,512]{3,2,1,0:T(8,128)(2,1)S(1)}, u32[]{:S(2)}, u32[]{:S(2)}) collective-permute-start(bf16[1,2,16,512]{3,2,1,0:T(8,128)(2,1)S(1)} %fusion.3), channel_id=1, source_target_pairs={{0,2},{1,3},{2,0},{3,1},{4,6},{5,7},{6,4},{7,5},{8,10},{9,11},{10,... | collective-permute-start | bytes 98312 | tf_op jit(solution)/shard_map/ppermute | solution.py:275
  126.6 4.7 %collective-permute-start.14 = (bf16[1,1,16,512]{3,2,1,0:T(8,128)(2,1)S(1)}, bf16[1,1,16,512]{3,2,1,0:T(8,128)(2,1)S(1)}, u32[]{:S(2)}, u32[]{:S(2)}) collective-permute-start(bf16[1,1,16,512]{3,2,1,0:T(8,128)(2,1)S(1)} %dynamic-slice_convert_fusion.3), channel_id=1, source_target_pairs={{0,4},{1,5},{2,6},{3,7},{4,0},{5,1},{6,2},{7,3},{8,12},{9,13},{10,... | collective-permute-start | bytes 49160 | tf_op jit(solution)/shard_map/ppermute | solution.py:275

commit v10 on v9

--- a/solution.py
+++ b/solution.py
@@ -11,6 +11,7 @@
 HEAD = 128
 SPAN = 64
 PARTS = 2
+GROUP = 2
 
 EPSILON = 1e-06
 FLOOR = -1e30
@@ -32,9 +33,11 @@
     (kv_hbm, kvt_hbm, out_ref, qg_ref, cg_ref, ad_ref,
      raw_ref, kv_ref, kvt_ref, proj_ref, grad_ref, score_ref, dprob_ref, prob_ref, dscore_ref,
      q2_ref, cot2_ref, acc_ref, sems, kv_sem) = rest[held_count:]
-    span = pl.program_id(0)
+    step = pl.program_id(0)
     per_device, slot_len, width = raw_ref.shape
     key_count = nbr_count * slot_len
+    span_count = per_device // nbr_count
+    group = span_count // pl.num_programs(0)
     head_cols = q_ref.shape[1]
     rank = down_ref.shape[1]
     scaling = HEAD ** (-0.5)
@@ -44,10 +47,18 @@
     pairs = [pl.ds(i * 2 * HEAD, 2 * HEAD) for i in range(HEADS // 2)]
     value_pairs = [pl.ds(head_cols + i * 2 * HEAD, 2 * HEAD) for i in range(HEADS // 2)]
     lanes = [pl.ds(i * 2 * SPAN, 2 * SPAN) for i in range(HEADS // 2)]
+    keys = [pl.ds(g * key_count, key_count) for g in range(group)]
+    tokens = [pl.ds(g * SPAN, SPAN) for g in range(group)]
+    double = [pl.ds(g * 2 * SPAN, 2 * SPAN) for g in range(group)]
+    spots = [
+        (g, cols, value_cols, lane)
+        for g in range(group)
+        for cols, value_cols, lane in zip(pairs, value_pairs, lanes)
+    ]
     kv_copy = pltpu.make_async_copy(kv_hbm, kv_ref, kv_sem.at[0])
     kvt_copy = pltpu.make_async_copy(kvt_hbm, kvt_ref, kv_sem.at[1])
 
-    @pl.when(span == 0)
+    @pl.when(step == 0)
     def _():
         for n in range(per_device):
             for b, held in enumerate(held_refs):
@@ -61,72 +72,87 @@
                     ).start()
         kv_copy.start()
         kvt_copy.start()
-
-    q2_ref[...] = jnp.zeros_like(q2_ref)
-    cot2_ref[...] = jnp.zeros_like(cot2_ref)
-    for i in range(HEADS):
-        cols = pl.ds(i * HEAD, HEAD)
-        tokens = pl.ds(i % 2 * SPAN, SPAN)
-        q2_ref[tokens, cols] = q_ref[:, cols]
-        cot2_ref[tokens, cols] = cot_ref[:, cols]
-
-    for n in range(nbr_count):
+        q2_ref[...] = jnp.zeros_like(q2_ref)
+        cot2_ref[...] = jnp.zeros_like(cot2_ref)
+
+    for g in range(group):
+        for i in range(HEADS):
+            cols = pl.ds(i * HEAD, HEAD)
+            part = pl.ds((2 * g + i % 2) * SPAN, SPAN)
+            q2_ref[part, cols] = q_ref[tokens[g], cols]
+            cot2_ref[part, cols] = cot_ref[tokens[g], cols]
+
+    for n in range(group * nbr_count):
         for part in range(parts):
-            item = span * nbr_count + n
+            item = step * group * nbr_count + n
             pltpu.make_async_copy(
                 held_refs[0].at[0],
                 raw_ref.at[item, pl.ds(part * piece, piece)],
                 sems.at[item * parts + part],
             ).wait()
-    raw = raw_ref[pl.ds(span * nbr_count, nbr_count)]
-    x_full = raw.reshape(key_count, width).astype(jnp.float32) + cond_ref[pl.ds(span, 1), :]
+    x_full = jnp.concatenate(
+        [
+            raw_ref[pl.ds((step * group + g) * nbr_count, nbr_count)]
+            .reshape(key_count, width)
+            .astype(jnp.float32)
+            + cond_ref[pl.ds(step * group + g, 1), :]
+            for g in range(group)
+        ],
+        axis=0,
+    )
     inv_rms = lax.rsqrt(jnp.mean(x_full * x_full, axis=-1, keepdims=True) + EPSILON)
     gain = gain_ref[...]
     hidden = (x_full * inv_rms * gain).astype(jnp.bfloat16)
     latent = dot(hidden, down_ref[...]).astype(jnp.bfloat16)
     encoded = (x_full + dot(latent, up_ref[...])).astype(jnp.bfloat16)
 
-    @pl.when(span == 0)
+    @pl.when(step == 0)
     def _():
         kv_copy.wait()
 
     for cols in pairs + value_pairs:
         proj_ref[:, cols] = dot(encoded, kv_ref[:, cols]).astype(jnp.bfloat16)
 
-    for cols, value_cols, lane in zip(pairs, value_pairs, lanes):
-        score_ref[:, lane] = dot(proj_ref[:, cols], q2_ref[:, cols], NT)
-        dprob_ref[:, lane] = dot(proj_ref[:, value_cols], cot2_ref[:, cols], NT)
+    for g, cols, value_cols, lane in spots:
+        score_ref[keys[g], lane] = dot(proj_ref[keys[g], cols], q2_ref[double[g], cols], NT)
+        dprob_ref[keys[g], lane] = dot(proj_ref[keys[g], value_cols], cot2_ref[double[g], cols], NT)
 
     slot = lax.broadcasted_iota(jnp.int32, (key_count, 2 * SPAN), 0)
-    limit = jnp.zeros((key_count, 2 * SPAN), jnp.int32)
-    for n in range(nbr_count):
-        here = jnp.logical_and(slot >= n * slot_len, slot < (n + 1) * slot_len)
-        limit = jnp.where(here, n * slot_len + meta[lens + span * nbr_count + n], limit)
-    usable = slot < limit
-    for lane in lanes:
-        scores = jnp.where(usable, score_ref[:, lane], FLOOR)
-        row_max = jnp.max(scores, axis=0, keepdims=True)
-        raised = jnp.exp2((scores - row_max) * (scaling * LOG2E))
-        probs = raised * (1.0 / jnp.sum(raised, axis=0, keepdims=True))
-        d_probs = dprob_ref[:, lane]
-        delta = jnp.sum(probs * d_probs, axis=0, keepdims=True)
-        prob_ref[:, lane] = probs.astype(jnp.bfloat16)
-        dscore_ref[:, lane] = (probs * (d_probs - delta) * scaling).astype(jnp.bfloat16)
-
-    for cols, value_cols, lane in zip(pairs, value_pairs, lanes):
-        grad_ref[:, cols] = dot(dscore_ref[:, lane], q2_ref[:, cols]).astype(jnp.bfloat16)
-        grad_ref[:, value_cols] = dot(prob_ref[:, lane], cot2_ref[:, cols]).astype(jnp.bfloat16)
+    for g in range(group):
+        limit = jnp.zeros((key_count, 2 * SPAN), jnp.int32)
+        for n in range(nbr_count):
+            here = jnp.logical_and(slot >= n * slot_len, slot < (n + 1) * slot_len)
+            item = (step * group + g) * nbr_count + n
+            limit = jnp.where(here, n * slot_len + meta[lens + item], limit)
+        usable = slot < limit
+        for lane in lanes:
+            scores = jnp.where(usable, score_ref[keys[g], lane], FLOOR)
+            row_max = jnp.max(scores, axis=0, keepdims=True)
+            raised = jnp.exp2((scores - row_max) * (scaling * LOG2E))
+            probs = raised * (1.0 / jnp.sum(raised, axis=0, keepdims=True))
+            d_probs = dprob_ref[keys[g], lane]
+            delta = jnp.sum(probs * d_probs, axis=0, keepdims=True)
+            prob_ref[keys[g], lane] = probs.astype(jnp.bfloat16)
+            dscore_ref[keys[g], lane] = (probs * (d_probs - delta) * scaling).astype(jnp.bfloat16)
+
+    for g, cols, value_cols, lane in spots:
+        grad_ref[keys[g], cols] = dot(
+            dscore_ref[keys[g], lane], q2_ref[double[g], cols]
+        ).astype(jnp.bfloat16)
+        grad_ref[keys[g], value_cols] = dot(
+            prob_ref[keys[g], lane], cot2_ref[double[g], cols]
+        ).astype(jnp.bfloat16)
 
     def diagonal(both):
         return jnp.concatenate([both[:SPAN, :HEAD], both[SPAN:, HEAD:]], axis=1)
 
-    for cols, value_cols, lane in zip(pairs, value_pairs, lanes):
-        out = diagonal(dot(prob_ref[:, lane].T, proj_ref[:, value_cols]))
-        grad = diagonal(dot(dscore_ref[:, lane].T, proj_ref[:, cols]))
-        out_ref[:, cols] = jnp.where(live, out, 0.0).astype(jnp.bfloat16)
-        qg_ref[:, cols] = jnp.where(live, grad, 0.0).astype(jnp.bfloat16)
-
-    @pl.when(span == 0)
+    for g, cols, value_cols, lane in spots:
+        out = diagonal(dot(prob_ref[keys[g], lane].T, proj_ref[keys[g], value_cols]))
+        grad = diagonal(dot(dscore_ref[keys[g], lane].T, proj_ref[keys[g], cols]))
+        out_ref[tokens[g], cols] = jnp.where(live, out, 0.0).astype(jnp.bfloat16)
+        qg_ref[tokens[g], cols] = jnp.where(live, grad, 0.0).astype(jnp.bfloat16)
+
+    @pl.when(step == 0)
     def _():
         kvt_copy.wait()
         acc_ref[...] = jnp.zeros_like(acc_ref)
@@ -138,12 +164,15 @@
     x_grad = enc_grad.astype(jnp.float32) + inv_rms * (
         scaled - normed * jnp.mean(scaled * normed, axis=-1, keepdims=True)
     )
-    span_grad = jnp.sum(x_grad, axis=0, keepdims=True)
-    cg_ref[pl.ds(span, 1), :] = jnp.where(live, span_grad, 0.0)
+    for g in range(group):
+        span_grad = jnp.sum(
+            x_grad[g * key_count : (g + 1) * key_count], axis=0, keepdims=True
+        )
+        cg_ref[pl.ds(step * group + g, 1), :] = jnp.where(live, span_grad, 0.0)
     acc_ref[:, :rank] += dot(hidden, lat_grad, TN)
     acc_ref[:, rank:] += dot(enc_grad, latent, TN)
 
-    @pl.when(span == pl.num_programs(0) - 1)
+    @pl.when(step == pl.num_programs(0) - 1)
     def _():
         ad_ref[...] = jnp.where(live, acc_ref[...], 0.0).astype(ad_ref.dtype)
 
@@ -154,11 +183,12 @@
     slot_len = held[0].shape[1] * parts
     rank = w_down.shape[1]
     whole = lambda a: pl.BlockSpec(a.shape, lambda s, m: (0,) * a.ndim, pipeline_mode=pl.Buffered(1))
-    tokens = pl.BlockSpec((SPAN, head_cols), lambda s, m: (s, 0))
+    group = GROUP if span_count % GROUP == 0 else 1
+    tokens = pl.BlockSpec((group * SPAN, head_cols), lambda s, m: (s, 0))
     small = [cond, gain.reshape(1, width), w_down, w_up, w_up.T, w_down.T]
     large = list(held) + [w_kv, w_kv_t]
     per_device = span_count * nbr_count
-    keys = nbr_count * slot_len
+    keys = group * nbr_count * slot_len
     rows = per_device * slot_len
     lanes = SPAN * HEADS
     flops = 2 * rows * (2 * width * 2 * head_cols + 6 * width * rank + 6 * SPAN * head_cols)
@@ -166,7 +196,7 @@
         functools.partial(span_kernel, len(held), nbr_count, parts),
         grid_spec=pltpu.PrefetchScalarGridSpec(
             num_scalar_prefetch=1,
-            grid=(span_count,),
+            grid=(span_count // group,),
             in_specs=[tokens, tokens]
             + [whole(a) for a in small]
             + [pl.BlockSpec(memory_space=pltpu.HBM)] * len(large),
@@ -186,8 +216,8 @@
                 pltpu.VMEM((keys, lanes), jnp.float32),
                 pltpu.VMEM((keys, lanes), jnp.bfloat16),
                 pltpu.VMEM((keys, lanes), jnp.bfloat16),
-                pltpu.VMEM((2 * SPAN, head_cols), jnp.bfloat16),
-                pltpu.VMEM((2 * SPAN, head_cols), jnp.bfloat16),
+                pltpu.VMEM((group * 2 * SPAN, head_cols), jnp.bfloat16),
+                pltpu.VMEM((group * 2 * SPAN, head_cols), jnp.bfloat16),
                 pltpu.VMEM((width, 2 * rank), jnp.float32),
                 pltpu.SemaphoreType.DMA((per_device * parts,)),
                 pltpu.SemaphoreType.DMA((2,)),
@@ -314,7 +344,8 @@
     parts = PARTS if slot_len % (PARTS * 16) == 0 else 1
     piece = slot_len // parts
     full_store = database.reshape(block_count, slot_len, width)
-    store = [full_store[:, i * piece : (i + 1) * piece] for i in range(parts)]
+    cut = lambda i: full_store[:, i * piece : (i + 1) * piece]
+    store = [cut(0)]
 
     def to_all(array, axis):
         copies = jnp.broadcast_to(array[None], (lax.axis_size(axis),) + array.shape)
@@ -325,7 +356,8 @@
     over = lambda a: hop(a, [(relay_row, relay_row - half)])
     across = [over(store[0])]
     table = to_all(info.reshape(-1, 128), axes)
-    store[1:], across, table = lax.optimization_barrier((store[1:], across, table))
+    full_store, across, table = lax.optimization_barrier((full_store, across, table))
+    store += [cut(i) for i in range(1, parts)]
     across += [over(a) for a in store[1:]]
     table = table.reshape(pool_count, columns, -1)
     by_column = jnp.swapaxes(table[:relay_row], 0, 1)
@@ -353,16 +385,15 @@
     held = []
     weight, weight_t = w_kv, None
     for i in range(parts):
+        if i == 1:
+            weight_t, across[i] = lax.optimization_barrier((weight.T, across[i]))
         near = jnp.where(row == relay_row, store[i], across[i])
         stores = [near]
         held_by = jnp.where(row % half == half - 1, 0, 1)
         for step in range(1, half):
             stores.append(hop(near, [(p, p - step) for p in (relay_row, relay_row - half)]))
             held_by = jnp.where(row % half == half - 1 - step, step, held_by)
-        wanted = slot_block
-        if i == 1:
-            weight_t, wanted = lax.optimization_barrier((weight.T, wanted))
-        sends = pick(held_by, wanted, stores)
+        sends = pick(held_by, slot_block, stores)
         if i == 0:
             weight, sends = lax.optimization_barrier((weight, sends))
         arrived = lax.all_to_all(sends, "dp", split_axis=0, concat_axis=0, tiled=True)

time: 133 us -> 138 us (1.038)
  waiting for transfers between devices: 32.6 us -> 51.5 us
  starting transfers between devices: 40.8 us -> 29.5 us
  Pallas kernels: 33.4 us -> 30.3 us
    ppermute x10, starting transfers between devices: 19.4 us -> 6.99 us  [hop(): lax.ppermute(array, axes, [(a * columns + j, b * columns + j) for a, b in...]
    ppermute x10, waiting for transfers between devices: 0.46 us -> 11.3 us  [hop(): lax.ppermute(array, axes, [(a * columns + j, b * columns + j) for a, b in...]
    all_to_all x2, waiting for transfers between devices: 7.09 us -> 15.5 us  [body(): lax.all_to_all(sends, 'dp', split_axis=0, concat_axis=0, tiled=True)]
    pallas_call x1, Pallas kernels: 28.3 us -> 26.2 us  [run_spans(): pl.pallas_call(functools.partial(span_kernel, len(held), nbr_count, parts...]
    all_to_all x2, starting transfers between devices: 9.74 us -> 11.8 us  [body(): lax.all_to_all(sends, 'dp', split_axis=0, concat_axis=0, tiled=True)]
    unnamed x36 -> x34, local copies, waits for them, and re-layouts: 2.61 us -> 3.54 us
    slice x1 -> x2, local copies, waits for them, and re-layouts: 3.23 us -> 2.5 us  [body(): cut = lambda i: full_store[:, i * piece:(i + 1) * piece]]
  transfers between devices with their start and end apart: 18 -> 18, of which waited for: 9 -> 11; matrix products, arithmetic and copies ran while one was open for 13% -> 12% of each run, Pallas kernels for 4% -> 3%
where the time goes in v10:
time: 138 us; the launch traced here: 137 us
  waiting for transfers between devices  51.5 us (37%)
  Pallas kernels  30.3 us (22%)
  starting transfers between devices  29.5 us (21%)
  local copies, waits for them, and re-layouts  16 us (12%)
  other arithmetic  8.59 us (6%)
    pallas_call x1, Pallas kernels, run_spans(): pl.pallas_call(functools.partial(span_kernel, len(held), nbr_count, parts...  26.2 us
    ppermute x5, waiting for transfers between devices, scatter_sum(): lax.ppermute(give.astype(jnp.bfloat16), axis, [(i, i ^ bit) for i in rang...  17.7 us
    all_to_all x2, waiting for transfers between devices, body(): lax.all_to_all(sends, 'dp', split_axis=0, concat_axis=0, tiled=True)  15.5 us
    all_to_all x2, starting transfers between devices, body(): lax.all_to_all(sends, 'dp', split_axis=0, concat_axis=0, tiled=True)  11.8 us
    ppermute x10, waiting for transfers between devices, hop(): lax.ppermute(array, axes, [(a * columns + j, b * columns + j) for a, b in...  11.3 us
    all_to_all x1, starting transfers between devices, to_all(): return lax.all_to_all(copies, axis, split_axis=0, concat_axis=0, tiled=True)  8.23 us
    ppermute x10, starting transfers between devices, hop(): lax.ppermute(array, axes, [(a * columns + j, b * columns + j) for a, b in...  6.99 us
    all_to_all x1, waiting for transfers between devices, to_all(): return lax.all_to_all(copies, axis, split_axis=0, concat_axis=0, tiled=True)  6.98 us
  transfers between devices with their start and end apart: 18, of which 11 were waited for; matrix products, arithmetic and copies ran while one was open for 12% of the time, Pallas kernels for 3%

profile of v10, /device:TPU:0, one launch (start us, length us, event | category | flops | bytes accessed | tf_op | source)
XLA Modules:
  0.0 137.0 jit_solution(5828188946044904153)
XLA Ops:
  0.7 1.5 %slice.28 = bf16[16,64,512]{2,1,0:T(8,128)(2,1)S(1)} slice(bf16[16,128,512]{2,1,0:T(8,128)(2,1)} %bitcast.57), slice={[0:16], [0:64], [0:512]} | slice | bytes 2097152 | tf_op jit(solution)/shard_map/slice | solution.py:347
  2.1 1.6 %collective-permute-start = (bf16[16,64,512]{2,1,0:T(8,128)(2,1)S(1)}, bf16[16,64,512]{2,1,0:T(8,128)(2,1)}, u32[]{:S(2)}, u32[]{:S(2)}) collective-permute-start(bf16[16,64,512]{2,1,0:T(8,128)(2,1)S(1)} %slice.28), channel_id=1, source_target_pairs={{24,8},{25,9},{26,10},{27,11},{28,12},{29,13},{30,14},{31,15}} | collective-permute-start | bytes 3145736 | tf_op jit(solution)/shard_map/ppermute | solution.py:340
  4.2 0.6 broadcast_in_dim.87
  4.9 8.2 %all-to-all-start = ((s32[32,1,128]{2,1,0:T(1,128)}), s32[32,1,128]{2,1,0:T(1,128)S(1)}, u32[]{:S(2)}, u32[]{:S(2)}) async-start(s32[32,1,128]{2,1,0:T(1,128)} %broadcast_in_dim.87), calls=%async_computation | async-start | bytes 32768 | tf_op jit(solution)/shard_map/all_to_all | solution.py:352
  13.3 7.0 %all-to-all-done = s32[32,1,128]{2,1,0:T(1,128)S(1)} async-done(((s32[32,1,128]{2,1,0:T(1,128)}), s32[32,1,128]{2,1,0:T(1,128)S(1)}, u32[]{:S(2)}, u32[]{:S(2)}) %all-to-all-start) | async-done | bytes 16416 | tf_op jit(solution)/shard_map/all_to_all | solution.py:352
  20.2 1.5 %broadcast_select_fusion.1.refs_0_ = bf16[16,64,512]{2,1,0:T(8,128)(2,1)S(1)} fusion(bf16[16,64,512]{2,1,0:T(8,128)(2,1)} %collective-permute-done, pred[]{:T(512)S(6)} %eq.148, bf16[16,128,512]{2,1,0:T(8,128)(2,1)S(1)} %bitcast.59), kind=kLoop, calls=%fused_computation.1 | loop fusion | flops 524288 | bytes 3145729 | tf_op jit(solution)/shard_map/jit(_where)/select_n | solution.py:390
  21.7 1.3 collective-permute-start.1
  23.0 1.0 slice.27
  24.1 1.6 %collective-permute-start.2 = (bf16[16,64,512]{2,1,0:T(8,128)(2,1)}, bf16[16,64,512]{2,1,0:T(8,128)(2,1)}, u32[]{:S(2)}, u32[]{:S(2)}) collective-permute-start(bf16[16,64,512]{2,1,0:T(8,128)(2,1)} %slice.27), channel_id=1, source_target_pairs={{24,8},{25,9},{26,10},{27,11},{28,12},{29,13},{30,14},{31,15}} | collective-permute-start | bytes 3145736 | tf_op jit(solution)/shard_map/ppermute | solution.py:340
  25.8 0.3 convert_reduce_fusion.3
  26.2 0.6 convert_reduce_fusion
  27.0 0.2 select_reduce_fusion
  27.2 1.4 %shard_map.138 = bf16[8,64,512]{2,1,0:T(8,128)(2,1)} custom-call(s32[9]{0:T(128)S(1)} %pad_add_fusion.2.meta, bf16[16,64,512]{2,1,0:T(8,128)(2,1)S(1)} %broadcast_select_fusion.1.refs_0_, bf16[16,64,512]{2,1,0:T(8,128)(2,1)S(1)} %collective-permute-done.1.refs_1_), custom_call_target="tpu_custom_call" | custom-call | tf_op jit(solution)/shard_map/pallas_call | solution.py:251
  28.6 6.5 %copy.67 = bf16[512,4096]{0,1:T(8,128)(2,1)} copy(bf16[512,4096]{1,0:T(8,128)(2,1)} %rest_8_.1) | data formatting | bytes 8388608 | tf_op jit(solution)/shard_map/optimization_barrier | solution.py:398
  35.1 1.7 %broadcast_select_fusion.refs_0_ = bf16[16,64,512]{2,1,0:T(8,128)(2,1)S(1)} fusion(bf16[16,64,512]{2,1,0:T(8,128)(2,1)} %collective-permute-done.2, pred[]{:T(512)S(6)} %eq.148, bf16[16,128,512]{2,1,0:T(8,128)(2,1)} %bitcast.58), kind=kLoop, calls=%fused_computation | loop fusion | flops 524288 | bytes 3145729 | tf_op jit(solution)/shard_map/jit(_where)/select_n | solution.py:390
  36.8 1.3 collective-permute-start.3
  38.1 4.9 %all-to-all-start.1 = ((bf16[8,64,512]{2,1,0:T(8,128)(2,1)}), bf16[8,64,512]{2,1,0:T(8,128)(2,1)S(1)}, u32[]{:S(2)}, u32[]{:S(2)}) async-start(bf16[8,64,512]{2,1,0:T(8,128)(2,1)} %shard_map.138), calls=%async_computation.1 | async-start | bytes 1048576 | tf_op jit(solution)/shard_map/all_to_all | solution.py:399
  43.0 3.2 %collective-permute-done.3.refs_1_ = bf16[16,64,512]{2,1,0:T(8,128)(2,1)S(1)} collective-permute-done((bf16[16,64,512]{2,1,0:T(8,128)(2,1)S(1)}, bf16[16,64,512]{2,1,0:T(8,128)(2,1)S(1)}, u32[]{:S(2)}, u32[]{:S(2)}) %collective-permute-start.3) | collective-permute-done | bytes 1048608 | tf_op jit(solution)/shard_map/ppermute | solution.py:340
  46.2 1.4 %shard_map.139 = bf16[8,64,512]{2,1,0:T(8,128)(2,1)} custom-call(s32[9]{0:T(128)S(1)} %pad_add_fusion.2.meta, bf16[16,64,512]{2,1,0:T(8,128)(2,1)S(1)} %broadcast_select_fusion.refs_0_, bf16[16,64,512]{2,1,0:T(8,128)(2,1)S(1)} %collective-permute-done.3.refs_1_), custom_call_target="tpu_custom_call" | custom-call | tf_op jit(solution)/shard_map/pallas_call | solution.py:251
  47.6 6.0 %all-to-all-done.1.refs_0_.rest_0_ = bf16[8,64,512]{2,1,0:T(8,128)(2,1)S(1)} async-done(((bf16[8,64,512]{2,1,0:T(8,128)(2,1)}), bf16[8,64,512]{2,1,0:T(8,128)(2,1)S(1)}, u32[]{:S(2)}, u32[]{:S(2)}) %all-to-all-start.1) | async-done | bytes 524320 | tf_op jit(solution)/shard_map/all_to_all | solution.py:399
  53.6 6.9 %all-to-all-start.2 = ((bf16[8,64,512]{2,1,0:T(8,128)(2,1)}), bf16[8,64,512]{2,1,0:T(8,128)(2,1)S(1)}, u32[]{:S(2)}, u32[]{:S(2)}) async-start(bf16[8,64,512]{2,1,0:T(8,128)(2,1)} %shard_map.139), calls=%async_computation.2 | async-start | bytes 1048576 | tf_op jit(solution)/shard_map/all_to_all | solution.py:399
  60.5 0.6 bitcast_convert_fusion.1.cond_ref
  61.1 1.8 %copy.61 = bf16[256,512]{0,1:T(8,128)(2,1)} copy(bf16[256,512]{1,0:T(8,128)(2,1)} %up_ref.1) | data formatting | bytes 524288 | tf_op args[9]
  62.9 0.8 copy.62
  64.0 0.5 broadcast.445
  64.5 0.7 fusion.35
  65.7 0.6 shard_map.140
  66.4 9.5 %all-to-all-done.2.refs_0_.rest_1_ = bf16[8,64,512]{2,1,0:T(8,128)(2,1)S(1)} async-done(((bf16[8,64,512]{2,1,0:T(8,128)(2,1)}), bf16[8,64,512]{2,1,0:T(8,128)(2,1)S(1)}, u32[]{:S(2)}, u32[]{:S(2)}) %all-to-all-start.2) | async-done | bytes 524320 | tf_op jit(solution)/shard_map/all_to_all | solution.py:399
  75.8 0.7 shard_map.141
  77.0 0.4 collective-permute-start.4
  77.6 0.5 collective-permute-start.8
  78.1 7.2 %collective-permute-done.7.rest_5_ = bf16[4,64,512]{2,1,0:T(8,128)(2,1)S(1)} collective-permute-done((bf16[4,64,512]{2,1,0:T(8,128)(2,1)S(1)}, bf16[4,64,512]{2,1,0:T(8,128)(2,1)S(1)}, u32[]{:S(2)}, u32[]{:S(2)}) %collective-permute-start.7) | collective-permute-done | bytes 262176 | tf_op jit(solution)/shard_map/ppermute | solution.py:340
  85.3 0.6 pad_add_fusion.1.meta
  86.0 0.9 collective-permute-done.9.rest_7_
  87.0 0.5 copy-done.14
  87.6 26.2 %shard_map.142 = (bf16[256,2048]{1,0:T(8,128)(2,1)}, bf16[256,2048]{1,0:T(8,128)(2,1)}, f32[4,512]{1,0:T(4,128)}, f32[512,512]{1,0:T(8,128)}) custom-call(s32[25]{0:T(128)} %pad_add_fusion.1.meta, bf16[256,2048]{1,0:T(8,128)(2,1)} %bitcast.75, bf16[256,2048]{1,0:T(8,128)(2,1)} %bitcast.76, f32[4,512]{1,0:T(4,128)} %bitcast_convert_fusion.1.cond_ref, ...), custom_call_target="tpu_custom_call" | custom-call | flops 11811160064 | bytes 16777216 | tf_op jit(solution)/shard_map/pallas_call | solution.py:195
  113.8 1.1 fusion
  114.8 0.2 collective-permute-start.10
  115.0 1.4 %collective-permute-done.10 = bf16[2,8,16,512]{3,2,1,0:T(8,128)(2,1)S(1)} collective-permute-done((bf16[2,8,16,512]{3,2,1,0:T(8,128)(2,1)S(1)}, bf16[2,8,16,512]{3,2,1,0:T(8,128)(2,1)S(1)}, u32[]{:S(2)}, u32[]{:S(2)}) %collective-permute-start.10) | collective-permute-done | bytes 262176 | tf_op jit(solution)/shard_map/ppermute | solution.py:305
  116.4 1.1 bitcast_add_fusion
  117.6 0.3 collective-permute-start.11
  117.9 5.3 %collective-permute-done.11 = bf16[1,8,16,512]{3,2,1,0:T(8,128)(2,1)S(1)} collective-permute-done((bf16[1,8,16,512]{3,2,1,0:T(8,128)(2,1)S(1)}, bf16[1,8,16,512]{3,2,1,0:T(8,128)(2,1)S(1)}, u32[]{:S(2)}, u32[]{:S(2)}) %collective-permute-start.11) | collective-permute-done | bytes 131104 | tf_op jit(solution)/shard_map/ppermute | solution.py:305
  123.3 1.5 %collective-permute-start.12 = (bf16[1,4,16,512]{3,2,1,0:T(8,128)(2,1)S(1)}, bf16[1,4,16,512]{3,2,1,0:T(8,128)(2,1)S(1)}, u32[]{:S(2)}, u32[]{:S(2)}) collective-permute-start(bf16[1,4,16,512]{3,2,1,0:T(8,128)(2,1)S(1)} %fusion.2), channel_id=1, source_target_pairs={{0,1},{1,0},{2,3},{3,2},{4,5},{5,4},{6,7},{7,6},{8,9},{9,8},{10,11... | collective-permute-start | bytes 196616 | tf_op jit(solution)/shard_map/ppermute | solution.py:305
  124.8 2.8 %collective-permute-done.12 = bf16[1,4,16,512]{3,2,1,0:T(8,128)(2,1)S(1)} collective-permute-done((bf16[1,4,16,512]{3,2,1,0:T(8,128)(2,1)S(1)}, bf16[1,4,16,512]{3,2,1,0:T(8,128)(2,1)S(1)}, u32[]{:S(2)}, u32[]{:S(2)}) %collective-permute-start.12) | collective-permute-done | bytes 65568 | tf_op jit(solution)/shard_map/ppermute | solution.py:305
  127.8 3.9 %collective-permute-done.13 = bf16[1,2,16,512]{3,2,1,0:T(8,128)(2,1)S(1)} collective-permute-done((bf16[1,2,16,512]{3,2,1,0:T(8,128)(2,1)S(1)}, bf16[1,2,16,512]{3,2,1,0:T(8,128)(2,1)S(1)}, u32[]{:S(2)}, u32[]{:S(2)}) %collective-permute-start.13) | collective-permute-done | bytes 32800 | tf_op jit(solution)/shard_map/ppermute | solution.py:305
  131.7 0.3 collective-permute-start.14
  132.0 4.4 %collective-permute-done.14 = bf16[1,1,16,512]{3,2,1,0:T(8,128)(2,1)S(1)} collective-permute-done((bf16[1,1,16,512]{3,2,1,0:T(8,128)(2,1)S(1)}, bf16[1,1,16,512]{3,2,1,0:T(8,128)(2,1)S(1)}, u32[]{:S(2)}, u32[]{:S(2)}) %collective-permute-start.14) | collective-permute-done | bytes 16416 | tf_op jit(solution)/shard_map/ppermute | solution.py:305
  136.4 0.6 add_bitcast_fusion
  (87 shorter events, 2.8 us)
Async XLA Ops:
  0.6 19.6 %copy-start.2 = (bf16[1,1,16,128,512]{4,3,2,1,0:T(8,128)(2,1)S(1)}, bf16[1,1,16,128,512]{4,3,2,1,0:T(8,128)(2,1)}, u32[]{:S(2)}) copy-start(bf16[1,1,16,128,512]{4,3,2,1,0:T(8,128)(2,1)} %param.16) | copy-start | bytes 6291460
  0.6 3.2 %copy-start.6 = (s32[1,1,4,2]{2,3,1,0:T(2,128)S(1)}, s32[1,1,4,2]{2,3,1,0:T(2,128)}, u32[]{:S(2)}) copy-start(s32[1,1,4,2]{2,3,1,0:T(2,128)} %param.14) | copy-start | bytes 100
  0.7 3.3 %copy-start.7 = (s32[1,1,4,2]{2,3,1,0:T(2,128)S(1)}, s32[1,1,4,2]{2,3,1,0:T(2,128)}, u32[]{:S(2)}) copy-start(s32[1,1,4,2]{2,3,1,0:T(2,128)} %param.15) | copy-start | bytes 100
  0.7 3.5 %copy-start.8 = (s32[1,1,16]{2,1,0:T(1,128)S(1)}, s32[1,1,16]{2,1,0:T(1,128)}, u32[]{:S(2)}) copy-start(s32[1,1,16]{2,1,0:T(1,128)} %param.17) | copy-start | bytes 196
  2.1 18.1 %collective-permute-start = (bf16[16,64,512]{2,1,0:T(8,128)(2,1)S(1)}, bf16[16,64,512]{2,1,0:T(8,128)(2,1)}, u32[]{:S(2)}, u32[]{:S(2)}) collective-permute-start(bf16[16,64,512]{2,1,0:T(8,128)(2,1)S(1)} %slice.28), channel_id=1, source_target_pairs={{24,8},{25,9},{26,10},{27,11},{28,12},{29,13},{30,14},{31,15}} | collective-permute-start | bytes 3145736 | tf_op jit(solution)/shard_map/ppermute | solution.py:340
  4.9 15.4 %all-to-all-start = ((s32[32,1,128]{2,1,0:T(1,128)}), s32[32,1,128]{2,1,0:T(1,128)S(1)}, u32[]{:S(2)}, u32[]{:S(2)}) async-start(s32[32,1,128]{2,1,0:T(1,128)} %broadcast_in_dim.87), calls=%async_computation | async-start | bytes 32768 | tf_op jit(solution)/shard_map/all_to_all | solution.py:352
  20.2 2.8 %copy-start.3 = (bf16[1,1,16,128,512]{4,3,2,1,0:T(8,128)(2,1)S(1)}, bf16[1,1,16,128,512]{4,3,2,1,0:T(8,128)(2,1)}, u32[]{:S(2)}) copy-start(bf16[1,1,16,128,512]{4,3,2,1,0:T(8,128)(2,1)} %param.16) | copy-start | bytes 6291460
  21.7 5.5 %collective-permute-start.1 = (bf16[16,64,512]{2,1,0:T(8,128)(2,1)S(1)}, bf16[16,64,512]{2,1,0:T(8,128)(2,1)S(1)}, u32[]{:S(2)}, u32[]{:S(2)}) collective-permute-start(bf16[16,64,512]{2,1,0:T(8,128)(2,1)S(1)} %broadcast_select_fusion.1.refs_0_), channel_id=1, source_target_pairs={{24,16},{25,17},{26,18},{27,19},{28,20},{29,21},{30,22},{31,23},{8... | collective-permute-start | bytes 3145736 | tf_op jit(solution)/shard_map/ppermute | solution.py:340
  24.1 11.0 %collective-permute-start.2 = (bf16[16,64,512]{2,1,0:T(8,128)(2,1)}, bf16[16,64,512]{2,1,0:T(8,128)(2,1)}, u32[]{:S(2)}, u32[]{:S(2)}) collective-permute-start(bf16[16,64,512]{2,1,0:T(8,128)(2,1)} %slice.27), channel_id=1, source_target_pairs={{24,8},{25,9},{26,10},{27,11},{28,12},{29,13},{30,14},{31,15}} | collective-permute-start | bytes 3145736 | tf_op jit(solution)/shard_map/ppermute | solution.py:340
  36.8 9.4 %collective-permute-start.3 = (bf16[16,64,512]{2,1,0:T(8,128)(2,1)S(1)}, bf16[16,64,512]{2,1,0:T(8,128)(2,1)S(1)}, u32[]{:S(2)}, u32[]{:S(2)}) collective-permute-start(bf16[16,64,512]{2,1,0:T(8,128)(2,1)S(1)} %broadcast_select_fusion.refs_0_), channel_id=1, source_target_pairs={{24,16},{25,17},{26,18},{27,19},{28,20},{29,21},{30,22},{31,23},{8... | collective-permute-start | bytes 3145736 | tf_op jit(solution)/shard_map/ppermute | solution.py:340
  38.1 15.5 %all-to-all-start.1 = ((bf16[8,64,512]{2,1,0:T(8,128)(2,1)}), bf16[8,64,512]{2,1,0:T(8,128)(2,1)S(1)}, u32[]{:S(2)}, u32[]{:S(2)}) async-start(bf16[8,64,512]{2,1,0:T(8,128)(2,1)} %shard_map.138), calls=%async_computation.1 | async-start | bytes 1048576 | tf_op jit(solution)/shard_map/all_to_all | solution.py:399
  43.0 17.5 %copy-start.5 = (bf16[1,1,4,512]{3,2,1,0:T(4,128)(2,1)S(1)}, bf16[1,1,4,512]{3,2,1,0:T(4,128)(2,1)}, u32[]{:S(2)}) copy-start(bf16[1,1,4,512]{3,2,1,0:T(4,128)(2,1)} %param.13) | copy-start | bytes 12292
  43.0 19.9 %copy-start.4 = (bf16[512,256]{1,0:T(8,128)(2,1)S(1)}, bf16[512,256]{1,0:T(8,128)(2,1)}, u32[]{:S(2)}) copy-start(bf16[512,256]{1,0:T(8,128)(2,1)} %down_ref.1) | copy-start | bytes 786436
  53.6 33.2 %copy-start = (bf16[8,64,512]{2,1,0:T(8,128)(2,1)}, bf16[8,64,512]{2,1,0:T(8,128)(2,1)S(1)}, u32[]{:S(2)}) copy-start(bf16[8,64,512]{2,1,0:T(8,128)(2,1)S(1)} %all-to-all-done.1.refs_0_.rest_0_) | copy-start | bytes 1572868
  53.6 22.2 %all-to-all-start.2 = ((bf16[8,64,512]{2,1,0:T(8,128)(2,1)}), bf16[8,64,512]{2,1,0:T(8,128)(2,1)S(1)}, u32[]{:S(2)}, u32[]{:S(2)}) async-start(bf16[8,64,512]{2,1,0:T(8,128)(2,1)} %shard_map.139), calls=%async_computation.2 | async-start | bytes 1048576 | tf_op jit(solution)/shard_map/all_to_all | solution.py:399
  66.3 11.3 %collective-permute-start.6 = (bf16[4,64,512]{2,1,0:T(8,128)(2,1)S(1)}, bf16[4,64,512]{2,1,0:T(8,128)(2,1)S(1)}, u32[]{:S(2)}, u32[]{:S(2)}) collective-permute-start(bf16[4,64,512]{2,1,0:T(8,128)(2,1)S(1)} %shard_map.140), channel_id=1, source_target_pairs={{0,16},{1,17},{2,18},{3,19},{4,20},{5,21},{6,22},{7,23},{8,24},{9,... | collective-permute-start | bytes 786440 | tf_op jit(solution)/shard_map/ppermute | solution.py:340
  75.8 11.0 %copy-start.1 = (bf16[8,64,512]{2,1,0:T(8,128)(2,1)}, bf16[8,64,512]{2,1,0:T(8,128)(2,1)S(1)}, u32[]{:S(2)}) copy-start(bf16[8,64,512]{2,1,0:T(8,128)(2,1)S(1)} %all-to-all-done.2.refs_0_.rest_1_) | copy-start | bytes 1572868
  76.6 8.7 %collective-permute-start.7 = (bf16[4,64,512]{2,1,0:T(8,128)(2,1)S(1)}, bf16[4,64,512]{2,1,0:T(8,128)(2,1)S(1)}, u32[]{:S(2)}, u32[]{:S(2)}) collective-permute-start(bf16[4,64,512]{2,1,0:T(8,128)(2,1)S(1)} %shard_map.141), channel_id=1, source_target_pairs={{0,16},{1,17},{2,18},{3,19},{4,20},{5,21},{6,22},{7,23},{8,24},{9,... | collective-permute-start | bytes 786440 | tf_op jit(solution)/shard_map/ppermute | solution.py:340
  77.0 8.9 %collective-permute-start.4 = (bf16[8,64,512]{2,1,0:T(8,128)(2,1)S(1)}, bf16[8,64,512]{2,1,0:T(8,128)(2,1)S(1)}, u32[]{:S(2)}, u32[]{:S(2)}) collective-permute-start(bf16[8,64,512]{2,1,0:T(8,128)(2,1)S(1)} %all-to-all-done.1.refs_0_.rest_0_), channel_id=1, source_target_pairs={{0,8},{1,9},{2,10},{3,11},{4,12},{5,13},{6,14},{7,15},{8,0},{9,1},... | collective-permute-start | bytes 1572872 | tf_op jit(solution)/shard_map/ppermute | solution.py:340
  77.5 8.5 %collective-permute-start.5 = (bf16[8,64,512]{2,1,0:T(8,128)(2,1)S(1)}, bf16[8,64,512]{2,1,0:T(8,128)(2,1)S(1)}, u32[]{:S(2)}, u32[]{:S(2)}) collective-permute-start(bf16[8,64,512]{2,1,0:T(8,128)(2,1)S(1)} %all-to-all-done.2.refs_0_.rest_1_), channel_id=1, source_target_pairs={{0,8},{1,9},{2,10},{3,11},{4,12},{5,13},{6,14},{7,15},{8,0},{9,1},... | collective-permute-start | bytes 1572872 | tf_op jit(solution)/shard_map/ppermute | solution.py:340
  77.6 9.3 %copy-start.11 = (bf16[4,64,512]{2,1,0:T(8,128)(2,1)}, bf16[4,64,512]{2,1,0:T(8,128)(2,1)S(1)}, u32[]{:S(2)}) copy-start(bf16[4,64,512]{2,1,0:T(8,128)(2,1)S(1)} %collective-permute-done.6.rest_4_) | copy-start | bytes 786436
  77.6 8.3 %collective-permute-start.8 = (bf16[4,64,512]{2,1,0:T(8,128)(2,1)S(1)}, bf16[4,64,512]{2,1,0:T(8,128)(2,1)S(1)}, u32[]{:S(2)}, u32[]{:S(2)}) collective-permute-start(bf16[4,64,512]{2,1,0:T(8,128)(2,1)S(1)} %collective-permute-done.6.rest_4_), channel_id=1, source_target_pairs={{0,8},{1,9},{2,10},{3,11},{4,12},{5,13},{6,14},{7,15},{8,0},{9,1},... | collective-permute-start | bytes 786440 | tf_op jit(solution)/shard_map/ppermute | solution.py:340
  85.3 1.6 %copy-start.12 = (bf16[4,64,512]{2,1,0:T(8,128)(2,1)}, bf16[4,64,512]{2,1,0:T(8,128)(2,1)S(1)}, u32[]{:S(2)}) copy-start(bf16[4,64,512]{2,1,0:T(8,128)(2,1)S(1)} %collective-permute-done.7.rest_5_) | copy-start | bytes 786436
  85.3 1.5 %collective-permute-start.9 = (bf16[4,64,512]{2,1,0:T(8,128)(2,1)S(1)}, bf16[4,64,512]{2,1,0:T(8,128)(2,1)S(1)}, u32[]{:S(2)}, u32[]{:S(2)}) collective-permute-start(bf16[4,64,512]{2,1,0:T(8,128)(2,1)S(1)} %collective-permute-done.7.rest_5_), channel_id=1, source_target_pairs={{0,8},{1,9},{2,10},{3,11},{4,12},{5,13},{6,14},{7,15},{8,0},{9,1},... | collective-permute-start | bytes 786440 | tf_op jit(solution)/shard_map/ppermute | solution.py:340
  85.9 0.9 copy-start.13
  85.9 0.9 copy-start.9
  86.0 1.1 copy-start.10
  86.8 0.7 copy-start.14
  114.8 1.6 %collective-permute-start.10 = (bf16[2,8,16,512]{3,2,1,0:T(8,128)(2,1)S(1)}, bf16[2,8,16,512]{3,2,1,0:T(8,128)(2,1)S(1)}, u32[]{:S(2)}, u32[]{:S(2)}) collective-permute-start(bf16[2,8,16,512]{3,2,1,0:T(8,128)(2,1)S(1)} %fusion), channel_id=1, source_target_pairs={{0,8},{8,0},{16,24},{24,16},{1,9},{9,1},{17,25},{25,17},{2,10},{10... | collective-permute-start | bytes 786440 | tf_op jit(solution)/shard_map/ppermute | solution.py:305
  117.6 5.6 %collective-permute-start.11 = (bf16[1,8,16,512]{3,2,1,0:T(8,128)(2,1)S(1)}, bf16[1,8,16,512]{3,2,1,0:T(8,128)(2,1)S(1)}, u32[]{:S(2)}, u32[]{:S(2)}) collective-permute-start(bf16[1,8,16,512]{3,2,1,0:T(8,128)(2,1)S(1)} %dynamic-slice_convert_fusion), channel_id=1, source_target_pairs={{0,16},{8,24},{16,0},{24,8},{1,17},{9,25},{17,1},{25,9},{2,18},{10... | collective-permute-start | bytes 393224 | tf_op jit(solution)/shard_map/ppermute | solution.py:305
  123.3 4.3 %collective-permute-start.12 = (bf16[1,4,16,512]{3,2,1,0:T(8,128)(2,1)S(1)}, bf16[1,4,16,512]{3,2,1,0:T(8,128)(2,1)S(1)}, u32[]{:S(2)}, u32[]{:S(2)}) collective-permute-start(bf16[1,4,16,512]{3,2,1,0:T(8,128)(2,1)S(1)} %fusion.2), channel_id=1, source_target_pairs={{0,1},{1,0},{2,3},{3,2},{4,5},{5,4},{6,7},{7,6},{8,9},{9,8},{10,11... | collective-permute-start | bytes 196616 | tf_op jit(solution)/shard_map/ppermute | solution.py:305
  127.7 4.0 %collective-permute-start.13 = (bf16[1,2,16,512]{3,2,1,0:T(8,128)(2,1)S(1)}, bf16[1,2,16,512]{3,2,1,0:T(8,128)(2,1)S(1)}, u32[]{:S(2)}, u32[]{:S(2)}) collective-permute-start(bf16[1,2,16,512]{3,2,1,0:T(8,128)(2,1)S(1)} %fusion.3), channel_id=1, source_target_pairs={{0,2},{1,3},{2,0},{3,1},{4,6},{5,7},{6,4},{7,5},{8,10},{9,11},{10,... | collective-permute-start | bytes 98312 | tf_op jit(solution)/shard_map/ppermute | solution.py:305
  131.7 4.7 %collective-permute-start.14 = (bf16[1,1,16,512]{3,2,1,0:T(8,128)(2,1)S(1)}, bf16[1,1,16,512]{3,2,1,0:T(8,128)(2,1)S(1)}, u32[]{:S(2)}, u32[]{:S(2)}) collective-permute-start(bf16[1,1,16,512]{3,2,1,0:T(8,128)(2,1)S(1)} %dynamic-slice_convert_fusion.3), channel_id=1, source_target_pairs={{0,4},{1,5},{2,6},{3,7},{4,0},{5,1},{6,2},{7,3},{8,12},{9,13},{10,... | collective-permute-start | bytes 49160 | tf_op jit(solution)/shard_map/ppermute | solution.py:305

commit v11 on v10

--- a/solution.py
+++ b/solution.py
@@ -261,6 +261,36 @@
     )(meta, *held)
 
 
+def cut_kernel(held_count, low, meta, *refs):
+    held_refs, out_ref, sems = refs[:held_count], refs[held_count], refs[held_count + 1]
+    count, piece = out_ref.shape[:2]
+    rows = pl.ds(low, piece)
+    for b, held in enumerate(held_refs):
+        @pl.when(meta[0] == b)
+        def _():
+            for n in range(count):
+                pltpu.make_async_copy(held.at[meta[1 + n], rows], out_ref.at[n], sems.at[n]).start()
+    for n in range(count):
+        pltpu.make_async_copy(held_refs[0].at[0, rows], out_ref.at[n], sems.at[n]).wait()
+
+
+def cut(which, index, held, low, piece):
+    count = index.shape[0]
+    meta = jnp.concatenate([jnp.reshape(which, (1,)), index]).astype(jnp.int32)
+    return pl.pallas_call(
+        functools.partial(cut_kernel, len(held), low),
+        grid_spec=pltpu.PrefetchScalarGridSpec(
+            num_scalar_prefetch=1,
+            grid=(1,),
+            in_specs=[pl.BlockSpec(memory_space=pltpu.HBM)] * len(held),
+            out_specs=pl.BlockSpec(memory_space=pltpu.VMEM),
+            scratch_shapes=[pltpu.SemaphoreType.DMA((count,))],
+        ),
+        out_shape=jax.ShapeDtypeStruct((count, piece, held[0].shape[2]), held[0].dtype),
+        compiler_params=pltpu.CompilerParams(vmem_limit_bytes=60 * 2**20),
+    )(meta, *held)
+
+
 def place_requests(owners, per_device, pool_count, lanes):
     half = pool_count // 2
     count = owners.shape[1]
@@ -343,22 +373,23 @@
 
     parts = PARTS if slot_len % (PARTS * 16) == 0 else 1
     piece = slot_len // parts
-    full_store = database.reshape(block_count, slot_len, width)
-    cut = lambda i: full_store[:, i * piece : (i + 1) * piece]
-    store = [cut(0)]
+    store = database.reshape(block_count, slot_len, width)
 
     def to_all(array, axis):
         copies = jnp.broadcast_to(array[None], (lax.axis_size(axis),) + array.shape)
         return lax.all_to_all(copies, axis, split_axis=0, concat_axis=0, tiled=True)
 
+    across = hop(store, [(relay_row, relay_row - half)])
     info = jnp.concatenate([nbr_owner.reshape(-1), nbr_block.reshape(-1), lengths.reshape(-1)])
     info = jnp.pad(info, (0, -info.shape[0] % 128))
-    over = lambda a: hop(a, [(relay_row, relay_row - half)])
-    across = [over(store[0])]
     table = to_all(info.reshape(-1, 128), axes)
-    full_store, across, table = lax.optimization_barrier((full_store, across, table))
-    store += [cut(i) for i in range(1, parts)]
-    across += [over(a) for a in store[1:]]
+    store, across, table = lax.optimization_barrier((store, across, table))
+    stores = [store, across]
+    held_by = jnp.where(row == relay_row, 0, 1)
+    for step in range(1, half):
+        for near, array in ((relay_row, store), (relay_row - half, across)):
+            held_by = jnp.where(row == near - step, len(stores), held_by)
+            stores.append(hop(array, [(near, near - step)]))
     table = table.reshape(pool_count, columns, -1)
     by_column = jnp.swapaxes(table[:relay_row], 0, 1)
     owners = by_column[:, :, :per_device].reshape(columns, live_count)
@@ -385,15 +416,10 @@
     held = []
     weight, weight_t = w_kv, None
     for i in range(parts):
+        wanted = slot_block
         if i == 1:
-            weight_t, across[i] = lax.optimization_barrier((weight.T, across[i]))
-        near = jnp.where(row == relay_row, store[i], across[i])
-        stores = [near]
-        held_by = jnp.where(row % half == half - 1, 0, 1)
-        for step in range(1, half):
-            stores.append(hop(near, [(p, p - step) for p in (relay_row, relay_row - half)]))
-            held_by = jnp.where(row % half == half - 1 - step, step, held_by)
-        sends = pick(held_by, slot_block, stores)
+            weight_t, wanted = lax.optimization_barrier((weight.T, wanted))
+        sends = cut(held_by, wanted, stores, i * piece, piece)
         if i == 0:
             weight, sends = lax.optimization_barrier((weight, sends))
         arrived = lax.all_to_all(sends, "dp", split_axis=0, concat_axis=0, tiled=True)

time: 138 us -> 148 us (1.072)
  blocking collectives: 0 us -> 46.1 us
  waiting for transfers between devices: 51.5 us -> 33.7 us
  starting transfers between devices: 29.5 us -> 13.5 us
  local copies, waits for them, and re-layouts: 16 us -> 13.3 us
  Pallas kernels: 30.3 us -> 32.7 us
    all_to_all x0 -> x2, blocking collectives: none -> 46.1 us  [the longest x1 26.3 us: to_all(): return lax.all_to_all(copies, axis, split_axis=0, concat_axis=0, tiled=True)]
    all_to_all x1 -> x0, starting transfers between devices: 8.23 us -> none  [to_all(): return lax.all_to_all(copies, axis, split_axis=0, concat_axis=0, tiled=True)]
    all_to_all x2 -> x1, starting transfers between devices: 11.8 us -> 3.64 us  [body(): lax.all_to_all(sends, 'dp', split_axis=0, concat_axis=0, tiled=True)]
    all_to_all x1 -> x0, waiting for transfers between devices: 6.98 us -> none  [to_all(): return lax.all_to_all(copies, axis, split_axis=0, concat_axis=0, tiled=True)]
    all_to_all x2 -> x1, waiting for transfers between devices: 15.5 us -> 9.3 us  [body(): lax.all_to_all(sends, 'dp', split_axis=0, concat_axis=0, tiled=True)]
    pallas_call x0 -> x2, Pallas kernels: none -> 5.23 us  [cut(): pl.pallas_call(functools.partial(cut_kernel, len(held), low), grid_spec=p...]
    select_n x2 -> x0, other arithmetic: 3.14 us -> none  [body(): near = jnp.where(row == relay_row, store[i], across[i])]
    pallas_call x4 -> x2, Pallas kernels: 4.09 us -> 1.32 us  [pick(): pl.pallas_call(functools.partial(pick_kernel, len(held)), grid_spec=pltpu...]
  transfers between devices with their start and end apart: 18 -> 15, of which waited for: 11 -> 9; matrix products, arithmetic and copies ran while one was open for 12% -> 7% of each run, Pallas kernels for 3% -> 1%
where the time goes in v11:
time: 148 us
  blocking collectives  46.1 us (31%)
  waiting for transfers between devices  33.7 us (23%)
  Pallas kernels  32.7 us (22%)
  starting transfers between devices  13.5 us (9%)
  local copies, waits for them, and re-layouts  13.3 us (9%)
  other arithmetic  7.28 us (5%)
    all_to_all x1, blocking collectives, to_all(): return lax.all_to_all(copies, axis, split_axis=0, concat_axis=0, tiled=True)  26.3 us
    pallas_call x1, Pallas kernels, run_spans(): pl.pallas_call(functools.partial(span_kernel, len(held), nbr_count, parts...  26.2 us
    all_to_all x1, blocking collectives, body(): lax.all_to_all(sends, 'dp', split_axis=0, concat_axis=0, tiled=True)  19.8 us
    ppermute x5, waiting for transfers between devices, scatter_sum(): lax.ppermute(give.astype(jnp.bfloat16), axis, [(i, i ^ bit) for i in rang...  15.4 us
    all_to_all x1, waiting for transfers between devices, body(): lax.all_to_all(sends, 'dp', split_axis=0, concat_axis=0, tiled=True)  9.3 us
    ppermute x9, waiting for transfers between devices, hop(): lax.ppermute(array, axes, [(a * columns + j, b * columns + j) for a, b in...  9 us
    optimization_barrier x1, local copies, waits for them, and re-layouts, body(): weight, sends = lax.optimization_barrier((weight, sends))  6.47 us
    pallas_call x2, Pallas kernels, cut(): pl.pallas_call(functools.partial(cut_kernel, len(held), low), grid_spec=p...  5.23 us
  transfers between devices with their start and end apart: 15, of which 9 were waited for; matrix products, arithmetic and copies ran while one was open for 7% of the time, Pallas kernels for 1%

profile of v11, /device:TPU:0, one launch (start us, length us, event | category | flops | bytes accessed | tf_op | source)
XLA Modules:
  0.0 147.5 jit_solution(9287583303481064289)
XLA Ops:
  0.6 0.8 collective-permute-start
  1.4 0.8 copy.56
  2.3 0.8 copy.57
  3.1 0.7 pad_add_fusion
  3.9 26.3 %all_to_all.15 = s32[32,1,128]{2,1,0:T(1,128)S(1)} all-to-all(s32[32,1,128]{2,1,0:T(1,128)S(1)} %broadcast_in_dim.87), channel_id=1, replica_groups=mesh['pool'=4,'dp'=8] {'pool','dp'}, dimensions={0} | all-to-all | bytes 32768 | tf_op jit(solution)/shard_map/all_to_all | solution.py:380
  30.2 2.0 %collective-permute-start.1 = (bf16[16,128,512]{2,1,0:T(8,128)(2,1)}, bf16[16,128,512]{2,1,0:T(8,128)(2,1)}, u32[]{:S(2)}, u32[]{:S(2)}) collective-permute-start(bf16[16,128,512]{2,1,0:T(8,128)(2,1)} %bitcast.58), channel_id=1, source_target_pairs={{24,16},{25,17},{26,18},{27,19},{28,20},{29,21},{30,22},{31,23}} | collective-permute-start | bytes 6291464 | tf_op jit(solution)/shard_map/ppermute | solution.py:370
  32.2 1.3 collective-permute-start.2
  33.7 0.3 convert_reduce_fusion.3
  34.1 0.6 convert_reduce_fusion
  34.9 0.2 select_reduce_fusion
  35.1 0.6 pad_add_fusion.2.meta
  35.7 2.7 %collective-permute-done.2.refs_3_ = bf16[16,128,512]{2,1,0:T(8,128)(2,1)} collective-permute-done((bf16[16,128,512]{2,1,0:T(8,128)(2,1)S(1)}, bf16[16,128,512]{2,1,0:T(8,128)(2,1)}, u32[]{:S(2)}, u32[]{:S(2)}) %collective-permute-start.2) | collective-permute-done | bytes 2097184 | tf_op jit(solution)/shard_map/ppermute | solution.py:370
  38.4 2.6 %shard_map.138 = bf16[8,64,512]{2,1,0:T(8,128)(2,1)} custom-call(s32[9]{0:T(128)} %pad_add_fusion.2.meta, bf16[16,128,512]{2,1,0:T(8,128)(2,1)} %bitcast.59, bf16[16,128,512]{2,1,0:T(8,128)(2,1)} %copy-done.2, bf16[16,128,512]{2,1,0:T(8,128)(2,1)} %collective-permute-done.1.refs_2_, bf16[16,128,512]{2,1,0:T(8,128)(2,1)} %collective-permute-done.2.refs_3_), custom_call_target="tpu_custom_call" | custom-call | tf_op jit(solution)/shard_map/pallas_call | solution.py:280
  41.0 6.5 %copy.67 = bf16[512,4096]{0,1:T(8,128)(2,1)} copy(bf16[512,4096]{1,0:T(8,128)(2,1)} %rest_8_.1) | data formatting | bytes 8388608 | tf_op jit(solution)/shard_map/optimization_barrier | solution.py:424
  47.5 0.6 pad_add_fusion.3.meta
  48.0 2.6 %shard_map.139 = bf16[8,64,512]{2,1,0:T(8,128)(2,1)} custom-call(s32[9]{0:T(128)} %pad_add_fusion.3.meta, bf16[16,128,512]{2,1,0:T(8,128)(2,1)} %bitcast.60, bf16[16,128,512]{2,1,0:T(8,128)(2,1)} %copy-done.2, bf16[16,128,512]{2,1,0:T(8,128)(2,1)} %collective-permute-done.1.refs_2_, bf16[16,128,512]{2,1,0:T(8,128)(2,1)} %collective-permute-done.2.refs_3_), custom_call_target="tpu_custom_call" | custom-call | tf_op jit(solution)/shard_map/pallas_call | solution.py:280
  50.7 19.8 %all_to_all.16.refs_0_.rest_1_ = bf16[8,64,512]{2,1,0:T(8,128)(2,1)S(1)} all-to-all(bf16[8,64,512]{2,1,0:T(8,128)(2,1)} %shard_map.139), channel_id=1, replica_groups=mesh['pool'=4,'dp'=8] {'dp'}, dimensions={0} | all-to-all | bytes 1048576 | tf_op jit(solution)/shard_map/all_to_all | solution.py:425
  70.5 3.6 %all-to-all-start.1 = ((bf16[8,64,512]{2,1,0:T(8,128)(2,1)}), bf16[8,64,512]{2,1,0:T(8,128)(2,1)S(1)}, u32[]{:S(2)}, u32[]{:S(2)}) async-start(bf16[8,64,512]{2,1,0:T(8,128)(2,1)} %shard_map.138), calls=%async_computation.1 | async-start | bytes 1048576 | tf_op jit(solution)/shard_map/all_to_all | solution.py:425
  74.1 0.6 bitcast_convert_fusion.1.cond_ref
  74.7 0.8 copy.61
  75.6 0.8 copy.62
  76.7 0.5 broadcast.444
  77.2 0.7 fusion.35
  77.8 0.2 select_reduce_fusion.1
  78.4 0.6 shard_map.141
  79.0 9.3 %all-to-all-done.1.refs_0_.rest_0_ = bf16[8,64,512]{2,1,0:T(8,128)(2,1)S(1)} async-done(((bf16[8,64,512]{2,1,0:T(8,128)(2,1)}), bf16[8,64,512]{2,1,0:T(8,128)(2,1)S(1)}, u32[]{:S(2)}, u32[]{:S(2)}) %all-to-all-start.1) | async-done | bytes 524320 | tf_op jit(solution)/shard_map/all_to_all | solution.py:425
  88.3 0.7 shard_map.140
  89.5 0.5 collective-permute-start.3
  90.1 0.1 collective-permute-start.8
  90.2 5.5 %collective-permute-done.5.rest_4_ = bf16[4,64,512]{2,1,0:T(8,128)(2,1)S(1)} collective-permute-done((bf16[4,64,512]{2,1,0:T(8,128)(2,1)S(1)}, bf16[4,64,512]{2,1,0:T(8,128)(2,1)S(1)}, u32[]{:S(2)}, u32[]{:S(2)}) %collective-permute-start.5) | collective-permute-done | bytes 262176 | tf_op jit(solution)/shard_map/ppermute | solution.py:370
  95.7 0.7 pad_add_fusion.1.meta
  96.4 0.8 collective-permute-done.7.rest_6_
  97.3 0.1 copy-done.7
  97.5 0.5 copy-done.11
  98.0 26.2 %shard_map.142 = (bf16[256,2048]{1,0:T(8,128)(2,1)}, bf16[256,2048]{1,0:T(8,128)(2,1)}, f32[4,512]{1,0:T(4,128)}, f32[512,512]{1,0:T(8,128)}) custom-call(s32[25]{0:T(128)} %pad_add_fusion.1.meta, bf16[256,2048]{1,0:T(8,128)(2,1)} %bitcast.75, bf16[256,2048]{1,0:T(8,128)(2,1)} %bitcast.76, f32[4,512]{1,0:T(4,128)} %bitcast_convert_fusion.1.cond_ref, ...), custom_call_target="tpu_custom_call" | custom-call | flops 11811160064 | bytes 16777216 | tf_op jit(solution)/shard_map/pallas_call | solution.py:195
  124.1 1.1 fusion
  125.2 0.2 collective-permute-start.9
  125.4 1.4 collective-permute-done.9
  126.8 1.1 bitcast_add_fusion
  128.0 0.4 collective-permute-start.10
  128.4 5.2 %collective-permute-done.10 = bf16[1,8,16,512]{3,2,1,0:T(8,128)(2,1)S(1)} collective-permute-done((bf16[1,8,16,512]{3,2,1,0:T(8,128)(2,1)S(1)}, bf16[1,8,16,512]{3,2,1,0:T(8,128)(2,1)S(1)}, u32[]{:S(2)}, u32[]{:S(2)}) %collective-permute-start.10) | collective-permute-done | bytes 131104 | tf_op jit(solution)/shard_map/ppermute | solution.py:335
  133.7 2.1 %collective-permute-start.11 = (bf16[1,4,16,512]{3,2,1,0:T(8,128)(2,1)S(1)}, bf16[1,4,16,512]{3,2,1,0:T(8,128)(2,1)S(1)}, u32[]{:S(2)}, u32[]{:S(2)}) collective-permute-start(bf16[1,4,16,512]{3,2,1,0:T(8,128)(2,1)S(1)} %fusion.2), channel_id=1, source_target_pairs={{0,1},{1,0},{2,3},{3,2},{4,5},{5,4},{6,7},{7,6},{8,9},{9,8},{10,11... | collective-permute-start | bytes 196616 | tf_op jit(solution)/shard_map/ppermute | solution.py:335
  135.8 2.2 %collective-permute-done.11 = bf16[1,4,16,512]{3,2,1,0:T(8,128)(2,1)S(1)} collective-permute-done((bf16[1,4,16,512]{3,2,1,0:T(8,128)(2,1)S(1)}, bf16[1,4,16,512]{3,2,1,0:T(8,128)(2,1)S(1)}, u32[]{:S(2)}, u32[]{:S(2)}) %collective-permute-start.11) | collective-permute-done | bytes 65568 | tf_op jit(solution)/shard_map/ppermute | solution.py:335
  138.1 0.5 collective-permute-start.12
  138.6 3.4 %collective-permute-done.12 = bf16[1,2,16,512]{3,2,1,0:T(8,128)(2,1)S(1)} collective-permute-done((bf16[1,2,16,512]{3,2,1,0:T(8,128)(2,1)S(1)}, bf16[1,2,16,512]{3,2,1,0:T(8,128)(2,1)S(1)}, u32[]{:S(2)}, u32[]{:S(2)}) %collective-permute-start.12) | collective-permute-done | bytes 32800 | tf_op jit(solution)/shard_map/ppermute | solution.py:335
  142.1 1.7 %collective-permute-start.13 = (bf16[1,1,16,512]{3,2,1,0:T(8,128)(2,1)S(1)}, bf16[1,1,16,512]{3,2,1,0:T(8,128)(2,1)S(1)}, u32[]{:S(2)}, u32[]{:S(2)}) collective-permute-start(bf16[1,1,16,512]{3,2,1,0:T(8,128)(2,1)S(1)} %dynamic-slice_convert_fusion.3), channel_id=1, source_target_pairs={{0,4},{1,5},{2,6},{3,7},{4,0},{5,1},{6,2},{7,3},{8,12},{9,13},{10,... | collective-permute-start | bytes 49160 | tf_op jit(solution)/shard_map/ppermute | solution.py:335
  143.8 3.1 %collective-permute-done.13 = bf16[1,1,16,512]{3,2,1,0:T(8,128)(2,1)S(1)} collective-permute-done((bf16[1,1,16,512]{3,2,1,0:T(8,128)(2,1)S(1)}, bf16[1,1,16,512]{3,2,1,0:T(8,128)(2,1)S(1)}, u32[]{:S(2)}, u32[]{:S(2)}) %collective-permute-start.13) | collective-permute-done | bytes 16416 | tf_op jit(solution)/shard_map/ppermute | solution.py:335
  146.9 0.6 add_bitcast_fusion
  (74 shorter events, 2.0 us)
Async XLA Ops:
  0.6 29.5 %collective-permute-start = (bf16[16,128,512]{2,1,0:T(8,128)(2,1)}, bf16[16,128,512]{2,1,0:T(8,128)(2,1)S(1)}, u32[]{:S(2)}, u32[]{:S(2)}) collective-permute-start(bf16[16,128,512]{2,1,0:T(8,128)(2,1)} %bitcast.57), channel_id=1, source_target_pairs={{24,8},{25,9},{26,10},{27,11},{28,12},{29,13},{30,14},{31,15}} | collective-permute-start | bytes 6291464 | tf_op jit(solution)/shard_map/ppermute | solution.py:370
  30.2 8.2 %copy-start.2 = (bf16[16,128,512]{2,1,0:T(8,128)(2,1)}, bf16[16,128,512]{2,1,0:T(8,128)(2,1)S(1)}, u32[]{:S(2)}) copy-start(bf16[16,128,512]{2,1,0:T(8,128)(2,1)S(1)} %collective-permute-done.refs_1_) | copy-start | bytes 6291460
  30.2 5.5 %collective-permute-start.1 = (bf16[16,128,512]{2,1,0:T(8,128)(2,1)}, bf16[16,128,512]{2,1,0:T(8,128)(2,1)}, u32[]{:S(2)}, u32[]{:S(2)}) collective-permute-start(bf16[16,128,512]{2,1,0:T(8,128)(2,1)} %bitcast.58), channel_id=1, source_target_pairs={{24,16},{25,17},{26,18},{27,19},{28,20},{29,21},{30,22},{31,23}} | collective-permute-start | bytes 6291464 | tf_op jit(solution)/shard_map/ppermute | solution.py:370
  32.2 6.2 %collective-permute-start.2 = (bf16[16,128,512]{2,1,0:T(8,128)(2,1)S(1)}, bf16[16,128,512]{2,1,0:T(8,128)(2,1)}, u32[]{:S(2)}, u32[]{:S(2)}) collective-permute-start(bf16[16,128,512]{2,1,0:T(8,128)(2,1)S(1)} %collective-permute-done.refs_1_), channel_id=1, source_target_pairs={{8,0},{9,1},{10,2},{11,3},{12,4},{13,5},{14,6},{15,7}} | collective-permute-start | bytes 6291464 | tf_op jit(solution)/shard_map/ppermute | solution.py:370
  50.7 23.5 %copy-start.5 = (bf16[1,1,4,512]{3,2,1,0:T(4,128)(2,1)S(1)}, bf16[1,1,4,512]{3,2,1,0:T(4,128)(2,1)}, u32[]{:S(2)}) copy-start(bf16[1,1,4,512]{3,2,1,0:T(4,128)(2,1)} %param.13) | copy-start | bytes 12292
  50.7 24.1 %copy-start.4 = (bf16[256,512]{1,0:T(8,128)(2,1)S(1)}, bf16[256,512]{1,0:T(8,128)(2,1)}, u32[]{:S(2)}) copy-start(bf16[256,512]{1,0:T(8,128)(2,1)} %up_ref.1) | copy-start | bytes 786436
  50.7 24.9 %copy-start.3 = (bf16[512,256]{1,0:T(8,128)(2,1)S(1)}, bf16[512,256]{1,0:T(8,128)(2,1)}, u32[]{:S(2)}) copy-start(bf16[512,256]{1,0:T(8,128)(2,1)} %down_ref.1) | copy-start | bytes 786436
  70.5 26.7 %copy-start = (bf16[8,64,512]{2,1,0:T(8,128)(2,1)}, bf16[8,64,512]{2,1,0:T(8,128)(2,1)S(1)}, u32[]{:S(2)}) copy-start(bf16[8,64,512]{2,1,0:T(8,128)(2,1)S(1)} %all_to_all.16.refs_0_.rest_1_) | copy-start | bytes 1572868
  70.5 17.8 %all-to-all-start.1 = ((bf16[8,64,512]{2,1,0:T(8,128)(2,1)}), bf16[8,64,512]{2,1,0:T(8,128)(2,1)S(1)}, u32[]{:S(2)}, u32[]{:S(2)}) async-start(bf16[8,64,512]{2,1,0:T(8,128)(2,1)} %shard_map.138), calls=%async_computation.1 | async-start | bytes 1048576 | tf_op jit(solution)/shard_map/all_to_all | solution.py:425
  78.9 11.1 %collective-permute-start.6 = (bf16[4,64,512]{2,1,0:T(8,128)(2,1)S(1)}, bf16[4,64,512]{2,1,0:T(8,128)(2,1)S(1)}, u32[]{:S(2)}, u32[]{:S(2)}) collective-permute-start(bf16[4,64,512]{2,1,0:T(8,128)(2,1)S(1)} %shard_map.141), channel_id=1, source_target_pairs={{0,16},{1,17},{2,18},{3,19},{4,20},{5,21},{6,22},{7,23},{8,24},{9,... | collective-permute-start | bytes 786440 | tf_op jit(solution)/shard_map/ppermute | solution.py:370
  88.3 8.9 %copy-start.1 = (bf16[8,64,512]{2,1,0:T(8,128)(2,1)}, bf16[8,64,512]{2,1,0:T(8,128)(2,1)S(1)}, u32[]{:S(2)}) copy-start(bf16[8,64,512]{2,1,0:T(8,128)(2,1)S(1)} %all-to-all-done.1.refs_0_.rest_0_) | copy-start | bytes 1572868
  89.1 6.6 %collective-permute-start.5 = (bf16[4,64,512]{2,1,0:T(8,128)(2,1)S(1)}, bf16[4,64,512]{2,1,0:T(8,128)(2,1)S(1)}, u32[]{:S(2)}, u32[]{:S(2)}) collective-permute-start(bf16[4,64,512]{2,1,0:T(8,128)(2,1)S(1)} %shard_map.140), channel_id=1, source_target_pairs={{0,16},{1,17},{2,18},{3,19},{4,20},{5,21},{6,22},{7,23},{8,24},{9,... | collective-permute-start | bytes 786440 | tf_op jit(solution)/shard_map/ppermute | solution.py:370
  89.5 6.9 %collective-permute-start.4 = (bf16[8,64,512]{2,1,0:T(8,128)(2,1)S(1)}, bf16[8,64,512]{2,1,0:T(8,128)(2,1)S(1)}, u32[]{:S(2)}, u32[]{:S(2)}) collective-permute-start(bf16[8,64,512]{2,1,0:T(8,128)(2,1)S(1)} %all_to_all.16.refs_0_.rest_1_), channel_id=1, source_target_pairs={{0,8},{1,9},{2,10},{3,11},{4,12},{5,13},{6,14},{7,15},{8,0},{9,1},... | collective-permute-start | bytes 1572872 | tf_op jit(solution)/shard_map/ppermute | solution.py:370
  89.5 6.9 %collective-permute-start.3 = (bf16[8,64,512]{2,1,0:T(8,128)(2,1)S(1)}, bf16[8,64,512]{2,1,0:T(8,128)(2,1)S(1)}, u32[]{:S(2)}, u32[]{:S(2)}) collective-permute-start(bf16[8,64,512]{2,1,0:T(8,128)(2,1)S(1)} %all-to-all-done.1.refs_0_.rest_0_), channel_id=1, source_target_pairs={{0,8},{1,9},{2,10},{3,11},{4,12},{5,13},{6,14},{7,15},{8,0},{9,1},... | collective-permute-start | bytes 1572872 | tf_op jit(solution)/shard_map/ppermute | solution.py:370
  90.1 7.2 %copy-start.8 = (bf16[4,64,512]{2,1,0:T(8,128)(2,1)}, bf16[4,64,512]{2,1,0:T(8,128)(2,1)S(1)}, u32[]{:S(2)}) copy-start(bf16[4,64,512]{2,1,0:T(8,128)(2,1)S(1)} %collective-permute-done.6.rest_5_) | copy-start | bytes 786436
  90.1 6.3 %collective-permute-start.8 = (bf16[4,64,512]{2,1,0:T(8,128)(2,1)S(1)}, bf16[4,64,512]{2,1,0:T(8,128)(2,1)S(1)}, u32[]{:S(2)}, u32[]{:S(2)}) collective-permute-start(bf16[4,64,512]{2,1,0:T(8,128)(2,1)S(1)} %collective-permute-done.6.rest_5_), channel_id=1, source_target_pairs={{0,8},{1,9},{2,10},{3,11},{4,12},{5,13},{6,14},{7,15},{8,0},{9,1},... | collective-permute-start | bytes 786440 | tf_op jit(solution)/shard_map/ppermute | solution.py:370
  95.7 1.6 %copy-start.9 = (bf16[4,64,512]{2,1,0:T(8,128)(2,1)}, bf16[4,64,512]{2,1,0:T(8,128)(2,1)S(1)}, u32[]{:S(2)}) copy-start(bf16[4,64,512]{2,1,0:T(8,128)(2,1)S(1)} %collective-permute-done.5.rest_4_) | copy-start | bytes 786436
  95.7 1.5 %collective-permute-start.7 = (bf16[4,64,512]{2,1,0:T(8,128)(2,1)S(1)}, bf16[4,64,512]{2,1,0:T(8,128)(2,1)S(1)}, u32[]{:S(2)}, u32[]{:S(2)}) collective-permute-start(bf16[4,64,512]{2,1,0:T(8,128)(2,1)S(1)} %collective-permute-done.5.rest_4_), channel_id=1, source_target_pairs={{0,8},{1,9},{2,10},{3,11},{4,12},{5,13},{6,14},{7,15},{8,0},{9,1},... | collective-permute-start | bytes 786440 | tf_op jit(solution)/shard_map/ppermute | solution.py:370
  96.4 0.9 copy-start.6
  96.4 1.0 copy-start.7
  96.4 1.0 copy-start.10
  97.2 0.7 copy-start.11
  125.2 1.6 %collective-permute-start.9 = (bf16[2,8,16,512]{3,2,1,0:T(8,128)(2,1)S(1)}, bf16[2,8,16,512]{3,2,1,0:T(8,128)(2,1)S(1)}, u32[]{:S(2)}, u32[]{:S(2)}) collective-permute-start(bf16[2,8,16,512]{3,2,1,0:T(8,128)(2,1)S(1)} %fusion), channel_id=1, source_target_pairs={{0,8},{8,0},{16,24},{24,16},{1,9},{9,1},{17,25},{25,17},{2,10},{10... | collective-permute-start | bytes 786440 | tf_op jit(solution)/shard_map/ppermute | solution.py:335
  128.0 5.6 %collective-permute-start.10 = (bf16[1,8,16,512]{3,2,1,0:T(8,128)(2,1)S(1)}, bf16[1,8,16,512]{3,2,1,0:T(8,128)(2,1)S(1)}, u32[]{:S(2)}, u32[]{:S(2)}) collective-permute-start(bf16[1,8,16,512]{3,2,1,0:T(8,128)(2,1)S(1)} %dynamic-slice_convert_fusion), channel_id=1, source_target_pairs={{0,16},{8,24},{16,0},{24,8},{1,17},{9,25},{17,1},{25,9},{2,18},{10... | collective-permute-start | bytes 393224 | tf_op jit(solution)/shard_map/ppermute | solution.py:335
  133.7 4.4 %collective-permute-start.11 = (bf16[1,4,16,512]{3,2,1,0:T(8,128)(2,1)S(1)}, bf16[1,4,16,512]{3,2,1,0:T(8,128)(2,1)S(1)}, u32[]{:S(2)}, u32[]{:S(2)}) collective-permute-start(bf16[1,4,16,512]{3,2,1,0:T(8,128)(2,1)S(1)} %fusion.2), channel_id=1, source_target_pairs={{0,1},{1,0},{2,3},{3,2},{4,5},{5,4},{6,7},{7,6},{8,9},{9,8},{10,11... | collective-permute-start | bytes 196616 | tf_op jit(solution)/shard_map/ppermute | solution.py:335
  138.1 4.0 %collective-permute-start.12 = (bf16[1,2,16,512]{3,2,1,0:T(8,128)(2,1)S(1)}, bf16[1,2,16,512]{3,2,1,0:T(8,128)(2,1)S(1)}, u32[]{:S(2)}, u32[]{:S(2)}) collective-permute-start(bf16[1,2,16,512]{3,2,1,0:T(8,128)(2,1)S(1)} %fusion.3), channel_id=1, source_target_pairs={{0,2},{1,3},{2,0},{3,1},{4,6},{5,7},{6,4},{7,5},{8,10},{9,11},{10,... | collective-permute-start | bytes 98312 | tf_op jit(solution)/shard_map/ppermute | solution.py:335
  142.1 4.8 %collective-permute-start.13 = (bf16[1,1,16,512]{3,2,1,0:T(8,128)(2,1)S(1)}, bf16[1,1,16,512]{3,2,1,0:T(8,128)(2,1)S(1)}, u32[]{:S(2)}, u32[]{:S(2)}) collective-permute-start(bf16[1,1,16,512]{3,2,1,0:T(8,128)(2,1)S(1)} %dynamic-slice_convert_fusion.3), channel_id=1, source_target_pairs={{0,4},{1,5},{2,6},{3,7},{4,0},{5,1},{6,2},{7,3},{8,12},{9,13},{10,... | collective-permute-start | bytes 49160 | tf_op jit(solution)/shard_map/ppermute | solution.py:335

commit v12 on v10

--- a/solution.py
+++ b/solution.py
@@ -10,7 +10,6 @@
 HEADS = 16
 HEAD = 128
 SPAN = 64
-PARTS = 2
 GROUP = 2
 
 EPSILON = 1e-06
@@ -26,7 +25,7 @@
 
 
 def span_kernel(
-    held_count, nbr_count, parts, meta,
+    held_count, nbr_count, bounds, meta,
     q_ref, cot_ref, cond_ref, gain_ref, down_ref, up_ref, upt_ref, downt_ref, *rest,
 ):
     held_refs = rest[:held_count]
@@ -43,7 +42,8 @@
     scaling = HEAD ** (-0.5)
     live = meta[0] == 1
     lens, which, index = 1, 1 + per_device, 1 + 2 * per_device
-    piece = slot_len // parts
+    parts = len(bounds) - 1
+    cuts = [pl.ds(low, high - low) for low, high in zip(bounds, bounds[1:])]
     pairs = [pl.ds(i * 2 * HEAD, 2 * HEAD) for i in range(HEADS // 2)]
     value_pairs = [pl.ds(head_cols + i * 2 * HEAD, 2 * HEAD) for i in range(HEADS // 2)]
     lanes = [pl.ds(i * 2 * SPAN, 2 * SPAN) for i in range(HEADS // 2)]
@@ -67,7 +67,7 @@
                     part = b % parts
                     pltpu.make_async_copy(
                         held.at[meta[index + n]],
-                        raw_ref.at[n, pl.ds(part * piece, piece)],
+                        raw_ref.at[n, cuts[part]],
                         sems.at[n * parts + part],
                     ).start()
         kv_copy.start()
@@ -86,8 +86,8 @@
         for part in range(parts):
             item = step * group * nbr_count + n
             pltpu.make_async_copy(
-                held_refs[0].at[0],
-                raw_ref.at[item, pl.ds(part * piece, piece)],
+                held_refs[part].at[0],
+                raw_ref.at[item, cuts[part]],
                 sems.at[item * parts + part],
             ).wait()
     x_full = jnp.concatenate(
@@ -177,10 +177,11 @@
         ad_ref[...] = jnp.where(live, acc_ref[...], 0.0).astype(ad_ref.dtype)
 
 
-def run_spans(meta, query, cot, cond, held, parts, gain, w_down, w_up, w_kv, w_kv_t, nbr_count):
+def run_spans(meta, query, cot, cond, held, bounds, gain, w_down, w_up, w_kv, w_kv_t, nbr_count):
     span_count, width = cond.shape
     token_count, head_cols = query.shape
-    slot_len = held[0].shape[1] * parts
+    slot_len = bounds[-1]
+    parts = len(bounds) - 1
     rank = w_down.shape[1]
     whole = lambda a: pl.BlockSpec(a.shape, lambda s, m: (0,) * a.ndim, pipeline_mode=pl.Buffered(1))
     group = GROUP if span_count % GROUP == 0 else 1
@@ -193,7 +194,7 @@
     lanes = SPAN * HEADS
     flops = 2 * rows * (2 * width * 2 * head_cols + 6 * width * rank + 6 * SPAN * head_cols)
     return pl.pallas_call(
-        functools.partial(span_kernel, len(held), nbr_count, parts),
+        functools.partial(span_kernel, len(held), nbr_count, bounds),
         grid_spec=pltpu.PrefetchScalarGridSpec(
             num_scalar_prefetch=1,
             grid=(span_count // group,),
@@ -341,10 +342,11 @@
             array, axes, [(a * columns + j, b * columns + j) for a, b in pairs for j in range(columns)]
         )
 
-    parts = PARTS if slot_len % (PARTS * 16) == 0 else 1
-    piece = slot_len // parts
+    first = slot_len // 16 * 3 // 4 * 16
+    bounds = [0, first, slot_len] if 0 < first < slot_len else [0, slot_len]
+    parts = len(bounds) - 1
     full_store = database.reshape(block_count, slot_len, width)
-    cut = lambda i: full_store[:, i * piece : (i + 1) * piece]
+    cut = lambda i: full_store[:, bounds[i] : bounds[i + 1]]
     store = [cut(0)]
 
     def to_all(array, axis):
@@ -385,15 +387,16 @@
     held = []
     weight, weight_t = w_kv, None
     for i in range(parts):
-        if i == 1:
-            weight_t, across[i] = lax.optimization_barrier((weight.T, across[i]))
         near = jnp.where(row == relay_row, store[i], across[i])
         stores = [near]
         held_by = jnp.where(row % half == half - 1, 0, 1)
         for step in range(1, half):
             stores.append(hop(near, [(p, p - step) for p in (relay_row, relay_row - half)]))
             held_by = jnp.where(row % half == half - 1 - step, step, held_by)
-        sends = pick(held_by, slot_block, stores)
+        wanted = slot_block
+        if i == 1:
+            weight_t, wanted = lax.optimization_barrier((weight.T, wanted))
+        sends = pick(held_by, wanted, stores)
         if i == 0:
             weight, sends = lax.optimization_barrier((weight, sends))
         arrived = lax.all_to_all(sends, "dp", split_axis=0, concat_axis=0, tiled=True)
@@ -426,7 +429,7 @@
         cotangent.reshape(token_count, head_cols),
         cond.reshape(span_count, width).astype(jnp.float32),
         held,
-        parts,
+        bounds,
         gain,
         w_down,
         w_up,

time: 138 us -> 132 us (0.957)
  waiting for transfers between devices: 51.5 us -> 38.8 us
  starting transfers between devices: 29.5 us -> 37.1 us
    all_to_all x2, waiting for transfers between devices: 15.5 us -> 4.4 us  [body(): lax.all_to_all(sends, 'dp', split_axis=0, concat_axis=0, tiled=True)]
    ppermute x10, starting transfers between devices: 6.99 us -> 13.8 us  [hop(): lax.ppermute(array, axes, [(a * columns + j, b * columns + j) for a, b in...]
    all_to_all x1, waiting for transfers between devices: 6.98 us -> 13.6 us  [to_all(): return lax.all_to_all(copies, axis, split_axis=0, concat_axis=0, tiled=True)]
    ppermute x10, waiting for transfers between devices: 11.3 us -> 6.92 us  [hop(): lax.ppermute(array, axes, [(a * columns + j, b * columns + j) for a, b in...]
    ppermute x5, starting transfers between devices: 2.45 us -> 6.54 us  [scatter_sum(): lax.ppermute(give.astype(jnp.bfloat16), axis, [(i, i ^ bit) for i in rang...]
    ppermute x5, waiting for transfers between devices: 17.7 us -> 13.9 us  [scatter_sum(): lax.ppermute(give.astype(jnp.bfloat16), axis, [(i, i ^ bit) for i in rang...]
    all_to_all x2, starting transfers between devices: 11.8 us -> 8.48 us  [body(): lax.all_to_all(sends, 'dp', split_axis=0, concat_axis=0, tiled=True)]
    unnamed x34 -> x32, local copies, waits for them, and re-layouts: 3.54 us -> 3 us
  transfers between devices with their start and end apart: 18 -> 18, of which waited for: 11 -> 12; matrix products, arithmetic and copies ran while one was open for 12% -> 13% of each run, Pallas kernels for 3% -> 2%
where the time goes in v12:
time: 132 us; the launch traced here: 131 us
  waiting for transfers between devices  38.8 us (29%)
  starting transfers between devices  37.1 us (28%)
  Pallas kernels  30.3 us (23%)
  local copies, waits for them, and re-layouts  15.6 us (12%)
  other arithmetic  8.24 us (6%)
    pallas_call x1, Pallas kernels, run_spans(): pl.pallas_call(functools.partial(span_kernel, len(held), nbr_count, bound...  26.2 us
    ppermute x5, waiting for transfers between devices, scatter_sum(): lax.ppermute(give.astype(jnp.bfloat16), axis, [(i, i ^ bit) for i in rang...  13.9 us
    ppermute x10, starting transfers between devices, hop(): lax.ppermute(array, axes, [(a * columns + j, b * columns + j) for a, b in...  13.8 us
    all_to_all x1, waiting for transfers between devices, to_all(): return lax.all_to_all(copies, axis, split_axis=0, concat_axis=0, tiled=True)  13.6 us
    all_to_all x2, starting transfers between devices, body(): lax.all_to_all(sends, 'dp', split_axis=0, concat_axis=0, tiled=True)  8.48 us
    all_to_all x1, starting transfers between devices, to_all(): return lax.all_to_all(copies, axis, split_axis=0, concat_axis=0, tiled=True)  8.23 us
    ppermute x10, waiting for transfers between devices, hop(): lax.ppermute(array, axes, [(a * columns + j, b * columns + j) for a, b in...  6.92 us
    ppermute x5, starting transfers between devices, scatter_sum(): lax.ppermute(give.astype(jnp.bfloat16), axis, [(i, i ^ bit) for i in rang...  6.54 us
  transfers between devices with their start and end apart: 18, of which 12 were waited for; matrix products, arithmetic and copies ran while one was open for 13% of the time, Pallas kernels for 2%

profile of v12, /device:TPU:0, one launch (start us, length us, event | category | flops | bytes accessed | tf_op | source)
XLA Modules:
  0.0 131.0 jit_solution(12647762177758257840)
XLA Ops:
  0.7 1.6 %slice.28 = bf16[16,96,512]{2,1,0:T(8,128)(2,1)S(1)} slice(bf16[16,128,512]{2,1,0:T(8,128)(2,1)} %bitcast.57), slice={[0:16], [0:96], [0:512]} | slice | bytes 3145728 | tf_op jit(solution)/shard_map/slice | solution.py:349
  2.2 0.8 collective-permute-start
  3.5 0.6 broadcast_in_dim.87
  4.1 8.2 %all-to-all-start = ((s32[32,1,128]{2,1,0:T(1,128)}), s32[32,1,128]{2,1,0:T(1,128)S(1)}, u32[]{:S(2)}, u32[]{:S(2)}) async-start(s32[32,1,128]{2,1,0:T(1,128)} %broadcast_in_dim.87), calls=%async_computation | async-start | bytes 32768 | tf_op jit(solution)/shard_map/all_to_all | solution.py:354
  12.4 13.6 %all-to-all-done = s32[32,1,128]{2,1,0:T(1,128)S(1)} async-done(((s32[32,1,128]{2,1,0:T(1,128)}), s32[32,1,128]{2,1,0:T(1,128)S(1)}, u32[]{:S(2)}, u32[]{:S(2)}) %all-to-all-start) | async-done | bytes 16416 | tf_op jit(solution)/shard_map/all_to_all | solution.py:354
  26.0 1.6 %broadcast_select_fusion.refs_0_ = bf16[16,96,512]{2,1,0:T(8,128)(2,1)S(1)} fusion(bf16[16,96,512]{2,1,0:T(8,128)(2,1)S(1)} %collective-permute-done, pred[]{:T(512)S(6)} %eq.148, bf16[16,128,512]{2,1,0:T(8,128)(2,1)} %bitcast.58), kind=kLoop, calls=%fused_computation | loop fusion | flops 786432 | bytes 4718593 | tf_op jit(solution)/shard_map/jit(_where)/select_n | solution.py:390
  27.5 1.3 collective-permute-start.1
  29.4 0.6 convert_reduce_fusion
  30.4 2.4 %collective-permute-done.1.refs_1_ = bf16[16,96,512]{2,1,0:T(8,128)(2,1)S(1)} collective-permute-done((bf16[16,96,512]{2,1,0:T(8,128)(2,1)S(1)}, bf16[16,96,512]{2,1,0:T(8,128)(2,1)S(1)}, u32[]{:S(2)}, u32[]{:S(2)}) %collective-permute-start.1) | collective-permute-done | bytes 1572896 | tf_op jit(solution)/shard_map/ppermute | solution.py:341
  32.8 1.5 %shard_map.138 = bf16[8,96,512]{2,1,0:T(8,128)(2,1)} custom-call(s32[9]{0:T(128)S(1)} %pad_add_fusion.2.meta, bf16[16,96,512]{2,1,0:T(8,128)(2,1)S(1)} %broadcast_select_fusion.refs_0_, bf16[16,96,512]{2,1,0:T(8,128)(2,1)S(1)} %collective-permute-done.1.refs_1_), custom_call_target="tpu_custom_call" | custom-call | tf_op jit(solution)/shard_map/pallas_call | solution.py:252
  34.3 4.9 %all-to-all-start.1 = ((bf16[8,96,512]{2,1,0:T(8,128)(2,1)}), bf16[8,96,512]{2,1,0:T(8,128)(2,1)S(1)}, u32[]{:S(2)}, u32[]{:S(2)}) async-start(bf16[8,96,512]{2,1,0:T(8,128)(2,1)} %shard_map.138), calls=%async_computation.1 | async-start | bytes 1572864 | tf_op jit(solution)/shard_map/all_to_all | solution.py:402
  39.2 1.1 slice.27
  40.3 0.7 collective-permute-start.2
  41.1 1.1 broadcast_select_fusion.1.refs_0_
  42.3 1.3 collective-permute-start.3
  43.6 0.5 broadcast.445
  44.1 0.7 fusion.35
  45.0 6.5 %copy.67 = bf16[512,4096]{0,1:T(8,128)(2,1)} copy(bf16[512,4096]{1,0:T(8,128)(2,1)} %rest_8_.1) | data formatting | bytes 8388608 | tf_op jit(solution)/shard_map/optimization_barrier | solution.py:401
  51.6 2.6 %collective-permute-done.3.refs_1_ = bf16[16,32,512]{2,1,0:T(8,128)(2,1)S(1)} collective-permute-done((bf16[16,32,512]{2,1,0:T(8,128)(2,1)S(1)}, bf16[16,32,512]{2,1,0:T(8,128)(2,1)S(1)}, u32[]{:S(2)}, u32[]{:S(2)}) %collective-permute-start.3) | collective-permute-done | bytes 524320 | tf_op jit(solution)/shard_map/ppermute | solution.py:341
  54.2 1.3 shard_map.139
  55.5 4.2 %all-to-all-done.1.refs_0_.rest_0_ = bf16[8,96,512]{2,1,0:T(8,128)(2,1)S(1)} async-done(((bf16[8,96,512]{2,1,0:T(8,128)(2,1)}), bf16[8,96,512]{2,1,0:T(8,128)(2,1)S(1)}, u32[]{:S(2)}, u32[]{:S(2)}) %all-to-all-start.1) | async-done | bytes 786464 | tf_op jit(solution)/shard_map/all_to_all | solution.py:402
  59.7 3.6 %all-to-all-start.2 = ((bf16[8,32,512]{2,1,0:T(8,128)(2,1)}), bf16[8,32,512]{2,1,0:T(8,128)(2,1)S(1)}, u32[]{:S(2)}, u32[]{:S(2)}) async-start(bf16[8,32,512]{2,1,0:T(8,128)(2,1)} %shard_map.139), calls=%async_computation.2 | async-start | bytes 524288 | tf_op jit(solution)/shard_map/all_to_all | solution.py:402
  63.3 0.6 shard_map.140
  63.9 0.6 bitcast_convert_fusion.1.cond_ref
  64.5 0.8 copy.61
  65.4 0.9 copy.62
  66.4 4.3 %collective-permute-start.4 = (bf16[8,96,512]{2,1,0:T(8,128)(2,1)S(1)}, bf16[8,96,512]{2,1,0:T(8,128)(2,1)S(1)}, u32[]{:S(2)}, u32[]{:S(2)}) collective-permute-start(bf16[8,96,512]{2,1,0:T(8,128)(2,1)S(1)} %all-to-all-done.1.refs_0_.rest_0_), channel_id=1, source_target_pairs={{0,8},{1,9},{2,10},{3,11},{4,12},{5,13},{6,14},{7,15},{8,0},{9,1},... | collective-permute-start | bytes 2359304 | tf_op jit(solution)/shard_map/ppermute | solution.py:341
  71.5 0.7 shard_map.141
  72.3 1.6 %collective-permute-start.7 = (bf16[4,32,512]{2,1,0:T(8,128)(2,1)S(1)}, bf16[4,32,512]{2,1,0:T(8,128)(2,1)S(1)}, u32[]{:S(2)}, u32[]{:S(2)}) collective-permute-start(bf16[4,32,512]{2,1,0:T(8,128)(2,1)S(1)} %shard_map.141), channel_id=1, source_target_pairs={{0,16},{1,17},{2,18},{3,19},{4,20},{5,21},{6,22},{7,23},{8,24},{9,... | collective-permute-start | bytes 393224 | tf_op jit(solution)/shard_map/ppermute | solution.py:341
  73.9 1.8 %collective-permute-start.8 = (bf16[4,96,512]{2,1,0:T(8,128)(2,1)S(1)}, bf16[4,96,512]{2,1,0:T(8,128)(2,1)S(1)}, u32[]{:S(2)}, u32[]{:S(2)}) collective-permute-start(bf16[4,96,512]{2,1,0:T(8,128)(2,1)S(1)} %collective-permute-done.6.rest_4_), channel_id=1, source_target_pairs={{0,8},{1,9},{2,10},{3,11},{4,12},{5,13},{6,14},{7,15},{8,0},{9,1},... | collective-permute-start | bytes 1179656 | tf_op jit(solution)/shard_map/ppermute | solution.py:341
  75.8 1.5 %collective-permute-done.7.rest_5_ = bf16[4,32,512]{2,1,0:T(8,128)(2,1)S(1)} collective-permute-done((bf16[4,32,512]{2,1,0:T(8,128)(2,1)S(1)}, bf16[4,32,512]{2,1,0:T(8,128)(2,1)S(1)}, u32[]{:S(2)}, u32[]{:S(2)}) %collective-permute-start.7) | collective-permute-done | bytes 131104 | tf_op jit(solution)/shard_map/ppermute | solution.py:341
  77.3 1.9 %collective-permute-start.9 = (bf16[4,32,512]{2,1,0:T(8,128)(2,1)S(1)}, bf16[4,32,512]{2,1,0:T(8,128)(2,1)S(1)}, u32[]{:S(2)}, u32[]{:S(2)}) collective-permute-start(bf16[4,32,512]{2,1,0:T(8,128)(2,1)S(1)} %collective-permute-done.7.rest_5_), channel_id=1, source_target_pairs={{0,8},{1,9},{2,10},{3,11},{4,12},{5,13},{6,14},{7,15},{8,0},{9,1},... | collective-permute-start | bytes 393224 | tf_op jit(solution)/shard_map/ppermute | solution.py:341
  79.2 0.6 pad_add_fusion.1.meta
  80.3 0.6 copy-done.13
  81.4 26.2 %shard_map.142 = (bf16[256,2048]{1,0:T(8,128)(2,1)}, bf16[256,2048]{1,0:T(8,128)(2,1)}, f32[4,512]{1,0:T(4,128)}, f32[512,512]{1,0:T(8,128)}) custom-call(s32[25]{0:T(128)} %pad_add_fusion.1.meta, bf16[256,2048]{1,0:T(8,128)(2,1)} %bitcast.75, bf16[256,2048]{1,0:T(8,128)(2,1)} %bitcast.76, f32[4,512]{1,0:T(4,128)} %bitcast_convert_fusion.1.cond_ref, ...), custom_call_target="tpu_custom_call" | custom-call | flops 11811160064 | bytes 16777216 | tf_op jit(solution)/shard_map/pallas_call | solution.py:196
  107.6 1.1 fusion
  108.7 0.4 collective-permute-start.10
  109.1 1.2 collective-permute-done.10
  110.3 1.1 bitcast_add_fusion
  111.4 0.9 collective-permute-start.11
  112.4 4.9 %collective-permute-done.11 = bf16[1,8,16,512]{3,2,1,0:T(8,128)(2,1)S(1)} collective-permute-done((bf16[1,8,16,512]{3,2,1,0:T(8,128)(2,1)S(1)}, bf16[1,8,16,512]{3,2,1,0:T(8,128)(2,1)S(1)}, u32[]{:S(2)}, u32[]{:S(2)}) %collective-permute-start.11) | collective-permute-done | bytes 131104 | tf_op jit(solution)/shard_map/ppermute | solution.py:306
  117.3 1.4 %collective-permute-start.12 = (bf16[1,4,16,512]{3,2,1,0:T(8,128)(2,1)S(1)}, bf16[1,4,16,512]{3,2,1,0:T(8,128)(2,1)S(1)}, u32[]{:S(2)}, u32[]{:S(2)}) collective-permute-start(bf16[1,4,16,512]{3,2,1,0:T(8,128)(2,1)S(1)} %fusion.2), channel_id=1, source_target_pairs={{0,1},{1,0},{2,3},{3,2},{4,5},{5,4},{6,7},{7,6},{8,9},{9,8},{10,11... | collective-permute-start | bytes 196616 | tf_op jit(solution)/shard_map/ppermute | solution.py:306
  118.7 3.0 %collective-permute-done.12 = bf16[1,4,16,512]{3,2,1,0:T(8,128)(2,1)S(1)} collective-permute-done((bf16[1,4,16,512]{3,2,1,0:T(8,128)(2,1)S(1)}, bf16[1,4,16,512]{3,2,1,0:T(8,128)(2,1)S(1)}, u32[]{:S(2)}, u32[]{:S(2)}) %collective-permute-start.12) | collective-permute-done | bytes 65568 | tf_op jit(solution)/shard_map/ppermute | solution.py:306
  121.7 1.4 %collective-permute-start.13 = (bf16[1,2,16,512]{3,2,1,0:T(8,128)(2,1)S(1)}, bf16[1,2,16,512]{3,2,1,0:T(8,128)(2,1)S(1)}, u32[]{:S(2)}, u32[]{:S(2)}) collective-permute-start(bf16[1,2,16,512]{3,2,1,0:T(8,128)(2,1)S(1)} %fusion.3), channel_id=1, source_target_pairs={{0,2},{1,3},{2,0},{3,1},{4,6},{5,7},{6,4},{7,5},{8,10},{9,11},{10,... | collective-permute-start | bytes 98312 | tf_op jit(solution)/shard_map/ppermute | solution.py:306
  123.1 2.6 %collective-permute-done.13 = bf16[1,2,16,512]{3,2,1,0:T(8,128)(2,1)S(1)} collective-permute-done((bf16[1,2,16,512]{3,2,1,0:T(8,128)(2,1)S(1)}, bf16[1,2,16,512]{3,2,1,0:T(8,128)(2,1)S(1)}, u32[]{:S(2)}, u32[]{:S(2)}) %collective-permute-start.13) | collective-permute-done | bytes 32800 | tf_op jit(solution)/shard_map/ppermute | solution.py:306
  125.7 2.4 %collective-permute-start.14 = (bf16[1,1,16,512]{3,2,1,0:T(8,128)(2,1)S(1)}, bf16[1,1,16,512]{3,2,1,0:T(8,128)(2,1)S(1)}, u32[]{:S(2)}, u32[]{:S(2)}) collective-permute-start(bf16[1,1,16,512]{3,2,1,0:T(8,128)(2,1)S(1)} %dynamic-slice_convert_fusion.3), channel_id=1, source_target_pairs={{0,4},{1,5},{2,6},{3,7},{4,0},{5,1},{6,2},{7,3},{8,12},{9,13},{10,... | collective-permute-start | bytes 49160 | tf_op jit(solution)/shard_map/ppermute | solution.py:306
  128.2 2.3 %collective-permute-done.14 = bf16[1,1,16,512]{3,2,1,0:T(8,128)(2,1)S(1)} collective-permute-done((bf16[1,1,16,512]{3,2,1,0:T(8,128)(2,1)S(1)}, bf16[1,1,16,512]{3,2,1,0:T(8,128)(2,1)S(1)}, u32[]{:S(2)}, u32[]{:S(2)}) %collective-permute-start.14) | collective-permute-done | bytes 16416 | tf_op jit(solution)/shard_map/ppermute | solution.py:306
  130.4 0.6 add_bitcast_fusion
  (86 shorter events, 4.1 us)
Async XLA Ops:
  0.6 2.4 %copy-start.5 = (s32[1,1,4,2]{2,3,1,0:T(2,128)S(1)}, s32[1,1,4,2]{2,3,1,0:T(2,128)}, u32[]{:S(2)}) copy-start(s32[1,1,4,2]{2,3,1,0:T(2,128)} %param.14) | copy-start | bytes 100
  0.6 2.6 %copy-start.6 = (s32[1,1,4,2]{2,3,1,0:T(2,128)S(1)}, s32[1,1,4,2]{2,3,1,0:T(2,128)}, u32[]{:S(2)}) copy-start(s32[1,1,4,2]{2,3,1,0:T(2,128)} %param.15) | copy-start | bytes 100
  0.7 2.7 %copy-start.7 = (s32[1,1,16]{2,1,0:T(1,128)S(1)}, s32[1,1,16]{2,1,0:T(1,128)}, u32[]{:S(2)}) copy-start(s32[1,1,16]{2,1,0:T(1,128)} %param.17) | copy-start | bytes 196
  2.2 23.7 %collective-permute-start = (bf16[16,96,512]{2,1,0:T(8,128)(2,1)S(1)}, bf16[16,96,512]{2,1,0:T(8,128)(2,1)S(1)}, u32[]{:S(2)}, u32[]{:S(2)}) collective-permute-start(bf16[16,96,512]{2,1,0:T(8,128)(2,1)S(1)} %slice.28), channel_id=1, source_target_pairs={{24,8},{25,9},{26,10},{27,11},{28,12},{29,13},{30,14},{31,15}} | collective-permute-start | bytes 4718600 | tf_op jit(solution)/shard_map/ppermute | solution.py:341
  4.1 21.9 %all-to-all-start = ((s32[32,1,128]{2,1,0:T(1,128)}), s32[32,1,128]{2,1,0:T(1,128)S(1)}, u32[]{:S(2)}, u32[]{:S(2)}) async-start(s32[32,1,128]{2,1,0:T(1,128)} %broadcast_in_dim.87), calls=%async_computation | async-start | bytes 32768 | tf_op jit(solution)/shard_map/all_to_all | solution.py:354
  27.5 5.3 %collective-permute-start.1 = (bf16[16,96,512]{2,1,0:T(8,128)(2,1)S(1)}, bf16[16,96,512]{2,1,0:T(8,128)(2,1)S(1)}, u32[]{:S(2)}, u32[]{:S(2)}) collective-permute-start(bf16[16,96,512]{2,1,0:T(8,128)(2,1)S(1)} %broadcast_select_fusion.refs_0_), channel_id=1, source_target_pairs={{24,16},{25,17},{26,18},{27,19},{28,20},{29,21},{30,22},{31,23},{8... | collective-permute-start | bytes 4718600 | tf_op jit(solution)/shard_map/ppermute | solution.py:341
  34.3 25.3 %all-to-all-start.1 = ((bf16[8,96,512]{2,1,0:T(8,128)(2,1)}), bf16[8,96,512]{2,1,0:T(8,128)(2,1)S(1)}, u32[]{:S(2)}, u32[]{:S(2)}) async-start(bf16[8,96,512]{2,1,0:T(8,128)(2,1)} %shard_map.138), calls=%async_computation.1 | async-start | bytes 1572864 | tf_op jit(solution)/shard_map/all_to_all | solution.py:402
  40.3 0.8 collective-permute-start.2
  42.3 11.9 %collective-permute-start.3 = (bf16[16,32,512]{2,1,0:T(8,128)(2,1)S(1)}, bf16[16,32,512]{2,1,0:T(8,128)(2,1)S(1)}, u32[]{:S(2)}, u32[]{:S(2)}) collective-permute-start(bf16[16,32,512]{2,1,0:T(8,128)(2,1)S(1)} %broadcast_select_fusion.1.refs_0_), channel_id=1, source_target_pairs={{24,16},{25,17},{26,18},{27,19},{28,20},{29,21},{30,22},{31,23},{8... | collective-permute-start | bytes 1572872 | tf_op jit(solution)/shard_map/ppermute | solution.py:341
  51.5 12.4 %copy-start.4 = (bf16[1,1,4,512]{3,2,1,0:T(4,128)(2,1)S(1)}, bf16[1,1,4,512]{3,2,1,0:T(4,128)(2,1)}, u32[]{:S(2)}) copy-start(bf16[1,1,4,512]{3,2,1,0:T(4,128)(2,1)} %param.13) | copy-start | bytes 12292
  51.5 13.1 %copy-start.3 = (bf16[256,512]{1,0:T(8,128)(2,1)S(1)}, bf16[256,512]{1,0:T(8,128)(2,1)}, u32[]{:S(2)}) copy-start(bf16[256,512]{1,0:T(8,128)(2,1)} %up_ref.1) | copy-start | bytes 786436
  51.5 13.8 %copy-start.2 = (bf16[512,256]{1,0:T(8,128)(2,1)S(1)}, bf16[512,256]{1,0:T(8,128)(2,1)}, u32[]{:S(2)}) copy-start(bf16[512,256]{1,0:T(8,128)(2,1)} %down_ref.1) | copy-start | bytes 786436
  59.7 12.6 %copy-start = (bf16[8,96,512]{2,1,0:T(8,128)(2,1)}, bf16[8,96,512]{2,1,0:T(8,128)(2,1)S(1)}, u32[]{:S(2)}) copy-start(bf16[8,96,512]{2,1,0:T(8,128)(2,1)S(1)} %all-to-all-done.1.refs_0_.rest_0_) | copy-start | bytes 2359300
  59.7 11.8 %all-to-all-start.2 = ((bf16[8,32,512]{2,1,0:T(8,128)(2,1)}), bf16[8,32,512]{2,1,0:T(8,128)(2,1)S(1)}, u32[]{:S(2)}, u32[]{:S(2)}) async-start(bf16[8,32,512]{2,1,0:T(8,128)(2,1)} %shard_map.139), calls=%async_computation.2 | async-start | bytes 524288 | tf_op jit(solution)/shard_map/all_to_all | solution.py:402
  63.8 10.0 %collective-permute-start.6 = (bf16[4,96,512]{2,1,0:T(8,128)(2,1)S(1)}, bf16[4,96,512]{2,1,0:T(8,128)(2,1)S(1)}, u32[]{:S(2)}, u32[]{:S(2)}) collective-permute-start(bf16[4,96,512]{2,1,0:T(8,128)(2,1)S(1)} %shard_map.140), channel_id=1, source_target_pairs={{0,16},{1,17},{2,18},{3,19},{4,20},{5,21},{6,22},{7,23},{8,24},{9,... | collective-permute-start | bytes 1179656 | tf_op jit(solution)/shard_map/ppermute | solution.py:341
  66.4 13.8 %collective-permute-start.4 = (bf16[8,96,512]{2,1,0:T(8,128)(2,1)S(1)}, bf16[8,96,512]{2,1,0:T(8,128)(2,1)S(1)}, u32[]{:S(2)}, u32[]{:S(2)}) collective-permute-start(bf16[8,96,512]{2,1,0:T(8,128)(2,1)S(1)} %all-to-all-done.1.refs_0_.rest_0_), channel_id=1, source_target_pairs={{0,8},{1,9},{2,10},{3,11},{4,12},{5,13},{6,14},{7,15},{8,0},{9,1},... | collective-permute-start | bytes 2359304 | tf_op jit(solution)/shard_map/ppermute | solution.py:341
  71.5 8.8 %copy-start.1 = (bf16[8,32,512]{2,1,0:T(8,128)(2,1)}, bf16[8,32,512]{2,1,0:T(8,128)(2,1)S(1)}, u32[]{:S(2)}) copy-start(bf16[8,32,512]{2,1,0:T(8,128)(2,1)S(1)} %all-to-all-done.2.refs_0_.rest_1_) | copy-start | bytes 786436
  72.3 5.0 %collective-permute-start.7 = (bf16[4,32,512]{2,1,0:T(8,128)(2,1)S(1)}, bf16[4,32,512]{2,1,0:T(8,128)(2,1)S(1)}, u32[]{:S(2)}, u32[]{:S(2)}) collective-permute-start(bf16[4,32,512]{2,1,0:T(8,128)(2,1)S(1)} %shard_map.141), channel_id=1, source_target_pairs={{0,16},{1,17},{2,18},{3,19},{4,20},{5,21},{6,22},{7,23},{8,24},{9,... | collective-permute-start | bytes 393224 | tf_op jit(solution)/shard_map/ppermute | solution.py:341
  73.9 6.4 %copy-start.9 = (bf16[4,96,512]{2,1,0:T(8,128)(2,1)}, bf16[4,96,512]{2,1,0:T(8,128)(2,1)S(1)}, u32[]{:S(2)}) copy-start(bf16[4,96,512]{2,1,0:T(8,128)(2,1)S(1)} %collective-permute-done.6.rest_4_) | copy-start | bytes 1179652
  73.9 6.4 %collective-permute-start.8 = (bf16[4,96,512]{2,1,0:T(8,128)(2,1)S(1)}, bf16[4,96,512]{2,1,0:T(8,128)(2,1)S(1)}, u32[]{:S(2)}, u32[]{:S(2)}) collective-permute-start(bf16[4,96,512]{2,1,0:T(8,128)(2,1)S(1)} %collective-permute-done.6.rest_4_), channel_id=1, source_target_pairs={{0,8},{1,9},{2,10},{3,11},{4,12},{5,13},{6,14},{7,15},{8,0},{9,1},... | collective-permute-start | bytes 1179656 | tf_op jit(solution)/shard_map/ppermute | solution.py:341
  75.7 4.5 %collective-permute-start.5 = (bf16[8,32,512]{2,1,0:T(8,128)(2,1)S(1)}, bf16[8,32,512]{2,1,0:T(8,128)(2,1)S(1)}, u32[]{:S(2)}, u32[]{:S(2)}) collective-permute-start(bf16[8,32,512]{2,1,0:T(8,128)(2,1)S(1)} %all-to-all-done.2.refs_0_.rest_1_), channel_id=1, source_target_pairs={{0,8},{1,9},{2,10},{3,11},{4,12},{5,13},{6,14},{7,15},{8,0},{9,1},... | collective-permute-start | bytes 786440 | tf_op jit(solution)/shard_map/ppermute | solution.py:341
  77.3 3.0 %copy-start.12 = (bf16[4,32,512]{2,1,0:T(8,128)(2,1)}, bf16[4,32,512]{2,1,0:T(8,128)(2,1)S(1)}, u32[]{:S(2)}) copy-start(bf16[4,32,512]{2,1,0:T(8,128)(2,1)S(1)} %collective-permute-done.7.rest_5_) | copy-start | bytes 393220
  77.3 2.9 %collective-permute-start.9 = (bf16[4,32,512]{2,1,0:T(8,128)(2,1)S(1)}, bf16[4,32,512]{2,1,0:T(8,128)(2,1)S(1)}, u32[]{:S(2)}, u32[]{:S(2)}) collective-permute-start(bf16[4,32,512]{2,1,0:T(8,128)(2,1)S(1)} %collective-permute-done.7.rest_5_), channel_id=1, source_target_pairs={{0,8},{1,9},{2,10},{3,11},{4,12},{5,13},{6,14},{7,15},{8,0},{9,1},... | collective-permute-start | bytes 393224 | tf_op jit(solution)/shard_map/ppermute | solution.py:341
  80.2 0.7 copy-start.13
  80.2 0.8 copy-start.11
  80.2 1.0 copy-start.8
  80.3 1.1 copy-start.10
  108.7 1.6 %collective-permute-start.10 = (bf16[2,8,16,512]{3,2,1,0:T(8,128)(2,1)S(1)}, bf16[2,8,16,512]{3,2,1,0:T(8,128)(2,1)S(1)}, u32[]{:S(2)}, u32[]{:S(2)}) collective-permute-start(bf16[2,8,16,512]{3,2,1,0:T(8,128)(2,1)S(1)} %fusion), channel_id=1, source_target_pairs={{0,8},{8,0},{16,24},{24,16},{1,9},{9,1},{17,25},{25,17},{2,10},{10... | collective-permute-start | bytes 786440 | tf_op jit(solution)/shard_map/ppermute | solution.py:306
  111.4 5.8 %collective-permute-start.11 = (bf16[1,8,16,512]{3,2,1,0:T(8,128)(2,1)S(1)}, bf16[1,8,16,512]{3,2,1,0:T(8,128)(2,1)S(1)}, u32[]{:S(2)}, u32[]{:S(2)}) collective-permute-start(bf16[1,8,16,512]{3,2,1,0:T(8,128)(2,1)S(1)} %dynamic-slice_convert_fusion), channel_id=1, source_target_pairs={{0,16},{8,24},{16,0},{24,8},{1,17},{9,25},{17,1},{25,9},{2,18},{10... | collective-permute-start | bytes 393224 | tf_op jit(solution)/shard_map/ppermute | solution.py:306
  117.3 4.3 %collective-permute-start.12 = (bf16[1,4,16,512]{3,2,1,0:T(8,128)(2,1)S(1)}, bf16[1,4,16,512]{3,2,1,0:T(8,128)(2,1)S(1)}, u32[]{:S(2)}, u32[]{:S(2)}) collective-permute-start(bf16[1,4,16,512]{3,2,1,0:T(8,128)(2,1)S(1)} %fusion.2), channel_id=1, source_target_pairs={{0,1},{1,0},{2,3},{3,2},{4,5},{5,4},{6,7},{7,6},{8,9},{9,8},{10,11... | collective-permute-start | bytes 196616 | tf_op jit(solution)/shard_map/ppermute | solution.py:306
  121.7 4.0 %collective-permute-start.13 = (bf16[1,2,16,512]{3,2,1,0:T(8,128)(2,1)S(1)}, bf16[1,2,16,512]{3,2,1,0:T(8,128)(2,1)S(1)}, u32[]{:S(2)}, u32[]{:S(2)}) collective-permute-start(bf16[1,2,16,512]{3,2,1,0:T(8,128)(2,1)S(1)} %fusion.3), channel_id=1, source_target_pairs={{0,2},{1,3},{2,0},{3,1},{4,6},{5,7},{6,4},{7,5},{8,10},{9,11},{10,... | collective-permute-start | bytes 98312 | tf_op jit(solution)/shard_map/ppermute | solution.py:306
  125.7 4.7 %collective-permute-start.14 = (bf16[1,1,16,512]{3,2,1,0:T(8,128)(2,1)S(1)}, bf16[1,1,16,512]{3,2,1,0:T(8,128)(2,1)S(1)}, u32[]{:S(2)}, u32[]{:S(2)}) collective-permute-start(bf16[1,1,16,512]{3,2,1,0:T(8,128)(2,1)S(1)} %dynamic-slice_convert_fusion.3), channel_id=1, source_target_pairs={{0,4},{1,5},{2,6},{3,7},{4,0},{5,1},{6,2},{7,3},{8,12},{9,13},{10,... | collective-permute-start | bytes 49160 | tf_op jit(solution)/shard_map/ppermute | solution.py:306

commit v13 on v12

--- a/solution.py
+++ b/solution.py
@@ -30,7 +30,7 @@
 ):
     held_refs = rest[:held_count]
     (kv_hbm, kvt_hbm, out_ref, qg_ref, cg_ref, ad_ref,
-     raw_ref, kv_ref, kvt_ref, proj_ref, grad_ref, score_ref, dprob_ref, prob_ref, dscore_ref,
+     raw_ref, kv_ref, kvt_ref, proj_ref, grad_ref, score_ref, dprob_ref,
      q2_ref, cot2_ref, acc_ref, sems, kv_sem) = rest[held_count:]
     step = pl.program_id(0)
     per_device, slot_len, width = raw_ref.shape
@@ -117,6 +117,9 @@
         score_ref[keys[g], lane] = dot(proj_ref[keys[g], cols], q2_ref[double[g], cols], NT)
         dprob_ref[keys[g], lane] = dot(proj_ref[keys[g], value_cols], cot2_ref[double[g], cols], NT)
 
+    def diagonal(both):
+        return jnp.concatenate([both[:SPAN, :HEAD], both[SPAN:, HEAD:]], axis=1)
+
     slot = lax.broadcasted_iota(jnp.int32, (key_count, 2 * SPAN), 0)
     for g in range(group):
         limit = jnp.zeros((key_count, 2 * SPAN), jnp.int32)
@@ -125,32 +128,23 @@
             item = (step * group + g) * nbr_count + n
             limit = jnp.where(here, n * slot_len + meta[lens + item], limit)
         usable = slot < limit
-        for lane in lanes:
+        for cols, value_cols, lane in zip(pairs, value_pairs, lanes):
             scores = jnp.where(usable, score_ref[keys[g], lane], FLOOR)
             row_max = jnp.max(scores, axis=0, keepdims=True)
             raised = jnp.exp2((scores - row_max) * (scaling * LOG2E))
             probs = raised * (1.0 / jnp.sum(raised, axis=0, keepdims=True))
             d_probs = dprob_ref[keys[g], lane]
             delta = jnp.sum(probs * d_probs, axis=0, keepdims=True)
-            prob_ref[keys[g], lane] = probs.astype(jnp.bfloat16)
-            dscore_ref[keys[g], lane] = (probs * (d_probs - delta) * scaling).astype(jnp.bfloat16)
-
-    for g, cols, value_cols, lane in spots:
-        grad_ref[keys[g], cols] = dot(
-            dscore_ref[keys[g], lane], q2_ref[double[g], cols]
-        ).astype(jnp.bfloat16)
-        grad_ref[keys[g], value_cols] = dot(
-            prob_ref[keys[g], lane], cot2_ref[double[g], cols]
-        ).astype(jnp.bfloat16)
-
-    def diagonal(both):
-        return jnp.concatenate([both[:SPAN, :HEAD], both[SPAN:, HEAD:]], axis=1)
-
-    for g, cols, value_cols, lane in spots:
-        out = diagonal(dot(prob_ref[keys[g], lane].T, proj_ref[keys[g], value_cols]))
-        grad = diagonal(dot(dscore_ref[keys[g], lane].T, proj_ref[keys[g], cols]))
-        out_ref[tokens[g], cols] = jnp.where(live, out, 0.0).astype(jnp.bfloat16)
-        qg_ref[tokens[g], cols] = jnp.where(live, grad, 0.0).astype(jnp.bfloat16)
+            probs_b = probs.astype(jnp.bfloat16)
+            d_scores = (probs * (d_probs - delta) * scaling).astype(jnp.bfloat16)
+            grad_ref[keys[g], cols] = dot(d_scores, q2_ref[double[g], cols]).astype(jnp.bfloat16)
+            grad_ref[keys[g], value_cols] = dot(probs_b, cot2_ref[double[g], cols]).astype(
+                jnp.bfloat16
+            )
+            out = diagonal(dot(probs_b.T, proj_ref[keys[g], value_cols]))
+            grad = diagonal(dot(d_scores.T, proj_ref[keys[g], cols]))
+            out_ref[tokens[g], cols] = jnp.where(live, out, 0.0).astype(jnp.bfloat16)
+            qg_ref[tokens[g], cols] = jnp.where(live, grad, 0.0).astype(jnp.bfloat16)
 
     @pl.when(step == 0)
     def _():
@@ -215,8 +209,6 @@
                 pltpu.VMEM((keys, 2 * head_cols), jnp.bfloat16),
                 pltpu.VMEM((keys, lanes), jnp.float32),
                 pltpu.VMEM((keys, lanes), jnp.float32),
-                pltpu.VMEM((keys, lanes), jnp.bfloat16),
-                pltpu.VMEM((keys, lanes), jnp.bfloat16),
                 pltpu.VMEM((group * 2 * SPAN, head_cols), jnp.bfloat16),
                 pltpu.VMEM((group * 2 * SPAN, head_cols), jnp.bfloat16),
                 pltpu.VMEM((width, 2 * rank), jnp.float32),
@@ -358,7 +350,10 @@
     over = lambda a: hop(a, [(relay_row, relay_row - half)])
     across = [over(store[0])]
     table = to_all(info.reshape(-1, 128), axes)
-    full_store, across, table = lax.optimization_barrier((full_store, across, table))
+    w_kv_t = w_kv.T
+    full_store, across, table, w_kv_t = lax.optimization_barrier(
+        (full_store, across, table, w_kv_t)
+    )
     store += [cut(i) for i in range(1, parts)]
     across += [over(a) for a in store[1:]]
     table = table.reshape(pool_count, columns, -1)
@@ -385,7 +380,6 @@
         return hop(array, [(p, p // half * half + (p + step) % half) for p in range(pool_count)])
 
     held = []
-    weight, weight_t = w_kv, None
     for i in range(parts):
         near = jnp.where(row == relay_row, store[i], across[i])
         stores = [near]
@@ -393,12 +387,7 @@
         for step in range(1, half):
             stores.append(hop(near, [(p, p - step) for p in (relay_row, relay_row - half)]))
             held_by = jnp.where(row % half == half - 1 - step, step, held_by)
-        wanted = slot_block
-        if i == 1:
-            weight_t, wanted = lax.optimization_barrier((weight.T, wanted))
-        sends = pick(held_by, wanted, stores)
-        if i == 0:
-            weight, sends = lax.optimization_barrier((weight, sends))
+        sends = pick(held_by, slot_block, stores)
         arrived = lax.all_to_all(sends, "dp", split_axis=0, concat_axis=0, tiled=True)
         here = [arrived] + [share(arrived, step) for step in range(1, half)]
         if crossing:
@@ -406,7 +395,6 @@
             landed = hop(leaving, [(p, (p + half) % pool_count) for p in range(pool_count)])
             here += [landed] + [share(landed, step) for step in range(1, half)]
         held.append(here)
-    weight_t = weight.T if weight_t is None else weight_t
     origin = jnp.where(my_cross, (my_carrier + half) % pool_count, my_carrier)
     which = (row - origin) % half + jnp.where(my_cross, half, 0)
     index = jnp.where(my_cross, my_number, place)
@@ -434,7 +422,7 @@
         w_down,
         w_up,
         w_kv,
-        weight_t,
+        w_kv_t,
         nbr_count,
     )
 

time: 132 us -> 129 us (0.977)
  starting transfers between devices: 37.1 us -> 26.6 us
  waiting for transfers between devices: 38.8 us -> 48.4 us
  Pallas kernels: 30.3 us -> 28.7 us
    ppermute x10, waiting for transfers between devices: 6.92 us -> 16.8 us  [hop(): lax.ppermute(array, axes, [(a * columns + j, b * columns + j) for a, b in...]
    ppermute x10, starting transfers between devices: 13.8 us -> 4.83 us  [hop(): lax.ppermute(array, axes, [(a * columns + j, b * columns + j) for a, b in...]
    unnamed x32 -> x31, local copies, waits for them, and re-layouts: 3 us -> 9.5 us
    optimization_barrier x1 -> x0, local copies, waits for them, and re-layouts: 6.49 us -> none  [body(): weight, sends = lax.optimization_barrier((weight, sends))]
    all_to_all x1, waiting for transfers between devices: 13.6 us -> 7.08 us  [to_all(): return lax.all_to_all(copies, axis, split_axis=0, concat_axis=0, tiled=True)]
    all_to_all x2, waiting for transfers between devices: 4.4 us -> 9.39 us  [body(): lax.all_to_all(sends, 'dp', split_axis=0, concat_axis=0, tiled=True)]
    pallas_call x1, Pallas kernels: 26.2 us -> 24.6 us  [run_spans(): pl.pallas_call(functools.partial(span_kernel, len(held), nbr_count, bound...]
    ppermute x5, starting transfers between devices: 6.54 us -> 5.09 us  [scatter_sum(): lax.ppermute(give.astype(jnp.bfloat16), axis, [(i, i ^ bit) for i in rang...]
  transfers between devices with their start and end apart: 18 -> 18, of which waited for: 12 -> 13; matrix products, arithmetic and copies ran while one was open for 13% -> 13% of each run, Pallas kernels for 2% -> 2%
where the time goes in v13:
time: 129 us
  waiting for transfers between devices  48.4 us (38%)
  Pallas kernels  28.7 us (22%)
  starting transfers between devices  26.6 us (21%)
  local copies, waits for them, and re-layouts  15.7 us (12%)
  other arithmetic  8.1 us (6%)
    pallas_call x1, Pallas kernels, run_spans(): pl.pallas_call(functools.partial(span_kernel, len(held), nbr_count, bound...  24.6 us
    ppermute x10, waiting for transfers between devices, hop(): lax.ppermute(array, axes, [(a * columns + j, b * columns + j) for a, b in...  16.8 us
    ppermute x5, waiting for transfers between devices, scatter_sum(): lax.ppermute(give.astype(jnp.bfloat16), axis, [(i, i ^ bit) for i in rang...  15.1 us
    unnamed x31, local copies, waits for them, and re-layouts  9.5 us
    all_to_all x2, waiting for transfers between devices, body(): lax.all_to_all(sends, 'dp', split_axis=0, concat_axis=0, tiled=True)  9.39 us
    all_to_all x2, starting transfers between devices, body(): lax.all_to_all(sends, 'dp', split_axis=0, concat_axis=0, tiled=True)  8.48 us
    all_to_all x1, starting transfers between devices, to_all(): return lax.all_to_all(copies, axis, split_axis=0, concat_axis=0, tiled=True)  8.23 us
    all_to_all x1, waiting for transfers between devices, to_all(): return lax.all_to_all(copies, axis, split_axis=0, concat_axis=0, tiled=True)  7.08 us
  transfers between devices with their start and end apart: 18, of which 13 were waited for; matrix products, arithmetic and copies ran while one was open for 13% of the time, Pallas kernels for 2%

profile of v13, /device:TPU:0, one launch (start us, length us, event | category | flops | bytes accessed | tf_op | source)
XLA Modules:
  0.0 128.5 jit_solution(7734985561930765569)
XLA Ops:
  0.7 1.6 %slice.28 = bf16[16,96,512]{2,1,0:T(8,128)(2,1)S(1)} slice(bf16[16,128,512]{2,1,0:T(8,128)(2,1)} %bitcast.57), slice={[0:16], [0:96], [0:512]} | slice | bytes 3145728 | tf_op jit(solution)/shard_map/slice | solution.py:341
  2.2 0.8 collective-permute-start
  3.5 0.6 broadcast_in_dim.87
  4.1 8.2 %all-to-all-start = ((s32[32,1,128]{2,1,0:T(1,128)}), s32[32,1,128]{2,1,0:T(1,128)S(1)}, u32[]{:S(2)}, u32[]{:S(2)}) async-start(s32[32,1,128]{2,1,0:T(1,128)} %broadcast_in_dim.87), calls=%async_computation | async-start | bytes 32768 | tf_op jit(solution)/shard_map/all_to_all | solution.py:346
  12.4 6.5 %copy.58 = bf16[512,4096]{0,1:T(8,128)(2,1)} copy(bf16[512,4096]{1,0:T(8,128)(2,1)} %rest_8_.1) | data formatting | bytes 8388608 | tf_op args[10]
  18.9 7.1 %all-to-all-done = s32[32,1,128]{2,1,0:T(1,128)S(1)} async-done(((s32[32,1,128]{2,1,0:T(1,128)}), s32[32,1,128]{2,1,0:T(1,128)S(1)}, u32[]{:S(2)}, u32[]{:S(2)}) %all-to-all-start) | async-done | bytes 16416 | tf_op jit(solution)/shard_map/all_to_all | solution.py:346
  26.0 1.6 %broadcast_select_fusion.refs_0_ = bf16[16,96,512]{2,1,0:T(8,128)(2,1)S(1)} fusion(bf16[16,96,512]{2,1,0:T(8,128)(2,1)S(1)} %collective-permute-done, pred[]{:T(512)S(6)} %eq.148, bf16[16,128,512]{2,1,0:T(8,128)(2,1)} %bitcast.58), kind=kLoop, calls=%fused_computation | loop fusion | flops 786432 | bytes 4718593 | tf_op jit(solution)/shard_map/jit(_where)/select_n | solution.py:384
  27.5 1.3 %collective-permute-start.1 = (bf16[16,96,512]{2,1,0:T(8,128)(2,1)S(1)}, bf16[16,96,512]{2,1,0:T(8,128)(2,1)S(1)}, u32[]{:S(2)}, u32[]{:S(2)}) collective-permute-start(bf16[16,96,512]{2,1,0:T(8,128)(2,1)S(1)} %broadcast_select_fusion.refs_0_), channel_id=1, source_target_pairs={{24,16},{25,17},{26,18},{27,19},{28,20},{29,21},{30,22},{31,23},{8... | collective-permute-start | bytes 4718600 | tf_op jit(solution)/shard_map/ppermute | solution.py:333
  29.0 0.3 convert_reduce_fusion.3
  29.4 0.6 convert_reduce_fusion
  30.4 2.4 %collective-permute-done.1.refs_1_ = bf16[16,96,512]{2,1,0:T(8,128)(2,1)S(1)} collective-permute-done((bf16[16,96,512]{2,1,0:T(8,128)(2,1)S(1)}, bf16[16,96,512]{2,1,0:T(8,128)(2,1)S(1)}, u32[]{:S(2)}, u32[]{:S(2)}) %collective-permute-start.1) | collective-permute-done | bytes 1572896 | tf_op jit(solution)/shard_map/ppermute | solution.py:333
  32.8 1.5 %shard_map.138 = bf16[8,96,512]{2,1,0:T(8,128)(2,1)} custom-call(s32[9]{0:T(128)S(1)} %pad_add_fusion.2.meta, bf16[16,96,512]{2,1,0:T(8,128)(2,1)S(1)} %broadcast_select_fusion.refs_0_, bf16[16,96,512]{2,1,0:T(8,128)(2,1)S(1)} %collective-permute-done.1.refs_1_), custom_call_target="tpu_custom_call" | custom-call | tf_op jit(solution)/shard_map/pallas_call | solution.py:244
  34.3 4.9 %all-to-all-start.1 = ((bf16[8,96,512]{2,1,0:T(8,128)(2,1)}), bf16[8,96,512]{2,1,0:T(8,128)(2,1)S(1)}, u32[]{:S(2)}, u32[]{:S(2)}) async-start(bf16[8,96,512]{2,1,0:T(8,128)(2,1)} %shard_map.138), calls=%async_computation.1 | async-start | bytes 1572864 | tf_op jit(solution)/shard_map/all_to_all | solution.py:391
  39.2 1.1 slice.27
  40.3 0.7 collective-permute-start.2
  41.1 1.1 broadcast_select_fusion.1.refs_0_
  42.3 1.4 %collective-permute-start.3 = (bf16[16,32,512]{2,1,0:T(8,128)(2,1)S(1)}, bf16[16,32,512]{2,1,0:T(8,128)(2,1)S(1)}, u32[]{:S(2)}, u32[]{:S(2)}) collective-permute-start(bf16[16,32,512]{2,1,0:T(8,128)(2,1)S(1)} %broadcast_select_fusion.1.refs_0_), channel_id=1, source_target_pairs={{24,16},{25,17},{26,18},{27,19},{28,20},{29,21},{30,22},{31,23},{8... | collective-permute-start | bytes 1572872 | tf_op jit(solution)/shard_map/ppermute | solution.py:333
  43.7 0.5 broadcast.445
  44.2 0.7 fusion.35
  45.1 9.2 %collective-permute-done.3.refs_1_ = bf16[16,32,512]{2,1,0:T(8,128)(2,1)S(1)} collective-permute-done((bf16[16,32,512]{2,1,0:T(8,128)(2,1)S(1)}, bf16[16,32,512]{2,1,0:T(8,128)(2,1)S(1)}, u32[]{:S(2)}, u32[]{:S(2)}) %collective-permute-start.3) | collective-permute-done | bytes 524320 | tf_op jit(solution)/shard_map/ppermute | solution.py:333
  54.3 1.3 shard_map.139
  55.6 4.1 %all-to-all-done.1.refs_0_.rest_0_ = bf16[8,96,512]{2,1,0:T(8,128)(2,1)S(1)} async-done(((bf16[8,96,512]{2,1,0:T(8,128)(2,1)}), bf16[8,96,512]{2,1,0:T(8,128)(2,1)S(1)}, u32[]{:S(2)}, u32[]{:S(2)}) %all-to-all-start.1) | async-done | bytes 786464 | tf_op jit(solution)/shard_map/all_to_all | solution.py:391
  59.7 3.6 %all-to-all-start.2 = ((bf16[8,32,512]{2,1,0:T(8,128)(2,1)}), bf16[8,32,512]{2,1,0:T(8,128)(2,1)S(1)}, u32[]{:S(2)}, u32[]{:S(2)}) async-start(bf16[8,32,512]{2,1,0:T(8,128)(2,1)} %shard_map.139), calls=%async_computation.2 | async-start | bytes 524288 | tf_op jit(solution)/shard_map/all_to_all | solution.py:391
  63.3 0.6 shard_map.140
  63.9 0.6 bitcast_convert_fusion.1.cond_ref
  64.5 0.8 copy.62
  65.4 0.8 copy.63
  67.0 5.3 %all-to-all-done.2.refs_0_.rest_1_ = bf16[8,32,512]{2,1,0:T(8,128)(2,1)S(1)} async-done(((bf16[8,32,512]{2,1,0:T(8,128)(2,1)}), bf16[8,32,512]{2,1,0:T(8,128)(2,1)S(1)}, u32[]{:S(2)}, u32[]{:S(2)}) %all-to-all-start.2) | async-done | bytes 262176 | tf_op jit(solution)/shard_map/all_to_all | solution.py:391
  72.4 0.7 shard_map.141
  73.2 2.2 %collective-permute-done.6.rest_4_ = bf16[4,96,512]{2,1,0:T(8,128)(2,1)} collective-permute-done((bf16[4,96,512]{2,1,0:T(8,128)(2,1)S(1)}, bf16[4,96,512]{2,1,0:T(8,128)(2,1)}, u32[]{:S(2)}, u32[]{:S(2)}) %collective-permute-start.6) | collective-permute-done | bytes 393248 | tf_op jit(solution)/shard_map/ppermute | solution.py:333
  75.4 0.5 collective-permute-start.5
  75.9 2.2 %collective-permute-done.7.rest_5_ = bf16[4,32,512]{2,1,0:T(8,128)(2,1)S(1)} collective-permute-done((bf16[4,32,512]{2,1,0:T(8,128)(2,1)S(1)}, bf16[4,32,512]{2,1,0:T(8,128)(2,1)S(1)}, u32[]{:S(2)}, u32[]{:S(2)}) %collective-permute-start.7) | collective-permute-done | bytes 131104 | tf_op jit(solution)/shard_map/ppermute | solution.py:333
  78.2 0.6 pad_add_fusion.1.meta
  78.7 0.8 collective-permute-done.9.rest_7_
  79.6 0.6 copy-done.12
  80.3 0.2 copy-done.8
  80.7 24.6 %shard_map.142 = (bf16[256,2048]{1,0:T(8,128)(2,1)}, bf16[256,2048]{1,0:T(8,128)(2,1)}, f32[4,512]{1,0:T(4,128)}, f32[512,512]{1,0:T(8,128)}) custom-call(s32[25]{0:T(128)} %pad_add_fusion.1.meta, bf16[256,2048]{1,0:T(8,128)(2,1)} %bitcast.75, bf16[256,2048]{1,0:T(8,128)(2,1)} %bitcast.76, f32[4,512]{1,0:T(4,128)} %bitcast_convert_fusion.1.cond_ref, ...), custom_call_target="tpu_custom_call" | custom-call | flops 11811160064 | bytes 16777216 | tf_op jit(solution)/shard_map/pallas_call | solution.py:190
  105.3 1.1 fusion
  106.6 1.4 %collective-permute-done.10 = bf16[2,8,16,512]{3,2,1,0:T(8,128)(2,1)S(1)} collective-permute-done((bf16[2,8,16,512]{3,2,1,0:T(8,128)(2,1)S(1)}, bf16[2,8,16,512]{3,2,1,0:T(8,128)(2,1)S(1)}, u32[]{:S(2)}, u32[]{:S(2)}) %collective-permute-start.10) | collective-permute-done | bytes 262176 | tf_op jit(solution)/shard_map/ppermute | solution.py:298
  108.0 1.1 bitcast_add_fusion
  109.2 5.5 %collective-permute-done.11 = bf16[1,8,16,512]{3,2,1,0:T(8,128)(2,1)S(1)} collective-permute-done((bf16[1,8,16,512]{3,2,1,0:T(8,128)(2,1)S(1)}, bf16[1,8,16,512]{3,2,1,0:T(8,128)(2,1)S(1)}, u32[]{:S(2)}, u32[]{:S(2)}) %collective-permute-start.11) | collective-permute-done | bytes 131104 | tf_op jit(solution)/shard_map/ppermute | solution.py:298
  114.8 1.5 %collective-permute-start.12 = (bf16[1,4,16,512]{3,2,1,0:T(8,128)(2,1)S(1)}, bf16[1,4,16,512]{3,2,1,0:T(8,128)(2,1)S(1)}, u32[]{:S(2)}, u32[]{:S(2)}) collective-permute-start(bf16[1,4,16,512]{3,2,1,0:T(8,128)(2,1)S(1)} %fusion.2), channel_id=1, source_target_pairs={{0,1},{1,0},{2,3},{3,2},{4,5},{5,4},{6,7},{7,6},{8,9},{9,8},{10,11... | collective-permute-start | bytes 196616 | tf_op jit(solution)/shard_map/ppermute | solution.py:298
  116.3 2.8 %collective-permute-done.12 = bf16[1,4,16,512]{3,2,1,0:T(8,128)(2,1)S(1)} collective-permute-done((bf16[1,4,16,512]{3,2,1,0:T(8,128)(2,1)S(1)}, bf16[1,4,16,512]{3,2,1,0:T(8,128)(2,1)S(1)}, u32[]{:S(2)}, u32[]{:S(2)}) %collective-permute-start.12) | collective-permute-done | bytes 65568 | tf_op jit(solution)/shard_map/ppermute | solution.py:298
  119.2 1.1 collective-permute-start.13
  120.3 2.9 %collective-permute-done.13 = bf16[1,2,16,512]{3,2,1,0:T(8,128)(2,1)S(1)} collective-permute-done((bf16[1,2,16,512]{3,2,1,0:T(8,128)(2,1)S(1)}, bf16[1,2,16,512]{3,2,1,0:T(8,128)(2,1)S(1)}, u32[]{:S(2)}, u32[]{:S(2)}) %collective-permute-start.13) | collective-permute-done | bytes 32800 | tf_op jit(solution)/shard_map/ppermute | solution.py:298
  123.2 2.2 %collective-permute-start.14 = (bf16[1,1,16,512]{3,2,1,0:T(8,128)(2,1)S(1)}, bf16[1,1,16,512]{3,2,1,0:T(8,128)(2,1)S(1)}, u32[]{:S(2)}, u32[]{:S(2)}) collective-permute-start(bf16[1,1,16,512]{3,2,1,0:T(8,128)(2,1)S(1)} %dynamic-slice_convert_fusion.3), channel_id=1, source_target_pairs={{0,4},{1,5},{2,6},{3,7},{4,0},{5,1},{6,2},{7,3},{8,12},{9,13},{10,... | collective-permute-start | bytes 49160 | tf_op jit(solution)/shard_map/ppermute | solution.py:298
  125.4 2.5 %collective-permute-done.14 = bf16[1,1,16,512]{3,2,1,0:T(8,128)(2,1)S(1)} collective-permute-done((bf16[1,1,16,512]{3,2,1,0:T(8,128)(2,1)S(1)}, bf16[1,1,16,512]{3,2,1,0:T(8,128)(2,1)S(1)}, u32[]{:S(2)}, u32[]{:S(2)}) %collective-permute-start.14) | collective-permute-done | bytes 16416 | tf_op jit(solution)/shard_map/ppermute | solution.py:298
  127.9 0.6 add_bitcast_fusion
  (83 shorter events, 3.2 us)
Async XLA Ops:
  0.6 2.4 %copy-start.5 = (s32[1,1,4,2]{2,3,1,0:T(2,128)S(1)}, s32[1,1,4,2]{2,3,1,0:T(2,128)}, u32[]{:S(2)}) copy-start(s32[1,1,4,2]{2,3,1,0:T(2,128)} %param.14) | copy-start | bytes 100
  0.6 2.6 %copy-start.6 = (s32[1,1,4,2]{2,3,1,0:T(2,128)S(1)}, s32[1,1,4,2]{2,3,1,0:T(2,128)}, u32[]{:S(2)}) copy-start(s32[1,1,4,2]{2,3,1,0:T(2,128)} %param.15) | copy-start | bytes 100
  0.7 2.7 %copy-start.7 = (s32[1,1,16]{2,1,0:T(1,128)S(1)}, s32[1,1,16]{2,1,0:T(1,128)}, u32[]{:S(2)}) copy-start(s32[1,1,16]{2,1,0:T(1,128)} %param.17) | copy-start | bytes 196
  2.2 23.7 %collective-permute-start = (bf16[16,96,512]{2,1,0:T(8,128)(2,1)S(1)}, bf16[16,96,512]{2,1,0:T(8,128)(2,1)S(1)}, u32[]{:S(2)}, u32[]{:S(2)}) collective-permute-start(bf16[16,96,512]{2,1,0:T(8,128)(2,1)S(1)} %slice.28), channel_id=1, source_target_pairs={{24,8},{25,9},{26,10},{27,11},{28,12},{29,13},{30,14},{31,15}} | collective-permute-start | bytes 4718600 | tf_op jit(solution)/shard_map/ppermute | solution.py:333
  4.1 21.9 %all-to-all-start = ((s32[32,1,128]{2,1,0:T(1,128)}), s32[32,1,128]{2,1,0:T(1,128)S(1)}, u32[]{:S(2)}, u32[]{:S(2)}) async-start(s32[32,1,128]{2,1,0:T(1,128)} %broadcast_in_dim.87), calls=%async_computation | async-start | bytes 32768 | tf_op jit(solution)/shard_map/all_to_all | solution.py:346
  27.5 5.3 %collective-permute-start.1 = (bf16[16,96,512]{2,1,0:T(8,128)(2,1)S(1)}, bf16[16,96,512]{2,1,0:T(8,128)(2,1)S(1)}, u32[]{:S(2)}, u32[]{:S(2)}) collective-permute-start(bf16[16,96,512]{2,1,0:T(8,128)(2,1)S(1)} %broadcast_select_fusion.refs_0_), channel_id=1, source_target_pairs={{24,16},{25,17},{26,18},{27,19},{28,20},{29,21},{30,22},{31,23},{8... | collective-permute-start | bytes 4718600 | tf_op jit(solution)/shard_map/ppermute | solution.py:333
  34.3 25.3 %all-to-all-start.1 = ((bf16[8,96,512]{2,1,0:T(8,128)(2,1)}), bf16[8,96,512]{2,1,0:T(8,128)(2,1)S(1)}, u32[]{:S(2)}, u32[]{:S(2)}) async-start(bf16[8,96,512]{2,1,0:T(8,128)(2,1)} %shard_map.138), calls=%async_computation.1 | async-start | bytes 1572864 | tf_op jit(solution)/shard_map/all_to_all | solution.py:391
  40.3 0.8 collective-permute-start.2
  42.2 21.7 %copy-start.4 = (bf16[1,1,4,512]{3,2,1,0:T(4,128)(2,1)S(1)}, bf16[1,1,4,512]{3,2,1,0:T(4,128)(2,1)}, u32[]{:S(2)}) copy-start(bf16[1,1,4,512]{3,2,1,0:T(4,128)(2,1)} %param.13) | copy-start | bytes 12292
  42.2 22.3 %copy-start.3 = (bf16[256,512]{1,0:T(8,128)(2,1)S(1)}, bf16[256,512]{1,0:T(8,128)(2,1)}, u32[]{:S(2)}) copy-start(bf16[256,512]{1,0:T(8,128)(2,1)} %up_ref.1) | copy-start | bytes 786436
  42.3 12.1 %collective-permute-start.3 = (bf16[16,32,512]{2,1,0:T(8,128)(2,1)S(1)}, bf16[16,32,512]{2,1,0:T(8,128)(2,1)S(1)}, u32[]{:S(2)}, u32[]{:S(2)}) collective-permute-start(bf16[16,32,512]{2,1,0:T(8,128)(2,1)S(1)} %broadcast_select_fusion.1.refs_0_), channel_id=1, source_target_pairs={{24,16},{25,17},{26,18},{27,19},{28,20},{29,21},{30,22},{31,23},{8... | collective-permute-start | bytes 1572872 | tf_op jit(solution)/shard_map/ppermute | solution.py:333
  45.1 20.3 %copy-start.2 = (bf16[512,256]{1,0:T(8,128)(2,1)S(1)}, bf16[512,256]{1,0:T(8,128)(2,1)}, u32[]{:S(2)}) copy-start(bf16[512,256]{1,0:T(8,128)(2,1)} %down_ref.1) | copy-start | bytes 786436
  59.7 13.4 %copy-start = (bf16[8,96,512]{2,1,0:T(8,128)(2,1)}, bf16[8,96,512]{2,1,0:T(8,128)(2,1)S(1)}, u32[]{:S(2)}) copy-start(bf16[8,96,512]{2,1,0:T(8,128)(2,1)S(1)} %all-to-all-done.1.refs_0_.rest_0_) | copy-start | bytes 2359300
  59.7 12.7 %all-to-all-start.2 = ((bf16[8,32,512]{2,1,0:T(8,128)(2,1)}), bf16[8,32,512]{2,1,0:T(8,128)(2,1)S(1)}, u32[]{:S(2)}, u32[]{:S(2)}) async-start(bf16[8,32,512]{2,1,0:T(8,128)(2,1)} %shard_map.139), calls=%async_computation.2 | async-start | bytes 524288 | tf_op jit(solution)/shard_map/all_to_all | solution.py:391
  63.8 11.5 %collective-permute-start.6 = (bf16[4,96,512]{2,1,0:T(8,128)(2,1)S(1)}, bf16[4,96,512]{2,1,0:T(8,128)(2,1)}, u32[]{:S(2)}, u32[]{:S(2)}) collective-permute-start(bf16[4,96,512]{2,1,0:T(8,128)(2,1)S(1)} %shard_map.140), channel_id=1, source_target_pairs={{0,16},{1,17},{2,18},{3,19},{4,20},{5,21},{6,22},{7,23},{8,24},{9,... | collective-permute-start | bytes 1179656 | tf_op jit(solution)/shard_map/ppermute | solution.py:333
  66.4 13.1 %collective-permute-start.4 = (bf16[8,96,512]{2,1,0:T(8,128)(2,1)S(1)}, bf16[8,96,512]{2,1,0:T(8,128)(2,1)S(1)}, u32[]{:S(2)}, u32[]{:S(2)}) collective-permute-start(bf16[8,96,512]{2,1,0:T(8,128)(2,1)S(1)} %all-to-all-done.1.refs_0_.rest_0_), channel_id=1, source_target_pairs={{0,8},{1,9},{2,10},{3,11},{4,12},{5,13},{6,14},{7,15},{8,0},{9,1},... | collective-permute-start | bytes 2359304 | tf_op jit(solution)/shard_map/ppermute | solution.py:333
  72.4 7.2 %copy-start.1 = (bf16[8,32,512]{2,1,0:T(8,128)(2,1)}, bf16[8,32,512]{2,1,0:T(8,128)(2,1)S(1)}, u32[]{:S(2)}) copy-start(bf16[8,32,512]{2,1,0:T(8,128)(2,1)S(1)} %all-to-all-done.2.refs_0_.rest_1_) | copy-start | bytes 786436
  73.1 5.0 %collective-permute-start.7 = (bf16[4,32,512]{2,1,0:T(8,128)(2,1)S(1)}, bf16[4,32,512]{2,1,0:T(8,128)(2,1)S(1)}, u32[]{:S(2)}, u32[]{:S(2)}) collective-permute-start(bf16[4,32,512]{2,1,0:T(8,128)(2,1)S(1)} %shard_map.141), channel_id=1, source_target_pairs={{0,16},{1,17},{2,18},{3,19},{4,20},{5,21},{6,22},{7,23},{8,24},{9,... | collective-permute-start | bytes 393224 | tf_op jit(solution)/shard_map/ppermute | solution.py:333
  75.4 4.1 %collective-permute-start.8 = (bf16[4,96,512]{2,1,0:T(8,128)(2,1)}, bf16[4,96,512]{2,1,0:T(8,128)(2,1)S(1)}, u32[]{:S(2)}, u32[]{:S(2)}) collective-permute-start(bf16[4,96,512]{2,1,0:T(8,128)(2,1)} %collective-permute-done.6.rest_4_), channel_id=1, source_target_pairs={{0,8},{1,9},{2,10},{3,11},{4,12},{5,13},{6,14},{7,15},{8,0},{9,1},... | collective-permute-start | bytes 1179656 | tf_op jit(solution)/shard_map/ppermute | solution.py:333
  75.4 4.1 %collective-permute-start.5 = (bf16[8,32,512]{2,1,0:T(8,128)(2,1)S(1)}, bf16[8,32,512]{2,1,0:T(8,128)(2,1)S(1)}, u32[]{:S(2)}, u32[]{:S(2)}) collective-permute-start(bf16[8,32,512]{2,1,0:T(8,128)(2,1)S(1)} %all-to-all-done.2.refs_0_.rest_1_), channel_id=1, source_target_pairs={{0,8},{1,9},{2,10},{3,11},{4,12},{5,13},{6,14},{7,15},{8,0},{9,1},... | collective-permute-start | bytes 786440 | tf_op jit(solution)/shard_map/ppermute | solution.py:333
  78.1 1.4 %copy-start.11 = (bf16[4,32,512]{2,1,0:T(8,128)(2,1)}, bf16[4,32,512]{2,1,0:T(8,128)(2,1)S(1)}, u32[]{:S(2)}) copy-start(bf16[4,32,512]{2,1,0:T(8,128)(2,1)S(1)} %collective-permute-done.7.rest_5_) | copy-start | bytes 393220
  78.2 1.3 %collective-permute-start.9 = (bf16[4,32,512]{2,1,0:T(8,128)(2,1)S(1)}, bf16[4,32,512]{2,1,0:T(8,128)(2,1)S(1)}, u32[]{:S(2)}, u32[]{:S(2)}) collective-permute-start(bf16[4,32,512]{2,1,0:T(8,128)(2,1)S(1)} %collective-permute-done.7.rest_5_), channel_id=1, source_target_pairs={{0,8},{1,9},{2,10},{3,11},{4,12},{5,13},{6,14},{7,15},{8,0},{9,1},... | collective-permute-start | bytes 393224 | tf_op jit(solution)/shard_map/ppermute | solution.py:333
  79.5 0.6 copy-start.12
  79.5 0.8 copy-start.10
  79.5 1.0 copy-start.8
  79.5 1.1 copy-start.9
  106.4 1.6 %collective-permute-start.10 = (bf16[2,8,16,512]{3,2,1,0:T(8,128)(2,1)S(1)}, bf16[2,8,16,512]{3,2,1,0:T(8,128)(2,1)S(1)}, u32[]{:S(2)}, u32[]{:S(2)}) collective-permute-start(bf16[2,8,16,512]{3,2,1,0:T(8,128)(2,1)S(1)} %fusion), channel_id=1, source_target_pairs={{0,8},{8,0},{16,24},{24,16},{1,9},{9,1},{17,25},{25,17},{2,10},{10... | collective-permute-start | bytes 786440 | tf_op jit(solution)/shard_map/ppermute | solution.py:298
  109.1 5.6 %collective-permute-start.11 = (bf16[1,8,16,512]{3,2,1,0:T(8,128)(2,1)S(1)}, bf16[1,8,16,512]{3,2,1,0:T(8,128)(2,1)S(1)}, u32[]{:S(2)}, u32[]{:S(2)}) collective-permute-start(bf16[1,8,16,512]{3,2,1,0:T(8,128)(2,1)S(1)} %dynamic-slice_convert_fusion), channel_id=1, source_target_pairs={{0,16},{8,24},{16,0},{24,8},{1,17},{9,25},{17,1},{25,9},{2,18},{10... | collective-permute-start | bytes 393224 | tf_op jit(solution)/shard_map/ppermute | solution.py:298
  114.8 4.3 %collective-permute-start.12 = (bf16[1,4,16,512]{3,2,1,0:T(8,128)(2,1)S(1)}, bf16[1,4,16,512]{3,2,1,0:T(8,128)(2,1)S(1)}, u32[]{:S(2)}, u32[]{:S(2)}) collective-permute-start(bf16[1,4,16,512]{3,2,1,0:T(8,128)(2,1)S(1)} %fusion.2), channel_id=1, source_target_pairs={{0,1},{1,0},{2,3},{3,2},{4,5},{5,4},{6,7},{7,6},{8,9},{9,8},{10,11... | collective-permute-start | bytes 196616 | tf_op jit(solution)/shard_map/ppermute | solution.py:298
  119.2 4.0 %collective-permute-start.13 = (bf16[1,2,16,512]{3,2,1,0:T(8,128)(2,1)S(1)}, bf16[1,2,16,512]{3,2,1,0:T(8,128)(2,1)S(1)}, u32[]{:S(2)}, u32[]{:S(2)}) collective-permute-start(bf16[1,2,16,512]{3,2,1,0:T(8,128)(2,1)S(1)} %fusion.3), channel_id=1, source_target_pairs={{0,2},{1,3},{2,0},{3,1},{4,6},{5,7},{6,4},{7,5},{8,10},{9,11},{10,... | collective-permute-start | bytes 98312 | tf_op jit(solution)/shard_map/ppermute | solution.py:298
  123.2 4.7 %collective-permute-start.14 = (bf16[1,1,16,512]{3,2,1,0:T(8,128)(2,1)S(1)}, bf16[1,1,16,512]{3,2,1,0:T(8,128)(2,1)S(1)}, u32[]{:S(2)}, u32[]{:S(2)}) collective-permute-start(bf16[1,1,16,512]{3,2,1,0:T(8,128)(2,1)S(1)} %dynamic-slice_convert_fusion.3), channel_id=1, source_target_pairs={{0,4},{1,5},{2,6},{3,7},{4,0},{5,1},{6,2},{7,3},{8,12},{9,13},{10,... | collective-permute-start | bytes 49160 | tf_op jit(solution)/shard_map/ppermute | solution.py:298

commit v14 on v13

--- a/solution.py
+++ b/solution.py
@@ -30,7 +30,7 @@
 ):
     held_refs = rest[:held_count]
     (kv_hbm, kvt_hbm, out_ref, qg_ref, cg_ref, ad_ref,
-     raw_ref, kv_ref, kvt_ref, proj_ref, grad_ref, score_ref, dprob_ref,
+     raw_ref, kv_ref, kvt_ref, proj_ref, grad_ref,
      q2_ref, cot2_ref, acc_ref, sems, kv_sem) = rest[held_count:]
     step = pl.program_id(0)
     per_device, slot_len, width = raw_ref.shape
@@ -46,15 +46,9 @@
     cuts = [pl.ds(low, high - low) for low, high in zip(bounds, bounds[1:])]
     pairs = [pl.ds(i * 2 * HEAD, 2 * HEAD) for i in range(HEADS // 2)]
     value_pairs = [pl.ds(head_cols + i * 2 * HEAD, 2 * HEAD) for i in range(HEADS // 2)]
-    lanes = [pl.ds(i * 2 * SPAN, 2 * SPAN) for i in range(HEADS // 2)]
     keys = [pl.ds(g * key_count, key_count) for g in range(group)]
     tokens = [pl.ds(g * SPAN, SPAN) for g in range(group)]
     double = [pl.ds(g * 2 * SPAN, 2 * SPAN) for g in range(group)]
-    spots = [
-        (g, cols, value_cols, lane)
-        for g in range(group)
-        for cols, value_cols, lane in zip(pairs, value_pairs, lanes)
-    ]
     kv_copy = pltpu.make_async_copy(kv_hbm, kv_ref, kv_sem.at[0])
     kvt_copy = pltpu.make_async_copy(kvt_hbm, kvt_ref, kv_sem.at[1])
 
@@ -113,10 +107,6 @@
     for cols in pairs + value_pairs:
         proj_ref[:, cols] = dot(encoded, kv_ref[:, cols]).astype(jnp.bfloat16)
 
-    for g, cols, value_cols, lane in spots:
-        score_ref[keys[g], lane] = dot(proj_ref[keys[g], cols], q2_ref[double[g], cols], NT)
-        dprob_ref[keys[g], lane] = dot(proj_ref[keys[g], value_cols], cot2_ref[double[g], cols], NT)
-
     def diagonal(both):
         return jnp.concatenate([both[:SPAN, :HEAD], both[SPAN:, HEAD:]], axis=1)
 
@@ -128,21 +118,23 @@
             item = (step * group + g) * nbr_count + n
             limit = jnp.where(here, n * slot_len + meta[lens + item], limit)
         usable = slot < limit
-        for cols, value_cols, lane in zip(pairs, value_pairs, lanes):
-            scores = jnp.where(usable, score_ref[keys[g], lane], FLOOR)
+        for cols, value_cols in zip(pairs, value_pairs):
+            q2 = q2_ref[double[g], cols]
+            cot2 = cot2_ref[double[g], cols]
+            key_rows = proj_ref[keys[g], cols]
+            value_rows = proj_ref[keys[g], value_cols]
+            scores = jnp.where(usable, dot(key_rows, q2, NT), FLOOR)
             row_max = jnp.max(scores, axis=0, keepdims=True)
             raised = jnp.exp2((scores - row_max) * (scaling * LOG2E))
             probs = raised * (1.0 / jnp.sum(raised, axis=0, keepdims=True))
-            d_probs = dprob_ref[keys[g], lane]
+            d_probs = dot(value_rows, cot2, NT)
             delta = jnp.sum(probs * d_probs, axis=0, keepdims=True)
             probs_b = probs.astype(jnp.bfloat16)
             d_scores = (probs * (d_probs - delta) * scaling).astype(jnp.bfloat16)
-            grad_ref[keys[g], cols] = dot(d_scores, q2_ref[double[g], cols]).astype(jnp.bfloat16)
-            grad_ref[keys[g], value_cols] = dot(probs_b, cot2_ref[double[g], cols]).astype(
-                jnp.bfloat16
-            )
-            out = diagonal(dot(probs_b.T, proj_ref[keys[g], value_cols]))
-            grad = diagonal(dot(d_scores.T, proj_ref[keys[g], cols]))
+            grad_ref[keys[g], cols] = dot(d_scores, q2).astype(jnp.bfloat16)
+            grad_ref[keys[g], value_cols] = dot(probs_b, cot2).astype(jnp.bfloat16)
+            out = diagonal(dot(probs_b.T, value_rows))
+            grad = diagonal(dot(d_scores.T, key_rows))
             out_ref[tokens[g], cols] = jnp.where(live, out, 0.0).astype(jnp.bfloat16)
             qg_ref[tokens[g], cols] = jnp.where(live, grad, 0.0).astype(jnp.bfloat16)
 
@@ -185,7 +177,6 @@
     per_device = span_count * nbr_count
     keys = group * nbr_count * slot_len
     rows = per_device * slot_len
-    lanes = SPAN * HEADS
     flops = 2 * rows * (2 * width * 2 * head_cols + 6 * width * rank + 6 * SPAN * head_cols)
     return pl.pallas_call(
         functools.partial(span_kernel, len(held), nbr_count, bounds),
@@ -207,8 +198,6 @@
                 pltpu.VMEM((2 * head_cols, width), jnp.bfloat16),
                 pltpu.VMEM((keys, 2 * head_cols), jnp.bfloat16),
                 pltpu.VMEM((keys, 2 * head_cols), jnp.bfloat16),
-                pltpu.VMEM((keys, lanes), jnp.float32),
-                pltpu.VMEM((keys, lanes), jnp.float32),
                 pltpu.VMEM((group * 2 * SPAN, head_cols), jnp.bfloat16),
                 pltpu.VMEM((group * 2 * SPAN, head_cols), jnp.bfloat16),
                 pltpu.VMEM((width, 2 * rank), jnp.float32),
@@ -281,7 +270,7 @@
     total = total.reshape(tuple(sizes) + (-1, width)).astype(jnp.float32)
     for at, axis in enumerate(axes):
         size, index = sizes[at], lax.axis_index(axis)
-        if size & (size - 1):
+        if size > 4 or size & (size - 1):
             lead = (size,) + tuple(d for i, d in enumerate(total.shape) if i != at)
             parts = jnp.moveaxis(total, at, 0).astype(jnp.bfloat16)
             parts = lax.all_to_all(parts, axis, split_axis=0, concat_axis=0, tiled=True)
@@ -334,7 +323,7 @@
             array, axes, [(a * columns + j, b * columns + j) for a, b in pairs for j in range(columns)]
         )
 
-    first = slot_len // 16 * 3 // 4 * 16
+    first = slot_len // 16 * 5 // 8 * 16
     bounds = [0, first, slot_len] if 0 < first < slot_len else [0, slot_len]
     parts = len(bounds) - 1
     full_store = database.reshape(block_count, slot_len, width)

time: 129 us -> 137 us (1.062)
  blocking collectives: 0 us -> 11.8 us
  waiting for transfers between devices: 48.4 us -> 37 us
  Pallas kernels: 28.7 us -> 35.6 us
  starting transfers between devices: 26.6 us -> 22.4 us
  local copies, waits for them, and re-layouts: 15.7 us -> 19.7 us
    all_to_all x0 -> x1, blocking collectives: none -> 11.8 us  [scatter_sum(): parts = lax.all_to_all(parts, axis, split_axis=0, concat_axis=0, tiled=True)]
    ppermute x5 -> x2, waiting for transfers between devices: 15.1 us -> 6.65 us  [scatter_sum(): lax.ppermute(give.astype(jnp.bfloat16), axis, [(i, i ^ bit) for i in rang...]
    pallas_call x1, Pallas kernels: 24.6 us -> 31.5 us  [run_spans(): pl.pallas_call(functools.partial(span_kernel, len(held), nbr_count, bound...]
    ppermute x10, waiting for transfers between devices: 16.8 us -> 10.3 us  [hop(): lax.ppermute(array, axes, [(a * columns + j, b * columns + j) for a, b in...]
    all_to_all x2, waiting for transfers between devices: 9.39 us -> 15.8 us  [body(): lax.all_to_all(sends, 'dp', split_axis=0, concat_axis=0, tiled=True)]
    ppermute x5 -> x2, starting transfers between devices: 5.09 us -> 0.55 us  [scatter_sum(): lax.ppermute(give.astype(jnp.bfloat16), axis, [(i, i ^ bit) for i in rang...]
    all_to_all x1, waiting for transfers between devices: 7.08 us -> 4.29 us  [to_all(): return lax.all_to_all(copies, axis, split_axis=0, concat_axis=0, tiled=True)]
    unnamed x31 -> x35, local copies, waits for them, and re-layouts: 9.5 us -> 11.7 us
  transfers between devices with their start and end apart: 18 -> 15, of which waited for: 13 -> 8; matrix products, arithmetic and copies ran while one was open for 13% -> 14% of each run, Pallas kernels for 2% -> 3%
where the time goes in v14:
time: 137 us; the launch traced here: 136 us
  waiting for transfers between devices  37 us (27%)
  Pallas kernels  35.6 us (26%)
  starting transfers between devices  22.4 us (16%)
  local copies, waits for them, and re-layouts  19.7 us (14%)
  blocking collectives  11.8 us (9%)
  other arithmetic  8.14 us (6%)
    pallas_call x1, Pallas kernels, run_spans(): pl.pallas_call(functools.partial(span_kernel, len(held), nbr_count, bound...  31.5 us
    all_to_all x2, waiting for transfers between devices, body(): lax.all_to_all(sends, 'dp', split_axis=0, concat_axis=0, tiled=True)  15.8 us
    all_to_all x1, blocking collectives, scatter_sum(): parts = lax.all_to_all(parts, axis, split_axis=0, concat_axis=0, tiled=True)  11.8 us
    unnamed x35, local copies, waits for them, and re-layouts  11.7 us
    ppermute x10, waiting for transfers between devices, hop(): lax.ppermute(array, axes, [(a * columns + j, b * columns + j) for a, b in...  10.3 us
    all_to_all x2, starting transfers between devices, body(): lax.all_to_all(sends, 'dp', split_axis=0, concat_axis=0, tiled=True)  8.78 us
    all_to_all x1, starting transfers between devices, to_all(): return lax.all_to_all(copies, axis, split_axis=0, concat_axis=0, tiled=True)  8.23 us
    ppermute x2, waiting for transfers between devices, scatter_sum(): lax.ppermute(give.astype(jnp.bfloat16), axis, [(i, i ^ bit) for i in rang...  6.65 us
  transfers between devices with their start and end apart: 15, of which 8 were waited for; matrix products, arithmetic and copies ran while one was open for 14% of the time, Pallas kernels for 3%

profile of v14, /device:TPU:0, one launch (start us, length us, event | category | flops | bytes accessed | tf_op | source)
XLA Modules:
  0.0 135.7 jit_solution(7311926687687209208)
XLA Ops:
  0.7 2.5 %slice.28 = bf16[16,80,512]{2,1,0:T(8,128)(2,1)} slice(bf16[16,128,512]{2,1,0:T(8,128)(2,1)} %bitcast.47), slice={[0:16], [0:80], [0:512]} | slice | bytes 2621440 | tf_op jit(solution)/shard_map/slice | solution.py:330
  3.2 0.7 collective-permute-start
  4.4 0.6 broadcast_in_dim.87
  5.0 8.2 %all-to-all-start = ((s32[32,1,128]{2,1,0:T(1,128)}), s32[32,1,128]{2,1,0:T(1,128)S(1)}, u32[]{:S(2)}, u32[]{:S(2)}) async-start(s32[32,1,128]{2,1,0:T(1,128)} %broadcast_in_dim.87), calls=%async_computation | async-start | bytes 32768 | tf_op jit(solution)/shard_map/all_to_all | solution.py:335
  13.4 6.6 %copy.46 = bf16[512,4096]{0,1:T(8,128)(2,1)} copy(bf16[512,4096]{1,0:T(8,128)(2,1)} %rest_8_.1) | data formatting | bytes 8388608 | tf_op args[10]
  20.0 4.3 %all-to-all-done = s32[32,1,128]{2,1,0:T(1,128)S(1)} async-done(((s32[32,1,128]{2,1,0:T(1,128)}), s32[32,1,128]{2,1,0:T(1,128)S(1)}, u32[]{:S(2)}, u32[]{:S(2)}) %all-to-all-start) | async-done | bytes 16416 | tf_op jit(solution)/shard_map/all_to_all | solution.py:335
  24.3 1.1 copy-done.3
  25.4 1.5 %broadcast_select_fusion.refs_0_ = bf16[16,80,512]{2,1,0:T(8,128)(2,1)S(1)} fusion(bf16[16,80,512]{2,1,0:T(8,128)(2,1)} %copy-done.3, pred[]{:T(512)S(6)} %eq.145, bf16[16,128,512]{2,1,0:T(8,128)(2,1)S(1)} %bitcast.50), kind=kLoop, calls=%fused_computation | loop fusion | flops 655360 | bytes 3932161 | tf_op jit(solution)/shard_map/jit(_where)/select_n | solution.py:373
  26.8 1.3 collective-permute-start.1
  28.2 2.1 %slice.27 = bf16[16,48,512]{2,1,0:T(8,128)(2,1)} slice(bf16[16,128,512]{2,1,0:T(8,128)(2,1)} %bitcast.48), slice={[0:16], [80:128], [0:512]} | slice | bytes 1572864 | tf_op jit(solution)/shard_map/slice | solution.py:330
  30.3 0.7 collective-permute-start.2
  31.0 0.3 convert_reduce_fusion.4
  31.4 0.6 convert_reduce_fusion.1
  32.2 0.2 select_reduce_fusion
  32.4 1.4 %shard_map.138 = bf16[8,80,512]{2,1,0:T(8,128)(2,1)} custom-call(s32[9]{0:T(128)S(1)} %pad_add_fusion.2.meta, bf16[16,80,512]{2,1,0:T(8,128)(2,1)S(1)} %broadcast_select_fusion.refs_0_, bf16[16,80,512]{2,1,0:T(8,128)(2,1)S(1)} %collective-permute-done.1.refs_1_), custom_call_target="tpu_custom_call" | custom-call | tf_op jit(solution)/shard_map/pallas_call | solution.py:233
  33.9 4.9 %all-to-all-start.1 = ((bf16[8,80,512]{2,1,0:T(8,128)(2,1)}), bf16[8,80,512]{2,1,0:T(8,128)(2,1)S(1)}, u32[]{:S(2)}, u32[]{:S(2)}) async-start(bf16[8,80,512]{2,1,0:T(8,128)(2,1)} %shard_map.138), calls=%async_computation.1 | async-start | bytes 1310720 | tf_op jit(solution)/shard_map/all_to_all | solution.py:380
  38.8 1.3 broadcast_select_fusion.1.refs_0_
  40.1 1.3 collective-permute-start.3
  41.4 0.9 copy.51
  42.3 1.8 %copy.50 = bf16[256,512]{0,1:T(8,128)(2,1)} copy(bf16[256,512]{1,0:T(8,128)(2,1)} %up_ref.1) | data formatting | bytes 524288 | tf_op args[9]
  44.1 0.6 bitcast_convert_fusion.1.cond_ref
  44.7 4.3 %collective-permute-done.3.refs_1_ = bf16[16,48,512]{2,1,0:T(8,128)(2,1)S(1)} collective-permute-done((bf16[16,48,512]{2,1,0:T(8,128)(2,1)S(1)}, bf16[16,48,512]{2,1,0:T(8,128)(2,1)S(1)}, u32[]{:S(2)}, u32[]{:S(2)}) %collective-permute-start.3) | collective-permute-done | bytes 786464 | tf_op jit(solution)/shard_map/ppermute | solution.py:322
  49.0 1.3 shard_map.139
  50.4 6.8 %all-to-all-done.1.refs_0_.rest_0_ = bf16[8,80,512]{2,1,0:T(8,128)(2,1)S(1)} async-done(((bf16[8,80,512]{2,1,0:T(8,128)(2,1)}), bf16[8,80,512]{2,1,0:T(8,128)(2,1)S(1)}, u32[]{:S(2)}, u32[]{:S(2)}) %all-to-all-start.1) | async-done | bytes 655392 | tf_op jit(solution)/shard_map/all_to_all | solution.py:380
  57.2 3.9 %all-to-all-start.2 = ((bf16[8,48,512]{2,1,0:T(8,128)(2,1)}), bf16[8,48,512]{2,1,0:T(8,128)(2,1)S(1)}, u32[]{:S(2)}, u32[]{:S(2)}) async-start(bf16[8,48,512]{2,1,0:T(8,128)(2,1)} %shard_map.139), calls=%async_computation.2 | async-start | bytes 786432 | tf_op jit(solution)/shard_map/all_to_all | solution.py:380
  61.6 0.5 broadcast.439
  62.2 0.7 fusion.34
  62.9 0.2 select_reduce_fusion.1
  63.2 0.1 select_reduce_fusion.2
  63.4 0.6 shard_map.140
  64.2 8.9 %all-to-all-done.2.refs_0_.rest_1_ = bf16[8,48,512]{2,1,0:T(8,128)(2,1)S(1)} async-done(((bf16[8,48,512]{2,1,0:T(8,128)(2,1)}), bf16[8,48,512]{2,1,0:T(8,128)(2,1)S(1)}, u32[]{:S(2)}, u32[]{:S(2)}) %all-to-all-start.2) | async-done | bytes 393248 | tf_op jit(solution)/shard_map/all_to_all | solution.py:380
  73.1 0.7 shard_map.141
  74.0 0.5 collective-permute-start.8
  74.6 5.1 %collective-permute-done.7.rest_5_ = bf16[4,48,512]{2,1,0:T(8,128)(2,1)S(1)} collective-permute-done((bf16[4,48,512]{2,1,0:T(8,128)(2,1)S(1)}, bf16[4,48,512]{2,1,0:T(8,128)(2,1)S(1)}, u32[]{:S(2)}, u32[]{:S(2)}) %collective-permute-start.7) | collective-permute-done | bytes 196640 | tf_op jit(solution)/shard_map/ppermute | solution.py:322
  79.7 0.6 pad_add_fusion.1.meta
  80.2 0.9 collective-permute-done.9.rest_7_
  81.2 0.6 copy-done.14
  81.8 0.1 copy-done.10
  81.9 0.2 copy-done.9
  82.3 31.5 %shard_map.142 = (bf16[256,2048]{1,0:T(8,128)(2,1)}, bf16[256,2048]{1,0:T(8,128)(2,1)}, f32[4,512]{1,0:T(4,128)}, f32[512,512]{1,0:T(8,128)}) custom-call(s32[25]{0:T(128)} %pad_add_fusion.1.meta, bf16[256,2048]{1,0:T(8,128)(2,1)} %bitcast.61, bf16[256,2048]{1,0:T(8,128)(2,1)} %bitcast.62, f32[4,512]{1,0:T(4,128)} %bitcast_convert_fusion.1.cond_ref, ...), custom_call_target="tpu_custom_call" | custom-call | flops 11811160064 | bytes 16777216 | tf_op jit(solution)/shard_map/pallas_call | solution.py:181
  113.8 1.1 fusion
  114.9 0.2 collective-permute-start.10
  115.1 1.4 %collective-permute-done.10 = bf16[2,8,16,512]{3,2,1,0:T(8,128)(2,1)S(1)} collective-permute-done((bf16[2,8,16,512]{3,2,1,0:T(8,128)(2,1)S(1)}, bf16[2,8,16,512]{3,2,1,0:T(8,128)(2,1)S(1)}, u32[]{:S(2)}, u32[]{:S(2)}) %collective-permute-start.10) | collective-permute-done | bytes 262176 | tf_op jit(solution)/shard_map/ppermute | solution.py:287
  116.5 1.1 bitcast_add_fusion
  117.6 0.3 collective-permute-start.11
  118.0 5.3 %collective-permute-done.11 = bf16[1,8,16,512]{3,2,1,0:T(8,128)(2,1)S(1)} collective-permute-done((bf16[1,8,16,512]{3,2,1,0:T(8,128)(2,1)S(1)}, bf16[1,8,16,512]{3,2,1,0:T(8,128)(2,1)S(1)}, u32[]{:S(2)}, u32[]{:S(2)}) %collective-permute-start.11) | collective-permute-done | bytes 131104 | tf_op jit(solution)/shard_map/ppermute | solution.py:287
  123.3 11.8 %all_to_all.20 = bf16[8,1,16,512]{3,2,1,0:T(8,128)(2,1)S(1)} all-to-all(bf16[8,1,16,512]{3,2,1,0:T(8,128)(2,1)S(1)} %fusion.1), channel_id=1, replica_groups=mesh['pool'=4,'dp'=8] {'dp'}, dimensions={0} | all-to-all | bytes 262144 | tf_op jit(solution)/shard_map/all_to_all | solution.py:276
  135.1 0.6 convert_reduce_fusion
  (77 shorter events, 2.3 us)
Async XLA Ops:
  0.6 3.3 %copy-start.6 = (s32[1,1,4,2]{2,3,1,0:T(2,128)S(1)}, s32[1,1,4,2]{2,3,1,0:T(2,128)}, u32[]{:S(2)}) copy-start(s32[1,1,4,2]{2,3,1,0:T(2,128)} %param.14) | copy-start | bytes 100
  0.6 3.5 %copy-start.7 = (s32[1,1,4,2]{2,3,1,0:T(2,128)S(1)}, s32[1,1,4,2]{2,3,1,0:T(2,128)}, u32[]{:S(2)}) copy-start(s32[1,1,4,2]{2,3,1,0:T(2,128)} %param.15) | copy-start | bytes 100
  0.7 3.6 %copy-start.8 = (s32[1,1,16]{2,1,0:T(1,128)S(1)}, s32[1,1,16]{2,1,0:T(1,128)}, u32[]{:S(2)}) copy-start(s32[1,1,16]{2,1,0:T(1,128)} %param.17) | copy-start | bytes 196
  3.2 21.1 %collective-permute-start = (bf16[16,80,512]{2,1,0:T(8,128)(2,1)}, bf16[16,80,512]{2,1,0:T(8,128)(2,1)S(1)}, u32[]{:S(2)}, u32[]{:S(2)}) collective-permute-start(bf16[16,80,512]{2,1,0:T(8,128)(2,1)} %slice.28), channel_id=1, source_target_pairs={{24,8},{25,9},{26,10},{27,11},{28,12},{29,13},{30,14},{31,15}} | collective-permute-start | bytes 3932168 | tf_op jit(solution)/shard_map/ppermute | solution.py:322
  5.0 19.3 %all-to-all-start = ((s32[32,1,128]{2,1,0:T(1,128)}), s32[32,1,128]{2,1,0:T(1,128)S(1)}, u32[]{:S(2)}, u32[]{:S(2)}) async-start(s32[32,1,128]{2,1,0:T(1,128)} %broadcast_in_dim.87), calls=%async_computation | async-start | bytes 32768 | tf_op jit(solution)/shard_map/all_to_all | solution.py:335
  13.4 12.0 %copy-start.2 = (bf16[1,1,16,128,512]{4,3,2,1,0:T(8,128)(2,1)S(1)}, bf16[1,1,16,128,512]{4,3,2,1,0:T(8,128)(2,1)}, u32[]{:S(2)}) copy-start(bf16[1,1,16,128,512]{4,3,2,1,0:T(8,128)(2,1)} %param.16) | copy-start | bytes 6291460
  24.3 1.1 copy-start.3
  26.8 5.6 %collective-permute-start.1 = (bf16[16,80,512]{2,1,0:T(8,128)(2,1)S(1)}, bf16[16,80,512]{2,1,0:T(8,128)(2,1)S(1)}, u32[]{:S(2)}, u32[]{:S(2)}) collective-permute-start(bf16[16,80,512]{2,1,0:T(8,128)(2,1)S(1)} %broadcast_select_fusion.refs_0_), channel_id=1, source_target_pairs={{24,16},{25,17},{26,18},{27,19},{28,20},{29,21},{30,22},{31,23},{8... | collective-permute-start | bytes 3932168 | tf_op jit(solution)/shard_map/ppermute | solution.py:322
  30.3 8.5 %collective-permute-start.2 = (bf16[16,48,512]{2,1,0:T(8,128)(2,1)}, bf16[16,48,512]{2,1,0:T(8,128)(2,1)S(1)}, u32[]{:S(2)}, u32[]{:S(2)}) collective-permute-start(bf16[16,48,512]{2,1,0:T(8,128)(2,1)} %slice.27), channel_id=1, source_target_pairs={{24,8},{25,9},{26,10},{27,11},{28,12},{29,13},{30,14},{31,15}} | collective-permute-start | bytes 2359304 | tf_op jit(solution)/shard_map/ppermute | solution.py:322
  33.9 23.3 %all-to-all-start.1 = ((bf16[8,80,512]{2,1,0:T(8,128)(2,1)}), bf16[8,80,512]{2,1,0:T(8,128)(2,1)S(1)}, u32[]{:S(2)}, u32[]{:S(2)}) async-start(bf16[8,80,512]{2,1,0:T(8,128)(2,1)} %shard_map.138), calls=%async_computation.1 | async-start | bytes 1310720 | tf_op jit(solution)/shard_map/all_to_all | solution.py:380
  38.8 2.6 %copy-start.4 = (bf16[512,256]{1,0:T(8,128)(2,1)S(1)}, bf16[512,256]{1,0:T(8,128)(2,1)}, u32[]{:S(2)}) copy-start(bf16[512,256]{1,0:T(8,128)(2,1)} %down_ref.1) | copy-start | bytes 786436
  38.8 5.3 %copy-start.5 = (bf16[1,1,4,512]{3,2,1,0:T(4,128)(2,1)S(1)}, bf16[1,1,4,512]{3,2,1,0:T(4,128)(2,1)}, u32[]{:S(2)}) copy-start(bf16[1,1,4,512]{3,2,1,0:T(4,128)(2,1)} %param.13) | copy-start | bytes 12292
  40.1 9.0 %collective-permute-start.3 = (bf16[16,48,512]{2,1,0:T(8,128)(2,1)S(1)}, bf16[16,48,512]{2,1,0:T(8,128)(2,1)S(1)}, u32[]{:S(2)}, u32[]{:S(2)}) collective-permute-start(bf16[16,48,512]{2,1,0:T(8,128)(2,1)S(1)} %broadcast_select_fusion.1.refs_0_), channel_id=1, source_target_pairs={{24,16},{25,17},{26,18},{27,19},{28,20},{29,21},{30,22},{31,23},{8... | collective-permute-start | bytes 2359304 | tf_op jit(solution)/shard_map/ppermute | solution.py:322
  57.2 23.9 %copy-start = (bf16[8,80,512]{2,1,0:T(8,128)(2,1)}, bf16[8,80,512]{2,1,0:T(8,128)(2,1)S(1)}, u32[]{:S(2)}) copy-start(bf16[8,80,512]{2,1,0:T(8,128)(2,1)S(1)} %all-to-all-done.1.refs_0_.rest_0_) | copy-start | bytes 1966084
  57.2 15.9 %all-to-all-start.2 = ((bf16[8,48,512]{2,1,0:T(8,128)(2,1)}), bf16[8,48,512]{2,1,0:T(8,128)(2,1)S(1)}, u32[]{:S(2)}, u32[]{:S(2)}) async-start(bf16[8,48,512]{2,1,0:T(8,128)(2,1)} %shard_map.139), calls=%async_computation.2 | async-start | bytes 786432 | tf_op jit(solution)/shard_map/all_to_all | solution.py:380
  64.0 10.0 %collective-permute-start.6 = (bf16[4,80,512]{2,1,0:T(8,128)(2,1)S(1)}, bf16[4,80,512]{2,1,0:T(8,128)(2,1)S(1)}, u32[]{:S(2)}, u32[]{:S(2)}) collective-permute-start(bf16[4,80,512]{2,1,0:T(8,128)(2,1)S(1)} %shard_map.140), channel_id=1, source_target_pairs={{0,16},{1,17},{2,18},{3,19},{4,20},{5,21},{6,22},{7,23},{8,24},{9,... | collective-permute-start | bytes 983048 | tf_op jit(solution)/shard_map/ppermute | solution.py:322
  64.0 17.1 %collective-permute-start.4 = (bf16[8,80,512]{2,1,0:T(8,128)(2,1)S(1)}, bf16[8,80,512]{2,1,0:T(8,128)(2,1)S(1)}, u32[]{:S(2)}, u32[]{:S(2)}) collective-permute-start(bf16[8,80,512]{2,1,0:T(8,128)(2,1)S(1)} %all-to-all-done.1.refs_0_.rest_0_), channel_id=1, source_target_pairs={{0,8},{1,9},{2,10},{3,11},{4,12},{5,13},{6,14},{7,15},{8,0},{9,1},... | collective-permute-start | bytes 1966088 | tf_op jit(solution)/shard_map/ppermute | solution.py:322
  73.1 8.1 %copy-start.1 = (bf16[8,48,512]{2,1,0:T(8,128)(2,1)}, bf16[8,48,512]{2,1,0:T(8,128)(2,1)S(1)}, u32[]{:S(2)}) copy-start(bf16[8,48,512]{2,1,0:T(8,128)(2,1)S(1)} %all-to-all-done.2.refs_0_.rest_1_) | copy-start | bytes 1179652
  73.8 5.8 %collective-permute-start.7 = (bf16[4,48,512]{2,1,0:T(8,128)(2,1)S(1)}, bf16[4,48,512]{2,1,0:T(8,128)(2,1)S(1)}, u32[]{:S(2)}, u32[]{:S(2)}) collective-permute-start(bf16[4,48,512]{2,1,0:T(8,128)(2,1)S(1)} %shard_map.141), channel_id=1, source_target_pairs={{0,16},{1,17},{2,18},{3,19},{4,20},{5,21},{6,22},{7,23},{8,24},{9,... | collective-permute-start | bytes 589832 | tf_op jit(solution)/shard_map/ppermute | solution.py:322
  73.9 7.2 %collective-permute-start.5 = (bf16[8,48,512]{2,1,0:T(8,128)(2,1)S(1)}, bf16[8,48,512]{2,1,0:T(8,128)(2,1)S(1)}, u32[]{:S(2)}, u32[]{:S(2)}) collective-permute-start(bf16[8,48,512]{2,1,0:T(8,128)(2,1)S(1)} %all-to-all-done.2.refs_0_.rest_1_), channel_id=1, source_target_pairs={{0,8},{1,9},{2,10},{3,11},{4,12},{5,13},{6,14},{7,15},{8,0},{9,1},... | collective-permute-start | bytes 1179656 | tf_op jit(solution)/shard_map/ppermute | solution.py:322
  74.0 7.2 %copy-start.11 = (bf16[4,80,512]{2,1,0:T(8,128)(2,1)}, bf16[4,80,512]{2,1,0:T(8,128)(2,1)S(1)}, u32[]{:S(2)}) copy-start(bf16[4,80,512]{2,1,0:T(8,128)(2,1)S(1)} %collective-permute-done.6.rest_4_) | copy-start | bytes 983044
  74.0 7.1 %collective-permute-start.8 = (bf16[4,80,512]{2,1,0:T(8,128)(2,1)S(1)}, bf16[4,80,512]{2,1,0:T(8,128)(2,1)S(1)}, u32[]{:S(2)}, u32[]{:S(2)}) collective-permute-start(bf16[4,80,512]{2,1,0:T(8,128)(2,1)S(1)} %collective-permute-done.6.rest_4_), channel_id=1, source_target_pairs={{0,8},{1,9},{2,10},{3,11},{4,12},{5,13},{6,14},{7,15},{8,0},{9,1},... | collective-permute-start | bytes 983048 | tf_op jit(solution)/shard_map/ppermute | solution.py:322
  79.7 1.5 %copy-start.13 = (bf16[4,48,512]{2,1,0:T(8,128)(2,1)}, bf16[4,48,512]{2,1,0:T(8,128)(2,1)S(1)}, u32[]{:S(2)}) copy-start(bf16[4,48,512]{2,1,0:T(8,128)(2,1)S(1)} %collective-permute-done.7.rest_5_) | copy-start | bytes 589828
  79.7 1.4 %collective-permute-start.9 = (bf16[4,48,512]{2,1,0:T(8,128)(2,1)S(1)}, bf16[4,48,512]{2,1,0:T(8,128)(2,1)S(1)}, u32[]{:S(2)}, u32[]{:S(2)}) collective-permute-start(bf16[4,48,512]{2,1,0:T(8,128)(2,1)S(1)} %collective-permute-done.7.rest_5_), channel_id=1, source_target_pairs={{0,8},{1,9},{2,10},{3,11},{4,12},{5,13},{6,14},{7,15},{8,0},{9,1},... | collective-permute-start | bytes 589832 | tf_op jit(solution)/shard_map/ppermute | solution.py:322
  81.1 0.7 copy-start.14
  81.1 0.8 copy-start.10
  81.1 1.1 copy-start.9
  81.1 1.1 copy-start.12
  114.9 1.6 %collective-permute-start.10 = (bf16[2,8,16,512]{3,2,1,0:T(8,128)(2,1)S(1)}, bf16[2,8,16,512]{3,2,1,0:T(8,128)(2,1)S(1)}, u32[]{:S(2)}, u32[]{:S(2)}) collective-permute-start(bf16[2,8,16,512]{3,2,1,0:T(8,128)(2,1)S(1)} %fusion), channel_id=1, source_target_pairs={{0,8},{8,0},{16,24},{24,16},{1,9},{9,1},{17,25},{25,17},{2,10},{10... | collective-permute-start | bytes 786440 | tf_op jit(solution)/shard_map/ppermute | solution.py:287
  117.6 5.6 %collective-permute-start.11 = (bf16[1,8,16,512]{3,2,1,0:T(8,128)(2,1)S(1)}, bf16[1,8,16,512]{3,2,1,0:T(8,128)(2,1)S(1)}, u32[]{:S(2)}, u32[]{:S(2)}) collective-permute-start(bf16[1,8,16,512]{3,2,1,0:T(8,128)(2,1)S(1)} %dynamic-slice_convert_fusion), channel_id=1, source_target_pairs={{0,16},{8,24},{16,0},{24,8},{1,17},{9,25},{17,1},{25,9},{2,18},{10... | collective-permute-start | bytes 393224 | tf_op jit(solution)/shard_map/ppermute | solution.py:287

commit v15 on v14

--- a/solution.py
+++ b/solution.py
@@ -25,12 +25,12 @@
 
 
 def span_kernel(
-    held_count, nbr_count, bounds, meta,
+    held_count, nbr_count, bounds, pool_count, meta,
     q_ref, cot_ref, cond_ref, gain_ref, down_ref, up_ref, upt_ref, downt_ref, *rest,
 ):
     held_refs = rest[:held_count]
-    (kv_hbm, kvt_hbm, out_ref, qg_ref, cg_ref, ad_ref,
-     raw_ref, kv_ref, kvt_ref, proj_ref, grad_ref,
+    (kv_hbm, kvt_hbm, out_ref, qg_ref, cg_ref, keep_ref, give_ref,
+     raw_ref, kv_ref, kvt_ref, proj_ref, grad_ref, score_ref, dprob_ref, prob_ref, dscore_ref,
      q2_ref, cot2_ref, acc_ref, sems, kv_sem) = rest[held_count:]
     step = pl.program_id(0)
     per_device, slot_len, width = raw_ref.shape
@@ -41,11 +41,12 @@
     rank = down_ref.shape[1]
     scaling = HEAD ** (-0.5)
     live = meta[0] == 1
-    lens, which, index = 1, 1 + per_device, 1 + 2 * per_device
+    lens, which, index = 2, 2 + per_device, 2 + 2 * per_device
     parts = len(bounds) - 1
     cuts = [pl.ds(low, high - low) for low, high in zip(bounds, bounds[1:])]
     pairs = [pl.ds(i * 2 * HEAD, 2 * HEAD) for i in range(HEADS // 2)]
     value_pairs = [pl.ds(head_cols + i * 2 * HEAD, 2 * HEAD) for i in range(HEADS // 2)]
+    lanes = [pl.ds(i * 2 * SPAN, 2 * SPAN) for i in range(HEADS // 2)]
     keys = [pl.ds(g * key_count, key_count) for g in range(group)]
     tokens = [pl.ds(g * SPAN, SPAN) for g in range(group)]
     double = [pl.ds(g * 2 * SPAN, 2 * SPAN) for g in range(group)]
@@ -104,39 +105,62 @@
     def _():
         kv_copy.wait()
 
-    for cols in pairs + value_pairs:
-        proj_ref[:, cols] = dot(encoded, kv_ref[:, cols]).astype(jnp.bfloat16)
-
-    def diagonal(both):
-        return jnp.concatenate([both[:SPAN, :HEAD], both[SPAN:, HEAD:]], axis=1)
-
     slot = lax.broadcasted_iota(jnp.int32, (key_count, 2 * SPAN), 0)
+    usable = []
     for g in range(group):
         limit = jnp.zeros((key_count, 2 * SPAN), jnp.int32)
         for n in range(nbr_count):
             here = jnp.logical_and(slot >= n * slot_len, slot < (n + 1) * slot_len)
             item = (step * group + g) * nbr_count + n
             limit = jnp.where(here, n * slot_len + meta[lens + item], limit)
-        usable = slot < limit
-        for cols, value_cols in zip(pairs, value_pairs):
-            q2 = q2_ref[double[g], cols]
-            cot2 = cot2_ref[double[g], cols]
-            key_rows = proj_ref[keys[g], cols]
-            value_rows = proj_ref[keys[g], value_cols]
-            scores = jnp.where(usable, dot(key_rows, q2, NT), FLOOR)
-            row_max = jnp.max(scores, axis=0, keepdims=True)
-            raised = jnp.exp2((scores - row_max) * (scaling * LOG2E))
-            probs = raised * (1.0 / jnp.sum(raised, axis=0, keepdims=True))
-            d_probs = dot(value_rows, cot2, NT)
-            delta = jnp.sum(probs * d_probs, axis=0, keepdims=True)
-            probs_b = probs.astype(jnp.bfloat16)
-            d_scores = (probs * (d_probs - delta) * scaling).astype(jnp.bfloat16)
-            grad_ref[keys[g], cols] = dot(d_scores, q2).astype(jnp.bfloat16)
-            grad_ref[keys[g], value_cols] = dot(probs_b, cot2).astype(jnp.bfloat16)
-            out = diagonal(dot(probs_b.T, value_rows))
-            grad = diagonal(dot(d_scores.T, key_rows))
-            out_ref[tokens[g], cols] = jnp.where(live, out, 0.0).astype(jnp.bfloat16)
-            qg_ref[tokens[g], cols] = jnp.where(live, grad, 0.0).astype(jnp.bfloat16)
+        usable.append(limit)
+
+    def diagonal(both):
+        return jnp.concatenate([both[:SPAN, :HEAD], both[SPAN:, HEAD:]], axis=1)
+
+    def project(i):
+        for cols in (pairs[i], value_pairs[i]):
+            proj_ref[:, cols] = dot(encoded, kv_ref[:, cols]).astype(jnp.bfloat16)
+
+    def score(i, g):
+        score_ref[keys[g], lanes[i]] = dot(proj_ref[keys[g], pairs[i]], q2_ref[double[g], pairs[i]], NT)
+        dprob_ref[keys[g], lanes[i]] = dot(
+            proj_ref[keys[g], value_pairs[i]], cot2_ref[double[g], pairs[i]], NT
+        )
+
+    def soften(i, g):
+        scores = jnp.where(slot < usable[g], score_ref[keys[g], lanes[i]], FLOOR)
+        row_max = jnp.max(scores, axis=0, keepdims=True)
+        raised = jnp.exp2((scores - row_max) * (scaling * LOG2E))
+        probs = raised * (1.0 / jnp.sum(raised, axis=0, keepdims=True))
+        d_probs = dprob_ref[keys[g], lanes[i]]
+        delta = jnp.sum(probs * d_probs, axis=0, keepdims=True)
+        prob_ref[keys[g], lanes[i]] = probs.astype(jnp.bfloat16)
+        dscore_ref[keys[g], lanes[i]] = (probs * (d_probs - delta) * scaling).astype(jnp.bfloat16)
+
+    def multiply(i, g):
+        probs, d_scores = prob_ref[keys[g], lanes[i]], dscore_ref[keys[g], lanes[i]]
+        grad_ref[keys[g], pairs[i]] = dot(d_scores, q2_ref[double[g], pairs[i]]).astype(jnp.bfloat16)
+        grad_ref[keys[g], value_pairs[i]] = dot(probs, cot2_ref[double[g], pairs[i]]).astype(
+            jnp.bfloat16
+        )
+        out = diagonal(dot(probs.T, proj_ref[keys[g], value_pairs[i]]))
+        grad = diagonal(dot(d_scores.T, proj_ref[keys[g], pairs[i]]))
+        out_ref[tokens[g], pairs[i]] = jnp.where(live, out, 0.0).astype(jnp.bfloat16)
+        qg_ref[tokens[g], pairs[i]] = jnp.where(live, grad, 0.0).astype(jnp.bfloat16)
+
+    spots = [(i, g) for i in range(HEADS // 2) for g in range(group)]
+    project(0)
+    score(*spots[0])
+    for k, spot in enumerate(spots):
+        if spot[1] == 0 and spot[0] + 1 < HEADS // 2:
+            project(spot[0] + 1)
+        if k + 1 < len(spots):
+            score(*spots[k + 1])
+        soften(*spot)
+        if k:
+            multiply(*spots[k - 1])
+    multiply(*spots[-1])
 
     @pl.when(step == 0)
     def _():
@@ -160,10 +184,15 @@
 
     @pl.when(step == pl.num_programs(0) - 1)
     def _():
-        ad_ref[...] = jnp.where(live, acc_ref[...], 0.0).astype(ad_ref.dtype)
-
-
-def run_spans(meta, query, cot, cond, held, bounds, gain, w_down, w_up, w_kv, w_kv_t, nbr_count):
+        chunk = width // pool_count
+        for k in range(pool_count // 2):
+            part = pl.ds(k * chunk, chunk)
+            for ref, own in ((keep_ref, meta[1]), (give_ref, 1 - meta[1])):
+                rows = acc_ref[pl.ds(pl.multiple_of((2 * k + own) * chunk, chunk), chunk), :]
+                ref[part, :] = jnp.where(live, rows, 0.0).astype(ref.dtype)
+
+
+def run_spans(meta, query, cot, cond, held, bounds, gain, w_down, w_up, w_kv, w_kv_t, nbr_count, pool_count):
     span_count, width = cond.shape
     token_count, head_cols = query.shape
     slot_len = bounds[-1]
@@ -179,7 +208,7 @@
     rows = per_device * slot_len
     flops = 2 * rows * (2 * width * 2 * head_cols + 6 * width * rank + 6 * SPAN * head_cols)
     return pl.pallas_call(
-        functools.partial(span_kernel, len(held), nbr_count, bounds),
+        functools.partial(span_kernel, len(held), nbr_count, bounds, pool_count),
         grid_spec=pltpu.PrefetchScalarGridSpec(
             num_scalar_prefetch=1,
             grid=(span_count // group,),
@@ -190,7 +219,8 @@
                 tokens,
                 tokens,
                 pl.BlockSpec((span_count, width), lambda s, m: (0, 0)),
-                pl.BlockSpec((width, 2 * rank), lambda s, m: (0, 0)),
+                pl.BlockSpec((width // 2, 2 * rank), lambda s, m: (0, 0)),
+                pl.BlockSpec((width // 2, 2 * rank), lambda s, m: (0, 0)),
             ],
             scratch_shapes=[
                 pltpu.VMEM((per_device, slot_len, width), jnp.bfloat16),
@@ -198,6 +228,10 @@
                 pltpu.VMEM((2 * head_cols, width), jnp.bfloat16),
                 pltpu.VMEM((keys, 2 * head_cols), jnp.bfloat16),
                 pltpu.VMEM((keys, 2 * head_cols), jnp.bfloat16),
+                pltpu.VMEM((keys, SPAN * HEADS), jnp.float32),
+                pltpu.VMEM((keys, SPAN * HEADS), jnp.float32),
+                pltpu.VMEM((keys, SPAN * HEADS), jnp.bfloat16),
+                pltpu.VMEM((keys, SPAN * HEADS), jnp.bfloat16),
                 pltpu.VMEM((group * 2 * SPAN, head_cols), jnp.bfloat16),
                 pltpu.VMEM((group * 2 * SPAN, head_cols), jnp.bfloat16),
                 pltpu.VMEM((width, 2 * rank), jnp.float32),
@@ -209,7 +243,8 @@
             jax.ShapeDtypeStruct((token_count, head_cols), jnp.bfloat16),
             jax.ShapeDtypeStruct((token_count, head_cols), jnp.bfloat16),
             jax.ShapeDtypeStruct((span_count, width), jnp.float32),
-            jax.ShapeDtypeStruct((width, 2 * rank), jnp.float32),
+            jax.ShapeDtypeStruct((width // 2, 2 * rank), jnp.float32),
+            jax.ShapeDtypeStruct((width // 2, 2 * rank), jnp.bfloat16),
         ],
         compiler_params=pltpu.CompilerParams(vmem_limit_bytes=60 * 2**20),
         cost_estimate=pl.CostEstimate(
@@ -264,32 +299,23 @@
     return row, lane // half, crosses, number // half
 
 
-def scatter_sum(total, axes):
-    width = total.shape[1]
-    sizes = [lax.axis_size(axis) for axis in axes]
-    total = total.reshape(tuple(sizes) + (-1, width)).astype(jnp.float32)
-    for at, axis in enumerate(axes):
-        size, index = sizes[at], lax.axis_index(axis)
-        if size > 4 or size & (size - 1):
-            lead = (size,) + tuple(d for i, d in enumerate(total.shape) if i != at)
-            parts = jnp.moveaxis(total, at, 0).astype(jnp.bfloat16)
-            parts = lax.all_to_all(parts, axis, split_axis=0, concat_axis=0, tiled=True)
-            total = jnp.sum(parts.reshape(lead).astype(jnp.float32), axis=0)
-            total = jnp.expand_dims(total, at)
-            continue
-        bit = 1
-        while bit < size:
-            shape = total.shape
-            split = total.reshape(shape[:at] + (shape[at] // 2, 2) + shape[at + 1 :])
-            mine = (index // bit) % 2
-            keep = lax.dynamic_index_in_dim(split, mine, at + 1, keepdims=False)
-            give = lax.dynamic_index_in_dim(split, 1 - mine, at + 1, keepdims=False)
-            got = lax.ppermute(
-                give.astype(jnp.bfloat16), axis, [(i, i ^ bit) for i in range(size)]
-            )
-            total = keep + got.astype(jnp.float32)
-            bit *= 2
-    return total.reshape(-1, width)
+def scatter_sum(keep, give, axes):
+    width = keep.shape[1]
+    size, columns = (lax.axis_size(axis) for axis in axes)
+    index = lax.axis_index(axes[0])
+    swap = lambda a, bit: lax.ppermute(a, axes[0], [(i, i ^ bit) for i in range(size)])
+    total = keep + swap(give, 1).astype(jnp.float32)
+    bit = 2
+    while bit < size:
+        split = total.reshape(size // bit // 2, 2, -1, width)
+        mine = (index // bit) % 2
+        keep = lax.dynamic_index_in_dim(split, mine, 1, keepdims=False)
+        give = lax.dynamic_index_in_dim(split, 1 - mine, 1, keepdims=False)
+        total = keep + swap(give.astype(jnp.bfloat16), bit).astype(jnp.float32)
+        bit *= 2
+    parts = total.reshape(columns, -1, width).astype(jnp.bfloat16)
+    parts = lax.all_to_all(parts, axes[1], split_axis=0, concat_axis=0, tiled=True)
+    return jnp.sum(parts.astype(jnp.float32), axis=0)
 
 
 def body(
@@ -323,7 +349,7 @@
             array, axes, [(a * columns + j, b * columns + j) for a, b in pairs for j in range(columns)]
         )
 
-    first = slot_len // 16 * 5 // 8 * 16
+    first = slot_len // 16 * 3 // 4 * 16
     bounds = [0, first, slot_len] if 0 < first < slot_len else [0, slot_len]
     parts = len(bounds) - 1
     full_store = database.reshape(block_count, slot_len, width)
@@ -368,6 +394,20 @@
     def share(array, step):
         return hop(array, [(p, p // half * half + (p + step) % half) for p in range(pool_count)])
 
+    origin = jnp.where(my_cross, (my_carrier + half) % pool_count, my_carrier)
+    which = (row - origin) % half + jnp.where(my_cross, half, 0)
+    index = jnp.where(my_cross, my_number, place)
+    own_row = jnp.minimum(row, relay_row - 1)
+    hot = (my_owner * block_count + my_block)[:, None] == jnp.arange(
+        columns * block_count, dtype=jnp.int32
+    )[None, :]
+    wanted_len = jnp.sum(jnp.where(hot, store_len.reshape(1, -1), 0), axis=1)
+    own = lambda a: lax.dynamic_index_in_dim(
+        a.reshape(relay_row, per_device), own_row, 0, keepdims=False
+    )
+    flags = jnp.stack([(row < relay_row).astype(jnp.int32), row % 2])
+    meta = jnp.concatenate([flags, own(wanted_len), own(which), own(index)]).astype(jnp.int32)
+
     held = []
     for i in range(parts):
         near = jnp.where(row == relay_row, store[i], across[i])
@@ -376,6 +416,8 @@
         for step in range(1, half):
             stores.append(hop(near, [(p, p - step) for p in (relay_row, relay_row - half)]))
             held_by = jnp.where(row % half == half - 1 - step, step, held_by)
+        if i:
+            slot_block, meta = lax.optimization_barrier((slot_block, meta))
         sends = pick(held_by, slot_block, stores)
         arrived = lax.all_to_all(sends, "dp", split_axis=0, concat_axis=0, tiled=True)
         here = [arrived] + [share(arrived, step) for step in range(1, half)]
@@ -384,23 +426,9 @@
             landed = hop(leaving, [(p, (p + half) % pool_count) for p in range(pool_count)])
             here += [landed] + [share(landed, step) for step in range(1, half)]
         held.append(here)
-    origin = jnp.where(my_cross, (my_carrier + half) % pool_count, my_carrier)
-    which = (row - origin) % half + jnp.where(my_cross, half, 0)
-    index = jnp.where(my_cross, my_number, place)
     held = [here[b] for b in range(len(held[0])) for here in held]
 
-    own_row = jnp.minimum(row, relay_row - 1)
-    hot = (my_owner * block_count + my_block)[:, None] == jnp.arange(
-        columns * block_count, dtype=jnp.int32
-    )[None, :]
-    wanted_len = jnp.sum(jnp.where(hot, store_len.reshape(1, -1), 0), axis=1)
-    own = lambda a: lax.dynamic_index_in_dim(
-        a.reshape(relay_row, per_device), own_row, 0, keepdims=False
-    )
-    live = (row < relay_row).astype(jnp.int32)
-    meta = jnp.concatenate([live[None], own(wanted_len), own(which), own(index)]).astype(jnp.int32)
-
-    attn_out, q_grad, cond_grad, terms = run_spans(
+    attn_out, q_grad, cond_grad, keep, give = run_spans(
         meta,
         queries.reshape(token_count, head_cols),
         cotangent.reshape(token_count, head_cols),
@@ -413,9 +441,10 @@
         w_kv,
         w_kv_t,
         nbr_count,
-    )
-
-    adapter_grad = scatter_sum(terms, axes)
+        pool_count,
+    )
+
+    adapter_grad = scatter_sum(keep, give, axes)
     return (
         attn_out.reshape(1, 1, token_count, head_cols),
         q_grad.reshape(1, 1, token_count, head_cols),

time: 137 us -> 135 us (0.985)
  waiting for transfers between devices: 37 us -> 44 us
  Pallas kernels: 35.6 us -> 29.8 us
  local copies, waits for them, and re-layouts: 19.7 us -> 15.8 us
    ppermute x10, waiting for transfers between devices: 10.3 us -> 17.2 us  [hop(): lax.ppermute(array, axes, [(a * columns + j, b * columns + j) for a, b in...]
    pallas_call x1, Pallas kernels: 31.5 us -> 25.7 us  [run_spans(): pl.pallas_call(functools.partial(span_kernel, len(held), nbr_count, bound...]
    all_to_all x2, waiting for transfers between devices: 15.8 us -> 12.9 us  [body(): lax.all_to_all(sends, 'dp', split_axis=0, concat_axis=0, tiled=True)]
    all_to_all x1, waiting for transfers between devices: 4.29 us -> 7 us  [to_all(): return lax.all_to_all(copies, axis, split_axis=0, concat_axis=0, tiled=True)]
    unnamed x35 -> x31, local copies, waits for them, and re-layouts: 11.7 us -> 9.34 us
  transfers between devices with their start and end apart: 15 -> 15, of which waited for: 8 -> 8; matrix products, arithmetic and copies ran while one was open for 14% -> 13% of each run, Pallas kernels for 3% -> 3%
where the time goes in v15:
time: 135 us; the launch traced here: 134 us
  waiting for transfers between devices  44 us (33%)
  Pallas kernels  29.8 us (22%)
  starting transfers between devices  22.8 us (17%)
  local copies, waits for them, and re-layouts  15.8 us (12%)
  blocking collectives  12.8 us (9%)
  other arithmetic  7.78 us (6%)
    pallas_call x1, Pallas kernels, run_spans(): pl.pallas_call(functools.partial(span_kernel, len(held), nbr_count, bound...  25.7 us
    ppermute x10, waiting for transfers between devices, hop(): lax.ppermute(array, axes, [(a * columns + j, b * columns + j) for a, b in...  17.2 us
    all_to_all x2, waiting for transfers between devices, body(): lax.all_to_all(sends, 'dp', split_axis=0, concat_axis=0, tiled=True)  12.9 us
    all_to_all x1, blocking collectives, scatter_sum(): lax.all_to_all(parts, axes[1], split_axis=0, concat_axis=0, tiled=True)  12.8 us
    unnamed x31, local copies, waits for them, and re-layouts  9.34 us
    all_to_all x2, starting transfers between devices, body(): lax.all_to_all(sends, 'dp', split_axis=0, concat_axis=0, tiled=True)  8.39 us
    all_to_all x1, starting transfers between devices, to_all(): return lax.all_to_all(copies, axis, split_axis=0, concat_axis=0, tiled=True)  8.23 us
    all_to_all x1, waiting for transfers between devices, to_all(): return lax.all_to_all(copies, axis, split_axis=0, concat_axis=0, tiled=True)  7 us
  transfers between devices with their start and end apart: 15, of which 8 were waited for; matrix products, arithmetic and copies ran while one was open for 13% of the time, Pallas kernels for 3%

profile of v15, /device:TPU:0, one launch (start us, length us, event | category | flops | bytes accessed | tf_op | source)
XLA Modules:
  0.0 134.0 jit_solution(17488801765770346306)
XLA Ops:
  0.7 1.6 %slice.28 = bf16[16,96,512]{2,1,0:T(8,128)(2,1)S(1)} slice(bf16[16,128,512]{2,1,0:T(8,128)(2,1)} %bitcast.45), slice={[0:16], [0:96], [0:512]} | slice | bytes 3145728 | tf_op jit(solution)/shard_map/slice | solution.py:356
  2.2 0.8 collective-permute-start
  3.0 0.1 copy.43
  3.5 0.6 broadcast_in_dim.52
  4.1 8.2 %all-to-all-start = ((s32[32,1,128]{2,1,0:T(1,128)}), s32[32,1,128]{2,1,0:T(1,128)S(1)}, u32[]{:S(2)}, u32[]{:S(2)}) async-start(s32[32,1,128]{2,1,0:T(1,128)} %broadcast_in_dim.52), calls=%async_computation | async-start | bytes 32768 | tf_op jit(solution)/shard_map/all_to_all | solution.py:361
  12.5 6.5 %copy.45 = bf16[512,4096]{0,1:T(8,128)(2,1)} copy(bf16[512,4096]{1,0:T(8,128)(2,1)} %rest_8_.1) | data formatting | bytes 8388608 | tf_op args[10]
  19.0 7.0 %all-to-all-done = s32[32,1,128]{2,1,0:T(1,128)S(1)} async-done(((s32[32,1,128]{2,1,0:T(1,128)}), s32[32,1,128]{2,1,0:T(1,128)S(1)}, u32[]{:S(2)}, u32[]{:S(2)}) %all-to-all-start) | async-done | bytes 16416 | tf_op jit(solution)/shard_map/all_to_all | solution.py:361
  26.1 1.6 %broadcast_select_fusion.refs_0_ = bf16[16,96,512]{2,1,0:T(8,128)(2,1)S(1)} fusion(bf16[16,96,512]{2,1,0:T(8,128)(2,1)S(1)} %collective-permute-done, pred[]{:T(512)S(6)} %eq.148, bf16[16,128,512]{2,1,0:T(8,128)(2,1)} %bitcast.46), kind=kLoop, calls=%fused_computation | loop fusion | flops 786432 | bytes 4718593 | tf_op jit(solution)/shard_map/jit(_where)/select_n | solution.py:413
  27.7 1.3 collective-permute-start.1
  29.1 0.3 convert_reduce_fusion.4
  29.5 0.6 convert_reduce_fusion.1
  30.5 1.9 %slice.27 = bf16[16,32,512]{2,1,0:T(8,128)(2,1)} slice(bf16[16,128,512]{2,1,0:T(8,128)(2,1)} %bitcast.47), slice={[0:16], [96:128], [0:512]} | slice | bytes 1048576 | tf_op jit(solution)/shard_map/slice | solution.py:356
  32.4 1.5 %collective-permute-start.2 = (bf16[16,32,512]{2,1,0:T(8,128)(2,1)}, bf16[16,32,512]{2,1,0:T(8,128)(2,1)}, u32[]{:S(2)}, u32[]{:S(2)}) collective-permute-start(bf16[16,32,512]{2,1,0:T(8,128)(2,1)} %slice.27), channel_id=1, source_target_pairs={{24,8},{25,9},{26,10},{27,11},{28,12},{29,13},{30,14},{31,15}} | collective-permute-start | bytes 1572872 | tf_op jit(solution)/shard_map/ppermute | solution.py:348
  33.8 0.2 fusion.36
  34.1 1.5 %shard_map.138 = bf16[8,96,512]{2,1,0:T(8,128)(2,1)} custom-call(s32[9]{0:T(128)S(1)} %pad_add_fusion.1.meta, bf16[16,96,512]{2,1,0:T(8,128)(2,1)S(1)} %broadcast_select_fusion.refs_0_, bf16[16,96,512]{2,1,0:T(8,128)(2,1)S(1)} %collective-permute-done.1.refs_1_), custom_call_target="tpu_custom_call" | custom-call | tf_op jit(solution)/shard_map/pallas_call | solution.py:268
  35.6 4.9 %all-to-all-start.1 = ((bf16[8,96,512]{2,1,0:T(8,128)(2,1)}), bf16[8,96,512]{2,1,0:T(8,128)(2,1)S(1)}, u32[]{:S(2)}, u32[]{:S(2)}) async-start(bf16[8,96,512]{2,1,0:T(8,128)(2,1)} %shard_map.138), calls=%async_computation.1 | async-start | bytes 1572864 | tf_op jit(solution)/shard_map/all_to_all | solution.py:422
  40.7 0.5 broadcast.430
  41.2 0.7 fusion.34
  41.9 0.2 select_reduce_fusion
  42.2 1.3 broadcast_select_fusion.1.refs_0_
  43.5 1.3 collective-permute-start.3
  44.9 0.6 concatenate.17.meta
  45.5 0.1 select_reduce_fusion.2
  45.7 2.1 %collective-permute-done.3.refs_1_ = bf16[16,32,512]{2,1,0:T(8,128)(2,1)S(1)} collective-permute-done((bf16[16,32,512]{2,1,0:T(8,128)(2,1)S(1)}, bf16[16,32,512]{2,1,0:T(8,128)(2,1)S(1)}, u32[]{:S(2)}, u32[]{:S(2)}) %collective-permute-start.3) | collective-permute-done | bytes 524320 | tf_op jit(solution)/shard_map/ppermute | solution.py:348
  47.8 1.3 shard_map.139
  49.1 12.9 %all-to-all-done.1.refs_0_.rest_0_ = bf16[8,96,512]{2,1,0:T(8,128)(2,1)S(1)} async-done(((bf16[8,96,512]{2,1,0:T(8,128)(2,1)}), bf16[8,96,512]{2,1,0:T(8,128)(2,1)S(1)}, u32[]{:S(2)}, u32[]{:S(2)}) %all-to-all-start.1) | async-done | bytes 786464 | tf_op jit(solution)/shard_map/all_to_all | solution.py:422
  62.0 3.5 %all-to-all-start.2 = ((bf16[8,32,512]{2,1,0:T(8,128)(2,1)}), bf16[8,32,512]{2,1,0:T(8,128)(2,1)S(1)}, u32[]{:S(2)}, u32[]{:S(2)}) async-start(bf16[8,32,512]{2,1,0:T(8,128)(2,1)} %shard_map.139), calls=%async_computation.2 | async-start | bytes 524288 | tf_op jit(solution)/shard_map/all_to_all | solution.py:422
  65.6 0.6 shard_map.140
  66.3 10.8 %collective-permute-done.6.rest_4_ = bf16[4,96,512]{2,1,0:T(8,128)(2,1)S(1)} collective-permute-done((bf16[4,96,512]{2,1,0:T(8,128)(2,1)S(1)}, bf16[4,96,512]{2,1,0:T(8,128)(2,1)S(1)}, u32[]{:S(2)}, u32[]{:S(2)}) %collective-permute-start.6) | collective-permute-done | bytes 393248 | tf_op jit(solution)/shard_map/ppermute | solution.py:348
  77.1 0.7 shard_map.141
  77.8 0.4 collective-permute-start.7
  78.2 0.3 collective-permute-start.5
  78.5 0.8 copy.54
  79.3 0.9 copy.53
  80.2 3.6 %collective-permute-done.7.rest_5_ = bf16[4,32,512]{2,1,0:T(8,128)(2,1)S(1)} collective-permute-done((bf16[4,32,512]{2,1,0:T(8,128)(2,1)S(1)}, bf16[4,32,512]{2,1,0:T(8,128)(2,1)S(1)}, u32[]{:S(2)}, u32[]{:S(2)}) %collective-permute-start.7) | collective-permute-done | bytes 131104 | tf_op jit(solution)/shard_map/ppermute | solution.py:348
  83.8 0.6 bitcast_convert_fusion.cond_ref
  84.4 0.7 collective-permute-done.9.rest_7_
  85.2 0.6 copy-done.12
  85.8 0.1 copy-done.10
  85.9 0.3 copy-done.8
  86.2 25.7 %shard_map.142 = (bf16[256,2048]{1,0:T(8,128)(2,1)}, bf16[256,2048]{1,0:T(8,128)(2,1)}, f32[4,512]{1,0:T(4,128)}, f32[256,512]{1,0:T(8,128)}, bf16[256,512]{1,0:T(8,128)(2,1)}) custom-call(s32[26]{0:T(128)} %concatenate.17.meta, bf16[256,2048]{1,0:T(8,128)(2,1)} %bitcast.60, bf16[256,2048]{1,0:T(8,128)(2,1)} %bitcast.61, ...), custom_call_target="tpu_custom_call" | custom-call | flops 11811160064 | bytes 16777216 | tf_op jit(solution)/shard_map/pallas_call | solution.py:210
  111.9 0.2 collective-permute-start.10
  112.1 1.6 %collective-permute-done.10 = bf16[256,512]{1,0:T(8,128)(2,1)S(1)} collective-permute-done((bf16[256,512]{1,0:T(8,128)(2,1)}, bf16[256,512]{1,0:T(8,128)(2,1)S(1)}, u32[]{:S(2)}, u32[]{:S(2)}) %collective-permute-start.10) | collective-permute-done | bytes 262176 | tf_op jit(solution)/shard_map/ppermute | solution.py:306
  113.7 1.1 convert_add_fusion
  114.9 0.4 collective-permute-start.11
  115.2 5.3 %collective-permute-done.11 = bf16[1,128,512]{2,1,0:T(8,128)(2,1)S(1)} collective-permute-done((bf16[1,128,512]{2,1,0:T(8,128)(2,1)S(1)}, bf16[1,128,512]{2,1,0:T(8,128)(2,1)S(1)}, u32[]{:S(2)}, u32[]{:S(2)}) %collective-permute-start.11) | collective-permute-done | bytes 131104 | tf_op jit(solution)/shard_map/ppermute | solution.py:306
  120.5 12.8 %all_to_all.20 = bf16[8,16,512]{2,1,0:T(8,128)(2,1)S(1)} all-to-all(bf16[8,16,512]{2,1,0:T(8,128)(2,1)S(1)} %bitcast.52), channel_id=1, replica_groups=mesh['pool'=4,'dp'=8] {'dp'}, dimensions={0} | all-to-all | bytes 262144 | tf_op jit(solution)/shard_map/all_to_all | solution.py:317
  133.4 0.6 convert_reduce_fusion
  (73 shorter events, 2.1 us)
Async XLA Ops:
  0.6 2.4 %copy-start.5 = (s32[1,1,4,2]{2,3,1,0:T(2,128)S(1)}, s32[1,1,4,2]{2,3,1,0:T(2,128)}, u32[]{:S(2)}) copy-start(s32[1,1,4,2]{2,3,1,0:T(2,128)} %param.14) | copy-start | bytes 100
  0.6 2.6 %copy-start.6 = (s32[1,1,4,2]{2,3,1,0:T(2,128)S(1)}, s32[1,1,4,2]{2,3,1,0:T(2,128)}, u32[]{:S(2)}) copy-start(s32[1,1,4,2]{2,3,1,0:T(2,128)} %param.15) | copy-start | bytes 100
  0.7 2.7 %copy-start.7 = (s32[1,1,16]{2,1,0:T(1,128)S(1)}, s32[1,1,16]{2,1,0:T(1,128)}, u32[]{:S(2)}) copy-start(s32[1,1,16]{2,1,0:T(1,128)} %param.17) | copy-start | bytes 196
  2.2 23.7 %collective-permute-start = (bf16[16,96,512]{2,1,0:T(8,128)(2,1)S(1)}, bf16[16,96,512]{2,1,0:T(8,128)(2,1)S(1)}, u32[]{:S(2)}, u32[]{:S(2)}) collective-permute-start(bf16[16,96,512]{2,1,0:T(8,128)(2,1)S(1)} %slice.28), channel_id=1, source_target_pairs={{24,8},{25,9},{26,10},{27,11},{28,12},{29,13},{30,14},{31,15}} | collective-permute-start | bytes 4718600 | tf_op jit(solution)/shard_map/ppermute | solution.py:348
  4.1 21.9 %all-to-all-start = ((s32[32,1,128]{2,1,0:T(1,128)}), s32[32,1,128]{2,1,0:T(1,128)S(1)}, u32[]{:S(2)}, u32[]{:S(2)}) async-start(s32[32,1,128]{2,1,0:T(1,128)} %broadcast_in_dim.52), calls=%async_computation | async-start | bytes 32768 | tf_op jit(solution)/shard_map/all_to_all | solution.py:361
  27.7 6.4 %collective-permute-start.1 = (bf16[16,96,512]{2,1,0:T(8,128)(2,1)S(1)}, bf16[16,96,512]{2,1,0:T(8,128)(2,1)S(1)}, u32[]{:S(2)}, u32[]{:S(2)}) collective-permute-start(bf16[16,96,512]{2,1,0:T(8,128)(2,1)S(1)} %broadcast_select_fusion.refs_0_), channel_id=1, source_target_pairs={{24,16},{25,17},{26,18},{27,19},{28,20},{29,21},{30,22},{31,23},{8... | collective-permute-start | bytes 4718600 | tf_op jit(solution)/shard_map/ppermute | solution.py:348
  32.4 9.9 %collective-permute-start.2 = (bf16[16,32,512]{2,1,0:T(8,128)(2,1)}, bf16[16,32,512]{2,1,0:T(8,128)(2,1)}, u32[]{:S(2)}, u32[]{:S(2)}) collective-permute-start(bf16[16,32,512]{2,1,0:T(8,128)(2,1)} %slice.27), channel_id=1, source_target_pairs={{24,8},{25,9},{26,10},{27,11},{28,12},{29,13},{30,14},{31,15}} | collective-permute-start | bytes 1572872 | tf_op jit(solution)/shard_map/ppermute | solution.py:348
  35.6 26.4 %all-to-all-start.1 = ((bf16[8,96,512]{2,1,0:T(8,128)(2,1)}), bf16[8,96,512]{2,1,0:T(8,128)(2,1)S(1)}, u32[]{:S(2)}, u32[]{:S(2)}) async-start(bf16[8,96,512]{2,1,0:T(8,128)(2,1)} %shard_map.138), calls=%async_computation.1 | async-start | bytes 1572864 | tf_op jit(solution)/shard_map/all_to_all | solution.py:422
  43.5 4.2 %collective-permute-start.3 = (bf16[16,32,512]{2,1,0:T(8,128)(2,1)S(1)}, bf16[16,32,512]{2,1,0:T(8,128)(2,1)S(1)}, u32[]{:S(2)}, u32[]{:S(2)}) collective-permute-start(bf16[16,32,512]{2,1,0:T(8,128)(2,1)S(1)} %broadcast_select_fusion.1.refs_0_), channel_id=1, source_target_pairs={{24,16},{25,17},{26,18},{27,19},{28,20},{29,21},{30,22},{31,23},{8... | collective-permute-start | bytes 1572872 | tf_op jit(solution)/shard_map/ppermute | solution.py:348
  45.7 32.8 %copy-start.2 = (bf16[512,256]{1,0:T(8,128)(2,1)S(1)}, bf16[512,256]{1,0:T(8,128)(2,1)}, u32[]{:S(2)}) copy-start(bf16[512,256]{1,0:T(8,128)(2,1)} %down_ref.1) | copy-start | bytes 786436
  49.0 30.3 %copy-start.3 = (bf16[256,512]{1,0:T(8,128)(2,1)S(1)}, bf16[256,512]{1,0:T(8,128)(2,1)}, u32[]{:S(2)}) copy-start(bf16[256,512]{1,0:T(8,128)(2,1)} %up_ref.1) | copy-start | bytes 786436
  49.0 34.8 %copy-start.4 = (bf16[1,1,4,512]{3,2,1,0:T(4,128)(2,1)S(1)}, bf16[1,1,4,512]{3,2,1,0:T(4,128)(2,1)}, u32[]{:S(2)}) copy-start(bf16[1,1,4,512]{3,2,1,0:T(4,128)(2,1)} %param.13) | copy-start | bytes 12292
  62.0 18.2 %copy-start = (bf16[8,96,512]{2,1,0:T(8,128)(2,1)}, bf16[8,96,512]{2,1,0:T(8,128)(2,1)S(1)}, u32[]{:S(2)}) copy-start(bf16[8,96,512]{2,1,0:T(8,128)(2,1)S(1)} %all-to-all-done.1.refs_0_.rest_0_) | copy-start | bytes 2359300
  62.0 15.1 %all-to-all-start.2 = ((bf16[8,32,512]{2,1,0:T(8,128)(2,1)}), bf16[8,32,512]{2,1,0:T(8,128)(2,1)S(1)}, u32[]{:S(2)}, u32[]{:S(2)}) async-start(bf16[8,32,512]{2,1,0:T(8,128)(2,1)} %shard_map.139), calls=%async_computation.2 | async-start | bytes 524288 | tf_op jit(solution)/shard_map/all_to_all | solution.py:422
  66.1 10.9 %collective-permute-start.6 = (bf16[4,96,512]{2,1,0:T(8,128)(2,1)S(1)}, bf16[4,96,512]{2,1,0:T(8,128)(2,1)S(1)}, u32[]{:S(2)}, u32[]{:S(2)}) collective-permute-start(bf16[4,96,512]{2,1,0:T(8,128)(2,1)S(1)} %shard_map.140), channel_id=1, source_target_pairs={{0,16},{1,17},{2,18},{3,19},{4,20},{5,21},{6,22},{7,23},{8,24},{9,... | collective-permute-start | bytes 1179656 | tf_op jit(solution)/shard_map/ppermute | solution.py:348
  66.2 18.9 %collective-permute-start.4 = (bf16[8,96,512]{2,1,0:T(8,128)(2,1)S(1)}, bf16[8,96,512]{2,1,0:T(8,128)(2,1)S(1)}, u32[]{:S(2)}, u32[]{:S(2)}) collective-permute-start(bf16[8,96,512]{2,1,0:T(8,128)(2,1)S(1)} %all-to-all-done.1.refs_0_.rest_0_), channel_id=1, source_target_pairs={{0,8},{1,9},{2,10},{3,11},{4,12},{5,13},{6,14},{7,15},{8,0},{9,1},... | collective-permute-start | bytes 2359304 | tf_op jit(solution)/shard_map/ppermute | solution.py:348
  77.1 8.1 %copy-start.9 = (bf16[4,96,512]{2,1,0:T(8,128)(2,1)}, bf16[4,96,512]{2,1,0:T(8,128)(2,1)S(1)}, u32[]{:S(2)}) copy-start(bf16[4,96,512]{2,1,0:T(8,128)(2,1)S(1)} %collective-permute-done.6.rest_4_) | copy-start | bytes 1179652
  77.1 8.1 %collective-permute-start.8 = (bf16[4,96,512]{2,1,0:T(8,128)(2,1)S(1)}, bf16[4,96,512]{2,1,0:T(8,128)(2,1)}, u32[]{:S(2)}, u32[]{:S(2)}) collective-permute-start(bf16[4,96,512]{2,1,0:T(8,128)(2,1)S(1)} %collective-permute-done.6.rest_4_), channel_id=1, source_target_pairs={{0,8},{1,9},{2,10},{3,11},{4,12},{5,13},{6,14},{7,15},{8,0},{9,1},... | collective-permute-start | bytes 1179656 | tf_op jit(solution)/shard_map/ppermute | solution.py:348
  77.1 8.1 %copy-start.1 = (bf16[8,32,512]{2,1,0:T(8,128)(2,1)}, bf16[8,32,512]{2,1,0:T(8,128)(2,1)S(1)}, u32[]{:S(2)}) copy-start(bf16[8,32,512]{2,1,0:T(8,128)(2,1)S(1)} %all-to-all-done.2.refs_0_.rest_1_) | copy-start | bytes 786436
  77.8 6.0 %collective-permute-start.7 = (bf16[4,32,512]{2,1,0:T(8,128)(2,1)S(1)}, bf16[4,32,512]{2,1,0:T(8,128)(2,1)S(1)}, u32[]{:S(2)}, u32[]{:S(2)}) collective-permute-start(bf16[4,32,512]{2,1,0:T(8,128)(2,1)S(1)} %shard_map.141), channel_id=1, source_target_pairs={{0,16},{1,17},{2,18},{3,19},{4,20},{5,21},{6,22},{7,23},{8,24},{9,... | collective-permute-start | bytes 393224 | tf_op jit(solution)/shard_map/ppermute | solution.py:348
  78.2 7.0 %collective-permute-start.5 = (bf16[8,32,512]{2,1,0:T(8,128)(2,1)S(1)}, bf16[8,32,512]{2,1,0:T(8,128)(2,1)S(1)}, u32[]{:S(2)}, u32[]{:S(2)}) collective-permute-start(bf16[8,32,512]{2,1,0:T(8,128)(2,1)S(1)} %all-to-all-done.2.refs_0_.rest_1_), channel_id=1, source_target_pairs={{0,8},{1,9},{2,10},{3,11},{4,12},{5,13},{6,14},{7,15},{8,0},{9,1},... | collective-permute-start | bytes 786440 | tf_op jit(solution)/shard_map/ppermute | solution.py:348
  83.8 1.4 %copy-start.11 = (bf16[4,32,512]{2,1,0:T(8,128)(2,1)}, bf16[4,32,512]{2,1,0:T(8,128)(2,1)S(1)}, u32[]{:S(2)}) copy-start(bf16[4,32,512]{2,1,0:T(8,128)(2,1)S(1)} %collective-permute-done.7.rest_5_) | copy-start | bytes 393220
  83.8 1.3 %collective-permute-start.9 = (bf16[4,32,512]{2,1,0:T(8,128)(2,1)S(1)}, bf16[4,32,512]{2,1,0:T(8,128)(2,1)S(1)}, u32[]{:S(2)}, u32[]{:S(2)}) collective-permute-start(bf16[4,32,512]{2,1,0:T(8,128)(2,1)S(1)} %collective-permute-done.7.rest_5_), channel_id=1, source_target_pairs={{0,8},{1,9},{2,10},{3,11},{4,12},{5,13},{6,14},{7,15},{8,0},{9,1},... | collective-permute-start | bytes 393224 | tf_op jit(solution)/shard_map/ppermute | solution.py:348
  85.2 0.7 copy-start.12
  85.2 0.8 copy-start.10
  85.2 1.0 copy-start.8
  111.9 1.8 %collective-permute-start.10 = (bf16[256,512]{1,0:T(8,128)(2,1)}, bf16[256,512]{1,0:T(8,128)(2,1)S(1)}, u32[]{:S(2)}, u32[]{:S(2)}) collective-permute-start(bf16[256,512]{1,0:T(8,128)(2,1)} %get-tuple-element.25), channel_id=1, source_target_pairs={{0,8},{8,0},{16,24},{24,16},{1,9},{9,1},{17,25},{25,17},{2,10},{10... | collective-permute-start | bytes 786440 | tf_op jit(solution)/shard_map/ppermute | solution.py:306
  114.9 5.6 %collective-permute-start.11 = (bf16[1,128,512]{2,1,0:T(8,128)(2,1)S(1)}, bf16[1,128,512]{2,1,0:T(8,128)(2,1)S(1)}, u32[]{:S(2)}, u32[]{:S(2)}) collective-permute-start(bf16[1,128,512]{2,1,0:T(8,128)(2,1)S(1)} %fusion.1), channel_id=1, source_target_pairs={{0,16},{8,24},{16,0},{24,8},{1,17},{9,25},{17,1},{25,9},{2,18},{10... | collective-permute-start | bytes 393224 | tf_op jit(solution)/shard_map/ppermute | solution.py:306

commit v16 on v13

--- a/solution.py
+++ b/solution.py
@@ -25,12 +25,12 @@
 
 
 def span_kernel(
-    held_count, nbr_count, bounds, meta,
+    held_count, nbr_count, bounds, pool_count, meta,
     q_ref, cot_ref, cond_ref, gain_ref, down_ref, up_ref, upt_ref, downt_ref, *rest,
 ):
     held_refs = rest[:held_count]
-    (kv_hbm, kvt_hbm, out_ref, qg_ref, cg_ref, ad_ref,
-     raw_ref, kv_ref, kvt_ref, proj_ref, grad_ref, score_ref, dprob_ref,
+    (kv_hbm, kvt_hbm, proj_hbm, prob_hbm, dscore_hbm, cg_ref, keep_ref, give_ref,
+     raw_ref, kv_ref, kvt_ref, proj_ref, grad_ref, score_ref, dprob_ref, prob_ref, dscore_ref,
      q2_ref, cot2_ref, acc_ref, sems, kv_sem) = rest[held_count:]
     step = pl.program_id(0)
     per_device, slot_len, width = raw_ref.shape
@@ -41,7 +41,7 @@
     rank = down_ref.shape[1]
     scaling = HEAD ** (-0.5)
     live = meta[0] == 1
-    lens, which, index = 1, 1 + per_device, 1 + 2 * per_device
+    lens, which, index = 2, 2 + per_device, 2 + 2 * per_device
     parts = len(bounds) - 1
     cuts = [pl.ds(low, high - low) for low, high in zip(bounds, bounds[1:])]
     pairs = [pl.ds(i * 2 * HEAD, 2 * HEAD) for i in range(HEADS // 2)]
@@ -116,9 +116,6 @@
     for g, cols, value_cols, lane in spots:
         score_ref[keys[g], lane] = dot(proj_ref[keys[g], cols], q2_ref[double[g], cols], NT)
         dprob_ref[keys[g], lane] = dot(proj_ref[keys[g], value_cols], cot2_ref[double[g], cols], NT)
-
-    def diagonal(both):
-        return jnp.concatenate([both[:SPAN, :HEAD], both[SPAN:, HEAD:]], axis=1)
 
     slot = lax.broadcasted_iota(jnp.int32, (key_count, 2 * SPAN), 0)
     for g in range(group):
@@ -141,10 +138,19 @@
             grad_ref[keys[g], value_cols] = dot(probs_b, cot2_ref[double[g], cols]).astype(
                 jnp.bfloat16
             )
-            out = diagonal(dot(probs_b.T, proj_ref[keys[g], value_cols]))
-            grad = diagonal(dot(d_scores.T, proj_ref[keys[g], cols]))
-            out_ref[tokens[g], cols] = jnp.where(live, out, 0.0).astype(jnp.bfloat16)
-            qg_ref[tokens[g], cols] = jnp.where(live, grad, 0.0).astype(jnp.bfloat16)
+            prob_ref[keys[g], lane] = probs_b
+            dscore_ref[keys[g], lane] = d_scores
+
+    rows = proj_ref.shape[0]
+    mine = pl.ds(pl.multiple_of(step * rows, rows), rows)
+    leaving = [
+        pltpu.make_async_copy(ref, hbm.at[mine], kv_sem.at[2 + i])
+        for i, (ref, hbm) in enumerate(
+            ((proj_ref, proj_hbm), (prob_ref, prob_hbm), (dscore_ref, dscore_hbm))
+        )
+    ]
+    for copy in leaving:
+        copy.start()
 
     @pl.when(step == 0)
     def _():
@@ -165,13 +171,59 @@
         cg_ref[pl.ds(step * group + g, 1), :] = jnp.where(live, span_grad, 0.0)
     acc_ref[:, :rank] += dot(hidden, lat_grad, TN)
     acc_ref[:, rank:] += dot(enc_grad, latent, TN)
+    for copy in leaving:
+        copy.wait()
 
     @pl.when(step == pl.num_programs(0) - 1)
     def _():
-        ad_ref[...] = jnp.where(live, acc_ref[...], 0.0).astype(ad_ref.dtype)
-
-
-def run_spans(meta, query, cot, cond, held, bounds, gain, w_down, w_up, w_kv, w_kv_t, nbr_count):
+        chunk = width // pool_count
+        for k in range(pool_count // 2):
+            part = pl.ds(k * chunk, chunk)
+            for ref, own in ((keep_ref, meta[1]), (give_ref, 1 - meta[1])):
+                rows = acc_ref[pl.ds(pl.multiple_of((2 * k + own) * chunk, chunk), chunk), :]
+                ref[part, :] = jnp.where(live, rows, 0.0).astype(ref.dtype)
+
+
+def out_kernel(meta, proj_ref, prob_ref, dscore_ref, out_ref, qg_ref):
+    live = meta[0] == 1
+    head_cols = out_ref.shape[1]
+
+    def diagonal(both):
+        return jnp.concatenate([both[:SPAN, :HEAD], both[SPAN:, HEAD:]], axis=1)
+
+    for i in range(HEADS // 2):
+        cols = pl.ds(i * 2 * HEAD, 2 * HEAD)
+        value_cols = pl.ds(head_cols + i * 2 * HEAD, 2 * HEAD)
+        lane = pl.ds(i * 2 * SPAN, 2 * SPAN)
+        out = diagonal(dot(prob_ref[:, lane].T, proj_ref[:, value_cols]))
+        grad = diagonal(dot(dscore_ref[:, lane].T, proj_ref[:, cols]))
+        out_ref[:, cols] = jnp.where(live, out, 0.0).astype(jnp.bfloat16)
+        qg_ref[:, cols] = jnp.where(live, grad, 0.0).astype(jnp.bfloat16)
+
+
+def run_outs(meta, proj, prob, dscore, span_count):
+    rows = proj.shape[0]
+    head_cols = proj.shape[1] // 2
+    keys = rows // span_count
+    blocks = lambda a: pl.BlockSpec((a.shape[0] // span_count, a.shape[1]), lambda s, m: (s, 0))
+    out = jax.ShapeDtypeStruct((span_count * SPAN, head_cols), jnp.bfloat16)
+    return pl.pallas_call(
+        out_kernel,
+        grid_spec=pltpu.PrefetchScalarGridSpec(
+            num_scalar_prefetch=1,
+            grid=(span_count,),
+            in_specs=[blocks(proj), blocks(prob), blocks(dscore)],
+            out_specs=[blocks(out), blocks(out)],
+        ),
+        out_shape=[out, out],
+        compiler_params=pltpu.CompilerParams(vmem_limit_bytes=48 * 2**20),
+        cost_estimate=pl.CostEstimate(
+            flops=8 * rows * SPAN * head_cols, bytes_accessed=14 * 2**20, transcendentals=0
+        ),
+    )(meta, proj, prob, dscore)
+
+
+def run_spans(meta, query, cot, cond, held, bounds, gain, w_down, w_up, w_kv, w_kv_t, nbr_count, pool_count):
     span_count, width = cond.shape
     token_count, head_cols = query.shape
     slot_len = bounds[-1]
@@ -188,18 +240,18 @@
     lanes = SPAN * HEADS
     flops = 2 * rows * (2 * width * 2 * head_cols + 6 * width * rank + 6 * SPAN * head_cols)
     return pl.pallas_call(
-        functools.partial(span_kernel, len(held), nbr_count, bounds),
+        functools.partial(span_kernel, len(held), nbr_count, bounds, pool_count),
         grid_spec=pltpu.PrefetchScalarGridSpec(
             num_scalar_prefetch=1,
             grid=(span_count // group,),
             in_specs=[tokens, tokens]
             + [whole(a) for a in small]
             + [pl.BlockSpec(memory_space=pltpu.HBM)] * len(large),
-            out_specs=[
-                tokens,
-                tokens,
+            out_specs=[pl.BlockSpec(memory_space=pltpu.HBM)] * 3
+            + [
                 pl.BlockSpec((span_count, width), lambda s, m: (0, 0)),
-                pl.BlockSpec((width, 2 * rank), lambda s, m: (0, 0)),
+                pl.BlockSpec((width // 2, 2 * rank), lambda s, m: (0, 0)),
+                pl.BlockSpec((width // 2, 2 * rank), lambda s, m: (0, 0)),
             ],
             scratch_shapes=[
                 pltpu.VMEM((per_device, slot_len, width), jnp.bfloat16),
@@ -209,18 +261,22 @@
                 pltpu.VMEM((keys, 2 * head_cols), jnp.bfloat16),
                 pltpu.VMEM((keys, lanes), jnp.float32),
                 pltpu.VMEM((keys, lanes), jnp.float32),
+                pltpu.VMEM((keys, lanes), jnp.bfloat16),
+                pltpu.VMEM((keys, lanes), jnp.bfloat16),
                 pltpu.VMEM((group * 2 * SPAN, head_cols), jnp.bfloat16),
                 pltpu.VMEM((group * 2 * SPAN, head_cols), jnp.bfloat16),
                 pltpu.VMEM((width, 2 * rank), jnp.float32),
                 pltpu.SemaphoreType.DMA((per_device * parts,)),
-                pltpu.SemaphoreType.DMA((2,)),
+                pltpu.SemaphoreType.DMA((5,)),
             ],
         ),
         out_shape=[
-            jax.ShapeDtypeStruct((token_count, head_cols), jnp.bfloat16),
-            jax.ShapeDtypeStruct((token_count, head_cols), jnp.bfloat16),
+            jax.ShapeDtypeStruct((rows, 2 * head_cols), jnp.bfloat16),
+            jax.ShapeDtypeStruct((rows, lanes), jnp.bfloat16),
+            jax.ShapeDtypeStruct((rows, lanes), jnp.bfloat16),
             jax.ShapeDtypeStruct((span_count, width), jnp.float32),
-            jax.ShapeDtypeStruct((width, 2 * rank), jnp.float32),
+            jax.ShapeDtypeStruct((width // 2, 2 * rank), jnp.float32),
+            jax.ShapeDtypeStruct((width // 2, 2 * rank), jnp.bfloat16),
         ],
         compiler_params=pltpu.CompilerParams(vmem_limit_bytes=60 * 2**20),
         cost_estimate=pl.CostEstimate(
@@ -275,32 +331,24 @@
     return row, lane // half, crosses, number // half
 
 
-def scatter_sum(total, axes):
-    width = total.shape[1]
-    sizes = [lax.axis_size(axis) for axis in axes]
-    total = total.reshape(tuple(sizes) + (-1, width)).astype(jnp.float32)
-    for at, axis in enumerate(axes):
-        size, index = sizes[at], lax.axis_index(axis)
-        if size & (size - 1):
-            lead = (size,) + tuple(d for i, d in enumerate(total.shape) if i != at)
-            parts = jnp.moveaxis(total, at, 0).astype(jnp.bfloat16)
-            parts = lax.all_to_all(parts, axis, split_axis=0, concat_axis=0, tiled=True)
-            total = jnp.sum(parts.reshape(lead).astype(jnp.float32), axis=0)
-            total = jnp.expand_dims(total, at)
-            continue
-        bit = 1
-        while bit < size:
-            shape = total.shape
-            split = total.reshape(shape[:at] + (shape[at] // 2, 2) + shape[at + 1 :])
-            mine = (index // bit) % 2
-            keep = lax.dynamic_index_in_dim(split, mine, at + 1, keepdims=False)
-            give = lax.dynamic_index_in_dim(split, 1 - mine, at + 1, keepdims=False)
-            got = lax.ppermute(
-                give.astype(jnp.bfloat16), axis, [(i, i ^ bit) for i in range(size)]
-            )
-            total = keep + got.astype(jnp.float32)
-            bit *= 2
-    return total.reshape(-1, width)
+def scatter_sum(keep, give, axes, beside):
+    width = keep.shape[1]
+    size, columns = (lax.axis_size(axis) for axis in axes)
+    index = lax.axis_index(axes[0])
+    swap = lambda a, bit: lax.ppermute(a, axes[0], [(i, i ^ bit) for i in range(size)])
+    total = keep + swap(give, 1).astype(jnp.float32)
+    bit = 2
+    while bit < size:
+        split = total.reshape(size // bit // 2, 2, -1, width)
+        mine = (index // bit) % 2
+        keep = lax.dynamic_index_in_dim(split, mine, 1, keepdims=False)
+        give = lax.dynamic_index_in_dim(split, 1 - mine, 1, keepdims=False)
+        total = keep + swap(give.astype(jnp.bfloat16), bit).astype(jnp.float32)
+        bit *= 2
+    parts = total.reshape(columns, -1, width).astype(jnp.bfloat16)
+    parts, tied = lax.optimization_barrier((parts, beside[1]))
+    parts = lax.all_to_all(parts, axes[1], split_axis=0, concat_axis=0, tiled=True)
+    return jnp.sum(parts.astype(jnp.float32), axis=0), beside[0](tied)
 
 
 def body(
@@ -408,10 +456,10 @@
     own = lambda a: lax.dynamic_index_in_dim(
         a.reshape(relay_row, per_device), own_row, 0, keepdims=False
     )
-    live = (row < relay_row).astype(jnp.int32)
-    meta = jnp.concatenate([live[None], own(wanted_len), own(which), own(index)]).astype(jnp.int32)
-
-    attn_out, q_grad, cond_grad, terms = run_spans(
+    flags = jnp.stack([(row < relay_row).astype(jnp.int32), row % 2])
+    meta = jnp.concatenate([flags, own(wanted_len), own(which), own(index)]).astype(jnp.int32)
+
+    proj, prob, dscore, cond_grad, keep, give = run_spans(
         meta,
         queries.reshape(token_count, head_cols),
         cotangent.reshape(token_count, head_cols),
@@ -424,9 +472,11 @@
         w_kv,
         w_kv_t,
         nbr_count,
-    )
-
-    adapter_grad = scatter_sum(terms, axes)
+        pool_count,
+    )
+
+    outs = lambda tied: run_outs(tied, proj, prob, dscore, span_count)
+    adapter_grad, (attn_out, q_grad) = scatter_sum(keep, give, axes, (outs, meta))
     return (
         attn_out.reshape(1, 1, token_count, head_cols),
         q_grad.reshape(1, 1, token_count, head_cols),

time: 129 us -> 132 us (1.023)
  waiting for transfers between devices: 48.4 us -> 40.5 us
  Pallas kernels: 28.7 us -> 35.8 us
  local copies, waits for them, and re-layouts: 15.7 us -> 17.4 us
    all_to_all x2, waiting for transfers between devices: 9.39 us -> 18.3 us  [body(): lax.all_to_all(sends, 'dp', split_axis=0, concat_axis=0, tiled=True)]
    ppermute x10, waiting for transfers between devices: 16.8 us -> 7.97 us  [hop(): lax.ppermute(array, axes, [(a * columns + j, b * columns + j) for a, b in...]
    ppermute x5 -> x2, waiting for transfers between devices: 15.1 us -> 7.13 us  [scatter_sum(): lax.ppermute(a, axes[0], [(i, i ^ bit) for i in range(size)])]
    pallas_call x0 -> x1, Pallas kernels: none -> 6.73 us  [run_outs(): pl.pallas_call(out_kernel, grid_spec=pltpu.PrefetchScalarGridSpec(num_sca...]
    all_to_all x0 -> x1, starting transfers between devices: none -> 5.12 us  [scatter_sum(): lax.all_to_all(parts, axes[1], split_axis=0, concat_axis=0, tiled=True)]
    ppermute x5 -> x2, starting transfers between devices: 5.09 us -> 0.3 us  [scatter_sum(): lax.ppermute(a, axes[0], [(i, i ^ bit) for i in range(size)])]
    unnamed x31 -> x37, local copies, waits for them, and re-layouts: 9.5 us -> 10.9 us
  transfers between devices with their start and end apart: 18 -> 16, of which waited for: 13 -> 9; matrix products, arithmetic and copies ran while one was open for 13% -> 13% of each run, Pallas kernels for 2% -> 8%
where the time goes in v16:
time: 132 us; the launch traced here: 131 us
  waiting for transfers between devices  40.5 us (31%)
  Pallas kernels  35.8 us (27%)
  starting transfers between devices  27.8 us (21%)
  local copies, waits for them, and re-layouts  17.4 us (13%)
  other arithmetic  8.37 us (6%)
    pallas_call x1, Pallas kernels, run_spans(): pl.pallas_call(functools.partial(span_kernel, len(held), nbr_count, bound...  25 us
    all_to_all x2, waiting for transfers between devices, body(): lax.all_to_all(sends, 'dp', split_axis=0, concat_axis=0, tiled=True)  18.3 us
    unnamed x37, local copies, waits for them, and re-layouts  10.9 us
    all_to_all x2, starting transfers between devices, body(): lax.all_to_all(sends, 'dp', split_axis=0, concat_axis=0, tiled=True)  8.39 us
    all_to_all x1, starting transfers between devices, to_all(): return lax.all_to_all(copies, axis, split_axis=0, concat_axis=0, tiled=True)  8.23 us
    ppermute x10, waiting for transfers between devices, hop(): lax.ppermute(array, axes, [(a * columns + j, b * columns + j) for a, b in...  7.97 us
    ppermute x2, waiting for transfers between devices, scatter_sum(): lax.ppermute(a, axes[0], [(i, i ^ bit) for i in range(size)])  7.13 us
    all_to_all x1, waiting for transfers between devices, to_all(): return lax.all_to_all(copies, axis, split_axis=0, concat_axis=0, tiled=True)  7.1 us
  transfers between devices with their start and end apart: 16, of which 9 were waited for; matrix products, arithmetic and copies ran while one was open for 13% of the time, Pallas kernels for 8%

profile of v16, /device:TPU:0, one launch (start us, length us, event | category | flops | bytes accessed | tf_op | source)
XLA Modules:
  0.0 130.8 jit_solution(13545028944422984139)
XLA Ops:
  0.7 1.6 %slice.28 = bf16[16,96,512]{2,1,0:T(8,128)(2,1)S(1)} slice(bf16[16,128,512]{2,1,0:T(8,128)(2,1)} %bitcast.45), slice={[0:16], [0:96], [0:512]} | slice | bytes 3145728 | tf_op jit(solution)/shard_map/slice | solution.py:389
  2.2 0.8 collective-permute-start
  3.5 0.6 broadcast_in_dim.52
  4.1 8.2 %all-to-all-start = ((s32[32,1,128]{2,1,0:T(1,128)}), s32[32,1,128]{2,1,0:T(1,128)S(1)}, u32[]{:S(2)}, u32[]{:S(2)}) async-start(s32[32,1,128]{2,1,0:T(1,128)} %broadcast_in_dim.52), calls=%async_computation | async-start | bytes 32768 | tf_op jit(solution)/shard_map/all_to_all | solution.py:394
  12.4 6.5 %copy.45 = bf16[512,4096]{0,1:T(8,128)(2,1)} copy(bf16[512,4096]{1,0:T(8,128)(2,1)} %rest_8_.1) | data formatting | bytes 8388608 | tf_op args[10]
  18.9 7.1 %all-to-all-done = s32[32,1,128]{2,1,0:T(1,128)S(1)} async-done(((s32[32,1,128]{2,1,0:T(1,128)}), s32[32,1,128]{2,1,0:T(1,128)S(1)}, u32[]{:S(2)}, u32[]{:S(2)}) %all-to-all-start) | async-done | bytes 16416 | tf_op jit(solution)/shard_map/all_to_all | solution.py:394
  26.0 1.6 %broadcast_select_fusion.refs_0_ = bf16[16,96,512]{2,1,0:T(8,128)(2,1)S(1)} fusion(bf16[16,96,512]{2,1,0:T(8,128)(2,1)S(1)} %collective-permute-done, pred[]{:T(512)S(6)} %eq.145, bf16[16,128,512]{2,1,0:T(8,128)(2,1)} %bitcast.46), kind=kLoop, calls=%fused_computation | loop fusion | flops 786432 | bytes 4718593 | tf_op jit(solution)/shard_map/jit(_where)/select_n | solution.py:432
  27.5 1.3 collective-permute-start.1
  29.0 0.3 convert_reduce_fusion.4
  29.4 0.6 convert_reduce_fusion.1
  30.2 1.9 %slice.27 = bf16[16,32,512]{2,1,0:T(8,128)(2,1)} slice(bf16[16,128,512]{2,1,0:T(8,128)(2,1)} %bitcast.47), slice={[0:16], [96:128], [0:512]} | slice | bytes 1048576 | tf_op jit(solution)/shard_map/slice | solution.py:389
  32.1 1.5 %collective-permute-start.2 = (bf16[16,32,512]{2,1,0:T(8,128)(2,1)}, bf16[16,32,512]{2,1,0:T(8,128)(2,1)}, u32[]{:S(2)}, u32[]{:S(2)}) collective-permute-start(bf16[16,32,512]{2,1,0:T(8,128)(2,1)} %slice.27), channel_id=1, source_target_pairs={{24,8},{25,9},{26,10},{27,11},{28,12},{29,13},{30,14},{31,15}} | collective-permute-start | bytes 1572872 | tf_op jit(solution)/shard_map/ppermute | solution.py:381
  33.5 0.2 select_reduce_fusion
  33.8 1.5 %shard_map.138 = bf16[8,96,512]{2,1,0:T(8,128)(2,1)} custom-call(s32[9]{0:T(128)S(1)} %pad_add_fusion.1.meta, bf16[16,96,512]{2,1,0:T(8,128)(2,1)S(1)} %broadcast_select_fusion.refs_0_, bf16[16,96,512]{2,1,0:T(8,128)(2,1)S(1)} %collective-permute-done.1.refs_1_), custom_call_target="tpu_custom_call" | custom-call | tf_op jit(solution)/shard_map/pallas_call | solution.py:300
  35.3 4.9 %all-to-all-start.1 = ((bf16[8,96,512]{2,1,0:T(8,128)(2,1)}), bf16[8,96,512]{2,1,0:T(8,128)(2,1)S(1)}, u32[]{:S(2)}, u32[]{:S(2)}) async-start(bf16[8,96,512]{2,1,0:T(8,128)(2,1)} %shard_map.138), calls=%async_computation.1 | async-start | bytes 1572864 | tf_op jit(solution)/shard_map/all_to_all | solution.py:439
  40.2 1.3 broadcast_select_fusion.1.refs_0_
  41.5 1.4 %collective-permute-start.3 = (bf16[16,32,512]{2,1,0:T(8,128)(2,1)S(1)}, bf16[16,32,512]{2,1,0:T(8,128)(2,1)S(1)}, u32[]{:S(2)}, u32[]{:S(2)}) collective-permute-start(bf16[16,32,512]{2,1,0:T(8,128)(2,1)S(1)} %broadcast_select_fusion.1.refs_0_), channel_id=1, source_target_pairs={{24,16},{25,17},{26,18},{27,19},{28,20},{29,21},{30,22},{31,23},{8... | collective-permute-start | bytes 1572872 | tf_op jit(solution)/shard_map/ppermute | solution.py:381
  43.1 0.5 broadcast.437
  43.6 0.7 fusion.34
  44.3 0.1 select_reduce_fusion.2
  44.4 3.2 %collective-permute-done.3.refs_1_ = bf16[16,32,512]{2,1,0:T(8,128)(2,1)S(1)} collective-permute-done((bf16[16,32,512]{2,1,0:T(8,128)(2,1)S(1)}, bf16[16,32,512]{2,1,0:T(8,128)(2,1)S(1)}, u32[]{:S(2)}, u32[]{:S(2)}) %collective-permute-start.3) | collective-permute-done | bytes 524320 | tf_op jit(solution)/shard_map/ppermute | solution.py:381
  47.6 1.3 shard_map.139
  48.9 12.8 %all-to-all-done.1.refs_0_.rest_0_ = bf16[8,96,512]{2,1,0:T(8,128)(2,1)S(1)} async-done(((bf16[8,96,512]{2,1,0:T(8,128)(2,1)}), bf16[8,96,512]{2,1,0:T(8,128)(2,1)S(1)}, u32[]{:S(2)}, u32[]{:S(2)}) %all-to-all-start.1) | async-done | bytes 786464 | tf_op jit(solution)/shard_map/all_to_all | solution.py:439
  61.7 3.5 %all-to-all-start.2 = ((bf16[8,32,512]{2,1,0:T(8,128)(2,1)}), bf16[8,32,512]{2,1,0:T(8,128)(2,1)S(1)}, u32[]{:S(2)}, u32[]{:S(2)}) async-start(bf16[8,32,512]{2,1,0:T(8,128)(2,1)} %shard_map.139), calls=%async_computation.2 | async-start | bytes 524288 | tf_op jit(solution)/shard_map/all_to_all | solution.py:439
  65.2 0.6 shard_map.140
  66.0 0.6 bitcast_convert_fusion.cond_ref
  66.6 0.9 copy.50
  67.5 0.9 copy.49
  68.9 5.5 %all-to-all-done.2.refs_0_.rest_1_ = bf16[8,32,512]{2,1,0:T(8,128)(2,1)S(1)} async-done(((bf16[8,32,512]{2,1,0:T(8,128)(2,1)}), bf16[8,32,512]{2,1,0:T(8,128)(2,1)S(1)}, u32[]{:S(2)}, u32[]{:S(2)}) %all-to-all-start.2) | async-done | bytes 262176 | tf_op jit(solution)/shard_map/all_to_all | solution.py:439
  74.4 0.7 shard_map.141
  75.2 2.2 %collective-permute-done.6.rest_4_ = bf16[4,96,512]{2,1,0:T(8,128)(2,1)S(1)} collective-permute-done((bf16[4,96,512]{2,1,0:T(8,128)(2,1)S(1)}, bf16[4,96,512]{2,1,0:T(8,128)(2,1)S(1)}, u32[]{:S(2)}, u32[]{:S(2)}) %collective-permute-start.6) | collective-permute-done | bytes 393248 | tf_op jit(solution)/shard_map/ppermute | solution.py:381
  77.4 0.2 select_reduce_fusion.1
  77.5 0.6 collective-permute-start.5
  78.1 2.0 %collective-permute-done.7.rest_5_ = bf16[4,32,512]{2,1,0:T(8,128)(2,1)S(1)} collective-permute-done((bf16[4,32,512]{2,1,0:T(8,128)(2,1)S(1)}, bf16[4,32,512]{2,1,0:T(8,128)(2,1)S(1)}, u32[]{:S(2)}, u32[]{:S(2)}) %collective-permute-start.7) | collective-permute-done | bytes 131104 | tf_op jit(solution)/shard_map/ppermute | solution.py:381
  80.2 0.7 concatenate.15.meta
  80.9 0.6 collective-permute-done.9.rest_7_
  81.6 0.6 copy-done.15
  82.2 0.2 copy-done.12
  82.4 25.0 %shard_map.142 = (bf16[1024,4096]{1,0:T(8,128)(2,1)}, bf16[1024,1024]{1,0:T(8,128)(2,1)}, bf16[1024,1024]{1,0:T(8,128)(2,1)}, f32[4,512]{1,0:T(4,128)}, f32[256,512]{1,0:T(8,128)}, /*index=5*/bf16[256,512]{1,0:T(8,128)(2,1)}) custom-call(s32[26]{0:T(128)} %concatenate.15.meta, bf16[256,2048]{1,0:T(8,128)(2,1)} %bitcast.59, bf16[256,2048]{1,0:T(8,128)(2,1)} %bitcast.60, ...), custom_call_target="tpu_custom_call" | custom-call | flops 11811160064 | bytes 16777216 | tf_op jit(solution)/shard_map/pallas_call | solution.py:242
  107.4 0.2 collective-permute-start.10
  107.6 1.6 %collective-permute-done.10 = bf16[256,512]{1,0:T(8,128)(2,1)S(1)} collective-permute-done((bf16[256,512]{1,0:T(8,128)(2,1)}, bf16[256,512]{1,0:T(8,128)(2,1)S(1)}, u32[]{:S(2)}, u32[]{:S(2)}) %collective-permute-start.10) | collective-permute-done | bytes 262176 | tf_op jit(solution)/shard_map/ppermute | solution.py:338
  109.2 1.1 convert_add_fusion
  110.5 5.5 %collective-permute-done.11 = bf16[1,128,512]{2,1,0:T(8,128)(2,1)S(1)} collective-permute-done((bf16[1,128,512]{2,1,0:T(8,128)(2,1)S(1)}, bf16[1,128,512]{2,1,0:T(8,128)(2,1)S(1)}, u32[]{:S(2)}, u32[]{:S(2)}) %collective-permute-start.11) | collective-permute-done | bytes 131104 | tf_op jit(solution)/shard_map/ppermute | solution.py:338
  116.0 0.7 fusion
  116.7 5.1 %all-to-all-start.3 = ((bf16[8,16,512]{2,1,0:T(8,128)(2,1)}), bf16[8,16,512]{2,1,0:T(8,128)(2,1)S(1)}, u32[]{:S(2)}, u32[]{:S(2)}) async-start(bf16[8,16,512]{2,1,0:T(8,128)(2,1)} %bitcast.27), calls=%async_computation.3 | async-start | bytes 262144 | tf_op jit(solution)/shard_map/all_to_all | solution.py:350
  121.8 1.6 %copy-done.2 = bf16[1024,1024]{1,0:T(8,128)(2,1)S(1)} copy-done((bf16[1024,1024]{1,0:T(8,128)(2,1)S(1)}, bf16[1024,1024]{1,0:T(8,128)(2,1)}, u32[]{:S(2)}) %copy-start.2) | copy-done | bytes 2097176
  123.4 6.7 %shard_map.143 = (bf16[256,2048]{1,0:T(8,128)(2,1)}, bf16[256,2048]{1,0:T(8,128)(2,1)}) custom-call(s32[26]{0:T(128)S(1)} %copy-done.4, bf16[1024,4096]{1,0:T(8,128)(2,1)} %get-tuple-element.25.proj_ref, bf16[1024,1024]{1,0:T(8,128)(2,1)S(1)} %copy-done.1, bf16[1024,1024]{1,0:T(8,128)(2,1)S(1)} %copy-done.2), custom_call_target="tpu_custom_call" | custom-call | flops 1073741824 | bytes 14680064 | tf_op jit(solution)/shard_map/pallas_call | solution.py:210
  130.2 0.6 convert_reduce_fusion
  (80 shorter events, 2.3 us)
Async XLA Ops:
  0.6 2.4 %copy-start.8 = (s32[1,1,4,2]{2,3,1,0:T(2,128)S(1)}, s32[1,1,4,2]{2,3,1,0:T(2,128)}, u32[]{:S(2)}) copy-start(s32[1,1,4,2]{2,3,1,0:T(2,128)} %param.14) | copy-start | bytes 100
  0.6 2.6 %copy-start.9 = (s32[1,1,4,2]{2,3,1,0:T(2,128)S(1)}, s32[1,1,4,2]{2,3,1,0:T(2,128)}, u32[]{:S(2)}) copy-start(s32[1,1,4,2]{2,3,1,0:T(2,128)} %param.15) | copy-start | bytes 100
  0.7 2.7 %copy-start.10 = (s32[1,1,16]{2,1,0:T(1,128)S(1)}, s32[1,1,16]{2,1,0:T(1,128)}, u32[]{:S(2)}) copy-start(s32[1,1,16]{2,1,0:T(1,128)} %param.17) | copy-start | bytes 196
  2.2 23.7 %collective-permute-start = (bf16[16,96,512]{2,1,0:T(8,128)(2,1)S(1)}, bf16[16,96,512]{2,1,0:T(8,128)(2,1)S(1)}, u32[]{:S(2)}, u32[]{:S(2)}) collective-permute-start(bf16[16,96,512]{2,1,0:T(8,128)(2,1)S(1)} %slice.28), channel_id=1, source_target_pairs={{24,8},{25,9},{26,10},{27,11},{28,12},{29,13},{30,14},{31,15}} | collective-permute-start | bytes 4718600 | tf_op jit(solution)/shard_map/ppermute | solution.py:381
  4.1 21.9 %all-to-all-start = ((s32[32,1,128]{2,1,0:T(1,128)}), s32[32,1,128]{2,1,0:T(1,128)S(1)}, u32[]{:S(2)}, u32[]{:S(2)}) async-start(s32[32,1,128]{2,1,0:T(1,128)} %broadcast_in_dim.52), calls=%async_computation | async-start | bytes 32768 | tf_op jit(solution)/shard_map/all_to_all | solution.py:394
  27.5 6.3 %collective-permute-start.1 = (bf16[16,96,512]{2,1,0:T(8,128)(2,1)S(1)}, bf16[16,96,512]{2,1,0:T(8,128)(2,1)S(1)}, u32[]{:S(2)}, u32[]{:S(2)}) collective-permute-start(bf16[16,96,512]{2,1,0:T(8,128)(2,1)S(1)} %broadcast_select_fusion.refs_0_), channel_id=1, source_target_pairs={{24,16},{25,17},{26,18},{27,19},{28,20},{29,21},{30,22},{31,23},{8... | collective-permute-start | bytes 4718600 | tf_op jit(solution)/shard_map/ppermute | solution.py:381
  32.1 8.1 %collective-permute-start.2 = (bf16[16,32,512]{2,1,0:T(8,128)(2,1)}, bf16[16,32,512]{2,1,0:T(8,128)(2,1)}, u32[]{:S(2)}, u32[]{:S(2)}) collective-permute-start(bf16[16,32,512]{2,1,0:T(8,128)(2,1)} %slice.27), channel_id=1, source_target_pairs={{24,8},{25,9},{26,10},{27,11},{28,12},{29,13},{30,14},{31,15}} | collective-permute-start | bytes 1572872 | tf_op jit(solution)/shard_map/ppermute | solution.py:381
  35.3 26.4 %all-to-all-start.1 = ((bf16[8,96,512]{2,1,0:T(8,128)(2,1)}), bf16[8,96,512]{2,1,0:T(8,128)(2,1)S(1)}, u32[]{:S(2)}, u32[]{:S(2)}) async-start(bf16[8,96,512]{2,1,0:T(8,128)(2,1)} %shard_map.138), calls=%async_computation.1 | async-start | bytes 1572864 | tf_op jit(solution)/shard_map/all_to_all | solution.py:439
  40.2 25.8 %copy-start.7 = (bf16[1,1,4,512]{3,2,1,0:T(4,128)(2,1)S(1)}, bf16[1,1,4,512]{3,2,1,0:T(4,128)(2,1)}, u32[]{:S(2)}) copy-start(bf16[1,1,4,512]{3,2,1,0:T(4,128)(2,1)} %param.13) | copy-start | bytes 12292
  40.2 26.4 %copy-start.5 = (bf16[512,256]{1,0:T(8,128)(2,1)S(1)}, bf16[512,256]{1,0:T(8,128)(2,1)}, u32[]{:S(2)}) copy-start(bf16[512,256]{1,0:T(8,128)(2,1)} %down_ref.1) | copy-start | bytes 786436
  41.5 26.0 %copy-start.6 = (bf16[256,512]{1,0:T(8,128)(2,1)S(1)}, bf16[256,512]{1,0:T(8,128)(2,1)}, u32[]{:S(2)}) copy-start(bf16[256,512]{1,0:T(8,128)(2,1)} %up_ref.1) | copy-start | bytes 786436
  41.5 6.1 %collective-permute-start.3 = (bf16[16,32,512]{2,1,0:T(8,128)(2,1)S(1)}, bf16[16,32,512]{2,1,0:T(8,128)(2,1)S(1)}, u32[]{:S(2)}, u32[]{:S(2)}) collective-permute-start(bf16[16,32,512]{2,1,0:T(8,128)(2,1)S(1)} %broadcast_select_fusion.1.refs_0_), channel_id=1, source_target_pairs={{24,16},{25,17},{26,18},{27,19},{28,20},{29,21},{30,22},{31,23},{8... | collective-permute-start | bytes 1572872 | tf_op jit(solution)/shard_map/ppermute | solution.py:381
  61.7 19.9 %copy-start = (bf16[8,96,512]{2,1,0:T(8,128)(2,1)}, bf16[8,96,512]{2,1,0:T(8,128)(2,1)S(1)}, u32[]{:S(2)}) copy-start(bf16[8,96,512]{2,1,0:T(8,128)(2,1)S(1)} %all-to-all-done.1.refs_0_.rest_0_) | copy-start | bytes 2359300
  61.7 12.7 %all-to-all-start.2 = ((bf16[8,32,512]{2,1,0:T(8,128)(2,1)}), bf16[8,32,512]{2,1,0:T(8,128)(2,1)S(1)}, u32[]{:S(2)}, u32[]{:S(2)}) async-start(bf16[8,32,512]{2,1,0:T(8,128)(2,1)} %shard_map.139), calls=%async_computation.2 | async-start | bytes 524288 | tf_op jit(solution)/shard_map/all_to_all | solution.py:439
  65.8 11.5 %collective-permute-start.6 = (bf16[4,96,512]{2,1,0:T(8,128)(2,1)S(1)}, bf16[4,96,512]{2,1,0:T(8,128)(2,1)S(1)}, u32[]{:S(2)}, u32[]{:S(2)}) collective-permute-start(bf16[4,96,512]{2,1,0:T(8,128)(2,1)S(1)} %shard_map.140), channel_id=1, source_target_pairs={{0,16},{1,17},{2,18},{3,19},{4,20},{5,21},{6,22},{7,23},{8,24},{9,... | collective-permute-start | bytes 1179656 | tf_op jit(solution)/shard_map/ppermute | solution.py:381
  65.9 15.6 %collective-permute-start.4 = (bf16[8,96,512]{2,1,0:T(8,128)(2,1)S(1)}, bf16[8,96,512]{2,1,0:T(8,128)(2,1)}, u32[]{:S(2)}, u32[]{:S(2)}) collective-permute-start(bf16[8,96,512]{2,1,0:T(8,128)(2,1)S(1)} %all-to-all-done.1.refs_0_.rest_0_), channel_id=1, source_target_pairs={{0,8},{1,9},{2,10},{3,11},{4,12},{5,13},{6,14},{7,15},{8,0},{9,1},... | collective-permute-start | bytes 2359304 | tf_op jit(solution)/shard_map/ppermute | solution.py:381
  74.4 7.2 %copy-start.3 = (bf16[8,32,512]{2,1,0:T(8,128)(2,1)}, bf16[8,32,512]{2,1,0:T(8,128)(2,1)S(1)}, u32[]{:S(2)}) copy-start(bf16[8,32,512]{2,1,0:T(8,128)(2,1)S(1)} %all-to-all-done.2.refs_0_.rest_1_) | copy-start | bytes 786436
  75.1 5.0 %collective-permute-start.7 = (bf16[4,32,512]{2,1,0:T(8,128)(2,1)S(1)}, bf16[4,32,512]{2,1,0:T(8,128)(2,1)S(1)}, u32[]{:S(2)}, u32[]{:S(2)}) collective-permute-start(bf16[4,32,512]{2,1,0:T(8,128)(2,1)S(1)} %shard_map.141), channel_id=1, source_target_pairs={{0,16},{1,17},{2,18},{3,19},{4,20},{5,21},{6,22},{7,23},{8,24},{9,... | collective-permute-start | bytes 393224 | tf_op jit(solution)/shard_map/ppermute | solution.py:381
  77.4 4.2 %copy-start.11 = (bf16[4,96,512]{2,1,0:T(8,128)(2,1)}, bf16[4,96,512]{2,1,0:T(8,128)(2,1)S(1)}, u32[]{:S(2)}) copy-start(bf16[4,96,512]{2,1,0:T(8,128)(2,1)S(1)} %collective-permute-done.6.rest_4_) | copy-start | bytes 1179652
  77.4 4.1 %collective-permute-start.8 = (bf16[4,96,512]{2,1,0:T(8,128)(2,1)S(1)}, bf16[4,96,512]{2,1,0:T(8,128)(2,1)S(1)}, u32[]{:S(2)}, u32[]{:S(2)}) collective-permute-start(bf16[4,96,512]{2,1,0:T(8,128)(2,1)S(1)} %collective-permute-done.6.rest_4_), channel_id=1, source_target_pairs={{0,8},{1,9},{2,10},{3,11},{4,12},{5,13},{6,14},{7,15},{8,0},{9,1},... | collective-permute-start | bytes 1179656 | tf_op jit(solution)/shard_map/ppermute | solution.py:381
  77.5 4.0 %collective-permute-start.5 = (bf16[8,32,512]{2,1,0:T(8,128)(2,1)S(1)}, bf16[8,32,512]{2,1,0:T(8,128)(2,1)S(1)}, u32[]{:S(2)}, u32[]{:S(2)}) collective-permute-start(bf16[8,32,512]{2,1,0:T(8,128)(2,1)S(1)} %all-to-all-done.2.refs_0_.rest_1_), channel_id=1, source_target_pairs={{0,8},{1,9},{2,10},{3,11},{4,12},{5,13},{6,14},{7,15},{8,0},{9,1},... | collective-permute-start | bytes 786440 | tf_op jit(solution)/shard_map/ppermute | solution.py:381
  80.1 1.4 %copy-start.14 = (bf16[4,32,512]{2,1,0:T(8,128)(2,1)}, bf16[4,32,512]{2,1,0:T(8,128)(2,1)S(1)}, u32[]{:S(2)}) copy-start(bf16[4,32,512]{2,1,0:T(8,128)(2,1)S(1)} %collective-permute-done.7.rest_5_) | copy-start | bytes 393220
  80.1 1.3 %collective-permute-start.9 = (bf16[4,32,512]{2,1,0:T(8,128)(2,1)S(1)}, bf16[4,32,512]{2,1,0:T(8,128)(2,1)S(1)}, u32[]{:S(2)}, u32[]{:S(2)}) collective-permute-start(bf16[4,32,512]{2,1,0:T(8,128)(2,1)S(1)} %collective-permute-done.7.rest_5_), channel_id=1, source_target_pairs={{0,8},{1,9},{2,10},{3,11},{4,12},{5,13},{6,14},{7,15},{8,0},{9,1},... | collective-permute-start | bytes 393224 | tf_op jit(solution)/shard_map/ppermute | solution.py:381
  81.5 0.7 copy-start.15
  81.5 0.8 copy-start.13
  81.5 0.9 copy-start.12
  107.4 14.4 %copy-start.1 = (bf16[1024,1024]{1,0:T(8,128)(2,1)S(1)}, bf16[1024,1024]{1,0:T(8,128)(2,1)}, u32[]{:S(2)}) copy-start(bf16[1024,1024]{1,0:T(8,128)(2,1)} %get-tuple-element.26.prob_ref) | copy-start | bytes 6291460
  107.4 14.4 %copy-start.4 = (s32[26]{0:T(128)S(1)}, s32[26]{0:T(128)}, u32[]{:S(2)}) copy-start(s32[26]{0:T(128)} %concatenate.15.meta) | copy-start | bytes 316
  107.4 1.8 %collective-permute-start.10 = (bf16[256,512]{1,0:T(8,128)(2,1)}, bf16[256,512]{1,0:T(8,128)(2,1)S(1)}, u32[]{:S(2)}, u32[]{:S(2)}) collective-permute-start(bf16[256,512]{1,0:T(8,128)(2,1)} %get-tuple-element.23), channel_id=1, source_target_pairs={{0,8},{8,0},{16,24},{24,16},{1,9},{9,1},{17,25},{25,17},{2,10},{10... | collective-permute-start | bytes 786440 | tf_op jit(solution)/shard_map/ppermute | solution.py:338
  110.4 5.6 %collective-permute-start.11 = (bf16[1,128,512]{2,1,0:T(8,128)(2,1)S(1)}, bf16[1,128,512]{2,1,0:T(8,128)(2,1)S(1)}, u32[]{:S(2)}, u32[]{:S(2)}) collective-permute-start(bf16[1,128,512]{2,1,0:T(8,128)(2,1)S(1)} %fusion.1), channel_id=1, source_target_pairs={{0,16},{8,24},{16,0},{24,8},{1,17},{9,25},{17,1},{25,9},{2,18},{10... | collective-permute-start | bytes 393224 | tf_op jit(solution)/shard_map/ppermute | solution.py:338
  116.7 13.5 %all-to-all-start.3 = ((bf16[8,16,512]{2,1,0:T(8,128)(2,1)}), bf16[8,16,512]{2,1,0:T(8,128)(2,1)S(1)}, u32[]{:S(2)}, u32[]{:S(2)}) async-start(bf16[8,16,512]{2,1,0:T(8,128)(2,1)} %bitcast.27), calls=%async_computation.3 | async-start | bytes 262144 | tf_op jit(solution)/shard_map/all_to_all | solution.py:350
  121.8 1.6 %copy-start.2 = (bf16[1024,1024]{1,0:T(8,128)(2,1)S(1)}, bf16[1024,1024]{1,0:T(8,128)(2,1)}, u32[]{:S(2)}) copy-start(bf16[1024,1024]{1,0:T(8,128)(2,1)} %get-tuple-element.27.dscore_ref) | copy-start | bytes 6291460

commit v17 on v15

--- a/solution.py
+++ b/solution.py
@@ -30,7 +30,7 @@
 ):
     held_refs = rest[:held_count]
     (kv_hbm, kvt_hbm, out_ref, qg_ref, cg_ref, keep_ref, give_ref,
-     raw_ref, kv_ref, kvt_ref, proj_ref, grad_ref, score_ref, dprob_ref, prob_ref, dscore_ref,
+     raw_ref, kv_ref, kvt_ref, proj_ref, grad_ref, score_ref, dprob_ref, stat_ref,
      q2_ref, cot2_ref, acc_ref, sems, kv_sem) = rest[held_count:]
     step = pl.program_id(0)
     per_device, slot_len, width = raw_ref.shape
@@ -40,8 +40,9 @@
     head_cols = q_ref.shape[1]
     rank = down_ref.shape[1]
     scaling = HEAD ** (-0.5)
-    live = meta[0] == 1
-    lens, which, index = 2, 2 + per_device, 2 + 2 * per_device
+    live = meta[0] % 2 == 1
+    odd = meta[0] // 2
+    lens, which, index = 1, 1 + per_device, 1 + 2 * per_device
     parts = len(bounds) - 1
     cuts = [pl.ds(low, high - low) for low, high in zip(bounds, bounds[1:])]
     pairs = [pl.ds(i * 2 * HEAD, 2 * HEAD) for i in range(HEADS // 2)]
@@ -50,6 +51,11 @@
     keys = [pl.ds(g * key_count, key_count) for g in range(group)]
     tokens = [pl.ds(g * SPAN, SPAN) for g in range(group)]
     double = [pl.ds(g * 2 * SPAN, 2 * SPAN) for g in range(group)]
+    spots = [
+        (g, cols, value_cols, lane)
+        for g in range(group)
+        for cols, value_cols, lane in zip(pairs, value_pairs, lanes)
+    ]
     kv_copy = pltpu.make_async_copy(kv_hbm, kv_ref, kv_sem.at[0])
     kvt_copy = pltpu.make_async_copy(kvt_hbm, kvt_ref, kv_sem.at[1])
 
@@ -105,6 +111,9 @@
     def _():
         kv_copy.wait()
 
+    for cols in pairs + value_pairs:
+        proj_ref[:, cols] = dot(encoded, kv_ref[:, cols]).astype(jnp.bfloat16)
+
     slot = lax.broadcasted_iota(jnp.int32, (key_count, 2 * SPAN), 0)
     usable = []
     for g in range(group):
@@ -113,54 +122,36 @@
             here = jnp.logical_and(slot >= n * slot_len, slot < (n + 1) * slot_len)
             item = (step * group + g) * nbr_count + n
             limit = jnp.where(here, n * slot_len + meta[lens + item], limit)
-        usable.append(limit)
+        usable.append(slot < limit)
 
     def diagonal(both):
         return jnp.concatenate([both[:SPAN, :HEAD], both[SPAN:, HEAD:]], axis=1)
 
-    def project(i):
-        for cols in (pairs[i], value_pairs[i]):
-            proj_ref[:, cols] = dot(encoded, kv_ref[:, cols]).astype(jnp.bfloat16)
-
-    def score(i, g):
-        score_ref[keys[g], lanes[i]] = dot(proj_ref[keys[g], pairs[i]], q2_ref[double[g], pairs[i]], NT)
-        dprob_ref[keys[g], lanes[i]] = dot(
-            proj_ref[keys[g], value_pairs[i]], cot2_ref[double[g], pairs[i]], NT
+    for g, cols, value_cols, lane in spots:
+        scores = jnp.where(usable[g], dot(proj_ref[keys[g], cols], q2_ref[double[g], cols], NT), FLOOR)
+        score_ref[keys[g], lane] = scores
+        stat_ref[g, 0:1, lane] = jnp.max(scores, axis=0, keepdims=True)
+        dprob_ref[keys[g], lane] = dot(proj_ref[keys[g], value_cols], cot2_ref[double[g], cols], NT)
+
+    for g, cols, value_cols, lane in spots:
+        raised = jnp.exp2((score_ref[keys[g], lane] - stat_ref[g, 0:1, lane]) * (scaling * LOG2E))
+        inv_sum = 1.0 / jnp.sum(raised, axis=0, keepdims=True)
+        score_ref[keys[g], lane] = raised
+        stat_ref[g, 1:2, lane] = inv_sum
+        stat_ref[g, 2:3, lane] = inv_sum * jnp.sum(
+            raised * dprob_ref[keys[g], lane], axis=0, keepdims=True
         )
 
-    def soften(i, g):
-        scores = jnp.where(slot < usable[g], score_ref[keys[g], lanes[i]], FLOOR)
-        row_max = jnp.max(scores, axis=0, keepdims=True)
-        raised = jnp.exp2((scores - row_max) * (scaling * LOG2E))
-        probs = raised * (1.0 / jnp.sum(raised, axis=0, keepdims=True))
-        d_probs = dprob_ref[keys[g], lanes[i]]
-        delta = jnp.sum(probs * d_probs, axis=0, keepdims=True)
-        prob_ref[keys[g], lanes[i]] = probs.astype(jnp.bfloat16)
-        dscore_ref[keys[g], lanes[i]] = (probs * (d_probs - delta) * scaling).astype(jnp.bfloat16)
-
-    def multiply(i, g):
-        probs, d_scores = prob_ref[keys[g], lanes[i]], dscore_ref[keys[g], lanes[i]]
-        grad_ref[keys[g], pairs[i]] = dot(d_scores, q2_ref[double[g], pairs[i]]).astype(jnp.bfloat16)
-        grad_ref[keys[g], value_pairs[i]] = dot(probs, cot2_ref[double[g], pairs[i]]).astype(
-            jnp.bfloat16
-        )
-        out = diagonal(dot(probs.T, proj_ref[keys[g], value_pairs[i]]))
-        grad = diagonal(dot(d_scores.T, proj_ref[keys[g], pairs[i]]))
-        out_ref[tokens[g], pairs[i]] = jnp.where(live, out, 0.0).astype(jnp.bfloat16)
-        qg_ref[tokens[g], pairs[i]] = jnp.where(live, grad, 0.0).astype(jnp.bfloat16)
-
-    spots = [(i, g) for i in range(HEADS // 2) for g in range(group)]
-    project(0)
-    score(*spots[0])
-    for k, spot in enumerate(spots):
-        if spot[1] == 0 and spot[0] + 1 < HEADS // 2:
-            project(spot[0] + 1)
-        if k + 1 < len(spots):
-            score(*spots[k + 1])
-        soften(*spot)
-        if k:
-            multiply(*spots[k - 1])
-    multiply(*spots[-1])
+    for g, cols, value_cols, lane in spots:
+        probs = score_ref[keys[g], lane] * stat_ref[g, 1:2, lane]
+        d_scores = probs * (dprob_ref[keys[g], lane] - stat_ref[g, 2:3, lane]) * scaling
+        probs_b, d_scores = probs.astype(jnp.bfloat16), d_scores.astype(jnp.bfloat16)
+        grad_ref[keys[g], cols] = dot(d_scores, q2_ref[double[g], cols]).astype(jnp.bfloat16)
+        grad_ref[keys[g], value_cols] = dot(probs_b, cot2_ref[double[g], cols]).astype(jnp.bfloat16)
+        out = diagonal(dot(probs_b.T, proj_ref[keys[g], value_cols]))
+        grad = diagonal(dot(d_scores.T, proj_ref[keys[g], cols]))
+        out_ref[tokens[g], cols] = jnp.where(live, out, 0.0).astype(jnp.bfloat16)
+        qg_ref[tokens[g], cols] = jnp.where(live, grad, 0.0).astype(jnp.bfloat16)
 
     @pl.when(step == 0)
     def _():
@@ -187,7 +178,7 @@
         chunk = width // pool_count
         for k in range(pool_count // 2):
             part = pl.ds(k * chunk, chunk)
-            for ref, own in ((keep_ref, meta[1]), (give_ref, 1 - meta[1])):
+            for ref, own in ((keep_ref, odd), (give_ref, 1 - odd)):
                 rows = acc_ref[pl.ds(pl.multiple_of((2 * k + own) * chunk, chunk), chunk), :]
                 ref[part, :] = jnp.where(live, rows, 0.0).astype(ref.dtype)
 
@@ -206,6 +197,7 @@
     per_device = span_count * nbr_count
     keys = group * nbr_count * slot_len
     rows = per_device * slot_len
+    lanes = SPAN * HEADS
     flops = 2 * rows * (2 * width * 2 * head_cols + 6 * width * rank + 6 * SPAN * head_cols)
     return pl.pallas_call(
         functools.partial(span_kernel, len(held), nbr_count, bounds, pool_count),
@@ -228,10 +220,9 @@
                 pltpu.VMEM((2 * head_cols, width), jnp.bfloat16),
                 pltpu.VMEM((keys, 2 * head_cols), jnp.bfloat16),
                 pltpu.VMEM((keys, 2 * head_cols), jnp.bfloat16),
-                pltpu.VMEM((keys, SPAN * HEADS), jnp.float32),
-                pltpu.VMEM((keys, SPAN * HEADS), jnp.float32),
-                pltpu.VMEM((keys, SPAN * HEADS), jnp.bfloat16),
-                pltpu.VMEM((keys, SPAN * HEADS), jnp.bfloat16),
+                pltpu.VMEM((keys, lanes), jnp.float32),
+                pltpu.VMEM((keys, lanes), jnp.float32),
+                pltpu.VMEM((group, 8, lanes), jnp.float32),
                 pltpu.VMEM((group * 2 * SPAN, head_cols), jnp.bfloat16),
                 pltpu.VMEM((group * 2 * SPAN, head_cols), jnp.bfloat16),
                 pltpu.VMEM((width, 2 * rank), jnp.float32),
@@ -394,20 +385,6 @@
     def share(array, step):
         return hop(array, [(p, p // half * half + (p + step) % half) for p in range(pool_count)])
 
-    origin = jnp.where(my_cross, (my_carrier + half) % pool_count, my_carrier)
-    which = (row - origin) % half + jnp.where(my_cross, half, 0)
-    index = jnp.where(my_cross, my_number, place)
-    own_row = jnp.minimum(row, relay_row - 1)
-    hot = (my_owner * block_count + my_block)[:, None] == jnp.arange(
-        columns * block_count, dtype=jnp.int32
-    )[None, :]
-    wanted_len = jnp.sum(jnp.where(hot, store_len.reshape(1, -1), 0), axis=1)
-    own = lambda a: lax.dynamic_index_in_dim(
-        a.reshape(relay_row, per_device), own_row, 0, keepdims=False
-    )
-    flags = jnp.stack([(row < relay_row).astype(jnp.int32), row % 2])
-    meta = jnp.concatenate([flags, own(wanted_len), own(which), own(index)]).astype(jnp.int32)
-
     held = []
     for i in range(parts):
         near = jnp.where(row == relay_row, store[i], across[i])
@@ -416,8 +393,6 @@
         for step in range(1, half):
             stores.append(hop(near, [(p, p - step) for p in (relay_row, relay_row - half)]))
             held_by = jnp.where(row % half == half - 1 - step, step, held_by)
-        if i:
-            slot_block, meta = lax.optimization_barrier((slot_block, meta))
         sends = pick(held_by, slot_block, stores)
         arrived = lax.all_to_all(sends, "dp", split_axis=0, concat_axis=0, tiled=True)
         here = [arrived] + [share(arrived, step) for step in range(1, half)]
@@ -426,7 +401,21 @@
             landed = hop(leaving, [(p, (p + half) % pool_count) for p in range(pool_count)])
             here += [landed] + [share(landed, step) for step in range(1, half)]
         held.append(here)
+    origin = jnp.where(my_cross, (my_carrier + half) % pool_count, my_carrier)
+    which = (row - origin) % half + jnp.where(my_cross, half, 0)
+    index = jnp.where(my_cross, my_number, place)
     held = [here[b] for b in range(len(held[0])) for here in held]
+
+    own_row = jnp.minimum(row, relay_row - 1)
+    hot = (my_owner * block_count + my_block)[:, None] == jnp.arange(
+        columns * block_count, dtype=jnp.int32
+    )[None, :]
+    wanted_len = jnp.sum(jnp.where(hot, store_len.reshape(1, -1), 0), axis=1)
+    own = lambda a: lax.dynamic_index_in_dim(
+        a.reshape(relay_row, per_device), own_row, 0, keepdims=False
+    )
+    live = (row < relay_row).astype(jnp.int32) + row % 2 * 2
+    meta = jnp.concatenate([live[None], own(wanted_len), own(which), own(index)]).astype(jnp.int32)
 
     attn_out, q_grad, cond_grad, keep, give = run_spans(
         meta,

time: 135 us -> 128 us (0.948)
  waiting for transfers between devices: 44 us -> 40.4 us
    all_to_all x2, waiting for transfers between devices: 12.9 us -> 9.49 us  [body(): lax.all_to_all(sends, 'dp', split_axis=0, concat_axis=0, tiled=True)]
  transfers between devices with their start and end apart: 15 -> 15, of which waited for: 8 -> 10; matrix products, arithmetic and copies ran while one was open for 13% -> 13% of each run, Pallas kernels for 3% -> 2%
where the time goes in v17:
time: 128 us; the launch traced here: 127 us
  waiting for transfers between devices  40.4 us (32%)
  Pallas kernels  28.8 us (22%)
  starting transfers between devices  21.8 us (17%)
  local copies, waits for them, and re-layouts  14.5 us (11%)
  blocking collectives  12.2 us (10%)
  other arithmetic  8.13 us (6%)
    pallas_call x1, Pallas kernels, run_spans(): pl.pallas_call(functools.partial(span_kernel, len(held), nbr_count, bound...  24.7 us
    ppermute x10, waiting for transfers between devices, hop(): lax.ppermute(array, axes, [(a * columns + j, b * columns + j) for a, b in...  16.7 us
    all_to_all x1, blocking collectives, scatter_sum(): lax.all_to_all(parts, axes[1], split_axis=0, concat_axis=0, tiled=True)  12.2 us
    all_to_all x2, waiting for transfers between devices, body(): lax.all_to_all(sends, 'dp', split_axis=0, concat_axis=0, tiled=True)  9.49 us
    unnamed x31, local copies, waits for them, and re-layouts  9.49 us
    all_to_all x2, starting transfers between devices, body(): lax.all_to_all(sends, 'dp', split_axis=0, concat_axis=0, tiled=True)  8.48 us
    all_to_all x1, starting transfers between devices, to_all(): return lax.all_to_all(copies, axis, split_axis=0, concat_axis=0, tiled=True)  8.23 us
    ppermute x2, waiting for transfers between devices, scatter_sum(): lax.ppermute(a, axes[0], [(i, i ^ bit) for i in range(size)])  7.13 us
  transfers between devices with their start and end apart: 15, of which 10 were waited for; matrix products, arithmetic and copies ran while one was open for 13% of the time, Pallas kernels for 2%

profile of v17, /device:TPU:0, one launch (start us, length us, event | category | flops | bytes accessed | tf_op | source)
XLA Modules:
  0.0 126.8 jit_solution(438167129530693271)
XLA Ops:
  0.7 1.6 %slice.28 = bf16[16,96,512]{2,1,0:T(8,128)(2,1)S(1)} slice(bf16[16,128,512]{2,1,0:T(8,128)(2,1)} %bitcast.44), slice={[0:16], [0:96], [0:512]} | slice | bytes 3145728 | tf_op jit(solution)/shard_map/slice | solution.py:347
  2.2 0.8 collective-permute-start
  3.5 0.6 broadcast_in_dim.83
  4.1 8.2 %all-to-all-start = ((s32[32,1,128]{2,1,0:T(1,128)}), s32[32,1,128]{2,1,0:T(1,128)S(1)}, u32[]{:S(2)}, u32[]{:S(2)}) async-start(s32[32,1,128]{2,1,0:T(1,128)} %broadcast_in_dim.83), calls=%async_computation | async-start | bytes 32768 | tf_op jit(solution)/shard_map/all_to_all | solution.py:352
  12.4 6.5 %copy.45 = bf16[512,4096]{0,1:T(8,128)(2,1)} copy(bf16[512,4096]{1,0:T(8,128)(2,1)} %rest_8_.1) | data formatting | bytes 8388608 | tf_op args[10]
  18.9 7.1 %all-to-all-done = s32[32,1,128]{2,1,0:T(1,128)S(1)} async-done(((s32[32,1,128]{2,1,0:T(1,128)}), s32[32,1,128]{2,1,0:T(1,128)S(1)}, u32[]{:S(2)}, u32[]{:S(2)}) %all-to-all-start) | async-done | bytes 16416 | tf_op jit(solution)/shard_map/all_to_all | solution.py:352
  26.0 1.6 %broadcast_select_fusion.refs_0_ = bf16[16,96,512]{2,1,0:T(8,128)(2,1)S(1)} fusion(bf16[16,96,512]{2,1,0:T(8,128)(2,1)S(1)} %collective-permute-done, pred[]{:T(512)S(6)} %eq.145, bf16[16,128,512]{2,1,0:T(8,128)(2,1)} %bitcast.45), kind=kLoop, calls=%fused_computation | loop fusion | flops 786432 | bytes 4718593 | tf_op jit(solution)/shard_map/jit(_where)/select_n | solution.py:390
  27.5 1.3 %collective-permute-start.1 = (bf16[16,96,512]{2,1,0:T(8,128)(2,1)S(1)}, bf16[16,96,512]{2,1,0:T(8,128)(2,1)S(1)}, u32[]{:S(2)}, u32[]{:S(2)}) collective-permute-start(bf16[16,96,512]{2,1,0:T(8,128)(2,1)S(1)} %broadcast_select_fusion.refs_0_), channel_id=1, source_target_pairs={{24,16},{25,17},{26,18},{27,19},{28,20},{29,21},{30,22},{31,23},{8... | collective-permute-start | bytes 4718600 | tf_op jit(solution)/shard_map/ppermute | solution.py:339
  29.0 0.3 convert_reduce_fusion.4
  29.4 0.6 convert_reduce_fusion.1
  30.2 0.2 select_reduce_fusion
  30.4 2.4 %collective-permute-done.1.refs_1_ = bf16[16,96,512]{2,1,0:T(8,128)(2,1)S(1)} collective-permute-done((bf16[16,96,512]{2,1,0:T(8,128)(2,1)S(1)}, bf16[16,96,512]{2,1,0:T(8,128)(2,1)S(1)}, u32[]{:S(2)}, u32[]{:S(2)}) %collective-permute-start.1) | collective-permute-done | bytes 1572896 | tf_op jit(solution)/shard_map/ppermute | solution.py:339
  32.8 1.5 %shard_map.138 = bf16[8,96,512]{2,1,0:T(8,128)(2,1)} custom-call(s32[9]{0:T(128)S(1)} %pad_add_fusion.2.meta, bf16[16,96,512]{2,1,0:T(8,128)(2,1)S(1)} %broadcast_select_fusion.refs_0_, bf16[16,96,512]{2,1,0:T(8,128)(2,1)S(1)} %collective-permute-done.1.refs_1_), custom_call_target="tpu_custom_call" | custom-call | tf_op jit(solution)/shard_map/pallas_call | solution.py:259
  34.3 4.9 %all-to-all-start.1 = ((bf16[8,96,512]{2,1,0:T(8,128)(2,1)}), bf16[8,96,512]{2,1,0:T(8,128)(2,1)S(1)}, u32[]{:S(2)}, u32[]{:S(2)}) async-start(bf16[8,96,512]{2,1,0:T(8,128)(2,1)} %shard_map.138), calls=%async_computation.1 | async-start | bytes 1572864 | tf_op jit(solution)/shard_map/all_to_all | solution.py:397
  39.2 1.1 slice.27
  40.3 0.7 collective-permute-start.2
  41.1 1.1 broadcast_select_fusion.1.refs_0_
  42.3 1.4 %collective-permute-start.3 = (bf16[16,32,512]{2,1,0:T(8,128)(2,1)S(1)}, bf16[16,32,512]{2,1,0:T(8,128)(2,1)S(1)}, u32[]{:S(2)}, u32[]{:S(2)}) collective-permute-start(bf16[16,32,512]{2,1,0:T(8,128)(2,1)S(1)} %broadcast_select_fusion.1.refs_0_), channel_id=1, source_target_pairs={{24,16},{25,17},{26,18},{27,19},{28,20},{29,21},{30,22},{31,23},{8... | collective-permute-start | bytes 1572872 | tf_op jit(solution)/shard_map/ppermute | solution.py:339
  43.7 0.5 broadcast.437
  44.2 0.7 fusion.34
  44.9 0.1 select_reduce_fusion.2
  45.1 9.2 %collective-permute-done.3.refs_1_ = bf16[16,32,512]{2,1,0:T(8,128)(2,1)S(1)} collective-permute-done((bf16[16,32,512]{2,1,0:T(8,128)(2,1)S(1)}, bf16[16,32,512]{2,1,0:T(8,128)(2,1)S(1)}, u32[]{:S(2)}, u32[]{:S(2)}) %collective-permute-start.3) | collective-permute-done | bytes 524320 | tf_op jit(solution)/shard_map/ppermute | solution.py:339
  54.3 1.3 %shard_map.139 = bf16[8,32,512]{2,1,0:T(8,128)(2,1)} custom-call(s32[9]{0:T(128)S(1)} %pad_add_fusion.2.meta, bf16[16,32,512]{2,1,0:T(8,128)(2,1)S(1)} %broadcast_select_fusion.1.refs_0_, bf16[16,32,512]{2,1,0:T(8,128)(2,1)S(1)} %collective-permute-done.3.refs_1_), custom_call_target="tpu_custom_call" | custom-call | tf_op jit(solution)/shard_map/pallas_call | solution.py:259
  55.6 4.1 %all-to-all-done.1.refs_0_.rest_0_ = bf16[8,96,512]{2,1,0:T(8,128)(2,1)S(1)} async-done(((bf16[8,96,512]{2,1,0:T(8,128)(2,1)}), bf16[8,96,512]{2,1,0:T(8,128)(2,1)S(1)}, u32[]{:S(2)}, u32[]{:S(2)}) %all-to-all-start.1) | async-done | bytes 786464 | tf_op jit(solution)/shard_map/all_to_all | solution.py:397
  59.7 3.6 %all-to-all-start.2 = ((bf16[8,32,512]{2,1,0:T(8,128)(2,1)}), bf16[8,32,512]{2,1,0:T(8,128)(2,1)S(1)}, u32[]{:S(2)}, u32[]{:S(2)}) async-start(bf16[8,32,512]{2,1,0:T(8,128)(2,1)} %shard_map.139), calls=%async_computation.2 | async-start | bytes 524288 | tf_op jit(solution)/shard_map/all_to_all | solution.py:397
  63.3 0.6 shard_map.140
  63.9 0.6 bitcast_convert_fusion.cond_ref
  64.5 0.8 copy.50
  65.4 0.8 copy.49
  66.7 0.2 select_reduce_fusion.1
  66.9 5.4 %all-to-all-done.2.refs_0_.rest_1_ = bf16[8,32,512]{2,1,0:T(8,128)(2,1)S(1)} async-done(((bf16[8,32,512]{2,1,0:T(8,128)(2,1)}), bf16[8,32,512]{2,1,0:T(8,128)(2,1)S(1)}, u32[]{:S(2)}, u32[]{:S(2)}) %all-to-all-start.2) | async-done | bytes 262176 | tf_op jit(solution)/shard_map/all_to_all | solution.py:397
  72.4 0.7 shard_map.141
  73.2 2.2 %collective-permute-done.6.rest_4_ = bf16[4,96,512]{2,1,0:T(8,128)(2,1)} collective-permute-done((bf16[4,96,512]{2,1,0:T(8,128)(2,1)S(1)}, bf16[4,96,512]{2,1,0:T(8,128)(2,1)}, u32[]{:S(2)}, u32[]{:S(2)}) %collective-permute-start.6) | collective-permute-done | bytes 393248 | tf_op jit(solution)/shard_map/ppermute | solution.py:339
  75.4 0.5 collective-permute-start.5
  76.0 2.2 %collective-permute-done.7.rest_5_ = bf16[4,32,512]{2,1,0:T(8,128)(2,1)S(1)} collective-permute-done((bf16[4,32,512]{2,1,0:T(8,128)(2,1)S(1)}, bf16[4,32,512]{2,1,0:T(8,128)(2,1)S(1)}, u32[]{:S(2)}, u32[]{:S(2)}) %collective-permute-start.7) | collective-permute-done | bytes 131104 | tf_op jit(solution)/shard_map/ppermute | solution.py:339
  78.2 0.6 pad_add_fusion.1.meta
  78.8 0.7 collective-permute-done.9.rest_7_
  79.6 0.6 copy-done.12
  80.1 0.1 copy-done.10
  80.3 0.3 copy-done.8
  80.5 0.1 copy-done.9
  80.7 24.7 %shard_map.142 = (bf16[256,2048]{1,0:T(8,128)(2,1)}, bf16[256,2048]{1,0:T(8,128)(2,1)}, f32[4,512]{1,0:T(4,128)}, f32[256,512]{1,0:T(8,128)}, bf16[256,512]{1,0:T(8,128)(2,1)}) custom-call(s32[25]{0:T(128)} %pad_add_fusion.1.meta, bf16[256,2048]{1,0:T(8,128)(2,1)} %bitcast.59, bf16[256,2048]{1,0:T(8,128)(2,1)} %bitcast.60, ...), custom_call_target="tpu_custom_call" | custom-call | flops 11811160064 | bytes 16777216 | tf_op jit(solution)/shard_map/pallas_call | solution.py:202
  105.4 0.2 collective-permute-start.10
  105.6 1.6 %collective-permute-done.10 = bf16[256,512]{1,0:T(8,128)(2,1)S(1)} collective-permute-done((bf16[256,512]{1,0:T(8,128)(2,1)}, bf16[256,512]{1,0:T(8,128)(2,1)S(1)}, u32[]{:S(2)}, u32[]{:S(2)}) %collective-permute-start.10) | collective-permute-done | bytes 262176 | tf_op jit(solution)/shard_map/ppermute | solution.py:297
  107.2 1.1 convert_add_fusion
  108.4 5.5 %collective-permute-done.11 = bf16[1,128,512]{2,1,0:T(8,128)(2,1)S(1)} collective-permute-done((bf16[1,128,512]{2,1,0:T(8,128)(2,1)S(1)}, bf16[1,128,512]{2,1,0:T(8,128)(2,1)S(1)}, u32[]{:S(2)}, u32[]{:S(2)}) %collective-permute-start.11) | collective-permute-done | bytes 131104 | tf_op jit(solution)/shard_map/ppermute | solution.py:297
  114.0 12.2 %all_to_all.20 = bf16[8,16,512]{2,1,0:T(8,128)(2,1)S(1)} all-to-all(bf16[8,16,512]{2,1,0:T(8,128)(2,1)S(1)} %bitcast.51), channel_id=1, replica_groups=mesh['pool'=4,'dp'=8] {'dp'}, dimensions={0} | all-to-all | bytes 262144 | tf_op jit(solution)/shard_map/all_to_all | solution.py:308
  126.2 0.6 convert_reduce_fusion
  (72 shorter events, 2.2 us)
Async XLA Ops:
  0.6 2.4 %copy-start.5 = (s32[1,1,4,2]{2,3,1,0:T(2,128)S(1)}, s32[1,1,4,2]{2,3,1,0:T(2,128)}, u32[]{:S(2)}) copy-start(s32[1,1,4,2]{2,3,1,0:T(2,128)} %param.14) | copy-start | bytes 100
  0.6 2.6 %copy-start.6 = (s32[1,1,4,2]{2,3,1,0:T(2,128)S(1)}, s32[1,1,4,2]{2,3,1,0:T(2,128)}, u32[]{:S(2)}) copy-start(s32[1,1,4,2]{2,3,1,0:T(2,128)} %param.15) | copy-start | bytes 100
  0.7 2.7 %copy-start.7 = (s32[1,1,16]{2,1,0:T(1,128)S(1)}, s32[1,1,16]{2,1,0:T(1,128)}, u32[]{:S(2)}) copy-start(s32[1,1,16]{2,1,0:T(1,128)} %param.17) | copy-start | bytes 196
  2.2 23.7 %collective-permute-start = (bf16[16,96,512]{2,1,0:T(8,128)(2,1)S(1)}, bf16[16,96,512]{2,1,0:T(8,128)(2,1)S(1)}, u32[]{:S(2)}, u32[]{:S(2)}) collective-permute-start(bf16[16,96,512]{2,1,0:T(8,128)(2,1)S(1)} %slice.28), channel_id=1, source_target_pairs={{24,8},{25,9},{26,10},{27,11},{28,12},{29,13},{30,14},{31,15}} | collective-permute-start | bytes 4718600 | tf_op jit(solution)/shard_map/ppermute | solution.py:339
  4.1 21.9 %all-to-all-start = ((s32[32,1,128]{2,1,0:T(1,128)}), s32[32,1,128]{2,1,0:T(1,128)S(1)}, u32[]{:S(2)}, u32[]{:S(2)}) async-start(s32[32,1,128]{2,1,0:T(1,128)} %broadcast_in_dim.83), calls=%async_computation | async-start | bytes 32768 | tf_op jit(solution)/shard_map/all_to_all | solution.py:352
  27.5 5.3 %collective-permute-start.1 = (bf16[16,96,512]{2,1,0:T(8,128)(2,1)S(1)}, bf16[16,96,512]{2,1,0:T(8,128)(2,1)S(1)}, u32[]{:S(2)}, u32[]{:S(2)}) collective-permute-start(bf16[16,96,512]{2,1,0:T(8,128)(2,1)S(1)} %broadcast_select_fusion.refs_0_), channel_id=1, source_target_pairs={{24,16},{25,17},{26,18},{27,19},{28,20},{29,21},{30,22},{31,23},{8... | collective-permute-start | bytes 4718600 | tf_op jit(solution)/shard_map/ppermute | solution.py:339
  34.3 25.3 %all-to-all-start.1 = ((bf16[8,96,512]{2,1,0:T(8,128)(2,1)}), bf16[8,96,512]{2,1,0:T(8,128)(2,1)S(1)}, u32[]{:S(2)}, u32[]{:S(2)}) async-start(bf16[8,96,512]{2,1,0:T(8,128)(2,1)} %shard_map.138), calls=%async_computation.1 | async-start | bytes 1572864 | tf_op jit(solution)/shard_map/all_to_all | solution.py:397
  40.3 0.8 collective-permute-start.2
  42.2 21.7 %copy-start.4 = (bf16[1,1,4,512]{3,2,1,0:T(4,128)(2,1)S(1)}, bf16[1,1,4,512]{3,2,1,0:T(4,128)(2,1)}, u32[]{:S(2)}) copy-start(bf16[1,1,4,512]{3,2,1,0:T(4,128)(2,1)} %param.13) | copy-start | bytes 12292
  42.2 22.3 %copy-start.2 = (bf16[512,256]{1,0:T(8,128)(2,1)S(1)}, bf16[512,256]{1,0:T(8,128)(2,1)}, u32[]{:S(2)}) copy-start(bf16[512,256]{1,0:T(8,128)(2,1)} %down_ref.1) | copy-start | bytes 786436
  42.3 12.1 %collective-permute-start.3 = (bf16[16,32,512]{2,1,0:T(8,128)(2,1)S(1)}, bf16[16,32,512]{2,1,0:T(8,128)(2,1)S(1)}, u32[]{:S(2)}, u32[]{:S(2)}) collective-permute-start(bf16[16,32,512]{2,1,0:T(8,128)(2,1)S(1)} %broadcast_select_fusion.1.refs_0_), channel_id=1, source_target_pairs={{24,16},{25,17},{26,18},{27,19},{28,20},{29,21},{30,22},{31,23},{8... | collective-permute-start | bytes 1572872 | tf_op jit(solution)/shard_map/ppermute | solution.py:339
  45.1 20.3 %copy-start.3 = (bf16[256,512]{1,0:T(8,128)(2,1)S(1)}, bf16[256,512]{1,0:T(8,128)(2,1)}, u32[]{:S(2)}) copy-start(bf16[256,512]{1,0:T(8,128)(2,1)} %up_ref.1) | copy-start | bytes 786436
  59.7 13.4 %copy-start = (bf16[8,96,512]{2,1,0:T(8,128)(2,1)}, bf16[8,96,512]{2,1,0:T(8,128)(2,1)S(1)}, u32[]{:S(2)}) copy-start(bf16[8,96,512]{2,1,0:T(8,128)(2,1)S(1)} %all-to-all-done.1.refs_0_.rest_0_) | copy-start | bytes 2359300
  59.7 12.7 %all-to-all-start.2 = ((bf16[8,32,512]{2,1,0:T(8,128)(2,1)}), bf16[8,32,512]{2,1,0:T(8,128)(2,1)S(1)}, u32[]{:S(2)}, u32[]{:S(2)}) async-start(bf16[8,32,512]{2,1,0:T(8,128)(2,1)} %shard_map.139), calls=%async_computation.2 | async-start | bytes 524288 | tf_op jit(solution)/shard_map/all_to_all | solution.py:397
  63.8 11.5 %collective-permute-start.6 = (bf16[4,96,512]{2,1,0:T(8,128)(2,1)S(1)}, bf16[4,96,512]{2,1,0:T(8,128)(2,1)}, u32[]{:S(2)}, u32[]{:S(2)}) collective-permute-start(bf16[4,96,512]{2,1,0:T(8,128)(2,1)S(1)} %shard_map.140), channel_id=1, source_target_pairs={{0,16},{1,17},{2,18},{3,19},{4,20},{5,21},{6,22},{7,23},{8,24},{9,... | collective-permute-start | bytes 1179656 | tf_op jit(solution)/shard_map/ppermute | solution.py:339
  66.7 12.8 %collective-permute-start.4 = (bf16[8,96,512]{2,1,0:T(8,128)(2,1)S(1)}, bf16[8,96,512]{2,1,0:T(8,128)(2,1)S(1)}, u32[]{:S(2)}, u32[]{:S(2)}) collective-permute-start(bf16[8,96,512]{2,1,0:T(8,128)(2,1)S(1)} %all-to-all-done.1.refs_0_.rest_0_), channel_id=1, source_target_pairs={{0,8},{1,9},{2,10},{3,11},{4,12},{5,13},{6,14},{7,15},{8,0},{9,1},... | collective-permute-start | bytes 2359304 | tf_op jit(solution)/shard_map/ppermute | solution.py:339
  72.4 7.2 %copy-start.1 = (bf16[8,32,512]{2,1,0:T(8,128)(2,1)}, bf16[8,32,512]{2,1,0:T(8,128)(2,1)S(1)}, u32[]{:S(2)}) copy-start(bf16[8,32,512]{2,1,0:T(8,128)(2,1)S(1)} %all-to-all-done.2.refs_0_.rest_1_) | copy-start | bytes 786436
  73.1 5.0 %collective-permute-start.7 = (bf16[4,32,512]{2,1,0:T(8,128)(2,1)S(1)}, bf16[4,32,512]{2,1,0:T(8,128)(2,1)S(1)}, u32[]{:S(2)}, u32[]{:S(2)}) collective-permute-start(bf16[4,32,512]{2,1,0:T(8,128)(2,1)S(1)} %shard_map.141), channel_id=1, source_target_pairs={{0,16},{1,17},{2,18},{3,19},{4,20},{5,21},{6,22},{7,23},{8,24},{9,... | collective-permute-start | bytes 393224 | tf_op jit(solution)/shard_map/ppermute | solution.py:339
  75.4 4.1 %collective-permute-start.8 = (bf16[4,96,512]{2,1,0:T(8,128)(2,1)}, bf16[4,96,512]{2,1,0:T(8,128)(2,1)S(1)}, u32[]{:S(2)}, u32[]{:S(2)}) collective-permute-start(bf16[4,96,512]{2,1,0:T(8,128)(2,1)} %collective-permute-done.6.rest_4_), channel_id=1, source_target_pairs={{0,8},{1,9},{2,10},{3,11},{4,12},{5,13},{6,14},{7,15},{8,0},{9,1},... | collective-permute-start | bytes 1179656 | tf_op jit(solution)/shard_map/ppermute | solution.py:339
  75.4 4.1 %collective-permute-start.5 = (bf16[8,32,512]{2,1,0:T(8,128)(2,1)S(1)}, bf16[8,32,512]{2,1,0:T(8,128)(2,1)S(1)}, u32[]{:S(2)}, u32[]{:S(2)}) collective-permute-start(bf16[8,32,512]{2,1,0:T(8,128)(2,1)S(1)} %all-to-all-done.2.refs_0_.rest_1_), channel_id=1, source_target_pairs={{0,8},{1,9},{2,10},{3,11},{4,12},{5,13},{6,14},{7,15},{8,0},{9,1},... | collective-permute-start | bytes 786440 | tf_op jit(solution)/shard_map/ppermute | solution.py:339
  78.1 1.4 %copy-start.11 = (bf16[4,32,512]{2,1,0:T(8,128)(2,1)}, bf16[4,32,512]{2,1,0:T(8,128)(2,1)S(1)}, u32[]{:S(2)}) copy-start(bf16[4,32,512]{2,1,0:T(8,128)(2,1)S(1)} %collective-permute-done.7.rest_5_) | copy-start | bytes 393220
  78.2 1.3 %collective-permute-start.9 = (bf16[4,32,512]{2,1,0:T(8,128)(2,1)S(1)}, bf16[4,32,512]{2,1,0:T(8,128)(2,1)S(1)}, u32[]{:S(2)}, u32[]{:S(2)}) collective-permute-start(bf16[4,32,512]{2,1,0:T(8,128)(2,1)S(1)} %collective-permute-done.7.rest_5_), channel_id=1, source_target_pairs={{0,8},{1,9},{2,10},{3,11},{4,12},{5,13},{6,14},{7,15},{8,0},{9,1},... | collective-permute-start | bytes 393224 | tf_op jit(solution)/shard_map/ppermute | solution.py:339
  79.5 0.6 copy-start.12
  79.5 0.8 copy-start.10
  79.5 1.0 copy-start.8
  79.5 1.1 copy-start.9
  105.4 1.8 %collective-permute-start.10 = (bf16[256,512]{1,0:T(8,128)(2,1)}, bf16[256,512]{1,0:T(8,128)(2,1)S(1)}, u32[]{:S(2)}, u32[]{:S(2)}) collective-permute-start(bf16[256,512]{1,0:T(8,128)(2,1)} %get-tuple-element.21), channel_id=1, source_target_pairs={{0,8},{8,0},{16,24},{24,16},{1,9},{9,1},{17,25},{25,17},{2,10},{10... | collective-permute-start | bytes 786440 | tf_op jit(solution)/shard_map/ppermute | solution.py:297
  108.3 5.6 %collective-permute-start.11 = (bf16[1,128,512]{2,1,0:T(8,128)(2,1)S(1)}, bf16[1,128,512]{2,1,0:T(8,128)(2,1)S(1)}, u32[]{:S(2)}, u32[]{:S(2)}) collective-permute-start(bf16[1,128,512]{2,1,0:T(8,128)(2,1)S(1)} %fusion.1), channel_id=1, source_target_pairs={{0,16},{8,24},{16,0},{24,8},{1,17},{9,25},{17,1},{25,9},{2,18},{10... | collective-permute-start | bytes 393224 | tf_op jit(solution)/shard_map/ppermute | solution.py:297

commit v18 on v17

--- a/solution.py
+++ b/solution.py
@@ -26,10 +26,11 @@
 
 def span_kernel(
     held_count, nbr_count, bounds, pool_count, meta,
-    q_ref, cot_ref, cond_ref, gain_ref, down_ref, up_ref, upt_ref, downt_ref, *rest,
+    cond_ref, gain_ref, down_ref, up_ref, upt_ref, downt_ref, *rest,
 ):
     held_refs = rest[:held_count]
-    (kv_hbm, kvt_hbm, out_ref, qg_ref, cg_ref, keep_ref, give_ref,
+    (q_hbm, cot_hbm, kv_hbm, kvt_hbm, out_hbm, qg_hbm, cg_ref, keep_ref, give_ref,
+     q_ref, cot_ref, out_ref, qg_ref,
      raw_ref, kv_ref, kvt_ref, proj_ref, grad_ref, score_ref, dprob_ref, stat_ref,
      q2_ref, cot2_ref, acc_ref, sems, kv_sem) = rest[held_count:]
     step = pl.program_id(0)
@@ -56,8 +57,25 @@
         for g in range(group)
         for cols, value_cols, lane in zip(pairs, value_pairs, lanes)
     ]
-    kv_copy = pltpu.make_async_copy(kv_hbm, kv_ref, kv_sem.at[0])
-    kvt_copy = pltpu.make_async_copy(kvt_hbm, kvt_ref, kv_sem.at[1])
+    kvt_copy = pltpu.make_async_copy(kvt_hbm, kvt_ref, kv_sem.at[0])
+    token_copies = [
+        pltpu.make_async_copy(q_hbm, q_ref, kv_sem.at[1]),
+        pltpu.make_async_copy(cot_hbm, cot_ref, kv_sem.at[2]),
+    ]
+    own_rows = pl.ds(pl.multiple_of(step * group * SPAN, SPAN), group * SPAN)
+    out_copies = [
+        pltpu.make_async_copy(out_ref, out_hbm.at[own_rows], kv_sem.at[3]),
+        pltpu.make_async_copy(qg_ref, qg_hbm.at[own_rows], kv_sem.at[4]),
+    ]
+    kv_piece = 4 * HEAD
+    kv_copies = [
+        pltpu.make_async_copy(
+            kv_hbm.at[:, pl.ds(i * kv_piece, kv_piece)],
+            kv_ref.at[:, pl.ds(i * kv_piece, kv_piece)],
+            kv_sem.at[5 + i],
+        )
+        for i in range(2 * head_cols // kv_piece)
+    ]
 
     @pl.when(step == 0)
     def _():
@@ -71,17 +89,10 @@
                         raw_ref.at[n, cuts[part]],
                         sems.at[n * parts + part],
                     ).start()
-        kv_copy.start()
-        kvt_copy.start()
+        for copy in kv_copies + token_copies:
+            copy.start()
         q2_ref[...] = jnp.zeros_like(q2_ref)
         cot2_ref[...] = jnp.zeros_like(cot2_ref)
-
-    for g in range(group):
-        for i in range(HEADS):
-            cols = pl.ds(i * HEAD, HEAD)
-            part = pl.ds((2 * g + i % 2) * SPAN, SPAN)
-            q2_ref[part, cols] = q_ref[tokens[g], cols]
-            cot2_ref[part, cols] = cot_ref[tokens[g], cols]
 
     for n in range(group * nbr_count):
         for part in range(parts):
@@ -107,12 +118,26 @@
     latent = dot(hidden, down_ref[...]).astype(jnp.bfloat16)
     encoded = (x_full + dot(latent, up_ref[...])).astype(jnp.bfloat16)
 
+    for i, cols in enumerate(pairs + value_pairs):
+        if i % 2 == 0:
+            @pl.when(step == 0)
+            def _():
+                kv_copies[i // 2].wait()
+
+        proj_ref[:, cols] = dot(encoded, kv_ref[:, cols]).astype(jnp.bfloat16)
+
     @pl.when(step == 0)
     def _():
-        kv_copy.wait()
-
-    for cols in pairs + value_pairs:
-        proj_ref[:, cols] = dot(encoded, kv_ref[:, cols]).astype(jnp.bfloat16)
+        kvt_copy.start()
+        for copy in token_copies:
+            copy.wait()
+
+    for g in range(group):
+        for i in range(HEADS):
+            cols = pl.ds(i * HEAD, HEAD)
+            part = pl.ds((2 * g + i % 2) * SPAN, SPAN)
+            q2_ref[part, cols] = q_ref[pl.ds(pl.multiple_of((step * group + g) * SPAN, SPAN), SPAN), cols]
+            cot2_ref[part, cols] = cot_ref[pl.ds(pl.multiple_of((step * group + g) * SPAN, SPAN), SPAN), cols]
 
     slot = lax.broadcasted_iota(jnp.int32, (key_count, 2 * SPAN), 0)
     usable = []
@@ -153,6 +178,9 @@
         out_ref[tokens[g], cols] = jnp.where(live, out, 0.0).astype(jnp.bfloat16)
         qg_ref[tokens[g], cols] = jnp.where(live, grad, 0.0).astype(jnp.bfloat16)
 
+    for copy in out_copies:
+        copy.start()
+
     @pl.when(step == 0)
     def _():
         kvt_copy.wait()
@@ -172,6 +200,8 @@
         cg_ref[pl.ds(step * group + g, 1), :] = jnp.where(live, span_grad, 0.0)
     acc_ref[:, :rank] += dot(hidden, lat_grad, TN)
     acc_ref[:, rank:] += dot(enc_grad, latent, TN)
+    for copy in out_copies:
+        copy.wait()
 
     @pl.when(step == pl.num_programs(0) - 1)
     def _():
@@ -191,9 +221,8 @@
     rank = w_down.shape[1]
     whole = lambda a: pl.BlockSpec(a.shape, lambda s, m: (0,) * a.ndim, pipeline_mode=pl.Buffered(1))
     group = GROUP if span_count % GROUP == 0 else 1
-    tokens = pl.BlockSpec((group * SPAN, head_cols), lambda s, m: (s, 0))
     small = [cond, gain.reshape(1, width), w_down, w_up, w_up.T, w_down.T]
-    large = list(held) + [w_kv, w_kv_t]
+    large = list(held) + [query, cot, w_kv, w_kv_t]
     per_device = span_count * nbr_count
     keys = group * nbr_count * slot_len
     rows = per_device * slot_len
@@ -204,17 +233,19 @@
         grid_spec=pltpu.PrefetchScalarGridSpec(
             num_scalar_prefetch=1,
             grid=(span_count // group,),
-            in_specs=[tokens, tokens]
-            + [whole(a) for a in small]
+            in_specs=[whole(a) for a in small]
             + [pl.BlockSpec(memory_space=pltpu.HBM)] * len(large),
-            out_specs=[
-                tokens,
-                tokens,
+            out_specs=[pl.BlockSpec(memory_space=pltpu.HBM)] * 2
+            + [
                 pl.BlockSpec((span_count, width), lambda s, m: (0, 0)),
                 pl.BlockSpec((width // 2, 2 * rank), lambda s, m: (0, 0)),
                 pl.BlockSpec((width // 2, 2 * rank), lambda s, m: (0, 0)),
             ],
             scratch_shapes=[
+                pltpu.VMEM((token_count, head_cols), jnp.bfloat16),
+                pltpu.VMEM((token_count, head_cols), jnp.bfloat16),
+                pltpu.VMEM((group * SPAN, head_cols), jnp.bfloat16),
+                pltpu.VMEM((group * SPAN, head_cols), jnp.bfloat16),
                 pltpu.VMEM((per_device, slot_len, width), jnp.bfloat16),
                 pltpu.VMEM((width, 2 * head_cols), jnp.bfloat16),
                 pltpu.VMEM((2 * head_cols, width), jnp.bfloat16),
@@ -227,7 +258,7 @@
                 pltpu.VMEM((group * 2 * SPAN, head_cols), jnp.bfloat16),
                 pltpu.VMEM((width, 2 * rank), jnp.float32),
                 pltpu.SemaphoreType.DMA((per_device * parts,)),
-                pltpu.SemaphoreType.DMA((2,)),
+                pltpu.SemaphoreType.DMA((5 + head_cols // (2 * HEAD),)),
             ],
         ),
         out_shape=[
@@ -241,7 +272,7 @@
         cost_estimate=pl.CostEstimate(
             flops=flops, bytes_accessed=16 * 2**20, transcendentals=rows * SPAN * HEADS
         ),
-    )(meta, query, cot, *small, *large)
+    )(meta, *small, *large)
 
 
 def pick_kernel(held_count, meta, *refs):

time: 128 us -> 130 us (1.016)
  Pallas kernels: 28.8 us -> 31.1 us
    pallas_call x1, Pallas kernels: 24.7 us -> 27.1 us  [run_spans(): pl.pallas_call(functools.partial(span_kernel, len(held), nbr_count, bound...]
where the time goes in v18:
time: 130 us; the launch traced here: 129 us
  waiting for transfers between devices  40.4 us (31%)
  Pallas kernels  31.1 us (24%)
  starting transfers between devices  21.8 us (17%)
  local copies, waits for them, and re-layouts  14.5 us (11%)
  blocking collectives  12.2 us (9%)
  other arithmetic  8.13 us (6%)
    pallas_call x1, Pallas kernels, run_spans(): pl.pallas_call(functools.partial(span_kernel, len(held), nbr_count, bound...  27.1 us
    ppermute x10, waiting for transfers between devices, hop(): lax.ppermute(array, axes, [(a * columns + j, b * columns + j) for a, b in...  16.7 us
    all_to_all x1, blocking collectives, scatter_sum(): lax.all_to_all(parts, axes[1], split_axis=0, concat_axis=0, tiled=True)  12.2 us
    all_to_all x2, waiting for transfers between devices, body(): lax.all_to_all(sends, 'dp', split_axis=0, concat_axis=0, tiled=True)  9.49 us
    unnamed x31, local copies, waits for them, and re-layouts  9.49 us
    all_to_all x2, starting transfers between devices, body(): lax.all_to_all(sends, 'dp', split_axis=0, concat_axis=0, tiled=True)  8.48 us
    all_to_all x1, starting transfers between devices, to_all(): return lax.all_to_all(copies, axis, split_axis=0, concat_axis=0, tiled=True)  8.23 us
    ppermute x2, waiting for transfers between devices, scatter_sum(): lax.ppermute(a, axes[0], [(i, i ^ bit) for i in range(size)])  7.13 us
  transfers between devices with their start and end apart: 15, of which 10 were waited for; matrix products, arithmetic and copies ran while one was open for 13% of the time, Pallas kernels for 2%

profile of v18, /device:TPU:0, one launch (start us, length us, event | category | flops | bytes accessed | tf_op | source)
XLA Modules:
  0.0 129.2 jit_solution(9592131554602531136)
XLA Ops:
  0.7 1.6 %slice.28 = bf16[16,96,512]{2,1,0:T(8,128)(2,1)S(1)} slice(bf16[16,128,512]{2,1,0:T(8,128)(2,1)} %bitcast.44), slice={[0:16], [0:96], [0:512]} | slice | bytes 3145728 | tf_op jit(solution)/shard_map/slice | solution.py:378
  2.2 0.8 collective-permute-start
  3.5 0.6 broadcast_in_dim.83
  4.1 8.2 %all-to-all-start = ((s32[32,1,128]{2,1,0:T(1,128)}), s32[32,1,128]{2,1,0:T(1,128)S(1)}, u32[]{:S(2)}, u32[]{:S(2)}) async-start(s32[32,1,128]{2,1,0:T(1,128)} %broadcast_in_dim.83), calls=%async_computation | async-start | bytes 32768 | tf_op jit(solution)/shard_map/all_to_all | solution.py:383
  12.4 6.5 %copy.45 = bf16[512,4096]{0,1:T(8,128)(2,1)} copy(bf16[512,4096]{1,0:T(8,128)(2,1)} %rest_10_.1) | data formatting | bytes 8388608 | tf_op args[10]
  18.9 7.1 %all-to-all-done = s32[32,1,128]{2,1,0:T(1,128)S(1)} async-done(((s32[32,1,128]{2,1,0:T(1,128)}), s32[32,1,128]{2,1,0:T(1,128)S(1)}, u32[]{:S(2)}, u32[]{:S(2)}) %all-to-all-start) | async-done | bytes 16416 | tf_op jit(solution)/shard_map/all_to_all | solution.py:383
  26.0 1.6 %broadcast_select_fusion.refs_0_ = bf16[16,96,512]{2,1,0:T(8,128)(2,1)S(1)} fusion(bf16[16,96,512]{2,1,0:T(8,128)(2,1)S(1)} %collective-permute-done, pred[]{:T(512)S(6)} %eq.145, bf16[16,128,512]{2,1,0:T(8,128)(2,1)} %bitcast.45), kind=kLoop, calls=%fused_computation | loop fusion | flops 786432 | bytes 4718593 | tf_op jit(solution)/shard_map/jit(_where)/select_n | solution.py:421
  27.5 1.3 %collective-permute-start.1 = (bf16[16,96,512]{2,1,0:T(8,128)(2,1)S(1)}, bf16[16,96,512]{2,1,0:T(8,128)(2,1)S(1)}, u32[]{:S(2)}, u32[]{:S(2)}) collective-permute-start(bf16[16,96,512]{2,1,0:T(8,128)(2,1)S(1)} %broadcast_select_fusion.refs_0_), channel_id=1, source_target_pairs={{24,16},{25,17},{26,18},{27,19},{28,20},{29,21},{30,22},{31,23},{8... | collective-permute-start | bytes 4718600 | tf_op jit(solution)/shard_map/ppermute | solution.py:370
  29.0 0.3 convert_reduce_fusion.4
  29.4 0.6 convert_reduce_fusion.1
  30.2 0.2 select_reduce_fusion
  30.4 2.4 %collective-permute-done.1.refs_1_ = bf16[16,96,512]{2,1,0:T(8,128)(2,1)S(1)} collective-permute-done((bf16[16,96,512]{2,1,0:T(8,128)(2,1)S(1)}, bf16[16,96,512]{2,1,0:T(8,128)(2,1)S(1)}, u32[]{:S(2)}, u32[]{:S(2)}) %collective-permute-start.1) | collective-permute-done | bytes 1572896 | tf_op jit(solution)/shard_map/ppermute | solution.py:370
  32.8 1.5 %shard_map.138 = bf16[8,96,512]{2,1,0:T(8,128)(2,1)} custom-call(s32[9]{0:T(128)S(1)} %pad_add_fusion.2.meta, bf16[16,96,512]{2,1,0:T(8,128)(2,1)S(1)} %broadcast_select_fusion.refs_0_, bf16[16,96,512]{2,1,0:T(8,128)(2,1)S(1)} %collective-permute-done.1.refs_1_), custom_call_target="tpu_custom_call" | custom-call | tf_op jit(solution)/shard_map/pallas_call | solution.py:290
  34.3 4.9 %all-to-all-start.1 = ((bf16[8,96,512]{2,1,0:T(8,128)(2,1)}), bf16[8,96,512]{2,1,0:T(8,128)(2,1)S(1)}, u32[]{:S(2)}, u32[]{:S(2)}) async-start(bf16[8,96,512]{2,1,0:T(8,128)(2,1)} %shard_map.138), calls=%async_computation.1 | async-start | bytes 1572864 | tf_op jit(solution)/shard_map/all_to_all | solution.py:428
  39.2 1.1 slice.27
  40.3 0.7 collective-permute-start.2
  41.1 1.1 broadcast_select_fusion.1.refs_0_
  42.3 1.4 %collective-permute-start.3 = (bf16[16,32,512]{2,1,0:T(8,128)(2,1)S(1)}, bf16[16,32,512]{2,1,0:T(8,128)(2,1)S(1)}, u32[]{:S(2)}, u32[]{:S(2)}) collective-permute-start(bf16[16,32,512]{2,1,0:T(8,128)(2,1)S(1)} %broadcast_select_fusion.1.refs_0_), channel_id=1, source_target_pairs={{24,16},{25,17},{26,18},{27,19},{28,20},{29,21},{30,22},{31,23},{8... | collective-permute-start | bytes 1572872 | tf_op jit(solution)/shard_map/ppermute | solution.py:370
  43.7 0.5 broadcast.437
  44.2 0.7 fusion.34
  44.9 0.1 select_reduce_fusion.2
  45.1 9.2 %collective-permute-done.3.refs_1_ = bf16[16,32,512]{2,1,0:T(8,128)(2,1)S(1)} collective-permute-done((bf16[16,32,512]{2,1,0:T(8,128)(2,1)S(1)}, bf16[16,32,512]{2,1,0:T(8,128)(2,1)S(1)}, u32[]{:S(2)}, u32[]{:S(2)}) %collective-permute-start.3) | collective-permute-done | bytes 524320 | tf_op jit(solution)/shard_map/ppermute | solution.py:370
  54.3 1.3 shard_map.139
  55.6 4.1 %all-to-all-done.1.refs_0_.rest_0_ = bf16[8,96,512]{2,1,0:T(8,128)(2,1)S(1)} async-done(((bf16[8,96,512]{2,1,0:T(8,128)(2,1)}), bf16[8,96,512]{2,1,0:T(8,128)(2,1)S(1)}, u32[]{:S(2)}, u32[]{:S(2)}) %all-to-all-start.1) | async-done | bytes 786464 | tf_op jit(solution)/shard_map/all_to_all | solution.py:428
  59.7 3.6 %all-to-all-start.2 = ((bf16[8,32,512]{2,1,0:T(8,128)(2,1)}), bf16[8,32,512]{2,1,0:T(8,128)(2,1)S(1)}, u32[]{:S(2)}, u32[]{:S(2)}) async-start(bf16[8,32,512]{2,1,0:T(8,128)(2,1)} %shard_map.139), calls=%async_computation.2 | async-start | bytes 524288 | tf_op jit(solution)/shard_map/all_to_all | solution.py:428
  63.3 0.6 shard_map.140
  63.9 0.6 bitcast_convert_fusion.cond_ref
  64.5 0.8 copy.50
  65.4 0.8 copy.49
  66.7 0.2 select_reduce_fusion.1
  66.9 5.4 %all-to-all-done.2.refs_0_.rest_1_ = bf16[8,32,512]{2,1,0:T(8,128)(2,1)S(1)} async-done(((bf16[8,32,512]{2,1,0:T(8,128)(2,1)}), bf16[8,32,512]{2,1,0:T(8,128)(2,1)S(1)}, u32[]{:S(2)}, u32[]{:S(2)}) %all-to-all-start.2) | async-done | bytes 262176 | tf_op jit(solution)/shard_map/all_to_all | solution.py:428
  72.4 0.7 shard_map.141
  73.2 2.2 %collective-permute-done.6.rest_4_ = bf16[4,96,512]{2,1,0:T(8,128)(2,1)} collective-permute-done((bf16[4,96,512]{2,1,0:T(8,128)(2,1)S(1)}, bf16[4,96,512]{2,1,0:T(8,128)(2,1)}, u32[]{:S(2)}, u32[]{:S(2)}) %collective-permute-start.6) | collective-permute-done | bytes 393248 | tf_op jit(solution)/shard_map/ppermute | solution.py:370
  75.4 0.5 collective-permute-start.5
  76.0 2.2 %collective-permute-done.7.rest_5_ = bf16[4,32,512]{2,1,0:T(8,128)(2,1)S(1)} collective-permute-done((bf16[4,32,512]{2,1,0:T(8,128)(2,1)S(1)}, bf16[4,32,512]{2,1,0:T(8,128)(2,1)S(1)}, u32[]{:S(2)}, u32[]{:S(2)}) %collective-permute-start.7) | collective-permute-done | bytes 131104 | tf_op jit(solution)/shard_map/ppermute | solution.py:370
  78.2 0.6 pad_add_fusion.1.meta
  78.8 0.7 collective-permute-done.9.rest_7_
  79.6 0.6 copy-done.12
  80.1 0.1 copy-done.10
  80.3 0.3 copy-done.8
  80.5 0.1 copy-done.9
  80.7 27.1 %shard_map.142 = (bf16[256,2048]{1,0:T(8,128)(2,1)}, bf16[256,2048]{1,0:T(8,128)(2,1)}, f32[4,512]{1,0:T(4,128)}, f32[256,512]{1,0:T(8,128)}, bf16[256,512]{1,0:T(8,128)(2,1)}) custom-call(s32[25]{0:T(128)} %pad_add_fusion.1.meta, f32[4,512]{1,0:T(4,128)} %bitcast_convert_fusion.cond_ref, f32[1,512]{1,0:T(1,128)} %bitcast.61, bf16[512,256]{1,0:T(8,128)(2,1)} %down_ref.1, ...), custom_call_target="tpu_custom_call" | custom-call | flops 11811160064 | bytes 16777216 | tf_op jit(solution)/shard_map/pallas_call | solution.py:231
  107.8 0.2 collective-permute-start.10
  108.0 1.6 %collective-permute-done.10 = bf16[256,512]{1,0:T(8,128)(2,1)S(1)} collective-permute-done((bf16[256,512]{1,0:T(8,128)(2,1)}, bf16[256,512]{1,0:T(8,128)(2,1)S(1)}, u32[]{:S(2)}, u32[]{:S(2)}) %collective-permute-start.10) | collective-permute-done | bytes 262176 | tf_op jit(solution)/shard_map/ppermute | solution.py:328
  109.6 1.1 convert_add_fusion
  110.8 5.5 %collective-permute-done.11 = bf16[1,128,512]{2,1,0:T(8,128)(2,1)S(1)} collective-permute-done((bf16[1,128,512]{2,1,0:T(8,128)(2,1)S(1)}, bf16[1,128,512]{2,1,0:T(8,128)(2,1)S(1)}, u32[]{:S(2)}, u32[]{:S(2)}) %collective-permute-start.11) | collective-permute-done | bytes 131104 | tf_op jit(solution)/shard_map/ppermute | solution.py:328
  116.4 12.2 %all_to_all.20 = bf16[8,16,512]{2,1,0:T(8,128)(2,1)S(1)} all-to-all(bf16[8,16,512]{2,1,0:T(8,128)(2,1)S(1)} %bitcast.51), channel_id=1, replica_groups=mesh['pool'=4,'dp'=8] {'dp'}, dimensions={0} | all-to-all | bytes 262144 | tf_op jit(solution)/shard_map/all_to_all | solution.py:339
  128.6 0.6 convert_reduce_fusion
  (72 shorter events, 2.2 us)
Async XLA Ops:
  0.6 2.4 %copy-start.5 = (s32[1,1,4,2]{2,3,1,0:T(2,128)S(1)}, s32[1,1,4,2]{2,3,1,0:T(2,128)}, u32[]{:S(2)}) copy-start(s32[1,1,4,2]{2,3,1,0:T(2,128)} %param.14) | copy-start | bytes 100
  0.6 2.6 %copy-start.6 = (s32[1,1,4,2]{2,3,1,0:T(2,128)S(1)}, s32[1,1,4,2]{2,3,1,0:T(2,128)}, u32[]{:S(2)}) copy-start(s32[1,1,4,2]{2,3,1,0:T(2,128)} %param.15) | copy-start | bytes 100
  0.7 2.7 %copy-start.7 = (s32[1,1,16]{2,1,0:T(1,128)S(1)}, s32[1,1,16]{2,1,0:T(1,128)}, u32[]{:S(2)}) copy-start(s32[1,1,16]{2,1,0:T(1,128)} %param.17) | copy-start | bytes 196
  2.2 23.7 %collective-permute-start = (bf16[16,96,512]{2,1,0:T(8,128)(2,1)S(1)}, bf16[16,96,512]{2,1,0:T(8,128)(2,1)S(1)}, u32[]{:S(2)}, u32[]{:S(2)}) collective-permute-start(bf16[16,96,512]{2,1,0:T(8,128)(2,1)S(1)} %slice.28), channel_id=1, source_target_pairs={{24,8},{25,9},{26,10},{27,11},{28,12},{29,13},{30,14},{31,15}} | collective-permute-start | bytes 4718600 | tf_op jit(solution)/shard_map/ppermute | solution.py:370
  4.1 21.9 %all-to-all-start = ((s32[32,1,128]{2,1,0:T(1,128)}), s32[32,1,128]{2,1,0:T(1,128)S(1)}, u32[]{:S(2)}, u32[]{:S(2)}) async-start(s32[32,1,128]{2,1,0:T(1,128)} %broadcast_in_dim.83), calls=%async_computation | async-start | bytes 32768 | tf_op jit(solution)/shard_map/all_to_all | solution.py:383
  27.5 5.3 %collective-permute-start.1 = (bf16[16,96,512]{2,1,0:T(8,128)(2,1)S(1)}, bf16[16,96,512]{2,1,0:T(8,128)(2,1)S(1)}, u32[]{:S(2)}, u32[]{:S(2)}) collective-permute-start(bf16[16,96,512]{2,1,0:T(8,128)(2,1)S(1)} %broadcast_select_fusion.refs_0_), channel_id=1, source_target_pairs={{24,16},{25,17},{26,18},{27,19},{28,20},{29,21},{30,22},{31,23},{8... | collective-permute-start | bytes 4718600 | tf_op jit(solution)/shard_map/ppermute | solution.py:370
  34.3 25.3 %all-to-all-start.1 = ((bf16[8,96,512]{2,1,0:T(8,128)(2,1)}), bf16[8,96,512]{2,1,0:T(8,128)(2,1)S(1)}, u32[]{:S(2)}, u32[]{:S(2)}) async-start(bf16[8,96,512]{2,1,0:T(8,128)(2,1)} %shard_map.138), calls=%async_computation.1 | async-start | bytes 1572864 | tf_op jit(solution)/shard_map/all_to_all | solution.py:428
  40.3 0.8 collective-permute-start.2
  42.2 21.7 %copy-start.4 = (bf16[1,1,4,512]{3,2,1,0:T(4,128)(2,1)S(1)}, bf16[1,1,4,512]{3,2,1,0:T(4,128)(2,1)}, u32[]{:S(2)}) copy-start(bf16[1,1,4,512]{3,2,1,0:T(4,128)(2,1)} %param.13) | copy-start | bytes 12292
  42.2 22.3 %copy-start.2 = (bf16[512,256]{1,0:T(8,128)(2,1)S(1)}, bf16[512,256]{1,0:T(8,128)(2,1)}, u32[]{:S(2)}) copy-start(bf16[512,256]{1,0:T(8,128)(2,1)} %down_ref.1) | copy-start | bytes 786436
  42.3 12.1 %collective-permute-start.3 = (bf16[16,32,512]{2,1,0:T(8,128)(2,1)S(1)}, bf16[16,32,512]{2,1,0:T(8,128)(2,1)S(1)}, u32[]{:S(2)}, u32[]{:S(2)}) collective-permute-start(bf16[16,32,512]{2,1,0:T(8,128)(2,1)S(1)} %broadcast_select_fusion.1.refs_0_), channel_id=1, source_target_pairs={{24,16},{25,17},{26,18},{27,19},{28,20},{29,21},{30,22},{31,23},{8... | collective-permute-start | bytes 1572872 | tf_op jit(solution)/shard_map/ppermute | solution.py:370
  45.1 20.3 %copy-start.3 = (bf16[256,512]{1,0:T(8,128)(2,1)S(1)}, bf16[256,512]{1,0:T(8,128)(2,1)}, u32[]{:S(2)}) copy-start(bf16[256,512]{1,0:T(8,128)(2,1)} %up_ref.1) | copy-start | bytes 786436
  59.7 13.4 %copy-start = (bf16[8,96,512]{2,1,0:T(8,128)(2,1)}, bf16[8,96,512]{2,1,0:T(8,128)(2,1)S(1)}, u32[]{:S(2)}) copy-start(bf16[8,96,512]{2,1,0:T(8,128)(2,1)S(1)} %all-to-all-done.1.refs_0_.rest_0_) | copy-start | bytes 2359300
  59.7 12.7 %all-to-all-start.2 = ((bf16[8,32,512]{2,1,0:T(8,128)(2,1)}), bf16[8,32,512]{2,1,0:T(8,128)(2,1)S(1)}, u32[]{:S(2)}, u32[]{:S(2)}) async-start(bf16[8,32,512]{2,1,0:T(8,128)(2,1)} %shard_map.139), calls=%async_computation.2 | async-start | bytes 524288 | tf_op jit(solution)/shard_map/all_to_all | solution.py:428
  63.8 11.5 %collective-permute-start.6 = (bf16[4,96,512]{2,1,0:T(8,128)(2,1)S(1)}, bf16[4,96,512]{2,1,0:T(8,128)(2,1)}, u32[]{:S(2)}, u32[]{:S(2)}) collective-permute-start(bf16[4,96,512]{2,1,0:T(8,128)(2,1)S(1)} %shard_map.140), channel_id=1, source_target_pairs={{0,16},{1,17},{2,18},{3,19},{4,20},{5,21},{6,22},{7,23},{8,24},{9,... | collective-permute-start | bytes 1179656 | tf_op jit(solution)/shard_map/ppermute | solution.py:370
  66.7 12.8 %collective-permute-start.4 = (bf16[8,96,512]{2,1,0:T(8,128)(2,1)S(1)}, bf16[8,96,512]{2,1,0:T(8,128)(2,1)S(1)}, u32[]{:S(2)}, u32[]{:S(2)}) collective-permute-start(bf16[8,96,512]{2,1,0:T(8,128)(2,1)S(1)} %all-to-all-done.1.refs_0_.rest_0_), channel_id=1, source_target_pairs={{0,8},{1,9},{2,10},{3,11},{4,12},{5,13},{6,14},{7,15},{8,0},{9,1},... | collective-permute-start | bytes 2359304 | tf_op jit(solution)/shard_map/ppermute | solution.py:370
  72.4 7.2 %copy-start.1 = (bf16[8,32,512]{2,1,0:T(8,128)(2,1)}, bf16[8,32,512]{2,1,0:T(8,128)(2,1)S(1)}, u32[]{:S(2)}) copy-start(bf16[8,32,512]{2,1,0:T(8,128)(2,1)S(1)} %all-to-all-done.2.refs_0_.rest_1_) | copy-start | bytes 786436
  73.1 5.0 %collective-permute-start.7 = (bf16[4,32,512]{2,1,0:T(8,128)(2,1)S(1)}, bf16[4,32,512]{2,1,0:T(8,128)(2,1)S(1)}, u32[]{:S(2)}, u32[]{:S(2)}) collective-permute-start(bf16[4,32,512]{2,1,0:T(8,128)(2,1)S(1)} %shard_map.141), channel_id=1, source_target_pairs={{0,16},{1,17},{2,18},{3,19},{4,20},{5,21},{6,22},{7,23},{8,24},{9,... | collective-permute-start | bytes 393224 | tf_op jit(solution)/shard_map/ppermute | solution.py:370
  75.4 4.1 %collective-permute-start.8 = (bf16[4,96,512]{2,1,0:T(8,128)(2,1)}, bf16[4,96,512]{2,1,0:T(8,128)(2,1)S(1)}, u32[]{:S(2)}, u32[]{:S(2)}) collective-permute-start(bf16[4,96,512]{2,1,0:T(8,128)(2,1)} %collective-permute-done.6.rest_4_), channel_id=1, source_target_pairs={{0,8},{1,9},{2,10},{3,11},{4,12},{5,13},{6,14},{7,15},{8,0},{9,1},... | collective-permute-start | bytes 1179656 | tf_op jit(solution)/shard_map/ppermute | solution.py:370
  75.4 4.1 %collective-permute-start.5 = (bf16[8,32,512]{2,1,0:T(8,128)(2,1)S(1)}, bf16[8,32,512]{2,1,0:T(8,128)(2,1)S(1)}, u32[]{:S(2)}, u32[]{:S(2)}) collective-permute-start(bf16[8,32,512]{2,1,0:T(8,128)(2,1)S(1)} %all-to-all-done.2.refs_0_.rest_1_), channel_id=1, source_target_pairs={{0,8},{1,9},{2,10},{3,11},{4,12},{5,13},{6,14},{7,15},{8,0},{9,1},... | collective-permute-start | bytes 786440 | tf_op jit(solution)/shard_map/ppermute | solution.py:370
  78.1 1.4 %copy-start.11 = (bf16[4,32,512]{2,1,0:T(8,128)(2,1)}, bf16[4,32,512]{2,1,0:T(8,128)(2,1)S(1)}, u32[]{:S(2)}) copy-start(bf16[4,32,512]{2,1,0:T(8,128)(2,1)S(1)} %collective-permute-done.7.rest_5_) | copy-start | bytes 393220
  78.2 1.3 %collective-permute-start.9 = (bf16[4,32,512]{2,1,0:T(8,128)(2,1)S(1)}, bf16[4,32,512]{2,1,0:T(8,128)(2,1)S(1)}, u32[]{:S(2)}, u32[]{:S(2)}) collective-permute-start(bf16[4,32,512]{2,1,0:T(8,128)(2,1)S(1)} %collective-permute-done.7.rest_5_), channel_id=1, source_target_pairs={{0,8},{1,9},{2,10},{3,11},{4,12},{5,13},{6,14},{7,15},{8,0},{9,1},... | collective-permute-start | bytes 393224 | tf_op jit(solution)/shard_map/ppermute | solution.py:370
  79.5 0.6 copy-start.12
  79.5 0.8 copy-start.10
  79.5 1.0 copy-start.8
  79.5 1.1 copy-start.9
  107.8 1.8 %collective-permute-start.10 = (bf16[256,512]{1,0:T(8,128)(2,1)}, bf16[256,512]{1,0:T(8,128)(2,1)S(1)}, u32[]{:S(2)}, u32[]{:S(2)}) collective-permute-start(bf16[256,512]{1,0:T(8,128)(2,1)} %get-tuple-element.21), channel_id=1, source_target_pairs={{0,8},{8,0},{16,24},{24,16},{1,9},{9,1},{17,25},{25,17},{2,10},{10... | collective-permute-start | bytes 786440 | tf_op jit(solution)/shard_map/ppermute | solution.py:328
  110.7 5.6 %collective-permute-start.11 = (bf16[1,128,512]{2,1,0:T(8,128)(2,1)S(1)}, bf16[1,128,512]{2,1,0:T(8,128)(2,1)S(1)}, u32[]{:S(2)}, u32[]{:S(2)}) collective-permute-start(bf16[1,128,512]{2,1,0:T(8,128)(2,1)S(1)} %fusion.1), channel_id=1, source_target_pairs={{0,16},{8,24},{16,0},{24,8},{1,17},{9,25},{17,1},{25,9},{2,18},{10... | collective-permute-start | bytes 393224 | tf_op jit(solution)/shard_map/ppermute | solution.py:328

commit v19 on v17

--- a/solution.py
+++ b/solution.py
@@ -357,9 +357,7 @@
     across = [over(store[0])]
     table = to_all(info.reshape(-1, 128), axes)
     w_kv_t = w_kv.T
-    full_store, across, table, w_kv_t = lax.optimization_barrier(
-        (full_store, across, table, w_kv_t)
-    )
+    full_store, table, w_kv_t = lax.optimization_barrier((full_store, table, w_kv_t))
     store += [cut(i) for i in range(1, parts)]
     across += [over(a) for a in store[1:]]
     table = table.reshape(pool_count, columns, -1)
@@ -384,6 +382,20 @@
 
     def share(array, step):
         return hop(array, [(p, p // half * half + (p + step) % half) for p in range(pool_count)])
+
+    origin = jnp.where(my_cross, (my_carrier + half) % pool_count, my_carrier)
+    which = (row - origin) % half + jnp.where(my_cross, half, 0)
+    index = jnp.where(my_cross, my_number, place)
+    own_row = jnp.minimum(row, relay_row - 1)
+    hot = (my_owner * block_count + my_block)[:, None] == jnp.arange(
+        columns * block_count, dtype=jnp.int32
+    )[None, :]
+    wanted_len = jnp.sum(jnp.where(hot, store_len.reshape(1, -1), 0), axis=1)
+    own = lambda a: lax.dynamic_index_in_dim(
+        a.reshape(relay_row, per_device), own_row, 0, keepdims=False
+    )
+    live = (row < relay_row).astype(jnp.int32) + row % 2 * 2
+    meta = jnp.concatenate([live[None], own(wanted_len), own(which), own(index)]).astype(jnp.int32)
 
     held = []
     for i in range(parts):
@@ -397,25 +409,13 @@
         arrived = lax.all_to_all(sends, "dp", split_axis=0, concat_axis=0, tiled=True)
         here = [arrived] + [share(arrived, step) for step in range(1, half)]
         if crossing:
+            if i:
+                leaving_place, meta = lax.optimization_barrier((leaving_place, meta))
             leaving = pick(0, leaving_place, [arrived])
             landed = hop(leaving, [(p, (p + half) % pool_count) for p in range(pool_count)])
             here += [landed] + [share(landed, step) for step in range(1, half)]
         held.append(here)
-    origin = jnp.where(my_cross, (my_carrier + half) % pool_count, my_carrier)
-    which = (row - origin) % half + jnp.where(my_cross, half, 0)
-    index = jnp.where(my_cross, my_number, place)
     held = [here[b] for b in range(len(held[0])) for here in held]
-
-    own_row = jnp.minimum(row, relay_row - 1)
-    hot = (my_owner * block_count + my_block)[:, None] == jnp.arange(
-        columns * block_count, dtype=jnp.int32
-    )[None, :]
-    wanted_len = jnp.sum(jnp.where(hot, store_len.reshape(1, -1), 0), axis=1)
-    own = lambda a: lax.dynamic_index_in_dim(
-        a.reshape(relay_row, per_device), own_row, 0, keepdims=False
-    )
-    live = (row < relay_row).astype(jnp.int32) + row % 2 * 2
-    meta = jnp.concatenate([live[None], own(wanted_len), own(which), own(index)]).astype(jnp.int32)
 
     attn_out, q_grad, cond_grad, keep, give = run_spans(
         meta,

time: 128 us -> 134 us (1.047)
  starting transfers between devices: 21.8 us -> 26.3 us
    ppermute x10, waiting for transfers between devices: 16.7 us -> 30.5 us  [hop(): lax.ppermute(array, axes, [(a * columns + j, b * columns + j) for a, b in...]
    all_to_all x2, waiting for transfers between devices: 9.49 us -> 0.01 us  [body(): lax.all_to_all(sends, 'dp', split_axis=0, concat_axis=0, tiled=True)]
    all_to_all x2, starting transfers between devices: 8.48 us -> 12.7 us  [body(): lax.all_to_all(sends, 'dp', split_axis=0, concat_axis=0, tiled=True)]
    all_to_all x1, waiting for transfers between devices: 7.09 us -> 4.1 us  [to_all(): return lax.all_to_all(copies, axis, split_axis=0, concat_axis=0, tiled=True)]
    unnamed x31 -> x29, local copies, waits for them, and re-layouts: 9.49 us -> 9.29 us
  transfers between devices with their start and end apart: 15 -> 15, of which waited for: 10 -> 8; matrix products, arithmetic and copies ran while one was open for 13% -> 14% of each run, Pallas kernels for 2% -> 2%
where the time goes in v19:
time: 134 us; the launch traced here: 133 us
  waiting for transfers between devices  41.5 us (31%)
  Pallas kernels  28.8 us (21%)
  starting transfers between devices  26.3 us (20%)
  local copies, waits for them, and re-layouts  14.3 us (11%)
  blocking collectives  12.9 us (10%)
  other arithmetic  8.2 us (6%)
    ppermute x10, waiting for transfers between devices, hop(): lax.ppermute(array, axes, [(a * columns + j, b * columns + j) for a, b in...  30.5 us
    pallas_call x1, Pallas kernels, run_spans(): pl.pallas_call(functools.partial(span_kernel, len(held), nbr_count, bound...  24.7 us
    all_to_all x1, blocking collectives, scatter_sum(): lax.all_to_all(parts, axes[1], split_axis=0, concat_axis=0, tiled=True)  12.9 us
    all_to_all x2, starting transfers between devices, body(): lax.all_to_all(sends, 'dp', split_axis=0, concat_axis=0, tiled=True)  12.7 us
    unnamed x29, local copies, waits for them, and re-layouts  9.29 us
    all_to_all x1, starting transfers between devices, to_all(): return lax.all_to_all(copies, axis, split_axis=0, concat_axis=0, tiled=True)  8.23 us
    ppermute x2, waiting for transfers between devices, scatter_sum(): lax.ppermute(a, axes[0], [(i, i ^ bit) for i in range(size)])  6.86 us
    ppermute x10, starting transfers between devices, hop(): lax.ppermute(array, axes, [(a * columns + j, b * columns + j) for a, b in...  4.77 us
  transfers between devices with their start and end apart: 15, of which 8 were waited for; matrix products, arithmetic and copies ran while one was open for 14% of the time, Pallas kernels for 2%

profile of v19, /device:TPU:0, one launch (start us, length us, event | category | flops | bytes accessed | tf_op | source)
XLA Modules:
  0.0 133.0 jit_solution(16639476299748060951)
XLA Ops:
  0.7 1.6 %slice.32 = bf16[16,96,512]{2,1,0:T(8,128)(2,1)S(1)} slice(bf16[16,128,512]{2,1,0:T(8,128)(2,1)} %bitcast.44), slice={[0:16], [0:96], [0:512]} | slice | bytes 3145728 | tf_op jit(solution)/shard_map/slice | solution.py:347
  2.2 0.8 collective-permute-start
  3.0 0.1 copy.43
  3.2 0.1 copy.44
  3.5 0.6 broadcast_in_dim.82
  4.1 8.2 %all-to-all-start = ((s32[32,1,128]{2,1,0:T(1,128)}), s32[32,1,128]{2,1,0:T(1,128)S(1)}, u32[]{:S(2)}, u32[]{:S(2)}) async-start(s32[32,1,128]{2,1,0:T(1,128)} %broadcast_in_dim.82), calls=%async_computation | async-start | bytes 32768 | tf_op jit(solution)/shard_map/all_to_all | solution.py:352
  12.4 1.6 %broadcast_select_fusion.refs_0_ = bf16[16,96,512]{2,1,0:T(8,128)(2,1)S(1)} fusion(bf16[16,96,512]{2,1,0:T(8,128)(2,1)S(1)} %collective-permute-done, pred[]{:T(512)S(6)} %eq.159, bf16[16,128,512]{2,1,0:T(8,128)(2,1)} %bitcast.45), kind=kLoop, calls=%fused_computation | loop fusion | flops 786432 | bytes 4718593 | tf_op jit(solution)/shard_map/jit(_where)/select_n | solution.py:402
  14.0 1.3 collective-permute-start.1
  15.4 6.5 %copy.45 = bf16[512,4096]{0,1:T(8,128)(2,1)} copy(bf16[512,4096]{1,0:T(8,128)(2,1)} %rest_8_.1) | data formatting | bytes 8388608 | tf_op args[10]
  21.8 4.1 %all-to-all-done = s32[32,1,128]{2,1,0:T(1,128)S(1)} async-done(((s32[32,1,128]{2,1,0:T(1,128)}), s32[32,1,128]{2,1,0:T(1,128)S(1)}, u32[]{:S(2)}, u32[]{:S(2)}) %all-to-all-start) | async-done | bytes 16416 | tf_op jit(solution)/shard_map/all_to_all | solution.py:352
  26.0 0.3 convert_reduce_fusion.4
  26.4 0.6 convert_reduce_fusion.1
  27.2 0.2 select_reduce_fusion
  27.5 2.3 %collective-permute-done.1.refs_1_ = bf16[16,96,512]{2,1,0:T(8,128)(2,1)S(1)} collective-permute-done((bf16[16,96,512]{2,1,0:T(8,128)(2,1)S(1)}, bf16[16,96,512]{2,1,0:T(8,128)(2,1)S(1)}, u32[]{:S(2)}, u32[]{:S(2)}) %collective-permute-start.1) | collective-permute-done | bytes 1572896 | tf_op jit(solution)/shard_map/ppermute | solution.py:339
  29.8 1.5 %shard_map.138 = bf16[8,96,512]{2,1,0:T(8,128)(2,1)} custom-call(s32[9]{0:T(128)S(1)} %pad_add_fusion.4.meta, bf16[16,96,512]{2,1,0:T(8,128)(2,1)S(1)} %broadcast_select_fusion.refs_0_, bf16[16,96,512]{2,1,0:T(8,128)(2,1)S(1)} %collective-permute-done.1.refs_1_), custom_call_target="tpu_custom_call" | custom-call | tf_op jit(solution)/shard_map/pallas_call | solution.py:259
  31.3 6.9 %all-to-all-start.1 = ((bf16[8,96,512]{2,1,0:T(8,128)(2,1)}), bf16[8,96,512]{2,1,0:T(8,128)(2,1)S(1)}, u32[]{:S(2)}, u32[]{:S(2)}) async-start(bf16[8,96,512]{2,1,0:T(8,128)(2,1)} %shard_map.138), calls=%async_computation.1 | async-start | bytes 1572864 | tf_op jit(solution)/shard_map/all_to_all | solution.py:409
  38.1 1.1 slice.27
  39.2 0.7 collective-permute-start.2
  40.5 0.5 broadcast.437
  41.0 0.7 fusion.34
  41.8 1.1 broadcast_select_fusion.1.refs_0_
  42.9 1.3 collective-permute-start.3
  44.2 0.1 select_reduce_fusion.2
  44.4 0.2 select_reduce_fusion.1
  44.6 13.6 %collective-permute-done.3.refs_1_ = bf16[16,32,512]{2,1,0:T(8,128)(2,1)S(1)} collective-permute-done((bf16[16,32,512]{2,1,0:T(8,128)(2,1)S(1)}, bf16[16,32,512]{2,1,0:T(8,128)(2,1)S(1)}, u32[]{:S(2)}, u32[]{:S(2)}) %collective-permute-start.3) | collective-permute-done | bytes 524320 | tf_op jit(solution)/shard_map/ppermute | solution.py:339
  58.3 1.3 shard_map.139
  59.6 5.9 %all-to-all-start.2 = ((bf16[8,32,512]{2,1,0:T(8,128)(2,1)}), bf16[8,32,512]{2,1,0:T(8,128)(2,1)S(1)}, u32[]{:S(2)}, u32[]{:S(2)}) async-start(bf16[8,32,512]{2,1,0:T(8,128)(2,1)} %shard_map.139), calls=%async_computation.2 | async-start | bytes 524288 | tf_op jit(solution)/shard_map/all_to_all | solution.py:409
  65.4 0.6 shard_map.140
  66.2 0.6 pad_add_fusion.3.meta
  66.8 10.2 %collective-permute-done.6.rest_4_ = bf16[4,96,512]{2,1,0:T(8,128)(2,1)} collective-permute-done((bf16[4,96,512]{2,1,0:T(8,128)(2,1)S(1)}, bf16[4,96,512]{2,1,0:T(8,128)(2,1)}, u32[]{:S(2)}, u32[]{:S(2)}) %collective-permute-start.6) | collective-permute-done | bytes 393248 | tf_op jit(solution)/shard_map/ppermute | solution.py:339
  77.1 0.7 shard_map.141
  77.9 0.4 collective-permute-start.7
  78.2 0.3 collective-permute-start.5
  78.5 0.8 copy.50
  79.4 0.9 copy.49
  80.2 3.6 %collective-permute-done.7.rest_5_ = bf16[4,32,512]{2,1,0:T(8,128)(2,1)S(1)} collective-permute-done((bf16[4,32,512]{2,1,0:T(8,128)(2,1)S(1)}, bf16[4,32,512]{2,1,0:T(8,128)(2,1)S(1)}, u32[]{:S(2)}, u32[]{:S(2)}) %collective-permute-start.7) | collective-permute-done | bytes 131104 | tf_op jit(solution)/shard_map/ppermute | solution.py:339
  83.9 0.6 bitcast_convert_fusion.cond_ref
  84.5 0.7 collective-permute-done.9.rest_7_
  85.2 0.6 copy-done.11
  85.8 0.3 copy-done.8
  86.1 24.7 %shard_map.142 = (bf16[256,2048]{1,0:T(8,128)(2,1)}, bf16[256,2048]{1,0:T(8,128)(2,1)}, f32[4,512]{1,0:T(4,128)}, f32[256,512]{1,0:T(8,128)}, bf16[256,512]{1,0:T(8,128)(2,1)}) custom-call(s32[25]{0:T(128)} %pad_add_fusion.3.meta, bf16[256,2048]{1,0:T(8,128)(2,1)} %bitcast.59, bf16[256,2048]{1,0:T(8,128)(2,1)} %bitcast.60, ...), custom_call_target="tpu_custom_call" | custom-call | flops 11811160064 | bytes 16777216 | tf_op jit(solution)/shard_map/pallas_call | solution.py:202
  110.8 0.2 collective-permute-start.10
  111.0 1.6 %collective-permute-done.10 = bf16[256,512]{1,0:T(8,128)(2,1)S(1)} collective-permute-done((bf16[256,512]{1,0:T(8,128)(2,1)}, bf16[256,512]{1,0:T(8,128)(2,1)S(1)}, u32[]{:S(2)}, u32[]{:S(2)}) %collective-permute-start.10) | collective-permute-done | bytes 262176 | tf_op jit(solution)/shard_map/ppermute | solution.py:297
  112.6 1.1 convert_add_fusion
  113.8 0.4 collective-permute-start.11
  114.2 5.3 %collective-permute-done.11 = bf16[1,128,512]{2,1,0:T(8,128)(2,1)S(1)} collective-permute-done((bf16[1,128,512]{2,1,0:T(8,128)(2,1)S(1)}, bf16[1,128,512]{2,1,0:T(8,128)(2,1)S(1)}, u32[]{:S(2)}, u32[]{:S(2)}) %collective-permute-start.11) | collective-permute-done | bytes 131104 | tf_op jit(solution)/shard_map/ppermute | solution.py:297
  119.4 12.9 %all_to_all.20 = bf16[8,16,512]{2,1,0:T(8,128)(2,1)S(1)} all-to-all(bf16[8,16,512]{2,1,0:T(8,128)(2,1)S(1)} %bitcast.51), channel_id=1, replica_groups=mesh['pool'=4,'dp'=8] {'dp'}, dimensions={0} | all-to-all | bytes 262144 | tf_op jit(solution)/shard_map/all_to_all | solution.py:308
  132.3 0.6 convert_reduce_fusion
  (71 shorter events, 2.0 us)
Async XLA Ops:
  0.6 2.4 %copy-start.5 = (s32[1,1,4,2]{2,3,1,0:T(2,128)S(1)}, s32[1,1,4,2]{2,3,1,0:T(2,128)}, u32[]{:S(2)}) copy-start(s32[1,1,4,2]{2,3,1,0:T(2,128)} %param.14) | copy-start | bytes 100
  0.6 2.6 %copy-start.6 = (s32[1,1,4,2]{2,3,1,0:T(2,128)S(1)}, s32[1,1,4,2]{2,3,1,0:T(2,128)}, u32[]{:S(2)}) copy-start(s32[1,1,4,2]{2,3,1,0:T(2,128)} %param.15) | copy-start | bytes 100
  0.7 2.7 %copy-start.7 = (s32[1,1,16]{2,1,0:T(1,128)S(1)}, s32[1,1,16]{2,1,0:T(1,128)}, u32[]{:S(2)}) copy-start(s32[1,1,16]{2,1,0:T(1,128)} %param.17) | copy-start | bytes 196
  2.2 10.1 %collective-permute-start = (bf16[16,96,512]{2,1,0:T(8,128)(2,1)S(1)}, bf16[16,96,512]{2,1,0:T(8,128)(2,1)S(1)}, u32[]{:S(2)}, u32[]{:S(2)}) collective-permute-start(bf16[16,96,512]{2,1,0:T(8,128)(2,1)S(1)} %slice.32), channel_id=1, source_target_pairs={{24,8},{25,9},{26,10},{27,11},{28,12},{29,13},{30,14},{31,15}} | collective-permute-start | bytes 4718600 | tf_op jit(solution)/shard_map/ppermute | solution.py:339
  4.1 21.9 %all-to-all-start = ((s32[32,1,128]{2,1,0:T(1,128)}), s32[32,1,128]{2,1,0:T(1,128)S(1)}, u32[]{:S(2)}, u32[]{:S(2)}) async-start(s32[32,1,128]{2,1,0:T(1,128)} %broadcast_in_dim.82), calls=%async_computation | async-start | bytes 32768 | tf_op jit(solution)/shard_map/all_to_all | solution.py:352
  14.0 15.8 %collective-permute-start.1 = (bf16[16,96,512]{2,1,0:T(8,128)(2,1)S(1)}, bf16[16,96,512]{2,1,0:T(8,128)(2,1)S(1)}, u32[]{:S(2)}, u32[]{:S(2)}) collective-permute-start(bf16[16,96,512]{2,1,0:T(8,128)(2,1)S(1)} %broadcast_select_fusion.refs_0_), channel_id=1, source_target_pairs={{24,16},{25,17},{26,18},{27,19},{28,20},{29,21},{30,22},{31,23},{8... | collective-permute-start | bytes 4718600 | tf_op jit(solution)/shard_map/ppermute | solution.py:339
  31.3 28.3 %all-to-all-start.1 = ((bf16[8,96,512]{2,1,0:T(8,128)(2,1)}), bf16[8,96,512]{2,1,0:T(8,128)(2,1)S(1)}, u32[]{:S(2)}, u32[]{:S(2)}) async-start(bf16[8,96,512]{2,1,0:T(8,128)(2,1)} %shard_map.138), calls=%async_computation.1 | async-start | bytes 1572864 | tf_op jit(solution)/shard_map/all_to_all | solution.py:409
  39.2 2.6 %collective-permute-start.2 = (bf16[16,32,512]{2,1,0:T(8,128)(2,1)S(1)}, bf16[16,32,512]{2,1,0:T(8,128)(2,1)S(1)}, u32[]{:S(2)}, u32[]{:S(2)}) collective-permute-start(bf16[16,32,512]{2,1,0:T(8,128)(2,1)S(1)} %slice.27), channel_id=1, source_target_pairs={{24,8},{25,9},{26,10},{27,11},{28,12},{29,13},{30,14},{31,15}} | collective-permute-start | bytes 1572872 | tf_op jit(solution)/shard_map/ppermute | solution.py:339
  42.9 15.4 %collective-permute-start.3 = (bf16[16,32,512]{2,1,0:T(8,128)(2,1)S(1)}, bf16[16,32,512]{2,1,0:T(8,128)(2,1)S(1)}, u32[]{:S(2)}, u32[]{:S(2)}) collective-permute-start(bf16[16,32,512]{2,1,0:T(8,128)(2,1)S(1)} %broadcast_select_fusion.1.refs_0_), channel_id=1, source_target_pairs={{24,16},{25,17},{26,18},{27,19},{28,20},{29,21},{30,22},{31,23},{8... | collective-permute-start | bytes 1572872 | tf_op jit(solution)/shard_map/ppermute | solution.py:339
  44.6 33.9 %copy-start.2 = (bf16[512,256]{1,0:T(8,128)(2,1)S(1)}, bf16[512,256]{1,0:T(8,128)(2,1)}, u32[]{:S(2)}) copy-start(bf16[512,256]{1,0:T(8,128)(2,1)} %down_ref.1) | copy-start | bytes 786436
  59.5 19.8 %copy-start.3 = (bf16[256,512]{1,0:T(8,128)(2,1)S(1)}, bf16[256,512]{1,0:T(8,128)(2,1)}, u32[]{:S(2)}) copy-start(bf16[256,512]{1,0:T(8,128)(2,1)} %up_ref.1) | copy-start | bytes 786436
  59.5 24.3 %copy-start.4 = (bf16[1,1,4,512]{3,2,1,0:T(4,128)(2,1)S(1)}, bf16[1,1,4,512]{3,2,1,0:T(4,128)(2,1)}, u32[]{:S(2)}) copy-start(bf16[1,1,4,512]{3,2,1,0:T(4,128)(2,1)} %param.13) | copy-start | bytes 12292
  59.5 20.7 %copy-start = (bf16[8,96,512]{2,1,0:T(8,128)(2,1)}, bf16[8,96,512]{2,1,0:T(8,128)(2,1)S(1)}, u32[]{:S(2)}) copy-start(bf16[8,96,512]{2,1,0:T(8,128)(2,1)S(1)} %all-to-all-done.1.refs_0_.rest_0_) | copy-start | bytes 2359300
  59.6 17.6 %all-to-all-start.2 = ((bf16[8,32,512]{2,1,0:T(8,128)(2,1)}), bf16[8,32,512]{2,1,0:T(8,128)(2,1)S(1)}, u32[]{:S(2)}, u32[]{:S(2)}) async-start(bf16[8,32,512]{2,1,0:T(8,128)(2,1)} %shard_map.139), calls=%async_computation.2 | async-start | bytes 524288 | tf_op jit(solution)/shard_map/all_to_all | solution.py:409
  66.0 11.0 %collective-permute-start.6 = (bf16[4,96,512]{2,1,0:T(8,128)(2,1)S(1)}, bf16[4,96,512]{2,1,0:T(8,128)(2,1)}, u32[]{:S(2)}, u32[]{:S(2)}) collective-permute-start(bf16[4,96,512]{2,1,0:T(8,128)(2,1)S(1)} %shard_map.140), channel_id=1, source_target_pairs={{0,16},{1,17},{2,18},{3,19},{4,20},{5,21},{6,22},{7,23},{8,24},{9,... | collective-permute-start | bytes 1179656 | tf_op jit(solution)/shard_map/ppermute | solution.py:339
  66.2 19.0 %collective-permute-start.4 = (bf16[8,96,512]{2,1,0:T(8,128)(2,1)S(1)}, bf16[8,96,512]{2,1,0:T(8,128)(2,1)S(1)}, u32[]{:S(2)}, u32[]{:S(2)}) collective-permute-start(bf16[8,96,512]{2,1,0:T(8,128)(2,1)S(1)} %all-to-all-done.1.refs_0_.rest_0_), channel_id=1, source_target_pairs={{0,8},{1,9},{2,10},{3,11},{4,12},{5,13},{6,14},{7,15},{8,0},{9,1},... | collective-permute-start | bytes 2359304 | tf_op jit(solution)/shard_map/ppermute | solution.py:339
  77.0 8.2 %collective-permute-start.8 = (bf16[4,96,512]{2,1,0:T(8,128)(2,1)}, bf16[4,96,512]{2,1,0:T(8,128)(2,1)}, u32[]{:S(2)}, u32[]{:S(2)}) collective-permute-start(bf16[4,96,512]{2,1,0:T(8,128)(2,1)} %collective-permute-done.6.rest_4_), channel_id=1, source_target_pairs={{0,8},{1,9},{2,10},{3,11},{4,12},{5,13},{6,14},{7,15},{8,0},{9,1},... | collective-permute-start | bytes 1179656 | tf_op jit(solution)/shard_map/ppermute | solution.py:339
  77.1 8.1 %copy-start.1 = (bf16[8,32,512]{2,1,0:T(8,128)(2,1)}, bf16[8,32,512]{2,1,0:T(8,128)(2,1)S(1)}, u32[]{:S(2)}) copy-start(bf16[8,32,512]{2,1,0:T(8,128)(2,1)S(1)} %all-to-all-done.2.refs_0_.rest_1_) | copy-start | bytes 786436
  77.9 6.0 %collective-permute-start.7 = (bf16[4,32,512]{2,1,0:T(8,128)(2,1)S(1)}, bf16[4,32,512]{2,1,0:T(8,128)(2,1)S(1)}, u32[]{:S(2)}, u32[]{:S(2)}) collective-permute-start(bf16[4,32,512]{2,1,0:T(8,128)(2,1)S(1)} %shard_map.141), channel_id=1, source_target_pairs={{0,16},{1,17},{2,18},{3,19},{4,20},{5,21},{6,22},{7,23},{8,24},{9,... | collective-permute-start | bytes 393224 | tf_op jit(solution)/shard_map/ppermute | solution.py:339
  78.2 6.3 %collective-permute-start.5 = (bf16[8,32,512]{2,1,0:T(8,128)(2,1)S(1)}, bf16[8,32,512]{2,1,0:T(8,128)(2,1)S(1)}, u32[]{:S(2)}, u32[]{:S(2)}) collective-permute-start(bf16[8,32,512]{2,1,0:T(8,128)(2,1)S(1)} %all-to-all-done.2.refs_0_.rest_1_), channel_id=1, source_target_pairs={{0,8},{1,9},{2,10},{3,11},{4,12},{5,13},{6,14},{7,15},{8,0},{9,1},... | collective-permute-start | bytes 786440 | tf_op jit(solution)/shard_map/ppermute | solution.py:339
  83.8 1.4 %copy-start.10 = (bf16[4,32,512]{2,1,0:T(8,128)(2,1)}, bf16[4,32,512]{2,1,0:T(8,128)(2,1)S(1)}, u32[]{:S(2)}) copy-start(bf16[4,32,512]{2,1,0:T(8,128)(2,1)S(1)} %collective-permute-done.7.rest_5_) | copy-start | bytes 393220
  83.8 1.3 %collective-permute-start.9 = (bf16[4,32,512]{2,1,0:T(8,128)(2,1)S(1)}, bf16[4,32,512]{2,1,0:T(8,128)(2,1)S(1)}, u32[]{:S(2)}, u32[]{:S(2)}) collective-permute-start(bf16[4,32,512]{2,1,0:T(8,128)(2,1)S(1)} %collective-permute-done.7.rest_5_), channel_id=1, source_target_pairs={{0,8},{1,9},{2,10},{3,11},{4,12},{5,13},{6,14},{7,15},{8,0},{9,1},... | collective-permute-start | bytes 393224 | tf_op jit(solution)/shard_map/ppermute | solution.py:339
  84.5 0.7 copy-start.9
  85.2 0.7 copy-start.11
  85.2 0.9 copy-start.8
  110.8 1.8 %collective-permute-start.10 = (bf16[256,512]{1,0:T(8,128)(2,1)}, bf16[256,512]{1,0:T(8,128)(2,1)S(1)}, u32[]{:S(2)}, u32[]{:S(2)}) collective-permute-start(bf16[256,512]{1,0:T(8,128)(2,1)} %get-tuple-element.23), channel_id=1, source_target_pairs={{0,8},{8,0},{16,24},{24,16},{1,9},{9,1},{17,25},{25,17},{2,10},{10... | collective-permute-start | bytes 786440 | tf_op jit(solution)/shard_map/ppermute | solution.py:297
  113.8 5.6 %collective-permute-start.11 = (bf16[1,128,512]{2,1,0:T(8,128)(2,1)S(1)}, bf16[1,128,512]{2,1,0:T(8,128)(2,1)S(1)}, u32[]{:S(2)}, u32[]{:S(2)}) collective-permute-start(bf16[1,128,512]{2,1,0:T(8,128)(2,1)S(1)} %fusion.1), channel_id=1, source_target_pairs={{0,16},{8,24},{16,0},{24,8},{1,17},{9,25},{17,1},{25,9},{2,18},{10... | collective-permute-start | bytes 393224 | tf_op jit(solution)/shard_map/ppermute | solution.py:297

commit v20 on v17

--- a/solution.py
+++ b/solution.py
@@ -378,12 +378,19 @@
         mine_of, (owners, blocks, carrier, slot, crosses, number)
     )
     place = my_owner * slots + my_slot
+    spare = crossing // 4
+    usual = crossing - spare
     ring = jnp.arange(crossing, dtype=jnp.int32)
     mine = (my_cross & (my_carrier == row))[None, :] & (my_number[None, :] == ring[:, None])
     leaving_place = jnp.sum(jnp.where(mine, place[None, :], 0), axis=1)
 
     def share(array, step):
         return hop(array, [(p, p // half * half + (p + step) % half) for p in range(pool_count)])
+
+    def cross(arrived, places):
+        leaving = pick(0, places, [arrived])
+        landed = hop(leaving, [(p, (p + half) % pool_count) for p in range(pool_count)])
+        return [landed] + [share(landed, step) for step in range(1, half)]
 
     held = []
     for i in range(parts):
@@ -397,13 +404,23 @@
         arrived = lax.all_to_all(sends, "dp", split_axis=0, concat_axis=0, tiled=True)
         here = [arrived] + [share(arrived, step) for step in range(1, half)]
         if crossing:
-            leaving = pick(0, leaving_place, [arrived])
-            landed = hop(leaving, [(p, (p + half) % pool_count) for p in range(pool_count)])
-            here += [landed] + [share(landed, step) for step in range(1, half)]
+            here += cross(arrived, leaving_place[:usual])
         held.append(here)
+    if spare:
+        first = [here[0] for here in held]
+        extra = lax.cond(
+            jnp.any(crosses & (number >= usual)),
+            lambda arrays: [cross(a, leaving_place[usual:]) for a in arrays],
+            lambda arrays: [
+                [jnp.zeros((spare,) + a.shape[1:], a.dtype)] * half for a in arrays
+            ],
+            first,
+        )
+        held = [here + more for here, more in zip(held, extra)]
     origin = jnp.where(my_cross, (my_carrier + half) % pool_count, my_carrier)
-    which = (row - origin) % half + jnp.where(my_cross, half, 0)
-    index = jnp.where(my_cross, my_number, place)
+    late = my_cross & (my_number >= usual)
+    which = (row - origin) % half + jnp.where(my_cross, half, 0) + jnp.where(late, half, 0)
+    index = jnp.where(my_cross, my_number - jnp.where(late, usual, 0), place)
     held = [here[b] for b in range(len(held[0])) for here in held]
 
     own_row = jnp.minimum(row, relay_row - 1)

time: 128 us -> 135 us (1.055)
  local copies, waits for them, and re-layouts: 14.5 us -> 18.7 us
    all_to_all x2, waiting for transfers between devices: 9.49 us -> 20.7 us  [body(): lax.all_to_all(sends, 'dp', split_axis=0, concat_axis=0, tiled=True)]
    ppermute x10, waiting for transfers between devices: 16.7 us -> 8.08 us  [hop(): lax.ppermute(array, axes, [(a * columns + j, b * columns + j) for a, b in...]
    all_to_all x1, waiting for transfers between devices: 7.09 us -> 4.46 us  [to_all(): return lax.all_to_all(copies, axis, split_axis=0, concat_axis=0, tiled=True)]
    another operation x0 -> x4, local copies, waits for them, and re-layouts: none -> 2.53 us
    unnamed x31 -> x27, local copies, waits for them, and re-layouts: 9.49 us -> 10.3 us
  transfers between devices with their start and end apart: 15 -> 15, of which waited for: 10 -> 9; matrix products, arithmetic and copies ran while one was open for 13% -> 16% of each run, Pallas kernels for 2% -> 3%
where the time goes in v20:
time: 135 us; the launch traced here: 134 us
  waiting for transfers between devices  40.5 us (30%)
  Pallas kernels  29.4 us (22%)
  starting transfers between devices  22.2 us (16%)
  local copies, waits for them, and re-layouts  18.7 us (14%)
  blocking collectives  12.9 us (10%)
  other arithmetic  8.92 us (7%)
  between operations  1.67 us (1%)
    pallas_call x1, Pallas kernels, run_spans(): pl.pallas_call(functools.partial(span_kernel, len(held), nbr_count, bound...  25.5 us
    all_to_all x2, waiting for transfers between devices, body(): lax.all_to_all(sends, 'dp', split_axis=0, concat_axis=0, tiled=True)  20.7 us
    all_to_all x1, blocking collectives, scatter_sum(): lax.all_to_all(parts, axes[1], split_axis=0, concat_axis=0, tiled=True)  12.9 us
    unnamed x27, local copies, waits for them, and re-layouts  10.3 us
    all_to_all x2, starting transfers between devices, body(): lax.all_to_all(sends, 'dp', split_axis=0, concat_axis=0, tiled=True)  8.54 us
    all_to_all x1, starting transfers between devices, to_all(): return lax.all_to_all(copies, axis, split_axis=0, concat_axis=0, tiled=True)  8.23 us
    ppermute x10, waiting for transfers between devices, hop(): lax.ppermute(array, axes, [(a * columns + j, b * columns + j) for a, b in...  8.08 us
    ppermute x2, waiting for transfers between devices, scatter_sum(): lax.ppermute(a, axes[0], [(i, i ^ bit) for i in range(size)])  7.21 us
  transfers between devices with their start and end apart: 15, of which 9 were waited for; matrix products, arithmetic and copies ran while one was open for 16% of the time, Pallas kernels for 3%

profile of v20, /device:TPU:0, one launch (start us, length us, event | category | flops | bytes accessed | tf_op | source)
XLA Modules:
  0.0 134.2 jit_solution(13748240138153951949)
XLA Ops:
  0.7 1.6 %slice.37 = bf16[16,96,512]{2,1,0:T(8,128)(2,1)S(1)} slice(bf16[16,128,512]{2,1,0:T(8,128)(2,1)} %bitcast.45), slice={[0:16], [0:96], [0:512]} | slice | bytes 3145728 | tf_op jit(solution)/shard_map/slice | solution.py:347
  2.3 0.8 collective-permute-start.4
  3.5 0.6 broadcast_in_dim.87
  4.1 8.2 %all-to-all-start = ((s32[32,1,128]{2,1,0:T(1,128)}), s32[32,1,128]{2,1,0:T(1,128)S(1)}, u32[]{:S(2)}, u32[]{:S(2)}) async-start(s32[32,1,128]{2,1,0:T(1,128)} %broadcast_in_dim.87), calls=%async_computation | async-start | bytes 32768 | tf_op jit(solution)/shard_map/all_to_all | solution.py:352
  12.4 0.8 copy.50
  13.3 1.8 %copy.49 = bf16[256,512]{0,1:T(8,128)(2,1)} copy(bf16[256,512]{1,0:T(8,128)(2,1)} %up_ref.1) | data formatting | bytes 524288 | tf_op args[9]
  15.1 6.5 %copy.45 = bf16[512,4096]{0,1:T(8,128)(2,1)} copy(bf16[512,4096]{1,0:T(8,128)(2,1)} %rest_12_.1) | data formatting | bytes 8388608 | tf_op args[10]
  21.5 4.5 %all-to-all-done = s32[32,1,128]{2,1,0:T(1,128)S(1)} async-done(((s32[32,1,128]{2,1,0:T(1,128)}), s32[32,1,128]{2,1,0:T(1,128)S(1)}, u32[]{:S(2)}, u32[]{:S(2)}) %all-to-all-start) | async-done | bytes 16416 | tf_op jit(solution)/shard_map/all_to_all | solution.py:352
  26.0 1.6 %broadcast_select_fusion.refs_0_ = bf16[16,96,512]{2,1,0:T(8,128)(2,1)S(1)} fusion(bf16[16,96,512]{2,1,0:T(8,128)(2,1)S(1)} %collective-permute-done.4, pred[]{:T(512)S(6)} %eq.145, bf16[16,128,512]{2,1,0:T(8,128)(2,1)} %bitcast.46), kind=kLoop, calls=%fused_computation.1 | loop fusion | flops 786432 | bytes 4718593 | tf_op jit(solution)/shard_map/jit(_where)/select_n | solution.py:397
  27.6 1.3 collective-permute-start.5
  29.1 0.3 convert_reduce_fusion.4
  29.4 0.6 convert_reduce_fusion.1
  30.2 1.9 %slice.35 = bf16[16,32,512]{2,1,0:T(8,128)(2,1)} slice(bf16[16,128,512]{2,1,0:T(8,128)(2,1)} %bitcast.47), slice={[0:16], [96:128], [0:512]} | slice | bytes 1048576 | tf_op jit(solution)/shard_map/slice | solution.py:347
  32.1 1.5 %collective-permute-start.6 = (bf16[16,32,512]{2,1,0:T(8,128)(2,1)}, bf16[16,32,512]{2,1,0:T(8,128)(2,1)}, u32[]{:S(2)}, u32[]{:S(2)}) collective-permute-start(bf16[16,32,512]{2,1,0:T(8,128)(2,1)} %slice.35), channel_id=1, source_target_pairs={{24,8},{25,9},{26,10},{27,11},{28,12},{29,13},{30,14},{31,15}} | collective-permute-start | bytes 1572872 | tf_op jit(solution)/shard_map/ppermute | solution.py:339
  33.6 0.2 select_reduce_fusion
  33.8 1.5 %shard_map.138 = bf16[8,96,512]{2,1,0:T(8,128)(2,1)} custom-call(s32[9]{0:T(128)S(1)} %pad_add_fusion.3.meta, bf16[16,96,512]{2,1,0:T(8,128)(2,1)S(1)} %broadcast_select_fusion.refs_0_, bf16[16,96,512]{2,1,0:T(8,128)(2,1)S(1)} %collective-permute-done.5.refs_1_), custom_call_target="tpu_custom_call" | custom-call | tf_op jit(solution)/shard_map/pallas_call | solution.py:259
  35.3 5.0 %all-to-all-start.1 = ((bf16[8,96,512]{2,1,0:T(8,128)(2,1)}), bf16[8,96,512]{2,1,0:T(8,128)(2,1)S(1)}, u32[]{:S(2)}, u32[]{:S(2)}) async-start(bf16[8,96,512]{2,1,0:T(8,128)(2,1)} %shard_map.138), calls=%async_computation.1 | async-start | bytes 1572864 | tf_op jit(solution)/shard_map/all_to_all | solution.py:404
  40.4 0.6 bitcast_convert_fusion.cond_ref
  41.1 0.6 and_reduce_fusion
  41.7 1.3 broadcast_select_fusion.1.refs_0_
  43.0 1.3 collective-permute-start.7
  44.3 0.5 broadcast.451
  44.8 0.7 fusion.35
  45.6 1.9 %collective-permute-done.7.refs_1_ = bf16[16,32,512]{2,1,0:T(8,128)(2,1)S(1)} collective-permute-done((bf16[16,32,512]{2,1,0:T(8,128)(2,1)S(1)}, bf16[16,32,512]{2,1,0:T(8,128)(2,1)S(1)}, u32[]{:S(2)}, u32[]{:S(2)}) %collective-permute-start.7) | collective-permute-done | bytes 524320 | tf_op jit(solution)/shard_map/ppermute | solution.py:339
  47.5 1.3 shard_map.139
  48.8 13.1 %all-to-all-done.1.refs_0_.rest_0_ = bf16[8,96,512]{2,1,0:T(8,128)(2,1)S(1)} async-done(((bf16[8,96,512]{2,1,0:T(8,128)(2,1)}), bf16[8,96,512]{2,1,0:T(8,128)(2,1)S(1)}, u32[]{:S(2)}, u32[]{:S(2)}) %all-to-all-start.1) | async-done | bytes 786464 | tf_op jit(solution)/shard_map/all_to_all | solution.py:404
  61.8 3.5 %all-to-all-start.2 = ((bf16[8,32,512]{2,1,0:T(8,128)(2,1)}), bf16[8,32,512]{2,1,0:T(8,128)(2,1)S(1)}, u32[]{:S(2)}, u32[]{:S(2)}) async-start(bf16[8,32,512]{2,1,0:T(8,128)(2,1)} %shard_map.139), calls=%async_computation.2 | async-start | bytes 524288 | tf_op jit(solution)/shard_map/all_to_all | solution.py:404
  65.8 0.6 shard_map.140
  66.9 7.6 %all-to-all-done.2.refs_0_.rest_1_ = bf16[8,32,512]{2,1,0:T(8,128)(2,1)S(1)} async-done(((bf16[8,32,512]{2,1,0:T(8,128)(2,1)}), bf16[8,32,512]{2,1,0:T(8,128)(2,1)S(1)}, u32[]{:S(2)}, u32[]{:S(2)}) %all-to-all-start.2) | async-done | bytes 262176 | tf_op jit(solution)/shard_map/all_to_all | solution.py:404
  74.5 0.6 collective-permute-done.10.rest_4_
  75.9 0.6 shard_map.141
  76.5 2.5 %conditional.1 = (bf16[1,96,512]{2,1,0:T(8,128)(2,1)}, bf16[1,96,512]{2,1,0:T(8,128)(2,1)}, bf16[1,32,512]{2,1,0:T(8,128)(2,1)}, bf16[1,32,512]{2,1,0:T(8,128)(2,1)}) conditional(s32[]{:T(128)} %convert_element_type.59, () %tuple.18, (s32[4]{0:T(128)S(1)}, bf16[8,96,512]{2,1,0:T(8,128)(2,1)S(1)}, bf16[8,32,512]{2,1,0:T(8,128)(2,1)S(1)}) %tuple.19), branch_computations={%region_8.9_spmd, %region_9.10_spmd} | conditional | flops 2 | bytes 1048792 | solution.py:411
  76.5 0.6 broadcast.384.clone
  77.1 0.6 broadcast.384
  77.7 0.7 broadcast.383.clone
  78.4 0.6 broadcast.383
  79.0 0.3 collective-permute-start.11
  79.3 4.9 %collective-permute-done.11.rest_5_ = bf16[3,32,512]{2,1,0:T(8,128)(2,1)S(1)} collective-permute-done((bf16[3,32,512]{2,1,0:T(8,128)(2,1)S(1)}, bf16[3,32,512]{2,1,0:T(8,128)(2,1)S(1)}, u32[]{:S(2)}, u32[]{:S(2)}) %collective-permute-start.11) | collective-permute-done | bytes 98336 | tf_op jit(solution)/shard_map/ppermute | solution.py:339
  84.2 0.6 pad_add_fusion.2.meta
  84.8 0.7 collective-permute-done.13.rest_7_
  85.6 0.6 copy-done.10
  86.4 0.2 copy-done.5
  86.6 25.5 %shard_map.142 = (bf16[256,2048]{1,0:T(8,128)(2,1)}, bf16[256,2048]{1,0:T(8,128)(2,1)}, f32[4,512]{1,0:T(4,128)}, f32[256,512]{1,0:T(8,128)}, bf16[256,512]{1,0:T(8,128)(2,1)}) custom-call(s32[25]{0:T(128)} %pad_add_fusion.2.meta, bf16[256,2048]{1,0:T(8,128)(2,1)} %bitcast.61, bf16[256,2048]{1,0:T(8,128)(2,1)} %bitcast.62, ...), custom_call_target="tpu_custom_call" | custom-call | flops 11811160064 | bytes 16777216 | tf_op jit(solution)/shard_map/pallas_call | solution.py:202
  112.2 1.7 %collective-permute-done.14 = bf16[256,512]{1,0:T(8,128)(2,1)S(1)} collective-permute-done((bf16[256,512]{1,0:T(8,128)(2,1)}, bf16[256,512]{1,0:T(8,128)(2,1)S(1)}, u32[]{:S(2)}, u32[]{:S(2)}) %collective-permute-start.14) | collective-permute-done | bytes 262176 | tf_op jit(solution)/shard_map/ppermute | solution.py:297
  113.9 1.1 convert_add_fusion
  115.2 5.5 %collective-permute-done.15 = bf16[1,128,512]{2,1,0:T(8,128)(2,1)S(1)} collective-permute-done((bf16[1,128,512]{2,1,0:T(8,128)(2,1)S(1)}, bf16[1,128,512]{2,1,0:T(8,128)(2,1)S(1)}, u32[]{:S(2)}, u32[]{:S(2)}) %collective-permute-start.15) | collective-permute-done | bytes 131104 | tf_op jit(solution)/shard_map/ppermute | solution.py:297
  120.7 12.9 %all_to_all.20 = bf16[8,16,512]{2,1,0:T(8,128)(2,1)S(1)} all-to-all(bf16[8,16,512]{2,1,0:T(8,128)(2,1)S(1)} %bitcast.52), channel_id=1, replica_groups=mesh['pool'=4,'dp'=8] {'dp'}, dimensions={0} | all-to-all | bytes 262144 | tf_op jit(solution)/shard_map/all_to_all | solution.py:308
  133.6 0.6 convert_reduce_fusion
  (74 shorter events, 2.8 us)
Async XLA Ops:
  0.6 2.4 %copy-start.2 = (s32[1,1,4,2]{2,3,1,0:T(2,128)S(1)}, s32[1,1,4,2]{2,3,1,0:T(2,128)}, u32[]{:S(2)}) copy-start(s32[1,1,4,2]{2,3,1,0:T(2,128)} %param.16) | copy-start | bytes 100
  0.6 2.6 %copy-start.3 = (s32[1,1,4,2]{2,3,1,0:T(2,128)S(1)}, s32[1,1,4,2]{2,3,1,0:T(2,128)}, u32[]{:S(2)}) copy-start(s32[1,1,4,2]{2,3,1,0:T(2,128)} %param.17) | copy-start | bytes 100
  0.7 2.8 %copy-start.4 = (s32[1,1,16]{2,1,0:T(1,128)S(1)}, s32[1,1,16]{2,1,0:T(1,128)}, u32[]{:S(2)}) copy-start(s32[1,1,16]{2,1,0:T(1,128)} %param.19) | copy-start | bytes 196
  0.7 11.8 %copy-start = (bf16[512,256]{1,0:T(8,128)(2,1)S(1)}, bf16[512,256]{1,0:T(8,128)(2,1)}, u32[]{:S(2)}) copy-start(bf16[512,256]{1,0:T(8,128)(2,1)} %down_ref.1) | copy-start | bytes 786436
  2.3 23.7 %collective-permute-start.4 = (bf16[16,96,512]{2,1,0:T(8,128)(2,1)S(1)}, bf16[16,96,512]{2,1,0:T(8,128)(2,1)S(1)}, u32[]{:S(2)}, u32[]{:S(2)}) collective-permute-start(bf16[16,96,512]{2,1,0:T(8,128)(2,1)S(1)} %slice.37), channel_id=1, source_target_pairs={{24,8},{25,9},{26,10},{27,11},{28,12},{29,13},{30,14},{31,15}} | collective-permute-start | bytes 4718600 | tf_op jit(solution)/shard_map/ppermute | solution.py:339
  4.1 21.9 %all-to-all-start = ((s32[32,1,128]{2,1,0:T(1,128)}), s32[32,1,128]{2,1,0:T(1,128)S(1)}, u32[]{:S(2)}, u32[]{:S(2)}) async-start(s32[32,1,128]{2,1,0:T(1,128)} %broadcast_in_dim.87), calls=%async_computation | async-start | bytes 32768 | tf_op jit(solution)/shard_map/all_to_all | solution.py:352
  27.6 6.3 %collective-permute-start.5 = (bf16[16,96,512]{2,1,0:T(8,128)(2,1)S(1)}, bf16[16,96,512]{2,1,0:T(8,128)(2,1)S(1)}, u32[]{:S(2)}, u32[]{:S(2)}) collective-permute-start(bf16[16,96,512]{2,1,0:T(8,128)(2,1)S(1)} %broadcast_select_fusion.refs_0_), channel_id=1, source_target_pairs={{24,16},{25,17},{26,18},{27,19},{28,20},{29,21},{30,22},{31,23},{8... | collective-permute-start | bytes 4718600 | tf_op jit(solution)/shard_map/ppermute | solution.py:339
  32.1 9.6 %collective-permute-start.6 = (bf16[16,32,512]{2,1,0:T(8,128)(2,1)}, bf16[16,32,512]{2,1,0:T(8,128)(2,1)}, u32[]{:S(2)}, u32[]{:S(2)}) collective-permute-start(bf16[16,32,512]{2,1,0:T(8,128)(2,1)} %slice.35), channel_id=1, source_target_pairs={{24,8},{25,9},{26,10},{27,11},{28,12},{29,13},{30,14},{31,15}} | collective-permute-start | bytes 1572872 | tf_op jit(solution)/shard_map/ppermute | solution.py:339
  35.3 5.0 %copy-start.1 = (bf16[1,1,4,512]{3,2,1,0:T(4,128)(2,1)S(1)}, bf16[1,1,4,512]{3,2,1,0:T(4,128)(2,1)}, u32[]{:S(2)}) copy-start(bf16[1,1,4,512]{3,2,1,0:T(4,128)(2,1)} %param.15) | copy-start | bytes 12292
  35.3 26.5 %all-to-all-start.1 = ((bf16[8,96,512]{2,1,0:T(8,128)(2,1)}), bf16[8,96,512]{2,1,0:T(8,128)(2,1)S(1)}, u32[]{:S(2)}, u32[]{:S(2)}) async-start(bf16[8,96,512]{2,1,0:T(8,128)(2,1)} %shard_map.138), calls=%async_computation.1 | async-start | bytes 1572864 | tf_op jit(solution)/shard_map/all_to_all | solution.py:404
  43.0 4.5 %collective-permute-start.7 = (bf16[16,32,512]{2,1,0:T(8,128)(2,1)S(1)}, bf16[16,32,512]{2,1,0:T(8,128)(2,1)S(1)}, u32[]{:S(2)}, u32[]{:S(2)}) collective-permute-start(bf16[16,32,512]{2,1,0:T(8,128)(2,1)S(1)} %broadcast_select_fusion.1.refs_0_), channel_id=1, source_target_pairs={{24,16},{25,17},{26,18},{27,19},{28,20},{29,21},{30,22},{31,23},{8... | collective-permute-start | bytes 1572872 | tf_op jit(solution)/shard_map/ppermute | solution.py:339
  61.8 12.7 %all-to-all-start.2 = ((bf16[8,32,512]{2,1,0:T(8,128)(2,1)}), bf16[8,32,512]{2,1,0:T(8,128)(2,1)S(1)}, u32[]{:S(2)}, u32[]{:S(2)}) async-start(bf16[8,32,512]{2,1,0:T(8,128)(2,1)} %shard_map.139), calls=%async_computation.2 | async-start | bytes 524288 | tf_op jit(solution)/shard_map/all_to_all | solution.py:404
  66.4 8.8 %collective-permute-start.10 = (bf16[3,96,512]{2,1,0:T(8,128)(2,1)S(1)}, bf16[3,96,512]{2,1,0:T(8,128)(2,1)S(1)}, u32[]{:S(2)}, u32[]{:S(2)}) collective-permute-start(bf16[3,96,512]{2,1,0:T(8,128)(2,1)S(1)} %shard_map.140), channel_id=1, source_target_pairs={{0,16},{1,17},{2,18},{3,19},{4,20},{5,21},{6,22},{7,23},{8,24},{9,... | collective-permute-start | bytes 884744 | tf_op jit(solution)/shard_map/ppermute | solution.py:339
  66.4 19.1 %collective-permute-start.8 = (bf16[8,96,512]{2,1,0:T(8,128)(2,1)S(1)}, bf16[8,96,512]{2,1,0:T(8,128)(2,1)S(1)}, u32[]{:S(2)}, u32[]{:S(2)}) collective-permute-start(bf16[8,96,512]{2,1,0:T(8,128)(2,1)S(1)} %all-to-all-done.1.refs_0_.rest_0_), channel_id=1, source_target_pairs={{0,8},{1,9},{2,10},{3,11},{4,12},{5,13},{6,14},{7,15},{8,0},{9,1},... | collective-permute-start | bytes 2359304 | tf_op jit(solution)/shard_map/ppermute | solution.py:339
  74.5 11.0 %collective-permute-start.9 = (bf16[8,32,512]{2,1,0:T(8,128)(2,1)S(1)}, bf16[8,32,512]{2,1,0:T(8,128)(2,1)S(1)}, u32[]{:S(2)}, u32[]{:S(2)}) collective-permute-start(bf16[8,32,512]{2,1,0:T(8,128)(2,1)S(1)} %all-to-all-done.2.refs_0_.rest_1_), channel_id=1, source_target_pairs={{0,8},{1,9},{2,10},{3,11},{4,12},{5,13},{6,14},{7,15},{8,0},{9,1},... | collective-permute-start | bytes 786440 | tf_op jit(solution)/shard_map/ppermute | solution.py:339
  75.2 10.4 %copy-start.6 = (bf16[3,96,512]{2,1,0:T(8,128)(2,1)}, bf16[3,96,512]{2,1,0:T(8,128)(2,1)S(1)}, u32[]{:S(2)}) copy-start(bf16[3,96,512]{2,1,0:T(8,128)(2,1)S(1)} %collective-permute-done.10.rest_4_) | copy-start | bytes 884740
  75.2 10.4 %collective-permute-start.12 = (bf16[3,96,512]{2,1,0:T(8,128)(2,1)S(1)}, bf16[3,96,512]{2,1,0:T(8,128)(2,1)S(1)}, u32[]{:S(2)}, u32[]{:S(2)}) collective-permute-start(bf16[3,96,512]{2,1,0:T(8,128)(2,1)S(1)} %collective-permute-done.10.rest_4_), channel_id=1, source_target_pairs={{0,8},{1,9},{2,10},{3,11},{4,12},{5,13},{6,14},{7,15},{8,0},{9,1},... | collective-permute-start | bytes 884744 | tf_op jit(solution)/shard_map/ppermute | solution.py:339
  79.0 5.2 %collective-permute-start.11 = (bf16[3,32,512]{2,1,0:T(8,128)(2,1)S(1)}, bf16[3,32,512]{2,1,0:T(8,128)(2,1)S(1)}, u32[]{:S(2)}, u32[]{:S(2)}) collective-permute-start(bf16[3,32,512]{2,1,0:T(8,128)(2,1)S(1)} %shard_map.141), channel_id=1, source_target_pairs={{0,16},{1,17},{2,18},{3,19},{4,20},{5,21},{6,22},{7,23},{8,24},{9,... | collective-permute-start | bytes 294920 | tf_op jit(solution)/shard_map/ppermute | solution.py:339
  84.2 1.4 %copy-start.9 = (bf16[3,32,512]{2,1,0:T(8,128)(2,1)}, bf16[3,32,512]{2,1,0:T(8,128)(2,1)S(1)}, u32[]{:S(2)}) copy-start(bf16[3,32,512]{2,1,0:T(8,128)(2,1)S(1)} %collective-permute-done.11.rest_5_) | copy-start | bytes 294916
  84.2 1.3 collective-permute-start.13
  85.5 0.6 copy-start.10
  85.5 0.7 copy-start.8
  85.5 0.8 copy-start.7
  85.6 1.1 copy-start.5
  112.1 1.8 %collective-permute-start.14 = (bf16[256,512]{1,0:T(8,128)(2,1)}, bf16[256,512]{1,0:T(8,128)(2,1)S(1)}, u32[]{:S(2)}, u32[]{:S(2)}) collective-permute-start(bf16[256,512]{1,0:T(8,128)(2,1)} %get-tuple-element.38), channel_id=1, source_target_pairs={{0,8},{8,0},{16,24},{24,16},{1,9},{9,1},{17,25},{25,17},{2,10},{10... | collective-permute-start | bytes 786440 | tf_op jit(solution)/shard_map/ppermute | solution.py:297
  115.1 5.6 %collective-permute-start.15 = (bf16[1,128,512]{2,1,0:T(8,128)(2,1)S(1)}, bf16[1,128,512]{2,1,0:T(8,128)(2,1)S(1)}, u32[]{:S(2)}, u32[]{:S(2)}) collective-permute-start(bf16[1,128,512]{2,1,0:T(8,128)(2,1)S(1)} %fusion.1), channel_id=1, source_target_pairs={{0,16},{8,24},{16,0},{24,8},{1,17},{9,25},{17,1},{25,9},{2,18},{10... | collective-permute-start | bytes 393224 | tf_op jit(solution)/shard_map/ppermute | solution.py:297

commit v21 on v17

--- a/solution.py
+++ b/solution.py
@@ -10,7 +10,7 @@
 HEADS = 16
 HEAD = 128
 SPAN = 64
-GROUP = 2
+GROUP = 4
 
 EPSILON = 1e-06
 FLOOR = -1e30

time: 128 us -> 127 us (level); the launches traced: 127 us -> 127 us
  blocking collectives: 12.2 us -> 14.4 us
  Pallas kernels: 28.8 us -> 27.2 us
    all_to_all x1, blocking collectives: 12.2 us -> 14.4 us  [scatter_sum(): lax.all_to_all(parts, axes[1], split_axis=0, concat_axis=0, tiled=True)]
    pallas_call x1, Pallas kernels: 24.7 us -> 23.1 us  [run_spans(): pl.pallas_call(functools.partial(span_kernel, len(held), nbr_count, bound...]
where the time goes in v21:
time: 127 us
  waiting for transfers between devices  40.4 us (32%)
  Pallas kernels  27.2 us (21%)
  starting transfers between devices  21.8 us (17%)
  local copies, waits for them, and re-layouts  14.5 us (11%)
  blocking collectives  14.4 us (11%)
  other arithmetic  8.13 us (6%)
    pallas_call x1, Pallas kernels, run_spans(): pl.pallas_call(functools.partial(span_kernel, len(held), nbr_count, bound...  23.1 us
    ppermute x10, waiting for transfers between devices, hop(): lax.ppermute(array, axes, [(a * columns + j, b * columns + j) for a, b in...  16.7 us
    all_to_all x1, blocking collectives, scatter_sum(): lax.all_to_all(parts, axes[1], split_axis=0, concat_axis=0, tiled=True)  14.4 us
    all_to_all x2, waiting for transfers between devices, body(): lax.all_to_all(sends, 'dp', split_axis=0, concat_axis=0, tiled=True)  9.49 us
    unnamed x31, local copies, waits for them, and re-layouts  9.49 us
    all_to_all x2, starting transfers between devices, body(): lax.all_to_all(sends, 'dp', split_axis=0, concat_axis=0, tiled=True)  8.48 us
    all_to_all x1, starting transfers between devices, to_all(): return lax.all_to_all(copies, axis, split_axis=0, concat_axis=0, tiled=True)  8.23 us
    ppermute x2, waiting for transfers between devices, scatter_sum(): lax.ppermute(a, axes[0], [(i, i ^ bit) for i in range(size)])  7.13 us
  transfers between devices with their start and end apart: 15, of which 10 were waited for; matrix products, arithmetic and copies ran while one was open for 13% of the time, Pallas kernels for 2%

profile of v21, /device:TPU:0, one launch (start us, length us, event | category | flops | bytes accessed | tf_op | source)
XLA Modules:
  0.0 127.4 jit_solution(10018322114453805746)
XLA Ops:
  0.7 1.6 %slice.28 = bf16[16,96,512]{2,1,0:T(8,128)(2,1)S(1)} slice(bf16[16,128,512]{2,1,0:T(8,128)(2,1)} %bitcast.44), slice={[0:16], [0:96], [0:512]} | slice | bytes 3145728 | tf_op jit(solution)/shard_map/slice | solution.py:347
  2.2 0.8 collective-permute-start
  3.5 0.6 broadcast_in_dim.83
  4.1 8.2 %all-to-all-start = ((s32[32,1,128]{2,1,0:T(1,128)}), s32[32,1,128]{2,1,0:T(1,128)S(1)}, u32[]{:S(2)}, u32[]{:S(2)}) async-start(s32[32,1,128]{2,1,0:T(1,128)} %broadcast_in_dim.83), calls=%async_computation | async-start | bytes 32768 | tf_op jit(solution)/shard_map/all_to_all | solution.py:352
  12.4 6.5 %copy.45 = bf16[512,4096]{0,1:T(8,128)(2,1)} copy(bf16[512,4096]{1,0:T(8,128)(2,1)} %rest_8_.1) | data formatting | bytes 8388608 | tf_op args[10]
  18.9 7.1 %all-to-all-done = s32[32,1,128]{2,1,0:T(1,128)S(1)} async-done(((s32[32,1,128]{2,1,0:T(1,128)}), s32[32,1,128]{2,1,0:T(1,128)S(1)}, u32[]{:S(2)}, u32[]{:S(2)}) %all-to-all-start) | async-done | bytes 16416 | tf_op jit(solution)/shard_map/all_to_all | solution.py:352
  26.0 1.6 %broadcast_select_fusion.refs_0_ = bf16[16,96,512]{2,1,0:T(8,128)(2,1)S(1)} fusion(bf16[16,96,512]{2,1,0:T(8,128)(2,1)S(1)} %collective-permute-done, pred[]{:T(512)S(6)} %eq.145, bf16[16,128,512]{2,1,0:T(8,128)(2,1)} %bitcast.45), kind=kLoop, calls=%fused_computation | loop fusion | flops 786432 | bytes 4718593 | tf_op jit(solution)/shard_map/jit(_where)/select_n | solution.py:390
  27.5 1.3 %collective-permute-start.1 = (bf16[16,96,512]{2,1,0:T(8,128)(2,1)S(1)}, bf16[16,96,512]{2,1,0:T(8,128)(2,1)S(1)}, u32[]{:S(2)}, u32[]{:S(2)}) collective-permute-start(bf16[16,96,512]{2,1,0:T(8,128)(2,1)S(1)} %broadcast_select_fusion.refs_0_), channel_id=1, source_target_pairs={{24,16},{25,17},{26,18},{27,19},{28,20},{29,21},{30,22},{31,23},{8... | collective-permute-start | bytes 4718600 | tf_op jit(solution)/shard_map/ppermute | solution.py:339
  29.0 0.3 convert_reduce_fusion.4
  29.4 0.6 convert_reduce_fusion.1
  30.2 0.2 select_reduce_fusion
  30.4 2.4 %collective-permute-done.1.refs_1_ = bf16[16,96,512]{2,1,0:T(8,128)(2,1)S(1)} collective-permute-done((bf16[16,96,512]{2,1,0:T(8,128)(2,1)S(1)}, bf16[16,96,512]{2,1,0:T(8,128)(2,1)S(1)}, u32[]{:S(2)}, u32[]{:S(2)}) %collective-permute-start.1) | collective-permute-done | bytes 1572896 | tf_op jit(solution)/shard_map/ppermute | solution.py:339
  32.8 1.5 %shard_map.138 = bf16[8,96,512]{2,1,0:T(8,128)(2,1)} custom-call(s32[9]{0:T(128)S(1)} %pad_add_fusion.2.meta, bf16[16,96,512]{2,1,0:T(8,128)(2,1)S(1)} %broadcast_select_fusion.refs_0_, bf16[16,96,512]{2,1,0:T(8,128)(2,1)S(1)} %collective-permute-done.1.refs_1_), custom_call_target="tpu_custom_call" | custom-call | tf_op jit(solution)/shard_map/pallas_call | solution.py:259
  34.3 4.9 %all-to-all-start.1 = ((bf16[8,96,512]{2,1,0:T(8,128)(2,1)}), bf16[8,96,512]{2,1,0:T(8,128)(2,1)S(1)}, u32[]{:S(2)}, u32[]{:S(2)}) async-start(bf16[8,96,512]{2,1,0:T(8,128)(2,1)} %shard_map.138), calls=%async_computation.1 | async-start | bytes 1572864 | tf_op jit(solution)/shard_map/all_to_all | solution.py:397
  39.2 1.1 slice.27
  40.3 0.7 collective-permute-start.2
  41.1 1.1 broadcast_select_fusion.1.refs_0_
  42.3 1.4 %collective-permute-start.3 = (bf16[16,32,512]{2,1,0:T(8,128)(2,1)S(1)}, bf16[16,32,512]{2,1,0:T(8,128)(2,1)S(1)}, u32[]{:S(2)}, u32[]{:S(2)}) collective-permute-start(bf16[16,32,512]{2,1,0:T(8,128)(2,1)S(1)} %broadcast_select_fusion.1.refs_0_), channel_id=1, source_target_pairs={{24,16},{25,17},{26,18},{27,19},{28,20},{29,21},{30,22},{31,23},{8... | collective-permute-start | bytes 1572872 | tf_op jit(solution)/shard_map/ppermute | solution.py:339
  43.7 0.5 broadcast.437
  44.2 0.7 fusion.34
  44.9 0.1 select_reduce_fusion.2
  45.1 9.2 %collective-permute-done.3.refs_1_ = bf16[16,32,512]{2,1,0:T(8,128)(2,1)S(1)} collective-permute-done((bf16[16,32,512]{2,1,0:T(8,128)(2,1)S(1)}, bf16[16,32,512]{2,1,0:T(8,128)(2,1)S(1)}, u32[]{:S(2)}, u32[]{:S(2)}) %collective-permute-start.3) | collective-permute-done | bytes 524320 | tf_op jit(solution)/shard_map/ppermute | solution.py:339
  54.3 1.3 %shard_map.139 = bf16[8,32,512]{2,1,0:T(8,128)(2,1)} custom-call(s32[9]{0:T(128)S(1)} %pad_add_fusion.2.meta, bf16[16,32,512]{2,1,0:T(8,128)(2,1)S(1)} %broadcast_select_fusion.1.refs_0_, bf16[16,32,512]{2,1,0:T(8,128)(2,1)S(1)} %collective-permute-done.3.refs_1_), custom_call_target="tpu_custom_call" | custom-call | tf_op jit(solution)/shard_map/pallas_call | solution.py:259
  55.6 4.1 %all-to-all-done.1.refs_0_.rest_0_ = bf16[8,96,512]{2,1,0:T(8,128)(2,1)S(1)} async-done(((bf16[8,96,512]{2,1,0:T(8,128)(2,1)}), bf16[8,96,512]{2,1,0:T(8,128)(2,1)S(1)}, u32[]{:S(2)}, u32[]{:S(2)}) %all-to-all-start.1) | async-done | bytes 786464 | tf_op jit(solution)/shard_map/all_to_all | solution.py:397
  59.7 3.6 %all-to-all-start.2 = ((bf16[8,32,512]{2,1,0:T(8,128)(2,1)}), bf16[8,32,512]{2,1,0:T(8,128)(2,1)S(1)}, u32[]{:S(2)}, u32[]{:S(2)}) async-start(bf16[8,32,512]{2,1,0:T(8,128)(2,1)} %shard_map.139), calls=%async_computation.2 | async-start | bytes 524288 | tf_op jit(solution)/shard_map/all_to_all | solution.py:397
  63.3 0.6 shard_map.140
  63.9 0.6 bitcast_convert_fusion.cond_ref
  64.5 0.8 copy.50
  65.4 0.8 copy.49
  66.7 0.2 select_reduce_fusion.1
  66.9 5.4 %all-to-all-done.2.refs_0_.rest_1_ = bf16[8,32,512]{2,1,0:T(8,128)(2,1)S(1)} async-done(((bf16[8,32,512]{2,1,0:T(8,128)(2,1)}), bf16[8,32,512]{2,1,0:T(8,128)(2,1)S(1)}, u32[]{:S(2)}, u32[]{:S(2)}) %all-to-all-start.2) | async-done | bytes 262176 | tf_op jit(solution)/shard_map/all_to_all | solution.py:397
  72.4 0.7 shard_map.141
  73.2 2.2 %collective-permute-done.6.rest_4_ = bf16[4,96,512]{2,1,0:T(8,128)(2,1)} collective-permute-done((bf16[4,96,512]{2,1,0:T(8,128)(2,1)S(1)}, bf16[4,96,512]{2,1,0:T(8,128)(2,1)}, u32[]{:S(2)}, u32[]{:S(2)}) %collective-permute-start.6) | collective-permute-done | bytes 393248 | tf_op jit(solution)/shard_map/ppermute | solution.py:339
  75.4 0.5 collective-permute-start.5
  76.0 2.2 %collective-permute-done.7.rest_5_ = bf16[4,32,512]{2,1,0:T(8,128)(2,1)S(1)} collective-permute-done((bf16[4,32,512]{2,1,0:T(8,128)(2,1)S(1)}, bf16[4,32,512]{2,1,0:T(8,128)(2,1)S(1)}, u32[]{:S(2)}, u32[]{:S(2)}) %collective-permute-start.7) | collective-permute-done | bytes 131104 | tf_op jit(solution)/shard_map/ppermute | solution.py:339
  78.2 0.6 pad_add_fusion.1.meta
  78.8 0.7 collective-permute-done.9.rest_7_
  79.6 0.6 copy-done.12
  80.1 0.1 copy-done.10
  80.3 0.3 copy-done.8
  80.5 0.1 copy-done.9
  80.7 23.1 %shard_map.142 = (bf16[256,2048]{1,0:T(8,128)(2,1)}, bf16[256,2048]{1,0:T(8,128)(2,1)}, f32[4,512]{1,0:T(4,128)}, f32[256,512]{1,0:T(8,128)}, bf16[256,512]{1,0:T(8,128)(2,1)}) custom-call(s32[25]{0:T(128)} %pad_add_fusion.1.meta, bf16[256,2048]{1,0:T(8,128)(2,1)} %bitcast.59, bf16[256,2048]{1,0:T(8,128)(2,1)} %bitcast.60, ...), custom_call_target="tpu_custom_call" | custom-call | flops 11811160064 | bytes 16777216 | tf_op jit(solution)/shard_map/pallas_call | solution.py:202
  103.8 0.2 collective-permute-start.10
  104.0 1.6 %collective-permute-done.10 = bf16[256,512]{1,0:T(8,128)(2,1)S(1)} collective-permute-done((bf16[256,512]{1,0:T(8,128)(2,1)}, bf16[256,512]{1,0:T(8,128)(2,1)S(1)}, u32[]{:S(2)}, u32[]{:S(2)}) %collective-permute-start.10) | collective-permute-done | bytes 262176 | tf_op jit(solution)/shard_map/ppermute | solution.py:297
  105.6 1.1 convert_add_fusion
  106.9 5.5 %collective-permute-done.11 = bf16[1,128,512]{2,1,0:T(8,128)(2,1)S(1)} collective-permute-done((bf16[1,128,512]{2,1,0:T(8,128)(2,1)S(1)}, bf16[1,128,512]{2,1,0:T(8,128)(2,1)S(1)}, u32[]{:S(2)}, u32[]{:S(2)}) %collective-permute-start.11) | collective-permute-done | bytes 131104 | tf_op jit(solution)/shard_map/ppermute | solution.py:297
  112.4 14.4 %all_to_all.20 = bf16[8,16,512]{2,1,0:T(8,128)(2,1)S(1)} all-to-all(bf16[8,16,512]{2,1,0:T(8,128)(2,1)S(1)} %bitcast.51), channel_id=1, replica_groups=mesh['pool'=4,'dp'=8] {'dp'}, dimensions={0} | all-to-all | bytes 262144 | tf_op jit(solution)/shard_map/all_to_all | solution.py:308
  126.8 0.6 convert_reduce_fusion
  (72 shorter events, 2.2 us)
Async XLA Ops:
  0.6 2.4 %copy-start.5 = (s32[1,1,4,2]{2,3,1,0:T(2,128)S(1)}, s32[1,1,4,2]{2,3,1,0:T(2,128)}, u32[]{:S(2)}) copy-start(s32[1,1,4,2]{2,3,1,0:T(2,128)} %param.14) | copy-start | bytes 100
  0.6 2.6 %copy-start.6 = (s32[1,1,4,2]{2,3,1,0:T(2,128)S(1)}, s32[1,1,4,2]{2,3,1,0:T(2,128)}, u32[]{:S(2)}) copy-start(s32[1,1,4,2]{2,3,1,0:T(2,128)} %param.15) | copy-start | bytes 100
  0.7 2.7 %copy-start.7 = (s32[1,1,16]{2,1,0:T(1,128)S(1)}, s32[1,1,16]{2,1,0:T(1,128)}, u32[]{:S(2)}) copy-start(s32[1,1,16]{2,1,0:T(1,128)} %param.17) | copy-start | bytes 196
  2.2 23.7 %collective-permute-start = (bf16[16,96,512]{2,1,0:T(8,128)(2,1)S(1)}, bf16[16,96,512]{2,1,0:T(8,128)(2,1)S(1)}, u32[]{:S(2)}, u32[]{:S(2)}) collective-permute-start(bf16[16,96,512]{2,1,0:T(8,128)(2,1)S(1)} %slice.28), channel_id=1, source_target_pairs={{24,8},{25,9},{26,10},{27,11},{28,12},{29,13},{30,14},{31,15}} | collective-permute-start | bytes 4718600 | tf_op jit(solution)/shard_map/ppermute | solution.py:339
  4.1 21.9 %all-to-all-start = ((s32[32,1,128]{2,1,0:T(1,128)}), s32[32,1,128]{2,1,0:T(1,128)S(1)}, u32[]{:S(2)}, u32[]{:S(2)}) async-start(s32[32,1,128]{2,1,0:T(1,128)} %broadcast_in_dim.83), calls=%async_computation | async-start | bytes 32768 | tf_op jit(solution)/shard_map/all_to_all | solution.py:352
  27.5 5.3 %collective-permute-start.1 = (bf16[16,96,512]{2,1,0:T(8,128)(2,1)S(1)}, bf16[16,96,512]{2,1,0:T(8,128)(2,1)S(1)}, u32[]{:S(2)}, u32[]{:S(2)}) collective-permute-start(bf16[16,96,512]{2,1,0:T(8,128)(2,1)S(1)} %broadcast_select_fusion.refs_0_), channel_id=1, source_target_pairs={{24,16},{25,17},{26,18},{27,19},{28,20},{29,21},{30,22},{31,23},{8... | collective-permute-start | bytes 4718600 | tf_op jit(solution)/shard_map/ppermute | solution.py:339
  34.3 25.3 %all-to-all-start.1 = ((bf16[8,96,512]{2,1,0:T(8,128)(2,1)}), bf16[8,96,512]{2,1,0:T(8,128)(2,1)S(1)}, u32[]{:S(2)}, u32[]{:S(2)}) async-start(bf16[8,96,512]{2,1,0:T(8,128)(2,1)} %shard_map.138), calls=%async_computation.1 | async-start | bytes 1572864 | tf_op jit(solution)/shard_map/all_to_all | solution.py:397
  40.3 0.8 collective-permute-start.2
  42.2 21.7 %copy-start.4 = (bf16[1,1,4,512]{3,2,1,0:T(4,128)(2,1)S(1)}, bf16[1,1,4,512]{3,2,1,0:T(4,128)(2,1)}, u32[]{:S(2)}) copy-start(bf16[1,1,4,512]{3,2,1,0:T(4,128)(2,1)} %param.13) | copy-start | bytes 12292
  42.2 22.3 %copy-start.2 = (bf16[512,256]{1,0:T(8,128)(2,1)S(1)}, bf16[512,256]{1,0:T(8,128)(2,1)}, u32[]{:S(2)}) copy-start(bf16[512,256]{1,0:T(8,128)(2,1)} %down_ref.1) | copy-start | bytes 786436
  42.3 12.1 %collective-permute-start.3 = (bf16[16,32,512]{2,1,0:T(8,128)(2,1)S(1)}, bf16[16,32,512]{2,1,0:T(8,128)(2,1)S(1)}, u32[]{:S(2)}, u32[]{:S(2)}) collective-permute-start(bf16[16,32,512]{2,1,0:T(8,128)(2,1)S(1)} %broadcast_select_fusion.1.refs_0_), channel_id=1, source_target_pairs={{24,16},{25,17},{26,18},{27,19},{28,20},{29,21},{30,22},{31,23},{8... | collective-permute-start | bytes 1572872 | tf_op jit(solution)/shard_map/ppermute | solution.py:339
  45.1 20.3 %copy-start.3 = (bf16[256,512]{1,0:T(8,128)(2,1)S(1)}, bf16[256,512]{1,0:T(8,128)(2,1)}, u32[]{:S(2)}) copy-start(bf16[256,512]{1,0:T(8,128)(2,1)} %up_ref.1) | copy-start | bytes 786436
  59.7 13.4 %copy-start = (bf16[8,96,512]{2,1,0:T(8,128)(2,1)}, bf16[8,96,512]{2,1,0:T(8,128)(2,1)S(1)}, u32[]{:S(2)}) copy-start(bf16[8,96,512]{2,1,0:T(8,128)(2,1)S(1)} %all-to-all-done.1.refs_0_.rest_0_) | copy-start | bytes 2359300
  59.7 12.7 %all-to-all-start.2 = ((bf16[8,32,512]{2,1,0:T(8,128)(2,1)}), bf16[8,32,512]{2,1,0:T(8,128)(2,1)S(1)}, u32[]{:S(2)}, u32[]{:S(2)}) async-start(bf16[8,32,512]{2,1,0:T(8,128)(2,1)} %shard_map.139), calls=%async_computation.2 | async-start | bytes 524288 | tf_op jit(solution)/shard_map/all_to_all | solution.py:397
  63.8 11.5 %collective-permute-start.6 = (bf16[4,96,512]{2,1,0:T(8,128)(2,1)S(1)}, bf16[4,96,512]{2,1,0:T(8,128)(2,1)}, u32[]{:S(2)}, u32[]{:S(2)}) collective-permute-start(bf16[4,96,512]{2,1,0:T(8,128)(2,1)S(1)} %shard_map.140), channel_id=1, source_target_pairs={{0,16},{1,17},{2,18},{3,19},{4,20},{5,21},{6,22},{7,23},{8,24},{9,... | collective-permute-start | bytes 1179656 | tf_op jit(solution)/shard_map/ppermute | solution.py:339
  66.7 12.8 %collective-permute-start.4 = (bf16[8,96,512]{2,1,0:T(8,128)(2,1)S(1)}, bf16[8,96,512]{2,1,0:T(8,128)(2,1)S(1)}, u32[]{:S(2)}, u32[]{:S(2)}) collective-permute-start(bf16[8,96,512]{2,1,0:T(8,128)(2,1)S(1)} %all-to-all-done.1.refs_0_.rest_0_), channel_id=1, source_target_pairs={{0,8},{1,9},{2,10},{3,11},{4,12},{5,13},{6,14},{7,15},{8,0},{9,1},... | collective-permute-start | bytes 2359304 | tf_op jit(solution)/shard_map/ppermute | solution.py:339
  72.4 7.2 %copy-start.1 = (bf16[8,32,512]{2,1,0:T(8,128)(2,1)}, bf16[8,32,512]{2,1,0:T(8,128)(2,1)S(1)}, u32[]{:S(2)}) copy-start(bf16[8,32,512]{2,1,0:T(8,128)(2,1)S(1)} %all-to-all-done.2.refs_0_.rest_1_) | copy-start | bytes 786436
  73.1 5.0 %collective-permute-start.7 = (bf16[4,32,512]{2,1,0:T(8,128)(2,1)S(1)}, bf16[4,32,512]{2,1,0:T(8,128)(2,1)S(1)}, u32[]{:S(2)}, u32[]{:S(2)}) collective-permute-start(bf16[4,32,512]{2,1,0:T(8,128)(2,1)S(1)} %shard_map.141), channel_id=1, source_target_pairs={{0,16},{1,17},{2,18},{3,19},{4,20},{5,21},{6,22},{7,23},{8,24},{9,... | collective-permute-start | bytes 393224 | tf_op jit(solution)/shard_map/ppermute | solution.py:339
  75.4 4.1 %collective-permute-start.8 = (bf16[4,96,512]{2,1,0:T(8,128)(2,1)}, bf16[4,96,512]{2,1,0:T(8,128)(2,1)S(1)}, u32[]{:S(2)}, u32[]{:S(2)}) collective-permute-start(bf16[4,96,512]{2,1,0:T(8,128)(2,1)} %collective-permute-done.6.rest_4_), channel_id=1, source_target_pairs={{0,8},{1,9},{2,10},{3,11},{4,12},{5,13},{6,14},{7,15},{8,0},{9,1},... | collective-permute-start | bytes 1179656 | tf_op jit(solution)/shard_map/ppermute | solution.py:339
  75.4 4.1 %collective-permute-start.5 = (bf16[8,32,512]{2,1,0:T(8,128)(2,1)S(1)}, bf16[8,32,512]{2,1,0:T(8,128)(2,1)S(1)}, u32[]{:S(2)}, u32[]{:S(2)}) collective-permute-start(bf16[8,32,512]{2,1,0:T(8,128)(2,1)S(1)} %all-to-all-done.2.refs_0_.rest_1_), channel_id=1, source_target_pairs={{0,8},{1,9},{2,10},{3,11},{4,12},{5,13},{6,14},{7,15},{8,0},{9,1},... | collective-permute-start | bytes 786440 | tf_op jit(solution)/shard_map/ppermute | solution.py:339
  78.1 1.4 %copy-start.11 = (bf16[4,32,512]{2,1,0:T(8,128)(2,1)}, bf16[4,32,512]{2,1,0:T(8,128)(2,1)S(1)}, u32[]{:S(2)}) copy-start(bf16[4,32,512]{2,1,0:T(8,128)(2,1)S(1)} %collective-permute-done.7.rest_5_) | copy-start | bytes 393220
  78.2 1.3 %collective-permute-start.9 = (bf16[4,32,512]{2,1,0:T(8,128)(2,1)S(1)}, bf16[4,32,512]{2,1,0:T(8,128)(2,1)S(1)}, u32[]{:S(2)}, u32[]{:S(2)}) collective-permute-start(bf16[4,32,512]{2,1,0:T(8,128)(2,1)S(1)} %collective-permute-done.7.rest_5_), channel_id=1, source_target_pairs={{0,8},{1,9},{2,10},{3,11},{4,12},{5,13},{6,14},{7,15},{8,0},{9,1},... | collective-permute-start | bytes 393224 | tf_op jit(solution)/shard_map/ppermute | solution.py:339
  79.5 0.6 copy-start.12
  79.5 0.8 copy-start.10
  79.5 1.0 copy-start.8
  79.5 1.1 copy-start.9
  103.8 1.8 %collective-permute-start.10 = (bf16[256,512]{1,0:T(8,128)(2,1)}, bf16[256,512]{1,0:T(8,128)(2,1)S(1)}, u32[]{:S(2)}, u32[]{:S(2)}) collective-permute-start(bf16[256,512]{1,0:T(8,128)(2,1)} %get-tuple-element.21), channel_id=1, source_target_pairs={{0,8},{8,0},{16,24},{24,16},{1,9},{9,1},{17,25},{25,17},{2,10},{10... | collective-permute-start | bytes 786440 | tf_op jit(solution)/shard_map/ppermute | solution.py:297
  106.8 5.6 %collective-permute-start.11 = (bf16[1,128,512]{2,1,0:T(8,128)(2,1)S(1)}, bf16[1,128,512]{2,1,0:T(8,128)(2,1)S(1)}, u32[]{:S(2)}, u32[]{:S(2)}) collective-permute-start(bf16[1,128,512]{2,1,0:T(8,128)(2,1)S(1)} %fusion.1), channel_id=1, source_target_pairs={{0,16},{8,24},{16,0},{24,8},{1,17},{9,25},{17,1},{25,9},{2,18},{10... | collective-permute-start | bytes 393224 | tf_op jit(solution)/shard_map/ppermute | solution.py:297

commit v22 on v18

--- a/solution.py
+++ b/solution.py
@@ -10,7 +10,7 @@
 HEADS = 16
 HEAD = 128
 SPAN = 64
-GROUP = 2
+GROUP = 4
 
 EPSILON = 1e-06
 FLOOR = -1e30
@@ -67,15 +67,7 @@
         pltpu.make_async_copy(out_ref, out_hbm.at[own_rows], kv_sem.at[3]),
         pltpu.make_async_copy(qg_ref, qg_hbm.at[own_rows], kv_sem.at[4]),
     ]
-    kv_piece = 4 * HEAD
-    kv_copies = [
-        pltpu.make_async_copy(
-            kv_hbm.at[:, pl.ds(i * kv_piece, kv_piece)],
-            kv_ref.at[:, pl.ds(i * kv_piece, kv_piece)],
-            kv_sem.at[5 + i],
-        )
-        for i in range(2 * head_cols // kv_piece)
-    ]
+    kv_copy = pltpu.make_async_copy(kv_hbm, kv_ref, kv_sem.at[5])
 
     @pl.when(step == 0)
     def _():
@@ -89,7 +81,7 @@
                         raw_ref.at[n, cuts[part]],
                         sems.at[n * parts + part],
                     ).start()
-        for copy in kv_copies + token_copies:
+        for copy in [kv_copy] + token_copies:
             copy.start()
         q2_ref[...] = jnp.zeros_like(q2_ref)
         cot2_ref[...] = jnp.zeros_like(cot2_ref)
@@ -118,12 +110,11 @@
     latent = dot(hidden, down_ref[...]).astype(jnp.bfloat16)
     encoded = (x_full + dot(latent, up_ref[...])).astype(jnp.bfloat16)
 
-    for i, cols in enumerate(pairs + value_pairs):
-        if i % 2 == 0:
-            @pl.when(step == 0)
-            def _():
-                kv_copies[i // 2].wait()
-
+    @pl.when(step == 0)
+    def _():
+        kv_copy.wait()
+
+    for cols in pairs + value_pairs:
         proj_ref[:, cols] = dot(encoded, kv_ref[:, cols]).astype(jnp.bfloat16)
 
     @pl.when(step == 0)
@@ -258,7 +249,7 @@
                 pltpu.VMEM((group * 2 * SPAN, head_cols), jnp.bfloat16),
                 pltpu.VMEM((width, 2 * rank), jnp.float32),
                 pltpu.SemaphoreType.DMA((per_device * parts,)),
-                pltpu.SemaphoreType.DMA((5 + head_cols // (2 * HEAD),)),
+                pltpu.SemaphoreType.DMA((6,)),
             ],
         ),
         out_shape=[

time: 130 us -> 128 us (0.985)
  Pallas kernels: 31.1 us -> 28.5 us
    pallas_call x1, Pallas kernels: 27.1 us -> 24.4 us  [run_spans(): pl.pallas_call(functools.partial(span_kernel, len(held), nbr_count, bound...]
where the time goes in v22:
time: 128 us; the launch traced here: 127 us
  waiting for transfers between devices  40.4 us (32%)
  Pallas kernels  28.5 us (22%)
  starting transfers between devices  21.8 us (17%)
  local copies, waits for them, and re-layouts  14.5 us (11%)
  blocking collectives  12.6 us (10%)
  other arithmetic  8.13 us (6%)
    pallas_call x1, Pallas kernels, run_spans(): pl.pallas_call(functools.partial(span_kernel, len(held), nbr_count, bound...  24.4 us
    ppermute x10, waiting for transfers between devices, hop(): lax.ppermute(array, axes, [(a * columns + j, b * columns + j) for a, b in...  16.7 us
    all_to_all x1, blocking collectives, scatter_sum(): lax.all_to_all(parts, axes[1], split_axis=0, concat_axis=0, tiled=True)  12.6 us
    all_to_all x2, waiting for transfers between devices, body(): lax.all_to_all(sends, 'dp', split_axis=0, concat_axis=0, tiled=True)  9.49 us
    unnamed x31, local copies, waits for them, and re-layouts  9.49 us
    all_to_all x2, starting transfers between devices, body(): lax.all_to_all(sends, 'dp', split_axis=0, concat_axis=0, tiled=True)  8.48 us
    all_to_all x1, starting transfers between devices, to_all(): return lax.all_to_all(copies, axis, split_axis=0, concat_axis=0, tiled=True)  8.23 us
    ppermute x2, waiting for transfers between devices, scatter_sum(): lax.ppermute(a, axes[0], [(i, i ^ bit) for i in range(size)])  7.13 us
  transfers between devices with their start and end apart: 15, of which 10 were waited for; matrix products, arithmetic and copies ran while one was open for 13% of the time, Pallas kernels for 2%

profile of v22, /device:TPU:0, one launch (start us, length us, event | category | flops | bytes accessed | tf_op | source)
XLA Modules:
  0.0 127.0 jit_solution(13739328867262012276)
XLA Ops:
  0.7 1.6 %slice.28 = bf16[16,96,512]{2,1,0:T(8,128)(2,1)S(1)} slice(bf16[16,128,512]{2,1,0:T(8,128)(2,1)} %bitcast.44), slice={[0:16], [0:96], [0:512]} | slice | bytes 3145728 | tf_op jit(solution)/shard_map/slice | solution.py:369
  2.2 0.8 collective-permute-start
  3.5 0.6 broadcast_in_dim.83
  4.1 8.2 %all-to-all-start = ((s32[32,1,128]{2,1,0:T(1,128)}), s32[32,1,128]{2,1,0:T(1,128)S(1)}, u32[]{:S(2)}, u32[]{:S(2)}) async-start(s32[32,1,128]{2,1,0:T(1,128)} %broadcast_in_dim.83), calls=%async_computation | async-start | bytes 32768 | tf_op jit(solution)/shard_map/all_to_all | solution.py:374
  12.4 6.5 %copy.45 = bf16[512,4096]{0,1:T(8,128)(2,1)} copy(bf16[512,4096]{1,0:T(8,128)(2,1)} %rest_10_.1) | data formatting | bytes 8388608 | tf_op args[10]
  18.9 7.1 %all-to-all-done = s32[32,1,128]{2,1,0:T(1,128)S(1)} async-done(((s32[32,1,128]{2,1,0:T(1,128)}), s32[32,1,128]{2,1,0:T(1,128)S(1)}, u32[]{:S(2)}, u32[]{:S(2)}) %all-to-all-start) | async-done | bytes 16416 | tf_op jit(solution)/shard_map/all_to_all | solution.py:374
  26.0 1.6 %broadcast_select_fusion.refs_0_ = bf16[16,96,512]{2,1,0:T(8,128)(2,1)S(1)} fusion(bf16[16,96,512]{2,1,0:T(8,128)(2,1)S(1)} %collective-permute-done, pred[]{:T(512)S(6)} %eq.145, bf16[16,128,512]{2,1,0:T(8,128)(2,1)} %bitcast.45), kind=kLoop, calls=%fused_computation | loop fusion | flops 786432 | bytes 4718593 | tf_op jit(solution)/shard_map/jit(_where)/select_n | solution.py:412
  27.5 1.3 %collective-permute-start.1 = (bf16[16,96,512]{2,1,0:T(8,128)(2,1)S(1)}, bf16[16,96,512]{2,1,0:T(8,128)(2,1)S(1)}, u32[]{:S(2)}, u32[]{:S(2)}) collective-permute-start(bf16[16,96,512]{2,1,0:T(8,128)(2,1)S(1)} %broadcast_select_fusion.refs_0_), channel_id=1, source_target_pairs={{24,16},{25,17},{26,18},{27,19},{28,20},{29,21},{30,22},{31,23},{8... | collective-permute-start | bytes 4718600 | tf_op jit(solution)/shard_map/ppermute | solution.py:361
  29.0 0.3 convert_reduce_fusion.4
  29.4 0.6 convert_reduce_fusion.1
  30.2 0.2 select_reduce_fusion
  30.4 2.4 %collective-permute-done.1.refs_1_ = bf16[16,96,512]{2,1,0:T(8,128)(2,1)S(1)} collective-permute-done((bf16[16,96,512]{2,1,0:T(8,128)(2,1)S(1)}, bf16[16,96,512]{2,1,0:T(8,128)(2,1)S(1)}, u32[]{:S(2)}, u32[]{:S(2)}) %collective-permute-start.1) | collective-permute-done | bytes 1572896 | tf_op jit(solution)/shard_map/ppermute | solution.py:361
  32.8 1.5 %shard_map.138 = bf16[8,96,512]{2,1,0:T(8,128)(2,1)} custom-call(s32[9]{0:T(128)S(1)} %pad_add_fusion.2.meta, bf16[16,96,512]{2,1,0:T(8,128)(2,1)S(1)} %broadcast_select_fusion.refs_0_, bf16[16,96,512]{2,1,0:T(8,128)(2,1)S(1)} %collective-permute-done.1.refs_1_), custom_call_target="tpu_custom_call" | custom-call | tf_op jit(solution)/shard_map/pallas_call | solution.py:281
  34.3 4.9 %all-to-all-start.1 = ((bf16[8,96,512]{2,1,0:T(8,128)(2,1)}), bf16[8,96,512]{2,1,0:T(8,128)(2,1)S(1)}, u32[]{:S(2)}, u32[]{:S(2)}) async-start(bf16[8,96,512]{2,1,0:T(8,128)(2,1)} %shard_map.138), calls=%async_computation.1 | async-start | bytes 1572864 | tf_op jit(solution)/shard_map/all_to_all | solution.py:419
  39.2 1.1 slice.27
  40.3 0.7 collective-permute-start.2
  41.1 1.1 broadcast_select_fusion.1.refs_0_
  42.3 1.4 %collective-permute-start.3 = (bf16[16,32,512]{2,1,0:T(8,128)(2,1)S(1)}, bf16[16,32,512]{2,1,0:T(8,128)(2,1)S(1)}, u32[]{:S(2)}, u32[]{:S(2)}) collective-permute-start(bf16[16,32,512]{2,1,0:T(8,128)(2,1)S(1)} %broadcast_select_fusion.1.refs_0_), channel_id=1, source_target_pairs={{24,16},{25,17},{26,18},{27,19},{28,20},{29,21},{30,22},{31,23},{8... | collective-permute-start | bytes 1572872 | tf_op jit(solution)/shard_map/ppermute | solution.py:361
  43.7 0.5 broadcast.437
  44.2 0.7 fusion.34
  44.9 0.1 select_reduce_fusion.2
  45.1 9.2 %collective-permute-done.3.refs_1_ = bf16[16,32,512]{2,1,0:T(8,128)(2,1)S(1)} collective-permute-done((bf16[16,32,512]{2,1,0:T(8,128)(2,1)S(1)}, bf16[16,32,512]{2,1,0:T(8,128)(2,1)S(1)}, u32[]{:S(2)}, u32[]{:S(2)}) %collective-permute-start.3) | collective-permute-done | bytes 524320 | tf_op jit(solution)/shard_map/ppermute | solution.py:361
  54.3 1.3 %shard_map.139 = bf16[8,32,512]{2,1,0:T(8,128)(2,1)} custom-call(s32[9]{0:T(128)S(1)} %pad_add_fusion.2.meta, bf16[16,32,512]{2,1,0:T(8,128)(2,1)S(1)} %broadcast_select_fusion.1.refs_0_, bf16[16,32,512]{2,1,0:T(8,128)(2,1)S(1)} %collective-permute-done.3.refs_1_), custom_call_target="tpu_custom_call" | custom-call | tf_op jit(solution)/shard_map/pallas_call | solution.py:281
  55.6 4.1 %all-to-all-done.1.refs_0_.rest_0_ = bf16[8,96,512]{2,1,0:T(8,128)(2,1)S(1)} async-done(((bf16[8,96,512]{2,1,0:T(8,128)(2,1)}), bf16[8,96,512]{2,1,0:T(8,128)(2,1)S(1)}, u32[]{:S(2)}, u32[]{:S(2)}) %all-to-all-start.1) | async-done | bytes 786464 | tf_op jit(solution)/shard_map/all_to_all | solution.py:419
  59.7 3.6 %all-to-all-start.2 = ((bf16[8,32,512]{2,1,0:T(8,128)(2,1)}), bf16[8,32,512]{2,1,0:T(8,128)(2,1)S(1)}, u32[]{:S(2)}, u32[]{:S(2)}) async-start(bf16[8,32,512]{2,1,0:T(8,128)(2,1)} %shard_map.139), calls=%async_computation.2 | async-start | bytes 524288 | tf_op jit(solution)/shard_map/all_to_all | solution.py:419
  63.3 0.6 shard_map.140
  63.9 0.6 bitcast_convert_fusion.cond_ref
  64.5 0.8 copy.50
  65.4 0.8 copy.49
  66.7 0.2 select_reduce_fusion.1
  66.9 5.4 %all-to-all-done.2.refs_0_.rest_1_ = bf16[8,32,512]{2,1,0:T(8,128)(2,1)S(1)} async-done(((bf16[8,32,512]{2,1,0:T(8,128)(2,1)}), bf16[8,32,512]{2,1,0:T(8,128)(2,1)S(1)}, u32[]{:S(2)}, u32[]{:S(2)}) %all-to-all-start.2) | async-done | bytes 262176 | tf_op jit(solution)/shard_map/all_to_all | solution.py:419
  72.4 0.7 shard_map.141
  73.2 2.2 %collective-permute-done.6.rest_4_ = bf16[4,96,512]{2,1,0:T(8,128)(2,1)} collective-permute-done((bf16[4,96,512]{2,1,0:T(8,128)(2,1)S(1)}, bf16[4,96,512]{2,1,0:T(8,128)(2,1)}, u32[]{:S(2)}, u32[]{:S(2)}) %collective-permute-start.6) | collective-permute-done | bytes 393248 | tf_op jit(solution)/shard_map/ppermute | solution.py:361
  75.4 0.5 collective-permute-start.5
  76.0 2.2 %collective-permute-done.7.rest_5_ = bf16[4,32,512]{2,1,0:T(8,128)(2,1)S(1)} collective-permute-done((bf16[4,32,512]{2,1,0:T(8,128)(2,1)S(1)}, bf16[4,32,512]{2,1,0:T(8,128)(2,1)S(1)}, u32[]{:S(2)}, u32[]{:S(2)}) %collective-permute-start.7) | collective-permute-done | bytes 131104 | tf_op jit(solution)/shard_map/ppermute | solution.py:361
  78.2 0.6 pad_add_fusion.1.meta
  78.8 0.7 collective-permute-done.9.rest_7_
  79.6 0.6 copy-done.12
  80.1 0.1 copy-done.10
  80.3 0.3 copy-done.8
  80.5 0.1 copy-done.9
  80.7 24.4 %shard_map.142 = (bf16[256,2048]{1,0:T(8,128)(2,1)}, bf16[256,2048]{1,0:T(8,128)(2,1)}, f32[4,512]{1,0:T(4,128)}, f32[256,512]{1,0:T(8,128)}, bf16[256,512]{1,0:T(8,128)(2,1)}) custom-call(s32[25]{0:T(128)} %pad_add_fusion.1.meta, f32[4,512]{1,0:T(4,128)} %bitcast_convert_fusion.cond_ref, f32[1,512]{1,0:T(1,128)} %bitcast.61, bf16[512,256]{1,0:T(8,128)(2,1)} %down_ref.1, ...), custom_call_target="tpu_custom_call" | custom-call | flops 11811160064 | bytes 16777216 | tf_op jit(solution)/shard_map/pallas_call | solution.py:222
  105.1 0.2 collective-permute-start.10
  105.4 1.6 %collective-permute-done.10 = bf16[256,512]{1,0:T(8,128)(2,1)S(1)} collective-permute-done((bf16[256,512]{1,0:T(8,128)(2,1)}, bf16[256,512]{1,0:T(8,128)(2,1)S(1)}, u32[]{:S(2)}, u32[]{:S(2)}) %collective-permute-start.10) | collective-permute-done | bytes 262176 | tf_op jit(solution)/shard_map/ppermute | solution.py:319
  106.9 1.1 convert_add_fusion
  108.2 5.5 %collective-permute-done.11 = bf16[1,128,512]{2,1,0:T(8,128)(2,1)S(1)} collective-permute-done((bf16[1,128,512]{2,1,0:T(8,128)(2,1)S(1)}, bf16[1,128,512]{2,1,0:T(8,128)(2,1)S(1)}, u32[]{:S(2)}, u32[]{:S(2)}) %collective-permute-start.11) | collective-permute-done | bytes 131104 | tf_op jit(solution)/shard_map/ppermute | solution.py:319
  113.8 12.6 %all_to_all.20 = bf16[8,16,512]{2,1,0:T(8,128)(2,1)S(1)} all-to-all(bf16[8,16,512]{2,1,0:T(8,128)(2,1)S(1)} %bitcast.51), channel_id=1, replica_groups=mesh['pool'=4,'dp'=8] {'dp'}, dimensions={0} | all-to-all | bytes 262144 | tf_op jit(solution)/shard_map/all_to_all | solution.py:330
  126.3 0.6 convert_reduce_fusion
  (72 shorter events, 2.2 us)
Async XLA Ops:
  0.6 2.4 %copy-start.5 = (s32[1,1,4,2]{2,3,1,0:T(2,128)S(1)}, s32[1,1,4,2]{2,3,1,0:T(2,128)}, u32[]{:S(2)}) copy-start(s32[1,1,4,2]{2,3,1,0:T(2,128)} %param.14) | copy-start | bytes 100
  0.6 2.6 %copy-start.6 = (s32[1,1,4,2]{2,3,1,0:T(2,128)S(1)}, s32[1,1,4,2]{2,3,1,0:T(2,128)}, u32[]{:S(2)}) copy-start(s32[1,1,4,2]{2,3,1,0:T(2,128)} %param.15) | copy-start | bytes 100
  0.7 2.7 %copy-start.7 = (s32[1,1,16]{2,1,0:T(1,128)S(1)}, s32[1,1,16]{2,1,0:T(1,128)}, u32[]{:S(2)}) copy-start(s32[1,1,16]{2,1,0:T(1,128)} %param.17) | copy-start | bytes 196
  2.2 23.7 %collective-permute-start = (bf16[16,96,512]{2,1,0:T(8,128)(2,1)S(1)}, bf16[16,96,512]{2,1,0:T(8,128)(2,1)S(1)}, u32[]{:S(2)}, u32[]{:S(2)}) collective-permute-start(bf16[16,96,512]{2,1,0:T(8,128)(2,1)S(1)} %slice.28), channel_id=1, source_target_pairs={{24,8},{25,9},{26,10},{27,11},{28,12},{29,13},{30,14},{31,15}} | collective-permute-start | bytes 4718600 | tf_op jit(solution)/shard_map/ppermute | solution.py:361
  4.1 21.9 %all-to-all-start = ((s32[32,1,128]{2,1,0:T(1,128)}), s32[32,1,128]{2,1,0:T(1,128)S(1)}, u32[]{:S(2)}, u32[]{:S(2)}) async-start(s32[32,1,128]{2,1,0:T(1,128)} %broadcast_in_dim.83), calls=%async_computation | async-start | bytes 32768 | tf_op jit(solution)/shard_map/all_to_all | solution.py:374
  27.5 5.3 %collective-permute-start.1 = (bf16[16,96,512]{2,1,0:T(8,128)(2,1)S(1)}, bf16[16,96,512]{2,1,0:T(8,128)(2,1)S(1)}, u32[]{:S(2)}, u32[]{:S(2)}) collective-permute-start(bf16[16,96,512]{2,1,0:T(8,128)(2,1)S(1)} %broadcast_select_fusion.refs_0_), channel_id=1, source_target_pairs={{24,16},{25,17},{26,18},{27,19},{28,20},{29,21},{30,22},{31,23},{8... | collective-permute-start | bytes 4718600 | tf_op jit(solution)/shard_map/ppermute | solution.py:361
  34.3 25.3 %all-to-all-start.1 = ((bf16[8,96,512]{2,1,0:T(8,128)(2,1)}), bf16[8,96,512]{2,1,0:T(8,128)(2,1)S(1)}, u32[]{:S(2)}, u32[]{:S(2)}) async-start(bf16[8,96,512]{2,1,0:T(8,128)(2,1)} %shard_map.138), calls=%async_computation.1 | async-start | bytes 1572864 | tf_op jit(solution)/shard_map/all_to_all | solution.py:419
  40.3 0.8 collective-permute-start.2
  42.2 21.7 %copy-start.4 = (bf16[1,1,4,512]{3,2,1,0:T(4,128)(2,1)S(1)}, bf16[1,1,4,512]{3,2,1,0:T(4,128)(2,1)}, u32[]{:S(2)}) copy-start(bf16[1,1,4,512]{3,2,1,0:T(4,128)(2,1)} %param.13) | copy-start | bytes 12292
  42.2 22.3 %copy-start.2 = (bf16[512,256]{1,0:T(8,128)(2,1)S(1)}, bf16[512,256]{1,0:T(8,128)(2,1)}, u32[]{:S(2)}) copy-start(bf16[512,256]{1,0:T(8,128)(2,1)} %down_ref.1) | copy-start | bytes 786436
  42.3 12.1 %collective-permute-start.3 = (bf16[16,32,512]{2,1,0:T(8,128)(2,1)S(1)}, bf16[16,32,512]{2,1,0:T(8,128)(2,1)S(1)}, u32[]{:S(2)}, u32[]{:S(2)}) collective-permute-start(bf16[16,32,512]{2,1,0:T(8,128)(2,1)S(1)} %broadcast_select_fusion.1.refs_0_), channel_id=1, source_target_pairs={{24,16},{25,17},{26,18},{27,19},{28,20},{29,21},{30,22},{31,23},{8... | collective-permute-start | bytes 1572872 | tf_op jit(solution)/shard_map/ppermute | solution.py:361
  45.1 20.3 %copy-start.3 = (bf16[256,512]{1,0:T(8,128)(2,1)S(1)}, bf16[256,512]{1,0:T(8,128)(2,1)}, u32[]{:S(2)}) copy-start(bf16[256,512]{1,0:T(8,128)(2,1)} %up_ref.1) | copy-start | bytes 786436
  59.7 13.4 %copy-start = (bf16[8,96,512]{2,1,0:T(8,128)(2,1)}, bf16[8,96,512]{2,1,0:T(8,128)(2,1)S(1)}, u32[]{:S(2)}) copy-start(bf16[8,96,512]{2,1,0:T(8,128)(2,1)S(1)} %all-to-all-done.1.refs_0_.rest_0_) | copy-start | bytes 2359300
  59.7 12.7 %all-to-all-start.2 = ((bf16[8,32,512]{2,1,0:T(8,128)(2,1)}), bf16[8,32,512]{2,1,0:T(8,128)(2,1)S(1)}, u32[]{:S(2)}, u32[]{:S(2)}) async-start(bf16[8,32,512]{2,1,0:T(8,128)(2,1)} %shard_map.139), calls=%async_computation.2 | async-start | bytes 524288 | tf_op jit(solution)/shard_map/all_to_all | solution.py:419
  63.8 11.5 %collective-permute-start.6 = (bf16[4,96,512]{2,1,0:T(8,128)(2,1)S(1)}, bf16[4,96,512]{2,1,0:T(8,128)(2,1)}, u32[]{:S(2)}, u32[]{:S(2)}) collective-permute-start(bf16[4,96,512]{2,1,0:T(8,128)(2,1)S(1)} %shard_map.140), channel_id=1, source_target_pairs={{0,16},{1,17},{2,18},{3,19},{4,20},{5,21},{6,22},{7,23},{8,24},{9,... | collective-permute-start | bytes 1179656 | tf_op jit(solution)/shard_map/ppermute | solution.py:361
  66.7 12.8 %collective-permute-start.4 = (bf16[8,96,512]{2,1,0:T(8,128)(2,1)S(1)}, bf16[8,96,512]{2,1,0:T(8,128)(2,1)S(1)}, u32[]{:S(2)}, u32[]{:S(2)}) collective-permute-start(bf16[8,96,512]{2,1,0:T(8,128)(2,1)S(1)} %all-to-all-done.1.refs_0_.rest_0_), channel_id=1, source_target_pairs={{0,8},{1,9},{2,10},{3,11},{4,12},{5,13},{6,14},{7,15},{8,0},{9,1},... | collective-permute-start | bytes 2359304 | tf_op jit(solution)/shard_map/ppermute | solution.py:361
  72.4 7.2 %copy-start.1 = (bf16[8,32,512]{2,1,0:T(8,128)(2,1)}, bf16[8,32,512]{2,1,0:T(8,128)(2,1)S(1)}, u32[]{:S(2)}) copy-start(bf16[8,32,512]{2,1,0:T(8,128)(2,1)S(1)} %all-to-all-done.2.refs_0_.rest_1_) | copy-start | bytes 786436
  73.1 5.0 %collective-permute-start.7 = (bf16[4,32,512]{2,1,0:T(8,128)(2,1)S(1)}, bf16[4,32,512]{2,1,0:T(8,128)(2,1)S(1)}, u32[]{:S(2)}, u32[]{:S(2)}) collective-permute-start(bf16[4,32,512]{2,1,0:T(8,128)(2,1)S(1)} %shard_map.141), channel_id=1, source_target_pairs={{0,16},{1,17},{2,18},{3,19},{4,20},{5,21},{6,22},{7,23},{8,24},{9,... | collective-permute-start | bytes 393224 | tf_op jit(solution)/shard_map/ppermute | solution.py:361
  75.4 4.1 %collective-permute-start.8 = (bf16[4,96,512]{2,1,0:T(8,128)(2,1)}, bf16[4,96,512]{2,1,0:T(8,128)(2,1)S(1)}, u32[]{:S(2)}, u32[]{:S(2)}) collective-permute-start(bf16[4,96,512]{2,1,0:T(8,128)(2,1)} %collective-permute-done.6.rest_4_), channel_id=1, source_target_pairs={{0,8},{1,9},{2,10},{3,11},{4,12},{5,13},{6,14},{7,15},{8,0},{9,1},... | collective-permute-start | bytes 1179656 | tf_op jit(solution)/shard_map/ppermute | solution.py:361
  75.4 4.1 %collective-permute-start.5 = (bf16[8,32,512]{2,1,0:T(8,128)(2,1)S(1)}, bf16[8,32,512]{2,1,0:T(8,128)(2,1)S(1)}, u32[]{:S(2)}, u32[]{:S(2)}) collective-permute-start(bf16[8,32,512]{2,1,0:T(8,128)(2,1)S(1)} %all-to-all-done.2.refs_0_.rest_1_), channel_id=1, source_target_pairs={{0,8},{1,9},{2,10},{3,11},{4,12},{5,13},{6,14},{7,15},{8,0},{9,1},... | collective-permute-start | bytes 786440 | tf_op jit(solution)/shard_map/ppermute | solution.py:361
  78.1 1.4 %copy-start.11 = (bf16[4,32,512]{2,1,0:T(8,128)(2,1)}, bf16[4,32,512]{2,1,0:T(8,128)(2,1)S(1)}, u32[]{:S(2)}) copy-start(bf16[4,32,512]{2,1,0:T(8,128)(2,1)S(1)} %collective-permute-done.7.rest_5_) | copy-start | bytes 393220
  78.2 1.3 %collective-permute-start.9 = (bf16[4,32,512]{2,1,0:T(8,128)(2,1)S(1)}, bf16[4,32,512]{2,1,0:T(8,128)(2,1)S(1)}, u32[]{:S(2)}, u32[]{:S(2)}) collective-permute-start(bf16[4,32,512]{2,1,0:T(8,128)(2,1)S(1)} %collective-permute-done.7.rest_5_), channel_id=1, source_target_pairs={{0,8},{1,9},{2,10},{3,11},{4,12},{5,13},{6,14},{7,15},{8,0},{9,1},... | collective-permute-start | bytes 393224 | tf_op jit(solution)/shard_map/ppermute | solution.py:361
  79.5 0.6 copy-start.12
  79.5 0.8 copy-start.10
  79.5 1.0 copy-start.8
  79.5 1.1 copy-start.9
  105.1 1.8 %collective-permute-start.10 = (bf16[256,512]{1,0:T(8,128)(2,1)}, bf16[256,512]{1,0:T(8,128)(2,1)S(1)}, u32[]{:S(2)}, u32[]{:S(2)}) collective-permute-start(bf16[256,512]{1,0:T(8,128)(2,1)} %get-tuple-element.21), channel_id=1, source_target_pairs={{0,8},{8,0},{16,24},{24,16},{1,9},{9,1},{17,25},{25,17},{2,10},{10... | collective-permute-start | bytes 786440 | tf_op jit(solution)/shard_map/ppermute | solution.py:319
  108.1 5.6 %collective-permute-start.11 = (bf16[1,128,512]{2,1,0:T(8,128)(2,1)S(1)}, bf16[1,128,512]{2,1,0:T(8,128)(2,1)S(1)}, u32[]{:S(2)}, u32[]{:S(2)}) collective-permute-start(bf16[1,128,512]{2,1,0:T(8,128)(2,1)S(1)} %fusion.1), channel_id=1, source_target_pairs={{0,16},{8,24},{16,0},{24,8},{1,17},{9,25},{17,1},{25,9},{2,18},{10... | collective-permute-start | bytes 393224 | tf_op jit(solution)/shard_map/ppermute | solution.py:319

commit v23 on v21

--- a/solution.py
+++ b/solution.py
@@ -135,16 +135,11 @@
 
     for g, cols, value_cols, lane in spots:
         raised = jnp.exp2((score_ref[keys[g], lane] - stat_ref[g, 0:1, lane]) * (scaling * LOG2E))
+        d_probs = dprob_ref[keys[g], lane]
         inv_sum = 1.0 / jnp.sum(raised, axis=0, keepdims=True)
-        score_ref[keys[g], lane] = raised
-        stat_ref[g, 1:2, lane] = inv_sum
-        stat_ref[g, 2:3, lane] = inv_sum * jnp.sum(
-            raised * dprob_ref[keys[g], lane], axis=0, keepdims=True
-        )
-
-    for g, cols, value_cols, lane in spots:
-        probs = score_ref[keys[g], lane] * stat_ref[g, 1:2, lane]
-        d_scores = probs * (dprob_ref[keys[g], lane] - stat_ref[g, 2:3, lane]) * scaling
+        delta = inv_sum * jnp.sum(raised * d_probs, axis=0, keepdims=True)
+        probs = raised * inv_sum
+        d_scores = probs * (d_probs - delta) * scaling
         probs_b, d_scores = probs.astype(jnp.bfloat16), d_scores.astype(jnp.bfloat16)
         grad_ref[keys[g], cols] = dot(d_scores, q2_ref[double[g], cols]).astype(jnp.bfloat16)
         grad_ref[keys[g], value_cols] = dot(probs_b, cot2_ref[double[g], cols]).astype(jnp.bfloat16)

time: 127 us -> 127 us (level); the launches traced: 127 us -> 125 us
  blocking collectives: 14.4 us -> 9.99 us
  starting transfers between devices: 21.8 us -> 24 us
    all_to_all x1, blocking collectives: 14.4 us -> 9.99 us  [scatter_sum(): lax.all_to_all(parts, axes[1], split_axis=0, concat_axis=0, tiled=True)]
    ppermute x2, starting transfers between devices: 0.28 us -> 2.48 us  [scatter_sum(): lax.ppermute(a, axes[0], [(i, i ^ bit) for i in range(size)])]
where the time goes in v23:
time: 127 us; the launch traced here: 125 us
  waiting for transfers between devices  40.4 us (32%)
  Pallas kernels  27.1 us (21%)
  starting transfers between devices  24 us (19%)
  local copies, waits for them, and re-layouts  14.5 us (11%)
  blocking collectives  9.99 us (8%)
  other arithmetic  8.13 us (6%)
    pallas_call x1, Pallas kernels, run_spans(): pl.pallas_call(functools.partial(span_kernel, len(held), nbr_count, bound...  23.1 us
    ppermute x10, waiting for transfers between devices, hop(): lax.ppermute(array, axes, [(a * columns + j, b * columns + j) for a, b in...  16.7 us
    all_to_all x1, blocking collectives, scatter_sum(): lax.all_to_all(parts, axes[1], split_axis=0, concat_axis=0, tiled=True)  9.99 us
    all_to_all x2, waiting for transfers between devices, body(): lax.all_to_all(sends, 'dp', split_axis=0, concat_axis=0, tiled=True)  9.49 us
    unnamed x31, local copies, waits for them, and re-layouts  9.49 us
    all_to_all x2, starting transfers between devices, body(): lax.all_to_all(sends, 'dp', split_axis=0, concat_axis=0, tiled=True)  8.48 us
    all_to_all x1, starting transfers between devices, to_all(): return lax.all_to_all(copies, axis, split_axis=0, concat_axis=0, tiled=True)  8.23 us
    ppermute x2, waiting for transfers between devices, scatter_sum(): lax.ppermute(a, axes[0], [(i, i ^ bit) for i in range(size)])  7.13 us
  transfers between devices with their start and end apart: 15, of which 10 were waited for; matrix products, arithmetic and copies ran while one was open for 13% of the time, Pallas kernels for 2%

profile of v23, /device:TPU:0, one launch (start us, length us, event | category | flops | bytes accessed | tf_op | source)
XLA Modules:
  0.0 125.2 jit_solution(14022084475093496402)
XLA Ops:
  0.7 1.6 %slice.28 = bf16[16,96,512]{2,1,0:T(8,128)(2,1)S(1)} slice(bf16[16,128,512]{2,1,0:T(8,128)(2,1)} %bitcast.44), slice={[0:16], [0:96], [0:512]} | slice | bytes 3145728 | tf_op jit(solution)/shard_map/slice | solution.py:342
  2.2 0.8 collective-permute-start
  3.5 0.6 broadcast_in_dim.83
  4.1 8.2 %all-to-all-start = ((s32[32,1,128]{2,1,0:T(1,128)}), s32[32,1,128]{2,1,0:T(1,128)S(1)}, u32[]{:S(2)}, u32[]{:S(2)}) async-start(s32[32,1,128]{2,1,0:T(1,128)} %broadcast_in_dim.83), calls=%async_computation | async-start | bytes 32768 | tf_op jit(solution)/shard_map/all_to_all | solution.py:347
  12.4 6.5 %copy.45 = bf16[512,4096]{0,1:T(8,128)(2,1)} copy(bf16[512,4096]{1,0:T(8,128)(2,1)} %rest_8_.1) | data formatting | bytes 8388608 | tf_op args[10]
  18.9 7.1 %all-to-all-done = s32[32,1,128]{2,1,0:T(1,128)S(1)} async-done(((s32[32,1,128]{2,1,0:T(1,128)}), s32[32,1,128]{2,1,0:T(1,128)S(1)}, u32[]{:S(2)}, u32[]{:S(2)}) %all-to-all-start) | async-done | bytes 16416 | tf_op jit(solution)/shard_map/all_to_all | solution.py:347
  26.0 1.6 %broadcast_select_fusion.refs_0_ = bf16[16,96,512]{2,1,0:T(8,128)(2,1)S(1)} fusion(bf16[16,96,512]{2,1,0:T(8,128)(2,1)S(1)} %collective-permute-done, pred[]{:T(512)S(6)} %eq.145, bf16[16,128,512]{2,1,0:T(8,128)(2,1)} %bitcast.45), kind=kLoop, calls=%fused_computation | loop fusion | flops 786432 | bytes 4718593 | tf_op jit(solution)/shard_map/jit(_where)/select_n | solution.py:385
  27.5 1.3 %collective-permute-start.1 = (bf16[16,96,512]{2,1,0:T(8,128)(2,1)S(1)}, bf16[16,96,512]{2,1,0:T(8,128)(2,1)S(1)}, u32[]{:S(2)}, u32[]{:S(2)}) collective-permute-start(bf16[16,96,512]{2,1,0:T(8,128)(2,1)S(1)} %broadcast_select_fusion.refs_0_), channel_id=1, source_target_pairs={{24,16},{25,17},{26,18},{27,19},{28,20},{29,21},{30,22},{31,23},{8... | collective-permute-start | bytes 4718600 | tf_op jit(solution)/shard_map/ppermute | solution.py:334
  29.0 0.3 convert_reduce_fusion.4
  29.4 0.6 convert_reduce_fusion.1
  30.2 0.2 select_reduce_fusion
  30.4 2.4 %collective-permute-done.1.refs_1_ = bf16[16,96,512]{2,1,0:T(8,128)(2,1)S(1)} collective-permute-done((bf16[16,96,512]{2,1,0:T(8,128)(2,1)S(1)}, bf16[16,96,512]{2,1,0:T(8,128)(2,1)S(1)}, u32[]{:S(2)}, u32[]{:S(2)}) %collective-permute-start.1) | collective-permute-done | bytes 1572896 | tf_op jit(solution)/shard_map/ppermute | solution.py:334
  32.8 1.5 %shard_map.138 = bf16[8,96,512]{2,1,0:T(8,128)(2,1)} custom-call(s32[9]{0:T(128)S(1)} %pad_add_fusion.2.meta, bf16[16,96,512]{2,1,0:T(8,128)(2,1)S(1)} %broadcast_select_fusion.refs_0_, bf16[16,96,512]{2,1,0:T(8,128)(2,1)S(1)} %collective-permute-done.1.refs_1_), custom_call_target="tpu_custom_call" | custom-call | tf_op jit(solution)/shard_map/pallas_call | solution.py:254
  34.3 4.9 %all-to-all-start.1 = ((bf16[8,96,512]{2,1,0:T(8,128)(2,1)}), bf16[8,96,512]{2,1,0:T(8,128)(2,1)S(1)}, u32[]{:S(2)}, u32[]{:S(2)}) async-start(bf16[8,96,512]{2,1,0:T(8,128)(2,1)} %shard_map.138), calls=%async_computation.1 | async-start | bytes 1572864 | tf_op jit(solution)/shard_map/all_to_all | solution.py:392
  39.2 1.1 slice.27
  40.3 0.7 collective-permute-start.2
  41.1 1.1 broadcast_select_fusion.1.refs_0_
  42.3 1.4 %collective-permute-start.3 = (bf16[16,32,512]{2,1,0:T(8,128)(2,1)S(1)}, bf16[16,32,512]{2,1,0:T(8,128)(2,1)S(1)}, u32[]{:S(2)}, u32[]{:S(2)}) collective-permute-start(bf16[16,32,512]{2,1,0:T(8,128)(2,1)S(1)} %broadcast_select_fusion.1.refs_0_), channel_id=1, source_target_pairs={{24,16},{25,17},{26,18},{27,19},{28,20},{29,21},{30,22},{31,23},{8... | collective-permute-start | bytes 1572872 | tf_op jit(solution)/shard_map/ppermute | solution.py:334
  43.7 0.5 broadcast.437
  44.2 0.7 fusion.34
  44.9 0.1 select_reduce_fusion.2
  45.1 9.2 %collective-permute-done.3.refs_1_ = bf16[16,32,512]{2,1,0:T(8,128)(2,1)S(1)} collective-permute-done((bf16[16,32,512]{2,1,0:T(8,128)(2,1)S(1)}, bf16[16,32,512]{2,1,0:T(8,128)(2,1)S(1)}, u32[]{:S(2)}, u32[]{:S(2)}) %collective-permute-start.3) | collective-permute-done | bytes 524320 | tf_op jit(solution)/shard_map/ppermute | solution.py:334
  54.3 1.3 %shard_map.139 = bf16[8,32,512]{2,1,0:T(8,128)(2,1)} custom-call(s32[9]{0:T(128)S(1)} %pad_add_fusion.2.meta, bf16[16,32,512]{2,1,0:T(8,128)(2,1)S(1)} %broadcast_select_fusion.1.refs_0_, bf16[16,32,512]{2,1,0:T(8,128)(2,1)S(1)} %collective-permute-done.3.refs_1_), custom_call_target="tpu_custom_call" | custom-call | tf_op jit(solution)/shard_map/pallas_call | solution.py:254
  55.6 4.1 %all-to-all-done.1.refs_0_.rest_0_ = bf16[8,96,512]{2,1,0:T(8,128)(2,1)S(1)} async-done(((bf16[8,96,512]{2,1,0:T(8,128)(2,1)}), bf16[8,96,512]{2,1,0:T(8,128)(2,1)S(1)}, u32[]{:S(2)}, u32[]{:S(2)}) %all-to-all-start.1) | async-done | bytes 786464 | tf_op jit(solution)/shard_map/all_to_all | solution.py:392
  59.7 3.6 %all-to-all-start.2 = ((bf16[8,32,512]{2,1,0:T(8,128)(2,1)}), bf16[8,32,512]{2,1,0:T(8,128)(2,1)S(1)}, u32[]{:S(2)}, u32[]{:S(2)}) async-start(bf16[8,32,512]{2,1,0:T(8,128)(2,1)} %shard_map.139), calls=%async_computation.2 | async-start | bytes 524288 | tf_op jit(solution)/shard_map/all_to_all | solution.py:392
  63.3 0.6 shard_map.140
  63.9 0.6 bitcast_convert_fusion.cond_ref
  64.5 0.8 copy.50
  65.4 0.8 copy.49
  66.7 0.2 select_reduce_fusion.1
  66.9 5.4 %all-to-all-done.2.refs_0_.rest_1_ = bf16[8,32,512]{2,1,0:T(8,128)(2,1)S(1)} async-done(((bf16[8,32,512]{2,1,0:T(8,128)(2,1)}), bf16[8,32,512]{2,1,0:T(8,128)(2,1)S(1)}, u32[]{:S(2)}, u32[]{:S(2)}) %all-to-all-start.2) | async-done | bytes 262176 | tf_op jit(solution)/shard_map/all_to_all | solution.py:392
  72.4 0.7 shard_map.141
  73.2 2.2 %collective-permute-done.6.rest_4_ = bf16[4,96,512]{2,1,0:T(8,128)(2,1)} collective-permute-done((bf16[4,96,512]{2,1,0:T(8,128)(2,1)S(1)}, bf16[4,96,512]{2,1,0:T(8,128)(2,1)}, u32[]{:S(2)}, u32[]{:S(2)}) %collective-permute-start.6) | collective-permute-done | bytes 393248 | tf_op jit(solution)/shard_map/ppermute | solution.py:334
  75.4 0.5 collective-permute-start.5
  76.0 2.2 %collective-permute-done.7.rest_5_ = bf16[4,32,512]{2,1,0:T(8,128)(2,1)S(1)} collective-permute-done((bf16[4,32,512]{2,1,0:T(8,128)(2,1)S(1)}, bf16[4,32,512]{2,1,0:T(8,128)(2,1)S(1)}, u32[]{:S(2)}, u32[]{:S(2)}) %collective-permute-start.7) | collective-permute-done | bytes 131104 | tf_op jit(solution)/shard_map/ppermute | solution.py:334
  78.2 0.6 pad_add_fusion.1.meta
  78.8 0.7 collective-permute-done.9.rest_7_
  79.6 0.6 copy-done.12
  80.1 0.1 copy-done.10
  80.3 0.3 copy-done.8
  80.5 0.1 copy-done.9
  80.7 23.1 %shard_map.142 = (bf16[256,2048]{1,0:T(8,128)(2,1)}, bf16[256,2048]{1,0:T(8,128)(2,1)}, f32[4,512]{1,0:T(4,128)}, f32[256,512]{1,0:T(8,128)}, bf16[256,512]{1,0:T(8,128)(2,1)}) custom-call(s32[25]{0:T(128)} %pad_add_fusion.1.meta, bf16[256,2048]{1,0:T(8,128)(2,1)} %bitcast.59, bf16[256,2048]{1,0:T(8,128)(2,1)} %bitcast.60, ...), custom_call_target="tpu_custom_call" | custom-call | flops 11811160064 | bytes 16777216 | tf_op jit(solution)/shard_map/pallas_call | solution.py:197
  103.8 2.4 %collective-permute-start.10 = (bf16[256,512]{1,0:T(8,128)(2,1)}, bf16[256,512]{1,0:T(8,128)(2,1)S(1)}, u32[]{:S(2)}, u32[]{:S(2)}) collective-permute-start(bf16[256,512]{1,0:T(8,128)(2,1)} %get-tuple-element.21), channel_id=1, source_target_pairs={{0,8},{8,0},{16,24},{24,16},{1,9},{9,1},{17,25},{25,17},{2,10},{10... | collective-permute-start | bytes 786440 | tf_op jit(solution)/shard_map/ppermute | solution.py:292
  106.2 1.4 %collective-permute-done.10 = bf16[256,512]{1,0:T(8,128)(2,1)S(1)} collective-permute-done((bf16[256,512]{1,0:T(8,128)(2,1)}, bf16[256,512]{1,0:T(8,128)(2,1)S(1)}, u32[]{:S(2)}, u32[]{:S(2)}) %collective-permute-start.10) | collective-permute-done | bytes 262176 | tf_op jit(solution)/shard_map/ppermute | solution.py:292
  107.5 1.1 convert_add_fusion
  108.8 5.8 %collective-permute-done.11 = bf16[1,128,512]{2,1,0:T(8,128)(2,1)S(1)} collective-permute-done((bf16[1,128,512]{2,1,0:T(8,128)(2,1)S(1)}, bf16[1,128,512]{2,1,0:T(8,128)(2,1)S(1)}, u32[]{:S(2)}, u32[]{:S(2)}) %collective-permute-start.11) | collective-permute-done | bytes 131104 | tf_op jit(solution)/shard_map/ppermute | solution.py:292
  114.6 10.0 %all_to_all.20 = bf16[8,16,512]{2,1,0:T(8,128)(2,1)S(1)} all-to-all(bf16[8,16,512]{2,1,0:T(8,128)(2,1)S(1)} %bitcast.51), channel_id=1, replica_groups=mesh['pool'=4,'dp'=8] {'dp'}, dimensions={0} | all-to-all | bytes 262144 | tf_op jit(solution)/shard_map/all_to_all | solution.py:303
  124.6 0.6 convert_reduce_fusion
  (72 shorter events, 2.2 us)
Async XLA Ops:
  0.6 2.4 %copy-start.5 = (s32[1,1,4,2]{2,3,1,0:T(2,128)S(1)}, s32[1,1,4,2]{2,3,1,0:T(2,128)}, u32[]{:S(2)}) copy-start(s32[1,1,4,2]{2,3,1,0:T(2,128)} %param.14) | copy-start | bytes 100
  0.6 2.6 %copy-start.6 = (s32[1,1,4,2]{2,3,1,0:T(2,128)S(1)}, s32[1,1,4,2]{2,3,1,0:T(2,128)}, u32[]{:S(2)}) copy-start(s32[1,1,4,2]{2,3,1,0:T(2,128)} %param.15) | copy-start | bytes 100
  0.7 2.7 %copy-start.7 = (s32[1,1,16]{2,1,0:T(1,128)S(1)}, s32[1,1,16]{2,1,0:T(1,128)}, u32[]{:S(2)}) copy-start(s32[1,1,16]{2,1,0:T(1,128)} %param.17) | copy-start | bytes 196
  2.2 23.7 %collective-permute-start = (bf16[16,96,512]{2,1,0:T(8,128)(2,1)S(1)}, bf16[16,96,512]{2,1,0:T(8,128)(2,1)S(1)}, u32[]{:S(2)}, u32[]{:S(2)}) collective-permute-start(bf16[16,96,512]{2,1,0:T(8,128)(2,1)S(1)} %slice.28), channel_id=1, source_target_pairs={{24,8},{25,9},{26,10},{27,11},{28,12},{29,13},{30,14},{31,15}} | collective-permute-start | bytes 4718600 | tf_op jit(solution)/shard_map/ppermute | solution.py:334
  4.1 21.9 %all-to-all-start = ((s32[32,1,128]{2,1,0:T(1,128)}), s32[32,1,128]{2,1,0:T(1,128)S(1)}, u32[]{:S(2)}, u32[]{:S(2)}) async-start(s32[32,1,128]{2,1,0:T(1,128)} %broadcast_in_dim.83), calls=%async_computation | async-start | bytes 32768 | tf_op jit(solution)/shard_map/all_to_all | solution.py:347
  27.5 5.3 %collective-permute-start.1 = (bf16[16,96,512]{2,1,0:T(8,128)(2,1)S(1)}, bf16[16,96,512]{2,1,0:T(8,128)(2,1)S(1)}, u32[]{:S(2)}, u32[]{:S(2)}) collective-permute-start(bf16[16,96,512]{2,1,0:T(8,128)(2,1)S(1)} %broadcast_select_fusion.refs_0_), channel_id=1, source_target_pairs={{24,16},{25,17},{26,18},{27,19},{28,20},{29,21},{30,22},{31,23},{8... | collective-permute-start | bytes 4718600 | tf_op jit(solution)/shard_map/ppermute | solution.py:334
  34.3 25.3 %all-to-all-start.1 = ((bf16[8,96,512]{2,1,0:T(8,128)(2,1)}), bf16[8,96,512]{2,1,0:T(8,128)(2,1)S(1)}, u32[]{:S(2)}, u32[]{:S(2)}) async-start(bf16[8,96,512]{2,1,0:T(8,128)(2,1)} %shard_map.138), calls=%async_computation.1 | async-start | bytes 1572864 | tf_op jit(solution)/shard_map/all_to_all | solution.py:392
  40.3 0.8 collective-permute-start.2
  42.2 21.7 %copy-start.4 = (bf16[1,1,4,512]{3,2,1,0:T(4,128)(2,1)S(1)}, bf16[1,1,4,512]{3,2,1,0:T(4,128)(2,1)}, u32[]{:S(2)}) copy-start(bf16[1,1,4,512]{3,2,1,0:T(4,128)(2,1)} %param.13) | copy-start | bytes 12292
  42.2 22.3 %copy-start.2 = (bf16[512,256]{1,0:T(8,128)(2,1)S(1)}, bf16[512,256]{1,0:T(8,128)(2,1)}, u32[]{:S(2)}) copy-start(bf16[512,256]{1,0:T(8,128)(2,1)} %down_ref.1) | copy-start | bytes 786436
  42.3 12.1 %collective-permute-start.3 = (bf16[16,32,512]{2,1,0:T(8,128)(2,1)S(1)}, bf16[16,32,512]{2,1,0:T(8,128)(2,1)S(1)}, u32[]{:S(2)}, u32[]{:S(2)}) collective-permute-start(bf16[16,32,512]{2,1,0:T(8,128)(2,1)S(1)} %broadcast_select_fusion.1.refs_0_), channel_id=1, source_target_pairs={{24,16},{25,17},{26,18},{27,19},{28,20},{29,21},{30,22},{31,23},{8... | collective-permute-start | bytes 1572872 | tf_op jit(solution)/shard_map/ppermute | solution.py:334
  45.1 20.3 %copy-start.3 = (bf16[256,512]{1,0:T(8,128)(2,1)S(1)}, bf16[256,512]{1,0:T(8,128)(2,1)}, u32[]{:S(2)}) copy-start(bf16[256,512]{1,0:T(8,128)(2,1)} %up_ref.1) | copy-start | bytes 786436
  59.7 13.4 %copy-start = (bf16[8,96,512]{2,1,0:T(8,128)(2,1)}, bf16[8,96,512]{2,1,0:T(8,128)(2,1)S(1)}, u32[]{:S(2)}) copy-start(bf16[8,96,512]{2,1,0:T(8,128)(2,1)S(1)} %all-to-all-done.1.refs_0_.rest_0_) | copy-start | bytes 2359300
  59.7 12.7 %all-to-all-start.2 = ((bf16[8,32,512]{2,1,0:T(8,128)(2,1)}), bf16[8,32,512]{2,1,0:T(8,128)(2,1)S(1)}, u32[]{:S(2)}, u32[]{:S(2)}) async-start(bf16[8,32,512]{2,1,0:T(8,128)(2,1)} %shard_map.139), calls=%async_computation.2 | async-start | bytes 524288 | tf_op jit(solution)/shard_map/all_to_all | solution.py:392
  63.8 11.5 %collective-permute-start.6 = (bf16[4,96,512]{2,1,0:T(8,128)(2,1)S(1)}, bf16[4,96,512]{2,1,0:T(8,128)(2,1)}, u32[]{:S(2)}, u32[]{:S(2)}) collective-permute-start(bf16[4,96,512]{2,1,0:T(8,128)(2,1)S(1)} %shard_map.140), channel_id=1, source_target_pairs={{0,16},{1,17},{2,18},{3,19},{4,20},{5,21},{6,22},{7,23},{8,24},{9,... | collective-permute-start | bytes 1179656 | tf_op jit(solution)/shard_map/ppermute | solution.py:334
  66.7 12.8 %collective-permute-start.4 = (bf16[8,96,512]{2,1,0:T(8,128)(2,1)S(1)}, bf16[8,96,512]{2,1,0:T(8,128)(2,1)S(1)}, u32[]{:S(2)}, u32[]{:S(2)}) collective-permute-start(bf16[8,96,512]{2,1,0:T(8,128)(2,1)S(1)} %all-to-all-done.1.refs_0_.rest_0_), channel_id=1, source_target_pairs={{0,8},{1,9},{2,10},{3,11},{4,12},{5,13},{6,14},{7,15},{8,0},{9,1},... | collective-permute-start | bytes 2359304 | tf_op jit(solution)/shard_map/ppermute | solution.py:334
  72.4 7.2 %copy-start.1 = (bf16[8,32,512]{2,1,0:T(8,128)(2,1)}, bf16[8,32,512]{2,1,0:T(8,128)(2,1)S(1)}, u32[]{:S(2)}) copy-start(bf16[8,32,512]{2,1,0:T(8,128)(2,1)S(1)} %all-to-all-done.2.refs_0_.rest_1_) | copy-start | bytes 786436
  73.1 5.0 %collective-permute-start.7 = (bf16[4,32,512]{2,1,0:T(8,128)(2,1)S(1)}, bf16[4,32,512]{2,1,0:T(8,128)(2,1)S(1)}, u32[]{:S(2)}, u32[]{:S(2)}) collective-permute-start(bf16[4,32,512]{2,1,0:T(8,128)(2,1)S(1)} %shard_map.141), channel_id=1, source_target_pairs={{0,16},{1,17},{2,18},{3,19},{4,20},{5,21},{6,22},{7,23},{8,24},{9,... | collective-permute-start | bytes 393224 | tf_op jit(solution)/shard_map/ppermute | solution.py:334
  75.4 4.1 %collective-permute-start.8 = (bf16[4,96,512]{2,1,0:T(8,128)(2,1)}, bf16[4,96,512]{2,1,0:T(8,128)(2,1)S(1)}, u32[]{:S(2)}, u32[]{:S(2)}) collective-permute-start(bf16[4,96,512]{2,1,0:T(8,128)(2,1)} %collective-permute-done.6.rest_4_), channel_id=1, source_target_pairs={{0,8},{1,9},{2,10},{3,11},{4,12},{5,13},{6,14},{7,15},{8,0},{9,1},... | collective-permute-start | bytes 1179656 | tf_op jit(solution)/shard_map/ppermute | solution.py:334
  75.4 4.1 %collective-permute-start.5 = (bf16[8,32,512]{2,1,0:T(8,128)(2,1)S(1)}, bf16[8,32,512]{2,1,0:T(8,128)(2,1)S(1)}, u32[]{:S(2)}, u32[]{:S(2)}) collective-permute-start(bf16[8,32,512]{2,1,0:T(8,128)(2,1)S(1)} %all-to-all-done.2.refs_0_.rest_1_), channel_id=1, source_target_pairs={{0,8},{1,9},{2,10},{3,11},{4,12},{5,13},{6,14},{7,15},{8,0},{9,1},... | collective-permute-start | bytes 786440 | tf_op jit(solution)/shard_map/ppermute | solution.py:334
  78.1 1.4 %copy-start.11 = (bf16[4,32,512]{2,1,0:T(8,128)(2,1)}, bf16[4,32,512]{2,1,0:T(8,128)(2,1)S(1)}, u32[]{:S(2)}) copy-start(bf16[4,32,512]{2,1,0:T(8,128)(2,1)S(1)} %collective-permute-done.7.rest_5_) | copy-start | bytes 393220
  78.2 1.3 %collective-permute-start.9 = (bf16[4,32,512]{2,1,0:T(8,128)(2,1)S(1)}, bf16[4,32,512]{2,1,0:T(8,128)(2,1)S(1)}, u32[]{:S(2)}, u32[]{:S(2)}) collective-permute-start(bf16[4,32,512]{2,1,0:T(8,128)(2,1)S(1)} %collective-permute-done.7.rest_5_), channel_id=1, source_target_pairs={{0,8},{1,9},{2,10},{3,11},{4,12},{5,13},{6,14},{7,15},{8,0},{9,1},... | collective-permute-start | bytes 393224 | tf_op jit(solution)/shard_map/ppermute | solution.py:334
  79.5 0.6 copy-start.12
  79.5 0.8 copy-start.10
  79.5 1.0 copy-start.8
  79.5 1.1 copy-start.9
  103.8 3.8 %collective-permute-start.10 = (bf16[256,512]{1,0:T(8,128)(2,1)}, bf16[256,512]{1,0:T(8,128)(2,1)S(1)}, u32[]{:S(2)}, u32[]{:S(2)}) collective-permute-start(bf16[256,512]{1,0:T(8,128)(2,1)} %get-tuple-element.21), channel_id=1, source_target_pairs={{0,8},{8,0},{16,24},{24,16},{1,9},{9,1},{17,25},{25,17},{2,10},{10... | collective-permute-start | bytes 786440 | tf_op jit(solution)/shard_map/ppermute | solution.py:292
  108.7 5.8 %collective-permute-start.11 = (bf16[1,128,512]{2,1,0:T(8,128)(2,1)S(1)}, bf16[1,128,512]{2,1,0:T(8,128)(2,1)S(1)}, u32[]{:S(2)}, u32[]{:S(2)}) collective-permute-start(bf16[1,128,512]{2,1,0:T(8,128)(2,1)S(1)} %fusion.1), channel_id=1, source_target_pairs={{0,16},{8,24},{16,0},{24,8},{1,17},{9,25},{17,1},{25,9},{2,18},{10... | collective-permute-start | bytes 393224 | tf_op jit(solution)/shard_map/ppermute | solution.py:292

commit v24 on v21

--- a/solution.py
+++ b/solution.py
@@ -61,6 +61,7 @@
 
     @pl.when(step == 0)
     def _():
+        kv_copy.start()
         for n in range(per_device):
             for b, held in enumerate(held_refs):
                 @pl.when(meta[which + n] == b // parts)
@@ -71,8 +72,6 @@
                         raw_ref.at[n, cuts[part]],
                         sems.at[n * parts + part],
                     ).start()
-        kv_copy.start()
-        kvt_copy.start()
         q2_ref[...] = jnp.zeros_like(q2_ref)
         cot2_ref[...] = jnp.zeros_like(cot2_ref)
 
@@ -110,6 +109,7 @@
     @pl.when(step == 0)
     def _():
         kv_copy.wait()
+        kvt_copy.start()
 
     for cols in pairs + value_pairs:
         proj_ref[:, cols] = dot(encoded, kv_ref[:, cols]).astype(jnp.bfloat16)

time: 127 us -> 127 us (level); the launches traced: 127 us -> 125 us
  blocking collectives: 14.4 us -> 11.2 us
  starting transfers between devices: 21.8 us -> 23.1 us
    all_to_all x1, blocking collectives: 14.4 us -> 11.2 us  [scatter_sum(): lax.all_to_all(parts, axes[1], split_axis=0, concat_axis=0, tiled=True)]
where the time goes in v24:
time: 127 us; the launch traced here: 125 us
  waiting for transfers between devices  40.2 us (32%)
  Pallas kernels  27.2 us (21%)
  starting transfers between devices  23.1 us (18%)
  local copies, waits for them, and re-layouts  14.5 us (11%)
  blocking collectives  11.2 us (9%)
  other arithmetic  8.13 us (6%)
    pallas_call x1, Pallas kernels, run_spans(): pl.pallas_call(functools.partial(span_kernel, len(held), nbr_count, bound...  23.1 us
    ppermute x10, waiting for transfers between devices, hop(): lax.ppermute(array, axes, [(a * columns + j, b * columns + j) for a, b in...  16.7 us
    all_to_all x1, blocking collectives, scatter_sum(): lax.all_to_all(parts, axes[1], split_axis=0, concat_axis=0, tiled=True)  11.2 us
    all_to_all x2, waiting for transfers between devices, body(): lax.all_to_all(sends, 'dp', split_axis=0, concat_axis=0, tiled=True)  9.49 us
    unnamed x31, local copies, waits for them, and re-layouts  9.49 us
    all_to_all x2, starting transfers between devices, body(): lax.all_to_all(sends, 'dp', split_axis=0, concat_axis=0, tiled=True)  8.48 us
    all_to_all x1, starting transfers between devices, to_all(): return lax.all_to_all(copies, axis, split_axis=0, concat_axis=0, tiled=True)  8.23 us
    all_to_all x1, waiting for transfers between devices, to_all(): return lax.all_to_all(copies, axis, split_axis=0, concat_axis=0, tiled=True)  7.09 us
  transfers between devices with their start and end apart: 15, of which 10 were waited for; matrix products, arithmetic and copies ran while one was open for 13% of the time, Pallas kernels for 2%

profile of v24, /device:TPU:0, one launch (start us, length us, event | category | flops | bytes accessed | tf_op | source)
XLA Modules:
  0.0 125.2 jit_solution(8920975738495443930)
XLA Ops:
  0.7 1.6 %slice.28 = bf16[16,96,512]{2,1,0:T(8,128)(2,1)S(1)} slice(bf16[16,128,512]{2,1,0:T(8,128)(2,1)} %bitcast.44), slice={[0:16], [0:96], [0:512]} | slice | bytes 3145728 | tf_op jit(solution)/shard_map/slice | solution.py:347
  2.2 0.8 collective-permute-start
  3.5 0.6 broadcast_in_dim.83
  4.1 8.2 %all-to-all-start = ((s32[32,1,128]{2,1,0:T(1,128)}), s32[32,1,128]{2,1,0:T(1,128)S(1)}, u32[]{:S(2)}, u32[]{:S(2)}) async-start(s32[32,1,128]{2,1,0:T(1,128)} %broadcast_in_dim.83), calls=%async_computation | async-start | bytes 32768 | tf_op jit(solution)/shard_map/all_to_all | solution.py:352
  12.4 6.5 %copy.45 = bf16[512,4096]{0,1:T(8,128)(2,1)} copy(bf16[512,4096]{1,0:T(8,128)(2,1)} %rest_8_.1) | data formatting | bytes 8388608 | tf_op args[10]
  18.9 7.1 %all-to-all-done = s32[32,1,128]{2,1,0:T(1,128)S(1)} async-done(((s32[32,1,128]{2,1,0:T(1,128)}), s32[32,1,128]{2,1,0:T(1,128)S(1)}, u32[]{:S(2)}, u32[]{:S(2)}) %all-to-all-start) | async-done | bytes 16416 | tf_op jit(solution)/shard_map/all_to_all | solution.py:352
  26.0 1.6 %broadcast_select_fusion.refs_0_ = bf16[16,96,512]{2,1,0:T(8,128)(2,1)S(1)} fusion(bf16[16,96,512]{2,1,0:T(8,128)(2,1)S(1)} %collective-permute-done, pred[]{:T(512)S(6)} %eq.145, bf16[16,128,512]{2,1,0:T(8,128)(2,1)} %bitcast.45), kind=kLoop, calls=%fused_computation | loop fusion | flops 786432 | bytes 4718593 | tf_op jit(solution)/shard_map/jit(_where)/select_n | solution.py:390
  27.5 1.3 %collective-permute-start.1 = (bf16[16,96,512]{2,1,0:T(8,128)(2,1)S(1)}, bf16[16,96,512]{2,1,0:T(8,128)(2,1)S(1)}, u32[]{:S(2)}, u32[]{:S(2)}) collective-permute-start(bf16[16,96,512]{2,1,0:T(8,128)(2,1)S(1)} %broadcast_select_fusion.refs_0_), channel_id=1, source_target_pairs={{24,16},{25,17},{26,18},{27,19},{28,20},{29,21},{30,22},{31,23},{8... | collective-permute-start | bytes 4718600 | tf_op jit(solution)/shard_map/ppermute | solution.py:339
  29.0 0.3 convert_reduce_fusion.4
  29.4 0.6 convert_reduce_fusion.1
  30.2 0.2 select_reduce_fusion
  30.4 2.4 %collective-permute-done.1.refs_1_ = bf16[16,96,512]{2,1,0:T(8,128)(2,1)S(1)} collective-permute-done((bf16[16,96,512]{2,1,0:T(8,128)(2,1)S(1)}, bf16[16,96,512]{2,1,0:T(8,128)(2,1)S(1)}, u32[]{:S(2)}, u32[]{:S(2)}) %collective-permute-start.1) | collective-permute-done | bytes 1572896 | tf_op jit(solution)/shard_map/ppermute | solution.py:339
  32.8 1.5 %shard_map.138 = bf16[8,96,512]{2,1,0:T(8,128)(2,1)} custom-call(s32[9]{0:T(128)S(1)} %pad_add_fusion.2.meta, bf16[16,96,512]{2,1,0:T(8,128)(2,1)S(1)} %broadcast_select_fusion.refs_0_, bf16[16,96,512]{2,1,0:T(8,128)(2,1)S(1)} %collective-permute-done.1.refs_1_), custom_call_target="tpu_custom_call" | custom-call | tf_op jit(solution)/shard_map/pallas_call | solution.py:259
  34.3 4.9 %all-to-all-start.1 = ((bf16[8,96,512]{2,1,0:T(8,128)(2,1)}), bf16[8,96,512]{2,1,0:T(8,128)(2,1)S(1)}, u32[]{:S(2)}, u32[]{:S(2)}) async-start(bf16[8,96,512]{2,1,0:T(8,128)(2,1)} %shard_map.138), calls=%async_computation.1 | async-start | bytes 1572864 | tf_op jit(solution)/shard_map/all_to_all | solution.py:397
  39.2 1.1 slice.27
  40.3 0.7 collective-permute-start.2
  41.1 1.1 broadcast_select_fusion.1.refs_0_
  42.3 1.4 %collective-permute-start.3 = (bf16[16,32,512]{2,1,0:T(8,128)(2,1)S(1)}, bf16[16,32,512]{2,1,0:T(8,128)(2,1)S(1)}, u32[]{:S(2)}, u32[]{:S(2)}) collective-permute-start(bf16[16,32,512]{2,1,0:T(8,128)(2,1)S(1)} %broadcast_select_fusion.1.refs_0_), channel_id=1, source_target_pairs={{24,16},{25,17},{26,18},{27,19},{28,20},{29,21},{30,22},{31,23},{8... | collective-permute-start | bytes 1572872 | tf_op jit(solution)/shard_map/ppermute | solution.py:339
  43.7 0.5 broadcast.437
  44.2 0.7 fusion.34
  45.1 9.2 %collective-permute-done.3.refs_1_ = bf16[16,32,512]{2,1,0:T(8,128)(2,1)S(1)} collective-permute-done((bf16[16,32,512]{2,1,0:T(8,128)(2,1)S(1)}, bf16[16,32,512]{2,1,0:T(8,128)(2,1)S(1)}, u32[]{:S(2)}, u32[]{:S(2)}) %collective-permute-start.3) | collective-permute-done | bytes 524320 | tf_op jit(solution)/shard_map/ppermute | solution.py:339
  54.3 1.3 %shard_map.139 = bf16[8,32,512]{2,1,0:T(8,128)(2,1)} custom-call(s32[9]{0:T(128)S(1)} %pad_add_fusion.2.meta, bf16[16,32,512]{2,1,0:T(8,128)(2,1)S(1)} %broadcast_select_fusion.1.refs_0_, bf16[16,32,512]{2,1,0:T(8,128)(2,1)S(1)} %collective-permute-done.3.refs_1_), custom_call_target="tpu_custom_call" | custom-call | tf_op jit(solution)/shard_map/pallas_call | solution.py:259
  55.6 4.1 %all-to-all-done.1.refs_0_.rest_0_ = bf16[8,96,512]{2,1,0:T(8,128)(2,1)S(1)} async-done(((bf16[8,96,512]{2,1,0:T(8,128)(2,1)}), bf16[8,96,512]{2,1,0:T(8,128)(2,1)S(1)}, u32[]{:S(2)}, u32[]{:S(2)}) %all-to-all-start.1) | async-done | bytes 786464 | tf_op jit(solution)/shard_map/all_to_all | solution.py:397
  59.7 3.6 %all-to-all-start.2 = ((bf16[8,32,512]{2,1,0:T(8,128)(2,1)}), bf16[8,32,512]{2,1,0:T(8,128)(2,1)S(1)}, u32[]{:S(2)}, u32[]{:S(2)}) async-start(bf16[8,32,512]{2,1,0:T(8,128)(2,1)} %shard_map.139), calls=%async_computation.2 | async-start | bytes 524288 | tf_op jit(solution)/shard_map/all_to_all | solution.py:397
  63.3 0.6 shard_map.140
  63.9 0.6 bitcast_convert_fusion.cond_ref
  64.5 0.8 copy.50
  65.4 0.8 copy.49
  66.7 0.2 select_reduce_fusion.1
  66.9 5.4 %all-to-all-done.2.refs_0_.rest_1_ = bf16[8,32,512]{2,1,0:T(8,128)(2,1)S(1)} async-done(((bf16[8,32,512]{2,1,0:T(8,128)(2,1)}), bf16[8,32,512]{2,1,0:T(8,128)(2,1)S(1)}, u32[]{:S(2)}, u32[]{:S(2)}) %all-to-all-start.2) | async-done | bytes 262176 | tf_op jit(solution)/shard_map/all_to_all | solution.py:397
  72.4 0.7 shard_map.141
  73.2 2.2 %collective-permute-done.6.rest_4_ = bf16[4,96,512]{2,1,0:T(8,128)(2,1)} collective-permute-done((bf16[4,96,512]{2,1,0:T(8,128)(2,1)S(1)}, bf16[4,96,512]{2,1,0:T(8,128)(2,1)}, u32[]{:S(2)}, u32[]{:S(2)}) %collective-permute-start.6) | collective-permute-done | bytes 393248 | tf_op jit(solution)/shard_map/ppermute | solution.py:339
  75.4 0.5 collective-permute-start.5
  76.0 2.2 %collective-permute-done.7.rest_5_ = bf16[4,32,512]{2,1,0:T(8,128)(2,1)S(1)} collective-permute-done((bf16[4,32,512]{2,1,0:T(8,128)(2,1)S(1)}, bf16[4,32,512]{2,1,0:T(8,128)(2,1)S(1)}, u32[]{:S(2)}, u32[]{:S(2)}) %collective-permute-start.7) | collective-permute-done | bytes 131104 | tf_op jit(solution)/shard_map/ppermute | solution.py:339
  78.2 0.6 pad_add_fusion.1.meta
  78.8 0.7 collective-permute-done.9.rest_7_
  79.6 0.6 copy-done.12
  80.1 0.1 copy-done.10
  80.3 0.3 copy-done.8
  80.5 0.1 copy-done.9
  80.7 23.1 %shard_map.142 = (bf16[256,2048]{1,0:T(8,128)(2,1)}, bf16[256,2048]{1,0:T(8,128)(2,1)}, f32[4,512]{1,0:T(4,128)}, f32[256,512]{1,0:T(8,128)}, bf16[256,512]{1,0:T(8,128)(2,1)}) custom-call(s32[25]{0:T(128)} %pad_add_fusion.1.meta, bf16[256,2048]{1,0:T(8,128)(2,1)} %bitcast.59, bf16[256,2048]{1,0:T(8,128)(2,1)} %bitcast.60, ...), custom_call_target="tpu_custom_call" | custom-call | flops 11811160064 | bytes 16777216 | tf_op jit(solution)/shard_map/pallas_call | solution.py:202
  103.8 1.2 collective-permute-start.10
  105.0 1.4 %collective-permute-done.10 = bf16[256,512]{1,0:T(8,128)(2,1)S(1)} collective-permute-done((bf16[256,512]{1,0:T(8,128)(2,1)}, bf16[256,512]{1,0:T(8,128)(2,1)S(1)}, u32[]{:S(2)}, u32[]{:S(2)}) %collective-permute-start.10) | collective-permute-done | bytes 262176 | tf_op jit(solution)/shard_map/ppermute | solution.py:297
  106.4 1.1 convert_add_fusion
  107.6 0.3 collective-permute-start.11
  107.8 5.6 %collective-permute-done.11 = bf16[1,128,512]{2,1,0:T(8,128)(2,1)S(1)} collective-permute-done((bf16[1,128,512]{2,1,0:T(8,128)(2,1)S(1)}, bf16[1,128,512]{2,1,0:T(8,128)(2,1)S(1)}, u32[]{:S(2)}, u32[]{:S(2)}) %collective-permute-start.11) | collective-permute-done | bytes 131104 | tf_op jit(solution)/shard_map/ppermute | solution.py:297
  113.4 11.2 %all_to_all.20 = bf16[8,16,512]{2,1,0:T(8,128)(2,1)S(1)} all-to-all(bf16[8,16,512]{2,1,0:T(8,128)(2,1)S(1)} %bitcast.51), channel_id=1, replica_groups=mesh['pool'=4,'dp'=8] {'dp'}, dimensions={0} | all-to-all | bytes 262144 | tf_op jit(solution)/shard_map/all_to_all | solution.py:308
  124.6 0.6 convert_reduce_fusion
  (72 shorter events, 2.2 us)
Async XLA Ops:
  0.6 2.4 %copy-start.5 = (s32[1,1,4,2]{2,3,1,0:T(2,128)S(1)}, s32[1,1,4,2]{2,3,1,0:T(2,128)}, u32[]{:S(2)}) copy-start(s32[1,1,4,2]{2,3,1,0:T(2,128)} %param.14) | copy-start | bytes 100
  0.6 2.6 %copy-start.6 = (s32[1,1,4,2]{2,3,1,0:T(2,128)S(1)}, s32[1,1,4,2]{2,3,1,0:T(2,128)}, u32[]{:S(2)}) copy-start(s32[1,1,4,2]{2,3,1,0:T(2,128)} %param.15) | copy-start | bytes 100
  0.7 2.7 %copy-start.7 = (s32[1,1,16]{2,1,0:T(1,128)S(1)}, s32[1,1,16]{2,1,0:T(1,128)}, u32[]{:S(2)}) copy-start(s32[1,1,16]{2,1,0:T(1,128)} %param.17) | copy-start | bytes 196
  2.2 23.7 %collective-permute-start = (bf16[16,96,512]{2,1,0:T(8,128)(2,1)S(1)}, bf16[16,96,512]{2,1,0:T(8,128)(2,1)S(1)}, u32[]{:S(2)}, u32[]{:S(2)}) collective-permute-start(bf16[16,96,512]{2,1,0:T(8,128)(2,1)S(1)} %slice.28), channel_id=1, source_target_pairs={{24,8},{25,9},{26,10},{27,11},{28,12},{29,13},{30,14},{31,15}} | collective-permute-start | bytes 4718600 | tf_op jit(solution)/shard_map/ppermute | solution.py:339
  4.1 21.9 %all-to-all-start = ((s32[32,1,128]{2,1,0:T(1,128)}), s32[32,1,128]{2,1,0:T(1,128)S(1)}, u32[]{:S(2)}, u32[]{:S(2)}) async-start(s32[32,1,128]{2,1,0:T(1,128)} %broadcast_in_dim.83), calls=%async_computation | async-start | bytes 32768 | tf_op jit(solution)/shard_map/all_to_all | solution.py:352
  27.5 5.3 %collective-permute-start.1 = (bf16[16,96,512]{2,1,0:T(8,128)(2,1)S(1)}, bf16[16,96,512]{2,1,0:T(8,128)(2,1)S(1)}, u32[]{:S(2)}, u32[]{:S(2)}) collective-permute-start(bf16[16,96,512]{2,1,0:T(8,128)(2,1)S(1)} %broadcast_select_fusion.refs_0_), channel_id=1, source_target_pairs={{24,16},{25,17},{26,18},{27,19},{28,20},{29,21},{30,22},{31,23},{8... | collective-permute-start | bytes 4718600 | tf_op jit(solution)/shard_map/ppermute | solution.py:339
  34.3 25.3 %all-to-all-start.1 = ((bf16[8,96,512]{2,1,0:T(8,128)(2,1)}), bf16[8,96,512]{2,1,0:T(8,128)(2,1)S(1)}, u32[]{:S(2)}, u32[]{:S(2)}) async-start(bf16[8,96,512]{2,1,0:T(8,128)(2,1)} %shard_map.138), calls=%async_computation.1 | async-start | bytes 1572864 | tf_op jit(solution)/shard_map/all_to_all | solution.py:397
  40.3 0.8 collective-permute-start.2
  42.2 21.7 %copy-start.4 = (bf16[1,1,4,512]{3,2,1,0:T(4,128)(2,1)S(1)}, bf16[1,1,4,512]{3,2,1,0:T(4,128)(2,1)}, u32[]{:S(2)}) copy-start(bf16[1,1,4,512]{3,2,1,0:T(4,128)(2,1)} %param.13) | copy-start | bytes 12292
  42.2 22.3 %copy-start.2 = (bf16[512,256]{1,0:T(8,128)(2,1)S(1)}, bf16[512,256]{1,0:T(8,128)(2,1)}, u32[]{:S(2)}) copy-start(bf16[512,256]{1,0:T(8,128)(2,1)} %down_ref.1) | copy-start | bytes 786436
  42.3 12.1 %collective-permute-start.3 = (bf16[16,32,512]{2,1,0:T(8,128)(2,1)S(1)}, bf16[16,32,512]{2,1,0:T(8,128)(2,1)S(1)}, u32[]{:S(2)}, u32[]{:S(2)}) collective-permute-start(bf16[16,32,512]{2,1,0:T(8,128)(2,1)S(1)} %broadcast_select_fusion.1.refs_0_), channel_id=1, source_target_pairs={{24,16},{25,17},{26,18},{27,19},{28,20},{29,21},{30,22},{31,23},{8... | collective-permute-start | bytes 1572872 | tf_op jit(solution)/shard_map/ppermute | solution.py:339
  45.1 20.3 %copy-start.3 = (bf16[256,512]{1,0:T(8,128)(2,1)S(1)}, bf16[256,512]{1,0:T(8,128)(2,1)}, u32[]{:S(2)}) copy-start(bf16[256,512]{1,0:T(8,128)(2,1)} %up_ref.1) | copy-start | bytes 786436
  59.7 13.4 %copy-start = (bf16[8,96,512]{2,1,0:T(8,128)(2,1)}, bf16[8,96,512]{2,1,0:T(8,128)(2,1)S(1)}, u32[]{:S(2)}) copy-start(bf16[8,96,512]{2,1,0:T(8,128)(2,1)S(1)} %all-to-all-done.1.refs_0_.rest_0_) | copy-start | bytes 2359300
  59.7 12.7 %all-to-all-start.2 = ((bf16[8,32,512]{2,1,0:T(8,128)(2,1)}), bf16[8,32,512]{2,1,0:T(8,128)(2,1)S(1)}, u32[]{:S(2)}, u32[]{:S(2)}) async-start(bf16[8,32,512]{2,1,0:T(8,128)(2,1)} %shard_map.139), calls=%async_computation.2 | async-start | bytes 524288 | tf_op jit(solution)/shard_map/all_to_all | solution.py:397
  63.8 11.5 %collective-permute-start.6 = (bf16[4,96,512]{2,1,0:T(8,128)(2,1)S(1)}, bf16[4,96,512]{2,1,0:T(8,128)(2,1)}, u32[]{:S(2)}, u32[]{:S(2)}) collective-permute-start(bf16[4,96,512]{2,1,0:T(8,128)(2,1)S(1)} %shard_map.140), channel_id=1, source_target_pairs={{0,16},{1,17},{2,18},{3,19},{4,20},{5,21},{6,22},{7,23},{8,24},{9,... | collective-permute-start | bytes 1179656 | tf_op jit(solution)/shard_map/ppermute | solution.py:339
  66.7 12.8 %collective-permute-start.4 = (bf16[8,96,512]{2,1,0:T(8,128)(2,1)S(1)}, bf16[8,96,512]{2,1,0:T(8,128)(2,1)S(1)}, u32[]{:S(2)}, u32[]{:S(2)}) collective-permute-start(bf16[8,96,512]{2,1,0:T(8,128)(2,1)S(1)} %all-to-all-done.1.refs_0_.rest_0_), channel_id=1, source_target_pairs={{0,8},{1,9},{2,10},{3,11},{4,12},{5,13},{6,14},{7,15},{8,0},{9,1},... | collective-permute-start | bytes 2359304 | tf_op jit(solution)/shard_map/ppermute | solution.py:339
  72.4 7.2 %copy-start.1 = (bf16[8,32,512]{2,1,0:T(8,128)(2,1)}, bf16[8,32,512]{2,1,0:T(8,128)(2,1)S(1)}, u32[]{:S(2)}) copy-start(bf16[8,32,512]{2,1,0:T(8,128)(2,1)S(1)} %all-to-all-done.2.refs_0_.rest_1_) | copy-start | bytes 786436
  73.1 5.0 %collective-permute-start.7 = (bf16[4,32,512]{2,1,0:T(8,128)(2,1)S(1)}, bf16[4,32,512]{2,1,0:T(8,128)(2,1)S(1)}, u32[]{:S(2)}, u32[]{:S(2)}) collective-permute-start(bf16[4,32,512]{2,1,0:T(8,128)(2,1)S(1)} %shard_map.141), channel_id=1, source_target_pairs={{0,16},{1,17},{2,18},{3,19},{4,20},{5,21},{6,22},{7,23},{8,24},{9,... | collective-permute-start | bytes 393224 | tf_op jit(solution)/shard_map/ppermute | solution.py:339
  75.4 4.1 %collective-permute-start.8 = (bf16[4,96,512]{2,1,0:T(8,128)(2,1)}, bf16[4,96,512]{2,1,0:T(8,128)(2,1)S(1)}, u32[]{:S(2)}, u32[]{:S(2)}) collective-permute-start(bf16[4,96,512]{2,1,0:T(8,128)(2,1)} %collective-permute-done.6.rest_4_), channel_id=1, source_target_pairs={{0,8},{1,9},{2,10},{3,11},{4,12},{5,13},{6,14},{7,15},{8,0},{9,1},... | collective-permute-start | bytes 1179656 | tf_op jit(solution)/shard_map/ppermute | solution.py:339
  75.4 4.1 %collective-permute-start.5 = (bf16[8,32,512]{2,1,0:T(8,128)(2,1)S(1)}, bf16[8,32,512]{2,1,0:T(8,128)(2,1)S(1)}, u32[]{:S(2)}, u32[]{:S(2)}) collective-permute-start(bf16[8,32,512]{2,1,0:T(8,128)(2,1)S(1)} %all-to-all-done.2.refs_0_.rest_1_), channel_id=1, source_target_pairs={{0,8},{1,9},{2,10},{3,11},{4,12},{5,13},{6,14},{7,15},{8,0},{9,1},... | collective-permute-start | bytes 786440 | tf_op jit(solution)/shard_map/ppermute | solution.py:339
  78.1 1.4 %copy-start.11 = (bf16[4,32,512]{2,1,0:T(8,128)(2,1)}, bf16[4,32,512]{2,1,0:T(8,128)(2,1)S(1)}, u32[]{:S(2)}) copy-start(bf16[4,32,512]{2,1,0:T(8,128)(2,1)S(1)} %collective-permute-done.7.rest_5_) | copy-start | bytes 393220
  78.2 1.3 %collective-permute-start.9 = (bf16[4,32,512]{2,1,0:T(8,128)(2,1)S(1)}, bf16[4,32,512]{2,1,0:T(8,128)(2,1)S(1)}, u32[]{:S(2)}, u32[]{:S(2)}) collective-permute-start(bf16[4,32,512]{2,1,0:T(8,128)(2,1)S(1)} %collective-permute-done.7.rest_5_), channel_id=1, source_target_pairs={{0,8},{1,9},{2,10},{3,11},{4,12},{5,13},{6,14},{7,15},{8,0},{9,1},... | collective-permute-start | bytes 393224 | tf_op jit(solution)/shard_map/ppermute | solution.py:339
  79.5 0.6 copy-start.12
  79.5 0.8 copy-start.10
  79.5 1.0 copy-start.8
  79.5 1.1 copy-start.9
  103.8 2.6 %collective-permute-start.10 = (bf16[256,512]{1,0:T(8,128)(2,1)}, bf16[256,512]{1,0:T(8,128)(2,1)S(1)}, u32[]{:S(2)}, u32[]{:S(2)}) collective-permute-start(bf16[256,512]{1,0:T(8,128)(2,1)} %get-tuple-element.21), channel_id=1, source_target_pairs={{0,8},{8,0},{16,24},{24,16},{1,9},{9,1},{17,25},{25,17},{2,10},{10... | collective-permute-start | bytes 786440 | tf_op jit(solution)/shard_map/ppermute | solution.py:297
  107.6 5.8 %collective-permute-start.11 = (bf16[1,128,512]{2,1,0:T(8,128)(2,1)S(1)}, bf16[1,128,512]{2,1,0:T(8,128)(2,1)S(1)}, u32[]{:S(2)}, u32[]{:S(2)}) collective-permute-start(bf16[1,128,512]{2,1,0:T(8,128)(2,1)S(1)} %fusion.1), channel_id=1, source_target_pairs={{0,16},{8,24},{16,0},{24,8},{1,17},{9,25},{17,1},{25,9},{2,18},{10... | collective-permute-start | bytes 393224 | tf_op jit(solution)/shard_map/ppermute | solution.py:297
